TPU v7x, 32 devices: a whole 2x2x4 slice. The times are simulated.
32 devices in a mesh: seq: 8 (over y, x, core), fsdp: 4 (over z).
Axes of the slice: x: 2, y: 2, z: 4, core: 2. Of those that a mesh axis runs over, the one named last changes fastest.
Arguments:
- block_input: bfloat16 [4, 1536, 2560], P('fsdp', 'seq'), may hold values from -6 to 6
- cotangent: bfloat16 [4, 1536, 2560], P('fsdp', 'seq'), may hold values from -6 to 6
- mixer_gain: bfloat16 [2560], P(('seq', 'fsdp')), may hold values from 0.099609375 to 1.8984375
- branch_proj: bfloat16 [2560, 2560], P(('seq', 'fsdp')), may hold values from -0.125 to 0.125
- gelu_proj: bfloat16 [2560, 2560], P(('seq', 'fsdp')), may hold values from -0.125 to 0.125
- conv_taps: bfloat16 [4, 2560], P(None, ('seq', 'fsdp')), may hold values from -3 to 3
- conv_bias: bfloat16 [2560], P(('seq', 'fsdp')), may hold values from -3 to 3
- rate_blocks: bfloat16 [2560, 256], P(('seq', 'fsdp')), may hold values from -0.375 to 0.375
- input_blocks: bfloat16 [2560, 256], P(('seq', 'fsdp')), may hold values from -0.375 to 0.375
- rate_bias: bfloat16 [2560], P(('seq', 'fsdp')), may hold values from -4 to 4
- input_bias: bfloat16 [2560], P(('seq', 'fsdp')), may hold values from -4 to 4
- decay_param: bfloat16 [2560], P(('seq', 'fsdp')), may hold values from 3 to 16
- out_proj: bfloat16 [2560, 2560], P(('seq', 'fsdp')), may hold values from -0.3125 to 0.3125
- mlp_gain: bfloat16 [2560], P(('seq', 'fsdp')), may hold values from 0.099609375 to 1.8984375
- gate_proj: bfloat16 [2560, 7680], P(('seq', 'fsdp')), may hold values from -0.125 to 0.125
- up_proj: bfloat16 [2560, 7680], P(('seq', 'fsdp')), may hold values from -0.125 to 0.125
- down_proj: bfloat16 [2560, 7680], P(('seq', 'fsdp')), may hold values from -0.0625 to 0.0625
Outputs:
- block_output: bfloat16 [4, 1536, 2560], P('fsdp', 'seq')
- input_grad: bfloat16 [4, 1536, 2560], P('fsdp', 'seq')
- dmixer_gain: float32 [2560], P(('seq', 'fsdp'))
- dbranch_proj: float32 [2560, 2560], P(('seq', 'fsdp'))
- dgelu_proj: float32 [2560, 2560], P(('seq', 'fsdp'))
- dconv_taps: float32 [4, 2560], P(None, ('seq', 'fsdp'))
- dconv_bias: float32 [2560], P(('seq', 'fsdp'))
- drate_blocks: float32 [2560, 256], P(('seq', 'fsdp'))
- dinput_blocks: float32 [2560, 256], P(('seq', 'fsdp'))
- drate_bias: float32 [2560], P(('seq', 'fsdp'))
- dinput_bias: float32 [2560], P(('seq', 'fsdp'))
- ddecay_param: float32 [2560], P(('seq', 'fsdp'))
- dout_proj: float32 [2560, 2560], P(('seq', 'fsdp'))
- dmlp_gain: float32 [2560], P(('seq', 'fsdp'))
- dgate_proj: float32 [2560, 7680], P(('seq', 'fsdp'))
- dup_proj: float32 [2560, 7680], P(('seq', 'fsdp'))
- ddown_proj: float32 [2560, 7680], P(('seq', 'fsdp'))
All inputs are finite; a program needn't handle non-finite values.
Results may differ from a plain program's by a relative error of at most 0.012.
Values may be sent and summed in bfloat16 or wider, within the bound.
A program may use at most 832 MiB of HBM per device.

v0:
```python
import jax
import jax.numpy as jnp
from jax import lax
from jax.sharding import PartitionSpec as P

epsilon = 1e-06


def from_behind(shard, axis, by):
    devices = lax.axis_size(axis)
    pairs = [(i, i + by) for i in range(devices) if 0 <= i + by < devices]
    return lax.ppermute(shard, axis, pairs)


def prefix(part, axis, combine, identity, reverse):
    count = lax.axis_size(axis)
    place = lax.axis_index(axis)
    ahead = count - 1 - place if reverse else place
    gathered = jax.tree.map(lambda a: lax.all_gather(a, axis), part)
    state = jax.tree.map(lambda a, e: jnp.zeros_like(a) + jnp.asarray(e, a.dtype), part, identity)

    def one(hop, state):
        source = count - 1 - hop if reverse else hop
        return combine(
            state, jax.tree.map(lambda a: lax.dynamic_index_in_dim(a, source, 0, False), gathered)
        )

    return lax.fori_loop(0, ahead, one, state)


def to_low(values):
    return values.astype(jnp.bfloat16)


def norm_rows(values, scales):
    return values * lax.rsqrt(jnp.mean(values * values, axis=-1, keepdims=True) + epsilon) * scales


def combine_pairs(earlier, later):
    return (earlier[0] * later[0], later[1] + later[0] * earlier[1])


def gelu_tanh(values):
    return jax.nn.gelu(values, approximate=True)


def gate_values(rate_pre, input_pre, conv_in, param_decay):
    decay_log = -8.0 * jax.nn.sigmoid(rate_pre) * jax.nn.softplus(-param_decay)
    driven = jnp.sqrt(-jnp.expm1(2.0 * decay_log)) * jax.nn.sigmoid(input_pre) * conv_in
    return (decay_log, driven)


def block_product(values, blocks):
    block_width = blocks.shape[1]
    head_count = blocks.shape[0] // block_width
    grouped = values.reshape(values.shape[0], head_count, block_width)
    result = jnp.einsum(
        "thi,hij->thj",
        grouped,
        blocks.reshape(head_count, block_width, block_width),
        preferred_element_type=jnp.float32,
    )
    return result.reshape(values.shape[0], head_count * block_width)


def block_back(grads, blocks):
    block_width = blocks.shape[1]
    head_count = blocks.shape[0] // block_width
    grouped = grads.reshape(grads.shape[0], head_count, block_width)
    result = jnp.einsum(
        "thj,hij->thi",
        grouped,
        blocks.reshape(head_count, block_width, block_width),
        preferred_element_type=jnp.float32,
    )
    return result.reshape(grads.shape[0], head_count * block_width)


def block_weights(values, grads, block_width):
    head_count = values.shape[1] // block_width
    left = values.reshape(values.shape[0], head_count, block_width)
    right = grads.reshape(grads.shape[0], head_count, block_width)
    result = jnp.einsum("thi,thj->hij", left, right, preferred_element_type=jnp.float32)
    return result.reshape(head_count * block_width, block_width)


def on_device(
    block_input,
    cotangent,
    mixer_gain,
    branch_proj,
    gelu_proj,
    conv_taps,
    conv_bias,
    rate_blocks,
    input_blocks,
    rate_bias,
    input_bias,
    decay_param,
    out_proj,
    mlp_gain,
    gate_proj,
    up_proj,
    down_proj,
):
    mixer_set = (
        lax.all_gather(mixer_gain, ("seq", "fsdp"), axis=0, tiled=True),
        lax.all_gather(branch_proj, ("seq", "fsdp"), axis=0, tiled=True),
        lax.all_gather(gelu_proj, ("seq", "fsdp"), axis=0, tiled=True),
        lax.all_gather(conv_taps, ("seq", "fsdp"), axis=1, tiled=True),
        lax.all_gather(conv_bias, ("seq", "fsdp"), axis=0, tiled=True),
        lax.all_gather(rate_blocks, ("seq", "fsdp"), axis=0, tiled=True),
        lax.all_gather(input_blocks, ("seq", "fsdp"), axis=0, tiled=True),
        lax.all_gather(rate_bias, ("seq", "fsdp"), axis=0, tiled=True),
        lax.all_gather(input_bias, ("seq", "fsdp"), axis=0, tiled=True),
        lax.all_gather(decay_param, ("seq", "fsdp"), axis=0, tiled=True),
        lax.all_gather(out_proj, ("seq", "fsdp"), axis=0, tiled=True),
        lax.all_gather(mlp_gain, ("seq", "fsdp"), axis=0, tiled=True),
    )
    gain_one = mixer_set[0].astype(jnp.float32)
    proj_branch = mixer_set[1]
    proj_gelu = mixer_set[2]
    tap_rows = mixer_set[3].astype(jnp.float32)
    bias_conv = mixer_set[4].astype(jnp.float32)
    blocks_rate = mixer_set[5]
    blocks_input = mixer_set[6]
    bias_rate = mixer_set[7].astype(jnp.float32)
    bias_input = mixer_set[8].astype(jnp.float32)
    param_decay = mixer_set[9].astype(jnp.float32)
    proj_out = mixer_set[10]
    gain_two = mixer_set[11].astype(jnp.float32)
    block_width = blocks_rate.shape[1]
    tokens = block_input[0].astype(jnp.float32)
    tok_count = tokens.shape[0]
    margin = tap_rows.shape[0] - 1
    normed = to_low(norm_rows(tokens, gain_one))
    gelu_pre = jnp.dot(normed, proj_gelu, preferred_element_type=jnp.float32)
    gelu_out = gelu_tanh(gelu_pre)
    branch = to_low(jnp.dot(normed, proj_branch, preferred_element_type=jnp.float32))
    prior = from_behind(branch[tok_count - margin :], "seq", 1)
    extended = jnp.concatenate([prior, branch], axis=0).astype(jnp.float32)
    conv_sum = bias_conv + jnp.zeros((tok_count, tap_rows.shape[1]), jnp.float32)
    for offset in range(margin + 1):
        conv_sum = (
            conv_sum + tap_rows[offset] * extended[margin - offset : margin - offset + tok_count]
        )
    conv_low = to_low(conv_sum)
    conv_in = conv_low.astype(jnp.float32)
    rate_pre = block_product(conv_low, blocks_rate) + bias_rate
    input_pre = block_product(conv_low, blocks_input) + bias_input
    decay_log, driven = gate_values(rate_pre, input_pre, conv_in, param_decay)
    decay = jnp.exp(decay_log)
    cum_decay, local_states = lax.associative_scan(combine_pairs, (decay, driven), axis=0)
    identity = (jnp.ones_like(decay[0]), jnp.zeros_like(decay[0]))
    carried = prefix((cum_decay[-1], local_states[-1]), "seq", combine_pairs, identity, False)[1]
    states = local_states + cum_decay * carried[None, :]
    prev_states = jnp.concatenate([carried[None, :], states[:-1]], axis=0)
    mixed = to_low(states * gelu_out)
    middle = tokens + jnp.einsum("tl,dl->td", mixed, proj_out, preferred_element_type=jnp.float32)
    normed_two = to_low(norm_rows(middle, gain_two))
    grad_out = cotangent[0]
    mlp_set = (
        lax.all_gather(gate_proj, ("seq", "fsdp"), axis=0, tiled=True),
        lax.all_gather(up_proj, ("seq", "fsdp"), axis=0, tiled=True),
        lax.all_gather(down_proj, ("seq", "fsdp"), axis=0, tiled=True),
    )
    proj_gate = mlp_set[0]
    proj_up = mlp_set[1]
    proj_down = mlp_set[2]
    gate = jnp.dot(normed_two, proj_gate, preferred_element_type=jnp.float32)
    up_val = jnp.dot(normed_two, proj_up, preferred_element_type=jnp.float32)
    gelu_gate = gelu_tanh(gate)
    hidden = to_low(gelu_gate * up_val)
    output = middle + jnp.einsum("tf,df->td", hidden, proj_down, preferred_element_type=jnp.float32)
    block_output = output.astype(jnp.bfloat16)[None]
    mixer_back = (
        lax.all_gather(mixer_gain, ("seq", "fsdp"), axis=0, tiled=True),
        lax.all_gather(branch_proj, ("seq", "fsdp"), axis=0, tiled=True),
        lax.all_gather(gelu_proj, ("seq", "fsdp"), axis=0, tiled=True),
        lax.all_gather(conv_taps, ("seq", "fsdp"), axis=1, tiled=True),
        lax.all_gather(conv_bias, ("seq", "fsdp"), axis=0, tiled=True),
        lax.all_gather(rate_blocks, ("seq", "fsdp"), axis=0, tiled=True),
        lax.all_gather(input_blocks, ("seq", "fsdp"), axis=0, tiled=True),
        lax.all_gather(rate_bias, ("seq", "fsdp"), axis=0, tiled=True),
        lax.all_gather(input_bias, ("seq", "fsdp"), axis=0, tiled=True),
        lax.all_gather(decay_param, ("seq", "fsdp"), axis=0, tiled=True),
        lax.all_gather(out_proj, ("seq", "fsdp"), axis=0, tiled=True),
    )
    proj_branch = mixer_back[1]
    proj_gelu = mixer_back[2]
    blocks_rate = mixer_back[5]
    blocks_input = mixer_back[6]
    proj_out = mixer_back[10]
    mlp_back = (
        lax.all_gather(gate_proj, ("seq", "fsdp"), axis=0, tiled=True),
        lax.all_gather(up_proj, ("seq", "fsdp"), axis=0, tiled=True),
        lax.all_gather(down_proj, ("seq", "fsdp"), axis=0, tiled=True),
    )
    proj_gate = mlp_back[0]
    proj_up = mlp_back[1]
    proj_down = mlp_back[2]
    gelu_pull = jax.vjp(gelu_tanh, gate)[1]
    width_ff = gate_proj.shape[1]
    grad_hidden = jnp.dot(grad_out, proj_down, preferred_element_type=jnp.float32)
    grad_gate = to_low(gelu_pull(grad_hidden * up_val)[0])
    grad_up = to_low(grad_hidden * gelu_gate)
    grad_normed_two = jnp.einsum(
        "tf,df->td", grad_gate, proj_gate, preferred_element_type=jnp.float32
    ) + jnp.einsum("tf,df->td", grad_up, proj_up, preferred_element_type=jnp.float32)
    term_gate = jnp.einsum("tc,tf->cf", normed_two, grad_gate, preferred_element_type=jnp.float32)
    term_up = jnp.einsum("tc,tf->cf", normed_two, grad_up, preferred_element_type=jnp.float32)
    term_down = jnp.einsum("tc,tf->cf", grad_out, hidden, preferred_element_type=jnp.float32)
    mlp_summed = lax.psum_scatter(
        jnp.concatenate([term_gate, term_up, term_down], axis=1),
        ("seq", "fsdp"),
        scatter_dimension=0,
        tiled=True,
    )
    dgate_proj = mlp_summed[:, :width_ff]
    dup_proj = mlp_summed[:, width_ff : 2 * width_ff]
    ddown_proj = mlp_summed[:, 2 * width_ff :]
    second_pull = jax.vjp(norm_rows, middle, gain_two)[1]
    grad_mid_part, grad_gain_two = second_pull(grad_normed_two)
    grad_middle = grad_out.astype(jnp.float32) + grad_mid_part
    grad_mix = to_low(grad_middle)
    grad_mixed = jnp.dot(grad_mix, proj_out, preferred_element_type=jnp.float32)
    pre_pull = jax.vjp(gelu_tanh, gelu_pre)[1]
    grad_gelu_pre = to_low(pre_pull(grad_mixed * states)[0])
    direct = grad_mixed * gelu_out
    decay_next = jnp.concatenate([decay[1:], jnp.ones((1, decay.shape[1]), jnp.float32)], axis=0)
    rev_cum, rev_grad = lax.associative_scan(
        combine_pairs, (decay_next, direct), axis=0, reverse=True
    )
    pair_decay = cum_decay[-1]
    pair_grad = decay[0] * rev_grad[0]
    incoming = prefix((pair_decay, pair_grad), "seq", combine_pairs, identity, True)[1]
    grad_states = rev_grad + rev_cum * incoming[None, :]
    grad_log = grad_states * decay * prev_states
    gate_pull = jax.vjp(gate_values, rate_pre, input_pre, conv_in, param_decay)[1]
    grad_rate_pre, grad_input_pre, grad_conv_direct, grad_decay = gate_pull((grad_log, grad_states))
    grad_rate = to_low(grad_rate_pre)
    grad_input = to_low(grad_input_pre)
    grad_conv = (
        grad_conv_direct + block_back(grad_rate, blocks_rate) + block_back(grad_input, blocks_input)
    )
    zero_rows = jnp.zeros((margin, grad_conv.shape[1]), jnp.float32)
    padded_grad = jnp.concatenate([zero_rows, grad_conv, zero_rows], axis=0)
    grad_extended = jnp.zeros((tok_count + margin, grad_conv.shape[1]), jnp.float32)
    tap_terms = []
    for offset in range(margin + 1):
        grad_extended = (
            grad_extended + tap_rows[offset] * padded_grad[offset : offset + tok_count + margin]
        )
        tap_terms.append(
            jnp.sum(grad_conv * extended[margin - offset : margin - offset + tok_count], axis=0)
        )
    tap_grads = jnp.stack(tap_terms, axis=0)
    received = from_behind(grad_extended[:margin], "seq", -1)
    own_rows = grad_extended[margin:]
    grad_branch = to_low(
        jnp.concatenate(
            [own_rows[: tok_count - margin], own_rows[tok_count - margin :] + received], axis=0
        )
    )
    grad_normed = jnp.einsum(
        "tl,dl->td", grad_branch, proj_branch, preferred_element_type=jnp.float32
    ) + jnp.einsum("tl,dl->td", grad_gelu_pre, proj_gelu, preferred_element_type=jnp.float32)
    first_pull = jax.vjp(norm_rows, tokens, gain_one)[1]
    grad_tok_part, grad_gain_one = first_pull(grad_normed)
    input_grad = (grad_middle + grad_tok_part).astype(jnp.bfloat16)[None]
    summed = (
        lax.psum_scatter(grad_gain_one, ("seq", "fsdp"), scatter_dimension=0, tiled=True),
        lax.psum_scatter(
            jnp.einsum("td,tl->dl", normed, grad_branch, preferred_element_type=jnp.float32),
            ("seq", "fsdp"),
            scatter_dimension=0,
            tiled=True,
        ),
        lax.psum_scatter(
            jnp.einsum("td,tl->dl", normed, grad_gelu_pre, preferred_element_type=jnp.float32),
            ("seq", "fsdp"),
            scatter_dimension=0,
            tiled=True,
        ),
        lax.psum_scatter(tap_grads, ("seq", "fsdp"), scatter_dimension=1, tiled=True),
        lax.psum_scatter(
            jnp.sum(grad_conv, axis=0), ("seq", "fsdp"), scatter_dimension=0, tiled=True
        ),
        lax.psum_scatter(
            block_weights(conv_low, grad_rate, block_width),
            ("seq", "fsdp"),
            scatter_dimension=0,
            tiled=True,
        ),
        lax.psum_scatter(
            block_weights(conv_low, grad_input, block_width),
            ("seq", "fsdp"),
            scatter_dimension=0,
            tiled=True,
        ),
        lax.psum_scatter(
            jnp.sum(grad_rate.astype(jnp.float32), axis=0),
            ("seq", "fsdp"),
            scatter_dimension=0,
            tiled=True,
        ),
        lax.psum_scatter(
            jnp.sum(grad_input.astype(jnp.float32), axis=0),
            ("seq", "fsdp"),
            scatter_dimension=0,
            tiled=True,
        ),
        lax.psum_scatter(grad_decay, ("seq", "fsdp"), scatter_dimension=0, tiled=True),
        lax.psum_scatter(
            jnp.einsum("td,tl->dl", grad_mix, mixed, preferred_element_type=jnp.float32),
            ("seq", "fsdp"),
            scatter_dimension=0,
            tiled=True,
        ),
        lax.psum_scatter(grad_gain_two, ("seq", "fsdp"), scatter_dimension=0, tiled=True),
    )
    return (
        block_output,
        input_grad,
        summed[0],
        summed[1],
        summed[2],
        summed[3],
        summed[4],
        summed[5],
        summed[6],
        summed[7],
        summed[8],
        summed[9],
        summed[10],
        summed[11],
        dgate_proj,
        dup_proj,
        ddown_proj,
    )


def solution(mesh):
    return jax.shard_map(
        on_device,
        mesh=mesh,
        in_specs=(
            P("fsdp", "seq", None),
            P("fsdp", "seq", None),
            P(("seq", "fsdp")),
            P(("seq", "fsdp"), None),
            P(("seq", "fsdp"), None),
            P(None, ("seq", "fsdp")),
            P(("seq", "fsdp")),
            P(("seq", "fsdp"), None),
            P(("seq", "fsdp"), None),
            P(("seq", "fsdp")),
            P(("seq", "fsdp")),
            P(("seq", "fsdp")),
            P(("seq", "fsdp"), None),
            P(("seq", "fsdp")),
            P(("seq", "fsdp"), None),
            P(("seq", "fsdp"), None),
            P(("seq", "fsdp"), None),
        ),
        out_specs=(
            P("fsdp", "seq", None),
            P("fsdp", "seq", None),
            P(("seq", "fsdp")),
            P(("seq", "fsdp"), None),
            P(("seq", "fsdp"), None),
            P(None, ("seq", "fsdp")),
            P(("seq", "fsdp")),
            P(("seq", "fsdp"), None),
            P(("seq", "fsdp"), None),
            P(("seq", "fsdp")),
            P(("seq", "fsdp")),
            P(("seq", "fsdp")),
            P(("seq", "fsdp"), None),
            P(("seq", "fsdp")),
            P(("seq", "fsdp"), None),
            P(("seq", "fsdp"), None),
            P(("seq", "fsdp"), None),
        ),
        check_vma=False,
    )
```

profile of v0, /device:TPU:0, one launch (start us, length us, event | category | flops | bytes accessed | tf_op | source)
XLA Modules:
  0.0 5410.9 jit_solution(8650864035307633781)
XLA Ops:
  14.3 43.9 all-reduce.73
  58.3 66.2 %all-gather = bf16[32,80,4]{1,2,0:T(4,128)(2,1)S(1)} all-gather(bf16[1,80,4]{1,2,0:T(4,128)(2,1)S(1)} %bitcast.134), channel_id=1, replica_groups=mesh['seq'=8,'fsdp'=4] {'seq','fsdp'}, dimensions={0}, use_global_device_ids=true | all-gather | bytes 21120 | tf_op jit(solution)/shard_map/all_gather | solution.py:110
  125.0 7.5 convolution_convert_fusion
  141.5 27.0 all-gather.17.cloned.1.call-done
  178.2 46.5 all-gather.15.cloned.1.call-done
  354.7 9.5 all-gather.1
  378.4 8.4 all-gather.2
  387.5 10.3 slice.607
  397.8 10.4 slice.597
  408.2 10.3 slice.601
  418.6 12.3 multiply_convert_fusion.3
  430.9 8.3 multiply_reduce_fusion.7
  439.5 209.0 %all-gather.25.cloned.1.call-done = bf16[2560,7680]{1,0:T(8,128)(2,1)} async-done(((bf16[80,7680]{1,0:T(8,128)(2,1)}), bf16[2560,7680]{1,0:T(8,128)(2,1)}) %all-gather.25.cloned.1.call-update) | async-done | bytes 39321616 | tf_op jit(solution)/shard_map/all_gather | solution.py:164
  648.5 20.1 fusion.97
  668.6 203.4 %all-gather.23.cloned.1.call-done = bf16[2560,7680]{1,0:T(8,128)(2,1)} async-done(((bf16[80,7680]{1,0:T(8,128)(2,1)}), bf16[2560,7680]{1,0:T(8,128)(2,1)}) %all-gather.23.cloned.1.call-update) | async-done | bytes 39321616 | tf_op jit(solution)/shard_map/all_gather | solution.py:163
  872.0 20.3 fusion.96
  892.3 203.2 %all-gather.27.cloned.1.call-done = bf16[2560,7680]{1,0:T(8,128)(2,1)} async-done(((bf16[80,7680]{1,0:T(8,128)(2,1)}), bf16[2560,7680]{1,0:T(8,128)(2,1)}) %all-gather.27.cloned.1.call-update) | async-done | bytes 39321616 | tf_op jit(solution)/shard_map/all_gather | solution.py:165
  1095.5 24.5 multiply_convert_fusion
  1119.9 20.2 fusion.98
  1140.1 21.9 multiply_reduce_fusion
  1165.1 9.8 fusion.40
  1181.7 10.4 slice.603
  1192.0 6.4 slice.599
  1226.0 6.6 slice.594
  1271.3 29.1 fusion.103
  1300.4 28.9 fusion.102
  1331.2 12.9 rev.8
  1344.2 9.4 all-gather.3
  1353.5 6.9 while.27
  1370.0 20.2 rev.9
  1390.3 6.6 multiply_reduce_fusion.1
  1425.6 7.0 multiply_reduce_fusion.5
  1434.3 29.2 convolution_bitcast_fusion
  1463.5 154.5 %pad_maximum_fusion = f32[2560,23040]{1,0:T(8,128)} fusion(f32[2560,7680]{1,0:T(8,128)} %convolution_bitcast_fusion, f32[2560,7680]{1,0:T(8,128)} %fusion.103, f32[2560,7680]{1,0:T(8,128)} %fusion.102), kind=kLoop, calls=%fused_computation.6 | loop fusion | flops 117964800 | bytes 471859200 | tf_op jit(solution)/shard_map/concatenate | solution.py:214
  1627.7 18.0 fusion.44
  1647.1 18.1 fusion.74
  1672.4 17.1 fusion.41
  1689.5 13.8 fusion.99
  1703.3 29.3 fusion.8
  1732.6 15.0 fusion.15
  1747.6 39.2 all-reduce.72
  1795.4 1639.8 %reduce-scatter.20.cloned.1.call-done = f32[80,23040]{1,0:T(8,128)} async-done(((f32[2560,23040]{1,0:T(8,128)}), f32[80,23040]{1,0:T(8,128)}) %reduce-scatter.20.cloned.1.call-update) | async-done | bytes 7372816 | tf_op jit(solution)/shard_map/reduce_scatter | solution.py:213
  3435.3 6.4 fusion.83
  3441.7 136.2 %reduce-scatter.14.cloned.1.call-done = f32[80,256]{1,0:T(8,128)} async-done(((f32[2560,256]{1,0:T(8,128)}), f32[80,256]{1,0:T(8,128)}) %reduce-scatter.14.cloned.1.call-update) | async-done | bytes 81936 | tf_op jit(solution)/shard_map/reduce_scatter | solution.py:289
  3577.9 141.2 %reduce-scatter.16.cloned.1.call-done = f32[80,256]{1,0:T(8,128)} async-done(((f32[2560,256]{1,0:T(8,128)}), f32[80,256]{1,0:T(8,128)}) %reduce-scatter.16.cloned.1.call-update) | async-done | bytes 81936 | tf_op jit(solution)/shard_map/reduce_scatter | solution.py:295
  3719.1 561.6 %reduce-scatter.18.cloned.1.call-done = f32[80,2560]{1,0:T(8,128)} async-done(((f32[2560,2560]{1,0:T(8,128)}), f32[80,2560]{1,0:T(8,128)}) %reduce-scatter.18.cloned.1.call-update) | async-done | bytes 819216 | tf_op jit(solution)/shard_map/reduce_scatter | solution.py:314
  4280.7 561.7 %reduce-scatter.12.cloned.1.call-done = f32[80,2560]{1,0:T(8,128)} async-done(((f32[2560,2560]{1,0:T(8,128)}), f32[80,2560]{1,0:T(8,128)}) %reduce-scatter.12.cloned.1.call-update) | async-done | bytes 819216 | tf_op jit(solution)/shard_map/reduce_scatter | solution.py:279
  4842.4 561.7 %reduce-scatter.10.cloned.1.call-done = f32[80,2560]{1,0:T(8,128)} async-done(((f32[2560,2560]{1,0:T(8,128)}), f32[80,2560]{1,0:T(8,128)}) %reduce-scatter.10.cloned.1.call-update) | async-done | bytes 819216 | tf_op jit(solution)/shard_map/reduce_scatter | solution.py:273
  (590 shorter events, 321.0 us)
Async XLA Ops:
  7.2 117.8 %all-gather.13.cloned.1.call-start = ((), (), s32[]{:S(2)}) async-start(), calls=%async_computation.7 | async-start | bytes 13516800 | tf_op jit(solution)/shard_map/all_gather | solution.py:108
  7.9 160.6 %all-gather.17.cloned.1.call-start = ((), (), s32[]{:S(2)}) async-start(), calls=%async_computation.9 | async-start | bytes 1351680 | tf_op jit(solution)/shard_map/all_gather | solution.py:113
  8.7 216.0 %all-gather.15.cloned.1.call-start = ((), (), s32[]{:S(2)}) async-start(), calls=%async_computation.8 | async-start | bytes 1351680 | tf_op jit(solution)/shard_map/all_gather | solution.py:112
  9.4 409.2 %all-gather.19.cloned.1.call-start = ((), (), s32[]{:S(2)}) async-start(), calls=%async_computation.10 | async-start | bytes 13516800 | tf_op jit(solution)/shard_map/all_gather | solution.py:109
  10.0 420.9 %all-gather.21.cloned.1.call-start = ((), (), s32[]{:S(2)}) async-start(), calls=%async_computation.11 | async-start | bytes 13516800 | tf_op jit(solution)/shard_map/all_gather | solution.py:117
  10.6 47.7 copy-start.108
  10.6 114.0 %copy-start.4 = (bf16[1,192,2560]{2,1,0:T(8,128)(2,1)S(1)}, bf16[1,192,2560]{2,1,0:T(8,128)(2,1)}, u32[]{:S(2)}) copy-start(bf16[1,192,2560]{2,1,0:T(8,128)(2,1)} %param.21) | copy-start | bytes 2949124
  10.7 637.8 %all-gather.25.cloned.1.call-start = ((), (), s32[]{:S(2)}) async-start(), calls=%async_computation.13 | async-start | bytes 40550400 | tf_op jit(solution)/shard_map/all_gather | solution.py:164
  11.2 860.7 %all-gather.23.cloned.1.call-start = ((), (), s32[]{:S(2)}) async-start(), calls=%async_computation.12 | async-start | bytes 40550400 | tf_op jit(solution)/shard_map/all_gather | solution.py:163
  12.0 1083.5 %all-gather.27.cloned.1.call-start = ((), (), s32[]{:S(2)}) async-start(), calls=%async_computation.14 | async-start | bytes 40550400 | tf_op jit(solution)/shard_map/all_gather | solution.py:165
  12.7 1781.3 %reduce-scatter.22.cloned.1.call-start = ((), (), s32[]{:S(2)}) async-start(), calls=%async_computation.21 | async-start | bytes 1351680
  58.3 74.2 %copy-start.103 = (bf16[2560]{0:T(1024)(128)(2,1)}, bf16[2560]{0:T(1024)(128)(2,1)S(1)}, u32[]{:S(2)}) copy-start(bf16[2560]{0:T(1024)(128)(2,1)S(1)} %get-tuple-element.186) | copy-start | bytes 15364
  58.3 360.3 %copy-start.49 = (f32[2560]{0:T(1024)}, f32[2560]{0:T(1024)S(1)}, u32[]{:S(2)}) copy-start(f32[2560]{0:T(1024)S(1)} %convert_element_type.89) | copy-start | bytes 30724
  124.9 293.7 %copy-start.75 = (f32[192]{0:T(256)}, f32[192]{0:T(256)S(1)}, u32[]{:S(2)}) copy-start(f32[192]{0:T(256)S(1)} %fusion.70) | copy-start | bytes 2308
  125.0 109.4 %copy-start.67 = (f32[2560]{0:T(1024)}, f32[2560]{0:T(1024)S(1)}, u32[]{:S(2)}) copy-start(f32[2560]{0:T(1024)S(1)} %broadcast_multiply_fusion) | copy-start | bytes 30724
  133.5 2.1 collective-permute-start
  134.9 99.5 %copy-start.54 = (f32[2560]{0:T(1024)}, f32[2560]{0:T(1024)S(1)}, u32[]{:S(2)}) copy-start(f32[2560]{0:T(1024)S(1)} %get-tuple-element.156) | copy-start | bytes 30724
  134.9 99.5 %copy-start.57 = (f32[2560]{0:T(1024)}, f32[2560]{0:T(1024)S(1)}, u32[]{:S(2)}) copy-start(f32[2560]{0:T(1024)S(1)} %get-tuple-element.157) | copy-start | bytes 30724
  134.9 99.5 %copy-start.60 = (f32[2560]{0:T(1024)}, f32[2560]{0:T(1024)S(1)}, u32[]{:S(2)}) copy-start(f32[2560]{0:T(1024)S(1)} %get-tuple-element.158) | copy-start | bytes 30724
  134.9 99.5 %copy-start.63 = (f32[2560]{0:T(1024)}, f32[2560]{0:T(1024)S(1)}, u32[]{:S(2)}) copy-start(f32[2560]{0:T(1024)S(1)} %get-tuple-element.159) | copy-start | bytes 30724
  135.0 99.5 %copy-start.73 = (f32[2560]{0:T(1024)}, f32[2560]{0:T(1024)S(1)}, u32[]{:S(2)}) copy-start(f32[2560]{0:T(1024)S(1)} %convert_element_type.87) | copy-start | bytes 30724
  135.0 99.5 %copy-start.69 = (f32[2560]{0:T(1024)}, f32[2560]{0:T(1024)S(1)}, u32[]{:S(2)}) copy-start(f32[2560]{0:T(1024)S(1)} %convert_element_type.94) | copy-start | bytes 30724
  135.0 99.4 %copy-start.71 = (f32[2560]{0:T(1024)}, f32[2560]{0:T(1024)S(1)}, u32[]{:S(2)}) copy-start(f32[2560]{0:T(1024)S(1)} %convert_element_type.96) | copy-start | bytes 30724
  137.1 97.4 %copy-start = (f32[195,2560]{1,0:T(8,128)}, f32[195,2560]{1,0:T(8,128)S(1)}, u32[]{:S(2)}) copy-start(f32[195,2560]{1,0:T(8,128)S(1)} %maximum_convert_fusion) | copy-start | bytes 5990404
  353.7 16.0 copy-start.84
  386.9 21.3 copy-start.66
  439.2 722.9 %copy-start.22 = (f32[192,2560]{1,0:T(8,128)}, f32[192,2560]{1,0:T(8,128)S(1)}, u32[]{:S(2)}) copy-start(f32[192,2560]{1,0:T(8,128)S(1)} %get-tuple-element.286) | copy-start | bytes 5898244
  1300.4 28.9 copy-start.32
  1344.1 18.7 copy-start.30
  1369.9 20.3 copy-start.1
  1369.9 20.3 copy-start.55
  1369.9 20.3 copy-start.58
  1369.9 20.3 copy-start.61
  1369.9 20.3 copy-start.64
  1369.9 20.3 copy-start.68
  1370.0 20.3 copy-start.70
  1370.0 20.3 copy-start.72
  1370.0 20.3 copy-start.74
  1370.0 20.3 copy-start.83
  1434.3 2001.0 %reduce-scatter.20.cloned.1.call-start = ((), (), s32[]{:S(2)}) async-start(), calls=%async_computation.20 | async-start | bytes 243302400 | tf_op jit(solution)/shard_map/reduce_scatter | solution.py:213
  1618.1 1959.8 %reduce-scatter.14.cloned.1.call-start = ((), (), s32[]{:S(2)}) async-start(), calls=%async_computation.17 | async-start | bytes 2703360 | tf_op jit(solution)/shard_map/reduce_scatter | solution.py:289
  1621.8 2097.3 %reduce-scatter.16.cloned.1.call-start = ((), (), s32[]{:S(2)}) async-start(), calls=%async_computation.18 | async-start | bytes 2703360 | tf_op jit(solution)/shard_map/reduce_scatter | solution.py:295
  1625.7 2655.0 %reduce-scatter.18.cloned.1.call-start = ((), (), s32[]{:S(2)}) async-start(), calls=%async_computation.19 | async-start | bytes 27033600 | tf_op jit(solution)/shard_map/reduce_scatter | solution.py:314
  1645.8 3196.7 %reduce-scatter.12.cloned.1.call-start = ((), (), s32[]{:S(2)}) async-start(), calls=%async_computation.16 | async-start | bytes 27033600 | tf_op jit(solution)/shard_map/reduce_scatter | solution.py:279
  1665.3 3738.8 %reduce-scatter.10.cloned.1.call-start = ((), (), s32[]{:S(2)}) async-start(), calls=%async_computation.15 | async-start | bytes 27033600 | tf_op jit(solution)/shard_map/reduce_scatter | solution.py:273
  1669.2 3.1 collective-permute-start.1
  1732.6 15.0 copy-start.82
  1732.6 57.7 %copy-start.107 = (f32[192]{0:T(256)S(1)}, f32[192]{0:T(256)}, u32[]{:S(2)}) copy-start(f32[192]{0:T(256)} %copy-done.106) | copy-start | bytes 2308
  (84 other events, 300.7 us)
Sparse Core Ops, SparseCore 0:
  10.9 102.0 all-gather.12
  115.8 52.6 all-gather.16
  171.3 53.3 all-gather.14
  227.4 97.4 all-gather.18
  327.6 97.4 all-gather.20
  427.8 220.6 all-gather.24
  651.3 220.6 all-gather.22
  874.8 220.6 all-gather.26
  1434.4 133.3 reduce-scatter.21
  1618.2 1817.0 reduce-scatter.19
  3438.2 139.6 reduce-scatter.13
  3580.7 138.3 reduce-scatter.15
  3722.1 558.5 reduce-scatter.17
  4283.6 558.7 reduce-scatter.11
  4845.3 558.7 reduce-scatter.9
where the time goes:
time: 5430 us; the launch traced here: 5410 us
  waiting for transfers between devices  4300 us (79%)
  matrix products  362 us (7%)
  local copies, waits for them, and re-layouts  308 us (6%)
  other arithmetic  246 us (5%)
  blocking collectives  177 us (3%)
    reduce_scatter x1, waiting for transfers between devices, on_device(): lax.psum_scatter(jnp.concatenate([term_gate, term_up, term_down], axis=1)...  1640 us
    reduce_scatter x1, waiting for transfers between devices, on_device(): lax.psum_scatter(jnp.einsum('td,tl->dl', normed, grad_gelu_pre, preferred...  562 us
    reduce_scatter x1, waiting for transfers between devices, on_device(): lax.psum_scatter(jnp.einsum('td,tl->dl', normed, grad_branch, preferred_e...  562 us
    reduce_scatter x1, waiting for transfers between devices, on_device(): lax.psum_scatter(jnp.einsum('td,tl->dl', grad_mix, mixed, preferred_eleme...  562 us
    all_gather x1, waiting for transfers between devices, on_device(): lax.all_gather(up_proj, ('seq', 'fsdp'), axis=0, tiled=True)  209 us
    all_gather x1, waiting for transfers between devices, on_device(): lax.all_gather(gate_proj, ('seq', 'fsdp'), axis=0, tiled=True)  203 us
    all_gather x1, waiting for transfers between devices, on_device(): lax.all_gather(down_proj, ('seq', 'fsdp'), axis=0, tiled=True)  203 us
    concatenate x1, other arithmetic, on_device(): jnp.concatenate([term_gate, term_up, term_down], axis=1)  154 us
  transfers between devices with their start and end apart: 17, of which 13 were waited for; matrix products, arithmetic and copies ran while one was open for 11% of the time, Pallas kernels for 0%

commit v1 on v0

v1 whole, which is shorter than its diff:
```python
import functools

import jax
import jax.numpy as jnp
from jax import lax
from jax.experimental import pallas as pl
from jax.experimental.pallas import tpu as pltpu
from jax.sharding import PartitionSpec as P

epsilon = 1e-06
f32 = jnp.float32
bf16 = jnp.bfloat16
both = ("seq", "fsdp")
TAP, CONV_BIAS, RATE_BIAS, INPUT_BIAS, SOFT, SOFT_SLOPE = 0, 4, 5, 6, 7, 8
GELU_C = 0.7978845608028654
GELU_A = 0.044715


def from_behind(shard, axis, by):
    devices = lax.axis_size(axis)
    pairs = [(i, i + by) for i in range(devices) if 0 <= i + by < devices]
    return lax.ppermute(shard, axis, pairs)


def prefix(part, axis, reverse):
    count = lax.axis_size(axis)
    place = lax.axis_index(axis)
    gathered = lax.all_gather(jnp.stack(part), axis)
    state = jnp.zeros_like(part[1])
    for hop in range(count):
        source = count - 1 - hop if reverse else hop
        ahead = source > place if reverse else source < place
        state = jnp.where(ahead, gathered[source, 1] + gathered[source, 0] * state, state)
    return state


def norm_rows(values, scales):
    return values * lax.rsqrt(jnp.mean(values * values, axis=-1, keepdims=True) + epsilon) * scales


def gelu_parts(x):
    inner = jnp.tanh(GELU_C * (x + GELU_A * x * x * x))
    return 0.5 * x * (1.0 + inner), 0.5 * (1.0 + inner) + 0.5 * x * (1.0 - inner * inner) * (
        GELU_C * (1.0 + 3.0 * GELU_A * x * x)
    )


def mm(left, right, dims):
    return lax.dot_general(left, right, (dims, ((), ())), preferred_element_type=f32)


def sigmoid(x):
    return 1.0 / (1.0 + jnp.exp(-x))


def scan_rows(decay, value, reverse):
    rows = decay.shape[0]
    place = lax.broadcasted_iota(jnp.int32, decay.shape, 0)
    step = 1
    while step < rows:
        shift = rows - step if reverse else step
        inside = place < rows - step if reverse else place >= step
        before_value = jnp.where(inside, pltpu.roll(value, shift, 0), 0.0)
        before_decay = jnp.where(inside, pltpu.roll(decay, shift, 0), 1.0)
        value = value + decay * before_value
        decay = decay * before_decay
        step *= 2
    return decay, value


def gates(rate_pre, input_pre, soft):
    rate = sigmoid(rate_pre)
    log_decay = -8.0 * rate * soft
    decay = jnp.exp(log_decay)
    square = decay * decay
    root = jnp.sqrt(-jnp.tanh(log_decay) * (1.0 + square))
    return rate, decay, square, root, sigmoid(input_pre)


def mixer_forward(branch, prior, small, rate_w, input_w, conv, rate_pre, input_pre, cum, local, ext):
    rows = branch.shape[0]
    ext[0:8, :] = prior[...]
    ext[8:, :] = branch[...].astype(f32)
    total = small[CONV_BIAS : CONV_BIAS + 1, :] + small[TAP : TAP + 1, :] * ext[8:, :]
    for offset in range(1, 4):
        total = total + small[TAP + offset : TAP + offset + 1, :] * ext[pl.ds(8 - offset, rows), :]
    low = total.astype(bf16)
    conv[...] = low
    rate = mm(low, rate_w[...], ((1,), (0,))) + small[RATE_BIAS : RATE_BIAS + 1, :]
    inp = mm(low, input_w[...], ((1,), (0,))) + small[INPUT_BIAS : INPUT_BIAS + 1, :]
    rate_pre[...] = rate
    input_pre[...] = inp
    _, decay, _, root, opened = gates(rate, inp, small[SOFT : SOFT + 1, :])
    product, states = scan_rows(decay, root * opened * low.astype(f32), False)
    cum[...] = product
    local[...] = states


def mixer_backward_scan(grad_mixed, gelu_pre, rate_pre, cum, local, carried, small, grad_pre, rev_cum, rev_grad, pair, ext):
    rows = grad_mixed.shape[0]
    states = local[...] + cum[...] * carried[0:1, :]
    value, slope = gelu_parts(gelu_pre[...])
    grad = grad_mixed[...]
    grad_pre[...] = (grad * states * slope).astype(bf16)
    decay = jnp.exp(-8.0 * sigmoid(rate_pre[...]) * small[SOFT : SOFT + 1, :])
    ext[0:rows, :] = decay
    ext[rows:, :] = jnp.ones((8, decay.shape[1]), f32)
    product, back = scan_rows(ext[pl.ds(1, rows), :], grad * value, True)
    rev_cum[...] = product
    rev_grad[...] = back
    pair[...] = jnp.broadcast_to(decay[0:1, :] * back[0:1, :], pair.shape)


def mixer_backward(
    rev_cum, rev_grad, incoming, cum, local, carried, rate_pre, input_pre, conv, branch, prior, small, rate_w, input_w,
    own, head, rate_w_grad, input_w_grad, sums, ext, gext,
):
    rows = rev_cum.shape[0]
    soft = small[SOFT : SOFT + 1, :]
    grad_states = rev_grad[...] + rev_cum[...] * incoming[0:1, :]
    rate, decay, square, root, opened = gates(rate_pre[...], input_pre[...], soft)
    ext[0:8, :] = jnp.broadcast_to(carried[0:1, :], (8, carried.shape[1]))
    ext[8:, :] = local[...] + cum[...] * carried[0:1, :]
    before = ext[pl.ds(7, rows), :]
    low = conv[...]
    conv_in = low.astype(f32)
    grad_log = grad_states * decay * before - grad_states * opened * conv_in * square / root
    driven = grad_states * root
    grad_input = (driven * conv_in * opened * (1.0 - opened)).astype(bf16)
    by_rate = grad_log * (-8.0 * rate)
    grad_rate = (by_rate * soft * (1.0 - rate)).astype(bf16)
    sums[6:7, :] = jnp.sum(by_rate, axis=0, keepdims=True) * small[SOFT_SLOPE : SOFT_SLOPE + 1, :]
    sums[4:5, :] = jnp.sum(grad_rate.astype(f32), axis=0, keepdims=True)
    sums[5:6, :] = jnp.sum(grad_input.astype(f32), axis=0, keepdims=True)
    rate_w_grad[...] = mm(low, grad_rate, ((0,), (0,))).astype(rate_w_grad.dtype)
    input_w_grad[...] = mm(low, grad_input, ((0,), (0,))).astype(input_w_grad.dtype)
    grad_conv = (
        driven * opened
        + mm(grad_rate, rate_w[...], ((1,), (1,)))
        + mm(grad_input, input_w[...], ((1,), (1,)))
    )
    sums[7:8, :] = jnp.sum(grad_conv, axis=0, keepdims=True)
    ext[0:8, :] = prior[...]
    ext[8:, :] = branch[...].astype(f32)
    gext[0:8, :] = jnp.zeros((8, grad_conv.shape[1]), f32)
    gext[8 : 8 + rows, :] = grad_conv
    gext[8 + rows :, :] = jnp.zeros((8, grad_conv.shape[1]), f32)
    back = jnp.zeros_like(grad_conv)
    front = jnp.zeros((8, grad_conv.shape[1]), f32)
    for offset in range(4):
        tap = small[TAP + offset : TAP + offset + 1, :]
        sums[offset : offset + 1, :] = jnp.sum(
            grad_conv * ext[pl.ds(8 - offset, rows), :], axis=0, keepdims=True
        )
        back = back + tap * gext[pl.ds(8 + offset, rows), :]
        front = front + tap * gext[pl.ds(offset, 8), :]
    own[...] = back
    head[...] = front


def call_heads(kernel, width, heads, ins, outs, scratch, name):
    def spec(rows_cols):
        rows, by_row = rows_cols
        if by_row:
            return pl.BlockSpec((rows, width), lambda h: (h, 0))
        return pl.BlockSpec((rows, width), lambda h: (0, h))

    in_specs = [spec((width, True)) if rowwise else spec((a.shape[0], False)) for a, rowwise in ins]
    out_specs = [spec((width, True)) if rowwise else spec((rows, False)) for rows, _, rowwise in outs]
    out_shape = [
        jax.ShapeDtypeStruct((heads * width, width) if rowwise else (rows, heads * width), kind)
        for rows, kind, rowwise in outs
    ]
    return pl.pallas_call(
        kernel,
        grid=(heads,),
        in_specs=in_specs,
        out_specs=out_specs,
        out_shape=out_shape,
        scratch_shapes=[pltpu.VMEM((rows, width), f32) for rows in scratch],
        compiler_params=pltpu.CompilerParams(vmem_limit_bytes=40 * 1024 * 1024),
        name=name,
    )(*[a for a, _ in ins])


def on_device(
    block_input,
    cotangent,
    mixer_gain,
    branch_proj,
    gelu_proj,
    conv_taps,
    conv_bias,
    rate_blocks,
    input_blocks,
    rate_bias,
    input_bias,
    decay_param,
    out_proj,
    mlp_gain,
    gate_proj,
    up_proj,
    down_proj,
):
    groups = lax.axis_size("fsdp")
    part_rows, lru = branch_proj.shape
    width = rate_blocks.shape[1]
    heads = lru // width
    margin = conv_taps.shape[0] - 1
    tokens = block_input[0].astype(f32)
    tok_count, model = tokens.shape
    ff = gate_proj.shape[1]
    ff_part = ff // groups
    grad_out = cotangent[0]

    smalls = jnp.stack(
        [conv_taps[k] for k in range(margin + 1)]
        + [conv_bias, rate_bias, input_bias, decay_param, mixer_gain, mlp_gain],
        axis=1,
    )
    small_count = smalls.shape[1]
    smalls = jnp.pad(smalls, ((0, 0), (0, 128 - small_count)))
    first = lax.all_gather(
        jnp.concatenate([smalls, rate_blocks, input_blocks], axis=1), both, axis=0, tiled=True
    )
    wide = lax.all_gather(jnp.concatenate([branch_proj, gelu_proj], axis=1), both, axis=0, tiled=True)
    proj_out = lax.all_gather(out_proj, both, axis=0, tiled=True)

    def to_columns(weight):
        return jnp.transpose(weight.reshape(part_rows, groups, ff_part), (1, 0, 2))

    mlp_own = jnp.stack([to_columns(w) for w in (gate_proj, up_proj, down_proj)], axis=2)
    mlp_mine = lax.all_to_all(mlp_own, "fsdp", 0, 0, tiled=True)
    mlp_mine = mlp_mine.reshape(groups * part_rows, 3 * ff_part)
    mlp_w = lax.all_gather(mlp_mine, "seq", axis=0, tiled=True)
    grad_out_all = lax.all_gather(grad_out, "fsdp", axis=0, tiled=True)

    table = first[:, :small_count].astype(f32).T
    blocks_rate = first[:, 128 : 128 + width]
    blocks_input = first[:, 128 + width :]
    param_decay = table[margin + 4]
    gain_one = table[margin + 5]
    gain_two = table[margin + 6]
    small = jnp.concatenate(
        [
            table[: margin + 4],
            jax.nn.softplus(-param_decay)[None],
            -jax.nn.sigmoid(-param_decay)[None],
            jnp.zeros((16 - margin - 6, lru), f32),
        ],
        axis=0,
    )

    normed = norm_rows(tokens, gain_one).astype(bf16)
    both_pre = mm(normed, wide, ((1,), (0,)))
    branch = both_pre[:, :lru].astype(bf16)
    gelu_pre = both_pre[:, lru:]
    prior = from_behind(branch[tok_count - margin :], "seq", 1).astype(f32)
    prior = jnp.concatenate([jnp.zeros((8 - margin, lru), f32), prior], axis=0)
    conv, rate_pre, input_pre, cum, local = call_heads(
        mixer_forward,
        width,
        heads,
        [(branch, False), (prior, False), (small, False), (blocks_rate, True), (blocks_input, True)],
        [(tok_count, bf16, False)] + [(tok_count, f32, False)] * 4,
        [tok_count + 8],
        "mixer_forward",
    )
    carried = prefix((cum[-1], local[-1]), "seq", False)
    states = local + cum * carried[None]
    mixed = (states * jax.nn.gelu(gelu_pre, approximate=True)).astype(bf16)
    middle = tokens + mm(mixed, proj_out, ((1,), (1,)))
    normed_two = norm_rows(middle, gain_two).astype(bf16)

    normed_all = lax.all_gather(normed_two, "fsdp", axis=0, tiled=True)
    w_pair = mlp_w[:, : 2 * ff_part]
    w_down = mlp_w[:, 2 * ff_part :]
    pair = mm(normed_all, w_pair, ((1,), (0,)))
    gate = pair[:, :ff_part]
    up_val = pair[:, ff_part:]
    gelu_gate, gelu_slope = gelu_parts(gate)
    hidden = (gelu_gate * up_val).astype(bf16)
    grad_hidden = mm(grad_out_all, w_down, ((1,), (0,)))
    grad_gate = (grad_hidden * up_val * gelu_slope).astype(bf16)
    grad_up = (grad_hidden * gelu_gate).astype(bf16)
    grad_pair = jnp.concatenate([grad_gate, grad_up], axis=1)
    grad_normed_two = lax.psum_scatter(
        mm(grad_pair, w_pair, ((1,), (1,))).astype(bf16), "fsdp", scatter_dimension=0, tiled=True
    ).astype(f32)
    out_part = lax.psum_scatter(
        mm(hidden, w_down, ((1,), (1,))).astype(bf16), "fsdp", scatter_dimension=0, tiled=True
    )
    block_output = (middle + out_part.astype(f32)).astype(bf16)[None]
    term_pair = mm(normed_all, grad_pair, ((0,), (0,))).astype(bf16)
    term_down = mm(grad_out_all, hidden, ((0,), (0,))).astype(bf16)
    mlp_sum = lax.psum_scatter(
        jnp.concatenate([term_pair, term_down], axis=1), "seq", scatter_dimension=0, tiled=True
    )
    mlp_back = lax.all_to_all(
        mlp_sum.reshape(groups, part_rows, 3, ff_part), "fsdp", 0, 0, tiled=True
    )
    mlp_grads = [
        jnp.transpose(mlp_back[:, :, i], (1, 0, 2)).reshape(part_rows, ff).astype(f32) for i in range(3)
    ]

    second_pull = jax.vjp(norm_rows, middle, gain_two)[1]
    grad_mid_part, grad_gain_two = second_pull(grad_normed_two)
    grad_middle = grad_out.astype(f32) + grad_mid_part
    grad_mix = grad_middle.astype(bf16)
    grad_mixed = mm(grad_mix, proj_out, ((1,), (0,)))
    carried_rows = jnp.broadcast_to(carried[None], (8, lru))
    grad_gelu_pre, rev_cum, rev_grad, pair_grad = call_heads(
        mixer_backward_scan,
        width,
        heads,
        [(a, False) for a in (grad_mixed, gelu_pre, rate_pre, cum, local, carried_rows, small)],
        [(tok_count, bf16, False), (tok_count, f32, False), (tok_count, f32, False), (8, f32, False)],
        [tok_count + 8],
        "mixer_backward_scan",
    )
    incoming = prefix((cum[-1], pair_grad[0]), "seq", True)
    incoming_rows = jnp.broadcast_to(incoming[None], (8, lru))
    own, head, rate_w_grad, input_w_grad, sums = call_heads(
        mixer_backward,
        width,
        heads,
        [
            (a, False)
            for a in (rev_cum, rev_grad, incoming_rows, cum, local, carried_rows, rate_pre, input_pre, conv, branch, prior, small)
        ]
        + [(blocks_rate, True), (blocks_input, True)],
        [(tok_count, f32, False), (8, f32, False), (0, bf16, True), (0, bf16, True), (8, f32, False)],
        [tok_count + 8, tok_count + 16],
        "mixer_backward",
    )
    received = from_behind(head[8 - margin :], "seq", -1)
    grad_branch = jnp.concatenate(
        [own[: tok_count - margin], own[tok_count - margin :] + received], axis=0
    ).astype(bf16)
    grad_both = jnp.concatenate([grad_branch, grad_gelu_pre], axis=1)
    grad_normed = mm(grad_both, wide, ((1,), (1,)))
    first_pull = jax.vjp(norm_rows, tokens, gain_one)[1]
    grad_tok_part, grad_gain_one = first_pull(grad_normed)
    input_grad = (grad_middle + grad_tok_part).astype(bf16)[None]
    term_wide = mm(normed, grad_both, ((0,), (0,))).astype(bf16)
    term_out = mm(grad_mix, mixed, ((0,), (0,))).astype(bf16)
    vectors = jnp.concatenate([sums, grad_gain_one[None], grad_gain_two[None]], axis=0).T
    vectors = jnp.pad(vectors, ((0, 0), (0, 128 - vectors.shape[1]))).astype(bf16)
    mixer_sum = lax.psum_scatter(
        jnp.concatenate([term_wide, term_out, rate_w_grad, input_w_grad, vectors], axis=1),
        "seq",
        scatter_dimension=0,
        tiled=True,
    )
    mixer_sum = lax.psum_scatter(mixer_sum, "fsdp", scatter_dimension=0, tiled=True).astype(f32)
    edges = [lru, 2 * lru, 3 * lru, 3 * lru + width, 3 * lru + 2 * width]
    dbranch, dgelu, dout, drate, dinput, vec = jnp.split(mixer_sum, edges, axis=1)
    vec = vec.T
    return (
        block_output,
        input_grad,
        vec[8],
        dbranch,
        dgelu,
        vec[: margin + 1],
        vec[7],
        drate,
        dinput,
        vec[4],
        vec[5],
        vec[6],
        dout,
        vec[9],
        mlp_grads[0],
        mlp_grads[1],
        mlp_grads[2],
    )


def solution(mesh):
    tokens = P("fsdp", "seq", None)
    vector = P(both)
    matrix = P(both, None)
    taps = P(None, both)
    return jax.shard_map(
        on_device,
        mesh=mesh,
        in_specs=(
            tokens, tokens, vector, matrix, matrix, taps, vector, matrix, matrix,
            vector, vector, vector, matrix, vector, matrix, matrix, matrix,
        ),
        out_specs=(
            tokens, tokens, vector, matrix, matrix, taps, vector, matrix, matrix,
            vector, vector, vector, matrix, vector, matrix, matrix, matrix,
        ),
        check_vma=False,
    )
```

time: 5430 us -> 1660 us (0.31)
  waiting for transfers between devices: 4300 us -> 1140 us
  local copies, waits for them, and re-layouts: 308 us -> 58.8 us
  other arithmetic: 246 us -> 51 us
  matrix products: 362 us -> 183 us
    reduce_scatter x6 -> x4, waiting for transfers between devices: 3600 us -> 313 us  [the longest x1 183 us: on_device(): lax.psum_scatter(jnp.concatenate([term_pair, term_down], axis=1), 'seq',...]
    all_gather x8 -> x6, waiting for transfers between devices: 689 us -> 465 us  [the longest x1 153 us: on_device(): lax.all_gather(jnp.concatenate([branch_proj, gelu_proj], axis=1), both, a...]
    unnamed x16 -> x12, waiting for transfers between devices: 5.14 us -> 202 us
    dot_general x24 -> x12, matrix products: 362 us -> 183 us  [mm(): lax.dot_general(left, right, (dims, ((), ())), preferred_element_type=f32)]
    all_to_all x0 -> x1, waiting for transfers between devices: none -> 154 us  [on_device(): lax.all_to_all(mlp_sum.reshape(groups, part_rows, 3, ff_part), 'fsdp', 0,...]
    slice x107 -> x10, local copies, waits for them, and re-layouts: 156 us -> 5.42 us  [the longest x1 3.02 us: on_device(): blocks_input = first[:, 128 + width:]]
    all_to_all x0 -> x1, blocking collectives: none -> 144 us  [on_device(): mlp_mine = lax.all_to_all(mlp_own, 'fsdp', 0, 0, tiled=True)]
    concatenate x28 -> x5, other arithmetic: 164 us -> 27 us  [the longest x1 23.4 us: on_device(): jnp.concatenate([term_pair, term_down], axis=1)]
  transfers between devices with their start and end apart: 17 -> 14, of which waited for: 13 -> 12; matrix products, arithmetic and copies ran while one was open for 11% -> 10% of each run, Pallas kernels for 0% -> 0%
where the time goes in v1:
time: 1660 us; the launch traced here: 1650 us
  waiting for transfers between devices  1140 us (69%)
  matrix products  183 us (11%)
  blocking collectives  166 us (10%)
  local copies, waits for them, and re-layouts  58.8 us (4%)
  other arithmetic  51 us (3%)
  Pallas kernels  31.3 us (2%)
    unnamed x12, waiting for transfers between devices  202 us
    reduce_scatter x1, waiting for transfers between devices, on_device(): lax.psum_scatter(jnp.concatenate([term_pair, term_down], axis=1), 'seq',...  183 us
    dot_general x12, matrix products, mm(): lax.dot_general(left, right, (dims, ((), ())), preferred_element_type=f32)  183 us
    all_to_all x1, waiting for transfers between devices, on_device(): lax.all_to_all(mlp_sum.reshape(groups, part_rows, 3, ff_part), 'fsdp', 0,...  154 us
    all_gather x1, waiting for transfers between devices, on_device(): lax.all_gather(jnp.concatenate([branch_proj, gelu_proj], axis=1), both, a...  153 us
    all_to_all x1, blocking collectives, on_device(): mlp_mine = lax.all_to_all(mlp_own, 'fsdp', 0, 0, tiled=True)  144 us
    all_gather x1, waiting for transfers between devices, on_device(): mlp_w = lax.all_gather(mlp_mine, 'seq', axis=0, tiled=True)  142 us
    reduce_scatter x1, waiting for transfers between devices, on_device(): lax.psum_scatter(mm(hidden, w_down, ((1,), (1,))).astype(bf16), 'fsdp', s...  71.5 us
  transfers between devices with their start and end apart: 14, of which 12 were waited for; matrix products, arithmetic and copies ran while one was open for 10% of the time, Pallas kernels for 0%

profile of v1, /device:TPU:0, one launch (start us, length us, event | category | flops | bytes accessed | tf_op | source)
XLA Modules:
  0.0 1651.4 jit_solution(10507401412220482833)
XLA Ops:
  11.2 2.1 pad_maximum_fusion.6
  17.6 55.9 %all-gather.12.cloned.1.call-done = bf16[2560,640]{1,0:T(8,128)(2,1)} async-done(((bf16[80,640]{1,0:T(8,128)(2,1)}), bf16[2560,640]{1,0:T(8,128)(2,1)}) %all-gather.12.cloned.1.call-update) | async-done | bytes 3276816 | tf_op jit(solution)/shard_map/all_gather | solution.py:223
  74.7 2.2 slice_reduce_fusion
  76.9 1.7 copy.146
  79.5 3.0 fusion.75
  82.5 153.0 %all-gather.14.cloned.1.call-done = bf16[2560,5120]{1,0:T(8,128)(2,1)} async-done(((bf16[80,5120]{1,0:T(8,128)(2,1)}), bf16[2560,5120]{1,0:T(8,128)(2,1)}) %all-gather.14.cloned.1.call-update) | async-done | bytes 26214416 | tf_op jit(solution)/shard_map/all_gather | solution.py:226
  235.5 11.2 fusion.78
  246.8 2.3 collective-permute-start
  249.9 7.2 mixer_forward.1
  261.4 12.9 all-gather.3
  274.7 2.3 fusion.74
  277.1 58.8 %all-gather.16.cloned.1.call-done = bf16[2560,2560]{1,0:T(8,128)(2,1)} async-done(((bf16[80,2560]{1,0:T(8,128)(2,1)}), bf16[2560,2560]{1,0:T(8,128)(2,1)}) %all-gather.16.cloned.1.call-update) | async-done | bytes 13107216 | tf_op jit(solution)/shard_map/all_gather | solution.py:227
  335.9 9.6 multiply_reduce_fusion
  348.2 3.4 copy_bitcast_fusion
  351.6 2.4 reshape.297
  357.0 144.0 %all_to_all.10 = bf16[4,80,3,1920]{3,1,2,0:T(8,128)(2,1)S(1)} all-to-all(bf16[4,80,3,1920]{3,1,2,0:T(8,128)(2,1)S(1)} %copy.150), channel_id=1, replica_groups=mesh['seq'=8,'fsdp'=4] {'fsdp'}, dimensions={0} | all-to-all | bytes 7372800 | tf_op jit(solution)/shard_map/all_to_all | solution.py:233
  501.0 1.9 copy.151
  502.9 2.4 copy.168
  506.0 141.5 %all-gather.20.cloned.1.call-done = bf16[2560,5760]{1,0:T(8,128)(2,1)} async-done(((bf16[320,5760]{1,0:T(8,128)(2,1)}), bf16[2560,5760]{1,0:T(8,128)(2,1)}) %all-gather.20.cloned.1.call-update) | async-done | bytes 29491216 | tf_op jit(solution)/shard_map/all_gather | solution.py:235
  647.5 21.7 %fusion.3 = f32[768,3840]{1,0:T(8,128)} fusion(bf16[768,2560]{1,0:T(8,128)(2,1)} %all-gather.18.cloned.1.call-done, bf16[2560,5760]{1,0:T(8,128)(2,1)} %all-gather.20.cloned.1.call-done), kind=kOutput, calls=%fused_computation.6 | convolution fusion | flops 15099494400 | bytes 35389440 | tf_op jit(solution)/shard_map/dot_general | solution.py:49
  669.2 56.2 %all-gather.22.cloned.1.call-done = bf16[1,768,2560]{2,1,0:T(8,128)(2,1)} async-done(((bf16[1,192,2560]{2,1,0:T(8,128)(2,1)}), bf16[1,768,2560]{2,1,0:T(8,128)(2,1)}) %all-gather.22.cloned.1.call-update) | async-done | bytes 3932176 | tf_op jit(solution)/shard_map/all_gather | solution.py:236
  725.4 20.5 %fusion.18 = (bf16[768,1920]{1,0:T(8,128)(2,1)}, bf16[768,1920]{1,0:T(8,128)(2,1)}, bf16[768,1920]{1,0:T(8,128)(2,1)}) fusion(f32[768,3840]{1,0:T(8,128)} %fusion.3, bf16[2560,5760]{1,0:T(8,128)(2,1)} %all-gather.20.cloned.1.call-done, bf16[1,768,2560]{2,1,0:T(8,128)(2,1)} %all-gather.22.cloned.1.call-done), kind=kOutput, calls=%fused_computation.25 | convolution fusion | flops 7586611200 | bytes 34406400 | tf_op jit(solution)/shard_map/dot_general | solution.py:49
  745.9 22.9 %fusion.20 = bf16[768,2560]{1,0:T(8,128)(2,1)} fusion(bf16[2560,5760]{1,0:T(8,128)(2,1)} %all-gather.20.cloned.1.call-done, bf16[768,1920]{1,0:T(8,128)(2,1)} %get-tuple-element.190, bf16[768,1920]{1,0:T(8,128)(2,1)} %get-tuple-element.189), kind=kOutput, calls=%fused_computation.32 | convolution fusion | flops 15113256960 | bytes 29491200 | tf_op jit(solution)/shard_map/dot_general | solution.py:49
  768.9 13.2 fusion.23
  782.2 58.0 %reduce-scatter.10.cloned.1.call-done = bf16[192,2560]{1,0:T(8,128)(2,1)} async-done(((bf16[768,2560]{1,0:T(8,128)(2,1)}), bf16[192,2560]{1,0:T(8,128)(2,1)}) %reduce-scatter.10.cloned.1.call-update) | async-done | bytes 983056 | tf_op jit(solution)/shard_map/reduce_scatter | solution.py:287
  840.2 2.6 fusion.35
  844.1 71.5 %reduce-scatter.8.cloned.1.call-done = bf16[192,2560]{1,0:T(8,128)(2,1)} async-done(((bf16[768,2560]{1,0:T(8,128)(2,1)}), bf16[192,2560]{1,0:T(8,128)(2,1)}) %reduce-scatter.8.cloned.1.call-update) | async-done | bytes 983056 | tf_op jit(solution)/shard_map/reduce_scatter | solution.py:290
  915.6 4.1 fusion.45
  919.7 7.0 fusion.54.grad_mixed
  926.8 12.8 mixer_backward_scan.1
  939.7 9.4 all-gather.4
  949.6 11.2 mixer_backward.1
  965.0 14.1 fusion
  979.2 8.3 fusion.5
  987.5 15.7 fusion.33
  1009.0 13.9 fusion.6
  1022.8 24.9 %convolution_convert_fusion.1 = bf16[2560,3840]{1,0:T(8,128)(2,1)} fusion(bf16[768,2560]{1,0:T(8,128)(2,1)} %all-gather.18.cloned.1.call-done, bf16[768,1920]{1,0:T(8,128)(2,1)} %get-tuple-element.190, bf16[768,1920]{1,0:T(8,128)(2,1)} %get-tuple-element.189), kind=kOutput, calls=%fused_computation.3 | convolution fusion | flops 15121121280 | bytes 29491200 | tf_op jit(solution)/shard_map/dot_general | solution.py:49
  1047.7 23.4 %pad_maximum_fusion = bf16[2560,5760]{1,0:T(8,128)(2,1)} fusion(bf16[2560,1920]{1,0:T(8,128)(2,1)} %fusion.6, bf16[2560,3840]{1,0:T(8,128)(2,1)} %convolution_convert_fusion.1), kind=kLoop, calls=%fused_computation | loop fusion | flops 58982400 | bytes 58982400 | tf_op jit(solution)/shard_map/concatenate | solution.py:297
  1071.2 200.8 %reduce-scatter.16.cloned.1.call-done = bf16[320,8320]{1,0:T(8,128)(2,1)} async-done(((bf16[2560,8320]{1,0:T(8,128)(2,1)}), bf16[320,8320]{1,0:T(8,128)(2,1)}) %reduce-scatter.16.cloned.1.call-update) | async-done | bytes 5324816
  1272.0 183.4 %reduce-scatter.14.cloned.1.call-done = bf16[320,5760]{1,0:T(8,128)(2,1)} async-done(((bf16[2560,5760]{1,0:T(8,128)(2,1)}), bf16[320,5760]{1,0:T(8,128)(2,1)}) %reduce-scatter.14.cloned.1.call-update) | async-done | bytes 3686416 | tf_op jit(solution)/shard_map/reduce_scatter | solution.py:296
  1455.5 7.8 reshape.303
  1463.3 5.4 copy.156
  1468.7 5.3 all-to-all-start.1
  1474.1 3.2 fusion.51
  1477.3 154.3 %all-to-all-done.1 = bf16[4,80,3,1920]{3,1,2,0:T(8,128)(2,1)} async-done(((bf16[4,80,3,1920]{3,1,2,0:T(8,128)(2,1)}), bf16[4,80,3,1920]{3,1,2,0:T(8,128)(2,1)}, u32[]{:S(2)}, u32[]{:S(2)}) %all-to-all-start.1) | async-done | bytes 3686432 | tf_op jit(solution)/shard_map/all_to_all | solution.py:299
  1631.6 2.5 convert_bitcast_fusion
  1634.2 1.7 copy.165
  1635.8 1.7 copy.166
  (156 shorter events, 40.9 us)
Async XLA Ops:
  7.2 6.9 copy-start.24
  7.2 8.2 copy-start.25
  7.2 66.3 %all-gather.12.cloned.1.call-start = ((), (), s32[]{:S(2)}) async-start(), calls=%async_computation.7 | async-start | bytes 3379200 | tf_op jit(solution)/shard_map/all_gather | solution.py:223
  11.2 224.3 %all-gather.14.cloned.1.call-start = ((), (), s32[]{:S(2)}) async-start(), calls=%async_computation.8 | async-start | bytes 27033600 | tf_op jit(solution)/shard_map/all_gather | solution.py:226
  13.3 3.4 copy-start.21
  13.3 322.6 %all-gather.16.cloned.1.call-start = ((), (), s32[]{:S(2)}) async-start(), calls=%async_computation.9 | async-start | bytes 13516800 | tf_op jit(solution)/shard_map/all_gather | solution.py:227
  14.1 491.9 %all-gather.18.cloned.1.call-start = ((), (), s32[]{:S(2)}) async-start(), calls=%async_computation.10 | async-start | bytes 4915200 | tf_op jit(solution)/shard_map/all_gather | solution.py:275
  17.6 217.9 %copy-start.34 = (f32[192]{0:T(256)}, f32[192]{0:T(256)S(1)}, u32[]{:S(2)}) copy-start(f32[192]{0:T(256)S(1)} %fusion.68) | copy-start | bytes 2308
  76.9 158.6 %copy-start.29 = (f32[2560]{0:T(1024)}, f32[2560]{0:T(1024)S(1)}, u32[]{:S(2)}) copy-start(f32[2560]{0:T(1024)S(1)} %get-tuple-element.152) | copy-start | bytes 30724
  79.5 156.0 %copy-start.22 = (bf16[1,192,2560]{2,1,0:T(8,128)(2,1)S(1)}, bf16[1,192,2560]{2,1,0:T(8,128)(2,1)}, u32[]{:S(2)}) copy-start(bf16[1,192,2560]{2,1,0:T(8,128)(2,1)} %param.17) | copy-start | bytes 2949124
  246.7 3.2 copy-start.2
  246.8 3.1 collective-permute-start
  249.2 7.9 copy-start.4
  257.2 1.3 copy-start.6
  258.5 1.3 copy-start.9
  259.8 0.9 copy-start.12
  260.7 14.0 copy-start.1
  260.7 666.0 %copy-start = (f32[192,2560]{1,0:T(8,128)}, f32[192,2560]{1,0:T(8,128)S(1)}, u32[]{:S(2)}) copy-start(f32[192,2560]{1,0:T(8,128)S(1)} %get-tuple-element.32.cum) | copy-start | bytes 5898244
  345.5 1.3 copy-start.15
  348.0 299.5 %all-gather.20.cloned.1.call-start = ((), (), s32[]{:S(2)}) async-start(), calls=%async_computation.11 | async-start | bytes 33177600 | tf_op jit(solution)/shard_map/all_gather | solution.py:235
  354.0 1.8 copy-start.19
  354.0 2.2 copy-start.20
  505.3 220.1 %all-gather.22.cloned.1.call-start = ((), (), s32[]{:S(2)}) async-start(), calls=%async_computation.16 | async-start | bytes 4915200 | tf_op jit(solution)/shard_map/all_gather | solution.py:236
  505.9 334.4 %reduce-scatter.10.cloned.1.call-start = ((), (), s32[]{:S(2)}) async-start(), calls=%async_computation.13 | async-start | bytes 4915200 | tf_op jit(solution)/shard_map/reduce_scatter | solution.py:287
  768.8 146.8 %reduce-scatter.8.cloned.1.call-start = ((), (), s32[]{:S(2)}) async-start(), calls=%async_computation.12 | async-start | bytes 4915200 | tf_op jit(solution)/shard_map/reduce_scatter | solution.py:290
  782.1 489.9 %reduce-scatter.16.cloned.1.call-start = ((), (), s32[]{:S(2)}) async-start(), calls=%async_computation.17 | async-start | bytes 47923200
  919.7 7.0 copy-start.17
  919.7 7.0 copy-start.7
  919.7 7.0 copy-start.8
  926.7 12.9 copy-start.28
  926.7 22.8 %copy-start.3 = (bf16[2560,256]{1,0:T(8,128)(2,1)S(1)}, bf16[2560,256]{1,0:T(8,128)(2,1)}, u32[]{:S(2)}) copy-start(bf16[2560,256]{1,0:T(8,128)(2,1)} %get-tuple-element.198.rate_w) | copy-start | bytes 3932164
  926.7 22.8 %copy-start.5 = (bf16[192,2560]{1,0:T(8,128)(2,1)S(1)}, bf16[192,2560]{1,0:T(8,128)(2,1)}, u32[]{:S(2)}) copy-start(bf16[192,2560]{1,0:T(8,128)(2,1)} %copy-done.4) | copy-start | bytes 2949124
  926.8 22.8 %copy-start.13 = (bf16[192,2560]{1,0:T(8,128)(2,1)S(1)}, bf16[192,2560]{1,0:T(8,128)(2,1)}, u32[]{:S(2)}) copy-start(bf16[192,2560]{1,0:T(8,128)(2,1)} %copy-done.12) | copy-start | bytes 2949124
  939.6 21.2 %copy-start.14 = (bf16[192,2560]{1,0:T(8,128)(2,1)}, bf16[192,2560]{1,0:T(8,128)(2,1)S(1)}, u32[]{:S(2)}) copy-start(bf16[192,2560]{1,0:T(8,128)(2,1)S(1)} %get-tuple-element.41) | copy-start | bytes 2949124
  949.5 15.5 copy-start.30
  949.6 15.5 copy-start.35
  960.8 1.1 copy-start.10
  961.9 3.1 collective-permute-start.1
  965.0 14.1 copy-start.26
  987.5 16.1 copy-start.11
  1007.1 1.8 copy-start.37
  1007.2 448.3 %reduce-scatter.14.cloned.1.call-start = ((), (), s32[]{:S(2)}) async-start(), calls=%async_computation.15 | async-start | bytes 33177600 | tf_op jit(solution)/shard_map/reduce_scatter | solution.py:296
  1071.2 568.0 %reduce-scatter.12.cloned.1.call-start = ((), (), s32[]{:S(2)}) async-start(), calls=%async_computation.14 | async-start | bytes 6656000 | tf_op jit(solution)/shard_map/reduce_scatter | solution.py:355
  1468.7 5.3 copy-start.33
  1468.7 5.3 copy-start.18
  1468.7 5.4 copy-start.23
  1468.7 162.9 %all-to-all-start.1 = ((bf16[4,80,3,1920]{3,1,2,0:T(8,128)(2,1)}), bf16[4,80,3,1920]{3,1,2,0:T(8,128)(2,1)}, u32[]{:S(2)}, u32[]{:S(2)}) async-start(bf16[4,80,3,1920]{3,1,2,0:T(8,128)(2,1)} %copy.156), calls=%async_computation.5 | async-start | bytes 7372800 | tf_op jit(solution)/shard_map/all_to_all | solution.py:299
  1639.2 3.1 copy-start.16
  (4 other events, 2.5 us)
Sparse Core Ops, SparseCore 0:
  11.4 62.0 all-gather.11
  76.9 158.5 all-gather.13
  238.3 97.5 all-gather.15
  348.1 143.2 all-gather.17
  505.4 142.0 all-gather.19
  648.9 76.4 all-gather.21
  769.0 71.2 reduce-scatter.9
  842.5 73.0 reduce-scatter.7
  1007.3 264.6 reduce-scatter.15
  1275.9 179.5 reduce-scatter.13
  1457.9 153.1 reduce-scatter.11

commit v2 on v1

--- a/solution.py
+++ b/solution.py
@@ -11,6 +11,7 @@
 f32 = jnp.float32
 bf16 = jnp.bfloat16
 both = ("seq", "fsdp")
+MESH = pl.DeviceIdType.MESH
 TAP, CONV_BIAS, RATE_BIAS, INPUT_BIAS, SOFT, SOFT_SLOPE = 0, 4, 5, 6, 7, 8
 GELU_C = 0.7978845608028654
 GELU_A = 0.044715
@@ -156,6 +157,257 @@
         front = front + tap * gext[pl.ds(offset, 8), :]
     own[...] = back
     head[...] = front
+
+
+def places():
+    s = lax.axis_index("seq")
+    z = lax.axis_index("fsdp")
+    core = s + 1 - 2 * (s % 2)
+    beside = s + 2 - 4 * ((s // 2) % 2)
+    across = s + 4 - 8 * (s // 4)
+    return s, z, core, beside, across
+
+
+def greet(peers):
+    barrier = pltpu.get_barrier_semaphore()
+    for peer in peers:
+        pl.semaphore_signal(barrier, inc=1, device_id=peer, device_id_type=MESH)
+    pl.semaphore_wait(barrier, len(peers))
+
+
+def gather_kernel(
+    mixer, gate, up, down, grad, mixer_all, mlp_all, grad_all,
+    flow_send, flow_recv, line_send, line_recv, swap_send, swap_recv, own_sem,
+):
+    s, z, core, beside, across = places()
+    rows = mixer.shape[0]
+    mixer_cols = mixer.shape[1]
+    ff_part = mlp_all.shape[2]
+    tok = grad.shape[0]
+    mixer_cut = mixer_cols // 256 * 128
+    mlp_cut = ff_part // 256 * 128
+    diag = beside + across - s
+    greet([(core, z), (beside, z), (across, z)] + [(s, (z + k) % 4) for k in range(1, 4)])
+
+    def remote(src, dst, send, recv, target):
+        return pltpu.make_async_remote_copy(
+            src_ref=src, dst_ref=dst, send_sem=send, recv_sem=recv, device_id=target, device_id_type=MESH
+        )
+
+    def span(seq, zz):
+        return pl.ds(pl.multiple_of((seq * 4 + zz) * rows, 16), rows)
+
+    def piece(kind, seq, zz, half=None):
+        if kind == 0:
+            if half is None:
+                return mixer_all.at[span(seq, zz), :]
+            cols = pl.ds(0, mixer_cut) if half == 0 else pl.ds(mixer_cut, mixer_cols - mixer_cut)
+            return mixer_all.at[span(seq, zz), cols]
+        if half is None:
+            return mlp_all.at[:, span(seq, zz), :]
+        cols = pl.ds(0, mlp_cut) if half == 0 else pl.ds(mlp_cut, ff_part - mlp_cut)
+        return mlp_all.at[:, span(seq, zz), cols]
+
+    def flow(kind, zz, index, seq, half, target, src=None):
+        ref = piece(kind, seq, zz, half)
+        return remote(
+            ref if src is None else src, ref, flow_send.at[kind, zz, index], flow_recv.at[kind, zz, index], (target, z)
+        )
+
+    def sends(kind, zz, src=None):
+        return [
+            flow(kind, zz, 0, s, None, beside, src),
+            flow(kind, zz, 1, s, None, across, src),
+            flow(kind, zz, 4, s, None, core, src),
+        ]
+
+    def spread(kind, zz, src=None):
+        for copy in sends(kind, zz, src):
+            copy.start()
+
+    def relay(kind, zz):
+        flow(kind, zz, 0, beside, None, beside).wait_recv()
+        flow(kind, zz, 3, beside, 0, across).start()
+        flow(kind, zz, 5, beside, None, core).start()
+        flow(kind, zz, 1, across, None, across).wait_recv()
+        flow(kind, zz, 2, across, 1, beside).start()
+        flow(kind, zz, 6, across, None, core).start()
+
+    def finish(kind, zz):
+        flow(kind, zz, 3, diag, 0, across).wait_recv()
+        flow(kind, zz, 7, diag, 0, core).start()
+        flow(kind, zz, 2, diag, 1, beside).wait_recv()
+        flow(kind, zz, 8, diag, 1, core).start()
+
+    def drain(kind, zz, src=None):
+        other = core
+        for copy in sends(kind, zz, src):
+            copy.wait_send()
+        flow(kind, zz, 3, beside, 0, across).wait_send()
+        flow(kind, zz, 5, beside, None, core).wait_send()
+        flow(kind, zz, 2, across, 1, beside).wait_send()
+        flow(kind, zz, 6, across, None, core).wait_send()
+        flow(kind, zz, 7, diag, 0, core).wait_send()
+        flow(kind, zz, 8, diag, 1, core).wait_send()
+        flip = core - s
+        flow(kind, zz, 4, other, None, core).wait_recv()
+        flow(kind, zz, 5, beside + flip, None, core).wait_recv()
+        flow(kind, zz, 6, across + flip, None, core).wait_recv()
+        flow(kind, zz, 7, diag + flip, 0, core).wait_recv()
+        flow(kind, zz, 8, diag + flip, 1, core).wait_recv()
+
+    def line(kind, zz, up_way, hop, src=None):
+        if kind == 0:
+            ref = mixer_all.at[span(s, zz), :]
+        else:
+            ref = grad_all.at[pl.ds(pl.multiple_of(zz * tok, 16), tok), :]
+        way = 0 if up_way else 1
+        target = z + 1 if up_way else z - 1
+        return remote(
+            ref if src is None else src, ref, line_send.at[kind, way, hop], line_recv.at[kind, way, hop], (s, target)
+        )
+
+    def line_start(kind, src):
+        pl.when(z < 3)(lambda: line(kind, z, True, 0, src).start())
+        pl.when(z > 0)(lambda: line(kind, z, False, 0, src).start())
+
+    def line_hop(kind, hop):
+        def below():
+            line(kind, z - hop, True, hop - 1).wait_recv()
+
+            @pl.when(z < 3)
+            def _():
+                line(kind, z - hop, True, hop).start()
+
+        def above():
+            line(kind, z + hop, False, hop - 1).wait_recv()
+
+            @pl.when(z > 0)
+            def _():
+                line(kind, z + hop, False, hop).start()
+
+        pl.when(z >= hop)(below)
+        pl.when(z + hop <= 3)(above)
+
+    def line_drain(kind, src):
+        pl.when(z < 3)(lambda: line(kind, z, True, 0, src).wait_send())
+        pl.when(z > 0)(lambda: line(kind, z, False, 0, src).wait_send())
+        for hop in range(1, 3):
+            pl.when((z >= hop) & (z < 3))(lambda: line(kind, z - hop, True, hop).wait_send())
+            pl.when((z + hop <= 3) & (z > 0))(lambda: line(kind, z + hop, False, hop).wait_send())
+
+    def at_hop(hop, act):
+        pl.when(z >= hop)(lambda: act(z - hop))
+        pl.when(z + hop <= 3)(lambda: act(z + hop))
+
+    def swap(k, m, arriving=False):
+        weight = (gate, up, down)[m]
+        to = (z + k) % 4
+        came = (z + 4 - k) % 4
+        cols = pl.ds(pl.multiple_of(to * ff_part, 128), ff_part)
+        dst = mlp_all.at[m, span(s, came if arriving else z), :]
+        return remote(weight.at[:, cols], dst, swap_send.at[k - 1, m], swap_recv.at[k - 1, m], (s, to))
+
+    own_cols = pl.ds(pl.multiple_of(z * ff_part, 128), ff_part)
+    local = [
+        pltpu.make_async_copy(weight.at[:, own_cols], mlp_all.at[m, span(s, z), :], own_sem.at[m])
+        for m, weight in enumerate((gate, up, down))
+    ]
+    local.append(pltpu.make_async_copy(mixer, mixer_all.at[span(s, z), :], own_sem.at[3]))
+    local.append(
+        pltpu.make_async_copy(grad, grad_all.at[pl.ds(pl.multiple_of(z * tok, 16), tok), :], own_sem.at[4])
+    )
+
+    line_start(0, mixer)
+    spread(0, z, mixer)
+    for copy in local:
+        copy.start()
+    line_hop(0, 1)
+    at_hop(1, lambda zz: spread(0, zz))
+    relay(0, z)
+    line_hop(0, 2)
+    at_hop(2, lambda zz: spread(0, zz))
+    finish(0, z)
+    at_hop(1, lambda zz: relay(0, zz))
+    line_hop(0, 3)
+    at_hop(3, lambda zz: spread(0, zz))
+    for k in (1, 3, 2):
+        for m in range(3):
+            swap(k, m).start()
+    for copy in local:
+        copy.wait()
+    spread(1, z)
+    at_hop(1, lambda zz: finish(0, zz))
+    at_hop(2, lambda zz: relay(0, zz))
+    at_hop(3, lambda zz: relay(0, zz))
+    relay(1, z)
+    at_hop(2, lambda zz: finish(0, zz))
+    at_hop(3, lambda zz: finish(0, zz))
+    for k in (1, 3, 2):
+        for m in range(3):
+            swap(k, m, True).wait_recv()
+        spread(1, (z + 4 - k) % 4)
+    line_start(1, grad)
+    finish(1, z)
+    line_hop(1, 1)
+    relay(1, (z + 3) % 4)
+    line_hop(1, 2)
+    relay(1, (z + 1) % 4)
+    finish(1, (z + 3) % 4)
+    line_hop(1, 3)
+    relay(1, (z + 2) % 4)
+    finish(1, (z + 1) % 4)
+    finish(1, (z + 2) % 4)
+    drain(0, z, mixer)
+    for hop in range(1, 4):
+        at_hop(hop, lambda zz: drain(0, zz))
+    drain(1, z)
+    for k in (1, 3, 2):
+        drain(1, (z + 4 - k) % 4)
+        for m in range(3):
+            swap(k, m).wait_send()
+    line_drain(0, mixer)
+    line_drain(1, grad)
+
+
+def gather(mixer, gate, up, down, grad):
+    rows, cols = mixer.shape
+    tok, model = grad.shape
+    ff_part = gate.shape[1] // 4
+    anyspec = pl.BlockSpec(memory_space=pl.ANY)
+    dma = pltpu.SemaphoreType.DMA
+    return pl.pallas_call(
+        gather_kernel,
+        in_specs=[anyspec] * 5,
+        out_specs=[anyspec] * 3,
+        out_shape=[
+            jax.ShapeDtypeStruct((32 * rows, cols), bf16),
+            jax.ShapeDtypeStruct((3, 32 * rows, ff_part), bf16),
+            jax.ShapeDtypeStruct((4 * tok, model), bf16),
+        ],
+        scratch_shapes=[
+            dma((2, 4, 9)), dma((2, 4, 9)), dma((2, 2, 3)), dma((2, 2, 3)), dma((3, 3)), dma((3, 3)), dma((5,)),
+        ],
+        compiler_params=pltpu.CompilerParams(collective_id=1, has_side_effects=True),
+        name="gather_weights",
+    )(mixer, gate, up, down, grad)
+
+
+def gather_plain(mixer, gate, up, down, grad):
+    groups = lax.axis_size("fsdp")
+    part_rows, ff = gate.shape
+
+    def columns(weight):
+        return jnp.transpose(weight.reshape(part_rows, groups, ff // groups), (1, 0, 2))
+
+    own = jnp.stack([columns(w) for w in (gate, up, down)], axis=1)
+    mine = lax.all_to_all(own, "fsdp", 0, 0, tiled=True)
+    mine = jnp.transpose(mine, (1, 0, 2, 3)).reshape(3, groups * part_rows, ff // groups)
+    return (
+        lax.all_gather(mixer, both, axis=0, tiled=True),
+        lax.all_gather(mine, "seq", axis=1, tiled=True),
+        lax.all_gather(grad, "fsdp", axis=0, tiled=True),
+    )
 
 
 def call_heads(kernel, width, heads, ins, outs, scratch, name):
@@ -220,20 +472,16 @@
     )
     small_count = smalls.shape[1]
     smalls = jnp.pad(smalls, ((0, 0), (0, 128 - small_count)))
-    first = lax.all_gather(
-        jnp.concatenate([smalls, rate_blocks, input_blocks], axis=1), both, axis=0, tiled=True
-    )
-    wide = lax.all_gather(jnp.concatenate([branch_proj, gelu_proj], axis=1), both, axis=0, tiled=True)
-    proj_out = lax.all_gather(out_proj, both, axis=0, tiled=True)
-
-    def to_columns(weight):
-        return jnp.transpose(weight.reshape(part_rows, groups, ff_part), (1, 0, 2))
-
-    mlp_own = jnp.stack([to_columns(w) for w in (gate_proj, up_proj, down_proj)], axis=2)
-    mlp_mine = lax.all_to_all(mlp_own, "fsdp", 0, 0, tiled=True)
-    mlp_mine = mlp_mine.reshape(groups * part_rows, 3 * ff_part)
-    mlp_w = lax.all_gather(mlp_mine, "seq", axis=0, tiled=True)
-    grad_out_all = lax.all_gather(grad_out, "fsdp", axis=0, tiled=True)
+    mixer_own = jnp.concatenate(
+        [smalls, rate_blocks, input_blocks, branch_proj, gelu_proj, out_proj], axis=1
+    )
+    if lax.axis_size("seq") == 8 and groups == 4:
+        mixer_w, mlp_w, grad_out_all = gather(mixer_own, gate_proj, up_proj, down_proj, grad_out)
+    else:
+        mixer_w, mlp_w, grad_out_all = gather_plain(mixer_own, gate_proj, up_proj, down_proj, grad_out)
+    first = mixer_w[:, : 128 + 2 * width]
+    wide = mixer_w[:, 128 + 2 * width : 128 + 2 * width + 2 * lru]
+    proj_out = mixer_w[:, 128 + 2 * width + 2 * lru :]
 
     table = first[:, :small_count].astype(f32).T
     blocks_rate = first[:, 128 : 128 + width]
@@ -273,19 +521,18 @@
     normed_two = norm_rows(middle, gain_two).astype(bf16)
 
     normed_all = lax.all_gather(normed_two, "fsdp", axis=0, tiled=True)
-    w_pair = mlp_w[:, : 2 * ff_part]
-    w_down = mlp_w[:, 2 * ff_part :]
-    pair = mm(normed_all, w_pair, ((1,), (0,)))
-    gate = pair[:, :ff_part]
-    up_val = pair[:, ff_part:]
+    w_gate, w_up, w_down = mlp_w[0], mlp_w[1], mlp_w[2]
+    gate = mm(normed_all, w_gate, ((1,), (0,)))
+    up_val = mm(normed_all, w_up, ((1,), (0,)))
     gelu_gate, gelu_slope = gelu_parts(gate)
     hidden = (gelu_gate * up_val).astype(bf16)
     grad_hidden = mm(grad_out_all, w_down, ((1,), (0,)))
     grad_gate = (grad_hidden * up_val * gelu_slope).astype(bf16)
     grad_up = (grad_hidden * gelu_gate).astype(bf16)
     grad_pair = jnp.concatenate([grad_gate, grad_up], axis=1)
+    grad_normed_part = mm(grad_gate, w_gate, ((1,), (1,))) + mm(grad_up, w_up, ((1,), (1,)))
     grad_normed_two = lax.psum_scatter(
-        mm(grad_pair, w_pair, ((1,), (1,))).astype(bf16), "fsdp", scatter_dimension=0, tiled=True
+        grad_normed_part.astype(bf16), "fsdp", scatter_dimension=0, tiled=True
     ).astype(f32)
     out_part = lax.psum_scatter(
         mm(hidden, w_down, ((1,), (1,))).astype(bf16), "fsdp", scatter_dimension=0, tiled=True

time: 1660 us -> 1450 us (0.87)
  waiting for transfers between devices: 1140 us -> 731 us
  Pallas kernels: 31.3 us -> 336 us
  blocking collectives: 166 us -> 18.7 us
  local copies, waits for them, and re-layouts: 58.8 us -> 95.1 us
    all_gather x5 -> x0, waiting for transfers between devices: 465 us -> none  [the longest x1 153 us: on_device(): lax.all_gather(jnp.concatenate([branch_proj, gelu_proj], axis=1), both, a...]
    pallas_call x0 -> x1, Pallas kernels: none -> 305 us  [gather(): pl.pallas_call(gather_kernel, in_specs=[anyspec] * 5, out_specs=[anyspec]...]
    all_to_all x1 -> x0, blocking collectives: 144 us -> none  [on_device(): mlp_mine = lax.all_to_all(mlp_own, 'fsdp', 0, 0, tiled=True)]
    all_gather x1, waiting for transfers between devices: 0.02 us -> 60.7 us  [on_device(): normed_all = lax.all_gather(normed_two, 'fsdp', axis=0, tiled=True)]
    pallas_call x0 -> x1, local copies, waits for them, and re-layouts: none -> 50.5 us  [gather(): pl.pallas_call(gather_kernel, in_specs=[anyspec] * 5, out_specs=[anyspec]...]
    dot_general x12 -> x14, matrix products: 183 us -> 193 us  [mm(): lax.dot_general(left, right, (dims, ((), ())), preferred_element_type=f32)]
    unnamed x12 -> x7, waiting for transfers between devices: 202 us -> 201 us
  transfers between devices with their start and end apart: 14 -> 9, of which waited for: 12 -> 7; matrix products, arithmetic and copies ran while one was open for 10% -> 9% of each run, Pallas kernels for 0% -> 0%
where the time goes in v2:
time: 1450 us; the launch traced here: 1440 us
  waiting for transfers between devices  731 us (50%)
  Pallas kernels  336 us (23%)
  matrix products  193 us (13%)
  local copies, waits for them, and re-layouts  95.1 us (7%)
  other arithmetic  44.2 us (3%)
  blocking collectives  18.7 us (1%)
  between operations  15.2 us (1%)
    pallas_call x1, Pallas kernels, gather(): pl.pallas_call(gather_kernel, in_specs=[anyspec] * 5, out_specs=[anyspec]...  305 us
    unnamed x7, waiting for transfers between devices  201 us
    dot_general x14, matrix products, mm(): lax.dot_general(left, right, (dims, ((), ())), preferred_element_type=f32)  193 us
    reduce_scatter x1, waiting for transfers between devices, on_device(): lax.psum_scatter(jnp.concatenate([term_pair, term_down], axis=1), 'seq',...  183 us
    all_to_all x1, waiting for transfers between devices, on_device(): lax.all_to_all(mlp_sum.reshape(groups, part_rows, 3, ff_part), 'fsdp', 0,...  155 us
    reduce_scatter x1, waiting for transfers between devices, on_device(): lax.psum_scatter(mm(hidden, w_down, ((1,), (1,))).astype(bf16), 'fsdp', s...  71.5 us
    all_gather x1, waiting for transfers between devices, on_device(): normed_all = lax.all_gather(normed_two, 'fsdp', axis=0, tiled=True)  60.7 us
    reduce_scatter x1, waiting for transfers between devices, on_device(): lax.psum_scatter(grad_normed_part.astype(bf16), 'fsdp', scatter_dimension...  58 us
  transfers between devices with their start and end apart: 9, of which 7 were waited for; matrix products, arithmetic and copies ran while one was open for 9% of the time, Pallas kernels for 0%

profile of v2, /device:TPU:0, one launch (start us, length us, event | category | flops | bytes accessed | tf_op | source)
XLA Modules:
  0.0 1442.5 jit_solution(5596469161846056982)
XLA Ops:
  8.1 1.4 stack.33
  15.4 304.7 %gather_weights.1 = (bf16[2560,8320]{1,0:T(8,128)(2,1)}, bf16[3,2560,1920]{2,1,0:T(8,128)(2,1)}, bf16[768,2560]{1,0:T(8,128)(2,1)}) custom-call(bf16[80,8320]{1,0:T(8,128)(2,1)} %copy-done.23, bf16[80,7680]{1,0:T(8,128)(2,1)} %gate.1, bf16[80,7680]{1,0:T(8,128)(2,1)} %up.1, bf16[80,7680]{1,0:T(8,128)(2,1)} %down.1, bf16[192,2560]{1,0:T(8,128)(2,1)} %bitcast.103), custom_call_target="tpu_custom_call" | custom-call | tf_op jit(solution)/shard_map/gather_weights/pallas_call | solution.py:379
  320.1 50.5 %copy.86 = bf16[2560,8320]{0,1:T(8,128)(2,1)} copy(bf16[2560,8320]{1,0:T(8,128)(2,1)} %get-tuple-element.34) | data formatting | bytes 85196800 | tf_op jit(solution)/shard_map/gather_weights/pallas_call | solution.py:379
  371.9 12.7 fusion.89
  384.7 2.3 collective-permute-start
  387.0 3.0 fusion.85
  391.2 1.3 copy-done.2
  393.7 7.2 mixer_forward.1
  401.7 9.3 all-gather.2
  411.4 2.0 fusion.86
  413.5 7.9 multiply_reduce_fusion
  424.2 13.8 fusion.10
  437.9 60.7 %all-gather.6.cloned.1.call-done = bf16[768,2560]{1,0:T(8,128)(2,1)} async-done(((bf16[192,2560]{1,0:T(8,128)(2,1)}), bf16[768,2560]{1,0:T(8,128)(2,1)}) %all-gather.6.cloned.1.call-update) | async-done | bytes 3932176 | tf_op jit(solution)/shard_map/all_gather | solution.py:523
  498.7 14.9 %fusion.16 = f32[768,1920]{1,0:T(8,128)} fusion(bf16[768,2560]{1,0:T(8,128)(2,1)} %all-gather.6.cloned.1.call-done, bf16[3,2560,1920]{2,1,0:T(8,128)(2,1)} %get-tuple-element.37), kind=kOutput, calls=%fused_computation.21 | convolution fusion | flops 7549747200 | bytes 19660800 | tf_op jit(solution)/shard_map/dot_general | solution.py:50
  513.5 19.6 %fusion.37 = (bf16[768,1920]{1,0:T(8,128)(2,1)}, bf16[768,1920]{1,0:T(8,128)(2,1)}, bf16[768,1920]{1,0:T(8,128)(2,1)}) fusion(f32[768,1920]{1,0:T(8,128)} %fusion.10, f32[768,1920]{1,0:T(8,128)} %fusion.16, bf16[768,2560]{1,0:T(8,128)(2,1)S(1)} %copy-done.37, bf16[3,2560,1920]{2,1,0:T(8,128)(2,1)} %get-tuple-element.37), kind=kOutput, calls=%fused_computation.43 | convolution fusion | flops 7586611200 | bytes 34406400 | tf_op jit(solution)/shard_map/dot_general | solution.py:50
  533.2 12.5 fusion.14
  545.7 12.4 add_convert_fusion
  558.1 13.2 fusion.41
  571.4 58.0 %reduce-scatter.10.cloned.1.call-done = bf16[192,2560]{1,0:T(8,128)(2,1)} async-done(((bf16[768,2560]{1,0:T(8,128)(2,1)}), bf16[192,2560]{1,0:T(8,128)(2,1)}) %reduce-scatter.10.cloned.1.call-update) | async-done | bytes 983056 | tf_op jit(solution)/shard_map/reduce_scatter | solution.py:534
  629.4 2.6 fusion.53
  633.3 71.5 %reduce-scatter.8.cloned.1.call-done = bf16[192,2560]{1,0:T(8,128)(2,1)} async-done(((bf16[768,2560]{1,0:T(8,128)(2,1)}), bf16[192,2560]{1,0:T(8,128)(2,1)}) %reduce-scatter.8.cloned.1.call-update) | async-done | bytes 983056 | tf_op jit(solution)/shard_map/reduce_scatter | solution.py:537
  704.8 4.1 fusion.63
  708.9 7.0 fusion.6.grad_mixed
  716.0 12.8 mixer_backward_scan.1
  728.9 9.4 all-gather.3
  738.8 11.2 mixer_backward.1
  751.1 1.3 collective-permute-start.1
  754.3 15.8 %fusion.51 = (bf16[2560]{0:T(1024)(128)(2,1)S(1)}, f32[192]{0:T(256)S(1)}, f32[192,2560]{1,0:T(8,128)}) fusion(bf16[1,192,2560]{2,1,0:T(8,128)(2,1)} %param.17, f32[192]{0:T(256)S(1)} %copy-done.35, f32[2560]{0:T(1024)S(1)} %copy-done.30, bf16[2560,8320]{1,0:T(8,128)(2,1)} %get-tuple-element.34, bf16[192,2560]{1,0:T(8,128)(2,1)} %copy-done.14, ...), kind=kOutput, calls=%fused_computation.69 | convolution fusion | flops 5042501120 | bytes 31161856 | tf_op jit(solution)/shard_map/dot_general | solution.py:50
  770.1 13.8 fusion
  783.8 10.3 fusion.5
  794.5 1.3 constant_dynamic-update-slice_fusion.7
  795.8 1.3 constant_dynamic-update-slice_fusion.6
  798.4 13.6 convolution_convert_fusion.3
  811.9 25.9 %convolution_convert_fusion.1 = bf16[2560,3840]{1,0:T(8,128)(2,1)} fusion(bf16[768,2560]{1,0:T(8,128)(2,1)} %all-gather.6.cloned.1.call-done, bf16[768,1920]{1,0:T(8,128)(2,1)} %get-tuple-element.164, bf16[768,1920]{1,0:T(8,128)(2,1)} %get-tuple-element.163), kind=kOutput, calls=%fused_computation.7 | convolution fusion | flops 15121121280 | bytes 29491200 | tf_op jit(solution)/shard_map/dot_general | solution.py:50
  837.9 23.4 %pad_maximum_fusion = bf16[2560,5760]{1,0:T(8,128)(2,1)} fusion(bf16[2560,1920]{1,0:T(8,128)(2,1)} %convolution_convert_fusion.3, bf16[2560,3840]{1,0:T(8,128)(2,1)} %convolution_convert_fusion.1), kind=kLoop, calls=%fused_computation | loop fusion | flops 58982400 | bytes 58982400 | tf_op jit(solution)/shard_map/concatenate | solution.py:544
  861.6 201.4 %reduce-scatter.16.cloned.1.call-done = bf16[320,8320]{1,0:T(8,128)(2,1)} async-done(((bf16[2560,8320]{1,0:T(8,128)(2,1)}), bf16[320,8320]{1,0:T(8,128)(2,1)}) %reduce-scatter.16.cloned.1.call-update) | async-done | bytes 5324816
  1063.0 183.4 %reduce-scatter.14.cloned.1.call-done = bf16[320,5760]{1,0:T(8,128)(2,1)} async-done(((bf16[2560,5760]{1,0:T(8,128)(2,1)}), bf16[320,5760]{1,0:T(8,128)(2,1)}) %reduce-scatter.14.cloned.1.call-update) | async-done | bytes 3686416 | tf_op jit(solution)/shard_map/reduce_scatter | solution.py:543
  1246.4 7.8 reshape.287
  1254.2 5.3 copy.90
  1259.6 5.1 all-to-all-start
  1264.7 3.2 fusion.69
  1267.9 154.5 %all-to-all-done = bf16[4,80,3,1920]{3,1,2,0:T(8,128)(2,1)} async-done(((bf16[4,80,3,1920]{3,1,2,0:T(8,128)(2,1)}), bf16[4,80,3,1920]{3,1,2,0:T(8,128)(2,1)}, u32[]{:S(2)}, u32[]{:S(2)}) %all-to-all-start) | async-done | bytes 3686432 | tf_op jit(solution)/shard_map/all_to_all | solution.py:546
  1422.4 2.5 convert_bitcast_fusion
  1425.0 1.7 copy.98
  1426.6 1.7 copy.99
  1428.3 1.7 copy.100
  1430.0 1.6 convert_element_type.126
  1433.0 1.5 fusion.87
  (140 shorter events, 23.3 us)
Async XLA Ops:
  7.2 491.5 %all-gather.6.cloned.1.call-start = ((), (), s32[]{:S(2)}) async-start(), calls=%async_computation.6 | async-start | bytes 4915200 | tf_op jit(solution)/shard_map/all_gather | solution.py:523
  14.3 1.1 copy-start.23
  320.1 51.5 %copy-start.20 = (bf16[1,192,2560]{2,1,0:T(8,128)(2,1)S(1)}, bf16[1,192,2560]{2,1,0:T(8,128)(2,1)}, u32[]{:S(2)}) copy-start(bf16[1,192,2560]{2,1,0:T(8,128)(2,1)} %param.17) | copy-start | bytes 2949124
  371.5 15.5 %copy-start.26 = (f32[10,2560]{1,0:T(8,128)}, f32[10,2560]{1,0:T(8,128)S(1)}, u32[]{:S(2)}) copy-start(f32[10,2560]{1,0:T(8,128)S(1)} %convert_bitcast_fusion.3) | copy-start | bytes 307204
  371.6 13.0 copy-start.29
  371.9 12.7 copy-start.32
  371.9 12.7 copy-start.34
  384.7 6.5 collective-permute-start
  386.9 3.1 slice-start
  391.2 1.3 copy-start.2
  392.5 1.2 copy-start.4
  393.7 17.7 %copy-start.24 = (f32[192,5120]{1,0:T(8,128)S(1)}, f32[192,5120]{1,0:T(8,128)}, u32[]{:S(2)}) copy-start(f32[192,5120]{1,0:T(8,128)} %get-tuple-element.185) | copy-start | bytes 11796484
  400.9 12.5 copy-start.1
  400.9 12.5 copy-start.6
  400.9 12.5 copy-start.9
  400.9 12.5 copy-start.12
  400.9 315.0 %copy-start = (f32[192,2560]{1,0:T(8,128)}, f32[192,2560]{1,0:T(8,128)S(1)}, u32[]{:S(2)}) copy-start(f32[192,2560]{1,0:T(8,128)S(1)} %get-tuple-element.36.cum) | copy-start | bytes 5898244
  401.0 0.7 copy-start.27
  411.4 2.0 copy-start.21
  413.5 8.0 copy-start.25
  421.4 1.3 copy-start.16
  422.0 0.7 copy-start.31
  423.9 205.5 %reduce-scatter.10.cloned.1.call-start = ((), (), s32[]{:S(2)}) async-start(), calls=%async_computation.8 | async-start | bytes 4915200 | tf_op jit(solution)/shard_map/reduce_scatter | solution.py:534
  498.7 14.9 %copy-start.37 = (bf16[768,2560]{1,0:T(8,128)(2,1)S(1)}, bf16[768,2560]{1,0:T(8,128)(2,1)}, u32[]{:S(2)}) copy-start(bf16[768,2560]{1,0:T(8,128)(2,1)} %all-gather.6.cloned.1.call-done) | copy-start | bytes 11796484
  533.2 12.5 copy-start.38
  558.1 146.8 %reduce-scatter.8.cloned.1.call-start = ((), (), s32[]{:S(2)}) async-start(), calls=%async_computation.7 | async-start | bytes 4915200 | tf_op jit(solution)/shard_map/reduce_scatter | solution.py:537
  571.3 491.6 %reduce-scatter.16.cloned.1.call-start = ((), (), s32[]{:S(2)}) async-start(), calls=%async_computation.11 | async-start | bytes 47923200
  708.9 7.0 copy-start.18
  708.9 7.0 copy-start.7
  708.9 7.0 copy-start.8
  715.9 12.9 copy-start.28
  716.0 22.8 %copy-start.3 = (bf16[2560,256]{1,0:T(8,128)(2,1)S(1)}, bf16[2560,256]{1,0:T(8,128)(2,1)}, u32[]{:S(2)}) copy-start(bf16[2560,256]{1,0:T(8,128)(2,1)} %get-tuple-element.162.rate_w) | copy-start | bytes 3932164
  716.0 22.8 %copy-start.5 = (bf16[192,2560]{1,0:T(8,128)(2,1)S(1)}, bf16[192,2560]{1,0:T(8,128)(2,1)}, u32[]{:S(2)}) copy-start(bf16[192,2560]{1,0:T(8,128)(2,1)} %slice.278.branch) | copy-start | bytes 2949124
  716.0 22.8 %copy-start.13 = (bf16[192,2560]{1,0:T(8,128)(2,1)S(1)}, bf16[192,2560]{1,0:T(8,128)(2,1)}, u32[]{:S(2)}) copy-start(bf16[192,2560]{1,0:T(8,128)(2,1)} %copy-done.12) | copy-start | bytes 2949124
  728.8 21.2 %copy-start.14 = (bf16[192,2560]{1,0:T(8,128)(2,1)}, bf16[192,2560]{1,0:T(8,128)(2,1)S(1)}, u32[]{:S(2)}) copy-start(bf16[192,2560]{1,0:T(8,128)(2,1)S(1)} %get-tuple-element.47) | copy-start | bytes 2949124
  738.8 15.5 %copy-start.30 = (f32[2560]{0:T(1024)S(1)}, f32[2560]{0:T(1024)}, u32[]{:S(2)}) copy-start(f32[2560]{0:T(1024)} %copy-done.29) | copy-start | bytes 30724
  738.8 15.5 %copy-start.35 = (f32[192]{0:T(256)S(1)}, f32[192]{0:T(256)}, u32[]{:S(2)}) copy-start(f32[192]{0:T(256)} %copy-done.34) | copy-start | bytes 2308
  750.0 1.1 copy-start.10
  751.1 3.1 collective-permute-start.1
  754.3 15.8 %copy-start.15 = (bf16[192,2560]{1,0:T(8,128)(2,1)S(1)}, bf16[192,2560]{1,0:T(8,128)(2,1)}, u32[]{:S(2)}) copy-start(bf16[192,2560]{1,0:T(8,128)(2,1)} %copy-done.14) | copy-start | bytes 2949124
  783.8 10.7 copy-start.11
  798.1 448.3 %reduce-scatter.14.cloned.1.call-start = ((), (), s32[]{:S(2)}) async-start(), calls=%async_computation.10 | async-start | bytes 33177600 | tf_op jit(solution)/shard_map/reduce_scatter | solution.py:543
  861.3 568.7 %reduce-scatter.12.cloned.1.call-start = ((), (), s32[]{:S(2)}) async-start(), calls=%async_computation.9 | async-start | bytes 6656000 | tf_op jit(solution)/shard_map/reduce_scatter | solution.py:602
  1259.5 5.1 copy-start.33
  1259.5 5.1 copy-start.19
  1259.6 5.1 copy-start.22
  1259.6 162.9 %all-to-all-start = ((bf16[4,80,3,1920]{3,1,2,0:T(8,128)(2,1)}), bf16[4,80,3,1920]{3,1,2,0:T(8,128)(2,1)}, u32[]{:S(2)}, u32[]{:S(2)}) async-start(bf16[4,80,3,1920]{3,1,2,0:T(8,128)(2,1)} %copy.90), calls=%async_computation.4 | async-start | bytes 7372800 | tf_op jit(solution)/shard_map/all_to_all | solution.py:546
  1430.0 3.1 copy-start.17
  (1 other events, 0.6 us)
Sparse Core Ops, SparseCore 0:
  424.0 74.5 all-gather.5
  558.2 71.2 reduce-scatter.9
  631.8 73.0 reduce-scatter.7
  798.2 264.6 reduce-scatter.15
  1066.8 179.5 reduce-scatter.13
  1248.7 153.1 reduce-scatter.11

commit v3 on v2

--- a/solution.py
+++ b/solution.py
@@ -393,6 +393,237 @@
     )(mixer, gate, up, down, grad)
 
 
+def add_columns(target, sources, start, size, step):
+    def one(turn, carry):
+        cols = pl.ds(pl.multiple_of(start + turn * step, 128), step)
+        total = target[:, cols].astype(f32)
+        for source in sources:
+            total = total + source[:, cols].astype(f32)
+        target[:, cols] = total.astype(target.dtype)
+        return carry
+
+    lax.fori_loop(0, size // step, one, 0)
+
+
+def scatter_kernel(
+    wide, outer, rest, mlp_pair, mlp_down, out, mixer_sum, mlp_back, out_sum,
+    held, cross, near, lined, held_out, lined_out,
+    load_sem, flow_send, flow_recv, line_send, line_recv, swap_send, swap_recv, own_sem,
+):
+    s, z, _, beside, across = places()
+    chip, chip_beside, chip_across = s // 2, beside // 2, across // 2
+    chip_diag = chip_beside + chip_across - chip
+    rows = held.shape[1] // 4
+    cols = held.shape[2]
+    cut = cols // 256 * 128
+    tok = held_out.shape[1]
+    ff_part = mlp_down.shape[1]
+    parts = (wide, outer, rest)
+    order = (3 * (1 - z // 2), (2 + 3 * z) % 5, 1 + z % 2, z)
+
+    def remote(src, dst, send, recv, target):
+        return pltpu.make_async_remote_copy(
+            src_ref=src, dst_ref=dst, send_sem=send, recv_sem=recv, device_id=target, device_id_type=MESH
+        )
+
+    def span(k):
+        return pl.ds(pl.multiple_of(k * rows, 16), rows)
+
+    def loads(i):
+        copies, start = [], 0
+        for n, part in enumerate(parts):
+            size = part.shape[2]
+            copies.append(
+                pltpu.make_async_copy(
+                    part.at[:, span(order[i]), :], held.at[:, span(order[i]), pl.ds(start, size)], load_sem.at[i, n]
+                )
+            )
+            start += size
+        return copies
+
+    left, right = pl.ds(0, cut), pl.ds(cut, cols - cut)
+
+    def block(q, i, side):
+        return held.at[q, span(order[i]), side]
+
+    def flow(i, index):
+        send, recv = flow_send.at[i, index], flow_recv.at[i, index]
+        to_beside, to_across = (beside, z), (across, z)
+        if index == 0:
+            return remote(block(chip_diag, i, left), cross.at[i, :, left], send, recv, to_across)
+        if index == 1:
+            return remote(block(chip_diag, i, right), cross.at[i, :, right], send, recv, to_beside)
+        if index == 2:
+            return remote(block(chip_beside, i, right), near.at[0, i, :, right], send, recv, to_beside)
+        if index == 3:
+            return remote(block(chip_beside, i, left), near.at[0, i, :, left], send, recv, to_beside)
+        if index == 4:
+            return remote(block(chip_across, i, left), near.at[1, i, :, left], send, recv, to_across)
+        return remote(block(chip_across, i, right), near.at[1, i, :, right], send, recv, to_across)
+
+    def cross_step(i):
+        flow(i, 0).wait_recv()
+        add_columns(held.at[chip_beside, span(order[i]), :], [cross.at[i]], 0, cut, 512)
+        flow(i, 3).start()
+        flow(i, 1).wait_recv()
+        add_columns(held.at[chip_across, span(order[i]), :], [cross.at[i]], cut, cols - cut, 384)
+        flow(i, 5).start()
+
+    def near_step(i):
+        for index in (2, 4, 3, 5):
+            flow(i, index).wait_recv()
+        add_columns(held.at[chip, span(order[i]), :], [near.at[0, i], near.at[1, i]], 0, cols, 640)
+
+    def mine(kind, k):
+        return held.at[chip, span(k), :] if kind == 0 else held_out.at[k]
+
+    def landing(kind, slot):
+        return lined.at[slot] if kind == 0 else lined_out.at[slot]
+
+    def line(kind, k, slot, target):
+        return remote(
+            mine(kind, k), landing(kind, slot), line_send.at[kind, k], line_recv.at[kind, slot], (s, target)
+        )
+
+    def absorb(kind, k, slot, source):
+        line(kind, k, slot, source).wait_recv()
+        if kind == 0:
+            add_columns(mine(kind, k), [landing(kind, slot)], 0, cols, 640)
+        else:
+            add_columns(mine(kind, k), [landing(kind, slot)], 0, held_out.shape[2], 512)
+
+    def chain(kind, i):
+        k = order[i]
+        if i == 3:
+            pl.when(z > 0)(lambda: absorb(kind, k, k, z - 1))
+            pl.when(z < 3)(lambda: absorb(kind, k, 4, z + 1))
+            return
+
+        @pl.when(k > z)
+        def _():
+            pl.when(z > 0)(lambda: absorb(kind, k, k, z - 1))
+            line(kind, k, k, z + 1).start()
+
+        @pl.when(k < z)
+        def _():
+            pl.when(z < 3)(lambda: absorb(kind, k, k, z + 1))
+            pl.when(k == z - 1)(lambda: line(kind, k, 4, z - 1).start())
+            pl.when(k < z - 1)(lambda: line(kind, k, k, z - 1).start())
+
+    def chain_drain(kind):
+        for i in range(3):
+            k = order[i]
+            line(kind, k, k, (z + 1) % 4).wait_send()
+
+    def pieces():
+        for m in range(3):
+            source = mlp_down if m == 2 else mlp_pair
+            yield m, source, pl.ds(0 if m == 2 else m * ff_part, ff_part)
+
+    def swap(k):
+        to = (z + k) % 4
+        here = pl.ds(pl.multiple_of(z * ff_part, 128), ff_part)
+        return [
+            remote(
+                source.at[span(to), at], mlp_back.at[m, :, here], swap_send.at[k - 1, m], swap_recv.at[k - 1, m], (s, to)
+            )
+            for m, source, at in pieces()
+        ]
+
+    own = [
+        pltpu.make_async_copy(
+            source.at[span(z), at], mlp_back.at[m, :, pl.ds(pl.multiple_of(z * ff_part, 128), ff_part)], own_sem.at[m]
+        )
+        for m, source, at in pieces()
+    ]
+    out_load = pltpu.make_async_copy(out, held_out, own_sem.at[3])
+    out_load.start()
+    for i in range(4):
+        for copy in loads(i):
+            copy.start()
+    greet([(beside, z), (across, z)] + [(s, (z + k) % 4) for k in range(1, 4)])
+    out_load.wait()
+    chain(1, 0)
+    for k in (1, 3, 2):
+        for copy in swap(k):
+            copy.start()
+    for copy in own:
+        copy.start()
+    for i in range(2):
+        for copy in loads(i):
+            copy.wait()
+        flow(i, 0).start()
+        flow(i, 1).start()
+        if i == 0:
+            flow(i, 2).start()
+            flow(i, 4).start()
+    for i in range(4):
+        cross_step(i)
+        if i + 1 < 4:
+            flow(i + 1, 2).start()
+            flow(i + 1, 4).start()
+        if i + 2 < 4:
+            for copy in loads(i + 2):
+                copy.wait()
+            flow(i + 2, 0).start()
+            flow(i + 2, 1).start()
+        if i + 1 < 4:
+            chain(1, i + 1)
+        if i > 0:
+            near_step(i - 1)
+            chain(0, i - 1)
+    out_done = pltpu.make_async_copy(held_out.at[z], out_sum, own_sem.at[4])
+    out_done.start()
+    near_step(3)
+    chain(0, 3)
+    done = pltpu.make_async_copy(held.at[chip, span(z), :], mixer_sum, own_sem.at[5])
+    done.start()
+    for i in range(4):
+        for index in range(6):
+            flow(i, index).wait_send()
+    chain_drain(0)
+    chain_drain(1)
+    for k in range(1, 4):
+        for copy in swap(k):
+            copy.wait()
+    for copy in own:
+        copy.wait()
+    out_done.wait()
+    done.wait()
+
+
+def scatter(wide, outer, rest, mlp_pair, mlp_down, out):
+    rows = wide.shape[1] // 4
+    cols = wide.shape[2] + outer.shape[2] + rest.shape[2]
+    _, tok, model = out.shape
+    ff_part = mlp_down.shape[1]
+    anyspec = pl.BlockSpec(memory_space=pl.ANY)
+    dma = pltpu.SemaphoreType.DMA
+    return pl.pallas_call(
+        scatter_kernel,
+        in_specs=[anyspec] * 6,
+        out_specs=[anyspec] * 3,
+        out_shape=[
+            jax.ShapeDtypeStruct((rows, cols), bf16),
+            jax.ShapeDtypeStruct((3, rows, 4 * ff_part), bf16),
+            jax.ShapeDtypeStruct((tok, model), bf16),
+        ],
+        scratch_shapes=[
+            pltpu.VMEM((4, 4 * rows, cols), bf16),
+            pltpu.VMEM((4, rows, cols), bf16),
+            pltpu.VMEM((2, 4, rows, cols), bf16),
+            pltpu.VMEM((5, rows, cols), bf16),
+            pltpu.VMEM((4, tok, model), bf16),
+            pltpu.VMEM((5, tok, model), bf16),
+            dma((4, 3)), dma((4, 6)), dma((4, 6)), dma((2, 4)), dma((2, 5)), dma((3, 3)), dma((3, 3)), dma((6,)),
+        ],
+        compiler_params=pltpu.CompilerParams(
+            collective_id=2, has_side_effects=True, vmem_limit_bytes=60 * 1024 * 1024
+        ),
+        name="scatter_gradients",
+    )(wide, outer, rest, mlp_pair, mlp_down, out)
+
+
 def gather_plain(mixer, gate, up, down, grad):
     groups = lax.axis_size("fsdp")
     part_rows, ff = gate.shape
@@ -408,6 +639,52 @@
         lax.all_gather(mine, "seq", axis=1, tiled=True),
         lax.all_gather(grad, "fsdp", axis=0, tiled=True),
     )
+
+
+def swap_cores(shard):
+    count = lax.axis_size("seq")
+    return lax.ppermute(shard, "seq", [(i, i + 1 - 2 * (i % 2)) for i in range(count)])
+
+
+def scatter_paired(normed, grad_both, grad_mix, mixed, rest, pair_sum, down_sum, out_part):
+    core = lax.axis_index("seq") % 2
+    chips = lax.axis_size("seq") // 2
+
+    def pairs(shard):
+        return jnp.concatenate([shard, swap_cores(shard)], axis=0)
+
+    def halves(values, which):
+        grouped = values.reshape(values.shape[0], chips, 2, values.shape[1] // (2 * chips))
+        return lax.dynamic_index_in_dim(grouped, which, 2, False).reshape(values.shape[0], -1)
+
+    def product(left, right):
+        result = mm(halves(left, core), right, ((0,), (0,))).astype(bf16)
+        return result.reshape(chips, -1, right.shape[1])
+
+    wide = product(pairs(normed), pairs(grad_both))
+    outer = product(pairs(grad_mix), pairs(mixed))
+    grouped = rest.reshape(chips, 2, -1, rest.shape[1])
+    own = lax.dynamic_index_in_dim(grouped, core, 1, False)
+    other = swap_cores(lax.dynamic_index_in_dim(grouped, 1 - core, 1, False))
+    rest = (own.astype(f32) + other.astype(f32)).astype(bf16)
+    groups = lax.axis_size("fsdp")
+    return scatter(wide, outer, rest, pair_sum, down_sum, out_part.reshape(groups, -1, out_part.shape[1]))
+
+
+def scatter_plain(normed, grad_both, grad_mix, mixed, rest, pair_sum, down_sum, out_part):
+    groups = lax.axis_size("fsdp")
+    term_wide = mm(normed, grad_both, ((0,), (0,))).astype(bf16)
+    term_out = mm(grad_mix, mixed, ((0,), (0,))).astype(bf16)
+    mixer_sum = lax.psum_scatter(
+        jnp.concatenate([term_wide, term_out, rest], axis=1), "seq", scatter_dimension=0, tiled=True
+    )
+    mixer_sum = lax.psum_scatter(mixer_sum, "fsdp", scatter_dimension=0, tiled=True)
+    ff_part = down_sum.shape[1]
+    part_rows = down_sum.shape[0] // groups
+    mlp_sum = jnp.concatenate([pair_sum, down_sum], axis=1).reshape(groups, part_rows, 3, ff_part)
+    mlp_back = lax.all_to_all(mlp_sum, "fsdp", 0, 0, tiled=True)
+    mlp_back = jnp.transpose(mlp_back, (2, 1, 0, 3)).reshape(3, part_rows, groups * ff_part)
+    return mixer_sum, mlp_back, lax.psum_scatter(out_part, "fsdp", scatter_dimension=0, tiled=True)
 
 
 def call_heads(kernel, width, heads, ins, outs, scratch, name):
@@ -475,11 +752,12 @@
     mixer_own = jnp.concatenate(
         [smalls, rate_blocks, input_blocks, branch_proj, gelu_proj, out_proj], axis=1
     )
-    if lax.axis_size("seq") == 8 and groups == 4:
+    custom = lax.axis_size("seq") == 8 and groups == 4
+    if custom:
         mixer_w, mlp_w, grad_out_all = gather(mixer_own, gate_proj, up_proj, down_proj, grad_out)
     else:
         mixer_w, mlp_w, grad_out_all = gather_plain(mixer_own, gate_proj, up_proj, down_proj, grad_out)
-    first = mixer_w[:, : 128 + 2 * width]
+    first = lax.optimization_barrier(mixer_w[:, : 128 + 2 * width])
     wide = mixer_w[:, 128 + 2 * width : 128 + 2 * width + 2 * lru]
     proj_out = mixer_w[:, 128 + 2 * width + 2 * lru :]
 
@@ -533,22 +811,16 @@
     grad_normed_part = mm(grad_gate, w_gate, ((1,), (1,))) + mm(grad_up, w_up, ((1,), (1,)))
     grad_normed_two = lax.psum_scatter(
         grad_normed_part.astype(bf16), "fsdp", scatter_dimension=0, tiled=True
-    ).astype(f32)
-    out_part = lax.psum_scatter(
-        mm(hidden, w_down, ((1,), (1,))).astype(bf16), "fsdp", scatter_dimension=0, tiled=True
-    )
-    block_output = (middle + out_part.astype(f32)).astype(bf16)[None]
+    )
+    out_part = mm(hidden, w_down, ((1,), (1,))).astype(bf16)
     term_pair = mm(normed_all, grad_pair, ((0,), (0,))).astype(bf16)
     term_down = mm(grad_out_all, hidden, ((0,), (0,))).astype(bf16)
-    mlp_sum = lax.psum_scatter(
-        jnp.concatenate([term_pair, term_down], axis=1), "seq", scatter_dimension=0, tiled=True
-    )
-    mlp_back = lax.all_to_all(
-        mlp_sum.reshape(groups, part_rows, 3, ff_part), "fsdp", 0, 0, tiled=True
-    )
-    mlp_grads = [
-        jnp.transpose(mlp_back[:, :, i], (1, 0, 2)).reshape(part_rows, ff).astype(f32) for i in range(3)
-    ]
+    term_pair, term_down, grad_normed_two = lax.optimization_barrier(
+        (term_pair, term_down, grad_normed_two)
+    )
+    grad_normed_two = grad_normed_two.astype(f32)
+    pair_sum = lax.psum_scatter(term_pair, "seq", scatter_dimension=0, tiled=True)
+    down_sum = lax.psum_scatter(term_down, "seq", scatter_dimension=0, tiled=True)
 
     second_pull = jax.vjp(norm_rows, middle, gain_two)[1]
     grad_mid_part, grad_gain_two = second_pull(grad_normed_two)
@@ -589,17 +861,17 @@
     first_pull = jax.vjp(norm_rows, tokens, gain_one)[1]
     grad_tok_part, grad_gain_one = first_pull(grad_normed)
     input_grad = (grad_middle + grad_tok_part).astype(bf16)[None]
-    term_wide = mm(normed, grad_both, ((0,), (0,))).astype(bf16)
-    term_out = mm(grad_mix, mixed, ((0,), (0,))).astype(bf16)
     vectors = jnp.concatenate([sums, grad_gain_one[None], grad_gain_two[None]], axis=0).T
     vectors = jnp.pad(vectors, ((0, 0), (0, 128 - vectors.shape[1]))).astype(bf16)
-    mixer_sum = lax.psum_scatter(
-        jnp.concatenate([term_wide, term_out, rate_w_grad, input_w_grad, vectors], axis=1),
-        "seq",
-        scatter_dimension=0,
-        tiled=True,
-    )
-    mixer_sum = lax.psum_scatter(mixer_sum, "fsdp", scatter_dimension=0, tiled=True).astype(f32)
+    rest = jnp.concatenate([rate_w_grad, input_w_grad, vectors], axis=1)
+    if custom:
+        scattered = scatter_paired(normed, grad_both, grad_mix, mixed, rest, pair_sum, down_sum, out_part)
+    else:
+        scattered = scatter_plain(normed, grad_both, grad_mix, mixed, rest, pair_sum, down_sum, out_part)
+    mixer_sum, mlp_back, out_sum = scattered
+    block_output = (middle + out_sum.astype(f32)).astype(bf16)[None]
+    mlp_grads = [mlp_back[m].astype(f32) for m in range(3)]
+    mixer_sum = mixer_sum.astype(f32)
     edges = [lru, 2 * lru, 3 * lru, 3 * lru + width, 3 * lru + 2 * width]
     dbranch, dgelu, dout, drate, dinput, vec = jnp.split(mixer_sum, edges, axis=1)
     vec = vec.T

time: 1450 us -> 1050 us (0.72)
  waiting for transfers between devices: 731 us -> 178 us
  Pallas kernels: 336 us -> 553 us
  local copies, waits for them, and re-layouts: 95.1 us -> 40.6 us
    pallas_call x0 -> x1, Pallas kernels: none -> 217 us  [scatter(): pl.pallas_call(scatter_kernel, in_specs=[anyspec] * 6, out_specs=[anyspec...]
    unnamed x7 -> x4, waiting for transfers between devices: 201 us -> 0.57 us
    reduce_scatter x3 -> x2, waiting for transfers between devices: 255 us -> 87.1 us  [the longest x1 87.1 us: on_device(): lax.psum_scatter(term_pair, 'seq', scatter_dimension=0, tiled=True)]
    all_to_all x1 -> x0, waiting for transfers between devices: 155 us -> none  [on_device(): lax.all_to_all(mlp_sum.reshape(groups, part_rows, 3, ff_part), 'fsdp', 0,...]
    pallas_call x1 -> x0, local copies, waits for them, and re-layouts: 50.5 us -> none  [gather(): pl.pallas_call(gather_kernel, in_specs=[anyspec] * 5, out_specs=[anyspec]...]
    reduce_scatter x1, waiting for transfers between devices: 58 us -> 26.6 us  [on_device(): lax.psum_scatter(grad_normed_part.astype(bf16), 'fsdp', scatter_dimension...]
    concatenate x1 -> x4, other arithmetic: 23.4 us -> 6.79 us  [the longest x2 4.94 us: pairs(): return jnp.concatenate([shard, swap_cores(shard)], axis=0)]
  transfers between devices with their start and end apart: 9 -> 11, of which waited for: 7 -> 4; matrix products, arithmetic and copies ran while one was open for 9% -> 14% of each run, Pallas kernels for 0% -> 2%
where the time goes in v3:
time: 1050 us; the launch traced here: 1040 us
  Pallas kernels  553 us (53%)
  matrix products  189 us (18%)
  waiting for transfers between devices  178 us (17%)
  local copies, waits for them, and re-layouts  40.6 us (4%)
  other arithmetic  34.4 us (3%)
  blocking collectives  19.3 us (2%)
  between operations  15.2 us (1%)
    pallas_call x1, Pallas kernels, gather(): pl.pallas_call(gather_kernel, in_specs=[anyspec] * 5, out_specs=[anyspec]...  305 us
    pallas_call x1, Pallas kernels, scatter(): pl.pallas_call(scatter_kernel, in_specs=[anyspec] * 6, out_specs=[anyspec...  217 us
    dot_general x14, matrix products, mm(): lax.dot_general(left, right, (dims, ((), ())), preferred_element_type=f32)  189 us
    reduce_scatter x1, waiting for transfers between devices, on_device(): lax.psum_scatter(term_pair, 'seq', scatter_dimension=0, tiled=True)  87.1 us
    all_gather x1, waiting for transfers between devices, on_device(): normed_all = lax.all_gather(normed_two, 'fsdp', axis=0, tiled=True)  60.9 us
    pallas_call x3, Pallas kernels, call_heads(): pl.pallas_call(kernel, grid=(heads,), in_specs=in_specs, out_specs=out_sp...  31.4 us
    reduce_scatter x1, waiting for transfers between devices, on_device(): lax.psum_scatter(grad_normed_part.astype(bf16), 'fsdp', scatter_dimension...  26.6 us
  transfers between devices with their start and end apart: 11, of which 4 were waited for; matrix products, arithmetic and copies ran while one was open for 14% of the time, Pallas kernels for 2%

profile of v3, /device:TPU:0, one launch (start us, length us, event | category | flops | bytes accessed | tf_op | source)
XLA Modules:
  0.0 1037.2 jit_solution(18059049534007877531)
XLA Ops:
  7.2 1.5 fusion.74
  15.9 304.7 %gather_weights.1 = (bf16[2560,8320]{1,0:T(8,128)(2,1)}, bf16[3,2560,1920]{2,1,0:T(8,128)(2,1)}, bf16[768,2560]{1,0:T(8,128)(2,1)}) custom-call(bf16[80,8320]{1,0:T(8,128)(2,1)} %copy-done.37, bf16[80,7680]{1,0:T(8,128)(2,1)} %gate.1, bf16[80,7680]{1,0:T(8,128)(2,1)} %up.1, bf16[80,7680]{1,0:T(8,128)(2,1)} %down.1, bf16[192,2560]{1,0:T(8,128)(2,1)} %bitcast.108), custom_call_target="tpu_custom_call" | custom-call | tf_op jit(solution)/shard_map/gather_weights/pallas_call | solution.py:379
  320.7 2.2 slice.212
  323.0 2.7 slice_reduce_fusion
  326.0 12.9 %fusion.97 = (bf16[192,5120]{1,0:T(8,128)(2,1)S(1)}, f32[192,5120]{1,0:T(8,128)}) fusion(bf16[192,2560]{1,0:T(8,128)(2,1)S(1)} %fusion.58, bf16[2560,8320]{1,0:T(8,128)(2,1)} %get-tuple-element.40), kind=kOutput, calls=%fused_computation.192 | convolution fusion | flops 5034147840 | bytes 33095680 | tf_op jit(solution)/shard_map/dot_general | solution.py:50
  338.9 2.3 collective-permute-start
  341.3 1.7 copy.79
  343.1 1.7 copy.80
  344.8 1.7 copy.81
  346.7 2.2 slice.278.branch
  350.2 7.2 mixer_forward.1
  358.2 9.5 all-gather.2
  368.2 2.0 fusion.93
  370.3 8.0 multiply_reduce_fusion
  380.7 13.8 %fusion.18 = f32[768,1920]{1,0:T(8,128)} fusion(bf16[768,2560]{1,0:T(8,128)(2,1)} %get-tuple-element.43, bf16[3,2560,1920]{2,1,0:T(8,128)(2,1)} %get-tuple-element.44), kind=kOutput, calls=%fused_computation.22 | convolution fusion | flops 7549747200 | bytes 19660800 | tf_op jit(solution)/shard_map/dot_general | solution.py:50
  394.6 60.9 %all-gather.6.cloned.1.call-done = bf16[768,2560]{1,0:T(8,128)(2,1)} async-done(((bf16[192,2560]{1,0:T(8,128)(2,1)}), bf16[768,2560]{1,0:T(8,128)(2,1)}) %all-gather.6.cloned.1.call-update) | async-done | bytes 3932176 | tf_op jit(solution)/shard_map/all_gather | solution.py:801
  455.5 13.4 %fusion.10 = f32[768,1920]{1,0:T(8,128)S(1)} fusion(bf16[768,2560]{1,0:T(8,128)(2,1)} %all-gather.6.cloned.1.call-done, bf16[3,2560,1920]{2,1,0:T(8,128)(2,1)} %get-tuple-element.44), kind=kOutput, calls=%fused_computation.14 | convolution fusion | flops 7549747200 | bytes 19660800 | tf_op jit(solution)/shard_map/dot_general | solution.py:50
  468.8 15.6 %multiply_convert_fusion = (bf16[768,1920]{1,0:T(8,128)(2,1)}, bf16[768,1920]{1,0:T(8,128)(2,1)S(1)}, bf16[768,1920]{1,0:T(8,128)(2,1)S(1)}) fusion(f32[768,1920]{1,0:T(8,128)S(1)} %fusion.10, f32[768,1920]{1,0:T(8,128)S(1)} %copy-done.55, bf16[768,2560]{1,0:T(8,128)(2,1)S(1)} %copy-done.54, bf16[3,2560,1920]{2,1,0:T(8,128)(2,1)} %get-tuple-element.44), kind=kOutput, calls=%fused_computation.46 | convolution fusion | flops 7586611200 | bytes 34406400 | tf_op jit(solution)/shard_map/dot_general | solution.py:50
  484.4 13.1 %fusion.8 = f32[768,2560]{1,0:T(8,128)S(1)} fusion(bf16[768,1920]{1,0:T(8,128)(2,1)S(1)} %get-tuple-element.174, bf16[3,2560,1920]{2,1,0:T(8,128)(2,1)} %get-tuple-element.44), kind=kOutput, calls=%fused_computation.12 | convolution fusion | flops 7549747200 | bytes 20643840 | tf_op jit(solution)/shard_map/dot_general | solution.py:50
  497.5 12.4 %add_convert_fusion = bf16[768,2560]{1,0:T(8,128)(2,1)} fusion(f32[768,2560]{1,0:T(8,128)S(1)} %fusion.8, bf16[768,1920]{1,0:T(8,128)(2,1)S(1)} %get-tuple-element.175, bf16[3,2560,1920]{2,1,0:T(8,128)(2,1)} %get-tuple-element.44), kind=kOutput, calls=%fused_computation.32 | convolution fusion | flops 7553679360 | bytes 24576000 | tf_op jit(solution)/shard_map/dot_general | solution.py:50
  510.0 21.9 %convolution_convert_fusion.3 = bf16[2560,1920]{1,0:T(8,128)(2,1)} fusion(bf16[768,2560]{1,0:T(8,128)(2,1)} %get-tuple-element.43, bf16[768,1920]{1,0:T(8,128)(2,1)} %get-tuple-element.173), kind=kOutput, calls=%fused_computation.11 | convolution fusion | flops 7554662400 | bytes 16711680 | tf_op jit(solution)/shard_map/dot_general | solution.py:50
  531.9 22.9 %convolution_convert_fusion = bf16[2560,3840]{1,0:T(8,128)(2,1)} fusion(bf16[768,2560]{1,0:T(8,128)(2,1)} %all-gather.6.cloned.1.call-done, bf16[768,1920]{1,0:T(8,128)(2,1)} %copy-done.56, bf16[768,1920]{1,0:T(8,128)(2,1)} %copy-done.58), kind=kOutput, calls=%fused_computation.4 | convolution fusion | flops 15121121280 | bytes 29491200 | tf_op jit(solution)/shard_map/dot_general | solution.py:50
  554.8 26.6 %reduce-scatter.4.cloned.1.call-done = bf16[192,2560]{1,0:T(8,128)(2,1)} async-done(((bf16[768,2560]{1,0:T(8,128)(2,1)}), bf16[192,2560]{1,0:T(8,128)(2,1)}) %reduce-scatter.4.cloned.1.call-update) | async-done | bytes 983056 | tf_op jit(solution)/shard_map/reduce_scatter | solution.py:812
  582.5 2.4 collective-permute-done.1
  584.9 2.9 pad_maximum_fusion
  587.8 4.2 copy.82
  592.0 3.4 fusion.61
  596.0 3.1 fusion.92
  599.2 7.7 fusion.4.grad_mixed
  607.1 12.8 %mixer_backward_scan.1 = (bf16[192,2560]{1,0:T(8,128)(2,1)S(1)}, f32[192,2560]{1,0:T(8,128)S(1)}, f32[192,2560]{1,0:T(8,128)S(1)}, f32[8,2560]{1,0:T(8,128)S(1)}) custom-call(f32[192,2560]{1,0:T(8,128)S(1)} %fusion.4.grad_mixed, f32[192,2560]{1,0:T(8,128)S(1)} %copy-done.7, f32[192,2560]{1,0:T(8,128)S(1)} %copy-done.6, f32[192,2560]{1,0:T(8,128)S(1)} %copy-done.1, ...), custom_call_target="tpu_custom_call" | custom-call | tf_op jit(solution)/shard_map/mixer_backward_scan/pallas_call | solution.py:703
  620.0 9.8 all-gather.3
  630.2 11.4 %mixer_backward.1 = (f32[192,2560]{1,0:T(8,128)S(1)}, f32[8,2560]{1,0:T(8,128)S(1)}, bf16[2560,256]{1,0:T(8,128)(2,1)S(1)}, bf16[2560,256]{1,0:T(8,128)(2,1)S(1)}, f32[8,2560]{1,0:T(8,128)S(1)}) custom-call(f32[192,2560]{1,0:T(8,128)S(1)} %get-tuple-element.47.rev_cum, f32[192,2560]{1,0:T(8,128)S(1)} %get-tuple-element.48.rev_grad, ...), custom_call_target="tpu_custom_call" | custom-call | tf_op jit(solution)/shard_map/mixer_backward/pallas_call | solution.py:703
  645.4 1.5 pad_maximum_fusion.1
  646.9 2.0 collective-permute-start.3
  649.0 16.1 %fusion.75 = (f32[192]{0:T(256)S(1)}, bf16[2560]{0:T(1024)(128)(2,1)S(1)}, f32[192,2560]{1,0:T(8,128)}) fusion(bf16[1,192,2560]{2,1,0:T(8,128)(2,1)} %param.17, f32[2560]{0:T(1024)S(1)} %copy-done.47, f32[192]{0:T(256)S(1)} %copy-done.53, bf16[192,5120]{1,0:T(8,128)(2,1)} %pad_maximum_fusion.1, bf16[2560,8320]{1,0:T(8,128)(2,1)} %get-tuple-element.40), kind=kOutput, calls=%fused_computation.92 | convolution fusion | flops 5036602880 | bytes 31146496 | tf_op jit(solution)/shard_map/dot_general | solution.py:50
  665.8 1.7 copy-done.23
  669.4 12.3 %fusion.40 = bf16[768,2560]{1,0:T(8,128)(2,1)} fusion(bf16[768,1920]{1,0:T(8,128)(2,1)S(1)} %copy-done.57, bf16[3,2560,1920]{2,1,0:T(8,128)(2,1)} %get-tuple-element.44), kind=kOutput, calls=%fused_computation.49 | convolution fusion | flops 7551713280 | bytes 16711680 | tf_op jit(solution)/shard_map/dot_general | solution.py:50
  681.7 2.0 pad_maximum_fusion.2
  683.7 2.3 copy.83
  686.0 1.5 constant_dynamic-slice_fusion
  687.5 7.7 convolution_convert_fusion.2
  695.3 3.3 fusion.53.rest
  698.6 11.7 %convolution_convert_fusion.1 = bf16[1280,5120]{1,0:T(8,128)(2,1)} fusion(bf16[384,1280]{0,1:T(8,128)(2,1)S(1)} %bitcast.114, bf16[192,5120]{1,0:T(8,128)(2,1)} %collective-permute-done.3, bf16[192,2560]{1,0:T(8,128)(2,1)S(1)} %copy-done.16, bf16[3,2560]{1,0:T(4,128)(2,1)S(1)} %add_convert_fusion.2, bf16[189,2560]{1,0:T(8,128)(2,1)S(1)} %copy-done.34), kind=kOutput, calls=%fused_computation.5 | convolution fusion | flops 5055447040 | bytes 18022400 | tf_op jit(solution)/shard_map/dot_general | solution.py:50
  710.3 87.1 %reduce-scatter.6.cloned.1.call-done.mlp_pair = bf16[320,3840]{1,0:T(8,128)(2,1)} async-done(((bf16[2560,3840]{1,0:T(8,128)(2,1)}), bf16[320,3840]{1,0:T(8,128)(2,1)}) %reduce-scatter.6.cloned.1.call-update) | async-done | bytes 2457616 | tf_op jit(solution)/shard_map/reduce_scatter | solution.py:822
  797.4 217.2 %scatter_gradients.1 = (bf16[80,8320]{1,0:T(8,128)(2,1)}, bf16[3,80,7680]{2,1,0:T(8,128)(2,1)}, bf16[192,2560]{1,0:T(8,128)(2,1)}) custom-call(bf16[4,320,5120]{2,1,0:T(8,128)(2,1)} %bitcast.105, bf16[4,320,2560]{2,1,0:T(8,128)(2,1)} %bitcast.109, bf16[4,320,640]{2,1,0:T(8,128)(2,1)} %fusion.53.rest, ...), custom_call_target="tpu_custom_call" | custom-call | tf_op jit(solution)/shard_map/scatter_gradients/pallas_call | solution.py:602
  1016.1 2.8 fusion.95
  1020.6 6.0 bitcast_convert_fusion
  1027.4 2.8 fusion.80
  (186 shorter events, 25.5 us)
Async XLA Ops:
  7.2 7.6 copy-start.43
  7.2 448.2 %all-gather.6.cloned.1.call-start = ((), (), s32[]{:S(2)}) async-start(), calls=%async_computation.3 | async-start | bytes 4915200 | tf_op jit(solution)/shard_map/all_gather | solution.py:801
  8.8 316.9 %copy-start.52 = (f32[192]{0:T(256)}, f32[192]{0:T(256)S(1)}, u32[]{:S(2)}) copy-start(f32[192]{0:T(256)S(1)} %fusion.87) | copy-start | bytes 2308
  325.7 13.2 %copy-start.46 = (f32[2560]{0:T(1024)}, f32[2560]{0:T(1024)S(1)}, u32[]{:S(2)}) copy-start(f32[2560]{0:T(1024)S(1)} %get-tuple-element.136) | copy-start | bytes 30724
  326.0 12.9 %copy-start.35 = (bf16[192,2560]{1,0:T(8,128)(2,1)}, bf16[192,2560]{1,0:T(8,128)(2,1)S(1)}, u32[]{:S(2)}) copy-start(bf16[192,2560]{1,0:T(8,128)(2,1)S(1)} %fusion.58) | copy-start | bytes 2949124
  338.9 10.0 collective-permute-start
  348.9 21.3 %copy-start.17 = (f32[8,2560]{1,0:T(8,128)}, f32[8,2560]{1,0:T(8,128)S(1)}, u32[]{:S(2)}) copy-start(f32[8,2560]{1,0:T(8,128)S(1)} %pad_convert_fusion.prior) | copy-start | bytes 245764
  350.2 18.0 %copy-start.38 = (f32[192,5120]{1,0:T(8,128)S(1)}, f32[192,5120]{1,0:T(8,128)}, u32[]{:S(2)}) copy-start(f32[192,5120]{1,0:T(8,128)} %get-tuple-element.197) | copy-start | bytes 11796484
  357.4 12.8 %copy-start = (f32[192,2560]{1,0:T(8,128)}, f32[192,2560]{1,0:T(8,128)S(1)}, u32[]{:S(2)}) copy-start(f32[192,2560]{1,0:T(8,128)S(1)} %get-tuple-element.42.cum) | copy-start | bytes 5898244
  357.4 12.8 %copy-start.2 = (f32[192,2560]{1,0:T(8,128)}, f32[192,2560]{1,0:T(8,128)S(1)}, u32[]{:S(2)}) copy-start(f32[192,2560]{1,0:T(8,128)S(1)} %get-tuple-element.41.local) | copy-start | bytes 5898244
  357.4 12.8 %copy-start.5 = (f32[192,2560]{1,0:T(8,128)}, f32[192,2560]{1,0:T(8,128)S(1)}, u32[]{:S(2)}) copy-start(f32[192,2560]{1,0:T(8,128)S(1)} %get-tuple-element.46.rate_pre) | copy-start | bytes 5898244
  357.4 12.8 %copy-start.8 = (f32[192,2560]{1,0:T(8,128)}, f32[192,2560]{1,0:T(8,128)S(1)}, u32[]{:S(2)}) copy-start(f32[192,2560]{1,0:T(8,128)S(1)} %get-tuple-element.50.input_pre) | copy-start | bytes 5898244
  357.4 12.8 %copy-start.13 = (bf16[192,2560]{1,0:T(8,128)(2,1)}, bf16[192,2560]{1,0:T(8,128)(2,1)S(1)}, u32[]{:S(2)}) copy-start(bf16[192,2560]{1,0:T(8,128)(2,1)S(1)} %get-tuple-element.51.conv) | copy-start | bytes 2949124
  370.2 8.0 copy-start.39
  380.7 200.7 %reduce-scatter.4.cloned.1.call-start = ((), (), s32[]{:S(2)}) async-start(), calls=%async_computation.4 | async-start | bytes 4915200 | tf_op jit(solution)/shard_map/reduce_scatter | solution.py:812
  455.4 13.4 %copy-start.54 = (bf16[768,2560]{1,0:T(8,128)(2,1)S(1)}, bf16[768,2560]{1,0:T(8,128)(2,1)}, u32[]{:S(2)}) copy-start(bf16[768,2560]{1,0:T(8,128)(2,1)} %all-gather.6.cloned.1.call-done) | copy-start | bytes 11796484
  455.4 13.4 %copy-start.55 = (f32[768,1920]{1,0:T(8,128)S(1)}, f32[768,1920]{1,0:T(8,128)}, u32[]{:S(2)}) copy-start(f32[768,1920]{1,0:T(8,128)} %fusion.18) | copy-start | bytes 17694724
  484.4 13.1 %copy-start.58 = (bf16[768,1920]{1,0:T(8,128)(2,1)}, bf16[768,1920]{1,0:T(8,128)(2,1)S(1)}, u32[]{:S(2)}) copy-start(bf16[768,1920]{1,0:T(8,128)(2,1)S(1)} %get-tuple-element.174) | copy-start | bytes 8847364
  484.4 13.1 %copy-start.56 = (bf16[768,1920]{1,0:T(8,128)(2,1)}, bf16[768,1920]{1,0:T(8,128)(2,1)S(1)}, u32[]{:S(2)}) copy-start(bf16[768,1920]{1,0:T(8,128)(2,1)S(1)} %get-tuple-element.175) | copy-start | bytes 8847364
  510.0 200.4 %reduce-scatter.8.cloned.1.call-start = ((), (), s32[]{:S(2)}) async-start(), calls=%async_computation.6 | async-start | bytes 11059200 | tf_op jit(solution)/shard_map/reduce_scatter | solution.py:823
  581.4 216.1 %reduce-scatter.6.cloned.1.call-start = ((), (), s32[]{:S(2)}) async-start(), calls=%async_computation.5 | async-start | bytes 22118400 | tf_op jit(solution)/shard_map/reduce_scatter | solution.py:822
  582.0 3.0 collective-permute-start.1
  582.1 105.5 %collective-permute-start.5 = (bf16[192,2560]{1,0:T(8,128)(2,1)}, bf16[192,2560]{1,0:T(8,128)(2,1)}, u32[]{:S(2)}, u32[]{:S(2)}) collective-permute-start(bf16[192,2560]{1,0:T(8,128)(2,1)} %copy-done.39), channel_id=1, source_target_pairs={{0,4},{4,0},{8,12},{12,8},{16,20},{20,16},{24,28},{28,24},{1,5},{5... | collective-permute-start | bytes 2949128 | tf_op jit(solution)/shard_map/ppermute | solution.py:646
  599.2 7.7 copy-start.45
  599.2 7.8 copy-start.1
  599.2 7.8 copy-start.6
  599.2 7.9 copy-start.7
  607.1 12.8 %copy-start.49 = (f32[1,2560]{1,0:T(1,128)S(1)}, f32[1,2560]{1,0:T(1,128)}, u32[]{:S(2)}) copy-start(f32[1,2560]{1,0:T(1,128)} %copy-done.48) | copy-start | bytes 30724
  607.1 23.1 %copy-start.4 = (bf16[192,2560]{1,0:T(8,128)(2,1)S(1)}, bf16[192,2560]{1,0:T(8,128)(2,1)}, u32[]{:S(2)}) copy-start(bf16[192,2560]{1,0:T(8,128)(2,1)} %slice.278.branch) | copy-start | bytes 2949124
  607.1 23.1 %copy-start.14 = (bf16[192,2560]{1,0:T(8,128)(2,1)S(1)}, bf16[192,2560]{1,0:T(8,128)(2,1)}, u32[]{:S(2)}) copy-start(bf16[192,2560]{1,0:T(8,128)(2,1)} %copy-done.13) | copy-start | bytes 2949124
  607.1 23.1 %copy-start.18 = (f32[8,2560]{1,0:T(8,128)S(1)}, f32[8,2560]{1,0:T(8,128)}, u32[]{:S(2)}) copy-start(f32[8,2560]{1,0:T(8,128)} %copy-done.17) | copy-start | bytes 245764
  619.9 25.5 %copy-start.15 = (bf16[192,2560]{1,0:T(8,128)(2,1)}, bf16[192,2560]{1,0:T(8,128)(2,1)S(1)}, u32[]{:S(2)}) copy-start(bf16[192,2560]{1,0:T(8,128)(2,1)S(1)} %get-tuple-element.54) | copy-start | bytes 2949124
  630.2 12.7 %copy-start.32 = (bf16[384,2560]{0,1:T(8,128)(2,1)S(1)}, bf16[384,2560]{0,1:T(8,128)(2,1)}, u32[]{:S(2)}) copy-start(bf16[384,2560]{0,1:T(8,128)(2,1)} %copy.82) | copy-start | bytes 5898244
  641.6 5.3 copy-start.9
  641.7 3.7 collective-permute-start.2
  644.0 37.7 %collective-permute-start.4 = (bf16[192,2560]{1,0:T(8,128)(2,1)}, bf16[192,2560]{1,0:T(8,128)(2,1)}, u32[]{:S(2)}, u32[]{:S(2)}) collective-permute-start(bf16[192,2560]{1,0:T(8,128)(2,1)} %fusion.92), channel_id=1, source_target_pairs={{0,4},{4,0},{8,12},{12,8},{16,20},{20,16},{24,28},{28,24},{1,5},{5... | collective-permute-start | bytes 2949128 | tf_op jit(solution)/shard_map/ppermute | solution.py:646
  646.9 51.6 %collective-permute-start.3 = (bf16[192,5120]{1,0:T(8,128)(2,1)}, bf16[192,5120]{1,0:T(8,128)(2,1)}, u32[]{:S(2)}, u32[]{:S(2)}) collective-permute-start(bf16[192,5120]{1,0:T(8,128)(2,1)} %pad_maximum_fusion.1), channel_id=1, source_target_pairs={{0,4},{4,0},{8,12},{12,8},{16,20},{20,16},{24,28},{28,24},{1,5},{5... | collective-permute-start | bytes 5898248 | tf_op jit(solution)/shard_map/ppermute | solution.py:646
  649.0 16.5 %copy-start.10 = (bf16[2560,256]{1,0:T(8,128)(2,1)S(1)}, bf16[2560,256]{1,0:T(8,128)(2,1)}, u32[]{:S(2)}) copy-start(bf16[2560,256]{1,0:T(8,128)(2,1)} %copy-done.9) | copy-start | bytes 3932164
  649.0 16.5 %copy-start.12 = (bf16[2560,256]{1,0:T(8,128)(2,1)S(1)}, bf16[2560,256]{1,0:T(8,128)(2,1)}, u32[]{:S(2)}) copy-start(bf16[2560,256]{1,0:T(8,128)(2,1)} %copy-done.11) | copy-start | bytes 3932164
  668.8 12.9 %copy-start.51 = (f32[192]{0:T(256)S(1)}, f32[192]{0:T(256)}, u32[]{:S(2)}) copy-start(f32[192]{0:T(256)} %copy-done.50) | copy-start | bytes 2308
  668.8 26.5 %collective-permute-start.6 = (bf16[4,320,640]{2,1,0:T(8,128)(2,1)}, bf16[4,320,640]{2,1,0:T(8,128)(2,1)}, u32[]{:S(2)}, u32[]{:S(2)}) collective-permute-start(bf16[4,320,640]{2,1,0:T(8,128)(2,1)} %dynamic-slice_bitcast_fusion), channel_id=1, source_target_pairs={{0,4},{4,0},{8,12},{12,8},{16,20},{20,16},{24,28},{28,24},{1,5},{5... | collective-permute-start | bytes 4915208 | tf_op jit(solution)/shard_map/ppermute | solution.py:646
  687.5 7.7 copy-start.24
  1020.6 6.0 copy-start.22
  1020.6 6.0 copy-start.27
  1020.6 6.0 copy-start.30
  1020.6 6.0 copy-start.31
  1020.6 6.0 copy-start.36
  1020.6 6.8 copy-start.41
  (22 other events, 56.8 us)
Sparse Core Ops, SparseCore 0:
  380.8 74.5 all-gather.5
  510.1 71.2 reduce-scatter.3
  584.9 79.2 reduce-scatter.7
  667.8 129.6 reduce-scatter.5

commit v4 on v3

--- a/solution.py
+++ b/solution.py
@@ -176,16 +176,13 @@
 
 
 def gather_kernel(
-    mixer, gate, up, down, grad, mixer_all, mlp_all, grad_all,
+    mixer, gate, up, down, mixer_all, mlp_mine,
     flow_send, flow_recv, line_send, line_recv, swap_send, swap_recv, own_sem,
 ):
     s, z, core, beside, across = places()
-    rows = mixer.shape[0]
-    mixer_cols = mixer.shape[1]
-    ff_part = mlp_all.shape[2]
-    tok = grad.shape[0]
-    mixer_cut = mixer_cols // 256 * 128
-    mlp_cut = ff_part // 256 * 128
+    rows, cols = mixer.shape
+    ff_part = mlp_mine.shape[1] // 3
+    cut = cols // 256 * 128
     diag = beside + across - s
     greet([(core, z), (beside, z), (across, z)] + [(s, (z + k) % 4) for k in range(1, 4)])
 
@@ -194,203 +191,156 @@
             src_ref=src, dst_ref=dst, send_sem=send, recv_sem=recv, device_id=target, device_id_type=MESH
         )
 
-    def span(seq, zz):
-        return pl.ds(pl.multiple_of((seq * 4 + zz) * rows, 16), rows)
-
-    def piece(kind, seq, zz, half=None):
-        if kind == 0:
-            if half is None:
-                return mixer_all.at[span(seq, zz), :]
-            cols = pl.ds(0, mixer_cut) if half == 0 else pl.ds(mixer_cut, mixer_cols - mixer_cut)
-            return mixer_all.at[span(seq, zz), cols]
+    def piece(seq, zz, half=None):
+        span = pl.ds(pl.multiple_of((seq * 4 + zz) * rows, 16), rows)
         if half is None:
-            return mlp_all.at[:, span(seq, zz), :]
-        cols = pl.ds(0, mlp_cut) if half == 0 else pl.ds(mlp_cut, ff_part - mlp_cut)
-        return mlp_all.at[:, span(seq, zz), cols]
-
-    def flow(kind, zz, index, seq, half, target, src=None):
-        ref = piece(kind, seq, zz, half)
+            return mixer_all.at[span, :]
+        return mixer_all.at[span, pl.ds(0, cut) if half == 0 else pl.ds(cut, cols - cut)]
+
+    def flow(zz, index, seq, half, target, src=None):
+        ref = piece(seq, zz, half)
         return remote(
-            ref if src is None else src, ref, flow_send.at[kind, zz, index], flow_recv.at[kind, zz, index], (target, z)
+            ref if src is None else src, ref, flow_send.at[zz, index], flow_recv.at[zz, index], (target, z)
         )
 
-    def sends(kind, zz, src=None):
+    def sends(zz, src=None):
         return [
-            flow(kind, zz, 0, s, None, beside, src),
-            flow(kind, zz, 1, s, None, across, src),
-            flow(kind, zz, 4, s, None, core, src),
+            flow(zz, 0, s, None, beside, src),
+            flow(zz, 1, s, None, across, src),
+            flow(zz, 4, s, None, core, src),
         ]
 
-    def spread(kind, zz, src=None):
-        for copy in sends(kind, zz, src):
+    def spread(zz, src=None):
+        for copy in sends(zz, src):
             copy.start()
 
-    def relay(kind, zz):
-        flow(kind, zz, 0, beside, None, beside).wait_recv()
-        flow(kind, zz, 3, beside, 0, across).start()
-        flow(kind, zz, 5, beside, None, core).start()
-        flow(kind, zz, 1, across, None, across).wait_recv()
-        flow(kind, zz, 2, across, 1, beside).start()
-        flow(kind, zz, 6, across, None, core).start()
-
-    def finish(kind, zz):
-        flow(kind, zz, 3, diag, 0, across).wait_recv()
-        flow(kind, zz, 7, diag, 0, core).start()
-        flow(kind, zz, 2, diag, 1, beside).wait_recv()
-        flow(kind, zz, 8, diag, 1, core).start()
-
-    def drain(kind, zz, src=None):
-        other = core
-        for copy in sends(kind, zz, src):
+    def relay(zz):
+        flow(zz, 0, beside, None, beside).wait_recv()
+        flow(zz, 3, beside, 0, across).start()
+        flow(zz, 5, beside, None, core).start()
+        flow(zz, 1, across, None, across).wait_recv()
+        flow(zz, 2, across, 1, beside).start()
+        flow(zz, 6, across, None, core).start()
+
+    def finish(zz):
+        flow(zz, 3, diag, 0, across).wait_recv()
+        flow(zz, 7, diag, 0, core).start()
+        flow(zz, 2, diag, 1, beside).wait_recv()
+        flow(zz, 8, diag, 1, core).start()
+
+    def drain(zz, src=None):
+        for copy in sends(zz, src):
             copy.wait_send()
-        flow(kind, zz, 3, beside, 0, across).wait_send()
-        flow(kind, zz, 5, beside, None, core).wait_send()
-        flow(kind, zz, 2, across, 1, beside).wait_send()
-        flow(kind, zz, 6, across, None, core).wait_send()
-        flow(kind, zz, 7, diag, 0, core).wait_send()
-        flow(kind, zz, 8, diag, 1, core).wait_send()
+        flow(zz, 3, beside, 0, across).wait_send()
+        flow(zz, 5, beside, None, core).wait_send()
+        flow(zz, 2, across, 1, beside).wait_send()
+        flow(zz, 6, across, None, core).wait_send()
+        flow(zz, 7, diag, 0, core).wait_send()
+        flow(zz, 8, diag, 1, core).wait_send()
         flip = core - s
-        flow(kind, zz, 4, other, None, core).wait_recv()
-        flow(kind, zz, 5, beside + flip, None, core).wait_recv()
-        flow(kind, zz, 6, across + flip, None, core).wait_recv()
-        flow(kind, zz, 7, diag + flip, 0, core).wait_recv()
-        flow(kind, zz, 8, diag + flip, 1, core).wait_recv()
-
-    def line(kind, zz, up_way, hop, src=None):
-        if kind == 0:
-            ref = mixer_all.at[span(s, zz), :]
-        else:
-            ref = grad_all.at[pl.ds(pl.multiple_of(zz * tok, 16), tok), :]
+        flow(zz, 4, core, None, core).wait_recv()
+        flow(zz, 5, beside + flip, None, core).wait_recv()
+        flow(zz, 6, across + flip, None, core).wait_recv()
+        flow(zz, 7, diag + flip, 0, core).wait_recv()
+        flow(zz, 8, diag + flip, 1, core).wait_recv()
+
+    def line(zz, up_way, hop, src=None):
+        ref = piece(s, zz)
         way = 0 if up_way else 1
         target = z + 1 if up_way else z - 1
         return remote(
-            ref if src is None else src, ref, line_send.at[kind, way, hop], line_recv.at[kind, way, hop], (s, target)
+            ref if src is None else src, ref, line_send.at[way, hop], line_recv.at[way, hop], (s, target)
         )
 
-    def line_start(kind, src):
-        pl.when(z < 3)(lambda: line(kind, z, True, 0, src).start())
-        pl.when(z > 0)(lambda: line(kind, z, False, 0, src).start())
-
-    def line_hop(kind, hop):
+    def line_hop(hop):
         def below():
-            line(kind, z - hop, True, hop - 1).wait_recv()
-
-            @pl.when(z < 3)
-            def _():
-                line(kind, z - hop, True, hop).start()
+            line(z - hop, True, hop - 1).wait_recv()
+            pl.when(z < 3)(lambda: line(z - hop, True, hop).start())
 
         def above():
-            line(kind, z + hop, False, hop - 1).wait_recv()
-
-            @pl.when(z > 0)
-            def _():
-                line(kind, z + hop, False, hop).start()
+            line(z + hop, False, hop - 1).wait_recv()
+            pl.when(z > 0)(lambda: line(z + hop, False, hop).start())
 
         pl.when(z >= hop)(below)
         pl.when(z + hop <= 3)(above)
-
-    def line_drain(kind, src):
-        pl.when(z < 3)(lambda: line(kind, z, True, 0, src).wait_send())
-        pl.when(z > 0)(lambda: line(kind, z, False, 0, src).wait_send())
-        for hop in range(1, 3):
-            pl.when((z >= hop) & (z < 3))(lambda: line(kind, z - hop, True, hop).wait_send())
-            pl.when((z + hop <= 3) & (z > 0))(lambda: line(kind, z + hop, False, hop).wait_send())
 
     def at_hop(hop, act):
         pl.when(z >= hop)(lambda: act(z - hop))
         pl.when(z + hop <= 3)(lambda: act(z + hop))
 
+    def landing(m, zz):
+        return mlp_mine.at[pl.ds(pl.multiple_of(zz * rows, 16), rows), pl.ds(m * ff_part, ff_part)]
+
+    def columns(m, zz):
+        return (gate, up, down)[m].at[:, pl.ds(pl.multiple_of(zz * ff_part, 128), ff_part)]
+
     def swap(k, m, arriving=False):
-        weight = (gate, up, down)[m]
         to = (z + k) % 4
         came = (z + 4 - k) % 4
-        cols = pl.ds(pl.multiple_of(to * ff_part, 128), ff_part)
-        dst = mlp_all.at[m, span(s, came if arriving else z), :]
-        return remote(weight.at[:, cols], dst, swap_send.at[k - 1, m], swap_recv.at[k - 1, m], (s, to))
-
-    own_cols = pl.ds(pl.multiple_of(z * ff_part, 128), ff_part)
-    local = [
-        pltpu.make_async_copy(weight.at[:, own_cols], mlp_all.at[m, span(s, z), :], own_sem.at[m])
-        for m, weight in enumerate((gate, up, down))
-    ]
-    local.append(pltpu.make_async_copy(mixer, mixer_all.at[span(s, z), :], own_sem.at[3]))
-    local.append(
-        pltpu.make_async_copy(grad, grad_all.at[pl.ds(pl.multiple_of(z * tok, 16), tok), :], own_sem.at[4])
-    )
-
-    line_start(0, mixer)
-    spread(0, z, mixer)
+        return remote(
+            columns(m, to), landing(m, came if arriving else z), swap_send.at[k - 1, m], swap_recv.at[k - 1, m], (s, to)
+        )
+
+    local = [pltpu.make_async_copy(columns(m, z), landing(m, z), own_sem.at[m]) for m in range(3)]
+    local.append(pltpu.make_async_copy(mixer, piece(s, z), own_sem.at[3]))
+
+    pl.when(z < 3)(lambda: line(z, True, 0, mixer).start())
+    pl.when(z > 0)(lambda: line(z, False, 0, mixer).start())
+    spread(z, mixer)
     for copy in local:
         copy.start()
-    line_hop(0, 1)
-    at_hop(1, lambda zz: spread(0, zz))
-    relay(0, z)
-    line_hop(0, 2)
-    at_hop(2, lambda zz: spread(0, zz))
-    finish(0, z)
-    at_hop(1, lambda zz: relay(0, zz))
-    line_hop(0, 3)
-    at_hop(3, lambda zz: spread(0, zz))
+    line_hop(1)
+    at_hop(1, spread)
+    relay(z)
+    line_hop(2)
+    at_hop(2, spread)
+    finish(z)
+    at_hop(1, relay)
+    line_hop(3)
+    at_hop(3, spread)
     for k in (1, 3, 2):
         for m in range(3):
             swap(k, m).start()
+    at_hop(1, finish)
+    at_hop(2, relay)
+    at_hop(3, relay)
+    at_hop(2, finish)
+    at_hop(3, finish)
+    drain(z, mixer)
+    for hop in range(1, 4):
+        at_hop(hop, drain)
     for copy in local:
         copy.wait()
-    spread(1, z)
-    at_hop(1, lambda zz: finish(0, zz))
-    at_hop(2, lambda zz: relay(0, zz))
-    at_hop(3, lambda zz: relay(0, zz))
-    relay(1, z)
-    at_hop(2, lambda zz: finish(0, zz))
-    at_hop(3, lambda zz: finish(0, zz))
     for k in (1, 3, 2):
         for m in range(3):
+            swap(k, m).wait_send()
             swap(k, m, True).wait_recv()
-        spread(1, (z + 4 - k) % 4)
-    line_start(1, grad)
-    finish(1, z)
-    line_hop(1, 1)
-    relay(1, (z + 3) % 4)
-    line_hop(1, 2)
-    relay(1, (z + 1) % 4)
-    finish(1, (z + 3) % 4)
-    line_hop(1, 3)
-    relay(1, (z + 2) % 4)
-    finish(1, (z + 1) % 4)
-    finish(1, (z + 2) % 4)
-    drain(0, z, mixer)
-    for hop in range(1, 4):
-        at_hop(hop, lambda zz: drain(0, zz))
-    drain(1, z)
-    for k in (1, 3, 2):
-        drain(1, (z + 4 - k) % 4)
-        for m in range(3):
-            swap(k, m).wait_send()
-    line_drain(0, mixer)
-    line_drain(1, grad)
-
-
-def gather(mixer, gate, up, down, grad):
+    pl.when(z < 3)(lambda: line(z, True, 0, mixer).wait_send())
+    pl.when(z > 0)(lambda: line(z, False, 0, mixer).wait_send())
+    for hop in range(1, 3):
+        pl.when((z >= hop) & (z < 3))(lambda: line(z - hop, True, hop).wait_send())
+        pl.when((z + hop <= 3) & (z > 0))(lambda: line(z + hop, False, hop).wait_send())
+
+
+def gather(mixer, gate, up, down):
     rows, cols = mixer.shape
-    tok, model = grad.shape
     ff_part = gate.shape[1] // 4
     anyspec = pl.BlockSpec(memory_space=pl.ANY)
     dma = pltpu.SemaphoreType.DMA
     return pl.pallas_call(
         gather_kernel,
-        in_specs=[anyspec] * 5,
-        out_specs=[anyspec] * 3,
+        in_specs=[anyspec] * 4,
+        out_specs=[anyspec] * 2,
         out_shape=[
             jax.ShapeDtypeStruct((32 * rows, cols), bf16),
-            jax.ShapeDtypeStruct((3, 32 * rows, ff_part), bf16),
-            jax.ShapeDtypeStruct((4 * tok, model), bf16),
+            jax.ShapeDtypeStruct((4 * rows, 3 * ff_part), bf16),
         ],
         scratch_shapes=[
-            dma((2, 4, 9)), dma((2, 4, 9)), dma((2, 2, 3)), dma((2, 2, 3)), dma((3, 3)), dma((3, 3)), dma((5,)),
+            dma((4, 9)), dma((4, 9)), dma((2, 3)), dma((2, 3)), dma((3, 3)), dma((3, 3)), dma((4,)),
         ],
         compiler_params=pltpu.CompilerParams(collective_id=1, has_side_effects=True),
         name="gather_weights",
-    )(mixer, gate, up, down, grad)
+    )(mixer, gate, up, down)
 
 
 def add_columns(target, sources, start, size, step):
@@ -406,8 +356,8 @@
 
 
 def scatter_kernel(
-    wide, outer, rest, mlp_pair, mlp_down, out, mixer_sum, mlp_back, out_sum,
-    held, cross, near, lined, held_out, lined_out,
+    wide, outer, rest, mlp_pair, mlp_down, mixer_sum, mlp_back,
+    held, cross, near, lined,
     load_sem, flow_send, flow_recv, line_send, line_recv, swap_send, swap_recv, own_sem,
 ):
     s, z, _, beside, across = places()
@@ -416,7 +366,6 @@
     rows = held.shape[1] // 4
     cols = held.shape[2]
     cut = cols // 256 * 128
-    tok = held_out.shape[1]
     ff_part = mlp_down.shape[1]
     parts = (wide, outer, rest)
     order = (3 * (1 - z // 2), (2 + 3 * z) % 5, 1 + z % 2, z)
@@ -474,46 +423,37 @@
             flow(i, index).wait_recv()
         add_columns(held.at[chip, span(order[i]), :], [near.at[0, i], near.at[1, i]], 0, cols, 640)
 
-    def mine(kind, k):
-        return held.at[chip, span(k), :] if kind == 0 else held_out.at[k]
-
-    def landing(kind, slot):
-        return lined.at[slot] if kind == 0 else lined_out.at[slot]
-
-    def line(kind, k, slot, target):
+    def line(k, slot, target):
         return remote(
-            mine(kind, k), landing(kind, slot), line_send.at[kind, k], line_recv.at[kind, slot], (s, target)
+            held.at[chip, span(k), :], lined.at[slot], line_send.at[k], line_recv.at[slot], (s, target)
         )
 
-    def absorb(kind, k, slot, source):
-        line(kind, k, slot, source).wait_recv()
-        if kind == 0:
-            add_columns(mine(kind, k), [landing(kind, slot)], 0, cols, 640)
-        else:
-            add_columns(mine(kind, k), [landing(kind, slot)], 0, held_out.shape[2], 512)
-
-    def chain(kind, i):
+    def absorb(k, slot, source):
+        line(k, slot, source).wait_recv()
+        add_columns(held.at[chip, span(k), :], [lined.at[slot]], 0, cols, 640)
+
+    def chain(i):
         k = order[i]
         if i == 3:
-            pl.when(z > 0)(lambda: absorb(kind, k, k, z - 1))
-            pl.when(z < 3)(lambda: absorb(kind, k, 4, z + 1))
+            pl.when(z > 0)(lambda: absorb(k, k, z - 1))
+            pl.when(z < 3)(lambda: absorb(k, 4, z + 1))
             return
 
         @pl.when(k > z)
         def _():
-            pl.when(z > 0)(lambda: absorb(kind, k, k, z - 1))
-            line(kind, k, k, z + 1).start()
+            pl.when(z > 0)(lambda: absorb(k, k, z - 1))
+            line(k, k, z + 1).start()
 
         @pl.when(k < z)
         def _():
-            pl.when(z < 3)(lambda: absorb(kind, k, k, z + 1))
-            pl.when(k == z - 1)(lambda: line(kind, k, 4, z - 1).start())
-            pl.when(k < z - 1)(lambda: line(kind, k, k, z - 1).start())
-
-    def chain_drain(kind):
+            pl.when(z < 3)(lambda: absorb(k, k, z + 1))
+            pl.when(k == z - 1)(lambda: line(k, 4, z - 1).start())
+            pl.when(k < z - 1)(lambda: line(k, k, z - 1).start())
+
+    def chain_drain():
         for i in range(3):
             k = order[i]
-            line(kind, k, k, (z + 1) % 4).wait_send()
+            line(k, k, (z + 1) % 4).wait_send()
 
     def pieces():
         for m in range(3):
@@ -536,14 +476,10 @@
         )
         for m, source, at in pieces()
     ]
-    out_load = pltpu.make_async_copy(out, held_out, own_sem.at[3])
-    out_load.start()
     for i in range(4):
         for copy in loads(i):
             copy.start()
     greet([(beside, z), (across, z)] + [(s, (z + k) % 4) for k in range(1, 4)])
-    out_load.wait()
-    chain(1, 0)
     for k in (1, 3, 2):
         for copy in swap(k):
             copy.start()
@@ -567,78 +503,71 @@
                 copy.wait()
             flow(i + 2, 0).start()
             flow(i + 2, 1).start()
-        if i + 1 < 4:
-            chain(1, i + 1)
         if i > 0:
             near_step(i - 1)
-            chain(0, i - 1)
-    out_done = pltpu.make_async_copy(held_out.at[z], out_sum, own_sem.at[4])
-    out_done.start()
+            chain(i - 1)
     near_step(3)
-    chain(0, 3)
-    done = pltpu.make_async_copy(held.at[chip, span(z), :], mixer_sum, own_sem.at[5])
+    chain(3)
+    done = pltpu.make_async_copy(held.at[chip, span(z), :], mixer_sum, own_sem.at[3])
     done.start()
     for i in range(4):
         for index in range(6):
             flow(i, index).wait_send()
-    chain_drain(0)
-    chain_drain(1)
+    chain_drain()
     for k in range(1, 4):
         for copy in swap(k):
             copy.wait()
     for copy in own:
         copy.wait()
-    out_done.wait()
     done.wait()
 
 
-def scatter(wide, outer, rest, mlp_pair, mlp_down, out):
+def scatter(wide, outer, rest, mlp_pair, mlp_down):
     rows = wide.shape[1] // 4
     cols = wide.shape[2] + outer.shape[2] + rest.shape[2]
-    _, tok, model = out.shape
     ff_part = mlp_down.shape[1]
     anyspec = pl.BlockSpec(memory_space=pl.ANY)
     dma = pltpu.SemaphoreType.DMA
     return pl.pallas_call(
         scatter_kernel,
-        in_specs=[anyspec] * 6,
-        out_specs=[anyspec] * 3,
+        in_specs=[anyspec] * 5,
+        out_specs=[anyspec] * 2,
         out_shape=[
             jax.ShapeDtypeStruct((rows, cols), bf16),
             jax.ShapeDtypeStruct((3, rows, 4 * ff_part), bf16),
-            jax.ShapeDtypeStruct((tok, model), bf16),
         ],
         scratch_shapes=[
             pltpu.VMEM((4, 4 * rows, cols), bf16),
             pltpu.VMEM((4, rows, cols), bf16),
             pltpu.VMEM((2, 4, rows, cols), bf16),
             pltpu.VMEM((5, rows, cols), bf16),
-            pltpu.VMEM((4, tok, model), bf16),
-            pltpu.VMEM((5, tok, model), bf16),
-            dma((4, 3)), dma((4, 6)), dma((4, 6)), dma((2, 4)), dma((2, 5)), dma((3, 3)), dma((3, 3)), dma((6,)),
+            dma((4, 3)), dma((4, 6)), dma((4, 6)), dma((4,)), dma((5,)), dma((3, 3)), dma((3, 3)), dma((4,)),
         ],
         compiler_params=pltpu.CompilerParams(
-            collective_id=2, has_side_effects=True, vmem_limit_bytes=60 * 1024 * 1024
+            collective_id=2, has_side_effects=True, vmem_limit_bytes=52 * 1024 * 1024
         ),
         name="scatter_gradients",
-    )(wide, outer, rest, mlp_pair, mlp_down, out)
-
-
-def gather_plain(mixer, gate, up, down, grad):
+    )(wide, outer, rest, mlp_pair, mlp_down)
+
+
+def gather_plain(mixer, gate, up, down):
     groups = lax.axis_size("fsdp")
     part_rows, ff = gate.shape
-
-    def columns(weight):
-        return jnp.transpose(weight.reshape(part_rows, groups, ff // groups), (1, 0, 2))
-
-    own = jnp.stack([columns(w) for w in (gate, up, down)], axis=1)
-    mine = lax.all_to_all(own, "fsdp", 0, 0, tiled=True)
-    mine = jnp.transpose(mine, (1, 0, 2, 3)).reshape(3, groups * part_rows, ff // groups)
-    return (
-        lax.all_gather(mixer, both, axis=0, tiled=True),
-        lax.all_gather(mine, "seq", axis=1, tiled=True),
-        lax.all_gather(grad, "fsdp", axis=0, tiled=True),
-    )
+    own = jnp.stack([w.reshape(part_rows, groups, ff // groups) for w in (gate, up, down)], axis=2)
+    mine = lax.all_to_all(jnp.transpose(own, (1, 0, 2, 3)), "fsdp", 0, 0, tiled=True)
+    return lax.all_gather(mixer, both, axis=0, tiled=True), mine.reshape(groups * part_rows, -1)
+
+
+def along_line(shard):
+    count = lax.axis_size("fsdp")
+    rows = shard.shape[0]
+    below, above = [shard], [shard]
+    for _ in range(count - 1):
+        below.append(from_behind(below[-1], "fsdp", 1))
+        above.append(from_behind(above[-1], "fsdp", -1))
+    pieces = jnp.concatenate(below[:0:-1] + above, axis=0)
+    start = (count - 1 - lax.axis_index("fsdp")) * rows
+    return lax.dynamic_slice_in_dim(pieces, start, count * rows, 0)
 
 
 def swap_cores(shard):
@@ -646,12 +575,61 @@
     return lax.ppermute(shard, "seq", [(i, i + 1 - 2 * (i % 2)) for i in range(count)])
 
 
-def scatter_paired(normed, grad_both, grad_mix, mixed, rest, pair_sum, down_sum, out_part):
+def swap_beside(shard):
+    return lax.ppermute(shard, "seq", [(i, i ^ 2) for i in range(8)])
+
+
+def swap_across(shard):
+    return lax.ppermute(shard, "seq", [(i, i ^ 4) for i in range(8)])
+
+
+def pairs(shard):
+    return jnp.concatenate([shard, swap_cores(shard)], axis=0)
+
+
+def partial_blocks(left, right):
+    place = lax.axis_index("seq")
+    blocks = jnp.transpose(left).reshape(lax.axis_size("seq"), -1, left.shape[0])
+    rows = blocks.shape[1]
+    half = rows // 2
+    core, beside, across = place % 2, (place // 2) % 2, place // 4
+
+    def block(flip_beside, flip_across, start, size):
+        x = 1 - beside if flip_beside else beside
+        y = 1 - across if flip_across else across
+        chosen = lax.dynamic_slice(
+            blocks, (y * 4 + x * 2 + core, start, 0), (1, size, blocks.shape[2])
+        )[0]
+        return mm(chosen, right, ((1,), (0,))).astype(bf16)
+
+    return (
+        block(True, True, 0, half),
+        block(True, True, half, half),
+        block(True, False, half, half),
+        block(False, True, 0, half),
+        block(True, False, 0, half),
+        block(False, True, half, half),
+        block(False, False, 0, rows),
+    )
+
+
+def sum_blocks(blocks):
+    diag_low, diag_high, beside_high, across_low, beside_low, across_high, mine = blocks
+    by_across = swap_across(diag_low)
+    by_beside = swap_beside(diag_high)
+    from_beside_high = swap_beside(beside_high)
+    from_across_low = swap_across(across_low)
+    from_beside_low = swap_beside((beside_low.astype(f32) + by_across.astype(f32)).astype(bf16))
+    from_across_high = swap_across((across_high.astype(f32) + by_beside.astype(f32)).astype(bf16))
+    half = diag_low.shape[0]
+    low = mine[:half].astype(f32) + from_across_low.astype(f32) + from_beside_low.astype(f32)
+    high = mine[half:].astype(f32) + from_across_high.astype(f32) + from_beside_high.astype(f32)
+    return jnp.concatenate([low.astype(bf16), high.astype(bf16)], axis=0)
+
+
+def scatter_paired(normed, grad_both, grad_mix, mixed, rest, pair_sum, down_sum):
     core = lax.axis_index("seq") % 2
     chips = lax.axis_size("seq") // 2
-
-    def pairs(shard):
-        return jnp.concatenate([shard, swap_cores(shard)], axis=0)
 
     def halves(values, which):
         grouped = values.reshape(values.shape[0], chips, 2, values.shape[1] // (2 * chips))
@@ -667,11 +645,10 @@
     own = lax.dynamic_index_in_dim(grouped, core, 1, False)
     other = swap_cores(lax.dynamic_index_in_dim(grouped, 1 - core, 1, False))
     rest = (own.astype(f32) + other.astype(f32)).astype(bf16)
-    groups = lax.axis_size("fsdp")
-    return scatter(wide, outer, rest, pair_sum, down_sum, out_part.reshape(groups, -1, out_part.shape[1]))
-
-
-def scatter_plain(normed, grad_both, grad_mix, mixed, rest, pair_sum, down_sum, out_part):
+    return scatter(wide, outer, rest, pair_sum, down_sum)
+
+
+def scatter_plain(normed, grad_both, grad_mix, mixed, rest, pair_sum, down_sum):
     groups = lax.axis_size("fsdp")
     term_wide = mm(normed, grad_both, ((0,), (0,))).astype(bf16)
     term_out = mm(grad_mix, mixed, ((0,), (0,))).astype(bf16)
@@ -684,7 +661,7 @@
     mlp_sum = jnp.concatenate([pair_sum, down_sum], axis=1).reshape(groups, part_rows, 3, ff_part)
     mlp_back = lax.all_to_all(mlp_sum, "fsdp", 0, 0, tiled=True)
     mlp_back = jnp.transpose(mlp_back, (2, 1, 0, 3)).reshape(3, part_rows, groups * ff_part)
-    return mixer_sum, mlp_back, lax.psum_scatter(out_part, "fsdp", scatter_dimension=0, tiled=True)
+    return mixer_sum, mlp_back
 
 
 def call_heads(kernel, width, heads, ins, outs, scratch, name):
@@ -754,9 +731,12 @@
     )
     custom = lax.axis_size("seq") == 8 and groups == 4
     if custom:
-        mixer_w, mlp_w, grad_out_all = gather(mixer_own, gate_proj, up_proj, down_proj, grad_out)
+        mixer_w, mlp_mine = gather(mixer_own, gate_proj, up_proj, down_proj)
     else:
-        mixer_w, mlp_w, grad_out_all = gather_plain(mixer_own, gate_proj, up_proj, down_proj, grad_out)
+        mixer_w, mlp_mine = gather_plain(mixer_own, gate_proj, up_proj, down_proj)
+    mlp_w = lax.all_gather(mlp_mine, "seq", axis=0, tiled=True)
+    grad_out_late = lax.optimization_barrier((grad_out, mlp_mine))[0]
+    grad_out_all = along_line(grad_out_late)
     first = lax.optimization_barrier(mixer_w[:, : 128 + 2 * width])
     wide = mixer_w[:, 128 + 2 * width : 128 + 2 * width + 2 * lru]
     proj_out = mixer_w[:, 128 + 2 * width + 2 * lru :]
@@ -798,8 +778,8 @@
     middle = tokens + mm(mixed, proj_out, ((1,), (1,)))
     normed_two = norm_rows(middle, gain_two).astype(bf16)
 
-    normed_all = lax.all_gather(normed_two, "fsdp", axis=0, tiled=True)
-    w_gate, w_up, w_down = mlp_w[0], mlp_w[1], mlp_w[2]
+    normed_all = along_line(normed_two)
+    w_gate, w_up, w_down = mlp_w[:, :ff_part], mlp_w[:, ff_part : 2 * ff_part], mlp_w[:, 2 * ff_part :]
     gate = mm(normed_all, w_gate, ((1,), (0,)))
     up_val = mm(normed_all, w_up, ((1,), (0,)))
     gelu_gate, gelu_slope = gelu_parts(gate)
@@ -813,14 +793,21 @@
         grad_normed_part.astype(bf16), "fsdp", scatter_dimension=0, tiled=True
     )
     out_part = mm(hidden, w_down, ((1,), (1,))).astype(bf16)
-    term_pair = mm(normed_all, grad_pair, ((0,), (0,))).astype(bf16)
-    term_down = mm(grad_out_all, hidden, ((0,), (0,))).astype(bf16)
-    term_pair, term_down, grad_normed_two = lax.optimization_barrier(
-        (term_pair, term_down, grad_normed_two)
-    )
+    if custom:
+        pair_blocks = partial_blocks(pairs(normed_all), pairs(grad_pair))
+        down_blocks = partial_blocks(pairs(grad_out_all), pairs(hidden))
+        pair_blocks, down_blocks, grad_normed_two = lax.optimization_barrier(
+            (pair_blocks, down_blocks, grad_normed_two)
+        )
+        pair_sum, down_sum = sum_blocks(pair_blocks), sum_blocks(down_blocks)
+    else:
+        term_pair = mm(normed_all, grad_pair, ((0,), (0,))).astype(bf16)
+        term_down = mm(grad_out_all, hidden, ((0,), (0,))).astype(bf16)
+        pair_sum = lax.psum_scatter(term_pair, "seq", scatter_dimension=0, tiled=True)
+        down_sum = lax.psum_scatter(term_down, "seq", scatter_dimension=0, tiled=True)
+    out_sum = lax.psum_scatter(out_part, "fsdp", scatter_dimension=0, tiled=True)
+    block_output = (middle + out_sum.astype(f32)).astype(bf16)[None]
     grad_normed_two = grad_normed_two.astype(f32)
-    pair_sum = lax.psum_scatter(term_pair, "seq", scatter_dimension=0, tiled=True)
-    down_sum = lax.psum_scatter(term_down, "seq", scatter_dimension=0, tiled=True)
 
     second_pull = jax.vjp(norm_rows, middle, gain_two)[1]
     grad_mid_part, grad_gain_two = second_pull(grad_normed_two)
@@ -864,12 +851,8 @@
     vectors = jnp.concatenate([sums, grad_gain_one[None], grad_gain_two[None]], axis=0).T
     vectors = jnp.pad(vectors, ((0, 0), (0, 128 - vectors.shape[1]))).astype(bf16)
     rest = jnp.concatenate([rate_w_grad, input_w_grad, vectors], axis=1)
-    if custom:
-        scattered = scatter_paired(normed, grad_both, grad_mix, mixed, rest, pair_sum, down_sum, out_part)
-    else:
-        scattered = scatter_plain(normed, grad_both, grad_mix, mixed, rest, pair_sum, down_sum, out_part)
-    mixer_sum, mlp_back, out_sum = scattered
-    block_output = (middle + out_sum.astype(f32)).astype(bf16)[None]
+    scatter_all = scatter_paired if custom else scatter_plain
+    mixer_sum, mlp_back = scatter_all(normed, grad_both, grad_mix, mixed, rest, pair_sum, down_sum)
     mlp_grads = [mlp_back[m].astype(f32) for m in range(3)]
     mixer_sum = mixer_sum.astype(f32)
     edges = [lru, 2 * lru, 3 * lru, 3 * lru + width, 3 * lru + 2 * width]

time: 1050 us -> 1150 us (1.095)
  matrix products: 189 us -> 365 us
  Pallas kernels: 553 us -> 394 us
  starting transfers between devices: 7.56 us -> 60.2 us
  local copies, waits for them, and re-layouts: 40.6 us -> 77.5 us
  waiting for transfers between devices: 178 us -> 147 us
  other arithmetic: 34.4 us -> 61.8 us
    dot_general x14 -> x26, matrix products: 189 us -> 365 us  [mm(): lax.dot_general(left, right, (dims, ((), ())), preferred_element_type=f32)]
    pallas_call x2, Pallas kernels: 522 us -> 363 us  [the longest x1 183 us: gather(): pl.pallas_call(gather_kernel, in_specs=[anyspec] * 4, out_specs=[anyspec]...]
    reduce_scatter x2 -> x1, waiting for transfers between devices: 87.1 us -> 0.02 us  [on_device(): lax.psum_scatter(out_part, 'fsdp', scatter_dimension=0, tiled=True)]
    ppermute x2 -> x14, waiting for transfers between devices: 0.01 us -> 67.9 us  [from_behind(): return lax.ppermute(shard, axis, pairs)]
    ppermute x0 -> x12, waiting for transfers between devices: none -> 66.1 us  [the longest x6 50 us: swap_beside(): return lax.ppermute(shard, 'seq', [(i, i ^ 2) for i in range(8)])]
    all_gather x1, waiting for transfers between devices: 60.9 us -> 0.01 us  [on_device(): mlp_w = lax.all_gather(mlp_mine, 'seq', axis=0, tiled=True)]
    ppermute x2 -> x14, starting transfers between devices: 3.58 us -> 44.6 us  [from_behind(): return lax.ppermute(shard, axis, pairs)]
    reduce_scatter x1, waiting for transfers between devices: 26.6 us -> 0.02 us  [on_device(): lax.psum_scatter(grad_normed_part.astype(bf16), 'fsdp', scatter_dimension...]
  transfers between devices with their start and end apart: 11 -> 38, of which waited for: 4 -> 13; matrix products, arithmetic and copies ran while one was open for 14% -> 35% of each run, Pallas kernels for 2% -> 3%
where the time goes in v4:
time: 1150 us; the launch traced here: 1140 us
  Pallas kernels  394 us (34%)
  matrix products  365 us (32%)
  waiting for transfers between devices  147 us (13%)
  local copies, waits for them, and re-layouts  77.5 us (7%)
  other arithmetic  61.8 us (5%)
  starting transfers between devices  60.2 us (5%)
  blocking collectives  20.1 us (2%)
  between operations  15.2 us (1%)
    dot_general x26, matrix products, mm(): lax.dot_general(left, right, (dims, ((), ())), preferred_element_type=f32)  365 us
    pallas_call x1, Pallas kernels, gather(): pl.pallas_call(gather_kernel, in_specs=[anyspec] * 4, out_specs=[anyspec]...  183 us
    pallas_call x1, Pallas kernels, scatter(): pl.pallas_call(scatter_kernel, in_specs=[anyspec] * 5, out_specs=[anyspec...  180 us
    ppermute x14, waiting for transfers between devices, from_behind(): return lax.ppermute(shard, axis, pairs)  67.9 us
    ppermute x6, waiting for transfers between devices, swap_beside(): return lax.ppermute(shard, 'seq', [(i, i ^ 2) for i in range(8)])  50 us
    ppermute x14, starting transfers between devices, from_behind(): return lax.ppermute(shard, axis, pairs)  44.6 us
    pallas_call x3, Pallas kernels, call_heads(): pl.pallas_call(kernel, grid=(heads,), in_specs=in_specs, out_specs=out_sp...  31.4 us
    unnamed x164, local copies, waits for them, and re-layouts  26.9 us
  transfers between devices with their start and end apart: 38, of which 13 were waited for; matrix products, arithmetic and copies ran while one was open for 35% of the time, Pallas kernels for 3%

profile of v4, /device:TPU:0, one launch (start us, length us, event | category | flops | bytes accessed | tf_op | source)
XLA Modules:
  0.0 1141.7 jit_solution(14708261473240938912)
XLA Ops:
  15.4 183.1 %gather_weights.1 = (bf16[2560,8320]{1,0:T(8,128)(2,1)}, bf16[320,5760]{1,0:T(8,128)(2,1)}) custom-call(bf16[80,8320]{1,0:T(8,128)(2,1)} %copy-done.42, bf16[80,7680]{1,0:T(8,128)(2,1)} %gate.1, bf16[80,7680]{1,0:T(8,128)(2,1)} %up.1, bf16[80,7680]{1,0:T(8,128)(2,1)} %down.1), custom_call_target="tpu_custom_call" | custom-call | tf_op jit(solution)/shard_map/gather_weights/pallas_call | solution.py:330
  198.5 8.3 collective-permute-start.8
  215.4 14.0 %fusion.135 = (bf16[192,5120]{1,0:T(8,128)(2,1)S(1)}, f32[192,5120]{1,0:T(8,128)}) fusion(bf16[192,2560]{1,0:T(8,128)(2,1)S(1)} %fusion.49, bf16[2560,8320]{1,0:T(8,128)(2,1)} %get-tuple-element.51), kind=kOutput, calls=%fused_computation.273 | convolution fusion | flops 5034147840 | bytes 33095680 | tf_op jit(solution)/shard_map/dot_general | solution.py:50
  239.2 7.2 mixer_forward.1
  247.2 11.2 all-gather.2
  260.9 10.3 multiply_reduce_fusion
  279.3 5.6 collective-permute-start.9
  286.2 13.0 %collective-permute-done.1 = bf16[192,2560]{1,0:T(8,128)(2,1)} collective-permute-done((bf16[192,2560]{1,0:T(8,128)(2,1)S(1)}, bf16[192,2560]{1,0:T(8,128)(2,1)}, u32[]{:S(2)}, u32[]{:S(2)}) %collective-permute-start.1) | collective-permute-done | bytes 983072 | tf_op jit(solution)/shard_map/ppermute | solution.py:23
  299.1 5.5 collective-permute-start.2
  305.9 14.4 %collective-permute-done.9 = bf16[192,2560]{1,0:T(8,128)(2,1)} collective-permute-done((bf16[192,2560]{1,0:T(8,128)(2,1)}, bf16[192,2560]{1,0:T(8,128)(2,1)}, u32[]{:S(2)}, u32[]{:S(2)}) %collective-permute-start.9) | collective-permute-done | bytes 983072 | tf_op jit(solution)/shard_map/ppermute | solution.py:23
  320.3 5.3 collective-permute-start.10
  327.0 14.4 %collective-permute-done.2 = bf16[192,2560]{1,0:T(8,128)(2,1)} collective-permute-done((bf16[192,2560]{1,0:T(8,128)(2,1)}, bf16[192,2560]{1,0:T(8,128)(2,1)}, u32[]{:S(2)}, u32[]{:S(2)}) %collective-permute-start.2) | collective-permute-done | bytes 983072 | tf_op jit(solution)/shard_map/ppermute | solution.py:23
  348.1 14.4 %collective-permute-done.10 = bf16[192,2560]{1,0:T(8,128)(2,1)} collective-permute-done((bf16[192,2560]{1,0:T(8,128)(2,1)}, bf16[192,2560]{1,0:T(8,128)(2,1)}, u32[]{:S(2)}, u32[]{:S(2)}) %collective-permute-start.10) | collective-permute-done | bytes 983072 | tf_op jit(solution)/shard_map/ppermute | solution.py:23
  372.3 10.8 collective-permute-done.3
  390.8 13.9 %fusion.8 = f32[768,1920]{1,0:T(8,128)} fusion(bf16[768,2560]{1,0:T(8,128)(2,1)} %constant_dynamic-slice_fusion.2, bf16[2560,5760]{1,0:T(8,128)(2,1)} %all-gather.6.cloned.1.call-done), kind=kOutput, calls=%fused_computation.13 | convolution fusion | flops 7549747200 | bytes 19660800 | tf_op jit(solution)/shard_map/dot_general | solution.py:50
  404.7 12.5 %fusion.14 = f32[768,1920]{1,0:T(8,128)} fusion(bf16[768,2560]{1,0:T(8,128)(2,1)S(1)} %copy-done.22, bf16[2560,5760]{1,0:T(8,128)(2,1)} %all-gather.6.cloned.1.call-done), kind=kOutput, calls=%fused_computation.19 | convolution fusion | flops 7549747200 | bytes 19660800 | tf_op jit(solution)/shard_map/dot_general | solution.py:50
  417.2 19.7 %fusion.30 = (bf16[768,1920]{1,0:T(8,128)(2,1)}, bf16[768,1920]{1,0:T(8,128)(2,1)}, bf16[768,1920]{1,0:T(8,128)(2,1)}) fusion(f32[768,1920]{1,0:T(8,128)} %fusion.8, f32[768,1920]{1,0:T(8,128)} %fusion.14, bf16[768,2560]{1,0:T(8,128)(2,1)S(1)} %copy-done.22, bf16[2560,5760]{1,0:T(8,128)(2,1)} %all-gather.6.cloned.1.call-done), kind=kOutput, calls=%fused_computation.37 | convolution fusion | flops 7586611200 | bytes 34406400 | tf_op jit(solution)/shard_map/dot_general | solution.py:50
  436.9 12.2 %fusion.12 = f32[768,2560]{1,0:T(8,128)S(1)} fusion(bf16[768,1920]{1,0:T(8,128)(2,1)} %get-tuple-element.196, bf16[2560,5760]{1,0:T(8,128)(2,1)} %all-gather.6.cloned.1.call-done), kind=kOutput, calls=%fused_computation.17 | convolution fusion | flops 7549747200 | bytes 20643840 | tf_op jit(solution)/shard_map/dot_general | solution.py:50
  449.1 12.4 %add_convert_fusion = bf16[768,2560]{1,0:T(8,128)(2,1)} fusion(f32[768,2560]{1,0:T(8,128)S(1)} %fusion.12, bf16[768,1920]{1,0:T(8,128)(2,1)S(1)} %copy-done.36, bf16[2560,5760]{1,0:T(8,128)(2,1)} %all-gather.6.cloned.1.call-done), kind=kOutput, calls=%fused_computation.27 | convolution fusion | flops 7553679360 | bytes 24576000 | tf_op jit(solution)/shard_map/dot_general | solution.py:50
  462.6 13.1 %collective-permute-done.18 = bf16[192,2560]{1,0:T(8,128)(2,1)} collective-permute-done((bf16[192,2560]{1,0:T(8,128)(2,1)}, bf16[192,2560]{1,0:T(8,128)(2,1)}, u32[]{:S(2)}, u32[]{:S(2)}) %collective-permute-start.18) | collective-permute-done | bytes 983072 | tf_op jit(solution)/shard_map/ppermute | solution.py:575
  482.7 5.7 pad_maximum_fusion.1
  488.9 6.9 maximum_bitcast_fusion.1
  495.8 10.7 copy.87
  506.5 7.0 maximum_bitcast_fusion
  513.5 10.7 copy.86
  524.2 13.5 %fusion.31 = bf16[768,2560]{1,0:T(8,128)(2,1)} fusion(bf16[768,1920]{1,0:T(8,128)(2,1)} %get-tuple-element.197, bf16[2560,5760]{1,0:T(8,128)(2,1)} %all-gather.6.cloned.1.call-done), kind=kOutput, calls=%fused_computation.44 | convolution fusion | flops 7551713280 | bytes 16711680 | tf_op jit(solution)/shard_map/dot_general | solution.py:50
  567.7 6.4 convolution_convert_fusion.9
  574.2 25.1 %convolution_convert_fusion.8 = bf16[160,3840]{1,0:T(8,128)(2,1)} fusion(bf16[8,320,1536]{2,1,0:T(8,128)(2,1)S(1)} %bitcast.133, s32[]{:T(128)S(6)} %select_n.258, bf16[768,3840]{1,0:T(8,128)(2,1)} %collective-permute-done.14, bf16[768,1920]{1,0:T(8,128)(2,1)S(1)} %copy-done.38, bf16[768,1920]{1,0:T(8,128)(2,1)S(1)} %copy-done.37), kind=kOutput, calls=%fused_computation.50 | convolution fusion | flops 1923440640 | bytes 13516804 | tf_op jit(solution)/shard_map/dot_general | solution.py:50
  599.3 24.8 %convolution_convert_fusion.7 = bf16[160,3840]{1,0:T(8,128)(2,1)} fusion(bf16[8,320,1536]{2,1,0:T(8,128)(2,1)S(1)} %bitcast.134, s32[]{:T(128)S(6)} %select_n.258, bf16[768,3840]{1,0:T(8,128)(2,1)} %collective-permute-done.14, bf16[768,1920]{1,0:T(8,128)(2,1)S(1)} %copy-done.38, bf16[768,1920]{1,0:T(8,128)(2,1)S(1)} %copy-done.37), kind=kOutput, calls=%fused_computation.49 | convolution fusion | flops 1923440640 | bytes 13516804 | tf_op jit(solution)/shard_map/dot_general | solution.py:50
  624.1 24.8 %convolution_convert_fusion.6 = bf16[160,3840]{1,0:T(8,128)(2,1)} fusion(bf16[8,320,1536]{2,1,0:T(8,128)(2,1)S(1)} %bitcast.135, s32[]{:T(128)S(6)} %select_n.259, bf16[768,3840]{1,0:T(8,128)(2,1)} %collective-permute-done.14, bf16[768,1920]{1,0:T(8,128)(2,1)S(1)} %copy-done.38, bf16[768,1920]{1,0:T(8,128)(2,1)S(1)} %copy-done.37), kind=kOutput, calls=%fused_computation.48 | convolution fusion | flops 1923440640 | bytes 13516804 | tf_op jit(solution)/shard_map/dot_general | solution.py:50
  648.9 25.0 %convolution_convert_fusion.5 = bf16[160,3840]{1,0:T(8,128)(2,1)} fusion(bf16[8,320,1536]{2,1,0:T(8,128)(2,1)S(1)} %bitcast.136, s32[]{:T(128)S(6)} %select_n.260, bf16[768,3840]{1,0:T(8,128)(2,1)} %collective-permute-done.14, bf16[768,1920]{1,0:T(8,128)(2,1)S(1)} %copy-done.38, bf16[768,1920]{1,0:T(8,128)(2,1)S(1)} %copy-done.37), kind=kOutput, calls=%fused_computation.47 | convolution fusion | flops 1923440640 | bytes 13516804 | tf_op jit(solution)/shard_map/dot_general | solution.py:50
  673.9 24.8 %convolution_convert_fusion.4 = bf16[160,3840]{1,0:T(8,128)(2,1)} fusion(bf16[8,320,1536]{2,1,0:T(8,128)(2,1)S(1)} %bitcast.137, s32[]{:T(128)S(6)} %select_n.259, bf16[768,3840]{1,0:T(8,128)(2,1)} %collective-permute-done.14, bf16[768,1920]{1,0:T(8,128)(2,1)S(1)} %copy-done.38, bf16[768,1920]{1,0:T(8,128)(2,1)S(1)} %copy-done.37), kind=kOutput, calls=%fused_computation.46 | convolution fusion | flops 1923440640 | bytes 13516804 | tf_op jit(solution)/shard_map/dot_general | solution.py:50
  698.8 26.2 %convolution_convert_fusion.2 = bf16[320,3840]{1,0:T(8,128)(2,1)} fusion(bf16[8,320,1536]{2,1,0:T(8,128)(2,1)S(1)} %bitcast.138, s32[]{:T(128)S(6)} %select_n.261, bf16[768,3840]{1,0:T(8,128)(2,1)} %collective-permute-done.14, bf16[768,1920]{1,0:T(8,128)(2,1)S(1)} %copy-done.38, bf16[768,1920]{1,0:T(8,128)(2,1)S(1)} %copy-done.37), kind=kOutput, calls=%fused_computation.43 | convolution fusion | flops 3811491840 | bytes 15237124 | tf_op jit(solution)/shard_map/dot_general | solution.py:50
  725.0 25.2 %convolution_convert_fusion.3 = bf16[160,3840]{1,0:T(8,128)(2,1)} fusion(bf16[8,320,1536]{2,1,0:T(8,128)(2,1)S(1)} %bitcast.139, s32[]{:T(128)S(6)} %select_n.260, bf16[768,3840]{1,0:T(8,128)(2,1)} %collective-permute-done.14, bf16[768,1920]{1,0:T(8,128)(2,1)S(1)} %copy-done.38, bf16[768,1920]{1,0:T(8,128)(2,1)S(1)} %copy-done.37), kind=kOutput, calls=%fused_computation.45 | convolution fusion | flops 1923440640 | bytes 13516804 | tf_op jit(solution)/shard_map/dot_general | solution.py:50
  756.1 6.7 fusion.4.grad_mixed
  762.9 12.8 %mixer_backward_scan.1 = (bf16[192,2560]{1,0:T(8,128)(2,1)S(1)}, f32[192,2560]{1,0:T(8,128)S(1)}, f32[192,2560]{1,0:T(8,128)S(1)}, f32[8,2560]{1,0:T(8,128)S(1)}) custom-call(f32[192,2560]{1,0:T(8,128)S(1)} %fusion.4.grad_mixed, f32[192,2560]{1,0:T(8,128)S(1)} %copy-done.7, f32[192,2560]{1,0:T(8,128)S(1)} %copy-done.6, f32[192,2560]{1,0:T(8,128)S(1)} %copy-done.1, ...), custom_call_target="tpu_custom_call" | custom-call | tf_op jit(solution)/shard_map/mixer_backward_scan/pallas_call | solution.py:680
  775.7 8.9 all-gather.3
  785.1 11.3 mixer_backward.1
  807.3 15.9 %fusion.50 = (bf16[2560]{0:T(1024)(128)(2,1)S(1)}, f32[192]{0:T(256)S(1)}, f32[192,2560]{1,0:T(8,128)}) fusion(bf16[1,192,2560]{2,1,0:T(8,128)(2,1)S(1)} %copy-done.29, f32[192]{0:T(256)S(1)} %copy-done.66, f32[2560]{0:T(1024)S(1)} %copy-done.58, bf16[192,5120]{1,0:T(8,128)(2,1)} %pad_maximum_fusion.4, bf16[2560,8320]{1,0:T(8,128)(2,1)} %get-tuple-element.51), kind=kOutput, calls=%fused_computation.89 | convolution fusion | flops 5036602880 | bytes 31146496 | tf_op jit(solution)/shard_map/dot_general | solution.py:50
  823.3 6.1 fusion.71
  844.2 7.2 convolution_convert_fusion.1
  853.8 7.9 collective-permute-done.31
  864.5 15.7 %collective-permute-done.24 = bf16[160,3840]{1,0:T(8,128)(2,1)S(1)} collective-permute-done((bf16[160,3840]{1,0:T(8,128)(2,1)}, bf16[160,3840]{1,0:T(8,128)(2,1)S(1)}, u32[]{:S(2)}, u32[]{:S(2)}) %collective-permute-start.24) | collective-permute-done | bytes 1228832 | tf_op jit(solution)/shard_map/ppermute | solution.py:583
  880.5 32.8 %collective-permute-done.26 = bf16[160,3840]{1,0:T(8,128)(2,1)S(1)} collective-permute-done((bf16[160,3840]{1,0:T(8,128)(2,1)S(1)}, bf16[160,3840]{1,0:T(8,128)(2,1)S(1)}, u32[]{:S(2)}, u32[]{:S(2)}) %collective-permute-start.26) | collective-permute-done | bytes 1228832 | tf_op jit(solution)/shard_map/ppermute | solution.py:579
  917.4 14.6 %convolution_convert_fusion = bf16[1280,5120]{1,0:T(8,128)(2,1)} fusion(bf16[384,1280]{0,1:T(8,128)(2,1)S(1)} %bitcast.151, bf16[192,5120]{1,0:T(8,128)(2,1)S(1)} %collective-permute-done.19, bf16[192,2560]{1,0:T(8,128)(2,1)S(1)} %copy-done.16, bf16[3,2560]{1,0:T(4,128)(2,1)S(1)} %add_convert_fusion.10, bf16[189,2560]{1,0:T(8,128)(2,1)S(1)} %copy-done.34), kind=kOutput, calls=%fused_computation.4 | convolution fusion | flops 5055447040 | bytes 18022400 | tf_op jit(solution)/shard_map/dot_general | solution.py:50
  932.0 9.3 collective-permute-done.25
  944.3 180.0 %scatter_gradients.1 = (bf16[80,8320]{1,0:T(8,128)(2,1)}, bf16[3,80,7680]{2,1,0:T(8,128)(2,1)}) custom-call(bf16[4,320,5120]{2,1,0:T(8,128)(2,1)} %bitcast.130, bf16[4,320,2560]{2,1,0:T(8,128)(2,1)} %bitcast.147, bf16[4,320,640]{2,1,0:T(8,128)(2,1)} %fusion.44.rest, bf16[320,3840]{1,0:T(8,128)(2,1)} %pad_maximum_fusion.3.mlp_pair, ...), custom_call_target="tpu_custom_call" | custom-call | tf_op jit(solution)/shard_map/scatter_gradients/pallas_call | solution.py:531
  1129.6 5.3 bitcast_convert_fusion
  (309 shorter events, 154.1 us)
Async XLA Ops:
  7.2 383.6 %all-gather.6.cloned.1.call-start = ((), (), s32[]{:S(2)}) async-start(), calls=%async_computation.2 | async-start | bytes 33177600 | tf_op jit(solution)/shard_map/all_gather | solution.py:737
  198.5 551.7 %reduce-scatter.5.cloned.1.call-start = ((), (), s32[]{:S(2)}) async-start(), calls=%async_computation.4 | async-start | bytes 4915200 | tf_op jit(solution)/shard_map/reduce_scatter | solution.py:792
  198.5 80.8 %collective-permute-start.8 = (bf16[192,2560]{1,0:T(8,128)(2,1)}, bf16[192,2560]{1,0:T(8,128)(2,1)}, u32[]{:S(2)}, u32[]{:S(2)}) collective-permute-start(bf16[192,2560]{1,0:T(8,128)(2,1)} %bitcast.15), channel_id=1, source_target_pairs={{0,1},{1,2},{2,3},{4,5},{5,6},{6,7},{8,9},{9,10},{10,11},{12,13},{... | collective-permute-start | bytes 2949128 | tf_op jit(solution)/shard_map/ppermute | solution.py:23
  206.9 78.0 %collective-permute-start.11 = (bf16[192,2560]{1,0:T(8,128)(2,1)}, bf16[192,2560]{1,0:T(8,128)(2,1)}, u32[]{:S(2)}, u32[]{:S(2)}) collective-permute-start(bf16[192,2560]{1,0:T(8,128)(2,1)} %bitcast.15), channel_id=1, source_target_pairs={{1,0},{2,1},{3,2},{5,4},{6,5},{7,6},{9,8},{10,9},{11,10},{13,12},{... | collective-permute-start | bytes 2949128 | tf_op jit(solution)/shard_map/ppermute | solution.py:23
  214.5 171.2 %copy-start.53 = (f32[2560]{0:T(1024)}, f32[2560]{0:T(1024)S(1)}, u32[]{:S(2)}) copy-start(f32[2560]{0:T(1024)S(1)} %get-tuple-element.157) | copy-start | bytes 30724
  230.7 7.2 collective-permute-start
  271.3 33.3 %copy-start.67 = (f32[192]{0:T(256)}, f32[192]{0:T(256)S(1)}, u32[]{:S(2)}) copy-start(f32[192]{0:T(256)S(1)} %get-tuple-element.224) | copy-start | bytes 2308
  271.3 114.4 %copy-start.61 = (f32[192]{0:T(256)}, f32[192]{0:T(256)S(1)}, u32[]{:S(2)}) copy-start(f32[192]{0:T(256)S(1)} %fusion.127) | copy-start | bytes 2308
  272.8 26.4 %collective-permute-start.1 = (bf16[192,2560]{1,0:T(8,128)(2,1)S(1)}, bf16[192,2560]{1,0:T(8,128)(2,1)}, u32[]{:S(2)}, u32[]{:S(2)}) collective-permute-start(bf16[192,2560]{1,0:T(8,128)(2,1)S(1)} %multiply_convert_fusion.2), channel_id=1, source_target_pairs={{0,1},{1,2},{2,3},{4,5},{5,6},{6,7},{8,9},{9,10},{10,11},{12,13},{... | collective-permute-start | bytes 2949128 | tf_op jit(solution)/shard_map/ppermute | solution.py:23
  278.0 26.6 %collective-permute-start.4 = (bf16[192,2560]{1,0:T(8,128)(2,1)S(1)}, bf16[192,2560]{1,0:T(8,128)(2,1)}, u32[]{:S(2)}, u32[]{:S(2)}) collective-permute-start(bf16[192,2560]{1,0:T(8,128)(2,1)S(1)} %multiply_convert_fusion.2), channel_id=1, source_target_pairs={{1,0},{2,1},{3,2},{5,4},{6,5},{7,6},{9,8},{10,9},{11,10},{13,12},{... | collective-permute-start | bytes 2949128 | tf_op jit(solution)/shard_map/ppermute | solution.py:23
  279.3 41.0 %collective-permute-start.9 = (bf16[192,2560]{1,0:T(8,128)(2,1)}, bf16[192,2560]{1,0:T(8,128)(2,1)}, u32[]{:S(2)}, u32[]{:S(2)}) collective-permute-start(bf16[192,2560]{1,0:T(8,128)(2,1)} %collective-permute-done.8), channel_id=1, source_target_pairs={{0,1},{1,2},{2,3},{4,5},{5,6},{6,7},{8,9},{9,10},{10,11},{12,13},{... | collective-permute-start | bytes 2949128 | tf_op jit(solution)/shard_map/ppermute | solution.py:23
  284.9 40.8 %collective-permute-start.12 = (bf16[192,2560]{1,0:T(8,128)(2,1)}, bf16[192,2560]{1,0:T(8,128)(2,1)}, u32[]{:S(2)}, u32[]{:S(2)}) collective-permute-start(bf16[192,2560]{1,0:T(8,128)(2,1)} %collective-permute-done.11), channel_id=1, source_target_pairs={{1,0},{2,1},{3,2},{5,4},{6,5},{7,6},{9,8},{10,9},{11,10},{13,12},{... | collective-permute-start | bytes 2949128 | tf_op jit(solution)/shard_map/ppermute | solution.py:23
  299.1 42.2 %collective-permute-start.2 = (bf16[192,2560]{1,0:T(8,128)(2,1)}, bf16[192,2560]{1,0:T(8,128)(2,1)}, u32[]{:S(2)}, u32[]{:S(2)}) collective-permute-start(bf16[192,2560]{1,0:T(8,128)(2,1)} %collective-permute-done.1), channel_id=1, source_target_pairs={{0,1},{1,2},{2,3},{4,5},{5,6},{6,7},{8,9},{9,10},{10,11},{12,13},{... | collective-permute-start | bytes 2949128 | tf_op jit(solution)/shard_map/ppermute | solution.py:23
  304.6 42.1 %collective-permute-start.5 = (bf16[192,2560]{1,0:T(8,128)(2,1)}, bf16[192,2560]{1,0:T(8,128)(2,1)}, u32[]{:S(2)}, u32[]{:S(2)}) collective-permute-start(bf16[192,2560]{1,0:T(8,128)(2,1)} %collective-permute-done.4), channel_id=1, source_target_pairs={{1,0},{2,1},{3,2},{5,4},{6,5},{7,6},{9,8},{10,9},{11,10},{13,12},{... | collective-permute-start | bytes 2949128 | tf_op jit(solution)/shard_map/ppermute | solution.py:23
  320.3 42.1 %collective-permute-start.10 = (bf16[192,2560]{1,0:T(8,128)(2,1)}, bf16[192,2560]{1,0:T(8,128)(2,1)}, u32[]{:S(2)}, u32[]{:S(2)}) collective-permute-start(bf16[192,2560]{1,0:T(8,128)(2,1)} %collective-permute-done.9), channel_id=1, source_target_pairs={{0,1},{1,2},{2,3},{4,5},{5,6},{6,7},{8,9},{9,10},{10,11},{12,13},{... | collective-permute-start | bytes 2949128 | tf_op jit(solution)/shard_map/ppermute | solution.py:23
  325.7 44.4 %collective-permute-start.13 = (bf16[192,2560]{1,0:T(8,128)(2,1)}, bf16[192,2560]{1,0:T(8,128)(2,1)S(1)}, u32[]{:S(2)}, u32[]{:S(2)}) collective-permute-start(bf16[192,2560]{1,0:T(8,128)(2,1)} %collective-permute-done.12), channel_id=1, source_target_pairs={{1,0},{2,1},{3,2},{5,4},{6,5},{7,6},{9,8},{10,9},{11,10},{13,12},{... | collective-permute-start | bytes 2949128 | tf_op jit(solution)/shard_map/ppermute | solution.py:23
  341.4 41.7 %collective-permute-start.3 = (bf16[192,2560]{1,0:T(8,128)(2,1)}, bf16[192,2560]{1,0:T(8,128)(2,1)S(1)}, u32[]{:S(2)}, u32[]{:S(2)}) collective-permute-start(bf16[192,2560]{1,0:T(8,128)(2,1)} %collective-permute-done.2), channel_id=1, source_target_pairs={{0,1},{1,2},{2,3},{4,5},{5,6},{6,7},{8,9},{9,10},{10,11},{12,13},{... | collective-permute-start | bytes 2949128 | tf_op jit(solution)/shard_map/ppermute | solution.py:23
  346.8 41.7 %collective-permute-start.6 = (bf16[192,2560]{1,0:T(8,128)(2,1)}, bf16[192,2560]{1,0:T(8,128)(2,1)S(1)}, u32[]{:S(2)}, u32[]{:S(2)}) collective-permute-start(bf16[192,2560]{1,0:T(8,128)(2,1)} %collective-permute-done.5), channel_id=1, source_target_pairs={{1,0},{2,1},{3,2},{5,4},{6,5},{7,6},{9,8},{10,9},{11,10},{13,12},{... | collective-permute-start | bytes 2949128 | tf_op jit(solution)/shard_map/ppermute | solution.py:23
  461.5 361.8 %reduce-scatter.3.cloned.1.call-start = ((), (), s32[]{:S(2)}) async-start(), calls=%async_computation.3 | async-start | bytes 4915200 | tf_op jit(solution)/shard_map/reduce_scatter | solution.py:808
  461.6 27.3 %collective-permute-start.15 = (bf16[768,2560]{1,0:T(8,128)(2,1)}, bf16[768,2560]{1,0:T(8,128)(2,1)}, u32[]{:S(2)}, u32[]{:S(2)}) collective-permute-start(bf16[768,2560]{1,0:T(8,128)(2,1)} %constant_dynamic-slice_fusion.2), channel_id=1, source_target_pairs={{0,4},{4,0},{8,12},{12,8},{16,20},{20,16},{24,28},{28,24},{1,5},{5... | collective-permute-start | bytes 11796488 | tf_op jit(solution)/shard_map/ppermute | solution.py:575
  461.6 44.9 %collective-permute-start.7 = (bf16[768,2560]{1,0:T(8,128)(2,1)}, bf16[768,2560]{1,0:T(8,128)(2,1)}, u32[]{:S(2)}, u32[]{:S(2)}) collective-permute-start(bf16[768,2560]{1,0:T(8,128)(2,1)} %constant_dynamic-slice_fusion.3), channel_id=1, source_target_pairs={{0,4},{4,0},{8,12},{12,8},{16,20},{20,16},{24,28},{28,24},{1,5},{5... | collective-permute-start | bytes 11796488 | tf_op jit(solution)/shard_map/ppermute | solution.py:575
  462.1 13.6 %collective-permute-start.18 = (bf16[192,2560]{1,0:T(8,128)(2,1)}, bf16[192,2560]{1,0:T(8,128)(2,1)}, u32[]{:S(2)}, u32[]{:S(2)}) collective-permute-start(bf16[192,2560]{1,0:T(8,128)(2,1)} %copy-done.35), channel_id=1, source_target_pairs={{0,4},{4,0},{8,12},{12,8},{16,20},{20,16},{24,28},{28,24},{1,5},{5... | collective-permute-start | bytes 2949128 | tf_op jit(solution)/shard_map/ppermute | solution.py:575
  462.2 380.9 %collective-permute-start.21 = (bf16[192,2560]{1,0:T(8,128)(2,1)}, bf16[192,2560]{1,0:T(8,128)(2,1)}, u32[]{:S(2)}, u32[]{:S(2)}) collective-permute-start(bf16[192,2560]{1,0:T(8,128)(2,1)} %copy-done.47), channel_id=1, source_target_pairs={{0,4},{4,0},{8,12},{12,8},{16,20},{20,16},{24,28},{28,24},{1,5},{5... | collective-permute-start | bytes 2949128 | tf_op jit(solution)/shard_map/ppermute | solution.py:575
  488.4 85.8 %collective-permute-start.14 = (bf16[768,3840]{1,0:T(8,128)(2,1)}, bf16[768,3840]{1,0:T(8,128)(2,1)}, u32[]{:S(2)}, u32[]{:S(2)}) collective-permute-start(bf16[768,3840]{1,0:T(8,128)(2,1)} %pad_maximum_fusion.1), channel_id=1, source_target_pairs={{0,4},{4,0},{8,12},{12,8},{16,20},{20,16},{24,28},{28,24},{1,5},{5... | collective-permute-start | bytes 17694728 | tf_op jit(solution)/shard_map/ppermute | solution.py:575
  488.4 49.3 %collective-permute-start.16 = (bf16[768,1920]{1,0:T(8,128)(2,1)}, bf16[768,1920]{1,0:T(8,128)(2,1)}, u32[]{:S(2)}, u32[]{:S(2)}) collective-permute-start(bf16[768,1920]{1,0:T(8,128)(2,1)} %get-tuple-element.197), channel_id=1, source_target_pairs={{0,4},{4,0},{8,12},{12,8},{16,20},{20,16},{24,28},{28,24},{1,5},{5... | collective-permute-start | bytes 8847368 | tf_op jit(solution)/shard_map/ppermute | solution.py:575
  725.0 25.3 %copy-start.62 = (f32[192]{0:T(256)S(1)}, f32[192]{0:T(256)}, u32[]{:S(2)}) copy-start(f32[192]{0:T(256)} %copy-done.61) | copy-start | bytes 2308
  725.0 28.1 %copy-start.68 = (f32[192]{0:T(256)S(1)}, f32[192]{0:T(256)}, u32[]{:S(2)}) copy-start(f32[192]{0:T(256)} %copy-done.67) | copy-start | bytes 2308
  775.7 30.1 %copy-start.15 = (bf16[192,2560]{1,0:T(8,128)(2,1)}, bf16[192,2560]{1,0:T(8,128)(2,1)S(1)}, u32[]{:S(2)}) copy-start(bf16[192,2560]{1,0:T(8,128)(2,1)S(1)} %get-tuple-element.65) | copy-start | bytes 2949124
  798.5 5.8 collective-permute-start.17
  800.9 35.9 %collective-permute-start.20 = (bf16[192,2560]{1,0:T(8,128)(2,1)}, bf16[192,2560]{1,0:T(8,128)(2,1)}, u32[]{:S(2)}, u32[]{:S(2)}) collective-permute-start(bf16[192,2560]{1,0:T(8,128)(2,1)} %fusion.130), channel_id=1, source_target_pairs={{0,4},{4,0},{8,12},{12,8},{16,20},{20,16},{24,28},{28,24},{1,5},{5... | collective-permute-start | bytes 2949128 | tf_op jit(solution)/shard_map/ppermute | solution.py:575
  802.2 29.3 %collective-permute-start.30 = (bf16[160,1920]{1,0:T(8,128)(2,1)}, bf16[160,1920]{1,0:T(8,128)(2,1)}, u32[]{:S(2)}, u32[]{:S(2)}) collective-permute-start(bf16[160,1920]{1,0:T(8,128)(2,1)} %convolution_convert_fusion.15), channel_id=1, source_target_pairs={{0,16},{4,20},{8,24},{12,28},{16,0},{20,4},{24,8},{28,12},{1,17},{... | collective-permute-start | bytes 1843208 | tf_op jit(solution)/shard_map/ppermute | solution.py:583
  804.1 47.3 %collective-permute-start.29 = (bf16[160,1920]{1,0:T(8,128)(2,1)}, bf16[160,1920]{1,0:T(8,128)(2,1)}, u32[]{:S(2)}, u32[]{:S(2)}) collective-permute-start(bf16[160,1920]{1,0:T(8,128)(2,1)} %convolution_convert_fusion.12), channel_id=1, source_target_pairs={{0,16},{4,20},{8,24},{12,28},{16,0},{20,4},{24,8},{28,12},{1,17},{... | collective-permute-start | bytes 1843208 | tf_op jit(solution)/shard_map/ppermute | solution.py:583
  804.3 29.1 %collective-permute-start.32 = (bf16[160,1920]{1,0:T(8,128)(2,1)}, bf16[160,1920]{1,0:T(8,128)(2,1)}, u32[]{:S(2)}, u32[]{:S(2)}) collective-permute-start(bf16[160,1920]{1,0:T(8,128)(2,1)} %convolution_convert_fusion.14), channel_id=1, source_target_pairs={{0,8},{4,12},{8,0},{12,4},{16,24},{20,28},{24,16},{28,20},{1,9},{5... | collective-permute-start | bytes 1843208 | tf_op jit(solution)/shard_map/ppermute | solution.py:579
  831.5 21.0 %collective-permute-start.34 = (bf16[160,1920]{1,0:T(8,128)(2,1)}, bf16[160,1920]{1,0:T(8,128)(2,1)}, u32[]{:S(2)}, u32[]{:S(2)}) collective-permute-start(bf16[160,1920]{1,0:T(8,128)(2,1)} %convolution_convert_fusion.13), channel_id=1, source_target_pairs={{0,8},{4,12},{8,0},{12,4},{16,24},{20,28},{24,16},{28,20},{1,9},{5... | collective-permute-start | bytes 1843208 | tf_op jit(solution)/shard_map/ppermute | solution.py:579
  833.5 28.2 %collective-permute-start.31 = (bf16[160,1920]{1,0:T(8,128)(2,1)S(1)}, bf16[160,1920]{1,0:T(8,128)(2,1)}, u32[]{:S(2)}, u32[]{:S(2)}) collective-permute-start(bf16[160,1920]{1,0:T(8,128)(2,1)S(1)} %add_convert_fusion.9), channel_id=1, source_target_pairs={{0,8},{4,12},{8,0},{12,4},{16,24},{20,28},{24,16},{28,20},{1,9},{5... | collective-permute-start | bytes 1843208 | tf_op jit(solution)/shard_map/ppermute | solution.py:579
  836.9 25.4 %collective-permute-start.33 = (bf16[160,1920]{1,0:T(8,128)(2,1)}, bf16[160,1920]{1,0:T(8,128)(2,1)}, u32[]{:S(2)}, u32[]{:S(2)}) collective-permute-start(bf16[160,1920]{1,0:T(8,128)(2,1)} %add_convert_fusion.7), channel_id=1, source_target_pairs={{0,16},{4,20},{8,24},{12,28},{16,0},{20,4},{24,8},{28,12},{1,17},{... | collective-permute-start | bytes 1843208 | tf_op jit(solution)/shard_map/ppermute | solution.py:583
  843.2 37.0 %collective-permute-start.24 = (bf16[160,3840]{1,0:T(8,128)(2,1)}, bf16[160,3840]{1,0:T(8,128)(2,1)S(1)}, u32[]{:S(2)}, u32[]{:S(2)}) collective-permute-start(bf16[160,3840]{1,0:T(8,128)(2,1)} %convolution_convert_fusion.8), channel_id=1, source_target_pairs={{0,16},{4,20},{8,24},{12,28},{16,0},{20,4},{24,8},{28,12},{1,17},{... | collective-permute-start | bytes 3686408 | tf_op jit(solution)/shard_map/ppermute | solution.py:583
  851.3 28.9 %copy-start.41 = (bf16[4,320,640]{2,1,0:T(8,128)(2,1)S(1)}, bf16[4,320,640]{2,1,0:T(8,128)(2,1)}, u32[]{:S(2)}) copy-start(bf16[4,320,640]{2,1,0:T(8,128)(2,1)} %dynamic-slice_bitcast_fusion) | copy-start | bytes 4915204
  851.3 28.9 %copy-start.44 = (bf16[160,3840]{1,0:T(8,128)(2,1)S(1)}, bf16[160,3840]{1,0:T(8,128)(2,1)}, u32[]{:S(2)}) copy-start(bf16[160,3840]{1,0:T(8,128)(2,1)} %convolution_convert_fusion.4) | copy-start | bytes 3686404
  851.4 80.7 %collective-permute-start.23 = (bf16[160,3840]{1,0:T(8,128)(2,1)}, bf16[160,3840]{1,0:T(8,128)(2,1)S(1)}, u32[]{:S(2)}, u32[]{:S(2)}) collective-permute-start(bf16[160,3840]{1,0:T(8,128)(2,1)} %convolution_convert_fusion.5), channel_id=1, source_target_pairs={{0,16},{4,20},{8,24},{12,28},{16,0},{20,4},{24,8},{28,12},{1,17},{... | collective-permute-start | bytes 3686408 | tf_op jit(solution)/shard_map/ppermute | solution.py:583
  852.5 79.5 %collective-permute-start.28 = (bf16[160,3840]{1,0:T(8,128)(2,1)S(1)}, bf16[160,3840]{1,0:T(8,128)(2,1)S(1)}, u32[]{:S(2)}, u32[]{:S(2)}) collective-permute-start(bf16[160,3840]{1,0:T(8,128)(2,1)S(1)} %copy-done.69), channel_id=1, source_target_pairs={{0,8},{4,12},{8,0},{12,4},{16,24},{20,28},{24,16},{28,20},{1,9},{5... | collective-permute-start | bytes 3686408 | tf_op jit(solution)/shard_map/ppermute | solution.py:579
  861.7 51.6 %collective-permute-start.26 = (bf16[160,3840]{1,0:T(8,128)(2,1)S(1)}, bf16[160,3840]{1,0:T(8,128)(2,1)S(1)}, u32[]{:S(2)}, u32[]{:S(2)}) collective-permute-start(bf16[160,3840]{1,0:T(8,128)(2,1)S(1)} %copy-done.70), channel_id=1, source_target_pairs={{0,8},{4,12},{8,0},{12,4},{16,24},{20,28},{24,16},{28,20},{1,9},{5... | collective-permute-start | bytes 3686408 | tf_op jit(solution)/shard_map/ppermute | solution.py:579
  862.3 55.1 %collective-permute-start.19 = (bf16[192,5120]{1,0:T(8,128)(2,1)S(1)}, bf16[192,5120]{1,0:T(8,128)(2,1)S(1)}, u32[]{:S(2)}, u32[]{:S(2)}) collective-permute-start(bf16[192,5120]{1,0:T(8,128)(2,1)S(1)} %copy-done.40), channel_id=1, source_target_pairs={{0,4},{4,0},{8,12},{12,8},{16,20},{20,16},{24,28},{28,24},{1,5},{5... | collective-permute-start | bytes 5898248 | tf_op jit(solution)/shard_map/ppermute | solution.py:575
  864.4 49.3 %copy-start.43 = (bf16[160,3840]{1,0:T(8,128)(2,1)S(1)}, bf16[160,3840]{1,0:T(8,128)(2,1)}, u32[]{:S(2)}) copy-start(bf16[160,3840]{1,0:T(8,128)(2,1)} %convolution_convert_fusion.3) | copy-start | bytes 3686404
  864.5 51.3 %copy-start.24 = (bf16[2560,640]{1,0:T(8,128)(2,1)S(1)}, bf16[2560,640]{1,0:T(8,128)(2,1)}, u32[]{:S(2)}) copy-start(bf16[2560,640]{1,0:T(8,128)(2,1)} %copy-done.23) | copy-start | bytes 9830404
  880.2 33.8 %collective-permute-start.22 = (bf16[4,320,640]{2,1,0:T(8,128)(2,1)S(1)}, bf16[4,320,640]{2,1,0:T(8,128)(2,1)S(1)}, u32[]{:S(2)}, u32[]{:S(2)}) collective-permute-start(bf16[4,320,640]{2,1,0:T(8,128)(2,1)S(1)} %copy-done.41), channel_id=1, source_target_pairs={{0,4},{4,0},{8,12},{12,8},{16,20},{20,16},{24,28},{28,24},{1,5},{5... | collective-permute-start | bytes 4915208 | tf_op jit(solution)/shard_map/ppermute | solution.py:575
  913.3 28.0 %collective-permute-start.25 = (bf16[160,3840]{1,0:T(8,128)(2,1)S(1)}, bf16[160,3840]{1,0:T(8,128)(2,1)S(1)}, u32[]{:S(2)}, u32[]{:S(2)}) collective-permute-start(bf16[160,3840]{1,0:T(8,128)(2,1)S(1)} %add_convert_fusion.4), channel_id=1, source_target_pairs={{0,8},{4,12},{8,0},{12,4},{16,24},{20,28},{24,16},{28,20},{1,9},{5... | collective-permute-start | bytes 3686408 | tf_op jit(solution)/shard_map/ppermute | solution.py:579
  914.1 27.7 %collective-permute-start.27 = (bf16[160,3840]{1,0:T(8,128)(2,1)S(1)}, bf16[160,3840]{1,0:T(8,128)(2,1)S(1)}, u32[]{:S(2)}, u32[]{:S(2)}) collective-permute-start(bf16[160,3840]{1,0:T(8,128)(2,1)S(1)} %add_convert_fusion.2), channel_id=1, source_target_pairs={{0,16},{4,20},{8,24},{12,28},{16,0},{20,4},{24,8},{28,12},{1,17},{... | collective-permute-start | bytes 3686408 | tf_op jit(solution)/shard_map/ppermute | solution.py:583
  (63 other events, 585.3 us)
Sparse Core Ops, SparseCore 0:
  198.6 148.7 all-gather.5
  461.6 74.4 reduce-scatter.4
  538.5 73.6 reduce-scatter.2

commit v5 on v4

--- a/solution.py
+++ b/solution.py
@@ -343,6 +343,181 @@
     )(mixer, gate, up, down)
 
 
+def rows_kernel(
+    normed, grad0, grad1, grad2, grad3, normed_all, normed_other, grad_all, grad_other,
+    line_send, line_recv, core_send, core_recv, own_sem,
+):
+    s, z, core, _, _ = places()
+    tok = normed.shape[0]
+    grads = (grad0, grad1, grad2, grad3)
+    greet([(core, z)] + [(s, (z + k) % 4) for k in range(1, 4)])
+
+    def rows(ref, zz):
+        return ref.at[pl.ds(pl.multiple_of(zz * tok, 16), tok), :]
+
+    def remote(src, dst, send, recv, target):
+        return pltpu.make_async_remote_copy(
+            src_ref=src, dst_ref=dst, send_sem=send, recv_sem=recv, device_id=target, device_id_type=MESH
+        )
+
+    def line(zz, up_way, hop):
+        way = 0 if up_way else 1
+        target = z + 1 if up_way else z - 1
+        src = normed if hop == 0 else rows(normed_all, zz)
+        return remote(src, rows(normed_all, zz), line_send.at[way, hop], line_recv.at[way, hop], (s, target))
+
+    def over(zz, own=False):
+        src = normed if own else rows(normed_all, zz)
+        return remote(src, rows(normed_other, zz), core_send.at[0, zz], core_recv.at[0, zz], (core, z))
+
+    def grad_over(k):
+        zz = (z + 4 - k) % 4
+        return remote(grads[k], rows(grad_other, zz), core_send.at[1, zz], core_recv.at[1, zz], (core, z))
+
+    def hop_step(hop):
+        def below():
+            line(z - hop, True, hop - 1).wait_recv()
+            pl.when(z < 3)(lambda: line(z - hop, True, hop).start())
+            over(z - hop).start()
+
+        def above():
+            line(z + hop, False, hop - 1).wait_recv()
+            pl.when(z > 0)(lambda: line(z + hop, False, hop).start())
+            over(z + hop).start()
+
+        pl.when(z >= hop)(below)
+        pl.when(z + hop <= 3)(above)
+
+    local = [
+        pltpu.make_async_copy(grads[k], rows(grad_all, (z + 4 - k) % 4), own_sem.at[k]) for k in range(4)
+    ]
+    local.append(pltpu.make_async_copy(normed, rows(normed_all, z), own_sem.at[4]))
+    pl.when(z < 3)(lambda: line(z, True, 0).start())
+    pl.when(z > 0)(lambda: line(z, False, 0).start())
+    over(z, True).start()
+    for copy in local:
+        copy.start()
+    for k in range(4):
+        grad_over(k).start()
+    for hop in range(1, 4):
+        hop_step(hop)
+    for copy in local:
+        copy.wait()
+    for k in range(4):
+        grad_over(k).wait()
+    over(z, True).wait()
+    for k in range(1, 4):
+        over((z + k) % 4).wait()
+    pl.when(z < 3)(lambda: line(z, True, 0).wait_send())
+    pl.when(z > 0)(lambda: line(z, False, 0).wait_send())
+    for hop in range(1, 3):
+        pl.when((z >= hop) & (z < 3))(lambda: line(z - hop, True, hop).wait_send())
+        pl.when((z + hop <= 3) & (z > 0))(lambda: line(z + hop, False, hop).wait_send())
+
+
+def gather_rows(normed, grads):
+    tok, model = normed.shape
+    anyspec = pl.BlockSpec(memory_space=pl.ANY)
+    dma = pltpu.SemaphoreType.DMA
+    return pl.pallas_call(
+        rows_kernel,
+        in_specs=[anyspec] * 5,
+        out_specs=[anyspec] * 4,
+        out_shape=[jax.ShapeDtypeStruct((4 * tok, model), bf16)] * 4,
+        scratch_shapes=[dma((2, 3)), dma((2, 3)), dma((2, 4)), dma((2, 4)), dma((5,))],
+        compiler_params=pltpu.CompilerParams(collective_id=3, has_side_effects=True),
+        name="gather_rows",
+    )(normed, *grads)
+
+
+def products_kernel(sides, tile, cuts, place, *refs):
+    lefts = 1 + max(side for side, _ in sides)
+    left_refs = refs[: 2 * lefts]
+    right_refs = refs[2 * lefts : 2 * lefts + 2 * len(sides)]
+    outs = refs[2 * lefts + 2 * len(sides) : -3]
+    turned, stage, right = refs[-3:]
+    tok = left_refs[0].shape[0]
+    chip_cols = left_refs[0].shape[1] // 4
+    half = chip_cols // 2
+    step = pl.program_id(0)
+
+    @pl.when(step == 0)
+    def _():
+        for side in range(lefts):
+            for q in range(4):
+                cols = pl.ds(pl.multiple_of(place[q] * chip_cols, 128), chip_cols)
+                stage[:, :] = jnp.concatenate(
+                    [left_refs[2 * side][:, cols], left_refs[2 * side + 1][:, cols]], axis=0
+                ).T
+                turned[side, q] = stage[pl.ds(pl.multiple_of(place[4] * half, 16), half), :]
+
+    first = 0
+    side_now = 0
+    for n, (side, tiles) in enumerate(sides):
+
+        @pl.when((step >= first) & (step < first + tiles))
+        def _(n=n):
+            right[0:tok, :] = right_refs[2 * n][...]
+            right[tok:, :] = right_refs[2 * n + 1][...]
+
+        side_now = jnp.where(step >= first, side, side_now)
+        first += tiles
+
+    start, index, inside = 0, 0, 0
+    for q in range(4):
+        block = mm(turned[side_now, q], right[...], ((1,), (0,))).astype(bf16)
+        taken = 0
+        while taken < half:
+            size = min(cuts[index] - inside, half - taken)
+            outs[index][inside : inside + size, :] = block[taken : taken + size]
+            taken += size
+            inside += size
+            if inside == cuts[index]:
+                index, inside = index + 1, 0
+
+
+def products(lefts, rights, cuts, name):
+    seq = lax.axis_index("seq")
+    core, x, y = seq % 2, (seq // 2) % 2, seq // 4
+    place = jnp.stack([(1 - y) * 2 + 1 - x, y * 2 + 1 - x, (1 - y) * 2 + x, y * 2 + x, core]).astype(jnp.int32)
+    tile = 640
+    tok, model = lefts[0][0].shape
+    sides = tuple((side, own.shape[1] // tile) for side, own, _ in rights)
+    total = sum(tiles for _, tiles in sides)
+    in_specs = [
+        pl.BlockSpec((tok, model), lambda j, place: (0, 0), pipeline_mode=pl.Buffered(1))
+    ] * (2 * len(lefts))
+    first = 0
+    for _, tiles in sides:
+
+        def index(j, place, first=first, tiles=tiles):
+            return (0, jnp.clip(j - first, 0, tiles - 1))
+
+        in_specs += [pl.BlockSpec((tok, tile), index)] * 2
+        first += tiles
+    half = model // 8
+    return pl.pallas_call(
+        functools.partial(products_kernel, sides, tile, cuts),
+        grid_spec=pltpu.PrefetchScalarGridSpec(
+            num_scalar_prefetch=1,
+            grid=(total,),
+            in_specs=in_specs,
+            out_specs=[pl.BlockSpec((rows, tile), lambda j, place: (0, j)) for rows in cuts],
+            scratch_shapes=[
+                pltpu.VMEM((len(lefts), 4, half, 2 * tok), bf16),
+                pltpu.VMEM((2 * half, 2 * tok), bf16),
+                pltpu.VMEM((2 * tok, tile), bf16),
+            ],
+        ),
+        out_shape=[jax.ShapeDtypeStruct((rows, total * tile), bf16) for rows in cuts],
+        compiler_params=pltpu.CompilerParams(vmem_limit_bytes=56 * 1024 * 1024),
+        cost_estimate=pl.CostEstimate(
+            flops=2 * 4 * half * 2 * tok * total * tile, bytes_accessed=4 * half * total * tile * 2, transcendentals=0
+        ),
+        name=name,
+    )(place, *[a for pair in lefts for a in pair], *[a for _, own, other in rights for a in (own, other)])
+
+
 def add_columns(target, sources, start, size, step):
     def one(turn, carry):
         cols = pl.ds(pl.multiple_of(start + turn * step, 128), step)
@@ -356,18 +531,17 @@
 
 
 def scatter_kernel(
-    wide, outer, rest, mlp_pair, mlp_down, mixer_sum, mlp_back,
+    main, rest, mlp, mixer_sum, mlp_back,
     held, cross, near, lined,
     load_sem, flow_send, flow_recv, line_send, line_recv, swap_send, swap_recv, own_sem,
 ):
     s, z, _, beside, across = places()
-    chip, chip_beside, chip_across = s // 2, beside // 2, across // 2
-    chip_diag = chip_beside + chip_across - chip
+    chip_diag, chip_beside, chip_across, chip = 0, 1, 2, 3
     rows = held.shape[1] // 4
     cols = held.shape[2]
     cut = cols // 256 * 128
-    ff_part = mlp_down.shape[1]
-    parts = (wide, outer, rest)
+    ff_part = mlp.shape[1] // 3
+    parts = (main, rest)
     order = (3 * (1 - z // 2), (2 + 3 * z) % 5, 1 + z % 2, z)
 
     def remote(src, dst, send, recv, target):
@@ -457,8 +631,7 @@
 
     def pieces():
         for m in range(3):
-            source = mlp_down if m == 2 else mlp_pair
-            yield m, source, pl.ds(0 if m == 2 else m * ff_part, ff_part)
+            yield m, mlp, pl.ds(m * ff_part, ff_part)
 
     def swap(k):
         to = (z + k) % 4
@@ -522,15 +695,15 @@
     done.wait()
 
 
-def scatter(wide, outer, rest, mlp_pair, mlp_down):
-    rows = wide.shape[1] // 4
-    cols = wide.shape[2] + outer.shape[2] + rest.shape[2]
-    ff_part = mlp_down.shape[1]
+def scatter(main, rest, mlp):
+    rows = main.shape[1] // 4
+    cols = main.shape[2] + rest.shape[2]
+    ff_part = mlp.shape[1] // 3
     anyspec = pl.BlockSpec(memory_space=pl.ANY)
     dma = pltpu.SemaphoreType.DMA
     return pl.pallas_call(
         scatter_kernel,
-        in_specs=[anyspec] * 5,
+        in_specs=[anyspec] * 3,
         out_specs=[anyspec] * 2,
         out_shape=[
             jax.ShapeDtypeStruct((rows, cols), bf16),
@@ -541,13 +714,13 @@
             pltpu.VMEM((4, rows, cols), bf16),
             pltpu.VMEM((2, 4, rows, cols), bf16),
             pltpu.VMEM((5, rows, cols), bf16),
-            dma((4, 3)), dma((4, 6)), dma((4, 6)), dma((4,)), dma((5,)), dma((3, 3)), dma((3, 3)), dma((4,)),
+            dma((4, 2)), dma((4, 6)), dma((4, 6)), dma((4,)), dma((5,)), dma((3, 3)), dma((3, 3)), dma((4,)),
         ],
         compiler_params=pltpu.CompilerParams(
             collective_id=2, has_side_effects=True, vmem_limit_bytes=52 * 1024 * 1024
         ),
         name="scatter_gradients",
-    )(wide, outer, rest, mlp_pair, mlp_down)
+    )(main, rest, mlp)
 
 
 def gather_plain(mixer, gate, up, down):
@@ -558,16 +731,11 @@
     return lax.all_gather(mixer, both, axis=0, tiled=True), mine.reshape(groups * part_rows, -1)
 
 
-def along_line(shard):
+def from_line(shard):
     count = lax.axis_size("fsdp")
-    rows = shard.shape[0]
-    below, above = [shard], [shard]
-    for _ in range(count - 1):
-        below.append(from_behind(below[-1], "fsdp", 1))
-        above.append(from_behind(above[-1], "fsdp", -1))
-    pieces = jnp.concatenate(below[:0:-1] + above, axis=0)
-    start = (count - 1 - lax.axis_index("fsdp")) * rows
-    return lax.dynamic_slice_in_dim(pieces, start, count * rows, 0)
+    return [shard] + [
+        lax.ppermute(shard, "fsdp", [(i, (i + k) % count) for i in range(count)]) for k in range(1, count)
+    ]
 
 
 def swap_cores(shard):
@@ -583,38 +751,8 @@
     return lax.ppermute(shard, "seq", [(i, i ^ 4) for i in range(8)])
 
 
-def pairs(shard):
-    return jnp.concatenate([shard, swap_cores(shard)], axis=0)
-
-
-def partial_blocks(left, right):
-    place = lax.axis_index("seq")
-    blocks = jnp.transpose(left).reshape(lax.axis_size("seq"), -1, left.shape[0])
-    rows = blocks.shape[1]
-    half = rows // 2
-    core, beside, across = place % 2, (place // 2) % 2, place // 4
-
-    def block(flip_beside, flip_across, start, size):
-        x = 1 - beside if flip_beside else beside
-        y = 1 - across if flip_across else across
-        chosen = lax.dynamic_slice(
-            blocks, (y * 4 + x * 2 + core, start, 0), (1, size, blocks.shape[2])
-        )[0]
-        return mm(chosen, right, ((1,), (0,))).astype(bf16)
-
-    return (
-        block(True, True, 0, half),
-        block(True, True, half, half),
-        block(True, False, half, half),
-        block(False, True, 0, half),
-        block(True, False, 0, half),
-        block(False, True, half, half),
-        block(False, False, 0, rows),
-    )
-
-
 def sum_blocks(blocks):
-    diag_low, diag_high, beside_high, across_low, beside_low, across_high, mine = blocks
+    diag_low, diag_high, beside_low, beside_high, across_low, across_high, mine = blocks
     by_across = swap_across(diag_low)
     by_beside = swap_beside(diag_high)
     from_beside_high = swap_beside(beside_high)
@@ -627,28 +765,34 @@
     return jnp.concatenate([low.astype(bf16), high.astype(bf16)], axis=0)
 
 
-def scatter_paired(normed, grad_both, grad_mix, mixed, rest, pair_sum, down_sum):
-    core = lax.axis_index("seq") % 2
-    chips = lax.axis_size("seq") // 2
-
-    def halves(values, which):
-        grouped = values.reshape(values.shape[0], chips, 2, values.shape[1] // (2 * chips))
-        return lax.dynamic_index_in_dim(grouped, which, 2, False).reshape(values.shape[0], -1)
-
-    def product(left, right):
-        result = mm(halves(left, core), right, ((0,), (0,))).astype(bf16)
-        return result.reshape(chips, -1, right.shape[1])
-
-    wide = product(pairs(normed), pairs(grad_both))
-    outer = product(pairs(grad_mix), pairs(mixed))
-    grouped = rest.reshape(chips, 2, -1, rest.shape[1])
+def scatter_paired(normed, grad_both, grad_mix, mixed, rest, mlp_sum):
+    seq = lax.axis_index("seq")
+    core, x, y = seq % 2, (seq // 2) % 2, seq // 4
+    main = products(
+        [(normed, swap_cores(normed)), (grad_mix, swap_cores(grad_mix))],
+        [(0, grad_both, swap_cores(grad_both)), (1, mixed, swap_cores(mixed))],
+        (lru_rows(normed),),
+        "mixer_products",
+    )[0]
+    grouped = rest.reshape(4, 2, -1, rest.shape[1])
     own = lax.dynamic_index_in_dim(grouped, core, 1, False)
     other = swap_cores(lax.dynamic_index_in_dim(grouped, 1 - core, 1, False))
     rest = (own.astype(f32) + other.astype(f32)).astype(bf16)
-    return scatter(wide, outer, rest, pair_sum, down_sum)
-
-
-def scatter_plain(normed, grad_both, grad_mix, mixed, rest, pair_sum, down_sum):
+    rest = jnp.concatenate(
+        [
+            lax.dynamic_slice_in_dim(rest, q, 1, 0)
+            for q in ((1 - y) * 2 + 1 - x, y * 2 + 1 - x, (1 - y) * 2 + x, y * 2 + x)
+        ],
+        axis=0,
+    )
+    return scatter(main.reshape(4, -1, main.shape[1]), rest, mlp_sum)
+
+
+def lru_rows(values):
+    return values.shape[1] // 2
+
+
+def scatter_plain(normed, grad_both, grad_mix, mixed, rest, mlp_sum):
     groups = lax.axis_size("fsdp")
     term_wide = mm(normed, grad_both, ((0,), (0,))).astype(bf16)
     term_out = mm(grad_mix, mixed, ((0,), (0,))).astype(bf16)
@@ -656,9 +800,9 @@
         jnp.concatenate([term_wide, term_out, rest], axis=1), "seq", scatter_dimension=0, tiled=True
     )
     mixer_sum = lax.psum_scatter(mixer_sum, "fsdp", scatter_dimension=0, tiled=True)
-    ff_part = down_sum.shape[1]
-    part_rows = down_sum.shape[0] // groups
-    mlp_sum = jnp.concatenate([pair_sum, down_sum], axis=1).reshape(groups, part_rows, 3, ff_part)
+    ff_part = mlp_sum.shape[1] // 3
+    part_rows = mlp_sum.shape[0] // groups
+    mlp_sum = mlp_sum.reshape(groups, part_rows, 3, ff_part)
     mlp_back = lax.all_to_all(mlp_sum, "fsdp", 0, 0, tiled=True)
     mlp_back = jnp.transpose(mlp_back, (2, 1, 0, 3)).reshape(3, part_rows, groups * ff_part)
     return mixer_sum, mlp_back
@@ -736,7 +880,8 @@
         mixer_w, mlp_mine = gather_plain(mixer_own, gate_proj, up_proj, down_proj)
     mlp_w = lax.all_gather(mlp_mine, "seq", axis=0, tiled=True)
     grad_out_late = lax.optimization_barrier((grad_out, mlp_mine))[0]
-    grad_out_all = along_line(grad_out_late)
+    if custom:
+        grad_pieces = from_line(grad_out_late)
     first = lax.optimization_barrier(mixer_w[:, : 128 + 2 * width])
     wide = mixer_w[:, 128 + 2 * width : 128 + 2 * width + 2 * lru]
     proj_out = mixer_w[:, 128 + 2 * width + 2 * lru :]
@@ -778,7 +923,11 @@
     middle = tokens + mm(mixed, proj_out, ((1,), (1,)))
     normed_two = norm_rows(middle, gain_two).astype(bf16)
 
-    normed_all = along_line(normed_two)
+    if custom:
+        normed_all, normed_other, grad_out_all, grad_out_other = gather_rows(normed_two, grad_pieces)
+    else:
+        normed_all = lax.all_gather(normed_two, "fsdp", axis=0, tiled=True)
+        grad_out_all = lax.all_gather(grad_out_late, "fsdp", axis=0, tiled=True)
     w_gate, w_up, w_down = mlp_w[:, :ff_part], mlp_w[:, ff_part : 2 * ff_part], mlp_w[:, 2 * ff_part :]
     gate = mm(normed_all, w_gate, ((1,), (0,)))
     up_val = mm(normed_all, w_up, ((1,), (0,)))
@@ -787,24 +936,32 @@
     grad_hidden = mm(grad_out_all, w_down, ((1,), (0,)))
     grad_gate = (grad_hidden * up_val * gelu_slope).astype(bf16)
     grad_up = (grad_hidden * gelu_gate).astype(bf16)
-    grad_pair = jnp.concatenate([grad_gate, grad_up], axis=1)
     grad_normed_part = mm(grad_gate, w_gate, ((1,), (1,))) + mm(grad_up, w_up, ((1,), (1,)))
     grad_normed_two = lax.psum_scatter(
         grad_normed_part.astype(bf16), "fsdp", scatter_dimension=0, tiled=True
     )
     out_part = mm(hidden, w_down, ((1,), (1,))).astype(bf16)
     if custom:
-        pair_blocks = partial_blocks(pairs(normed_all), pairs(grad_pair))
-        down_blocks = partial_blocks(pairs(grad_out_all), pairs(hidden))
-        pair_blocks, down_blocks, grad_normed_two = lax.optimization_barrier(
-            (pair_blocks, down_blocks, grad_normed_two)
+        half = model // 16
+        blocks = products(
+            [(normed_all, normed_other), (grad_out_all, grad_out_other)],
+            [
+                (0, grad_gate, swap_cores(grad_gate)),
+                (0, grad_up, swap_cores(grad_up)),
+                (1, hidden, swap_cores(hidden)),
+            ],
+            (half,) * 6 + (2 * half,),
+            "feed_forward_products",
         )
-        pair_sum, down_sum = sum_blocks(pair_blocks), sum_blocks(down_blocks)
+        blocks, grad_normed_two = lax.optimization_barrier((blocks, grad_normed_two))
+        mlp_sum = sum_blocks(blocks)
     else:
+        grad_pair = jnp.concatenate([grad_gate, grad_up], axis=1)
         term_pair = mm(normed_all, grad_pair, ((0,), (0,))).astype(bf16)
         term_down = mm(grad_out_all, hidden, ((0,), (0,))).astype(bf16)
         pair_sum = lax.psum_scatter(term_pair, "seq", scatter_dimension=0, tiled=True)
         down_sum = lax.psum_scatter(term_down, "seq", scatter_dimension=0, tiled=True)
+        mlp_sum = jnp.concatenate([pair_sum, down_sum], axis=1)
     out_sum = lax.psum_scatter(out_part, "fsdp", scatter_dimension=0, tiled=True)
     block_output = (middle + out_sum.astype(f32)).astype(bf16)[None]
     grad_normed_two = grad_normed_two.astype(f32)
@@ -852,7 +1009,7 @@
     vectors = jnp.pad(vectors, ((0, 0), (0, 128 - vectors.shape[1]))).astype(bf16)
     rest = jnp.concatenate([rate_w_grad, input_w_grad, vectors], axis=1)
     scatter_all = scatter_paired if custom else scatter_plain
-    mixer_sum, mlp_back = scatter_all(normed, grad_both, grad_mix, mixed, rest, pair_sum, down_sum)
+    mixer_sum, mlp_back = scatter_all(normed, grad_both, grad_mix, mixed, rest, mlp_sum)
     mlp_grads = [mlp_back[m].astype(f32) for m in range(3)]
     mixer_sum = mixer_sum.astype(f32)
     edges = [lru, 2 * lru, 3 * lru, 3 * lru + width, 3 * lru + 2 * width]

time: 1150 us -> 976 us (0.85)
  matrix products: 365 us -> 129 us
  Pallas kernels: 394 us -> 626 us
  waiting for transfers between devices: 147 us -> 79.4 us
  local copies, waits for them, and re-layouts: 77.5 us -> 32.5 us
  starting transfers between devices: 60.2 us -> 21.7 us
  other arithmetic: 61.8 us -> 43.4 us
    dot_general x26 -> x10, matrix products: 365 us -> 129 us  [mm(): lax.dot_general(left, right, (dims, ((), ())), preferred_element_type=f32)]
    pallas_call x1 -> x4, Pallas kernels: 180 us -> 411 us  [the longest x1 177 us: scatter(): pl.pallas_call(scatter_kernel, in_specs=[anyspec] * 3, out_specs=[anyspec...]
    ppermute x14 -> x2, waiting for transfers between devices: 67.9 us -> 0.01 us  [from_behind(): return lax.ppermute(shard, axis, pairs)]
    ppermute x14 -> x2, starting transfers between devices: 44.6 us -> 2.71 us  [from_behind(): return lax.ppermute(shard, axis, pairs)]
    transpose x2 -> x0, local copies, waits for them, and re-layouts: 21.4 us -> none  [partial_blocks(): jnp.transpose(left).reshape(lax.axis_size('seq'), -1, left.shape[0])]
    transpose x2 -> x0, other arithmetic: 13.9 us -> none  [partial_blocks(): jnp.transpose(left).reshape(lax.axis_size('seq'), -1, left.shape[0])]
    ppermute x9 -> x8, waiting for transfers between devices: 13.2 us -> 0.02 us  [swap_cores(): lax.ppermute(shard, 'seq', [(i, i + 1 - 2 * (i % 2)) for i in range(count)])]
    reduce_scatter x1, waiting for transfers between devices: 0.02 us -> 12.3 us  [on_device(): lax.psum_scatter(grad_normed_part.astype(bf16), 'fsdp', scatter_dimension...]
  transfers between devices with their start and end apart: 38 -> 22, of which waited for: 13 -> 5; matrix products, arithmetic and copies ran while one was open for 35% -> 11% of each run, Pallas kernels for 3% -> 27%
where the time goes in v5:
time: 976 us; the launch traced here: 968 us
  Pallas kernels  626 us (64%)
  matrix products  129 us (13%)
  waiting for transfers between devices  79.4 us (8%)
  other arithmetic  43.4 us (4%)
  local copies, waits for them, and re-layouts  32.5 us (3%)
  starting transfers between devices  21.7 us (2%)
  blocking collectives  21 us (2%)
  between operations  15.1 us (2%)
    pallas_call x1, Pallas kernels, gather(): pl.pallas_call(gather_kernel, in_specs=[anyspec] * 4, out_specs=[anyspec]...  183 us
    pallas_call x1, Pallas kernels, scatter(): pl.pallas_call(scatter_kernel, in_specs=[anyspec] * 3, out_specs=[anyspec...  177 us
    pallas_call x1, Pallas kernels, gather_rows(): pl.pallas_call(rows_kernel, in_specs=[anyspec] * 5, out_specs=[anyspec] *...  166 us
    dot_general x10, matrix products, mm(): lax.dot_general(left, right, (dims, ((), ())), preferred_element_type=f32)  129 us
    pallas_call x2, Pallas kernels, products(): pl.pallas_call(functools.partial(products_kernel, sides, tile, cuts), gri...  67.8 us
    ppermute x3, waiting for transfers between devices, swap_beside(): return lax.ppermute(shard, 'seq', [(i, i ^ 2) for i in range(8)])  40.1 us
    pallas_call x3, Pallas kernels, call_heads(): pl.pallas_call(kernel, grid=(heads,), in_specs=in_specs, out_specs=out_sp...  31.5 us
    ppermute x3, waiting for transfers between devices, swap_across(): return lax.ppermute(shard, 'seq', [(i, i ^ 4) for i in range(8)])  26.9 us
  transfers between devices with their start and end apart: 22, of which 5 were waited for; matrix products, arithmetic and copies ran while one was open for 11% of the time, Pallas kernels for 27%

profile of v5, /device:TPU:0, one launch (start us, length us, event | category | flops | bytes accessed | tf_op | source)
XLA Modules:
  0.0 967.9 jit_solution(8791708755898864852)
XLA Ops:
  14.4 183.1 %gather_weights.1 = (bf16[2560,8320]{1,0:T(8,128)(2,1)}, bf16[320,5760]{1,0:T(8,128)(2,1)}) custom-call(bf16[80,8320]{1,0:T(8,128)(2,1)} %copy-done.35, bf16[80,7680]{1,0:T(8,128)(2,1)} %gate.1, bf16[80,7680]{1,0:T(8,128)(2,1)} %up.1, bf16[80,7680]{1,0:T(8,128)(2,1)} %down.1), custom_call_target="tpu_custom_call" | custom-call | tf_op jit(solution)/shard_map/gather_weights/pallas_call | solution.py:330
  197.6 5.4 collective-permute-start.1
  203.0 3.4 collective-permute-start.2
  206.4 2.3 slice.218
  209.9 2.8 slice_reduce_fusion
  213.9 14.6 %fusion.75 = (bf16[192,5120]{1,0:T(8,128)(2,1)S(1)}, f32[192,5120]{1,0:T(8,128)}) fusion(bf16[192,2560]{1,0:T(8,128)(2,1)} %fusion.42.refs_0_, bf16[2560,8320]{1,0:T(8,128)(2,1)} %get-tuple-element.55), kind=kOutput, calls=%fused_computation.172 | convolution fusion | flops 5034147840 | bytes 33095680 | tf_op jit(solution)/shard_map/dot_general | solution.py:50
  231.1 1.7 copy.77
  233.7 2.1 fusion.72
  238.4 7.2 mixer_forward.1
  246.4 11.8 %all-gather.2 = f32[8,2,2560]{2,1,0:T(2,128)S(1)} all-gather(f32[1,2,2560]{2,1,0:T(2,128)S(1)} %fusion.62), channel_id=2, replica_groups=mesh['seq'=8,'fsdp'=4] {'seq'}, dimensions={0}, use_global_device_ids=true | all-gather | bytes 184320 | tf_op jit(solution)/shard_map/all_gather | solution.py:29
  258.6 2.0 fusion.71
  260.7 9.8 %multiply_reduce_fusion = (f32[192]{0:T(256)S(1)}, f32[192,2560]{1,0:T(8,128)S(1)}) fusion(bf16[192,2560]{1,0:T(8,128)(2,1)S(1)} %get-tuple-element.207.refs_6_, bf16[2560,8320]{1,0:T(8,128)(2,1)} %get-tuple-element.55, bf16[1,192,2560]{2,1,0:T(8,128)(2,1)S(1)} %copy-done.27), kind=kOutput, calls=%fused_computation.82 | convolution fusion | flops 2518548224 | bytes 17040128 | tf_op jit(solution)/shard_map/dot_general | solution.py:50
  273.0 166.3 %gather_rows.1 = (bf16[768,2560]{1,0:T(8,128)(2,1)}, bf16[768,2560]{1,0:T(8,128)(2,1)}, bf16[768,2560]{1,0:T(8,128)(2,1)}, bf16[768,2560]{1,0:T(8,128)(2,1)}) custom-call(bf16[192,2560]{1,0:T(8,128)(2,1)} %multiply_convert_fusion.2.normed, bf16[192,2560]{1,0:T(8,128)(2,1)} %bitcast.14.grad0, bf16[192,2560]{1,0:T(8,128)(2,1)} %collective-permute-done.1.grad1, ...), custom_call_target="tpu_custom_call" | custom-call | tf_op jit(solution)/shard_map/gather_rows/pallas_call | solution.py:422
  439.4 12.4 %fusion.18 = f32[768,1920]{1,0:T(8,128)S(1)} fusion(bf16[768,2560]{1,0:T(8,128)(2,1)} %get-tuple-element.60.refs_0_, bf16[2560,5760]{1,0:T(8,128)(2,1)} %all-gather.6.cloned.1.call-done), kind=kOutput, calls=%fused_computation.20 | convolution fusion | flops 7549747200 | bytes 19660800 | tf_op jit(solution)/shard_map/dot_general | solution.py:50
  451.9 12.9 %fusion.14 = f32[768,1920]{1,0:T(8,128)} fusion(bf16[768,2560]{1,0:T(8,128)(2,1)S(1)} %copy-done.50, bf16[2560,5760]{1,0:T(8,128)(2,1)} %all-gather.6.cloned.1.call-done), kind=kOutput, calls=%fused_computation.16 | convolution fusion | flops 7549747200 | bytes 19660800 | tf_op jit(solution)/shard_map/dot_general | solution.py:50
  464.7 17.4 %multiply_convert_fusion = (bf16[768,1920]{1,0:T(8,128)(2,1)S(1)}, bf16[768,1920]{1,0:T(8,128)(2,1)S(1)}, bf16[768,1920]{1,0:T(8,128)(2,1)}) fusion(f32[768,1920]{1,0:T(8,128)S(1)} %fusion.18, f32[768,1920]{1,0:T(8,128)} %fusion.14, bf16[768,2560]{1,0:T(8,128)(2,1)S(1)} %copy-done.51, bf16[2560,5760]{1,0:T(8,128)(2,1)} %all-gather.6.cloned.1.call-done), kind=kOutput, calls=%fused_computation.33 | convolution fusion | flops 7586611200 | bytes 34406400 | tf_op jit(solution)/shard_map/dot_general | solution.py:50
  482.1 13.1 %fusion.12 = f32[768,2560]{1,0:T(8,128)S(1)} fusion(bf16[768,1920]{1,0:T(8,128)(2,1)S(1)} %get-tuple-element.203.refs_6_, bf16[2560,5760]{1,0:T(8,128)(2,1)} %all-gather.6.cloned.1.call-done), kind=kOutput, calls=%fused_computation.14 | convolution fusion | flops 7549747200 | bytes 20643840 | tf_op jit(solution)/shard_map/dot_general | solution.py:50
  495.2 12.5 %add_convert_fusion = bf16[768,2560]{1,0:T(8,128)(2,1)} fusion(f32[768,2560]{1,0:T(8,128)S(1)} %fusion.12, bf16[768,1920]{1,0:T(8,128)(2,1)S(1)} %get-tuple-element.204.refs_4_, bf16[2560,5760]{1,0:T(8,128)(2,1)} %all-gather.6.cloned.1.call-done), kind=kOutput, calls=%fused_computation.22 | convolution fusion | flops 7553679360 | bytes 24576000 | tf_op jit(solution)/shard_map/dot_general | solution.py:50
  509.0 13.4 %fusion.31 = bf16[768,2560]{1,0:T(8,128)(2,1)} fusion(bf16[768,1920]{1,0:T(8,128)(2,1)} %get-tuple-element.205.refs_8_, bf16[2560,5760]{1,0:T(8,128)(2,1)} %all-gather.6.cloned.1.call-done), kind=kOutput, calls=%fused_computation.36 | convolution fusion | flops 7551713280 | bytes 16711680 | tf_op jit(solution)/shard_map/dot_general | solution.py:50
  522.4 44.9 %feed_forward_products.1 = (bf16[160,5760]{1,0:T(8,128)(2,1)}, bf16[160,5760]{1,0:T(8,128)(2,1)}, bf16[160,5760]{1,0:T(8,128)(2,1)}, bf16[160,5760]{1,0:T(8,128)...) custom-call(s32[5]{0:T(128)} %stack.64.place, ...), custom_call_target="tpu_custom_call" | custom-call | flops 22649241600 | bytes 14745600 | tf_op jit(solution)/shard_map/feed_forward_products/pallas_call | solution.py:499
  567.3 12.3 %reduce-scatter.5.cloned.1.call-done = bf16[192,2560]{1,0:T(8,128)(2,1)} async-done(((bf16[768,2560]{1,0:T(8,128)(2,1)}), bf16[192,2560]{1,0:T(8,128)(2,1)}) %reduce-scatter.5.cloned.1.call-update) | async-done | bytes 983056 | tf_op jit(solution)/shard_map/reduce_scatter | solution.py:940
  579.6 2.8 fusion.45
  582.4 2.0 fusion.70.refs_2_
  584.4 7.3 fusion.4.grad_mixed
  592.0 13.0 %mixer_backward_scan.1 = (bf16[192,2560]{1,0:T(8,128)(2,1)S(1)}, f32[192,2560]{1,0:T(8,128)S(1)}, f32[192,2560]{1,0:T(8,128)S(1)}, f32[8,2560]{1,0:T(8,128)S(1)}) custom-call(f32[192,2560]{1,0:T(8,128)S(1)} %fusion.4.grad_mixed, f32[192,2560]{1,0:T(8,128)S(1)} %copy-done.7, f32[192,2560]{1,0:T(8,128)S(1)} %copy-done.6, f32[192,2560]{1,0:T(8,128)S(1)} %copy-done.1, ...), custom_call_target="tpu_custom_call" | custom-call | tf_op jit(solution)/shard_map/mixer_backward_scan/pallas_call | solution.py:824
  605.1 9.2 all-gather.3
  614.8 11.2 %mixer_backward.1 = (f32[192,2560]{1,0:T(8,128)S(1)}, f32[8,2560]{1,0:T(8,128)S(1)}, bf16[2560,256]{1,0:T(8,128)(2,1)S(1)}, bf16[2560,256]{1,0:T(8,128)(2,1)S(1)}, f32[8,2560]{1,0:T(8,128)S(1)}) custom-call(f32[192,2560]{1,0:T(8,128)S(1)} %get-tuple-element.73.rev_cum, f32[192,2560]{1,0:T(8,128)S(1)} %get-tuple-element.74.rev_grad, ...), custom_call_target="tpu_custom_call" | custom-call | tf_op jit(solution)/shard_map/mixer_backward/pallas_call | solution.py:824
  632.6 1.6 slice.430
  634.3 2.6 collective-permute-start.14
  638.4 1.5 pad_maximum_fusion.1.refs_4_
  639.9 15.9 %fusion.43 = (bf16[2560]{0:T(1024)(128)(2,1)S(1)}, f32[192]{0:T(256)S(1)}, f32[192,2560]{1,0:T(8,128)}) fusion(bf16[1,192,2560]{2,1,0:T(8,128)(2,1)} %param.17, f32[192]{0:T(256)S(1)} %copy-done.49, f32[2560]{0:T(1024)S(1)} %copy-done.43, bf16[192,5120]{1,0:T(8,128)(2,1)} %pad_maximum_fusion.1.refs_4_, bf16[2560,8320]{1,0:T(8,128)(2,1)} %get-tuple-element.55), kind=kOutput, calls=%fused_computation.61 | convolution fusion | flops 5036602880 | bytes 31146496 | tf_op jit(solution)/shard_map/dot_general | solution.py:50
  656.6 1.6 copy-done.23
  658.4 19.5 %collective-permute-done.14 = bf16[160,5760]{1,0:T(8,128)(2,1)} collective-permute-done((bf16[160,5760]{1,0:T(8,128)(2,1)}, bf16[160,5760]{1,0:T(8,128)(2,1)}, u32[]{:S(2)}, u32[]{:S(2)}) %collective-permute-start.14) | collective-permute-done | bytes 1843232 | tf_op jit(solution)/shard_map/ppermute | solution.py:751
  677.9 3.2 add_convert_fusion.4
  681.6 3.3 add_convert_fusion.2
  684.9 1.7 collective-permute-start.13
  687.2 1.5 collective-permute-start.15
  689.0 5.5 fusion.61
  694.6 1.8 fusion.37
  698.0 22.9 %mixer_products.1 = bf16[1280,7680]{1,0:T(8,128)(2,1)} custom-call(s32[5]{0:T(128)} %stack.64.place, bf16[192,2560]{1,0:T(8,128)(2,1)} %fusion.42.refs_0_, bf16[192,2560]{1,0:T(8,128)(2,1)} %collective-permute-done.8.refs_1_, bf16[192,2560]{1,0:T(8,128)(2,1)} %copy-done.31, bf16[192,2560]{1,0:T(8,128)(2,1)} %collective-permute-done.9.refs_3_, ...), custom_call_target="tpu_custom_call" | custom-call | flops 7549747200 | bytes 19660800 | tf_op jit(solution)/shard_map/mixer_products/pallas_call | solution.py:499
  720.9 7.4 collective-permute-done.13
  728.3 1.8 collective-permute-done.18
  730.1 38.3 %collective-permute-done.15 = bf16[160,5760]{1,0:T(8,128)(2,1)} collective-permute-done((bf16[160,5760]{1,0:T(8,128)(2,1)}, bf16[160,5760]{1,0:T(8,128)(2,1)}, u32[]{:S(2)}, u32[]{:S(2)}) %collective-permute-start.15) | collective-permute-done | bytes 1843232 | tf_op jit(solution)/shard_map/ppermute | solution.py:747
  768.4 4.5 add_convert_fusion.3
  772.9 2.1 pad_maximum_fusion.mlp
  775.0 176.8 %scatter_gradients.1 = (bf16[80,8320]{1,0:T(8,128)(2,1)S(1)}, bf16[3,80,7680]{2,1,0:T(8,128)(2,1)}) custom-call(bf16[4,320,7680]{2,1,0:T(8,128)(2,1)} %bitcast.77, bf16[4,320,640]{2,1,0:T(8,128)(2,1)} %pad_maximum_fusion.2.rest, bf16[320,5760]{1,0:T(8,128)(2,1)} %pad_maximum_fusion.mlp), custom_call_target="tpu_custom_call" | custom-call | tf_op jit(solution)/shard_map/scatter_gradients/pallas_call | solution.py:704
  952.0 1.5 fusion.73
  955.7 5.3 bitcast_convert_fusion
  (197 shorter events, 35.6 us)
Async XLA Ops:
  7.2 432.2 %all-gather.6.cloned.1.call-start = ((), (), s32[]{:S(2)}) async-start(), calls=%async_computation.2 | async-start | bytes 33177600 | tf_op jit(solution)/shard_map/all_gather | solution.py:881
  197.5 382.1 %reduce-scatter.5.cloned.1.call-start = ((), (), s32[]{:S(2)}) async-start(), calls=%async_computation.4 | async-start | bytes 4915200 | tf_op jit(solution)/shard_map/reduce_scatter | solution.py:940
  197.6 75.4 %collective-permute-start.1 = (bf16[192,2560]{1,0:T(8,128)(2,1)}, bf16[192,2560]{1,0:T(8,128)(2,1)}, u32[]{:S(2)}, u32[]{:S(2)}) collective-permute-start(bf16[192,2560]{1,0:T(8,128)(2,1)} %bitcast.14.grad0), channel_id=1, source_target_pairs={{0,1},{1,2},{2,3},{3,0},{4,5},{5,6},{6,7},{7,4},{8,9},{9,10},{10,1... | collective-permute-start | bytes 2949128 | tf_op jit(solution)/shard_map/ppermute | solution.py:737
  203.0 70.0 %collective-permute-start.2 = (bf16[192,2560]{1,0:T(8,128)(2,1)}, bf16[192,2560]{1,0:T(8,128)(2,1)}, u32[]{:S(2)}, u32[]{:S(2)}) collective-permute-start(bf16[192,2560]{1,0:T(8,128)(2,1)} %bitcast.14.grad0), channel_id=1, source_target_pairs={{0,2},{1,3},{2,0},{3,1},{4,6},{5,7},{6,4},{7,5},{8,10},{9,11},{10,... | collective-permute-start | bytes 2949128 | tf_op jit(solution)/shard_map/ppermute | solution.py:737
  206.4 66.6 %collective-permute-start.3 = (bf16[192,2560]{1,0:T(8,128)(2,1)}, bf16[192,2560]{1,0:T(8,128)(2,1)}, u32[]{:S(2)}, u32[]{:S(2)}) collective-permute-start(bf16[192,2560]{1,0:T(8,128)(2,1)} %bitcast.14.grad0), channel_id=1, source_target_pairs={{0,3},{1,0},{2,1},{3,2},{4,7},{5,4},{6,5},{7,6},{8,11},{9,8},{10,9... | collective-permute-start | bytes 2949128 | tf_op jit(solution)/shard_map/ppermute | solution.py:737
  229.8 7.3 collective-permute-start
  237.1 9.3 copy-start.17
  238.4 20.3 %copy-start.36 = (f32[192,5120]{1,0:T(8,128)S(1)}, f32[192,5120]{1,0:T(8,128)}, u32[]{:S(2)}) copy-start(f32[192,5120]{1,0:T(8,128)} %get-tuple-element.233) | copy-start | bytes 11796484
  245.6 15.1 %copy-start = (f32[192,2560]{1,0:T(8,128)}, f32[192,2560]{1,0:T(8,128)S(1)}, u32[]{:S(2)}) copy-start(f32[192,2560]{1,0:T(8,128)S(1)} %get-tuple-element.57.cum) | copy-start | bytes 5898244
  245.6 15.1 %copy-start.2 = (f32[192,2560]{1,0:T(8,128)}, f32[192,2560]{1,0:T(8,128)S(1)}, u32[]{:S(2)}) copy-start(f32[192,2560]{1,0:T(8,128)S(1)} %get-tuple-element.56.local) | copy-start | bytes 5898244
  245.6 15.0 %copy-start.5 = (f32[192,2560]{1,0:T(8,128)}, f32[192,2560]{1,0:T(8,128)S(1)}, u32[]{:S(2)}) copy-start(f32[192,2560]{1,0:T(8,128)S(1)} %get-tuple-element.72.rate_pre) | copy-start | bytes 5898244
  245.6 15.0 %copy-start.8 = (f32[192,2560]{1,0:T(8,128)}, f32[192,2560]{1,0:T(8,128)S(1)}, u32[]{:S(2)}) copy-start(f32[192,2560]{1,0:T(8,128)S(1)} %get-tuple-element.76.input_pre) | copy-start | bytes 5898244
  245.6 15.0 %copy-start.13 = (bf16[192,2560]{1,0:T(8,128)(2,1)}, bf16[192,2560]{1,0:T(8,128)(2,1)S(1)}, u32[]{:S(2)}) copy-start(bf16[192,2560]{1,0:T(8,128)(2,1)S(1)} %get-tuple-element.77.conv) | copy-start | bytes 2949124
  260.7 9.9 %copy-start.30 = (bf16[192,2560]{1,0:T(8,128)(2,1)}, bf16[192,2560]{1,0:T(8,128)(2,1)S(1)}, u32[]{:S(2)}) copy-start(bf16[192,2560]{1,0:T(8,128)(2,1)S(1)} %get-tuple-element.207.refs_6_) | copy-start | bytes 2949124
  439.4 12.4 %copy-start.50 = (bf16[768,2560]{1,0:T(8,128)(2,1)S(1)}, bf16[768,2560]{1,0:T(8,128)(2,1)}, u32[]{:S(2)}) copy-start(bf16[768,2560]{1,0:T(8,128)(2,1)} %get-tuple-element.60.refs_0_) | copy-start | bytes 11796484
  451.9 12.9 %copy-start.51 = (bf16[768,2560]{1,0:T(8,128)(2,1)S(1)}, bf16[768,2560]{1,0:T(8,128)(2,1)}, u32[]{:S(2)}) copy-start(bf16[768,2560]{1,0:T(8,128)(2,1)} %get-tuple-element.62.refs_2_) | copy-start | bytes 11796484
  482.1 13.1 %copy-start.52 = (bf16[768,1920]{1,0:T(8,128)(2,1)}, bf16[768,1920]{1,0:T(8,128)(2,1)S(1)}, u32[]{:S(2)}) copy-start(bf16[768,1920]{1,0:T(8,128)(2,1)S(1)} %get-tuple-element.203.refs_6_) | copy-start | bytes 8847364
  482.1 13.1 %copy-start.53 = (bf16[768,1920]{1,0:T(8,128)(2,1)}, bf16[768,1920]{1,0:T(8,128)(2,1)S(1)}, u32[]{:S(2)}) copy-start(bf16[768,1920]{1,0:T(8,128)(2,1)S(1)} %get-tuple-element.204.refs_4_) | copy-start | bytes 8847364
  507.7 181.3 %reduce-scatter.3.cloned.1.call-start = ((), (), s32[]{:S(2)}) async-start(), calls=%async_computation.3 | async-start | bytes 4915200 | tf_op jit(solution)/shard_map/reduce_scatter | solution.py:965
  507.8 14.7 %collective-permute-start.4 = (bf16[768,1920]{1,0:T(8,128)(2,1)}, bf16[768,1920]{1,0:T(8,128)(2,1)}, u32[]{:S(2)}, u32[]{:S(2)}) collective-permute-start(bf16[768,1920]{1,0:T(8,128)(2,1)} %copy-done.53), channel_id=1, source_target_pairs={{0,4},{4,0},{8,12},{12,8},{16,20},{20,16},{24,28},{28,24},{1,5},{5... | collective-permute-start | bytes 8847368 | tf_op jit(solution)/shard_map/ppermute | solution.py:743
  507.8 14.6 %collective-permute-start.5 = (bf16[768,1920]{1,0:T(8,128)(2,1)}, bf16[768,1920]{1,0:T(8,128)(2,1)}, u32[]{:S(2)}, u32[]{:S(2)}) collective-permute-start(bf16[768,1920]{1,0:T(8,128)(2,1)} %copy-done.52), channel_id=1, source_target_pairs={{0,4},{4,0},{8,12},{12,8},{16,20},{20,16},{24,28},{28,24},{1,5},{5... | collective-permute-start | bytes 8847368 | tf_op jit(solution)/shard_map/ppermute | solution.py:743
  508.3 14.1 %collective-permute-start.6 = (bf16[768,1920]{1,0:T(8,128)(2,1)}, bf16[768,1920]{1,0:T(8,128)(2,1)}, u32[]{:S(2)}, u32[]{:S(2)}) collective-permute-start(bf16[768,1920]{1,0:T(8,128)(2,1)} %get-tuple-element.205.refs_8_), channel_id=1, source_target_pairs={{0,4},{4,0},{8,12},{12,8},{16,20},{20,16},{24,28},{28,24},{1,5},{5... | collective-permute-start | bytes 8847368 | tf_op jit(solution)/shard_map/ppermute | solution.py:743
  584.4 7.4 copy-start.1
  584.4 7.6 copy-start.7
  592.0 13.1 %copy-start.45 = (f32[1,2560]{1,0:T(1,128)S(1)}, f32[1,2560]{1,0:T(1,128)}, u32[]{:S(2)}) copy-start(f32[1,2560]{1,0:T(1,128)} %copy-done.44) | copy-start | bytes 30724
  592.0 22.8 %copy-start.4 = (bf16[192,2560]{1,0:T(8,128)(2,1)S(1)}, bf16[192,2560]{1,0:T(8,128)(2,1)}, u32[]{:S(2)}) copy-start(bf16[192,2560]{1,0:T(8,128)(2,1)} %slice.286.branch) | copy-start | bytes 2949124
  592.0 22.8 %copy-start.14 = (bf16[192,2560]{1,0:T(8,128)(2,1)S(1)}, bf16[192,2560]{1,0:T(8,128)(2,1)}, u32[]{:S(2)}) copy-start(bf16[192,2560]{1,0:T(8,128)(2,1)} %copy-done.13) | copy-start | bytes 2949124
  592.0 22.8 %copy-start.18 = (f32[8,2560]{1,0:T(8,128)S(1)}, f32[8,2560]{1,0:T(8,128)}, u32[]{:S(2)}) copy-start(f32[8,2560]{1,0:T(8,128)} %copy-done.17) | copy-start | bytes 245764
  605.1 21.0 %copy-start.15 = (bf16[192,2560]{1,0:T(8,128)(2,1)}, bf16[192,2560]{1,0:T(8,128)(2,1)S(1)}, u32[]{:S(2)}) copy-start(bf16[192,2560]{1,0:T(8,128)(2,1)S(1)} %get-tuple-element.80) | copy-start | bytes 2949124
  629.5 8.9 copy-start.16
  629.5 7.4 collective-permute-start.7
  630.9 54.0 %collective-permute-start.8 = (bf16[192,2560]{1,0:T(8,128)(2,1)}, bf16[192,2560]{1,0:T(8,128)(2,1)}, u32[]{:S(2)}, u32[]{:S(2)}) collective-permute-start(bf16[192,2560]{1,0:T(8,128)(2,1)} %fusion.42.refs_0_), channel_id=1, source_target_pairs={{0,4},{4,0},{8,12},{12,8},{16,20},{20,16},{24,28},{28,24},{1,5},{5... | collective-permute-start | bytes 2949128 | tf_op jit(solution)/shard_map/ppermute | solution.py:743
  632.1 54.6 %collective-permute-start.11 = (bf16[192,2560]{1,0:T(8,128)(2,1)}, bf16[192,2560]{1,0:T(8,128)(2,1)}, u32[]{:S(2)}, u32[]{:S(2)}) collective-permute-start(bf16[192,2560]{1,0:T(8,128)(2,1)} %copy-done.30), channel_id=1, source_target_pairs={{0,4},{4,0},{8,12},{12,8},{16,20},{20,16},{24,28},{28,24},{1,5},{5... | collective-permute-start | bytes 2949128 | tf_op jit(solution)/shard_map/ppermute | solution.py:743
  632.2 55.0 %collective-permute-start.9 = (bf16[192,2560]{1,0:T(8,128)(2,1)}, bf16[192,2560]{1,0:T(8,128)(2,1)}, u32[]{:S(2)}, u32[]{:S(2)}) collective-permute-start(bf16[192,2560]{1,0:T(8,128)(2,1)} %copy-done.31), channel_id=1, source_target_pairs={{0,4},{4,0},{8,12},{12,8},{16,20},{20,16},{24,28},{28,24},{1,5},{5... | collective-permute-start | bytes 2949128 | tf_op jit(solution)/shard_map/ppermute | solution.py:743
  634.3 43.6 %collective-permute-start.14 = (bf16[160,5760]{1,0:T(8,128)(2,1)}, bf16[160,5760]{1,0:T(8,128)(2,1)}, u32[]{:S(2)}, u32[]{:S(2)}) collective-permute-start(bf16[160,5760]{1,0:T(8,128)(2,1)} %get-tuple-element.87), channel_id=1, source_target_pairs={{0,16},{4,20},{8,24},{12,28},{16,0},{20,4},{24,8},{28,12},{1,17},{... | collective-permute-start | bytes 5529608 | tf_op jit(solution)/shard_map/ppermute | solution.py:751
  636.9 44.2 %collective-permute-start.16 = (bf16[160,5760]{1,0:T(8,128)(2,1)}, bf16[160,5760]{1,0:T(8,128)(2,1)}, u32[]{:S(2)}, u32[]{:S(2)}) collective-permute-start(bf16[160,5760]{1,0:T(8,128)(2,1)} %get-tuple-element.89), channel_id=1, source_target_pairs={{0,8},{4,12},{8,0},{12,4},{16,24},{20,28},{24,16},{28,20},{1,9},{5... | collective-permute-start | bytes 5529608 | tf_op jit(solution)/shard_map/ppermute | solution.py:747
  639.9 16.3 %copy-start.10 = (bf16[2560,256]{1,0:T(8,128)(2,1)S(1)}, bf16[2560,256]{1,0:T(8,128)(2,1)}, u32[]{:S(2)}) copy-start(bf16[2560,256]{1,0:T(8,128)(2,1)} %copy-done.9) | copy-start | bytes 3932164
  639.9 16.3 %copy-start.12 = (bf16[2560,256]{1,0:T(8,128)(2,1)S(1)}, bf16[2560,256]{1,0:T(8,128)(2,1)}, u32[]{:S(2)}) copy-start(bf16[2560,256]{1,0:T(8,128)(2,1)} %copy-done.11) | copy-start | bytes 3932164
  656.6 21.4 %copy-start.34 = (bf16[160,5760]{1,0:T(8,128)(2,1)S(1)}, bf16[160,5760]{1,0:T(8,128)(2,1)}, u32[]{:S(2)}) copy-start(bf16[160,5760]{1,0:T(8,128)(2,1)} %get-tuple-element.86) | copy-start | bytes 5529604
  658.4 23.2 %copy-start.33 = (bf16[160,5760]{1,0:T(8,128)(2,1)S(1)}, bf16[160,5760]{1,0:T(8,128)(2,1)}, u32[]{:S(2)}) copy-start(bf16[160,5760]{1,0:T(8,128)(2,1)} %get-tuple-element.88) | copy-start | bytes 5529604
  677.9 10.8 %collective-permute-start.12 = (bf16[4,320,640]{2,1,0:T(8,128)(2,1)S(1)}, bf16[4,320,640]{2,1,0:T(8,128)(2,1)}, u32[]{:S(2)}, u32[]{:S(2)}) collective-permute-start(bf16[4,320,640]{2,1,0:T(8,128)(2,1)S(1)} %dynamic-slice_bitcast_fusion), channel_id=1, source_target_pairs={{0,4},{4,0},{8,12},{12,8},{16,20},{20,16},{24,28},{28,24},{1,5},{5... | collective-permute-start | bytes 4915208 | tf_op jit(solution)/shard_map/ppermute | solution.py:743
  681.1 7.9 copy-start.22
  681.1 16.9 %collective-permute-start.10 = (bf16[192,5120]{1,0:T(8,128)(2,1)}, bf16[192,5120]{1,0:T(8,128)(2,1)}, u32[]{:S(2)}, u32[]{:S(2)}) collective-permute-start(bf16[192,5120]{1,0:T(8,128)(2,1)} %pad_maximum_fusion.1.refs_4_), channel_id=1, source_target_pairs={{0,4},{4,0},{8,12},{12,8},{16,20},{20,16},{24,28},{28,24},{1,5},{5... | collective-permute-start | bytes 5898248 | tf_op jit(solution)/shard_map/ppermute | solution.py:743
  684.9 43.4 %collective-permute-start.13 = (bf16[160,5760]{1,0:T(8,128)(2,1)}, bf16[160,5760]{1,0:T(8,128)(2,1)}, u32[]{:S(2)}, u32[]{:S(2)}) collective-permute-start(bf16[160,5760]{1,0:T(8,128)(2,1)} %get-tuple-element.85), channel_id=1, source_target_pairs={{0,16},{4,20},{8,24},{12,28},{16,0},{20,4},{24,8},{28,12},{1,17},{... | collective-permute-start | bytes 5529608 | tf_op jit(solution)/shard_map/ppermute | solution.py:751
  686.7 43.4 %collective-permute-start.18 = (bf16[160,5760]{1,0:T(8,128)(2,1)}, bf16[160,5760]{1,0:T(8,128)(2,1)}, u32[]{:S(2)}, u32[]{:S(2)}) collective-permute-start(bf16[160,5760]{1,0:T(8,128)(2,1)} %get-tuple-element.90), channel_id=1, source_target_pairs={{0,8},{4,12},{8,0},{12,4},{16,24},{20,28},{24,16},{28,20},{1,9},{5... | collective-permute-start | bytes 5529608 | tf_op jit(solution)/shard_map/ppermute | solution.py:747
  687.2 81.1 %collective-permute-start.15 = (bf16[160,5760]{1,0:T(8,128)(2,1)}, bf16[160,5760]{1,0:T(8,128)(2,1)}, u32[]{:S(2)}, u32[]{:S(2)}) collective-permute-start(bf16[160,5760]{1,0:T(8,128)(2,1)} %add_convert_fusion.4), channel_id=1, source_target_pairs={{0,8},{4,12},{8,0},{12,4},{16,24},{20,28},{24,16},{28,20},{1,9},{5... | collective-permute-start | bytes 5529608 | tf_op jit(solution)/shard_map/ppermute | solution.py:747
  688.7 79.7 %collective-permute-start.17 = (bf16[160,5760]{1,0:T(8,128)(2,1)}, bf16[160,5760]{1,0:T(8,128)(2,1)}, u32[]{:S(2)}, u32[]{:S(2)}) collective-permute-start(bf16[160,5760]{1,0:T(8,128)(2,1)} %add_convert_fusion.2), channel_id=1, source_target_pairs={{0,16},{4,20},{8,24},{12,28},{16,0},{20,4},{24,8},{28,12},{1,17},{... | collective-permute-start | bytes 5529608 | tf_op jit(solution)/shard_map/ppermute | solution.py:751
  698.0 70.4 %copy-start.32 = (bf16[320,5760]{1,0:T(8,128)(2,1)S(1)}, bf16[320,5760]{1,0:T(8,128)(2,1)}, u32[]{:S(2)}) copy-start(bf16[320,5760]{1,0:T(8,128)(2,1)} %get-tuple-element.84) | copy-start | bytes 11059204
  (28 other events, 76.9 us)
Sparse Core Ops, SparseCore 0:
  197.6 150.0 all-gather.5
  507.8 71.7 reduce-scatter.4
  581.9 73.0 reduce-scatter.2

commit v6 on v5

--- a/solution.py
+++ b/solution.py
@@ -345,10 +345,11 @@
 
 def rows_kernel(
     normed, grad0, grad1, grad2, grad3, normed_all, normed_other, grad_all, grad_other,
-    line_send, line_recv, core_send, core_recv, own_sem,
+    line_send, line_recv, core_send, core_recv, own_sem, held,
 ):
     s, z, core, _, _ = places()
     tok = normed.shape[0]
+    cuts = 4
     grads = (grad0, grad1, grad2, grad3)
     greet([(core, z)] + [(s, (z + k) % 4) for k in range(1, 4)])
 
@@ -360,11 +361,19 @@
             src_ref=src, dst_ref=dst, send_sem=send, recv_sem=recv, device_id=target, device_id_type=MESH
         )
 
+    def parts(ref):
+        size = tok // cuts
+        return [ref.at[pl.ds(n * size, size), :] for n in range(cuts)]
+
     def line(zz, up_way, hop):
         way = 0 if up_way else 1
         target = z + 1 if up_way else z - 1
         src = normed if hop == 0 else rows(normed_all, zz)
-        return remote(src, rows(normed_all, zz), line_send.at[way, hop], line_recv.at[way, hop], (s, target))
+        dst = rows(normed_all, zz)
+        return [
+            remote(a, b, line_send.at[way, hop, n], line_recv.at[way, hop, n], (s, target))
+            for n, (a, b) in enumerate(zip(parts(src), parts(dst)))
+        ]
 
     def over(zz, own=False):
         src = normed if own else rows(normed_all, zz)
@@ -374,45 +383,62 @@
         zz = (z + 4 - k) % 4
         return remote(grads[k], rows(grad_other, zz), core_send.at[1, zz], core_recv.at[1, zz], (core, z))
 
+    def line_start(zz, up_way, hop):
+        for copy in line(zz, up_way, hop):
+            copy.start()
+
+    def line_drain(zz, up_way, hop):
+        for copy in line(zz, up_way, hop):
+            copy.wait_send()
+
     def hop_step(hop):
         def below():
-            line(z - hop, True, hop - 1).wait_recv()
-            pl.when(z < 3)(lambda: line(z - hop, True, hop).start())
+            for came, on in zip(line(z - hop, True, hop - 1), line(z - hop, True, hop) if hop < 3 else [None] * cuts):
+                came.wait_recv()
+                if on is not None:
+                    pl.when(z < 3)(on.start)
             over(z - hop).start()
 
         def above():
-            line(z + hop, False, hop - 1).wait_recv()
-            pl.when(z > 0)(lambda: line(z + hop, False, hop).start())
+            for came, on in zip(line(z + hop, False, hop - 1), line(z + hop, False, hop) if hop < 3 else [None] * cuts):
+                came.wait_recv()
+                if on is not None:
+                    pl.when(z > 0)(on.start)
             over(z + hop).start()
 
         pl.when(z >= hop)(below)
         pl.when(z + hop <= 3)(above)
 
-    local = [
-        pltpu.make_async_copy(grads[k], rows(grad_all, (z + 4 - k) % 4), own_sem.at[k]) for k in range(4)
+    local = [pltpu.make_async_copy(grads[k], held.at[k], own_sem.at[k]) for k in range(4)]
+    local.append(pltpu.make_async_copy(normed, held.at[4], own_sem.at[4]))
+    stored = [
+        pltpu.make_async_copy(held.at[k], rows(grad_all, (z + 4 - k) % 4), own_sem.at[k]) for k in range(4)
     ]
-    local.append(pltpu.make_async_copy(normed, rows(normed_all, z), own_sem.at[4]))
-    pl.when(z < 3)(lambda: line(z, True, 0).start())
-    pl.when(z > 0)(lambda: line(z, False, 0).start())
+    stored.append(pltpu.make_async_copy(held.at[4], rows(normed_all, z), own_sem.at[4]))
+    pl.when(z < 3)(lambda: line_start(z, True, 0))
+    pl.when(z > 0)(lambda: line_start(z, False, 0))
     over(z, True).start()
     for copy in local:
         copy.start()
     for k in range(4):
         grad_over(k).start()
+    for copy, store in zip(local, stored):
+        copy.wait()
+        store.start()
     for hop in range(1, 4):
         hop_step(hop)
-    for copy in local:
+    for copy in stored:
         copy.wait()
     for k in range(4):
         grad_over(k).wait()
     over(z, True).wait()
     for k in range(1, 4):
         over((z + k) % 4).wait()
-    pl.when(z < 3)(lambda: line(z, True, 0).wait_send())
-    pl.when(z > 0)(lambda: line(z, False, 0).wait_send())
+    pl.when(z < 3)(lambda: line_drain(z, True, 0))
+    pl.when(z > 0)(lambda: line_drain(z, False, 0))
     for hop in range(1, 3):
-        pl.when((z >= hop) & (z < 3))(lambda: line(z - hop, True, hop).wait_send())
-        pl.when((z + hop <= 3) & (z > 0))(lambda: line(z + hop, False, hop).wait_send())
+        pl.when((z >= hop) & (z < 3))(lambda: line_drain(z - hop, True, hop))
+        pl.when((z + hop <= 3) & (z > 0))(lambda: line_drain(z + hop, False, hop))
 
 
 def gather_rows(normed, grads):
@@ -424,7 +450,7 @@
         in_specs=[anyspec] * 5,
         out_specs=[anyspec] * 4,
         out_shape=[jax.ShapeDtypeStruct((4 * tok, model), bf16)] * 4,
-        scratch_shapes=[dma((2, 3)), dma((2, 3)), dma((2, 4)), dma((2, 4)), dma((5,))],
+        scratch_shapes=[dma((2, 3, 4)), dma((2, 3, 4)), dma((2, 4)), dma((2, 4)), dma((5,)), pltpu.VMEM((5, tok, model), bf16)],
         compiler_params=pltpu.CompilerParams(collective_id=3, has_side_effects=True),
         name="gather_rows",
     )(normed, *grads)
@@ -751,18 +777,8 @@
     return lax.ppermute(shard, "seq", [(i, i ^ 4) for i in range(8)])
 
 
-def sum_blocks(blocks):
-    diag_low, diag_high, beside_low, beside_high, across_low, across_high, mine = blocks
-    by_across = swap_across(diag_low)
-    by_beside = swap_beside(diag_high)
-    from_beside_high = swap_beside(beside_high)
-    from_across_low = swap_across(across_low)
-    from_beside_low = swap_beside((beside_low.astype(f32) + by_across.astype(f32)).astype(bf16))
-    from_across_high = swap_across((across_high.astype(f32) + by_beside.astype(f32)).astype(bf16))
-    half = diag_low.shape[0]
-    low = mine[:half].astype(f32) + from_across_low.astype(f32) + from_beside_low.astype(f32)
-    high = mine[half:].astype(f32) + from_across_high.astype(f32) + from_beside_high.astype(f32)
-    return jnp.concatenate([low.astype(bf16), high.astype(bf16)], axis=0)
+def add_low(left, right):
+    return (left.astype(f32) + right.astype(f32)).astype(bf16)
 
 
 def scatter_paired(normed, grad_both, grad_mix, mixed, rest, mlp_sum):
@@ -954,7 +970,9 @@
             "feed_forward_products",
         )
         blocks, grad_normed_two = lax.optimization_barrier((blocks, grad_normed_two))
-        mlp_sum = sum_blocks(blocks)
+        diag_low, diag_high, beside_low, beside_high, across_low, across_high, mine = blocks
+        by_across = swap_across(diag_low)
+        by_beside = swap_beside(diag_high)
     else:
         grad_pair = jnp.concatenate([grad_gate, grad_up], axis=1)
         term_pair = mm(normed_all, grad_pair, ((0,), (0,))).astype(bf16)
@@ -971,6 +989,10 @@
     grad_middle = grad_out.astype(f32) + grad_mid_part
     grad_mix = grad_middle.astype(bf16)
     grad_mixed = mm(grad_mix, proj_out, ((1,), (0,)))
+    if custom:
+        beside_high, across_low, grad_mixed = lax.optimization_barrier((beside_high, across_low, grad_mixed))
+        from_beside_high = swap_beside(beside_high)
+        from_across_low = swap_across(across_low)
     carried_rows = jnp.broadcast_to(carried[None], (8, lru))
     grad_gelu_pre, rev_cum, rev_grad, pair_grad = call_heads(
         mixer_backward_scan,
@@ -996,6 +1018,20 @@
         [tok_count + 8, tok_count + 16],
         "mixer_backward",
     )
+    if custom:
+        by_across, by_beside, own = lax.optimization_barrier((by_across, by_beside, own))
+        beside_low, across_high = add_low(beside_low, by_across), add_low(across_high, by_beside)
+        beside_low, across_high, own = lax.optimization_barrier((beside_low, across_high, own))
+        from_beside_low = swap_beside(beside_low)
+        from_across_high = swap_across(across_high)
+        mlp_sum = mine.astype(f32) + jnp.concatenate(
+            [
+                from_across_low.astype(f32) + from_beside_low.astype(f32),
+                from_across_high.astype(f32) + from_beside_high.astype(f32),
+            ],
+            axis=0,
+        )
+        mlp_sum = mlp_sum.astype(bf16)
     received = from_behind(head[8 - margin :], "seq", -1)
     grad_branch = jnp.concatenate(
         [own[: tok_count - margin], own[tok_count - margin :] + received], axis=0

time: 976 us -> 903 us (0.925)
  Pallas kernels: 626 us -> 546 us
  blocking collectives: 21 us -> 34.1 us
    pallas_call x1, Pallas kernels: 166 us -> 85.7 us  [gather_rows(): pl.pallas_call(rows_kernel, in_specs=[anyspec] * 5, out_specs=[anyspec] *...]
    all_gather x2, blocking collectives: 21 us -> 34.1 us  [prefix(): gathered = lax.all_gather(jnp.stack(part), axis)]
    ppermute x3, waiting for transfers between devices: 26.9 us -> 37.3 us  [swap_across(): return lax.ppermute(shard, 'seq', [(i, i ^ 4) for i in range(8)])]
    ppermute x3, waiting for transfers between devices: 40.1 us -> 30.2 us  [swap_beside(): return lax.ppermute(shard, 'seq', [(i, i ^ 2) for i in range(8)])]
  transfers between devices with their start and end apart: 22 -> 22, of which waited for: 5 -> 4; matrix products, arithmetic and copies ran while one was open for 11% -> 12% of each run, Pallas kernels for 27% -> 18%
where the time goes in v6:
time: 903 us; the launch traced here: 894 us
  Pallas kernels  546 us (60%)
  matrix products  130 us (14%)
  waiting for transfers between devices  77 us (9%)
  other arithmetic  41.3 us (5%)
  blocking collectives  34.1 us (4%)
  local copies, waits for them, and re-layouts  28.8 us (3%)
  starting transfers between devices  21.2 us (2%)
  between operations  15.1 us (2%)
    pallas_call x1, Pallas kernels, gather(): pl.pallas_call(gather_kernel, in_specs=[anyspec] * 4, out_specs=[anyspec]...  183 us
    pallas_call x1, Pallas kernels, scatter(): pl.pallas_call(scatter_kernel, in_specs=[anyspec] * 3, out_specs=[anyspec...  179 us
    dot_general x10, matrix products, mm(): lax.dot_general(left, right, (dims, ((), ())), preferred_element_type=f32)  130 us
    pallas_call x1, Pallas kernels, gather_rows(): pl.pallas_call(rows_kernel, in_specs=[anyspec] * 5, out_specs=[anyspec] *...  85.7 us
    pallas_call x2, Pallas kernels, products(): pl.pallas_call(functools.partial(products_kernel, sides, tile, cuts), gri...  67.3 us
    ppermute x3, waiting for transfers between devices, swap_across(): return lax.ppermute(shard, 'seq', [(i, i ^ 4) for i in range(8)])  37.3 us
    all_gather x2, blocking collectives, prefix(): gathered = lax.all_gather(jnp.stack(part), axis)  34.1 us
    pallas_call x3, Pallas kernels, call_heads(): pl.pallas_call(kernel, grid=(heads,), in_specs=in_specs, out_specs=out_sp...  31.4 us
  transfers between devices with their start and end apart: 22, of which 4 were waited for; matrix products, arithmetic and copies ran while one was open for 12% of the time, Pallas kernels for 18%

profile of v6, /device:TPU:0, one launch (start us, length us, event | category | flops | bytes accessed | tf_op | source)
XLA Modules:
  0.0 893.6 jit_solution(3025572035114505826)
XLA Ops:
  8.1 1.4 stack.57
  14.4 183.1 %gather_weights.1 = (bf16[2560,8320]{1,0:T(8,128)(2,1)}, bf16[320,5760]{1,0:T(8,128)(2,1)}) custom-call(bf16[80,8320]{1,0:T(8,128)(2,1)} %copy-done.35, bf16[80,7680]{1,0:T(8,128)(2,1)} %gate.1, bf16[80,7680]{1,0:T(8,128)(2,1)} %up.1, bf16[80,7680]{1,0:T(8,128)(2,1)} %down.1), custom_call_target="tpu_custom_call" | custom-call | tf_op jit(solution)/shard_map/gather_weights/pallas_call | solution.py:330
  197.6 5.4 collective-permute-start.1
  203.0 3.4 collective-permute-start.2
  206.4 2.3 slice.212
  209.9 2.8 slice_reduce_fusion
  213.9 14.6 %fusion.76 = (bf16[192,5120]{1,0:T(8,128)(2,1)S(1)}, f32[192,5120]{1,0:T(8,128)}) fusion(bf16[192,2560]{1,0:T(8,128)(2,1)} %fusion.43.refs_0_, bf16[2560,8320]{1,0:T(8,128)(2,1)} %get-tuple-element.64), kind=kOutput, calls=%fused_computation.173 | convolution fusion | flops 5034147840 | bytes 33095680 | tf_op jit(solution)/shard_map/dot_general | solution.py:50
  231.1 1.7 copy.77
  233.7 2.1 fusion.73
  238.4 7.2 mixer_forward.1
  246.4 11.8 %all-gather.2 = f32[8,2,2560]{2,1,0:T(2,128)S(1)} all-gather(f32[1,2,2560]{2,1,0:T(2,128)S(1)} %fusion.63), channel_id=2, replica_groups=mesh['seq'=8,'fsdp'=4] {'seq'}, dimensions={0}, use_global_device_ids=true | all-gather | bytes 184320 | tf_op jit(solution)/shard_map/all_gather | solution.py:29
  258.6 2.0 fusion.72
  260.7 9.8 %multiply_reduce_fusion = (f32[192]{0:T(256)S(1)}, f32[192,2560]{1,0:T(8,128)S(1)}) fusion(bf16[192,2560]{1,0:T(8,128)(2,1)S(1)} %get-tuple-element.225.refs_6_, bf16[2560,8320]{1,0:T(8,128)(2,1)} %get-tuple-element.64, bf16[1,192,2560]{2,1,0:T(8,128)(2,1)S(1)} %copy-done.24), kind=kOutput, calls=%fused_computation.83 | convolution fusion | flops 2518548224 | bytes 17040128 | tf_op jit(solution)/shard_map/dot_general | solution.py:50
  273.0 85.7 %gather_rows.1 = (bf16[768,2560]{1,0:T(8,128)(2,1)}, bf16[768,2560]{1,0:T(8,128)(2,1)}, bf16[768,2560]{1,0:T(8,128)(2,1)}, bf16[768,2560]{1,0:T(8,128)(2,1)}) custom-call(bf16[192,2560]{1,0:T(8,128)(2,1)} %multiply_convert_fusion.2.normed, bf16[192,2560]{1,0:T(8,128)(2,1)} %bitcast.14.grad0, bf16[192,2560]{1,0:T(8,128)(2,1)} %collective-permute-done.1.grad1, ...), custom_call_target="tpu_custom_call" | custom-call | tf_op jit(solution)/shard_map/gather_rows/pallas_call | solution.py:448
  358.7 12.4 %fusion.18 = f32[768,1920]{1,0:T(8,128)S(1)} fusion(bf16[768,2560]{1,0:T(8,128)(2,1)} %get-tuple-element.69.refs_0_, bf16[2560,5760]{1,0:T(8,128)(2,1)} %all-gather.6.cloned.1.call-done), kind=kOutput, calls=%fused_computation.20 | convolution fusion | flops 7549747200 | bytes 19660800 | tf_op jit(solution)/shard_map/dot_general | solution.py:50
  371.2 12.9 %fusion.14 = f32[768,1920]{1,0:T(8,128)} fusion(bf16[768,2560]{1,0:T(8,128)(2,1)S(1)} %copy-done.50, bf16[2560,5760]{1,0:T(8,128)(2,1)} %all-gather.6.cloned.1.call-done), kind=kOutput, calls=%fused_computation.16 | convolution fusion | flops 7549747200 | bytes 19660800 | tf_op jit(solution)/shard_map/dot_general | solution.py:50
  384.0 17.4 %multiply_convert_fusion = (bf16[768,1920]{1,0:T(8,128)(2,1)S(1)}, bf16[768,1920]{1,0:T(8,128)(2,1)S(1)}, bf16[768,1920]{1,0:T(8,128)(2,1)}) fusion(f32[768,1920]{1,0:T(8,128)S(1)} %fusion.18, f32[768,1920]{1,0:T(8,128)} %fusion.14, bf16[768,2560]{1,0:T(8,128)(2,1)S(1)} %copy-done.51, bf16[2560,5760]{1,0:T(8,128)(2,1)} %all-gather.6.cloned.1.call-done), kind=kOutput, calls=%fused_computation.35 | convolution fusion | flops 7586611200 | bytes 34406400 | tf_op jit(solution)/shard_map/dot_general | solution.py:50
  401.5 13.1 %fusion.12 = f32[768,2560]{1,0:T(8,128)S(1)} fusion(bf16[768,1920]{1,0:T(8,128)(2,1)S(1)} %get-tuple-element.221.refs_6_, bf16[2560,5760]{1,0:T(8,128)(2,1)} %all-gather.6.cloned.1.call-done), kind=kOutput, calls=%fused_computation.14 | convolution fusion | flops 7549747200 | bytes 20643840 | tf_op jit(solution)/shard_map/dot_general | solution.py:50
  414.6 12.5 %add_convert_fusion = bf16[768,2560]{1,0:T(8,128)(2,1)} fusion(f32[768,2560]{1,0:T(8,128)S(1)} %fusion.12, bf16[768,1920]{1,0:T(8,128)(2,1)S(1)} %get-tuple-element.222.refs_4_, bf16[2560,5760]{1,0:T(8,128)(2,1)} %all-gather.6.cloned.1.call-done), kind=kOutput, calls=%fused_computation.22 | convolution fusion | flops 7553679360 | bytes 24576000 | tf_op jit(solution)/shard_map/dot_general | solution.py:50
  428.7 14.1 %fusion.32 = bf16[768,2560]{1,0:T(8,128)(2,1)} fusion(bf16[768,1920]{1,0:T(8,128)(2,1)} %get-tuple-element.223.refs_8_, bf16[2560,5760]{1,0:T(8,128)(2,1)} %all-gather.6.cloned.1.call-done), kind=kOutput, calls=%fused_computation.38 | convolution fusion | flops 7551713280 | bytes 16711680 | tf_op jit(solution)/shard_map/dot_general | solution.py:50
  442.8 45.0 %feed_forward_products.1 = (bf16[160,5760]{1,0:T(8,128)(2,1)}, bf16[160,5760]{1,0:T(8,128)(2,1)}, bf16[160,5760]{1,0:T(8,128)(2,1)}, bf16[160,5760]{1,0:T(8,128)...) custom-call(s32[5]{0:T(128)} %stack.64.place, ...), custom_call_target="tpu_custom_call" | custom-call | flops 22649241600 | bytes 14745600 | tf_op jit(solution)/shard_map/feed_forward_products/pallas_call | solution.py:525
  487.8 9.5 %reduce-scatter.5.cloned.1.call-done = bf16[192,2560]{1,0:T(8,128)(2,1)} async-done(((bf16[768,2560]{1,0:T(8,128)(2,1)}), bf16[192,2560]{1,0:T(8,128)(2,1)}) %reduce-scatter.5.cloned.1.call-update) | async-done | bytes 983056 | tf_op jit(solution)/shard_map/reduce_scatter | solution.py:956
  497.2 2.8 fusion.46
  500.0 1.5 collective-permute-start.7
  501.6 1.5 collective-permute-start.8
  503.0 2.0 fusion.71.refs_2_
  505.0 7.1 fusion.4.grad_mixed
  512.4 12.8 %mixer_backward_scan.1 = (bf16[192,2560]{1,0:T(8,128)(2,1)S(1)}, f32[192,2560]{1,0:T(8,128)S(1)}, f32[192,2560]{1,0:T(8,128)S(1)}, f32[8,2560]{1,0:T(8,128)S(1)}) custom-call(f32[192,2560]{1,0:T(8,128)S(1)} %fusion.4.grad_mixed, f32[192,2560]{1,0:T(8,128)S(1)} %copy-done.7, f32[192,2560]{1,0:T(8,128)S(1)} %copy-done.6, f32[192,2560]{1,0:T(8,128)S(1)} %copy-done.1, ...), custom_call_target="tpu_custom_call" | custom-call | tf_op jit(solution)/shard_map/mixer_backward_scan/pallas_call | solution.py:840
  525.2 22.4 %all-gather.3 = f32[8,2,2560]{2,1,0:T(2,128)S(1)} all-gather(f32[1,2,2560]{2,1,0:T(2,128)S(1)} %fusion.64), channel_id=3, replica_groups=mesh['seq'=8,'fsdp'=4] {'seq'}, dimensions={0}, use_global_device_ids=true | all-gather | bytes 184320 | tf_op jit(solution)/shard_map/all_gather | solution.py:29
  548.1 11.4 %mixer_backward.1 = (f32[192,2560]{1,0:T(8,128)S(1)}, f32[8,2560]{1,0:T(8,128)S(1)}, bf16[2560,256]{1,0:T(8,128)(2,1)S(1)}, bf16[2560,256]{1,0:T(8,128)(2,1)S(1)}, f32[8,2560]{1,0:T(8,128)S(1)}) custom-call(f32[192,2560]{1,0:T(8,128)S(1)} %get-tuple-element.88.rev_cum, f32[192,2560]{1,0:T(8,128)S(1)} %get-tuple-element.89.rev_grad, ...), custom_call_target="tpu_custom_call" | custom-call | tf_op jit(solution)/shard_map/mixer_backward/pallas_call | solution.py:840
  560.9 3.0 add_convert_fusion.1
  564.0 1.5 pad_maximum_fusion.refs_4_
  565.6 16.1 %fusion.44 = (bf16[2560]{0:T(1024)(128)(2,1)S(1)}, f32[192]{0:T(256)S(1)}, f32[192,2560]{1,0:T(8,128)}) fusion(bf16[1,192,2560]{2,1,0:T(8,128)(2,1)} %param.17, f32[192]{0:T(256)S(1)} %copy-done.49, f32[2560]{0:T(1024)S(1)} %copy-done.43, bf16[192,5120]{1,0:T(8,128)(2,1)} %pad_maximum_fusion.refs_4_, bf16[2560,8320]{1,0:T(8,128)(2,1)} %get-tuple-element.64), kind=kOutput, calls=%fused_computation.62 | convolution fusion | flops 5036602880 | bytes 31146496 | tf_op jit(solution)/shard_map/dot_general | solution.py:50
  582.4 1.6 copy-done.20
  585.4 1.6 collective-permute-start.14
  588.5 1.8 collective-permute-start.15
  590.4 5.5 fusion.62
  596.7 1.8 fusion.38
  598.8 1.4 pad_maximum_fusion.1.rest
  600.2 30.2 %collective-permute-done.18 = bf16[160,5760]{1,0:T(8,128)(2,1)} collective-permute-done((bf16[160,5760]{1,0:T(8,128)(2,1)}, bf16[160,5760]{1,0:T(8,128)(2,1)}, u32[]{:S(2)}, u32[]{:S(2)}) %collective-permute-start.18) | collective-permute-done | bytes 1843232 | tf_op jit(solution)/shard_map/ppermute | solution.py:773
  631.7 2.4 convert_add_fusion.1
  634.1 36.0 %collective-permute-done.15 = bf16[160,5760]{1,0:T(8,128)(2,1)} collective-permute-done((bf16[160,5760]{1,0:T(8,128)(2,1)}, bf16[160,5760]{1,0:T(8,128)(2,1)}, u32[]{:S(2)}, u32[]{:S(2)}) %collective-permute-start.15) | collective-permute-done | bytes 1843232 | tf_op jit(solution)/shard_map/ppermute | solution.py:777
  670.1 1.9 convert_add_fusion.2
  672.0 4.6 fusion.20.mlp
  676.6 22.3 %mixer_products.1 = bf16[1280,7680]{1,0:T(8,128)(2,1)} custom-call(s32[5]{0:T(128)} %stack.64.place, bf16[192,2560]{1,0:T(8,128)(2,1)} %fusion.43.refs_0_, bf16[192,2560]{1,0:T(8,128)(2,1)} %collective-permute-done.10.refs_1_, bf16[192,2560]{1,0:T(8,128)(2,1)} %copy-done.30, bf16[192,2560]{1,0:T(8,128)(2,1)} %collective-permute-done.11.refs_3_, ...), custom_call_target="tpu_custom_call" | custom-call | flops 7549747200 | bytes 19660800 | tf_op jit(solution)/shard_map/mixer_products/pallas_call | solution.py:525
  698.9 178.7 %scatter_gradients.1 = (bf16[80,8320]{1,0:T(8,128)(2,1)S(1)}, bf16[3,80,7680]{2,1,0:T(8,128)(2,1)}) custom-call(bf16[4,320,7680]{2,1,0:T(8,128)(2,1)} %bitcast.77, bf16[4,320,640]{2,1,0:T(8,128)(2,1)} %pad_maximum_fusion.1.rest, bf16[320,5760]{1,0:T(8,128)(2,1)} %fusion.20.mlp), custom_call_target="tpu_custom_call" | custom-call | tf_op jit(solution)/shard_map/scatter_gradients/pallas_call | solution.py:730
  877.8 1.5 fusion.74
  881.4 5.3 bitcast_convert_fusion
  (197 shorter events, 29.9 us)
Async XLA Ops:
  7.2 351.5 %all-gather.6.cloned.1.call-start = ((), (), s32[]{:S(2)}) async-start(), calls=%async_computation.2 | async-start | bytes 33177600 | tf_op jit(solution)/shard_map/all_gather | solution.py:897
  197.5 299.7 %reduce-scatter.5.cloned.1.call-start = ((), (), s32[]{:S(2)}) async-start(), calls=%async_computation.4 | async-start | bytes 4915200 | tf_op jit(solution)/shard_map/reduce_scatter | solution.py:956
  197.6 75.4 %collective-permute-start.1 = (bf16[192,2560]{1,0:T(8,128)(2,1)}, bf16[192,2560]{1,0:T(8,128)(2,1)}, u32[]{:S(2)}, u32[]{:S(2)}) collective-permute-start(bf16[192,2560]{1,0:T(8,128)(2,1)} %bitcast.14.grad0), channel_id=1, source_target_pairs={{0,1},{1,2},{2,3},{3,0},{4,5},{5,6},{6,7},{7,4},{8,9},{9,10},{10,1... | collective-permute-start | bytes 2949128 | tf_op jit(solution)/shard_map/ppermute | solution.py:763
  203.0 70.0 %collective-permute-start.2 = (bf16[192,2560]{1,0:T(8,128)(2,1)}, bf16[192,2560]{1,0:T(8,128)(2,1)}, u32[]{:S(2)}, u32[]{:S(2)}) collective-permute-start(bf16[192,2560]{1,0:T(8,128)(2,1)} %bitcast.14.grad0), channel_id=1, source_target_pairs={{0,2},{1,3},{2,0},{3,1},{4,6},{5,7},{6,4},{7,5},{8,10},{9,11},{10,... | collective-permute-start | bytes 2949128 | tf_op jit(solution)/shard_map/ppermute | solution.py:763
  206.4 66.6 %collective-permute-start.3 = (bf16[192,2560]{1,0:T(8,128)(2,1)}, bf16[192,2560]{1,0:T(8,128)(2,1)}, u32[]{:S(2)}, u32[]{:S(2)}) collective-permute-start(bf16[192,2560]{1,0:T(8,128)(2,1)} %bitcast.14.grad0), channel_id=1, source_target_pairs={{0,3},{1,0},{2,1},{3,2},{4,7},{5,4},{6,5},{7,6},{8,11},{9,8},{10,9... | collective-permute-start | bytes 2949128 | tf_op jit(solution)/shard_map/ppermute | solution.py:763
  229.8 7.3 collective-permute-start
  237.1 9.3 %copy-start.15 = (f32[8,2560]{1,0:T(8,128)}, f32[8,2560]{1,0:T(8,128)S(1)}, u32[]{:S(2)}) copy-start(f32[8,2560]{1,0:T(8,128)S(1)} %pad_convert_fusion.prior) | copy-start | bytes 245764
  238.4 20.3 %copy-start.36 = (f32[192,5120]{1,0:T(8,128)S(1)}, f32[192,5120]{1,0:T(8,128)}, u32[]{:S(2)}) copy-start(f32[192,5120]{1,0:T(8,128)} %get-tuple-element.249) | copy-start | bytes 11796484
  245.6 15.1 %copy-start = (f32[192,2560]{1,0:T(8,128)}, f32[192,2560]{1,0:T(8,128)S(1)}, u32[]{:S(2)}) copy-start(f32[192,2560]{1,0:T(8,128)S(1)} %get-tuple-element.66.cum) | copy-start | bytes 5898244
  245.6 15.1 %copy-start.2 = (f32[192,2560]{1,0:T(8,128)}, f32[192,2560]{1,0:T(8,128)S(1)}, u32[]{:S(2)}) copy-start(f32[192,2560]{1,0:T(8,128)S(1)} %get-tuple-element.65.local) | copy-start | bytes 5898244
  245.6 15.0 %copy-start.5 = (f32[192,2560]{1,0:T(8,128)}, f32[192,2560]{1,0:T(8,128)S(1)}, u32[]{:S(2)}) copy-start(f32[192,2560]{1,0:T(8,128)S(1)} %get-tuple-element.87.rate_pre) | copy-start | bytes 5898244
  245.6 15.0 %copy-start.8 = (f32[192,2560]{1,0:T(8,128)}, f32[192,2560]{1,0:T(8,128)S(1)}, u32[]{:S(2)}) copy-start(f32[192,2560]{1,0:T(8,128)S(1)} %get-tuple-element.91.input_pre) | copy-start | bytes 5898244
  245.6 15.0 %copy-start.13 = (bf16[192,2560]{1,0:T(8,128)(2,1)}, bf16[192,2560]{1,0:T(8,128)(2,1)S(1)}, u32[]{:S(2)}) copy-start(bf16[192,2560]{1,0:T(8,128)(2,1)S(1)} %get-tuple-element.92.conv) | copy-start | bytes 2949124
  260.7 9.9 %copy-start.28 = (bf16[192,2560]{1,0:T(8,128)(2,1)}, bf16[192,2560]{1,0:T(8,128)(2,1)S(1)}, u32[]{:S(2)}) copy-start(bf16[192,2560]{1,0:T(8,128)(2,1)S(1)} %get-tuple-element.225.refs_6_) | copy-start | bytes 2949124
  358.7 12.4 %copy-start.50 = (bf16[768,2560]{1,0:T(8,128)(2,1)S(1)}, bf16[768,2560]{1,0:T(8,128)(2,1)}, u32[]{:S(2)}) copy-start(bf16[768,2560]{1,0:T(8,128)(2,1)} %get-tuple-element.69.refs_0_) | copy-start | bytes 11796484
  371.2 12.9 %copy-start.51 = (bf16[768,2560]{1,0:T(8,128)(2,1)S(1)}, bf16[768,2560]{1,0:T(8,128)(2,1)}, u32[]{:S(2)}) copy-start(bf16[768,2560]{1,0:T(8,128)(2,1)} %get-tuple-element.71.refs_2_) | copy-start | bytes 11796484
  401.5 13.1 %copy-start.52 = (bf16[768,1920]{1,0:T(8,128)(2,1)}, bf16[768,1920]{1,0:T(8,128)(2,1)S(1)}, u32[]{:S(2)}) copy-start(bf16[768,1920]{1,0:T(8,128)(2,1)S(1)} %get-tuple-element.221.refs_6_) | copy-start | bytes 8847364
  401.5 13.1 %copy-start.53 = (bf16[768,1920]{1,0:T(8,128)(2,1)}, bf16[768,1920]{1,0:T(8,128)(2,1)S(1)}, u32[]{:S(2)}) copy-start(bf16[768,1920]{1,0:T(8,128)(2,1)S(1)} %get-tuple-element.222.refs_4_) | copy-start | bytes 8847364
  427.1 163.3 %reduce-scatter.3.cloned.1.call-start = ((), (), s32[]{:S(2)}) async-start(), calls=%async_computation.3 | async-start | bytes 4915200 | tf_op jit(solution)/shard_map/reduce_scatter | solution.py:983
  427.1 15.7 %collective-permute-start.4 = (bf16[768,1920]{1,0:T(8,128)(2,1)}, bf16[768,1920]{1,0:T(8,128)(2,1)}, u32[]{:S(2)}, u32[]{:S(2)}) collective-permute-start(bf16[768,1920]{1,0:T(8,128)(2,1)} %copy-done.53), channel_id=1, source_target_pairs={{0,4},{4,0},{8,12},{12,8},{16,20},{20,16},{24,28},{28,24},{1,5},{5... | collective-permute-start | bytes 8847368 | tf_op jit(solution)/shard_map/ppermute | solution.py:769
  427.5 15.3 %collective-permute-start.5 = (bf16[768,1920]{1,0:T(8,128)(2,1)}, bf16[768,1920]{1,0:T(8,128)(2,1)}, u32[]{:S(2)}, u32[]{:S(2)}) collective-permute-start(bf16[768,1920]{1,0:T(8,128)(2,1)} %copy-done.52), channel_id=1, source_target_pairs={{0,4},{4,0},{8,12},{12,8},{16,20},{20,16},{24,28},{28,24},{1,5},{5... | collective-permute-start | bytes 8847368 | tf_op jit(solution)/shard_map/ppermute | solution.py:769
  427.7 15.1 %collective-permute-start.6 = (bf16[768,1920]{1,0:T(8,128)(2,1)}, bf16[768,1920]{1,0:T(8,128)(2,1)}, u32[]{:S(2)}, u32[]{:S(2)}) collective-permute-start(bf16[768,1920]{1,0:T(8,128)(2,1)} %get-tuple-element.223.refs_8_), channel_id=1, source_target_pairs={{0,4},{4,0},{8,12},{12,8},{16,20},{20,16},{24,28},{28,24},{1,5},{5... | collective-permute-start | bytes 8847368 | tf_op jit(solution)/shard_map/ppermute | solution.py:769
  500.0 60.8 %collective-permute-start.7 = (bf16[160,5760]{1,0:T(8,128)(2,1)}, bf16[160,5760]{1,0:T(8,128)(2,1)S(1)}, u32[]{:S(2)}, u32[]{:S(2)}) collective-permute-start(bf16[160,5760]{1,0:T(8,128)(2,1)} %get-tuple-element.82), channel_id=1, source_target_pairs={{0,16},{4,20},{8,24},{12,28},{16,0},{20,4},{24,8},{28,12},{1,17},{... | collective-permute-start | bytes 5529608 | tf_op jit(solution)/shard_map/ppermute | solution.py:777
  501.6 59.3 %collective-permute-start.8 = (bf16[160,5760]{1,0:T(8,128)(2,1)}, bf16[160,5760]{1,0:T(8,128)(2,1)S(1)}, u32[]{:S(2)}, u32[]{:S(2)}) collective-permute-start(bf16[160,5760]{1,0:T(8,128)(2,1)} %get-tuple-element.83), channel_id=1, source_target_pairs={{0,8},{4,12},{8,0},{12,4},{16,24},{20,28},{24,16},{28,20},{1,9},{5... | collective-permute-start | bytes 5529608 | tf_op jit(solution)/shard_map/ppermute | solution.py:773
  505.0 7.3 copy-start.7
  512.3 12.8 %copy-start.45 = (f32[1,2560]{1,0:T(1,128)S(1)}, f32[1,2560]{1,0:T(1,128)}, u32[]{:S(2)}) copy-start(f32[1,2560]{1,0:T(1,128)} %copy-done.44) | copy-start | bytes 30724
  512.3 35.7 %copy-start.4 = (bf16[192,2560]{1,0:T(8,128)(2,1)S(1)}, bf16[192,2560]{1,0:T(8,128)(2,1)}, u32[]{:S(2)}) copy-start(bf16[192,2560]{1,0:T(8,128)(2,1)} %slice.278.branch) | copy-start | bytes 2949124
  512.3 35.7 %copy-start.14 = (bf16[192,2560]{1,0:T(8,128)(2,1)S(1)}, bf16[192,2560]{1,0:T(8,128)(2,1)}, u32[]{:S(2)}) copy-start(bf16[192,2560]{1,0:T(8,128)(2,1)} %copy-done.13) | copy-start | bytes 2949124
  512.3 35.7 %copy-start.16 = (f32[8,2560]{1,0:T(8,128)S(1)}, f32[8,2560]{1,0:T(8,128)}, u32[]{:S(2)}) copy-start(f32[8,2560]{1,0:T(8,128)} %copy-done.15) | copy-start | bytes 245764
  548.1 12.8 %copy-start.33 = (bf16[160,5760]{1,0:T(8,128)(2,1)S(1)}, bf16[160,5760]{1,0:T(8,128)(2,1)}, u32[]{:S(2)}) copy-start(bf16[160,5760]{1,0:T(8,128)(2,1)} %get-tuple-element.81) | copy-start | bytes 5529604
  548.1 12.8 %copy-start.34 = (bf16[160,5760]{1,0:T(8,128)(2,1)S(1)}, bf16[160,5760]{1,0:T(8,128)(2,1)}, u32[]{:S(2)}) copy-start(bf16[160,5760]{1,0:T(8,128)(2,1)} %get-tuple-element.95) | copy-start | bytes 5529604
  559.5 4.4 collective-permute-start.9
  565.6 16.5 %copy-start.10 = (bf16[2560,256]{1,0:T(8,128)(2,1)S(1)}, bf16[2560,256]{1,0:T(8,128)(2,1)}, u32[]{:S(2)}) copy-start(bf16[2560,256]{1,0:T(8,128)(2,1)} %copy-done.9) | copy-start | bytes 3932164
  565.6 16.5 %copy-start.12 = (bf16[2560,256]{1,0:T(8,128)(2,1)S(1)}, bf16[2560,256]{1,0:T(8,128)(2,1)}, u32[]{:S(2)}) copy-start(bf16[2560,256]{1,0:T(8,128)(2,1)} %copy-done.11) | copy-start | bytes 3932164
  582.4 7.9 copy-start.47
  582.4 8.0 copy-start.19
  585.4 10.5 %collective-permute-start.14 = (bf16[4,320,640]{2,1,0:T(8,128)(2,1)}, bf16[4,320,640]{2,1,0:T(8,128)(2,1)}, u32[]{:S(2)}, u32[]{:S(2)}) collective-permute-start(bf16[4,320,640]{2,1,0:T(8,128)(2,1)} %dynamic-slice_bitcast_fusion), channel_id=1, source_target_pairs={{0,4},{4,0},{8,12},{12,8},{16,20},{20,16},{24,28},{28,24},{1,5},{5... | collective-permute-start | bytes 4915208 | tf_op jit(solution)/shard_map/ppermute | solution.py:769
  587.0 43.4 %collective-permute-start.18 = (bf16[160,5760]{1,0:T(8,128)(2,1)}, bf16[160,5760]{1,0:T(8,128)(2,1)}, u32[]{:S(2)}, u32[]{:S(2)}) collective-permute-start(bf16[160,5760]{1,0:T(8,128)(2,1)} %get-tuple-element.108), channel_id=1, source_target_pairs={{0,8},{4,12},{8,0},{12,4},{16,24},{20,28},{24,16},{28,20},{1,9},{5... | collective-permute-start | bytes 5529608 | tf_op jit(solution)/shard_map/ppermute | solution.py:773
  588.3 43.4 %collective-permute-start.17 = (bf16[160,5760]{1,0:T(8,128)(2,1)}, bf16[160,5760]{1,0:T(8,128)(2,1)}, u32[]{:S(2)}, u32[]{:S(2)}) collective-permute-start(bf16[160,5760]{1,0:T(8,128)(2,1)} %get-tuple-element.107), channel_id=1, source_target_pairs={{0,16},{4,20},{8,24},{12,28},{16,0},{20,4},{24,8},{28,12},{1,17},{... | collective-permute-start | bytes 5529608 | tf_op jit(solution)/shard_map/ppermute | solution.py:777
  588.5 88.1 %collective-permute-start.10 = (bf16[192,2560]{1,0:T(8,128)(2,1)}, bf16[192,2560]{1,0:T(8,128)(2,1)}, u32[]{:S(2)}, u32[]{:S(2)}) collective-permute-start(bf16[192,2560]{1,0:T(8,128)(2,1)} %fusion.43.refs_0_), channel_id=1, source_target_pairs={{0,4},{4,0},{8,12},{12,8},{16,20},{20,16},{24,28},{28,24},{1,5},{5... | collective-permute-start | bytes 2949128 | tf_op jit(solution)/shard_map/ppermute | solution.py:769
  588.5 81.6 %collective-permute-start.15 = (bf16[160,5760]{1,0:T(8,128)(2,1)}, bf16[160,5760]{1,0:T(8,128)(2,1)}, u32[]{:S(2)}, u32[]{:S(2)}) collective-permute-start(bf16[160,5760]{1,0:T(8,128)(2,1)} %get-tuple-element.105), channel_id=1, source_target_pairs={{0,16},{4,20},{8,24},{12,28},{16,0},{20,4},{24,8},{28,12},{1,17},{... | collective-permute-start | bytes 5529608 | tf_op jit(solution)/shard_map/ppermute | solution.py:777
  595.9 74.1 %collective-permute-start.16 = (bf16[160,5760]{1,0:T(8,128)(2,1)S(1)}, bf16[160,5760]{1,0:T(8,128)(2,1)S(1)}, u32[]{:S(2)}, u32[]{:S(2)}) collective-permute-start(bf16[160,5760]{1,0:T(8,128)(2,1)S(1)} %copy-done.32), channel_id=1, source_target_pairs={{0,8},{4,12},{8,0},{12,4},{16,24},{20,28},{24,16},{28,20},{1,9},{5... | collective-permute-start | bytes 5529608 | tf_op jit(solution)/shard_map/ppermute | solution.py:773
  598.7 31.6 %copy-start.29 = (bf16[192,2560]{1,0:T(8,128)(2,1)S(1)}, bf16[192,2560]{1,0:T(8,128)(2,1)}, u32[]{:S(2)}) copy-start(bf16[192,2560]{1,0:T(8,128)(2,1)} %copy-done.28) | copy-start | bytes 2949124
  598.8 32.9 %copy-start.31 = (bf16[192,2560]{1,0:T(8,128)(2,1)S(1)}, bf16[192,2560]{1,0:T(8,128)(2,1)}, u32[]{:S(2)}) copy-start(bf16[192,2560]{1,0:T(8,128)(2,1)} %copy-done.30) | copy-start | bytes 2949124
  600.2 69.9 %copy-start.26 = (bf16[192,5120]{1,0:T(8,128)(2,1)S(1)}, bf16[192,5120]{1,0:T(8,128)(2,1)}, u32[]{:S(2)}) copy-start(bf16[192,5120]{1,0:T(8,128)(2,1)} %pad_maximum_fusion.refs_4_) | copy-start | bytes 5898244
  630.4 46.2 %collective-permute-start.13 = (bf16[192,2560]{1,0:T(8,128)(2,1)S(1)}, bf16[192,2560]{1,0:T(8,128)(2,1)}, u32[]{:S(2)}, u32[]{:S(2)}) collective-permute-start(bf16[192,2560]{1,0:T(8,128)(2,1)S(1)} %copy-done.29), channel_id=1, source_target_pairs={{0,4},{4,0},{8,12},{12,8},{16,20},{20,16},{24,28},{28,24},{1,5},{5... | collective-permute-start | bytes 2949128 | tf_op jit(solution)/shard_map/ppermute | solution.py:769
  631.7 44.9 %collective-permute-start.11 = (bf16[192,2560]{1,0:T(8,128)(2,1)S(1)}, bf16[192,2560]{1,0:T(8,128)(2,1)}, u32[]{:S(2)}, u32[]{:S(2)}) collective-permute-start(bf16[192,2560]{1,0:T(8,128)(2,1)S(1)} %copy-done.31), channel_id=1, source_target_pairs={{0,4},{4,0},{8,12},{12,8},{16,20},{20,16},{24,28},{28,24},{1,5},{5... | collective-permute-start | bytes 2949128 | tf_op jit(solution)/shard_map/ppermute | solution.py:769
  670.1 6.5 collective-permute-start.12
  (28 other events, 99.1 us)
Sparse Core Ops, SparseCore 0:
  197.6 150.0 all-gather.5
  427.2 70.0 reduce-scatter.4
  499.5 73.0 reduce-scatter.2

commit v7 on v6

--- a/solution.py
+++ b/solution.py
@@ -781,7 +781,7 @@
     return (left.astype(f32) + right.astype(f32)).astype(bf16)
 
 
-def scatter_paired(normed, grad_both, grad_mix, mixed, rest, mlp_sum):
+def scatter_paired(normed, grad_both, grad_mix, mixed, rest, mlp_parts):
     seq = lax.axis_index("seq")
     core, x, y = seq % 2, (seq // 2) % 2, seq // 4
     main = products(
@@ -801,7 +801,10 @@
         ],
         axis=0,
     )
-    return scatter(main.reshape(4, -1, main.shape[1]), rest, mlp_sum)
+    main, rest, mlp_parts = lax.optimization_barrier((main, rest, mlp_parts))
+    mine, *sent = [part.astype(f32) for part in mlp_parts]
+    mlp_sum = mine + jnp.concatenate([sent[0] + sent[2], sent[1] + sent[3]], axis=0)
+    return scatter(main.reshape(4, -1, main.shape[1]), rest, mlp_sum.astype(bf16))
 
 
 def lru_rows(values):
@@ -969,8 +972,8 @@
             (half,) * 6 + (2 * half,),
             "feed_forward_products",
         )
-        blocks, grad_normed_two = lax.optimization_barrier((blocks, grad_normed_two))
-        diag_low, diag_high, beside_low, beside_high, across_low, across_high, mine = blocks
+        mine, grad_normed_two = lax.optimization_barrier((blocks[6], grad_normed_two))
+        diag_low, diag_high, beside_low, beside_high, across_low, across_high = blocks[:6]
         by_across = swap_across(diag_low)
         by_beside = swap_beside(diag_high)
     else:
@@ -1024,14 +1027,7 @@
         beside_low, across_high, own = lax.optimization_barrier((beside_low, across_high, own))
         from_beside_low = swap_beside(beside_low)
         from_across_high = swap_across(across_high)
-        mlp_sum = mine.astype(f32) + jnp.concatenate(
-            [
-                from_across_low.astype(f32) + from_beside_low.astype(f32),
-                from_across_high.astype(f32) + from_beside_high.astype(f32),
-            ],
-            axis=0,
-        )
-        mlp_sum = mlp_sum.astype(bf16)
+        mlp_parts = (mine, from_across_low, from_across_high, from_beside_low, from_beside_high)
     received = from_behind(head[8 - margin :], "seq", -1)
     grad_branch = jnp.concatenate(
         [own[: tok_count - margin], own[tok_count - margin :] + received], axis=0
@@ -1044,8 +1040,10 @@
     vectors = jnp.concatenate([sums, grad_gain_one[None], grad_gain_two[None]], axis=0).T
     vectors = jnp.pad(vectors, ((0, 0), (0, 128 - vectors.shape[1]))).astype(bf16)
     rest = jnp.concatenate([rate_w_grad, input_w_grad, vectors], axis=1)
-    scatter_all = scatter_paired if custom else scatter_plain
-    mixer_sum, mlp_back = scatter_all(normed, grad_both, grad_mix, mixed, rest, mlp_sum)
+    if custom:
+        mixer_sum, mlp_back = scatter_paired(normed, grad_both, grad_mix, mixed, rest, mlp_parts)
+    else:
+        mixer_sum, mlp_back = scatter_plain(normed, grad_both, grad_mix, mixed, rest, mlp_sum)
     mlp_grads = [mlp_back[m].astype(f32) for m in range(3)]
     mixer_sum = mixer_sum.astype(f32)
     edges = [lru, 2 * lru, 3 * lru, 3 * lru + width, 3 * lru + 2 * width]

time: 903 us -> 877 us (0.971)
  waiting for transfers between devices: 77 us -> 60.3 us
  blocking collectives: 34.1 us -> 23.4 us
    ppermute x3, waiting for transfers between devices: 30.2 us -> 2.87 us  [swap_beside(): return lax.ppermute(shard, 'seq', [(i, i ^ 2) for i in range(8)])]
    all_gather x2, blocking collectives: 34.1 us -> 23.4 us  [prefix(): gathered = lax.all_gather(jnp.stack(part), axis)]
  transfers between devices with their start and end apart: 22 -> 22, of which waited for: 4 -> 5; matrix products, arithmetic and copies ran while one was open for 12% -> 12% of each run, Pallas kernels for 18% -> 21%
where the time goes in v7:
time: 877 us; the launch traced here: 869 us
  Pallas kernels  544 us (62%)
  matrix products  130 us (15%)
  waiting for transfers between devices  60.3 us (7%)
  other arithmetic  45.1 us (5%)
  local copies, waits for them, and re-layouts  28.7 us (3%)
  blocking collectives  23.4 us (3%)
  starting transfers between devices  22.4 us (3%)
  between operations  15 us (2%)
    pallas_call x1, Pallas kernels, gather(): pl.pallas_call(gather_kernel, in_specs=[anyspec] * 4, out_specs=[anyspec]...  183 us
    pallas_call x1, Pallas kernels, scatter(): pl.pallas_call(scatter_kernel, in_specs=[anyspec] * 3, out_specs=[anyspec...  177 us
    dot_general x10, matrix products, mm(): lax.dot_general(left, right, (dims, ((), ())), preferred_element_type=f32)  130 us
    pallas_call x1, Pallas kernels, gather_rows(): pl.pallas_call(rows_kernel, in_specs=[anyspec] * 5, out_specs=[anyspec] *...  85.1 us
    pallas_call x2, Pallas kernels, products(): pl.pallas_call(functools.partial(products_kernel, sides, tile, cuts), gri...  67.3 us
    ppermute x3, waiting for transfers between devices, swap_across(): return lax.ppermute(shard, 'seq', [(i, i ^ 4) for i in range(8)])  45.6 us
    pallas_call x3, Pallas kernels, call_heads(): pl.pallas_call(kernel, grid=(heads,), in_specs=in_specs, out_specs=out_sp...  31.4 us
    all_gather x2, blocking collectives, prefix(): gathered = lax.all_gather(jnp.stack(part), axis)  23.4 us
  transfers between devices with their start and end apart: 22, of which 5 were waited for; matrix products, arithmetic and copies ran while one was open for 12% of the time, Pallas kernels for 21%

profile of v7, /device:TPU:0, one launch (start us, length us, event | category | flops | bytes accessed | tf_op | source)
XLA Modules:
  0.0 869.2 jit_solution(9684649356242022344)
XLA Ops:
  8.1 1.4 stack.57
  14.4 183.1 %gather_weights.1 = (bf16[2560,8320]{1,0:T(8,128)(2,1)}, bf16[320,5760]{1,0:T(8,128)(2,1)}) custom-call(bf16[80,8320]{1,0:T(8,128)(2,1)} %copy-done.29, bf16[80,7680]{1,0:T(8,128)(2,1)} %gate.1, bf16[80,7680]{1,0:T(8,128)(2,1)} %up.1, bf16[80,7680]{1,0:T(8,128)(2,1)} %down.1), custom_call_target="tpu_custom_call" | custom-call | tf_op jit(solution)/shard_map/gather_weights/pallas_call | solution.py:330
  197.6 5.4 collective-permute-start.1
  203.0 3.4 collective-permute-start.2
  206.4 2.3 slice.212
  209.9 2.8 slice_reduce_fusion
  213.9 14.6 %fusion.76 = (bf16[192,5120]{1,0:T(8,128)(2,1)S(1)}, f32[192,5120]{1,0:T(8,128)}) fusion(bf16[192,2560]{1,0:T(8,128)(2,1)} %fusion.43.refs_0_, bf16[2560,8320]{1,0:T(8,128)(2,1)} %get-tuple-element.65), kind=kOutput, calls=%fused_computation.173 | convolution fusion | flops 5034147840 | bytes 33095680 | tf_op jit(solution)/shard_map/dot_general | solution.py:50
  231.1 1.7 copy.77
  233.7 2.1 fusion.73
  238.4 7.2 mixer_forward.1
  246.4 11.8 %all-gather.2 = f32[8,2,2560]{2,1,0:T(2,128)S(1)} all-gather(f32[1,2,2560]{2,1,0:T(2,128)S(1)} %fusion.63), channel_id=2, replica_groups=mesh['seq'=8,'fsdp'=4] {'seq'}, dimensions={0}, use_global_device_ids=true | all-gather | bytes 184320 | tf_op jit(solution)/shard_map/all_gather | solution.py:29
  258.6 2.3 fusion.72
  261.0 10.0 %multiply_reduce_fusion = (f32[192]{0:T(256)S(1)}, f32[192,2560]{1,0:T(8,128)S(1)}) fusion(bf16[192,2560]{1,0:T(8,128)(2,1)} %get-tuple-element.227.refs_6_, bf16[2560,8320]{1,0:T(8,128)(2,1)} %get-tuple-element.65, bf16[1,192,2560]{2,1,0:T(8,128)(2,1)S(1)} %copy-done.24), kind=kOutput, calls=%fused_computation.83 | convolution fusion | flops 2518548224 | bytes 17040128 | tf_op jit(solution)/shard_map/dot_general | solution.py:50
  273.5 85.1 %gather_rows.1 = (bf16[768,2560]{1,0:T(8,128)(2,1)}, bf16[768,2560]{1,0:T(8,128)(2,1)}, bf16[768,2560]{1,0:T(8,128)(2,1)}, bf16[768,2560]{1,0:T(8,128)(2,1)}) custom-call(bf16[192,2560]{1,0:T(8,128)(2,1)} %multiply_convert_fusion.2.normed, bf16[192,2560]{1,0:T(8,128)(2,1)} %bitcast.14.grad0, bf16[192,2560]{1,0:T(8,128)(2,1)} %collective-permute-done.1.grad1, ...), custom_call_target="tpu_custom_call" | custom-call | tf_op jit(solution)/shard_map/gather_rows/pallas_call | solution.py:448
  358.7 12.4 %fusion.18 = f32[768,1920]{1,0:T(8,128)S(1)} fusion(bf16[768,2560]{1,0:T(8,128)(2,1)} %get-tuple-element.70.refs_0_, bf16[2560,5760]{1,0:T(8,128)(2,1)} %all-gather.6.cloned.1.call-done), kind=kOutput, calls=%fused_computation.20 | convolution fusion | flops 7549747200 | bytes 19660800 | tf_op jit(solution)/shard_map/dot_general | solution.py:50
  371.2 12.9 %fusion.14 = f32[768,1920]{1,0:T(8,128)} fusion(bf16[768,2560]{1,0:T(8,128)(2,1)S(1)} %copy-done.44, bf16[2560,5760]{1,0:T(8,128)(2,1)} %all-gather.6.cloned.1.call-done), kind=kOutput, calls=%fused_computation.16 | convolution fusion | flops 7549747200 | bytes 19660800 | tf_op jit(solution)/shard_map/dot_general | solution.py:50
  384.0 17.4 %multiply_convert_fusion = (bf16[768,1920]{1,0:T(8,128)(2,1)S(1)}, bf16[768,1920]{1,0:T(8,128)(2,1)S(1)}, bf16[768,1920]{1,0:T(8,128)(2,1)}) fusion(f32[768,1920]{1,0:T(8,128)S(1)} %fusion.18, f32[768,1920]{1,0:T(8,128)} %fusion.14, bf16[768,2560]{1,0:T(8,128)(2,1)S(1)} %copy-done.45, bf16[2560,5760]{1,0:T(8,128)(2,1)} %all-gather.6.cloned.1.call-done), kind=kOutput, calls=%fused_computation.35 | convolution fusion | flops 7586611200 | bytes 34406400 | tf_op jit(solution)/shard_map/dot_general | solution.py:50
  401.5 13.1 %fusion.12 = f32[768,2560]{1,0:T(8,128)S(1)} fusion(bf16[768,1920]{1,0:T(8,128)(2,1)S(1)} %get-tuple-element.223.refs_6_, bf16[2560,5760]{1,0:T(8,128)(2,1)} %all-gather.6.cloned.1.call-done), kind=kOutput, calls=%fused_computation.14 | convolution fusion | flops 7549747200 | bytes 20643840 | tf_op jit(solution)/shard_map/dot_general | solution.py:50
  414.6 12.5 %add_convert_fusion = bf16[768,2560]{1,0:T(8,128)(2,1)} fusion(f32[768,2560]{1,0:T(8,128)S(1)} %fusion.12, bf16[768,1920]{1,0:T(8,128)(2,1)S(1)} %get-tuple-element.224.refs_4_, bf16[2560,5760]{1,0:T(8,128)(2,1)} %all-gather.6.cloned.1.call-done), kind=kOutput, calls=%fused_computation.22 | convolution fusion | flops 7553679360 | bytes 24576000 | tf_op jit(solution)/shard_map/dot_general | solution.py:50
  428.7 14.1 %fusion.32 = bf16[768,2560]{1,0:T(8,128)(2,1)} fusion(bf16[768,1920]{1,0:T(8,128)(2,1)} %get-tuple-element.225.refs_8_, bf16[2560,5760]{1,0:T(8,128)(2,1)} %all-gather.6.cloned.1.call-done), kind=kOutput, calls=%fused_computation.38 | convolution fusion | flops 7551713280 | bytes 16711680 | tf_op jit(solution)/shard_map/dot_general | solution.py:50
  442.8 45.0 %feed_forward_products.1 = (bf16[160,5760]{1,0:T(8,128)(2,1)}, bf16[160,5760]{1,0:T(8,128)(2,1)}, bf16[160,5760]{1,0:T(8,128)(2,1)}, bf16[160,5760]{1,0:T(8,128)...) custom-call(s32[5]{0:T(128)} %stack.64.place, ...), custom_call_target="tpu_custom_call" | custom-call | flops 22649241600 | bytes 14745600 | tf_op jit(solution)/shard_map/feed_forward_products/pallas_call | solution.py:525
  487.8 1.6 collective-permute-start.7
  489.4 7.8 reduce-scatter.5.cloned.1.call-done
  497.2 2.8 fusion.46
  500.0 2.9 fusion.71.refs_2_
  502.9 7.4 fusion.4.grad_mixed
  510.5 12.8 %mixer_backward_scan.1 = (bf16[192,2560]{1,0:T(8,128)(2,1)S(1)}, f32[192,2560]{1,0:T(8,128)S(1)}, f32[192,2560]{1,0:T(8,128)S(1)}, f32[8,2560]{1,0:T(8,128)S(1)}) custom-call(f32[192,2560]{1,0:T(8,128)S(1)} %fusion.4.grad_mixed, f32[192,2560]{1,0:T(8,128)S(1)} %copy-done.7, f32[192,2560]{1,0:T(8,128)S(1)} %copy-done.6, f32[192,2560]{1,0:T(8,128)S(1)} %copy-done.1, ...), custom_call_target="tpu_custom_call" | custom-call | tf_op jit(solution)/shard_map/mixer_backward_scan/pallas_call | solution.py:843
  523.4 11.6 %all-gather.3 = f32[8,2,2560]{2,1,0:T(2,128)S(1)} all-gather(f32[1,2,2560]{2,1,0:T(2,128)S(1)} %fusion.64), channel_id=3, replica_groups=mesh['seq'=8,'fsdp'=4] {'seq'}, dimensions={0}, use_global_device_ids=true | all-gather | bytes 184320 | tf_op jit(solution)/shard_map/all_gather | solution.py:29
  535.4 11.4 %mixer_backward.1 = (f32[192,2560]{1,0:T(8,128)S(1)}, f32[8,2560]{1,0:T(8,128)S(1)}, bf16[2560,256]{1,0:T(8,128)(2,1)S(1)}, bf16[2560,256]{1,0:T(8,128)(2,1)S(1)}, f32[8,2560]{1,0:T(8,128)S(1)}) custom-call(f32[192,2560]{1,0:T(8,128)S(1)} %get-tuple-element.83.rev_cum, f32[192,2560]{1,0:T(8,128)S(1)} %get-tuple-element.84.rev_grad, ...), custom_call_target="tpu_custom_call" | custom-call | tf_op jit(solution)/shard_map/mixer_backward/pallas_call | solution.py:843
  548.2 5.0 add_convert_fusion.1
  553.4 1.5 pad_maximum_fusion.refs_4_
  554.9 16.1 %fusion.44 = (bf16[2560]{0:T(1024)(128)(2,1)S(1)}, f32[192]{0:T(256)S(1)}, f32[192,2560]{1,0:T(8,128)}) fusion(bf16[1,192,2560]{2,1,0:T(8,128)(2,1)} %param.17, f32[192]{0:T(256)S(1)} %copy-done.43, f32[2560]{0:T(1024)S(1)} %copy-done.37, bf16[192,5120]{1,0:T(8,128)(2,1)} %pad_maximum_fusion.refs_4_, bf16[2560,8320]{1,0:T(8,128)(2,1)} %get-tuple-element.65), kind=kOutput, calls=%fused_computation.62 | convolution fusion | flops 5036602880 | bytes 31146496 | tf_op jit(solution)/shard_map/dot_general | solution.py:50
  571.8 1.6 copy-done.20
  576.8 3.8 collective-permute-done.10.refs_1_
  580.6 2.9 collective-permute-start.15
  585.5 1.5 collective-permute-start.18
  587.0 5.5 fusion.62
  592.5 1.8 fusion.38
  595.9 22.3 %mixer_products.1 = bf16[1280,7680]{1,0:T(8,128)(2,1)} custom-call(s32[5]{0:T(128)} %stack.64.place, bf16[192,2560]{1,0:T(8,128)(2,1)} %fusion.43.refs_0_, bf16[192,2560]{1,0:T(8,128)(2,1)} %collective-permute-done.10.refs_1_, bf16[192,2560]{1,0:T(8,128)(2,1)} %fusion.71.refs_2_, bf16[192,2560]{1,0:T(8,128)(2,1)} %collective-permute-done.11.refs_3_, ...), custom_call_target="tpu_custom_call" | custom-call | flops 7549747200 | bytes 19660800 | tf_op jit(solution)/shard_map/mixer_products/pallas_call | solution.py:525
  618.2 6.6 collective-permute-done.15
  624.8 39.0 %collective-permute-done.16 = bf16[160,5760]{1,0:T(8,128)(2,1)} collective-permute-done((bf16[160,5760]{1,0:T(8,128)(2,1)}, bf16[160,5760]{1,0:T(8,128)(2,1)}, u32[]{:S(2)}, u32[]{:S(2)}) %collective-permute-start.16) | collective-permute-done | bytes 1843232 | tf_op jit(solution)/shard_map/ppermute | solution.py:777
  663.8 2.9 collective-permute-done.18
  666.7 2.4 convert_add_fusion.1
  669.1 2.4 convert_add_fusion.2
  671.5 4.6 fusion.20.mlp
  676.1 177.1 %scatter_gradients.1 = (bf16[80,8320]{1,0:T(8,128)(2,1)S(1)}, bf16[3,80,7680]{2,1,0:T(8,128)(2,1)}) custom-call(bf16[4,320,7680]{2,1,0:T(8,128)(2,1)} %bitcast.77, bf16[4,320,640]{2,1,0:T(8,128)(2,1)} %pad_maximum_fusion.1.rest, bf16[320,5760]{1,0:T(8,128)(2,1)} %fusion.20.mlp), custom_call_target="tpu_custom_call" | custom-call | tf_op jit(solution)/shard_map/scatter_gradients/pallas_call | solution.py:730
  853.4 1.5 fusion.74
  857.1 5.3 bitcast_convert_fusion
  (185 shorter events, 31.5 us)
Async XLA Ops:
  7.2 351.5 %all-gather.6.cloned.1.call-start = ((), (), s32[]{:S(2)}) async-start(), calls=%async_computation.2 | async-start | bytes 33177600 | tf_op jit(solution)/shard_map/all_gather | solution.py:900
  197.5 299.7 %reduce-scatter.5.cloned.1.call-start = ((), (), s32[]{:S(2)}) async-start(), calls=%async_computation.4 | async-start | bytes 4915200 | tf_op jit(solution)/shard_map/reduce_scatter | solution.py:959
  197.6 75.9 %collective-permute-start.1 = (bf16[192,2560]{1,0:T(8,128)(2,1)}, bf16[192,2560]{1,0:T(8,128)(2,1)}, u32[]{:S(2)}, u32[]{:S(2)}) collective-permute-start(bf16[192,2560]{1,0:T(8,128)(2,1)} %bitcast.14.grad0), channel_id=1, source_target_pairs={{0,1},{1,2},{2,3},{3,0},{4,5},{5,6},{6,7},{7,4},{8,9},{9,10},{10,1... | collective-permute-start | bytes 2949128 | tf_op jit(solution)/shard_map/ppermute | solution.py:763
  203.0 70.5 %collective-permute-start.2 = (bf16[192,2560]{1,0:T(8,128)(2,1)}, bf16[192,2560]{1,0:T(8,128)(2,1)}, u32[]{:S(2)}, u32[]{:S(2)}) collective-permute-start(bf16[192,2560]{1,0:T(8,128)(2,1)} %bitcast.14.grad0), channel_id=1, source_target_pairs={{0,2},{1,3},{2,0},{3,1},{4,6},{5,7},{6,4},{7,5},{8,10},{9,11},{10,... | collective-permute-start | bytes 2949128 | tf_op jit(solution)/shard_map/ppermute | solution.py:763
  206.4 67.1 %collective-permute-start.3 = (bf16[192,2560]{1,0:T(8,128)(2,1)}, bf16[192,2560]{1,0:T(8,128)(2,1)}, u32[]{:S(2)}, u32[]{:S(2)}) collective-permute-start(bf16[192,2560]{1,0:T(8,128)(2,1)} %bitcast.14.grad0), channel_id=1, source_target_pairs={{0,3},{1,0},{2,1},{3,2},{4,7},{5,4},{6,5},{7,6},{8,11},{9,8},{10,9... | collective-permute-start | bytes 2949128 | tf_op jit(solution)/shard_map/ppermute | solution.py:763
  229.8 7.3 collective-permute-start
  237.1 9.3 %copy-start.15 = (f32[8,2560]{1,0:T(8,128)}, f32[8,2560]{1,0:T(8,128)S(1)}, u32[]{:S(2)}) copy-start(f32[8,2560]{1,0:T(8,128)S(1)} %pad_convert_fusion.prior) | copy-start | bytes 245764
  238.4 20.3 %copy-start.30 = (f32[192,5120]{1,0:T(8,128)S(1)}, f32[192,5120]{1,0:T(8,128)}, u32[]{:S(2)}) copy-start(f32[192,5120]{1,0:T(8,128)} %get-tuple-element.251) | copy-start | bytes 11796484
  245.6 15.4 %copy-start = (f32[192,2560]{1,0:T(8,128)}, f32[192,2560]{1,0:T(8,128)S(1)}, u32[]{:S(2)}) copy-start(f32[192,2560]{1,0:T(8,128)S(1)} %get-tuple-element.67.cum) | copy-start | bytes 5898244
  245.6 15.4 %copy-start.2 = (f32[192,2560]{1,0:T(8,128)}, f32[192,2560]{1,0:T(8,128)S(1)}, u32[]{:S(2)}) copy-start(f32[192,2560]{1,0:T(8,128)S(1)} %get-tuple-element.66.local) | copy-start | bytes 5898244
  245.6 15.4 %copy-start.5 = (f32[192,2560]{1,0:T(8,128)}, f32[192,2560]{1,0:T(8,128)S(1)}, u32[]{:S(2)}) copy-start(f32[192,2560]{1,0:T(8,128)S(1)} %get-tuple-element.82.rate_pre) | copy-start | bytes 5898244
  245.6 15.4 %copy-start.8 = (f32[192,2560]{1,0:T(8,128)}, f32[192,2560]{1,0:T(8,128)S(1)}, u32[]{:S(2)}) copy-start(f32[192,2560]{1,0:T(8,128)S(1)} %get-tuple-element.86.input_pre) | copy-start | bytes 5898244
  245.6 15.4 %copy-start.13 = (bf16[192,2560]{1,0:T(8,128)(2,1)}, bf16[192,2560]{1,0:T(8,128)(2,1)S(1)}, u32[]{:S(2)}) copy-start(bf16[192,2560]{1,0:T(8,128)(2,1)S(1)} %get-tuple-element.87.conv) | copy-start | bytes 2949124
  358.7 12.4 %copy-start.44 = (bf16[768,2560]{1,0:T(8,128)(2,1)S(1)}, bf16[768,2560]{1,0:T(8,128)(2,1)}, u32[]{:S(2)}) copy-start(bf16[768,2560]{1,0:T(8,128)(2,1)} %get-tuple-element.70.refs_0_) | copy-start | bytes 11796484
  371.2 12.9 %copy-start.45 = (bf16[768,2560]{1,0:T(8,128)(2,1)S(1)}, bf16[768,2560]{1,0:T(8,128)(2,1)}, u32[]{:S(2)}) copy-start(bf16[768,2560]{1,0:T(8,128)(2,1)} %get-tuple-element.72.refs_2_) | copy-start | bytes 11796484
  401.5 13.1 %copy-start.46 = (bf16[768,1920]{1,0:T(8,128)(2,1)}, bf16[768,1920]{1,0:T(8,128)(2,1)S(1)}, u32[]{:S(2)}) copy-start(bf16[768,1920]{1,0:T(8,128)(2,1)S(1)} %get-tuple-element.223.refs_6_) | copy-start | bytes 8847364
  401.5 13.1 %copy-start.47 = (bf16[768,1920]{1,0:T(8,128)(2,1)}, bf16[768,1920]{1,0:T(8,128)(2,1)S(1)}, u32[]{:S(2)}) copy-start(bf16[768,1920]{1,0:T(8,128)(2,1)S(1)} %get-tuple-element.224.refs_4_) | copy-start | bytes 8847364
  427.1 159.9 %reduce-scatter.3.cloned.1.call-start = ((), (), s32[]{:S(2)}) async-start(), calls=%async_computation.3 | async-start | bytes 4915200 | tf_op jit(solution)/shard_map/reduce_scatter | solution.py:986
  427.1 15.7 %collective-permute-start.4 = (bf16[768,1920]{1,0:T(8,128)(2,1)}, bf16[768,1920]{1,0:T(8,128)(2,1)}, u32[]{:S(2)}, u32[]{:S(2)}) collective-permute-start(bf16[768,1920]{1,0:T(8,128)(2,1)} %copy-done.47), channel_id=1, source_target_pairs={{0,4},{4,0},{8,12},{12,8},{16,20},{20,16},{24,28},{28,24},{1,5},{5... | collective-permute-start | bytes 8847368 | tf_op jit(solution)/shard_map/ppermute | solution.py:769
  427.5 15.3 %collective-permute-start.5 = (bf16[768,1920]{1,0:T(8,128)(2,1)}, bf16[768,1920]{1,0:T(8,128)(2,1)}, u32[]{:S(2)}, u32[]{:S(2)}) collective-permute-start(bf16[768,1920]{1,0:T(8,128)(2,1)} %copy-done.46), channel_id=1, source_target_pairs={{0,4},{4,0},{8,12},{12,8},{16,20},{20,16},{24,28},{28,24},{1,5},{5... | collective-permute-start | bytes 8847368 | tf_op jit(solution)/shard_map/ppermute | solution.py:769
  427.7 15.1 %collective-permute-start.6 = (bf16[768,1920]{1,0:T(8,128)(2,1)}, bf16[768,1920]{1,0:T(8,128)(2,1)}, u32[]{:S(2)}, u32[]{:S(2)}) collective-permute-start(bf16[768,1920]{1,0:T(8,128)(2,1)} %get-tuple-element.225.refs_8_), channel_id=1, source_target_pairs={{0,4},{4,0},{8,12},{12,8},{16,20},{20,16},{24,28},{28,24},{1,5},{5... | collective-permute-start | bytes 8847368 | tf_op jit(solution)/shard_map/ppermute | solution.py:769
  487.8 60.4 %collective-permute-start.7 = (bf16[160,5760]{1,0:T(8,128)(2,1)}, bf16[160,5760]{1,0:T(8,128)(2,1)}, u32[]{:S(2)}, u32[]{:S(2)}) collective-permute-start(bf16[160,5760]{1,0:T(8,128)(2,1)} %get-tuple-element.77), channel_id=1, source_target_pairs={{0,16},{4,20},{8,24},{12,28},{16,0},{20,4},{24,8},{28,12},{1,17},{... | collective-permute-start | bytes 5529608 | tf_op jit(solution)/shard_map/ppermute | solution.py:777
  489.4 58.8 %collective-permute-start.8 = (bf16[160,5760]{1,0:T(8,128)(2,1)}, bf16[160,5760]{1,0:T(8,128)(2,1)}, u32[]{:S(2)}, u32[]{:S(2)}) collective-permute-start(bf16[160,5760]{1,0:T(8,128)(2,1)} %get-tuple-element.78), channel_id=1, source_target_pairs={{0,8},{4,12},{8,0},{12,4},{16,24},{20,28},{24,16},{28,20},{1,9},{5... | collective-permute-start | bytes 5529608 | tf_op jit(solution)/shard_map/ppermute | solution.py:773
  502.9 7.4 copy-start.35
  502.9 7.4 copy-start.1
  502.9 7.4 copy-start.6
  502.9 7.5 copy-start.7
  510.5 12.8 %copy-start.39 = (f32[1,2560]{1,0:T(1,128)S(1)}, f32[1,2560]{1,0:T(1,128)}, u32[]{:S(2)}) copy-start(f32[1,2560]{1,0:T(1,128)} %copy-done.38) | copy-start | bytes 30724
  510.5 24.9 %copy-start.4 = (bf16[192,2560]{1,0:T(8,128)(2,1)S(1)}, bf16[192,2560]{1,0:T(8,128)(2,1)}, u32[]{:S(2)}) copy-start(bf16[192,2560]{1,0:T(8,128)(2,1)} %slice.278.branch) | copy-start | bytes 2949124
  510.5 24.9 %copy-start.14 = (bf16[192,2560]{1,0:T(8,128)(2,1)S(1)}, bf16[192,2560]{1,0:T(8,128)(2,1)}, u32[]{:S(2)}) copy-start(bf16[192,2560]{1,0:T(8,128)(2,1)} %copy-done.13) | copy-start | bytes 2949124
  510.5 24.9 %copy-start.16 = (f32[8,2560]{1,0:T(8,128)S(1)}, f32[8,2560]{1,0:T(8,128)}, u32[]{:S(2)}) copy-start(f32[8,2560]{1,0:T(8,128)} %copy-done.15) | copy-start | bytes 245764
  535.4 12.8 %copy-start.27 = (bf16[160,5760]{1,0:T(8,128)(2,1)S(1)}, bf16[160,5760]{1,0:T(8,128)(2,1)}, u32[]{:S(2)}) copy-start(bf16[160,5760]{1,0:T(8,128)(2,1)} %get-tuple-element.76) | copy-start | bytes 5529604
  535.4 12.8 %copy-start.28 = (bf16[160,5760]{1,0:T(8,128)(2,1)S(1)}, bf16[160,5760]{1,0:T(8,128)(2,1)}, u32[]{:S(2)}) copy-start(bf16[160,5760]{1,0:T(8,128)(2,1)} %get-tuple-element.90) | copy-start | bytes 5529604
  546.8 6.3 copy-start.9
  546.9 6.3 copy-start.11
  546.9 6.4 collective-permute-start.9
  554.9 16.5 %copy-start.10 = (bf16[2560,256]{1,0:T(8,128)(2,1)S(1)}, bf16[2560,256]{1,0:T(8,128)(2,1)}, u32[]{:S(2)}) copy-start(bf16[2560,256]{1,0:T(8,128)(2,1)} %copy-done.9) | copy-start | bytes 3932164
  554.9 16.5 %copy-start.12 = (bf16[2560,256]{1,0:T(8,128)(2,1)S(1)}, bf16[2560,256]{1,0:T(8,128)(2,1)}, u32[]{:S(2)}) copy-start(bf16[2560,256]{1,0:T(8,128)(2,1)} %copy-done.11) | copy-start | bytes 3932164
  571.7 15.2 %copy-start.19 = (f32[192,2560]{1,0:T(8,128)S(1)}, f32[192,2560]{1,0:T(8,128)}, u32[]{:S(2)}) copy-start(f32[192,2560]{1,0:T(8,128)} %copy-done.17) | copy-start | bytes 5898244
  574.8 10.7 %collective-permute-start.14 = (bf16[4,320,640]{2,1,0:T(8,128)(2,1)}, bf16[4,320,640]{2,1,0:T(8,128)(2,1)}, u32[]{:S(2)}, u32[]{:S(2)}) collective-permute-start(bf16[4,320,640]{2,1,0:T(8,128)(2,1)} %dynamic-slice_bitcast_fusion), channel_id=1, source_target_pairs={{0,4},{4,0},{8,12},{12,8},{16,20},{20,16},{24,28},{28,24},{1,5},{5... | collective-permute-start | bytes 4915208 | tf_op jit(solution)/shard_map/ppermute | solution.py:769
  575.7 4.9 collective-permute-start.10
  575.7 7.8 collective-permute-start.13
  576.3 8.7 collective-permute-start.11
  576.3 19.7 %collective-permute-start.12 = (bf16[192,5120]{1,0:T(8,128)(2,1)}, bf16[192,5120]{1,0:T(8,128)(2,1)}, u32[]{:S(2)}, u32[]{:S(2)}) collective-permute-start(bf16[192,5120]{1,0:T(8,128)(2,1)} %pad_maximum_fusion.refs_4_), channel_id=1, source_target_pairs={{0,4},{4,0},{8,12},{12,8},{16,20},{20,16},{24,28},{28,24},{1,5},{5... | collective-permute-start | bytes 5898248 | tf_op jit(solution)/shard_map/ppermute | solution.py:769
  580.6 44.2 %collective-permute-start.15 = (bf16[160,5760]{1,0:T(8,128)(2,1)}, bf16[160,5760]{1,0:T(8,128)(2,1)}, u32[]{:S(2)}, u32[]{:S(2)}) collective-permute-start(bf16[160,5760]{1,0:T(8,128)(2,1)} %get-tuple-element.100), channel_id=1, source_target_pairs={{0,16},{4,20},{8,24},{12,28},{16,0},{20,4},{24,8},{28,12},{1,17},{... | collective-permute-start | bytes 5529608 | tf_op jit(solution)/shard_map/ppermute | solution.py:777
  583.5 80.3 %collective-permute-start.16 = (bf16[160,5760]{1,0:T(8,128)(2,1)}, bf16[160,5760]{1,0:T(8,128)(2,1)}, u32[]{:S(2)}, u32[]{:S(2)}) collective-permute-start(bf16[160,5760]{1,0:T(8,128)(2,1)} %get-tuple-element.101), channel_id=1, source_target_pairs={{0,16},{4,20},{8,24},{12,28},{16,0},{20,4},{24,8},{28,12},{1,17},{... | collective-permute-start | bytes 5529608 | tf_op jit(solution)/shard_map/ppermute | solution.py:777
  584.9 78.9 %collective-permute-start.17 = (bf16[160,5760]{1,0:T(8,128)(2,1)}, bf16[160,5760]{1,0:T(8,128)(2,1)}, u32[]{:S(2)}, u32[]{:S(2)}) collective-permute-start(bf16[160,5760]{1,0:T(8,128)(2,1)} %get-tuple-element.102), channel_id=1, source_target_pairs={{0,8},{4,12},{8,0},{12,4},{16,24},{20,28},{24,16},{28,20},{1,9},{5... | collective-permute-start | bytes 5529608 | tf_op jit(solution)/shard_map/ppermute | solution.py:773
  585.5 81.2 %collective-permute-start.18 = (bf16[160,5760]{1,0:T(8,128)(2,1)}, bf16[160,5760]{1,0:T(8,128)(2,1)}, u32[]{:S(2)}, u32[]{:S(2)}) collective-permute-start(bf16[160,5760]{1,0:T(8,128)(2,1)} %get-tuple-element.103), channel_id=1, source_target_pairs={{0,8},{4,12},{8,0},{12,4},{16,24},{20,28},{24,16},{28,20},{1,9},{5... | collective-permute-start | bytes 5529608 | tf_op jit(solution)/shard_map/ppermute | solution.py:773
  (22 other events, 55.1 us)
Sparse Core Ops, SparseCore 0:
  197.6 150.0 all-gather.5
  427.2 70.0 reduce-scatter.4
  499.5 73.0 reduce-scatter.2

commit v8 on v7

--- a/solution.py
+++ b/solution.py
@@ -456,90 +456,223 @@
     )(normed, *grads)
 
 
-def products_kernel(sides, tile, cuts, place, *refs):
+def column_tiles(cols, size=512):
+    return [(start, min(size, cols - start)) for start in range(0, cols, size)]
+
+
+def feed_forward_kernel(
+    normed, grad_out, weights, hidden, hidden_other, pair, pair_other, back,
+    held, hidden_now, pair_now, sems, store_sem, core_send, core_recv,
+):
+    s, z, core, _, _ = places()
+    step = pl.program_id(0)
+    ff_part = held.shape[2]
+    model = held.shape[1]
+    rows = normed.shape[0]
+    tiles = column_tiles(ff_part)
+    made = ((hidden_now, hidden, hidden_other), (pair_now, pair, pair_other))
+
+    def load(n, m):
+        start, size = tiles[n]
+        return pltpu.make_async_copy(
+            weights.at[:, pl.ds(m * ff_part + start, size)], held.at[m, :, pl.ds(start, size)], sems.at[n, m]
+        )
+
+    def kept(n, turn):
+        now, mine, _ = made[n]
+        return pltpu.make_async_copy(now.at[turn], mine.at[pl.ds(turn * rows, rows), :], store_sem.at[turn, n])
+
+    def handed(n, turn):
+        now, _, other = made[n]
+        return pltpu.make_async_remote_copy(
+            src_ref=now.at[turn],
+            dst_ref=other.at[pl.ds(turn * rows, rows), :],
+            send_sem=core_send.at[turn, n],
+            recv_sem=core_recv.at[turn, n],
+            device_id=(core, z),
+            device_id_type=MESH,
+        )
+
+    @pl.when(step == 0)
+    def _():
+        for n in range(len(tiles)):
+            for m in range(3):
+                load(n, m).start()
+        greet([(core, z)])
+
+    for n, (start, size) in enumerate(tiles):
+        cols = slice(start, start + size)
+
+        @pl.when(step == 0)
+        def _(n=n):
+            for m in range(3):
+                load(n, m).wait()
+
+        gate = mm(normed[...], held[0, :, cols], ((1,), (0,)))
+        value, slope = gelu_parts(gate)
+        up = mm(normed[...], held[1, :, cols], ((1,), (0,)))
+        hidden_now[step, :, cols] = (value * up).astype(bf16)
+        grad_hidden = mm(grad_out[...], held[2, :, cols], ((1,), (0,)))
+        pair_now[step, :, cols] = (grad_hidden * up * slope).astype(bf16)
+        pair_now[step, :, slice(ff_part + start, ff_part + start + size)] = (grad_hidden * value).astype(bf16)
+
+    for turn in range(2):
+
+        @pl.when(step == turn)
+        def _(turn=turn):
+            for n in range(2):
+                handed(n, turn).start()
+                kept(n, turn).start()
+
+    def back_tile(turn, carry):
+        cols = pl.ds(pl.multiple_of(turn * 512, 512), 512)
+        total = mm(pair_now[step, :, :ff_part], held[0, cols, :], ((1,), (1,)))
+        total = total + mm(pair_now[step, :, ff_part:], held[1, cols, :], ((1,), (1,)))
+        back[:, cols] = total.astype(bf16)
+        return carry
+
+    lax.fori_loop(0, model // 512, back_tile, 0)
+
+    @pl.when(step == 1)
+    def _():
+        for turn in range(2):
+            for n in range(2):
+                kept(n, turn).wait()
+                handed(n, turn).wait()
+
+
+def feed_forward(normed, grad_out, weights):
+    tok, model = normed.shape
+    ff_part = weights.shape[1] // 3
+    rows = tok // 2
+    anyspec = pl.BlockSpec(memory_space=pl.ANY)
+    dma = pltpu.SemaphoreType.DMA
+    block = pl.BlockSpec((rows, model), lambda i: (i, 0))
+    return pl.pallas_call(
+        feed_forward_kernel,
+        grid=(2,),
+        in_specs=[block, block, anyspec],
+        out_specs=[anyspec] * 4 + [block],
+        out_shape=[
+            jax.ShapeDtypeStruct((tok, cols), bf16)
+            for cols in (ff_part, ff_part, 2 * ff_part, 2 * ff_part, model)
+        ],
+        scratch_shapes=[
+            pltpu.VMEM((3, model, ff_part), bf16),
+            pltpu.VMEM((2, rows, ff_part), bf16),
+            pltpu.VMEM((2, rows, 2 * ff_part), bf16),
+            dma((len(column_tiles(ff_part)), 3)), dma((2, 2)), dma((2, 2)), dma((2, 2)),
+        ],
+        compiler_params=pltpu.CompilerParams(
+            collective_id=4, has_side_effects=True, vmem_limit_bytes=60 * 1024 * 1024
+        ),
+        name="feed_forward",
+    )(normed, grad_out, weights)
+
+
+def products_kernel(sides, cuts, spots, place, *refs):
     lefts = 1 + max(side for side, _ in sides)
     left_refs = refs[: 2 * lefts]
     right_refs = refs[2 * lefts : 2 * lefts + 2 * len(sides)]
-    outs = refs[2 * lefts + 2 * len(sides) : -3]
-    turned, stage, right = refs[-3:]
+    outs = refs[2 * lefts + 2 * len(sides) : -4]
+    turned, slots, stage, sems = refs[-4:]
     tok = left_refs[0].shape[0]
     chip_cols = left_refs[0].shape[1] // 4
     half = chip_cols // 2
     step = pl.program_id(0)
 
-    @pl.when(step == 0)
-    def _():
-        for side in range(lefts):
-            for q in range(4):
-                cols = pl.ds(pl.multiple_of(place[q] * chip_cols, 128), chip_cols)
-                stage[:, :] = jnp.concatenate(
-                    [left_refs[2 * side][:, cols], left_refs[2 * side + 1][:, cols]], axis=0
-                ).T
-                turned[side, q] = stage[pl.ds(pl.multiple_of(place[4] * half, 16), half), :]
+    def load(side, q, who):
+        cols = pl.ds(pl.multiple_of(place[q] * chip_cols, 128), chip_cols)
+        return pltpu.make_async_copy(
+            left_refs[2 * side + who].at[:, cols], slots.at[q % 2, who], sems.at[q % 2, who]
+        )
+
+    def fetch(side):
+        for q in range(2):
+            for who in range(2):
+                load(side, q, who).start()
+
+    def turn(side):
+        piece = half // 2
+        for q in range(4):
+            for who in range(2):
+                load(side, q, who).wait()
+                stage[...] = slots[q % 2, who].T
+                for part in range(2):
+                    spot = spots[2 * q + part] * piece
+                    turned[who, spot : spot + piece, :] = stage[
+                        pl.ds(pl.multiple_of(place[4] * half + part * piece, 16), piece), :
+                    ]
+                if q < 2:
+                    load(side, q + 2, who).start()
+
+    def multiply(own, other):
+        def tile(cols):
+            block = mm(turned[0], own[:, cols], ((1,), (0,)))
+            block = (block + mm(turned[1], other[:, cols], ((1,), (0,)))).astype(bf16)
+            start = 0
+            for out, size in zip(outs, cuts):
+                out[:, cols] = block[start : start + size]
+                start += size
+
+        width = own.shape[1]
+
+        def one(turn, carry):
+            tile(pl.ds(pl.multiple_of(turn * 512, 512), 512))
+            return carry
+
+        lax.fori_loop(0, width // 512, one, 0)
+        if width % 512:
+            tile(slice(width // 512 * 512, width))
 
     first = 0
-    side_now = 0
-    for n, (side, tiles) in enumerate(sides):
-
-        @pl.when((step >= first) & (step < first + tiles))
-        def _(n=n):
-            right[0:tok, :] = right_refs[2 * n][...]
-            right[tok:, :] = right_refs[2 * n + 1][...]
-
-        side_now = jnp.where(step >= first, side, side_now)
-        first += tiles
-
-    start, index, inside = 0, 0, 0
-    for q in range(4):
-        block = mm(turned[side_now, q], right[...], ((1,), (0,))).astype(bf16)
-        taken = 0
-        while taken < half:
-            size = min(cuts[index] - inside, half - taken)
-            outs[index][inside : inside + size, :] = block[taken : taken + size]
-            taken += size
-            inside += size
-            if inside == cuts[index]:
-                index, inside = index + 1, 0
-
-
-def products(lefts, rights, cuts, name):
+    before = None
+    for n, (side, blocks) in enumerate(sides):
+        if side != before:
+            if first == 0:
+                pl.when(step == 0)(functools.partial(fetch, side))
+            pl.when(step == first)(functools.partial(turn, side))
+        before = side
+        inside = (step >= first) & (step < first + blocks)
+        pl.when(inside)(functools.partial(multiply, right_refs[2 * n], right_refs[2 * n + 1]))
+        first += blocks
+        if n + 1 < len(sides) and sides[n + 1][0] != side:
+            pl.when(step == first - 1)(functools.partial(fetch, sides[n + 1][0]))
+
+
+def products(lefts, rights, cuts, spots, width, name):
     seq = lax.axis_index("seq")
     core, x, y = seq % 2, (seq // 2) % 2, seq // 4
     place = jnp.stack([(1 - y) * 2 + 1 - x, y * 2 + 1 - x, (1 - y) * 2 + x, y * 2 + x, core]).astype(jnp.int32)
-    tile = 640
     tok, model = lefts[0][0].shape
-    sides = tuple((side, own.shape[1] // tile) for side, own, _ in rights)
-    total = sum(tiles for _, tiles in sides)
-    in_specs = [
-        pl.BlockSpec((tok, model), lambda j, place: (0, 0), pipeline_mode=pl.Buffered(1))
-    ] * (2 * len(lefts))
+    sides = tuple((side, own.shape[1] // width) for side, own, _ in rights)
+    total = sum(blocks for _, blocks in sides)
+    in_specs = [pl.BlockSpec(memory_space=pl.ANY)] * (2 * len(lefts))
     first = 0
-    for _, tiles in sides:
-
-        def index(j, place, first=first, tiles=tiles):
-            return (0, jnp.clip(j - first, 0, tiles - 1))
-
-        in_specs += [pl.BlockSpec((tok, tile), index)] * 2
-        first += tiles
+    for _, blocks in sides:
+
+        def index(j, place, first=first, blocks=blocks):
+            return (0, jnp.clip(j - first, 0, blocks - 1))
+
+        in_specs += [pl.BlockSpec((tok, width), index)] * 2
+        first += blocks
     half = model // 8
     return pl.pallas_call(
-        functools.partial(products_kernel, sides, tile, cuts),
+        functools.partial(products_kernel, sides, cuts, spots),
         grid_spec=pltpu.PrefetchScalarGridSpec(
             num_scalar_prefetch=1,
             grid=(total,),
             in_specs=in_specs,
-            out_specs=[pl.BlockSpec((rows, tile), lambda j, place: (0, j)) for rows in cuts],
+            out_specs=[pl.BlockSpec((rows, width), lambda j, place: (0, j)) for rows in cuts],
             scratch_shapes=[
-                pltpu.VMEM((len(lefts), 4, half, 2 * tok), bf16),
-                pltpu.VMEM((2 * half, 2 * tok), bf16),
-                pltpu.VMEM((2 * tok, tile), bf16),
+                pltpu.VMEM((2, 4 * half, tok), bf16),
+                pltpu.VMEM((2, 2, tok, 2 * half), bf16),
+                pltpu.VMEM((2 * half, tok), bf16),
+                pltpu.SemaphoreType.DMA((2, 2)),
             ],
         ),
-        out_shape=[jax.ShapeDtypeStruct((rows, total * tile), bf16) for rows in cuts],
-        compiler_params=pltpu.CompilerParams(vmem_limit_bytes=56 * 1024 * 1024),
-        cost_estimate=pl.CostEstimate(
-            flops=2 * 4 * half * 2 * tok * total * tile, bytes_accessed=4 * half * total * tile * 2, transcendentals=0
-        ),
+        out_shape=[jax.ShapeDtypeStruct((rows, total * width), bf16) for rows in cuts],
+        compiler_params=pltpu.CompilerParams(vmem_limit_bytes=58 * 1024 * 1024),
         name=name,
     )(place, *[a for pair in lefts for a in pair], *[a for _, own, other in rights for a in (own, other)])
 
@@ -787,7 +920,9 @@
     main = products(
         [(normed, swap_cores(normed)), (grad_mix, swap_cores(grad_mix))],
         [(0, grad_both, swap_cores(grad_both)), (1, mixed, swap_cores(mixed))],
-        (lru_rows(normed),),
+        (normed.shape[1] // 2,),
+        tuple(range(8)),
+        normed.shape[1],
         "mixer_products",
     )[0]
     grouped = rest.reshape(4, 2, -1, rest.shape[1])
@@ -805,10 +940,6 @@
     mine, *sent = [part.astype(f32) for part in mlp_parts]
     mlp_sum = mine + jnp.concatenate([sent[0] + sent[2], sent[1] + sent[3]], axis=0)
     return scatter(main.reshape(4, -1, main.shape[1]), rest, mlp_sum.astype(bf16))
-
-
-def lru_rows(values):
-    return values.shape[1] // 2
 
 
 def scatter_plain(normed, grad_both, grad_mix, mixed, rest, mlp_sum):
@@ -948,34 +1079,37 @@
         normed_all = lax.all_gather(normed_two, "fsdp", axis=0, tiled=True)
         grad_out_all = lax.all_gather(grad_out_late, "fsdp", axis=0, tiled=True)
     w_gate, w_up, w_down = mlp_w[:, :ff_part], mlp_w[:, ff_part : 2 * ff_part], mlp_w[:, 2 * ff_part :]
-    gate = mm(normed_all, w_gate, ((1,), (0,)))
-    up_val = mm(normed_all, w_up, ((1,), (0,)))
-    gelu_gate, gelu_slope = gelu_parts(gate)
-    hidden = (gelu_gate * up_val).astype(bf16)
-    grad_hidden = mm(grad_out_all, w_down, ((1,), (0,)))
-    grad_gate = (grad_hidden * up_val * gelu_slope).astype(bf16)
-    grad_up = (grad_hidden * gelu_gate).astype(bf16)
-    grad_normed_part = mm(grad_gate, w_gate, ((1,), (1,))) + mm(grad_up, w_up, ((1,), (1,)))
-    grad_normed_two = lax.psum_scatter(
-        grad_normed_part.astype(bf16), "fsdp", scatter_dimension=0, tiled=True
-    )
-    out_part = mm(hidden, w_down, ((1,), (1,))).astype(bf16)
+    if custom:
+        hidden, hidden_other, grad_pair, pair_other, grad_normed_part = feed_forward(
+            normed_all, grad_out_all, mlp_w
+        )
+    else:
+        gate = mm(normed_all, w_gate, ((1,), (0,)))
+        up_val = mm(normed_all, w_up, ((1,), (0,)))
+        gelu_gate, gelu_slope = gelu_parts(gate)
+        hidden = (gelu_gate * up_val).astype(bf16)
+        grad_hidden = mm(grad_out_all, w_down, ((1,), (0,)))
+        grad_gate = (grad_hidden * up_val * gelu_slope).astype(bf16)
+        grad_up = (grad_hidden * gelu_gate).astype(bf16)
+        grad_normed_part = (
+            mm(grad_gate, w_gate, ((1,), (1,))) + mm(grad_up, w_up, ((1,), (1,)))
+        ).astype(bf16)
+    grad_normed_two = lax.psum_scatter(grad_normed_part, "fsdp", scatter_dimension=0, tiled=True)
     if custom:
         half = model // 16
-        blocks = products(
+        early_across, early_beside, beside_low, across_high, mine = products(
             [(normed_all, normed_other), (grad_out_all, grad_out_other)],
-            [
-                (0, grad_gate, swap_cores(grad_gate)),
-                (0, grad_up, swap_cores(grad_up)),
-                (1, hidden, swap_cores(hidden)),
-            ],
-            (half,) * 6 + (2 * half,),
+            [(0, grad_pair, pair_other), (1, hidden, hidden_other)],
+            (2 * half, 2 * half, half, half, 2 * half),
+            (0, 2, 4, 3, 1, 5, 6, 7),
+            ff_part,
             "feed_forward_products",
         )
-        mine, grad_normed_two = lax.optimization_barrier((blocks[6], grad_normed_two))
-        diag_low, diag_high, beside_low, beside_high, across_low, across_high = blocks[:6]
-        by_across = swap_across(diag_low)
-        by_beside = swap_beside(diag_high)
+        hidden = lax.optimization_barrier((hidden, mine))[0]
+        out_part = mm(hidden, w_down, ((1,), (1,))).astype(bf16)
+        out_part, grad_normed_two = lax.optimization_barrier((out_part, grad_normed_two))
+        from_across = swap_across(early_across)
+        from_beside = swap_beside(early_beside)
     else:
         grad_pair = jnp.concatenate([grad_gate, grad_up], axis=1)
         term_pair = mm(normed_all, grad_pair, ((0,), (0,))).astype(bf16)
@@ -983,6 +1117,7 @@
         pair_sum = lax.psum_scatter(term_pair, "seq", scatter_dimension=0, tiled=True)
         down_sum = lax.psum_scatter(term_down, "seq", scatter_dimension=0, tiled=True)
         mlp_sum = jnp.concatenate([pair_sum, down_sum], axis=1)
+        out_part = mm(hidden, w_down, ((1,), (1,))).astype(bf16)
     out_sum = lax.psum_scatter(out_part, "fsdp", scatter_dimension=0, tiled=True)
     block_output = (middle + out_sum.astype(f32)).astype(bf16)[None]
     grad_normed_two = grad_normed_two.astype(f32)
@@ -992,10 +1127,6 @@
     grad_middle = grad_out.astype(f32) + grad_mid_part
     grad_mix = grad_middle.astype(bf16)
     grad_mixed = mm(grad_mix, proj_out, ((1,), (0,)))
-    if custom:
-        beside_high, across_low, grad_mixed = lax.optimization_barrier((beside_high, across_low, grad_mixed))
-        from_beside_high = swap_beside(beside_high)
-        from_across_low = swap_across(across_low)
     carried_rows = jnp.broadcast_to(carried[None], (8, lru))
     grad_gelu_pre, rev_cum, rev_grad, pair_grad = call_heads(
         mixer_backward_scan,
@@ -1021,19 +1152,20 @@
         [tok_count + 8, tok_count + 16],
         "mixer_backward",
     )
-    if custom:
-        by_across, by_beside, own = lax.optimization_barrier((by_across, by_beside, own))
-        beside_low, across_high = add_low(beside_low, by_across), add_low(across_high, by_beside)
-        beside_low, across_high, own = lax.optimization_barrier((beside_low, across_high, own))
-        from_beside_low = swap_beside(beside_low)
-        from_across_high = swap_across(across_high)
-        mlp_parts = (mine, from_across_low, from_across_high, from_beside_low, from_beside_high)
     received = from_behind(head[8 - margin :], "seq", -1)
     grad_branch = jnp.concatenate(
         [own[: tok_count - margin], own[tok_count - margin :] + received], axis=0
     ).astype(bf16)
     grad_both = jnp.concatenate([grad_branch, grad_gelu_pre], axis=1)
     grad_normed = mm(grad_both, wide, ((1,), (1,)))
+    if custom:
+        from_across, from_beside, grad_normed = lax.optimization_barrier((from_across, from_beside, grad_normed))
+        beside_low = add_low(beside_low, from_across[:half])
+        across_high = add_low(across_high, from_beside[:half])
+        beside_low, across_high, grad_normed = lax.optimization_barrier((beside_low, across_high, grad_normed))
+        mlp_parts = (
+            mine, from_across[half:], swap_across(across_high), swap_beside(beside_low), from_beside[half:]
+        )
     first_pull = jax.vjp(norm_rows, tokens, gain_one)[1]
     grad_tok_part, grad_gain_one = first_pull(grad_normed)
     input_grad = (grad_middle + grad_tok_part).astype(bf16)[None]

time: 877 us -> 853 us (0.973)
  matrix products: 130 us -> 61.4 us
  Pallas kernels: 544 us -> 599 us
  waiting for transfers between devices: 60.3 us -> 14.4 us
  blocking collectives: 23.4 us -> 47.4 us
  local copies, waits for them, and re-layouts: 28.7 us -> 42.5 us
    dot_general x10 -> x5, matrix products: 130 us -> 61.4 us  [mm(): lax.dot_general(left, right, (dims, ((), ())), preferred_element_type=f32)]
    pallas_call x2 -> x3, Pallas kernels: 67.3 us -> 123 us  [the longest x2 70.5 us: products(): pl.pallas_call(functools.partial(products_kernel, sides, cuts, spots), gr...]
    ppermute x3 -> x2, waiting for transfers between devices: 45.6 us -> 2.41 us  [swap_across(): return lax.ppermute(shard, 'seq', [(i, i ^ 4) for i in range(8)])]
    all_gather x2, blocking collectives: 23.4 us -> 47.4 us  [prefix(): gathered = lax.all_gather(jnp.stack(part), axis)]
    unnamed x103 -> x105, local copies, waits for them, and re-layouts: 13 us -> 20.6 us
  transfers between devices with their start and end apart: 22 -> 17, of which waited for: 5 -> 5; matrix products, arithmetic and copies ran while one was open for 12% -> 13% of each run, Pallas kernels for 21% -> 43%
where the time goes in v8:
time: 853 us; the launch traced here: 844 us
  Pallas kernels  599 us (70%)
  matrix products  61.4 us (7%)
  blocking collectives  47.4 us (6%)
  other arithmetic  44.6 us (5%)
  local copies, waits for them, and re-layouts  42.5 us (5%)
  starting transfers between devices  19.7 us (2%)
  between operations  14.8 us (2%)
  waiting for transfers between devices  14.4 us (2%)
    pallas_call x1, Pallas kernels, gather(): pl.pallas_call(gather_kernel, in_specs=[anyspec] * 4, out_specs=[anyspec]...  183 us
    pallas_call x1, Pallas kernels, scatter(): pl.pallas_call(scatter_kernel, in_specs=[anyspec] * 3, out_specs=[anyspec...  178 us
    pallas_call x1, Pallas kernels, gather_rows(): pl.pallas_call(rows_kernel, in_specs=[anyspec] * 5, out_specs=[anyspec] *...  84.2 us
    pallas_call x2, Pallas kernels, products(): pl.pallas_call(functools.partial(products_kernel, sides, cuts, spots), gr...  70.5 us
    dot_general x5, matrix products, mm(): lax.dot_general(left, right, (dims, ((), ())), preferred_element_type=f32)  61.4 us
    pallas_call x1, Pallas kernels, feed_forward(): pl.pallas_call(feed_forward_kernel, grid=(2,), in_specs=[block, block, an...  52 us
    all_gather x2, blocking collectives, prefix(): gathered = lax.all_gather(jnp.stack(part), axis)  47.4 us
    pallas_call x3, Pallas kernels, call_heads(): pl.pallas_call(kernel, grid=(heads,), in_specs=in_specs, out_specs=out_sp...  31.3 us
  transfers between devices with their start and end apart: 17, of which 5 were waited for; matrix products, arithmetic and copies ran while one was open for 13% of the time, Pallas kernels for 43%

profile of v8, /device:TPU:0, one launch (start us, length us, event | category | flops | bytes accessed | tf_op | source)
XLA Modules:
  0.0 843.7 jit_solution(8857536096060577287)
XLA Ops:
  8.1 1.4 stack.57
  14.4 183.1 %gather_weights.1 = (bf16[2560,8320]{1,0:T(8,128)(2,1)}, bf16[320,5760]{1,0:T(8,128)(2,1)}) custom-call(bf16[80,8320]{1,0:T(8,128)(2,1)} %copy-done.33, bf16[80,7680]{1,0:T(8,128)(2,1)} %gate.1, bf16[80,7680]{1,0:T(8,128)(2,1)} %up.1, bf16[80,7680]{1,0:T(8,128)(2,1)} %down.1), custom_call_target="tpu_custom_call" | custom-call | tf_op jit(solution)/shard_map/gather_weights/pallas_call | solution.py:330
  197.6 5.4 collective-permute-start.1
  203.0 3.4 collective-permute-start.2
  206.4 2.3 slice.218
  209.9 2.2 slice_reduce_fusion
  212.4 14.9 %fusion.56 = (bf16[192,5120]{1,0:T(8,128)(2,1)S(1)}, f32[192,5120]{1,0:T(8,128)}) fusion(bf16[192,2560]{1,0:T(8,128)(2,1)S(1)} %fusion.23.refs_0_, bf16[2560,8320]{1,0:T(8,128)(2,1)} %get-tuple-element.66), kind=kOutput, calls=%fused_computation.149 | convolution fusion | flops 5034147840 | bytes 33095680 | tf_op jit(solution)/shard_map/dot_general | solution.py:50
  229.9 1.7 copy.76
  232.5 3.1 fusion.53
  239.3 7.2 mixer_forward.1
  247.3 11.1 %all-gather.2 = f32[8,2,2560]{2,1,0:T(2,128)S(1)} all-gather(f32[1,2,2560]{2,1,0:T(2,128)S(1)} %fusion.43), channel_id=2, replica_groups=mesh['seq'=8,'fsdp'=4] {'seq'}, dimensions={0}, use_global_device_ids=true | all-gather | bytes 184320 | tf_op jit(solution)/shard_map/all_gather | solution.py:29
  258.9 2.3 fusion.52
  261.3 10.6 %multiply_reduce_fusion = (f32[192]{0:T(256)S(1)}, f32[192,2560]{1,0:T(8,128)S(1)}) fusion(bf16[192,2560]{1,0:T(8,128)(2,1)} %get-tuple-element.226.refs_6_, bf16[2560,8320]{1,0:T(8,128)(2,1)} %get-tuple-element.66, bf16[1,192,2560]{2,1,0:T(8,128)(2,1)S(1)} %copy-done.21), kind=kOutput, calls=%fused_computation.59 | convolution fusion | flops 2518548224 | bytes 17040128 | tf_op jit(solution)/shard_map/dot_general | solution.py:50
  274.4 84.2 %gather_rows.1 = (bf16[768,2560]{1,0:T(8,128)(2,1)}, bf16[768,2560]{1,0:T(8,128)(2,1)}, bf16[768,2560]{1,0:T(8,128)(2,1)}, bf16[768,2560]{1,0:T(8,128)(2,1)}) custom-call(bf16[192,2560]{1,0:T(8,128)(2,1)} %multiply_convert_fusion.normed, bf16[192,2560]{1,0:T(8,128)(2,1)} %bitcast.14.grad0, bf16[192,2560]{1,0:T(8,128)(2,1)} %collective-permute-done.1.grad1, ...), custom_call_target="tpu_custom_call" | custom-call | tf_op jit(solution)/shard_map/gather_rows/pallas_call | solution.py:448
  358.7 52.0 %feed_forward.1 = (bf16[768,1920]{1,0:T(8,128)(2,1)}, bf16[768,1920]{1,0:T(8,128)(2,1)}, bf16[768,3840]{1,0:T(8,128)(2,1)}, bf16[768,3840]{1,0:T(8,128)(2,1)}, bf16[768,2560]{1,0:T(8,128)(2,1)}) custom-call(bf16[768,2560]{1,0:T(8,128)(2,1)} %get-tuple-element.71.normed.refs_0_, bf16[768,2560]{1,0:T(8,128)(2,1)} %get-tuple-element.72.grad_out.refs_2_, ...), custom_call_target="tpu_custom_call" | custom-call | tf_op jit(solution)/shard_map/feed_forward/pallas_call | solution.py:551
  411.4 45.9 %feed_forward_products.1 = (bf16[320,5760]{1,0:T(8,128)(2,1)}, bf16[320,5760]{1,0:T(8,128)(2,1)}, bf16[160,5760]{1,0:T(8,128)(2,1)}, bf16[160,5760]{1,0:T(8,128)(2,1)}, bf16[320,5760]{1,0:T(8,128)(2,1)}) custom-call(s32[5]{0:T(128)} %stack.64.place, bf16[768,2560]{1,0:T(8,128)(2,1)} %get-tuple-element.71.normed.refs_0_, ...), custom_call_target="tpu_custom_call" | custom-call | tf_op jit(solution)/shard_map/feed_forward_products/pallas_call | solution.py:660
  457.4 1.6 collective-permute-start.4
  459.0 13.6 %fusion.12 = bf16[768,2560]{1,0:T(8,128)(2,1)} fusion(bf16[768,1920]{1,0:T(8,128)(2,1)} %get-tuple-element.80.refs_6_, bf16[2560,5760]{1,0:T(8,128)(2,1)} %all-gather.6.cloned.1.call-done.weights), kind=kOutput, calls=%fused_computation.14 | convolution fusion | flops 7551713280 | bytes 16711680 | tf_op jit(solution)/shard_map/dot_general | solution.py:50
  472.6 8.3 reduce-scatter.3.cloned.1.call-done
  480.9 3.3 fusion.26
  485.5 2.9 fusion.51.refs_2_
  488.4 6.6 fusion.4.grad_mixed
  495.1 12.8 %mixer_backward_scan.1 = (bf16[192,2560]{1,0:T(8,128)(2,1)S(1)}, f32[192,2560]{1,0:T(8,128)S(1)}, f32[192,2560]{1,0:T(8,128)S(1)}, f32[8,2560]{1,0:T(8,128)S(1)}) custom-call(f32[192,2560]{1,0:T(8,128)S(1)} %fusion.4.grad_mixed, f32[192,2560]{1,0:T(8,128)S(1)} %copy-done.8, f32[192,2560]{1,0:T(8,128)S(1)} %copy-done.7, ...), custom_call_target="tpu_custom_call" | custom-call | tf_op jit(solution)/shard_map/mixer_backward_scan/pallas_call | solution.py:974
  508.0 36.3 %all-gather.3 = f32[8,2,2560]{2,1,0:T(2,128)S(1)} all-gather(f32[1,2,2560]{2,1,0:T(2,128)S(1)} %fusion.44), channel_id=3, replica_groups=mesh['seq'=8,'fsdp'=4] {'seq'}, dimensions={0}, use_global_device_ids=true | all-gather | bytes 184320 | tf_op jit(solution)/shard_map/all_gather | solution.py:29
  544.8 11.2 %mixer_backward.1 = (f32[192,2560]{1,0:T(8,128)S(1)}, f32[8,2560]{1,0:T(8,128)S(1)}, bf16[2560,256]{1,0:T(8,128)(2,1)S(1)}, bf16[2560,256]{1,0:T(8,128)(2,1)S(1)}, f32[8,2560]{1,0:T(8,128)S(1)}) custom-call(f32[192,2560]{1,0:T(8,128)S(1)} %get-tuple-element.88.rev_cum, f32[192,2560]{1,0:T(8,128)S(1)} %get-tuple-element.89.rev_grad, ...), custom_call_target="tpu_custom_call" | custom-call | tf_op jit(solution)/shard_map/mixer_backward/pallas_call | solution.py:974
  558.4 1.4 collective-permute-start.6
  559.8 1.6 slice.416
  562.5 1.5 pad_maximum_fusion.refs_4_
  564.1 15.6 %fusion = f32[192,2560]{1,0:T(8,128)} fusion(bf16[192,5120]{1,0:T(8,128)(2,1)} %pad_maximum_fusion.refs_4_, bf16[2560,8320]{1,0:T(8,128)(2,1)} %get-tuple-element.66), kind=kOutput, calls=%fused_computation | convolution fusion | flops 5033164800 | bytes 30146560 | tf_op jit(solution)/shard_map/dot_general | solution.py:50
  579.6 6.0 add_convert_fusion
  587.3 1.7 copy-done.24
  589.1 2.6 collective-permute-start.11
  592.8 1.5 collective-permute-start.12
  595.3 2.2 collective-permute-done.7.refs_1_
  598.7 2.9 slice.272
  601.6 2.0 slice.273
  604.8 1.8 fusion.18
  606.8 1.4 pad_maximum_fusion.1.rest
  608.2 24.6 %mixer_products.1 = bf16[1280,7680]{1,0:T(8,128)(2,1)} custom-call(s32[5]{0:T(128)} %stack.64.place, bf16[192,2560]{1,0:T(8,128)(2,1)} %copy-done.30, bf16[192,2560]{1,0:T(8,128)(2,1)} %copy-done.35, bf16[192,2560]{1,0:T(8,128)(2,1)} %fusion.51.refs_2_, bf16[192,2560]{1,0:T(8,128)(2,1)} %collective-permute-done.8.refs_3_, ...), custom_call_target="tpu_custom_call" | custom-call | tf_op jit(solution)/shard_map/mixer_products/pallas_call | solution.py:660
  632.8 2.4 collective-permute-done.12
  636.5 2.4 convert_add_fusion.2
  638.9 1.9 convert_add_fusion.1
  640.8 4.5 fusion.10.mlp
  645.3 177.8 %scatter_gradients.1 = (bf16[80,8320]{1,0:T(8,128)(2,1)S(1)}, bf16[3,80,7680]{2,1,0:T(8,128)(2,1)}) custom-call(bf16[4,320,7680]{2,1,0:T(8,128)(2,1)} %bitcast.72, bf16[4,320,640]{2,1,0:T(8,128)(2,1)} %pad_maximum_fusion.1.rest, bf16[320,5760]{1,0:T(8,128)(2,1)} %fusion.10.mlp), custom_call_target="tpu_custom_call" | custom-call | tf_op jit(solution)/shard_map/scatter_gradients/pallas_call | solution.py:863
  825.5 1.5 fusion.54
  827.0 1.4 copy-done.32
  828.4 3.4 bitcast_convert_fusion
  831.9 5.1 fusion.42
  (176 shorter events, 33.7 us)
Async XLA Ops:
  7.2 6.1 copy-start.38
  7.2 351.5 %all-gather.6.cloned.1.call-start = ((), (), s32[]{:S(2)}) async-start(), calls=%async_computation.2 | async-start | bytes 33177600 | tf_op jit(solution)/shard_map/all_gather | solution.py:1031
  197.5 283.4 %reduce-scatter.3.cloned.1.call-start = ((), (), s32[]{:S(2)}) async-start(), calls=%async_computation.3 | async-start | bytes 4915200 | tf_op jit(solution)/shard_map/reduce_scatter | solution.py:1097
  197.6 76.8 %collective-permute-start.1 = (bf16[192,2560]{1,0:T(8,128)(2,1)}, bf16[192,2560]{1,0:T(8,128)(2,1)}, u32[]{:S(2)}, u32[]{:S(2)}) collective-permute-start(bf16[192,2560]{1,0:T(8,128)(2,1)} %bitcast.14.grad0), channel_id=1, source_target_pairs={{0,1},{1,2},{2,3},{3,0},{4,5},{5,6},{6,7},{7,4},{8,9},{9,10},{10,1... | collective-permute-start | bytes 2949128 | tf_op jit(solution)/shard_map/ppermute | solution.py:896
  203.0 71.4 %collective-permute-start.2 = (bf16[192,2560]{1,0:T(8,128)(2,1)}, bf16[192,2560]{1,0:T(8,128)(2,1)}, u32[]{:S(2)}, u32[]{:S(2)}) collective-permute-start(bf16[192,2560]{1,0:T(8,128)(2,1)} %bitcast.14.grad0), channel_id=1, source_target_pairs={{0,2},{1,3},{2,0},{3,1},{4,6},{5,7},{6,4},{7,5},{8,10},{9,11},{10,... | collective-permute-start | bytes 2949128 | tf_op jit(solution)/shard_map/ppermute | solution.py:896
  206.4 68.0 %collective-permute-start.3 = (bf16[192,2560]{1,0:T(8,128)(2,1)}, bf16[192,2560]{1,0:T(8,128)(2,1)}, u32[]{:S(2)}, u32[]{:S(2)}) collective-permute-start(bf16[192,2560]{1,0:T(8,128)(2,1)} %bitcast.14.grad0), channel_id=1, source_target_pairs={{0,3},{1,0},{2,1},{3,2},{4,7},{5,4},{6,5},{7,6},{8,11},{9,8},{10,9... | collective-permute-start | bytes 2949128 | tf_op jit(solution)/shard_map/ppermute | solution.py:896
  208.7 3.4 copy-start.26
  212.4 14.9 %copy-start.30 = (bf16[192,2560]{1,0:T(8,128)(2,1)}, bf16[192,2560]{1,0:T(8,128)(2,1)S(1)}, u32[]{:S(2)}) copy-start(bf16[192,2560]{1,0:T(8,128)(2,1)S(1)} %fusion.23.refs_0_) | copy-start | bytes 2949124
  228.6 8.1 collective-permute-start
  232.5 3.2 copy-start.37
  239.3 19.6 %copy-start.34 = (f32[192,5120]{1,0:T(8,128)S(1)}, f32[192,5120]{1,0:T(8,128)}, u32[]{:S(2)}) copy-start(f32[192,5120]{1,0:T(8,128)} %get-tuple-element.250) | copy-start | bytes 11796484
  246.5 14.7 %copy-start.1 = (f32[192,2560]{1,0:T(8,128)}, f32[192,2560]{1,0:T(8,128)S(1)}, u32[]{:S(2)}) copy-start(f32[192,2560]{1,0:T(8,128)S(1)} %get-tuple-element.67.local) | copy-start | bytes 5898244
  246.5 14.7 %copy-start.6 = (f32[192,2560]{1,0:T(8,128)}, f32[192,2560]{1,0:T(8,128)S(1)}, u32[]{:S(2)}) copy-start(f32[192,2560]{1,0:T(8,128)S(1)} %get-tuple-element.87.rate_pre) | copy-start | bytes 5898244
  246.6 14.7 %copy-start.9 = (f32[192,2560]{1,0:T(8,128)}, f32[192,2560]{1,0:T(8,128)S(1)}, u32[]{:S(2)}) copy-start(f32[192,2560]{1,0:T(8,128)S(1)} %get-tuple-element.91.input_pre) | copy-start | bytes 5898244
  246.6 14.7 %copy-start.12 = (bf16[192,2560]{1,0:T(8,128)(2,1)}, bf16[192,2560]{1,0:T(8,128)(2,1)S(1)}, u32[]{:S(2)}) copy-start(bf16[192,2560]{1,0:T(8,128)(2,1)S(1)} %get-tuple-element.92.conv) | copy-start | bytes 2949124
  246.6 248.5 %copy-start = (f32[192,2560]{1,0:T(8,128)}, f32[192,2560]{1,0:T(8,128)S(1)}, u32[]{:S(2)}) copy-start(f32[192,2560]{1,0:T(8,128)S(1)} %get-tuple-element.68.cum) | copy-start | bytes 5898244
  410.7 421.1 %reduce-scatter.5.cloned.1.call-start = ((), (), s32[]{:S(2)}) async-start(), calls=%async_computation.4 | async-start | bytes 4915200 | tf_op jit(solution)/shard_map/reduce_scatter | solution.py:1121
  457.4 122.2 %collective-permute-start.4 = (bf16[320,5760]{1,0:T(8,128)(2,1)}, bf16[320,5760]{1,0:T(8,128)(2,1)}, u32[]{:S(2)}, u32[]{:S(2)}) collective-permute-start(bf16[320,5760]{1,0:T(8,128)(2,1)} %get-tuple-element.85), channel_id=1, source_target_pairs={{0,16},{4,20},{8,24},{12,28},{16,0},{20,4},{24,8},{28,12},{1,17},{... | collective-permute-start | bytes 11059208 | tf_op jit(solution)/shard_map/ppermute | solution.py:910
  459.0 120.6 %collective-permute-start.5 = (bf16[320,5760]{1,0:T(8,128)(2,1)}, bf16[320,5760]{1,0:T(8,128)(2,1)}, u32[]{:S(2)}, u32[]{:S(2)}) collective-permute-start(bf16[320,5760]{1,0:T(8,128)(2,1)} %get-tuple-element.86), channel_id=1, source_target_pairs={{0,8},{4,12},{8,0},{12,4},{16,24},{20,28},{24,16},{28,20},{1,9},{5... | collective-permute-start | bytes 11059208 | tf_op jit(solution)/shard_map/ppermute | solution.py:906
  480.9 4.6 copy-start.18
  480.9 4.6 copy-start.27
  488.4 6.7 copy-start.40
  488.4 6.7 copy-start.7
  488.4 6.7 copy-start.8
  495.1 12.9 %copy-start.42 = (f32[1,2560]{1,0:T(1,128)S(1)}, f32[1,2560]{1,0:T(1,128)}, u32[]{:S(2)}) copy-start(f32[1,2560]{1,0:T(1,128)} %copy-done.41) | copy-start | bytes 30724
  495.1 49.7 %copy-start.3 = (bf16[2560,256]{1,0:T(8,128)(2,1)S(1)}, bf16[2560,256]{1,0:T(8,128)(2,1)}, u32[]{:S(2)}) copy-start(bf16[2560,256]{1,0:T(8,128)(2,1)} %get-tuple-element.231.rate_w) | copy-start | bytes 3932164
  495.1 49.7 %copy-start.5 = (bf16[192,2560]{1,0:T(8,128)(2,1)S(1)}, bf16[192,2560]{1,0:T(8,128)(2,1)}, u32[]{:S(2)}) copy-start(bf16[192,2560]{1,0:T(8,128)(2,1)} %slice.286.branch) | copy-start | bytes 2949124
  495.1 49.7 %copy-start.13 = (bf16[192,2560]{1,0:T(8,128)(2,1)S(1)}, bf16[192,2560]{1,0:T(8,128)(2,1)}, u32[]{:S(2)}) copy-start(bf16[192,2560]{1,0:T(8,128)(2,1)} %copy-done.12) | copy-start | bytes 2949124
  508.0 48.1 %copy-start.14 = (bf16[192,2560]{1,0:T(8,128)(2,1)}, bf16[192,2560]{1,0:T(8,128)(2,1)S(1)}, u32[]{:S(2)}) copy-start(bf16[192,2560]{1,0:T(8,128)(2,1)S(1)} %get-tuple-element.95) | copy-start | bytes 2949124
  558.4 3.1 copy-start.43
  558.4 4.2 copy-start.15
  558.4 3.2 collective-permute-start.6
  579.6 6.0 copy-start.22
  579.6 6.0 copy-start.29
  587.3 4.5 copy-start.31
  587.3 4.6 copy-start.28
  589.1 8.6 %collective-permute-start.11 = (bf16[4,320,640]{2,1,0:T(8,128)(2,1)S(1)}, bf16[4,320,640]{2,1,0:T(8,128)(2,1)}, u32[]{:S(2)}, u32[]{:S(2)}) collective-permute-start(bf16[4,320,640]{2,1,0:T(8,128)(2,1)S(1)} %dynamic-slice_bitcast_fusion), channel_id=1, source_target_pairs={{0,4},{4,0},{8,12},{12,8},{16,20},{20,16},{24,28},{28,24},{1,5},{5... | collective-permute-start | bytes 4915208 | tf_op jit(solution)/shard_map/ppermute | solution.py:902
  591.8 5.8 collective-permute-start.7
  591.8 16.4 %collective-permute-start.9 = (bf16[192,5120]{1,0:T(8,128)(2,1)S(1)}, bf16[192,5120]{1,0:T(8,128)(2,1)}, u32[]{:S(2)}, u32[]{:S(2)}) collective-permute-start(bf16[192,5120]{1,0:T(8,128)(2,1)S(1)} %copy-done.28), channel_id=1, source_target_pairs={{0,4},{4,0},{8,12},{12,8},{16,20},{20,16},{24,28},{28,24},{1,5},{5... | collective-permute-start | bytes 5898248 | tf_op jit(solution)/shard_map/ppermute | solution.py:902
  592.8 42.4 %collective-permute-start.12 = (bf16[160,5760]{1,0:T(8,128)(2,1)}, bf16[160,5760]{1,0:T(8,128)(2,1)}, u32[]{:S(2)}, u32[]{:S(2)}) collective-permute-start(bf16[160,5760]{1,0:T(8,128)(2,1)} %get-tuple-element.104), channel_id=1, source_target_pairs={{0,16},{4,20},{8,24},{12,28},{16,0},{20,4},{24,8},{28,12},{1,17},{... | collective-permute-start | bytes 5529608 | tf_op jit(solution)/shard_map/ppermute | solution.py:910
  594.4 42.1 %collective-permute-start.13 = (bf16[160,5760]{1,0:T(8,128)(2,1)}, bf16[160,5760]{1,0:T(8,128)(2,1)}, u32[]{:S(2)}, u32[]{:S(2)}) collective-permute-start(bf16[160,5760]{1,0:T(8,128)(2,1)} %get-tuple-element.105), channel_id=1, source_target_pairs={{0,8},{4,12},{8,0},{12,4},{16,24},{20,28},{24,16},{28,20},{1,9},{5... | collective-permute-start | bytes 5529608 | tf_op jit(solution)/shard_map/ppermute | solution.py:906
  597.6 10.7 %collective-permute-start.10 = (bf16[192,2560]{1,0:T(8,128)(2,1)}, bf16[192,2560]{1,0:T(8,128)(2,1)}, u32[]{:S(2)}, u32[]{:S(2)}) collective-permute-start(bf16[192,2560]{1,0:T(8,128)(2,1)} %get-tuple-element.226.refs_6_), channel_id=1, source_target_pairs={{0,4},{4,0},{8,12},{12,8},{16,20},{20,16},{24,28},{28,24},{1,5},{5... | collective-permute-start | bytes 2949128 | tf_op jit(solution)/shard_map/ppermute | solution.py:902
  598.5 9.7 %collective-permute-start.8 = (bf16[192,2560]{1,0:T(8,128)(2,1)}, bf16[192,2560]{1,0:T(8,128)(2,1)}, u32[]{:S(2)}, u32[]{:S(2)}) collective-permute-start(bf16[192,2560]{1,0:T(8,128)(2,1)} %fusion.51.refs_2_), channel_id=1, source_target_pairs={{0,4},{4,0},{8,12},{12,8},{16,20},{20,16},{24,28},{28,24},{1,5},{5... | collective-permute-start | bytes 2949128 | tf_op jit(solution)/shard_map/ppermute | solution.py:902
  601.6 3.2 copy-start.25
  825.5 2.9 copy-start.32
  828.4 3.4 copy-start.19
  828.4 3.5 copy-start.23
  828.4 3.5 copy-start.47
  (18 other events, 26.0 us)
Sparse Core Ops, SparseCore 0:
  197.6 150.0 all-gather.5
  410.8 70.0 reduce-scatter.2
  598.8 100.5 reduce-scatter.4

commit v9 on v8

--- a/solution.py
+++ b/solution.py
@@ -37,6 +37,18 @@
 
 def norm_rows(values, scales):
     return values * lax.rsqrt(jnp.mean(values * values, axis=-1, keepdims=True) + epsilon) * scales
+
+
+def norm_back(values, scales, grads):
+    inverse = lax.rsqrt(jnp.mean(values * values, axis=-1, keepdims=True) + epsilon)
+    scaled = grads * scales
+    shared = jnp.mean(values * scaled, axis=-1, keepdims=True)
+    return inverse * scaled - values * (inverse * inverse * inverse * shared)
+
+
+def gain_back(gain, *pairs):
+    total = sum(jnp.sum(weight.astype(f32) * grad, axis=1) for weight, grad in pairs)
+    return total / gain.astype(f32)
 
 
 def gelu_parts(x):
@@ -176,14 +188,20 @@
 
 
 def gather_kernel(
-    mixer, gate, up, down, mixer_all, mlp_mine,
-    flow_send, flow_recv, line_send, line_recv, swap_send, swap_recv, own_sem,
+    first, branch, gelu, outer, gate, up, down, mixer_all, mlp_mine,
+    mixer, load_sem, flow_send, flow_recv, line_send, line_recv, swap_send, swap_recv, own_sem,
 ):
     s, z, core, beside, across = places()
     rows, cols = mixer.shape
     ff_part = mlp_mine.shape[1] // 3
     cut = cols // 256 * 128
     diag = beside + across - s
+    loads, start = [], 0
+    for n, part in enumerate((first, branch, gelu, outer)):
+        size = part.shape[1]
+        loads.append(pltpu.make_async_copy(part, mixer.at[:, pl.ds(start, size)], load_sem.at[n]))
+        loads[-1].start()
+        start += size
     greet([(core, z), (beside, z), (across, z)] + [(s, (z + k) % 4) for k in range(1, 4)])
 
     def remote(src, dst, send, recv, target):
@@ -283,6 +301,8 @@
 
     local = [pltpu.make_async_copy(columns(m, z), landing(m, z), own_sem.at[m]) for m in range(3)]
     local.append(pltpu.make_async_copy(mixer, piece(s, z), own_sem.at[3]))
+    for copy in loads:
+        copy.wait()
 
     pl.when(z < 3)(lambda: line(z, True, 0, mixer).start())
     pl.when(z > 0)(lambda: line(z, False, 0, mixer).start())
@@ -322,25 +342,27 @@
         pl.when((z + hop <= 3) & (z > 0))(lambda: line(z + hop, False, hop).wait_send())
 
 
-def gather(mixer, gate, up, down):
-    rows, cols = mixer.shape
+def gather(first, branch, gelu, outer, gate, up, down):
+    rows = first.shape[0]
+    cols = first.shape[1] + branch.shape[1] + gelu.shape[1] + outer.shape[1]
     ff_part = gate.shape[1] // 4
     anyspec = pl.BlockSpec(memory_space=pl.ANY)
     dma = pltpu.SemaphoreType.DMA
     return pl.pallas_call(
         gather_kernel,
-        in_specs=[anyspec] * 4,
+        in_specs=[anyspec] * 7,
         out_specs=[anyspec] * 2,
         out_shape=[
             jax.ShapeDtypeStruct((32 * rows, cols), bf16),
             jax.ShapeDtypeStruct((4 * rows, 3 * ff_part), bf16),
         ],
         scratch_shapes=[
+            pltpu.VMEM((rows, cols), bf16), dma((4,)),
             dma((4, 9)), dma((4, 9)), dma((2, 3)), dma((2, 3)), dma((3, 3)), dma((3, 3)), dma((4,)),
         ],
         compiler_params=pltpu.CompilerParams(collective_id=1, has_side_effects=True),
         name="gather_weights",
-    )(mixer, gate, up, down)
+    )(first, branch, gelu, outer, gate, up, down)
 
 
 def rows_kernel(
@@ -570,7 +592,7 @@
     )(normed, grad_out, weights)
 
 
-def products_kernel(sides, cuts, spots, place, *refs):
+def products_kernel(sides, cuts, chips, spots, place, *refs):
     lefts = 1 + max(side for side, _ in sides)
     left_refs = refs[: 2 * lefts]
     right_refs = refs[2 * lefts : 2 * lefts + 2 * len(sides)]
@@ -582,19 +604,19 @@
     step = pl.program_id(0)
 
     def load(side, q, who):
-        cols = pl.ds(pl.multiple_of(place[q] * chip_cols, 128), chip_cols)
+        cols = pl.ds(pl.multiple_of(place[chips[q]] * chip_cols, 128), chip_cols)
         return pltpu.make_async_copy(
             left_refs[2 * side + who].at[:, cols], slots.at[q % 2, who], sems.at[q % 2, who]
         )
 
     def fetch(side):
-        for q in range(2):
+        for q in range(min(2, len(chips))):
             for who in range(2):
                 load(side, q, who).start()
 
     def turn(side):
         piece = half // 2
-        for q in range(4):
+        for q in range(len(chips)):
             for who in range(2):
                 load(side, q, who).wait()
                 stage[...] = slots[q % 2, who].T
@@ -603,7 +625,7 @@
                     turned[who, spot : spot + piece, :] = stage[
                         pl.ds(pl.multiple_of(place[4] * half + part * piece, 16), piece), :
                     ]
-                if q < 2:
+                if q + 2 < len(chips):
                     load(side, q + 2, who).start()
 
     def multiply(own, other):
@@ -640,7 +662,7 @@
             pl.when(step == first - 1)(functools.partial(fetch, sides[n + 1][0]))
 
 
-def products(lefts, rights, cuts, spots, width, name):
+def products(lefts, rights, cuts, chips, spots, width, name):
     seq = lax.axis_index("seq")
     core, x, y = seq % 2, (seq // 2) % 2, seq // 4
     place = jnp.stack([(1 - y) * 2 + 1 - x, y * 2 + 1 - x, (1 - y) * 2 + x, y * 2 + x, core]).astype(jnp.int32)
@@ -658,14 +680,14 @@
         first += blocks
     half = model // 8
     return pl.pallas_call(
-        functools.partial(products_kernel, sides, cuts, spots),
+        functools.partial(products_kernel, sides, cuts, chips, spots),
         grid_spec=pltpu.PrefetchScalarGridSpec(
             num_scalar_prefetch=1,
             grid=(total,),
             in_specs=in_specs,
             out_specs=[pl.BlockSpec((rows, width), lambda j, place: (0, j)) for rows in cuts],
             scratch_shapes=[
-                pltpu.VMEM((2, 4 * half, tok), bf16),
+                pltpu.VMEM((2, len(chips) * half, tok), bf16),
                 pltpu.VMEM((2, 2, tok, 2 * half), bf16),
                 pltpu.VMEM((2 * half, tok), bf16),
                 pltpu.SemaphoreType.DMA((2, 2)),
@@ -690,8 +712,8 @@
 
 
 def scatter_kernel(
-    main, rest, mlp, mixer_sum, mlp_back,
-    held, cross, near, lined,
+    main, rest, mlp_low, mlp_high, grad_both, mixer_w, tokens, grad_middle, gain, mixer_sum, mlp_back, input_grad,
+    held, cross, near, lined, both_now, wide_now, back_now, tokens_now, middle_now, gain_now, wide_sem,
     load_sem, flow_send, flow_recv, line_send, line_recv, swap_send, swap_recv, own_sem,
 ):
     s, z, _, beside, across = places()
@@ -699,7 +721,7 @@
     rows = held.shape[1] // 4
     cols = held.shape[2]
     cut = cols // 256 * 128
-    ff_part = mlp.shape[1] // 3
+    ff_part = mlp_low.shape[1] // 3
     parts = (main, rest)
     order = (3 * (1 - z // 2), (2 + 3 * z) % 5, 1 + z % 2, z)
 
@@ -788,35 +810,86 @@
             k = order[i]
             line(k, k, (z + 1) % 4).wait_send()
 
-    def pieces():
-        for m in range(3):
-            yield m, mlp, pl.ds(m * ff_part, ff_part)
-
-    def swap(k):
+    def swap(k, high=False):
         to = (z + k) % 4
         here = pl.ds(pl.multiple_of(z * ff_part, 128), ff_part)
+        source = (mlp_high if high else mlp_low).at[span(to % 2), :]
         return [
             remote(
-                source.at[span(to), at], mlp_back.at[m, :, here], swap_send.at[k - 1, m], swap_recv.at[k - 1, m], (s, to)
+                source.at[:, pl.ds(m * ff_part, ff_part)],
+                mlp_back.at[m, :, here],
+                swap_send.at[k - 1, m],
+                swap_recv.at[k - 1, m],
+                (s, to),
             )
-            for m, source, at in pieces()
+            for m in range(3)
         ]
 
-    own = [
-        pltpu.make_async_copy(
-            source.at[span(z), at], mlp_back.at[m, :, pl.ds(pl.multiple_of(z * ff_part, 128), ff_part)], own_sem.at[m]
-        )
-        for m, source, at in pieces()
+    def swap_start(k):
+        to = (z + k) % 4
+
+        @pl.when(to < 2)
+        def _():
+            for copy in swap(k):
+                copy.start()
+
+        @pl.when(to >= 2)
+        def _():
+            for copy in swap(k, True):
+                copy.start()
+
+    def own(high=False):
+        here = pl.ds(pl.multiple_of(z * ff_part, 128), ff_part)
+        source = (mlp_high if high else mlp_low).at[span(z % 2), :]
+        return [
+            pltpu.make_async_copy(source.at[:, pl.ds(m * ff_part, ff_part)], mlp_back.at[m, :, here], own_sem.at[m])
+            for m in range(3)
+        ]
+
+    wide_rows = wide_now.shape[1]
+    wide_start = mixer_w.shape[1] - wide_now.shape[2] - tokens.shape[1]
+
+    def wide(j):
+        source = mixer_w.at[pl.ds(j * wide_rows, wide_rows), pl.ds(wide_start, wide_now.shape[2])]
+        return pltpu.make_async_copy(source, wide_now.at[j % 2], wide_sem.at[j % 2])
+
+    plain_loads = [
+        pltpu.make_async_copy(source, target, wide_sem.at[2 + n])
+        for n, (source, target) in enumerate(
+            ((grad_both, both_now), (tokens, tokens_now), (grad_middle, middle_now), (gain, gain_now))
+        )
     ]
+
+    def back(first, last):
+        for j in range(first, last):
+            wide(j).wait()
+            back_now[:, pl.ds(j * wide_rows, wide_rows)] = mm(both_now[...], wide_now[j % 2], ((1,), (1,)))
+            if (j + 2) * wide_rows < mixer_w.shape[0]:
+                wide(j + 2).start()
+
+    def finish_rows(turn, carry):
+        rows = pl.ds(pl.multiple_of(turn * 16, 16), 16)
+        result = middle_now[rows, :] + norm_back(tokens_now[rows, :].astype(f32), gain_now[0:1, :], back_now[rows, :])
+        tokens_now[rows, :] = result.astype(bf16)
+        return carry
+
     for i in range(4):
         for copy in loads(i):
             copy.start()
     greet([(beside, z), (across, z)] + [(s, (z + k) % 4) for k in range(1, 4)])
     for k in (1, 3, 2):
-        for copy in swap(k):
+        swap_start(k)
+
+    @pl.when(z < 2)
+    def _():
+        for copy in own():
             copy.start()
-    for copy in own:
-        copy.start()
+
+    @pl.when(z >= 2)
+    def _():
+        for copy in own(True):
+            copy.start()
+
     for i in range(2):
         for copy in loads(i):
             copy.wait()
@@ -835,9 +908,23 @@
                 copy.wait()
             flow(i + 2, 0).start()
             flow(i + 2, 1).start()
+        if i == 0:
+            for copy in plain_loads:
+                copy.start()
+            wide(0).start()
+            wide(1).start()
         if i > 0:
             near_step(i - 1)
             chain(i - 1)
+        if i == 1:
+            for copy in plain_loads:
+                copy.wait()
+        if i > 0:
+            back(3 * i - 3, 3 * i)
+    back(9, mixer_w.shape[0] // wide_rows)
+    lax.fori_loop(0, tokens.shape[0] // 16, finish_rows, 0)
+    finished = pltpu.make_async_copy(tokens_now, input_grad, wide_sem.at[2])
+    finished.start()
     near_step(3)
     chain(3)
     done = pltpu.make_async_copy(held.at[chip, span(z), :], mixer_sum, own_sem.at[3])
@@ -849,37 +936,47 @@
     for k in range(1, 4):
         for copy in swap(k):
             copy.wait()
-    for copy in own:
+    for copy in own():
         copy.wait()
+    finished.wait()
     done.wait()
 
 
-def scatter(main, rest, mlp):
+def scatter(main, rest, mlp_low, mlp_high, grad_both, mixer_w, tokens, grad_middle, gain):
     rows = main.shape[1] // 4
     cols = main.shape[2] + rest.shape[2]
-    ff_part = mlp.shape[1] // 3
+    ff_part = mlp_low.shape[1] // 3
+    tok, model = tokens.shape
     anyspec = pl.BlockSpec(memory_space=pl.ANY)
     dma = pltpu.SemaphoreType.DMA
     return pl.pallas_call(
         scatter_kernel,
-        in_specs=[anyspec] * 3,
-        out_specs=[anyspec] * 2,
+        in_specs=[anyspec] * 9,
+        out_specs=[anyspec] * 3,
         out_shape=[
             jax.ShapeDtypeStruct((rows, cols), bf16),
             jax.ShapeDtypeStruct((3, rows, 4 * ff_part), bf16),
+            jax.ShapeDtypeStruct((tok, model), bf16),
         ],
         scratch_shapes=[
             pltpu.VMEM((4, 4 * rows, cols), bf16),
             pltpu.VMEM((4, rows, cols), bf16),
             pltpu.VMEM((2, 4, rows, cols), bf16),
             pltpu.VMEM((5, rows, cols), bf16),
+            pltpu.VMEM(grad_both.shape, bf16),
+            pltpu.VMEM((2, 256, grad_both.shape[1]), bf16),
+            pltpu.VMEM((tok, model), f32),
+            pltpu.VMEM((tok, model), bf16),
+            pltpu.VMEM((tok, model), f32),
+            pltpu.VMEM((8, model), f32),
+            dma((6,)),
             dma((4, 2)), dma((4, 6)), dma((4, 6)), dma((4,)), dma((5,)), dma((3, 3)), dma((3, 3)), dma((4,)),
         ],
         compiler_params=pltpu.CompilerParams(
-            collective_id=2, has_side_effects=True, vmem_limit_bytes=52 * 1024 * 1024
+            collective_id=2, has_side_effects=True, vmem_limit_bytes=62 * 1024 * 1024
         ),
         name="scatter_gradients",
-    )(main, rest, mlp)
+    )(main, rest, mlp_low, mlp_high, grad_both, mixer_w, tokens, grad_middle, gain)
 
 
 def gather_plain(mixer, gate, up, down):
@@ -914,15 +1011,18 @@
     return (left.astype(f32) + right.astype(f32)).astype(bf16)
 
 
-def scatter_paired(normed, grad_both, grad_mix, mixed, rest, mlp_parts):
+def scatter_paired(
+    normed, grad_both, grad_mix, mixed, rest, mlp_parts, mixer_w, tokens, grad_middle, gain
+):
     seq = lax.axis_index("seq")
     core, x, y = seq % 2, (seq // 2) % 2, seq // 4
     main = products(
         [(normed, swap_cores(normed)), (grad_mix, swap_cores(grad_mix))],
         [(0, grad_both, swap_cores(grad_both)), (1, mixed, swap_cores(mixed))],
         (normed.shape[1] // 2,),
+        (0, 1, 2, 3),
         tuple(range(8)),
-        normed.shape[1],
+        normed.shape[1] // 2,
         "mixer_products",
     )[0]
     grouped = rest.reshape(4, 2, -1, rest.shape[1])
@@ -937,9 +1037,11 @@
         axis=0,
     )
     main, rest, mlp_parts = lax.optimization_barrier((main, rest, mlp_parts))
-    mine, *sent = [part.astype(f32) for part in mlp_parts]
-    mlp_sum = mine + jnp.concatenate([sent[0] + sent[2], sent[1] + sent[3]], axis=0)
-    return scatter(main.reshape(4, -1, main.shape[1]), rest, mlp_sum.astype(bf16))
+    low, high = [sum(part.astype(f32) for part in parts).astype(bf16) for parts in mlp_parts]
+    gain = jnp.broadcast_to(gain[None], (8, gain.shape[0]))
+    return scatter(
+        main.reshape(4, -1, main.shape[1]), rest, low, high, grad_both, mixer_w, tokens, grad_middle, gain
+    )
 
 
 def scatter_plain(normed, grad_both, grad_mix, mixed, rest, mlp_sum):
@@ -1020,14 +1122,13 @@
     )
     small_count = smalls.shape[1]
     smalls = jnp.pad(smalls, ((0, 0), (0, 128 - small_count)))
-    mixer_own = jnp.concatenate(
-        [smalls, rate_blocks, input_blocks, branch_proj, gelu_proj, out_proj], axis=1
-    )
+    first_own = jnp.concatenate([smalls, rate_blocks, input_blocks], axis=1)
+    mixer_own = (first_own, branch_proj, gelu_proj, out_proj)
     custom = lax.axis_size("seq") == 8 and groups == 4
     if custom:
-        mixer_w, mlp_mine = gather(mixer_own, gate_proj, up_proj, down_proj)
+        mixer_w, mlp_mine = gather(*mixer_own, gate_proj, up_proj, down_proj)
     else:
-        mixer_w, mlp_mine = gather_plain(mixer_own, gate_proj, up_proj, down_proj)
+        mixer_w, mlp_mine = gather_plain(jnp.concatenate(mixer_own, axis=1), gate_proj, up_proj, down_proj)
     mlp_w = lax.all_gather(mlp_mine, "seq", axis=0, tiled=True)
     grad_out_late = lax.optimization_barrier((grad_out, mlp_mine))[0]
     if custom:
@@ -1097,19 +1198,19 @@
     grad_normed_two = lax.psum_scatter(grad_normed_part, "fsdp", scatter_dimension=0, tiled=True)
     if custom:
         half = model // 16
-        early_across, early_beside, beside_low, across_high, mine = products(
-            [(normed_all, normed_other), (grad_out_all, grad_out_other)],
-            [(0, grad_pair, pair_other), (1, hidden, hidden_other)],
-            (2 * half, 2 * half, half, half, 2 * half),
-            (0, 2, 4, 3, 1, 5, 6, 7),
-            ff_part,
-            "feed_forward_products",
-        )
+        lefts = [(normed_all, normed_other), (grad_out_all, grad_out_other)]
+        rights = [(0, grad_pair, pair_other), (1, hidden, hidden_other)]
+        diag_low, diag_high = products(lefts, rights, (half, half), (0,), (0, 1), ff_part, "diagonal_products")
+        from_across, from_beside = swap_across(diag_low), swap_beside(diag_high)
+        late = lax.optimization_barrier((grad_pair, diag_low))[0]
+        rights = [(0, late, pair_other), (1, hidden, hidden_other)]
+        beside_low, beside_high, across_low, across_high, mine = products(
+            lefts, rights, (half,) * 4 + (2 * half,), (1, 2, 3), tuple(range(6)), ff_part, "feed_forward_products"
+        )
+        from_beside_high, from_across_low = swap_beside(beside_high), swap_across(across_low)
         hidden = lax.optimization_barrier((hidden, mine))[0]
         out_part = mm(hidden, w_down, ((1,), (1,))).astype(bf16)
         out_part, grad_normed_two = lax.optimization_barrier((out_part, grad_normed_two))
-        from_across = swap_across(early_across)
-        from_beside = swap_beside(early_beside)
     else:
         grad_pair = jnp.concatenate([grad_gate, grad_up], axis=1)
         term_pair = mm(normed_all, grad_pair, ((0,), (0,))).astype(bf16)
@@ -1122,9 +1223,7 @@
     block_output = (middle + out_sum.astype(f32)).astype(bf16)[None]
     grad_normed_two = grad_normed_two.astype(f32)
 
-    second_pull = jax.vjp(norm_rows, middle, gain_two)[1]
-    grad_mid_part, grad_gain_two = second_pull(grad_normed_two)
-    grad_middle = grad_out.astype(f32) + grad_mid_part
+    grad_middle = grad_out.astype(f32) + norm_back(middle, gain_two, grad_normed_two)
     grad_mix = grad_middle.astype(bf16)
     grad_mixed = mm(grad_mix, proj_out, ((1,), (0,)))
     carried_rows = jnp.broadcast_to(carried[None], (8, lru))
@@ -1152,30 +1251,31 @@
         [tok_count + 8, tok_count + 16],
         "mixer_backward",
     )
+    if custom:
+        from_across, from_beside, own = lax.optimization_barrier((from_across, from_beside, own))
+        beside_low, across_high = add_low(beside_low, from_across), add_low(across_high, from_beside)
+        beside_low, across_high, own = lax.optimization_barrier((beside_low, across_high, own))
+        from_beside_low, from_across_high = swap_beside(beside_low), swap_across(across_high)
     received = from_behind(head[8 - margin :], "seq", -1)
     grad_branch = jnp.concatenate(
         [own[: tok_count - margin], own[tok_count - margin :] + received], axis=0
     ).astype(bf16)
     grad_both = jnp.concatenate([grad_branch, grad_gelu_pre], axis=1)
-    grad_normed = mm(grad_both, wide, ((1,), (1,)))
-    if custom:
-        from_across, from_beside, grad_normed = lax.optimization_barrier((from_across, from_beside, grad_normed))
-        beside_low = add_low(beside_low, from_across[:half])
-        across_high = add_low(across_high, from_beside[:half])
-        beside_low, across_high, grad_normed = lax.optimization_barrier((beside_low, across_high, grad_normed))
-        mlp_parts = (
-            mine, from_across[half:], swap_across(across_high), swap_beside(beside_low), from_beside[half:]
-        )
-    first_pull = jax.vjp(norm_rows, tokens, gain_one)[1]
-    grad_tok_part, grad_gain_one = first_pull(grad_normed)
-    input_grad = (grad_middle + grad_tok_part).astype(bf16)[None]
-    vectors = jnp.concatenate([sums, grad_gain_one[None], grad_gain_two[None]], axis=0).T
-    vectors = jnp.pad(vectors, ((0, 0), (0, 128 - vectors.shape[1]))).astype(bf16)
+    vectors = jnp.pad(sums.T, ((0, 0), (0, 128 - sums.shape[0]))).astype(bf16)
     rest = jnp.concatenate([rate_w_grad, input_w_grad, vectors], axis=1)
     if custom:
-        mixer_sum, mlp_back = scatter_paired(normed, grad_both, grad_mix, mixed, rest, mlp_parts)
+        mlp_parts = (
+            (mine[:half], from_across_low, from_beside_low),
+            (mine[half:], from_across_high, from_beside_high),
+        )
+        mixer_sum, mlp_back, input_grad = scatter_paired(
+            normed, grad_both, grad_mix, mixed, rest, mlp_parts, mixer_w, block_input[0], grad_middle, gain_one
+        )
     else:
         mixer_sum, mlp_back = scatter_plain(normed, grad_both, grad_mix, mixed, rest, mlp_sum)
+        grad_normed = mm(grad_both, wide, ((1,), (1,)))
+        input_grad = (grad_middle + norm_back(tokens, gain_one, grad_normed)).astype(bf16)
+    input_grad = input_grad[None]
     mlp_grads = [mlp_back[m].astype(f32) for m in range(3)]
     mixer_sum = mixer_sum.astype(f32)
     edges = [lru, 2 * lru, 3 * lru, 3 * lru + width, 3 * lru + 2 * width]
@@ -1184,7 +1284,7 @@
     return (
         block_output,
         input_grad,
-        vec[8],
+        gain_back(mixer_gain, (branch_proj, dbranch), (gelu_proj, dgelu)),
         dbranch,
         dgelu,
         vec[: margin + 1],
@@ -1195,7 +1295,7 @@
         vec[5],
         vec[6],
         dout,
-        vec[9],
+        gain_back(mlp_gain, (gate_proj, mlp_grads[0]), (up_proj, mlp_grads[1])),
         mlp_grads[0],
         mlp_grads[1],
         mlp_grads[2],

time: 853 us -> 921 us (1.080)
  waiting for transfers between devices: 14.4 us -> 131 us
  blocking collectives: 47.4 us -> 20.1 us
  matrix products: 61.4 us -> 44.7 us
  local copies, waits for them, and re-layouts: 42.5 us -> 26.3 us
    reduce_scatter x1, waiting for transfers between devices: 0.01 us -> 64.2 us  [on_device(): lax.psum_scatter(out_part, 'fsdp', scatter_dimension=0, tiled=True)]
    ppermute x2 -> x3, waiting for transfers between devices: 1.27 us -> 50 us  [swap_beside(): return lax.ppermute(shard, 'seq', [(i, i ^ 2) for i in range(8)])]
    all_gather x2, blocking collectives: 47.4 us -> 20.1 us  [prefix(): gathered = lax.all_gather(jnp.stack(part), axis)]
    pallas_call x4 -> x5, Pallas kernels: 431 us -> 454 us  [the longest x1 183 us: gather(): pl.pallas_call(gather_kernel, in_specs=[anyspec] * 7, out_specs=[anyspec]...]
    dot_general x5 -> x4, matrix products: 61.4 us -> 44.7 us  [mm(): lax.dot_general(left, right, (dims, ((), ())), preferred_element_type=f32)]
    ppermute x3, waiting for transfers between devices: 0.01 us -> 15.1 us  [from_line(): lax.ppermute(shard, 'fsdp', [(i, (i + k) % count) for i in range(count)])]
    pallas_call x1, Pallas kernels: 84.2 us -> 70.4 us  [gather_rows(): pl.pallas_call(rows_kernel, in_specs=[anyspec] * 5, out_specs=[anyspec] *...]
    unnamed x105 -> x93, local copies, waits for them, and re-layouts: 20.6 us -> 11.5 us
  transfers between devices with their start and end apart: 17 -> 19, of which waited for: 5 -> 5; matrix products, arithmetic and copies ran while one was open for 13% -> 9% of each run, Pallas kernels for 43% -> 21%
where the time goes in v9:
time: 921 us; the launch traced here: 912 us
  Pallas kernels  608 us (66%)
  waiting for transfers between devices  131 us (14%)
  matrix products  44.7 us (5%)
  other arithmetic  44.4 us (5%)
  local copies, waits for them, and re-layouts  26.3 us (3%)
  starting transfers between devices  22.4 us (2%)
  blocking collectives  20.1 us (2%)
  between operations  15 us (2%)
    pallas_call x1, Pallas kernels, gather(): pl.pallas_call(gather_kernel, in_specs=[anyspec] * 7, out_specs=[anyspec]...  183 us
    pallas_call x1, Pallas kernels, scatter(): pl.pallas_call(scatter_kernel, in_specs=[anyspec] * 9, out_specs=[anyspec...  179 us
    pallas_call x3, Pallas kernels, products(): pl.pallas_call(functools.partial(products_kernel, sides, cuts, chips, spo...  91.7 us
    pallas_call x1, Pallas kernels, gather_rows(): pl.pallas_call(rows_kernel, in_specs=[anyspec] * 5, out_specs=[anyspec] *...  70.4 us
    reduce_scatter x1, waiting for transfers between devices, on_device(): lax.psum_scatter(out_part, 'fsdp', scatter_dimension=0, tiled=True)  64.2 us
    pallas_call x1, Pallas kernels, feed_forward(): pl.pallas_call(feed_forward_kernel, grid=(2,), in_specs=[block, block, an...  52 us
    ppermute x3, waiting for transfers between devices, swap_beside(): return lax.ppermute(shard, 'seq', [(i, i ^ 2) for i in range(8)])  50 us
    dot_general x4, matrix products, mm(): lax.dot_general(left, right, (dims, ((), ())), preferred_element_type=f32)  44.7 us
  transfers between devices with their start and end apart: 19, of which 5 were waited for; matrix products, arithmetic and copies ran while one was open for 9% of the time, Pallas kernels for 21%

profile of v9, /device:TPU:0, one launch (start us, length us, event | category | flops | bytes accessed | tf_op | source)
XLA Modules:
  0.0 911.8 jit_solution(4195954269654557719)
XLA Ops:
  8.1 1.4 stack.63
  9.6 1.5 fusion.32.first
  11.1 182.9 %gather_weights.1 = (bf16[2560,8320]{1,0:T(8,128)(2,1)}, bf16[320,5760]{1,0:T(8,128)(2,1)}) custom-call(bf16[80,640]{1,0:T(8,128)(2,1)} %fusion.32.first, bf16[80,2560]{1,0:T(8,128)(2,1)} %branch.1, bf16[80,2560]{1,0:T(8,128)(2,1)} %gelu.1, bf16[80,2560]{1,0:T(8,128)(2,1)} %outer.1, bf16[80,7680]{1,0:T(8,128)(2,1)} %gate.1, bf16[80,7680]{1,0:T(8,128)(2,1)} %up.1, ...), custom_call_target="tpu_custom_call" | custom-call | tf_op jit(solution)/shard_map/gather_weights/pallas_call | solution.py:351
  194.1 8.3 collective-permute-start.3
  203.0 2.3 slice.206
  205.7 2.2 slice_reduce_fusion
  208.4 14.8 %fusion.45 = (bf16[192,5120]{1,0:T(8,128)(2,1)S(1)}, f32[192,5120]{1,0:T(8,128)}) fusion(bf16[192,2560]{1,0:T(8,128)(2,1)S(1)} %fusion.19.refs_0_, bf16[2560,8320]{1,0:T(8,128)(2,1)} %get-tuple-element.71.mixer_w), kind=kOutput, calls=%fused_computation.131 | convolution fusion | flops 5034147840 | bytes 33095680 | tf_op jit(solution)/shard_map/dot_general | solution.py:62
  223.1 1.3 copy-done.37
  224.4 1.3 collective-permute-start
  226.1 1.7 copy.76
  228.3 3.1 fusion.43
  232.6 1.3 copy-done.2
  235.1 7.2 mixer_forward.1
  243.1 10.9 %all-gather.2 = f32[8,2,2560]{2,1,0:T(2,128)S(1)} all-gather(f32[1,2,2560]{2,1,0:T(2,128)S(1)} %fusion.33), channel_id=2, replica_groups=mesh['seq'=8,'fsdp'=4] {'seq'}, dimensions={0}, use_global_device_ids=true | all-gather | bytes 184320 | tf_op jit(solution)/shard_map/all_gather | solution.py:29
  254.5 2.0 fusion.41
  256.5 10.0 %multiply_reduce_fusion.3 = (f32[192]{0:T(256)S(1)}, f32[192,2560]{1,0:T(8,128)S(1)}) fusion(bf16[192,2560]{1,0:T(8,128)(2,1)S(1)} %get-tuple-element.240.refs_6_, bf16[2560,8320]{1,0:T(8,128)(2,1)} %get-tuple-element.71.mixer_w, bf16[1,192,2560]{2,1,0:T(8,128)(2,1)S(1)} %copy-done.22), kind=kOutput, calls=%fused_computation.44 | convolution fusion | flops 2518548224 | bytes 17040128 | tf_op jit(solution)/shard_map/dot_general | solution.py:62
  266.5 1.2 copy-done.17
  269.0 15.1 %collective-permute-done.2.grad2 = bf16[192,2560]{1,0:T(8,128)(2,1)} collective-permute-done((bf16[192,2560]{1,0:T(8,128)(2,1)}, bf16[192,2560]{1,0:T(8,128)(2,1)}, u32[]{:S(2)}, u32[]{:S(2)}) %collective-permute-start.2) | collective-permute-done | bytes 983072 | tf_op jit(solution)/shard_map/ppermute | solution.py:993
  284.1 70.4 %gather_rows.1 = (bf16[768,2560]{1,0:T(8,128)(2,1)}, bf16[768,2560]{1,0:T(8,128)(2,1)}, bf16[768,2560]{1,0:T(8,128)(2,1)}, bf16[768,2560]{1,0:T(8,128)(2,1)}) custom-call(bf16[192,2560]{1,0:T(8,128)(2,1)} %multiply_convert_fusion.normed, bf16[192,2560]{1,0:T(8,128)(2,1)} %bitcast.13.grad0, bf16[192,2560]{1,0:T(8,128)(2,1)} %collective-permute-done.1.grad1, ...), custom_call_target="tpu_custom_call" | custom-call | tf_op jit(solution)/shard_map/gather_rows/pallas_call | solution.py:470
  354.5 52.0 %feed_forward.1 = (bf16[768,1920]{1,0:T(8,128)(2,1)}, bf16[768,1920]{1,0:T(8,128)(2,1)}, bf16[768,3840]{1,0:T(8,128)(2,1)}, bf16[768,3840]{1,0:T(8,128)(2,1)}, bf16[768,2560]{1,0:T(8,128)(2,1)}) custom-call(bf16[768,2560]{1,0:T(8,128)(2,1)} %get-tuple-element.76.normed.refs_0_, bf16[768,2560]{1,0:T(8,128)(2,1)} %get-tuple-element.77.grad_out.refs_2_, ...), custom_call_target="tpu_custom_call" | custom-call | tf_op jit(solution)/shard_map/feed_forward/pallas_call | solution.py:573
  407.2 31.7 %diagonal_products.1 = (bf16[160,5760]{1,0:T(8,128)(2,1)}, bf16[160,5760]{1,0:T(8,128)(2,1)}) custom-call(s32[5]{0:T(128)} %stack.70.place, bf16[768,2560]{1,0:T(8,128)(2,1)} %get-tuple-element.76.normed.refs_0_, bf16[768,2560]{1,0:T(8,128)(2,1)} %get-tuple-element.79.refs_1_, bf16[768,2560]{1,0:T(8,128)(2,1)} %get-tuple-element.77.grad_out.refs_2_, ...), custom_call_target="tpu_custom_call" | custom-call | tf_op jit(solution)/shard_map/diagonal_products/pallas_call | solution.py:682
  438.9 36.6 %feed_forward_products.1 = (bf16[160,5760]{1,0:T(8,128)(2,1)}, bf16[160,5760]{1,0:T(8,128)(2,1)}, bf16[160,5760]{1,0:T(8,128)(2,1)}, bf16[160,5760]{1,0:T(8,128)(2,1)}, bf16[320,5760]{1,0:T(8,128)(2,1)}) custom-call(s32[5]{0:T(128)} %stack.70.place, bf16[768,2560]{1,0:T(8,128)(2,1)} %get-tuple-element.76.normed.refs_0_, ...), custom_call_target="tpu_custom_call" | custom-call | tf_op jit(solution)/shard_map/feed_forward_products/pallas_call | solution.py:682
  475.5 13.3 %fusion.9 = bf16[768,2560]{1,0:T(8,128)(2,1)} fusion(bf16[768,1920]{1,0:T(8,128)(2,1)} %get-tuple-element.87.refs_6_, bf16[2560,5760]{1,0:T(8,128)(2,1)} %all-gather.6.cloned.1.call-done.weights), kind=kOutput, calls=%fused_computation.10 | convolution fusion | flops 7551713280 | bytes 16711680 | tf_op jit(solution)/shard_map/dot_general | solution.py:62
  489.4 1.4 collective-permute-start.6
  492.6 2.8 multiply_reduce_fusion.2
  495.9 64.2 %reduce-scatter.5.cloned.1.call-done = bf16[192,2560]{1,0:T(8,128)(2,1)} async-done(((bf16[768,2560]{1,0:T(8,128)(2,1)}), bf16[192,2560]{1,0:T(8,128)(2,1)}) %reduce-scatter.5.cloned.1.call-update) | async-done | bytes 983056 | tf_op jit(solution)/shard_map/reduce_scatter | solution.py:1222
  560.1 4.8 fusion.40
  564.9 6.6 fusion.2.grad_mixed
  571.6 12.8 %mixer_backward_scan.1 = (bf16[192,2560]{1,0:T(8,128)(2,1)S(1)}, f32[192,2560]{1,0:T(8,128)S(1)}, f32[192,2560]{1,0:T(8,128)S(1)}, f32[8,2560]{1,0:T(8,128)S(1)}) custom-call(f32[192,2560]{1,0:T(8,128)S(1)} %fusion.2.grad_mixed, f32[192,2560]{1,0:T(8,128)S(1)} %copy-done.8, f32[192,2560]{1,0:T(8,128)S(1)} %copy-done.7, ...), custom_call_target="tpu_custom_call" | custom-call | tf_op jit(solution)/shard_map/mixer_backward_scan/pallas_call | solution.py:1076
  584.5 9.2 %all-gather.3 = f32[8,2,2560]{2,1,0:T(2,128)S(1)} all-gather(f32[1,2,2560]{2,1,0:T(2,128)S(1)} %fusion.34), channel_id=3, replica_groups=mesh['seq'=8,'fsdp'=4] {'seq'}, dimensions={0}, use_global_device_ids=true | all-gather | bytes 184320 | tf_op jit(solution)/shard_map/all_gather | solution.py:29
  594.2 11.2 %mixer_backward.1 = (f32[192,2560]{1,0:T(8,128)S(1)}, f32[8,2560]{1,0:T(8,128)S(1)}, bf16[2560,256]{1,0:T(8,128)(2,1)S(1)}, bf16[2560,256]{1,0:T(8,128)(2,1)S(1)}, f32[8,2560]{1,0:T(8,128)S(1)}) custom-call(f32[192,2560]{1,0:T(8,128)S(1)} %get-tuple-element.94.rev_cum, f32[192,2560]{1,0:T(8,128)S(1)} %get-tuple-element.95.rev_grad, ...), custom_call_target="tpu_custom_call" | custom-call | tf_op jit(solution)/shard_map/mixer_backward/pallas_call | solution.py:1076
  606.5 1.3 copy-done.15
  607.8 1.3 collective-permute-start.8
  609.5 1.8 fusion.15
  612.8 5.1 add_convert_fusion.2
  620.5 1.8 collective-permute-start.15
  622.6 2.6 collective-permute-start.14
  626.1 1.5 pad_maximum_fusion.1.rest
  627.6 1.8 collective-permute-done.9.refs_5_
  629.3 23.4 %mixer_products.1 = bf16[1280,7680]{1,0:T(8,128)(2,1)} custom-call(s32[5]{0:T(128)} %stack.70.place, bf16[192,2560]{1,0:T(8,128)(2,1)} %copy-done.25, bf16[192,2560]{1,0:T(8,128)(2,1)} %collective-permute-done.4.refs_1_, bf16[192,2560]{1,0:T(8,128)(2,1)} %copy-done.27, bf16[192,2560]{1,0:T(8,128)(2,1)} %copy-done.35, bf16[192,5120]{1,0:T(8,128)(2,1)} %copy-done.18, ...), custom_call_target="tpu_custom_call" | custom-call | tf_op jit(solution)/shard_map/mixer_products/pallas_call | solution.py:682
  652.7 11.2 %collective-permute-done.15 = bf16[160,5760]{1,0:T(8,128)(2,1)} collective-permute-done((bf16[160,5760]{1,0:T(8,128)(2,1)}, bf16[160,5760]{1,0:T(8,128)(2,1)}, u32[]{:S(2)}, u32[]{:S(2)}) %collective-permute-start.15) | collective-permute-done | bytes 1843232 | tf_op jit(solution)/shard_map/ppermute | solution.py:1003
  663.9 38.8 %collective-permute-done.13 = bf16[160,5760]{1,0:T(8,128)(2,1)} collective-permute-done((bf16[160,5760]{1,0:T(8,128)(2,1)}, bf16[160,5760]{1,0:T(8,128)(2,1)}, u32[]{:S(2)}, u32[]{:S(2)}) %collective-permute-start.13) | collective-permute-done | bytes 1843232 | tf_op jit(solution)/shard_map/ppermute | solution.py:1003
  702.7 4.1 add_convert_fusion.1.mlp_low
  706.8 4.0 add_convert_fusion.mlp_high
  711.4 179.5 %scatter_gradients.1 = (bf16[80,8320]{1,0:T(8,128)(2,1)}, bf16[3,80,7680]{2,1,0:T(8,128)(2,1)}, bf16[192,2560]{1,0:T(8,128)(2,1)}) custom-call(bf16[4,320,7680]{2,1,0:T(8,128)(2,1)} %bitcast.65, bf16[4,320,640]{2,1,0:T(8,128)(2,1)} %pad_maximum_fusion.1.rest, bf16[160,5760]{1,0:T(8,128)(2,1)} %add_convert_fusion.1.mlp_low, ...), custom_call_target="tpu_custom_call" | custom-call | tf_op jit(solution)/shard_map/scatter_gradients/pallas_call | solution.py:952
  890.9 3.1 bitcast_convert_fusion
  894.0 4.8 multiply_reduce_fusion
  899.6 1.6 multiply_reduce_fusion.4
  (164 shorter events, 23.7 us)
Async XLA Ops:
  7.2 347.3 %all-gather.6.cloned.1.call-start = ((), (), s32[]{:S(2)}) async-start(), calls=%async_computation.2 | async-start | bytes 33177600 | tf_op jit(solution)/shard_map/all_gather | solution.py:1132
  194.0 294.8 %reduce-scatter.3.cloned.1.call-start = ((), (), s32[]{:S(2)}) async-start(), calls=%async_computation.3 | async-start | bytes 4915200 | tf_op jit(solution)/shard_map/reduce_scatter | solution.py:1198
  194.1 74.9 %collective-permute-start.3 = (bf16[192,2560]{1,0:T(8,128)(2,1)}, bf16[192,2560]{1,0:T(8,128)(2,1)}, u32[]{:S(2)}, u32[]{:S(2)}) collective-permute-start(bf16[192,2560]{1,0:T(8,128)(2,1)} %bitcast.13.grad0), channel_id=1, source_target_pairs={{0,3},{1,0},{2,1},{3,2},{4,7},{5,4},{6,5},{7,6},{8,11},{9,8},{10,9... | collective-permute-start | bytes 2949128 | tf_op jit(solution)/shard_map/ppermute | solution.py:993
  202.4 81.7 %collective-permute-start.2 = (bf16[192,2560]{1,0:T(8,128)(2,1)}, bf16[192,2560]{1,0:T(8,128)(2,1)}, u32[]{:S(2)}, u32[]{:S(2)}) collective-permute-start(bf16[192,2560]{1,0:T(8,128)(2,1)} %bitcast.13.grad0), channel_id=1, source_target_pairs={{0,2},{1,3},{2,0},{3,1},{4,6},{5,7},{6,4},{7,5},{8,10},{9,11},{10,... | collective-permute-start | bytes 2949128 | tf_op jit(solution)/shard_map/ppermute | solution.py:993
  202.4 81.7 %collective-permute-start.1 = (bf16[192,2560]{1,0:T(8,128)(2,1)}, bf16[192,2560]{1,0:T(8,128)(2,1)}, u32[]{:S(2)}, u32[]{:S(2)}) collective-permute-start(bf16[192,2560]{1,0:T(8,128)(2,1)} %bitcast.13.grad0), channel_id=1, source_target_pairs={{0,1},{1,2},{2,3},{3,0},{4,5},{5,6},{6,7},{7,4},{8,9},{9,10},{10,1... | collective-permute-start | bytes 2949128 | tf_op jit(solution)/shard_map/ppermute | solution.py:993
  208.0 15.1 %copy-start.39 = (f32[2560]{0:T(1024)}, f32[2560]{0:T(1024)S(1)}, u32[]{:S(2)}) copy-start(f32[2560]{0:T(1024)S(1)} %get-tuple-element.194) | copy-start | bytes 30724
  208.3 14.8 %copy-start.25 = (bf16[192,2560]{1,0:T(8,128)(2,1)}, bf16[192,2560]{1,0:T(8,128)(2,1)S(1)}, u32[]{:S(2)}) copy-start(bf16[192,2560]{1,0:T(8,128)(2,1)S(1)} %fusion.19.refs_0_) | copy-start | bytes 2949124
  224.4 8.1 collective-permute-start
  228.3 3.2 copy-start.38
  235.1 19.4 %copy-start.34 = (f32[192,5120]{1,0:T(8,128)S(1)}, f32[192,5120]{1,0:T(8,128)}, u32[]{:S(2)}) copy-start(f32[192,5120]{1,0:T(8,128)} %get-tuple-element.264) | copy-start | bytes 11796484
  242.3 14.2 %copy-start.1 = (f32[192,2560]{1,0:T(8,128)}, f32[192,2560]{1,0:T(8,128)S(1)}, u32[]{:S(2)}) copy-start(f32[192,2560]{1,0:T(8,128)S(1)} %get-tuple-element.72.local) | copy-start | bytes 5898244
  242.4 14.1 %copy-start.6 = (f32[192,2560]{1,0:T(8,128)}, f32[192,2560]{1,0:T(8,128)S(1)}, u32[]{:S(2)}) copy-start(f32[192,2560]{1,0:T(8,128)S(1)} %get-tuple-element.93.rate_pre) | copy-start | bytes 5898244
  242.4 14.1 %copy-start.9 = (f32[192,2560]{1,0:T(8,128)}, f32[192,2560]{1,0:T(8,128)S(1)}, u32[]{:S(2)}) copy-start(f32[192,2560]{1,0:T(8,128)S(1)} %get-tuple-element.97.input_pre) | copy-start | bytes 5898244
  242.4 14.1 %copy-start.11 = (bf16[192,2560]{1,0:T(8,128)(2,1)}, bf16[192,2560]{1,0:T(8,128)(2,1)S(1)}, u32[]{:S(2)}) copy-start(bf16[192,2560]{1,0:T(8,128)(2,1)S(1)} %get-tuple-element.98.conv) | copy-start | bytes 2949124
  242.4 329.2 %copy-start = (f32[192,2560]{1,0:T(8,128)}, f32[192,2560]{1,0:T(8,128)S(1)}, u32[]{:S(2)}) copy-start(f32[192,2560]{1,0:T(8,128)S(1)} %get-tuple-element.73.cum) | copy-start | bytes 5898244
  256.5 10.0 %copy-start.26 = (bf16[192,2560]{1,0:T(8,128)(2,1)}, bf16[192,2560]{1,0:T(8,128)(2,1)S(1)}, u32[]{:S(2)}) copy-start(bf16[192,2560]{1,0:T(8,128)(2,1)S(1)} %get-tuple-element.240.refs_6_) | copy-start | bytes 2949124
  406.5 153.6 %reduce-scatter.5.cloned.1.call-start = ((), (), s32[]{:S(2)}) async-start(), calls=%async_computation.4 | async-start | bytes 4915200 | tf_op jit(solution)/shard_map/reduce_scatter | solution.py:1222
  488.8 131.7 %collective-permute-start.4 = (bf16[192,2560]{1,0:T(8,128)(2,1)}, bf16[192,2560]{1,0:T(8,128)(2,1)}, u32[]{:S(2)}, u32[]{:S(2)}) collective-permute-start(bf16[192,2560]{1,0:T(8,128)(2,1)} %copy-done.25), channel_id=1, source_target_pairs={{0,4},{4,0},{8,12},{12,8},{16,20},{20,16},{24,28},{28,24},{1,5},{5... | collective-permute-start | bytes 2949128 | tf_op jit(solution)/shard_map/ppermute | solution.py:999
  489.3 133.0 %collective-permute-start.10 = (bf16[192,2560]{1,0:T(8,128)(2,1)}, bf16[192,2560]{1,0:T(8,128)(2,1)}, u32[]{:S(2)}, u32[]{:S(2)}) collective-permute-start(bf16[192,2560]{1,0:T(8,128)(2,1)} %copy-done.26), channel_id=1, source_target_pairs={{0,4},{4,0},{8,12},{12,8},{16,20},{20,16},{24,28},{28,24},{1,5},{5... | collective-permute-start | bytes 2949128 | tf_op jit(solution)/shard_map/ppermute | solution.py:999
  489.4 118.4 %collective-permute-start.6 = (bf16[160,5760]{1,0:T(8,128)(2,1)}, bf16[160,5760]{1,0:T(8,128)(2,1)}, u32[]{:S(2)}, u32[]{:S(2)}) collective-permute-start(bf16[160,5760]{1,0:T(8,128)(2,1)} %get-tuple-element.84), channel_id=1, source_target_pairs={{0,16},{4,20},{8,24},{12,28},{16,0},{20,4},{24,8},{28,12},{1,17},{... | collective-permute-start | bytes 5529608 | tf_op jit(solution)/shard_map/ppermute | solution.py:1007
  490.9 161.8 %collective-permute-start.12 = (bf16[160,5760]{1,0:T(8,128)(2,1)}, bf16[160,5760]{1,0:T(8,128)(2,1)}, u32[]{:S(2)}, u32[]{:S(2)}) collective-permute-start(bf16[160,5760]{1,0:T(8,128)(2,1)} %get-tuple-element.110), channel_id=1, source_target_pairs={{0,16},{4,20},{8,24},{12,28},{16,0},{20,4},{24,8},{28,12},{1,17},{... | collective-permute-start | bytes 5529608 | tf_op jit(solution)/shard_map/ppermute | solution.py:1007
  491.5 116.3 %collective-permute-start.7 = (bf16[160,5760]{1,0:T(8,128)(2,1)}, bf16[160,5760]{1,0:T(8,128)(2,1)}, u32[]{:S(2)}, u32[]{:S(2)}) collective-permute-start(bf16[160,5760]{1,0:T(8,128)(2,1)} %get-tuple-element.92), channel_id=1, source_target_pairs={{0,8},{4,12},{8,0},{12,4},{16,24},{20,28},{24,16},{28,20},{1,9},{5... | collective-permute-start | bytes 5529608 | tf_op jit(solution)/shard_map/ppermute | solution.py:1003
  564.9 6.6 copy-start.27
  564.9 6.7 copy-start.7
  564.9 6.7 copy-start.8
  571.6 12.9 %copy-start.42 = (f32[1,2560]{1,0:T(1,128)S(1)}, f32[1,2560]{1,0:T(1,128)}, u32[]{:S(2)}) copy-start(f32[1,2560]{1,0:T(1,128)} %copy-done.41) | copy-start | bytes 30724
  571.6 22.6 %copy-start.3 = (bf16[2560,256]{1,0:T(8,128)(2,1)S(1)}, bf16[2560,256]{1,0:T(8,128)(2,1)}, u32[]{:S(2)}) copy-start(bf16[2560,256]{1,0:T(8,128)(2,1)} %get-tuple-element.246.rate_w) | copy-start | bytes 3932164
  571.6 22.6 %copy-start.5 = (bf16[192,2560]{1,0:T(8,128)(2,1)S(1)}, bf16[192,2560]{1,0:T(8,128)(2,1)}, u32[]{:S(2)}) copy-start(bf16[192,2560]{1,0:T(8,128)(2,1)} %slice.270.branch) | copy-start | bytes 2949124
  571.6 22.6 %copy-start.12 = (bf16[192,2560]{1,0:T(8,128)(2,1)S(1)}, bf16[192,2560]{1,0:T(8,128)(2,1)}, u32[]{:S(2)}) copy-start(bf16[192,2560]{1,0:T(8,128)(2,1)} %copy-done.11) | copy-start | bytes 2949124
  584.4 21.0 %copy-start.13 = (bf16[192,2560]{1,0:T(8,128)(2,1)}, bf16[192,2560]{1,0:T(8,128)(2,1)S(1)}, u32[]{:S(2)}) copy-start(bf16[192,2560]{1,0:T(8,128)(2,1)S(1)} %get-tuple-element.106) | copy-start | bytes 2949124
  607.8 10.2 %collective-permute-start.8 = (f32[3,2560]{1,0:T(4,128)S(1)}, f32[3,2560]{1,0:T(4,128)S(1)}, u32[]{:S(2)}, u32[]{:S(2)}) collective-permute-start(f32[3,2560]{1,0:T(4,128)S(1)} %slice.257), channel_id=1, source_target_pairs={{4,0},{8,4},{12,8},{16,12},{20,16},{24,20},{28,24},{5,1},{9,5},{13... | collective-permute-start | bytes 92168 | tf_op jit(solution)/shard_map/ppermute | solution.py:23
  609.5 3.2 copy-start.31
  611.4 13.8 %collective-permute-start.11 = (bf16[4,320,640]{2,1,0:T(8,128)(2,1)S(1)}, bf16[4,320,640]{2,1,0:T(8,128)(2,1)S(1)}, u32[]{:S(2)}, u32[]{:S(2)}) collective-permute-start(bf16[4,320,640]{2,1,0:T(8,128)(2,1)S(1)} %dynamic-slice_bitcast_fusion), channel_id=1, source_target_pairs={{0,4},{4,0},{8,12},{12,8},{16,20},{20,16},{24,28},{28,24},{1,5},{5... | collective-permute-start | bytes 4915208 | tf_op jit(solution)/shard_map/ppermute | solution.py:999
  612.8 5.1 copy-start.16
  619.1 3.5 collective-permute-start.5
  620.2 5.0 copy-start.29
  620.5 5.0 copy-start.18
  620.5 43.4 %collective-permute-start.15 = (bf16[160,5760]{1,0:T(8,128)(2,1)}, bf16[160,5760]{1,0:T(8,128)(2,1)}, u32[]{:S(2)}, u32[]{:S(2)}) collective-permute-start(bf16[160,5760]{1,0:T(8,128)(2,1)} %get-tuple-element.113), channel_id=1, source_target_pairs={{0,8},{4,12},{8,0},{12,4},{16,24},{20,28},{24,16},{28,20},{1,9},{5... | collective-permute-start | bytes 5529608 | tf_op jit(solution)/shard_map/ppermute | solution.py:1003
  622.3 80.4 %collective-permute-start.13 = (bf16[160,5760]{1,0:T(8,128)(2,1)}, bf16[160,5760]{1,0:T(8,128)(2,1)}, u32[]{:S(2)}, u32[]{:S(2)}) collective-permute-start(bf16[160,5760]{1,0:T(8,128)(2,1)} %get-tuple-element.111), channel_id=1, source_target_pairs={{0,8},{4,12},{8,0},{12,4},{16,24},{20,28},{24,16},{28,20},{1,9},{5... | collective-permute-start | bytes 5529608 | tf_op jit(solution)/shard_map/ppermute | solution.py:1003
  622.6 2.9 copy-start.35
  622.6 80.1 %collective-permute-start.14 = (bf16[160,5760]{1,0:T(8,128)(2,1)}, bf16[160,5760]{1,0:T(8,128)(2,1)}, u32[]{:S(2)}, u32[]{:S(2)}) collective-permute-start(bf16[160,5760]{1,0:T(8,128)(2,1)} %get-tuple-element.112), channel_id=1, source_target_pairs={{0,16},{4,20},{8,24},{12,28},{16,0},{20,4},{24,8},{28,12},{1,17},{... | collective-permute-start | bytes 5529608 | tf_op jit(solution)/shard_map/ppermute | solution.py:1007
  625.2 4.1 collective-permute-start.9
  706.8 4.0 copy-start.40
  890.9 3.1 copy-start.23
  890.9 3.1 copy-start.24
  894.0 4.9 copy-start.20
  894.0 5.5 copy-start.32
  894.0 5.5 copy-start.33
  (16 other events, 26.7 us)
Sparse Core Ops, SparseCore 0:
  194.1 149.1 all-gather.5
  406.6 71.0 reduce-scatter.2
  489.0 71.1 reduce-scatter.4

commit v10 on v9

--- a/solution.py
+++ b/solution.py
@@ -695,6 +695,7 @@
         ),
         out_shape=[jax.ShapeDtypeStruct((rows, total * width), bf16) for rows in cuts],
         compiler_params=pltpu.CompilerParams(vmem_limit_bytes=58 * 1024 * 1024),
+        cost_estimate=pl.CostEstimate(flops=1, bytes_accessed=1, transcendentals=0),
         name=name,
     )(place, *[a for pair in lefts for a in pair], *[a for _, own, other in rights for a in (own, other)])
 
@@ -709,6 +710,147 @@
         return carry
 
     lax.fori_loop(0, size // step, one, 0)
+
+
+def shared_products_kernel(
+    normed, normed_other, grad, grad_other, pair, pair_other, hidden, hidden_other,
+    beside_high, across_low, mine, beside_low, across_high,
+    turned, slots, stage, diag, landed, waiting, load_sem, send_sem, recv_sem, store_sem,
+):
+    s, z, _, beside, across = places()
+    step = pl.program_id(0)
+    lefts = ((normed, normed_other), (grad, grad_other))
+    chip_cols = normed.shape[1] // 4
+    half = chip_cols // 2
+    piece = half // 2
+    width = pair.shape[1]
+    diagonal = beside + across - s
+    chips = [q // 2 for q in (diagonal, beside, across, s)]
+
+    def load(side, q, who):
+        cols = pl.ds(pl.multiple_of(chips[q] * chip_cols, 128), chip_cols)
+        return pltpu.make_async_copy(lefts[side][who].at[:, cols], slots.at[q % 2, who], load_sem.at[q % 2, who])
+
+    def fetch(side):
+        for q in range(2):
+            for who in range(2):
+                load(side, q, who).start()
+
+    def turn(side):
+        for q in range(4):
+            for who in range(2):
+                load(side, q, who).wait()
+                stage[...] = slots[q % 2, who].T
+                turned[who, q * half : (q + 1) * half, :] = stage[
+                    pl.ds(pl.multiple_of(s % 2 * half, 16), half), :
+                ]
+                if q < 2:
+                    load(side, q + 2, who).start()
+
+    def tile(own, other, start, size):
+        cols = pl.ds(start, size)
+        block = mm(turned[0], own[:, cols], ((1,), (0,)))
+        block = (block + mm(turned[1], other[:, cols], ((1,), (0,)))).astype(bf16)
+        parts = [block[n * piece : (n + 1) * piece] for n in range(8)]
+        there = pl.ds(pl.multiple_of(step * width + start, 128), size)
+        diag[0, :, there] = parts[0]
+        diag[1, :, there] = parts[1]
+        waiting[0, :, there] = parts[2]
+        beside_high[:, cols] = parts[3]
+        across_low[:, cols] = parts[4]
+        waiting[1, :, there] = parts[5]
+        mine[0:piece, cols] = parts[6]
+        mine[piece:, cols] = parts[7]
+
+    def multiply(own, other):
+        def one(turn, carry):
+            tile(own, other, pl.multiple_of(turn * 512, 512), 512)
+            return carry
+
+        lax.fori_loop(0, width // 512, one, 0)
+        if width % 512:
+            tile(own, other, width // 512 * 512, width % 512)
+
+    def push(way, j):
+        cols = pl.ds(j * width, width)
+        return pltpu.make_async_remote_copy(
+            src_ref=diag.at[way, :, cols],
+            dst_ref=landed.at[way, :, cols],
+            send_sem=send_sem.at[way, j],
+            recv_sem=recv_sem.at[way, j],
+            device_id=(across if way == 0 else beside, z),
+            device_id_type=MESH,
+        )
+
+    def store(way, j):
+        cols = pl.ds(j * width, width)
+        return pltpu.make_async_copy(
+            waiting.at[way, :, cols], (beside_low, across_high)[way].at[:, cols], store_sem.at[way, j]
+        )
+
+    @pl.when(step == 0)
+    def _():
+        fetch(0)
+        greet([(beside, z), (across, z)])
+        turn(0)
+
+    pl.when(step == 2)(functools.partial(turn, 1))
+    pl.when(step < 2)(functools.partial(multiply, pair, pair_other))
+    pl.when(step == 1)(functools.partial(fetch, 1))
+    pl.when(step == 2)(functools.partial(multiply, hidden, hidden_other))
+    for j in range(3):
+
+        @pl.when(step == j)
+        def _(j=j):
+            push(0, j).start()
+            push(1, j).start()
+
+    @pl.when(step == 2)
+    def _():
+        for j in range(3):
+            for way in range(2):
+                push(way, j).wait_recv()
+                add_columns(waiting.at[way], [landed.at[way]], j * width, width, 384)
+                store(way, j).start()
+        for j in range(3):
+            for way in range(2):
+                push(way, j).wait_send()
+                store(way, j).wait()
+
+
+def shared_products(lefts, pair, hidden):
+    tok, model = lefts[0].shape
+    width = hidden[0].shape[1]
+    half = model // 8
+    anyspec = pl.BlockSpec(memory_space=pl.ANY)
+    dma = pltpu.SemaphoreType.DMA
+
+    def block(rows):
+        return pl.BlockSpec((rows, width), lambda j: (0, j))
+
+    pair_spec = pl.BlockSpec((tok, width), lambda j: (0, jnp.minimum(j, 1)))
+    hidden_spec = pl.BlockSpec((tok, width), lambda j: (0, 0))
+    rows_out = (half // 2, half // 2, half, half // 2, half // 2)
+    return pl.pallas_call(
+        shared_products_kernel,
+        grid=(3,),
+        in_specs=[anyspec] * 4 + [pair_spec] * 2 + [hidden_spec] * 2,
+        out_specs=[block(rows) for rows in rows_out[:3]] + [anyspec] * 2,
+        out_shape=[jax.ShapeDtypeStruct((rows, 3 * width), bf16) for rows in rows_out],
+        scratch_shapes=[
+            pltpu.VMEM((2, 4 * half, tok), bf16),
+            pltpu.VMEM((2, 2, tok, 2 * half), bf16),
+            pltpu.VMEM((2 * half, tok), bf16),
+            pltpu.VMEM((2, half // 2, 3 * width), bf16),
+            pltpu.VMEM((2, half // 2, 3 * width), bf16),
+            pltpu.VMEM((2, half // 2, 3 * width), bf16),
+            dma((2, 2)), dma((2, 3)), dma((2, 3)), dma((2, 3)),
+        ],
+        compiler_params=pltpu.CompilerParams(
+            collective_id=5, has_side_effects=True, vmem_limit_bytes=60 * 1024 * 1024
+        ),
+        name="feed_forward_products",
+    )(*lefts, *pair, *hidden)
 
 
 def scatter_kernel(
@@ -1081,6 +1223,7 @@
         out_shape=out_shape,
         scratch_shapes=[pltpu.VMEM((rows, width), f32) for rows in scratch],
         compiler_params=pltpu.CompilerParams(vmem_limit_bytes=40 * 1024 * 1024),
+        cost_estimate=pl.CostEstimate(flops=1, bytes_accessed=1, transcendentals=0),
         name=name,
     )(*[a for a, _ in ins])
 
@@ -1198,14 +1341,8 @@
     grad_normed_two = lax.psum_scatter(grad_normed_part, "fsdp", scatter_dimension=0, tiled=True)
     if custom:
         half = model // 16
-        lefts = [(normed_all, normed_other), (grad_out_all, grad_out_other)]
-        rights = [(0, grad_pair, pair_other), (1, hidden, hidden_other)]
-        diag_low, diag_high = products(lefts, rights, (half, half), (0,), (0, 1), ff_part, "diagonal_products")
-        from_across, from_beside = swap_across(diag_low), swap_beside(diag_high)
-        late = lax.optimization_barrier((grad_pair, diag_low))[0]
-        rights = [(0, late, pair_other), (1, hidden, hidden_other)]
-        beside_low, beside_high, across_low, across_high, mine = products(
-            lefts, rights, (half,) * 4 + (2 * half,), (1, 2, 3), tuple(range(6)), ff_part, "feed_forward_products"
+        beside_high, across_low, mine, beside_low, across_high = shared_products(
+            (normed_all, normed_other, grad_out_all, grad_out_other), (grad_pair, pair_other), (hidden, hidden_other)
         )
         from_beside_high, from_across_low = swap_beside(beside_high), swap_across(across_low)
         hidden = lax.optimization_barrier((hidden, mine))[0]
@@ -1220,7 +1357,6 @@
         mlp_sum = jnp.concatenate([pair_sum, down_sum], axis=1)
         out_part = mm(hidden, w_down, ((1,), (1,))).astype(bf16)
     out_sum = lax.psum_scatter(out_part, "fsdp", scatter_dimension=0, tiled=True)
-    block_output = (middle + out_sum.astype(f32)).astype(bf16)[None]
     grad_normed_two = grad_normed_two.astype(f32)
 
     grad_middle = grad_out.astype(f32) + norm_back(middle, gain_two, grad_normed_two)
@@ -1236,7 +1372,14 @@
         [tok_count + 8],
         "mixer_backward_scan",
     )
+    if custom:
+        from_beside_high, from_across_low, pair_grad = lax.optimization_barrier(
+            (from_beside_high, from_across_low, pair_grad)
+        )
     incoming = prefix((cum[-1], pair_grad[0]), "seq", True)
+    if custom:
+        beside_low, across_high, incoming = lax.optimization_barrier((beside_low, across_high, incoming))
+        from_beside_low, from_across_high = swap_beside(beside_low), swap_across(across_high)
     incoming_rows = jnp.broadcast_to(incoming[None], (8, lru))
     own, head, rate_w_grad, input_w_grad, sums = call_heads(
         mixer_backward,
@@ -1251,16 +1394,13 @@
         [tok_count + 8, tok_count + 16],
         "mixer_backward",
     )
-    if custom:
-        from_across, from_beside, own = lax.optimization_barrier((from_across, from_beside, own))
-        beside_low, across_high = add_low(beside_low, from_across), add_low(across_high, from_beside)
-        beside_low, across_high, own = lax.optimization_barrier((beside_low, across_high, own))
-        from_beside_low, from_across_high = swap_beside(beside_low), swap_across(across_high)
     received = from_behind(head[8 - margin :], "seq", -1)
     grad_branch = jnp.concatenate(
         [own[: tok_count - margin], own[tok_count - margin :] + received], axis=0
     ).astype(bf16)
     grad_both = jnp.concatenate([grad_branch, grad_gelu_pre], axis=1)
+    middle, out_sum, sums = lax.optimization_barrier((middle, out_sum, sums))
+    block_output = (middle + out_sum.astype(f32)).astype(bf16)[None]
     vectors = jnp.pad(sums.T, ((0, 0), (0, 128 - sums.shape[0]))).astype(bf16)
     rest = jnp.concatenate([rate_w_grad, input_w_grad, vectors], axis=1)
     if custom:

time: 921 us -> 821 us (0.89)
  waiting for transfers between devices: 131 us -> 27.4 us
    pallas_call x3 -> x1, Pallas kernels: 91.7 us -> 23.5 us  [products(): pl.pallas_call(functools.partial(products_kernel, sides, cuts, chips, spo...]
    pallas_call x0 -> x1, Pallas kernels: none -> 65.4 us  [shared_products(): pl.pallas_call(shared_products_kernel, grid=(3,), in_specs=[anyspec] * 4...]
    reduce_scatter x1, waiting for transfers between devices: 64.2 us -> 0.01 us  [on_device(): lax.psum_scatter(out_part, 'fsdp', scatter_dimension=0, tiled=True)]
    ppermute x3 -> x2, waiting for transfers between devices: 50 us -> 19 us  [swap_beside(): return lax.ppermute(shard, 'seq', [(i, i ^ 2) for i in range(8)])]
    ppermute x3, waiting for transfers between devices: 15.1 us -> 0.01 us  [from_line(): lax.ppermute(shard, 'fsdp', [(i, (i + k) % count) for i in range(count)])]
    pallas_call x1, Pallas kernels: 70.4 us -> 83.8 us  [gather_rows(): pl.pallas_call(rows_kernel, in_specs=[anyspec] * 5, out_specs=[anyspec] *...]
  transfers between devices with their start and end apart: 19 -> 17, of which waited for: 5 -> 4; matrix products, arithmetic and copies ran while one was open for 9% -> 10% of each run, Pallas kernels for 21% -> 25%
where the time goes in v10:
time: 821 us; the launch traced here: 812 us
  Pallas kernels  617 us (75%)
  matrix products  45.4 us (6%)
  other arithmetic  38.2 us (5%)
  local copies, waits for them, and re-layouts  31 us (4%)
  waiting for transfers between devices  27.4 us (3%)
  blocking collectives  20.3 us (2%)
  starting transfers between devices  17.6 us (2%)
  between operations  15.1 us (2%)
    pallas_call x1, Pallas kernels, gather(): pl.pallas_call(gather_kernel, in_specs=[anyspec] * 7, out_specs=[anyspec]...  183 us
    pallas_call x1, Pallas kernels, scatter(): pl.pallas_call(scatter_kernel, in_specs=[anyspec] * 9, out_specs=[anyspec...  179 us
    pallas_call x1, Pallas kernels, gather_rows(): pl.pallas_call(rows_kernel, in_specs=[anyspec] * 5, out_specs=[anyspec] *...  83.8 us
    pallas_call x1, Pallas kernels, shared_products(): pl.pallas_call(shared_products_kernel, grid=(3,), in_specs=[anyspec] * 4...  65.4 us
    pallas_call x1, Pallas kernels, feed_forward(): pl.pallas_call(feed_forward_kernel, grid=(2,), in_specs=[block, block, an...  52 us
    dot_general x4, matrix products, mm(): lax.dot_general(left, right, (dims, ((), ())), preferred_element_type=f32)  45.4 us
    pallas_call x3, Pallas kernels, call_heads(): pl.pallas_call(kernel, grid=(heads,), in_specs=in_specs, out_specs=out_sp...  31.3 us
    pallas_call x1, Pallas kernels, products(): pl.pallas_call(functools.partial(products_kernel, sides, cuts, chips, spo...  23.5 us
  transfers between devices with their start and end apart: 17, of which 4 were waited for; matrix products, arithmetic and copies ran while one was open for 10% of the time, Pallas kernels for 25%

profile of v10, /device:TPU:0, one launch (start us, length us, event | category | flops | bytes accessed | tf_op | source)
XLA Modules:
  0.0 812.4 jit_solution(2558983745455083507)
XLA Ops:
  8.1 1.4 stack.51
  9.6 1.5 fusion.32.first
  11.1 182.9 %gather_weights.1 = (bf16[2560,8320]{1,0:T(8,128)(2,1)}, bf16[320,5760]{1,0:T(8,128)(2,1)}) custom-call(bf16[80,640]{1,0:T(8,128)(2,1)} %fusion.32.first, bf16[80,2560]{1,0:T(8,128)(2,1)} %branch.1, bf16[80,2560]{1,0:T(8,128)(2,1)} %gelu.1, bf16[80,2560]{1,0:T(8,128)(2,1)} %outer.1, bf16[80,7680]{1,0:T(8,128)(2,1)} %gate.1, bf16[80,7680]{1,0:T(8,128)(2,1)} %up.1, ...), custom_call_target="tpu_custom_call" | custom-call | tf_op jit(solution)/shard_map/gather_weights/pallas_call | solution.py:351
  194.1 5.5 collective-permute-start.1
  199.5 3.4 collective-permute-start.2
  202.9 2.3 slice.206
  205.6 2.2 slice_reduce_fusion
  209.1 15.0 %fusion.45 = (bf16[192,5120]{1,0:T(8,128)(2,1)S(1)}, f32[192,5120]{1,0:T(8,128)}) fusion(bf16[192,2560]{1,0:T(8,128)(2,1)} %fusion.19.refs_0_, bf16[2560,8320]{1,0:T(8,128)(2,1)} %get-tuple-element.71.mixer_w), kind=kOutput, calls=%fused_computation.129 | convolution fusion | flops 5034147840 | bytes 33095680 | tf_op jit(solution)/shard_map/dot_general | solution.py:62
  224.1 1.3 copy-done.43
  225.4 1.3 collective-permute-start
  226.7 1.7 copy.76
  229.3 3.1 fusion.43
  233.6 1.3 copy-done.2
  236.1 7.2 mixer_forward.1
  244.1 10.9 %all-gather.2 = f32[8,2,2560]{2,1,0:T(2,128)S(1)} all-gather(f32[1,2,2560]{2,1,0:T(2,128)S(1)} %fusion.33), channel_id=2, replica_groups=mesh['seq'=8,'fsdp'=4] {'seq'}, dimensions={0}, use_global_device_ids=true | all-gather | bytes 184320 | tf_op jit(solution)/shard_map/all_gather | solution.py:29
  255.5 2.0 fusion.41
  257.5 10.3 %multiply_reduce_fusion.3 = (f32[192]{0:T(256)S(1)}, f32[192,2560]{1,0:T(8,128)S(1)}) fusion(bf16[192,2560]{1,0:T(8,128)(2,1)S(1)} %get-tuple-element.240.refs_6_, bf16[2560,8320]{1,0:T(8,128)(2,1)} %get-tuple-element.71.mixer_w, bf16[1,192,2560]{2,1,0:T(8,128)(2,1)S(1)} %copy-done.27), kind=kOutput, calls=%fused_computation.42 | convolution fusion | flops 2518548224 | bytes 17040128 | tf_op jit(solution)/shard_map/dot_general | solution.py:62
  267.9 1.2 copy-done.19
  270.3 83.8 %gather_rows.1 = (bf16[768,2560]{1,0:T(8,128)(2,1)}, bf16[768,2560]{1,0:T(8,128)(2,1)}, bf16[768,2560]{1,0:T(8,128)(2,1)}, bf16[768,2560]{1,0:T(8,128)(2,1)}) custom-call(bf16[192,2560]{1,0:T(8,128)(2,1)} %multiply_convert_fusion.normed, bf16[192,2560]{1,0:T(8,128)(2,1)} %bitcast.13.grad0, bf16[192,2560]{1,0:T(8,128)(2,1)} %collective-permute-done.1.grad1, ...), custom_call_target="tpu_custom_call" | custom-call | tf_op jit(solution)/shard_map/gather_rows/pallas_call | solution.py:470
  354.1 52.0 %feed_forward.1 = (bf16[768,1920]{1,0:T(8,128)(2,1)}, bf16[768,1920]{1,0:T(8,128)(2,1)}, bf16[768,3840]{1,0:T(8,128)(2,1)}, bf16[768,3840]{1,0:T(8,128)(2,1)}, bf16[768,2560]{1,0:T(8,128)(2,1)}) custom-call(bf16[768,2560]{1,0:T(8,128)(2,1)} %get-tuple-element.76.normed, bf16[768,2560]{1,0:T(8,128)(2,1)} %get-tuple-element.77.grad_out.grad, ...), custom_call_target="tpu_custom_call" | custom-call | tf_op jit(solution)/shard_map/feed_forward/pallas_call | solution.py:573
  406.2 65.4 %feed_forward_products.1 = (bf16[160,5760]{1,0:T(8,128)(2,1)}, bf16[160,5760]{1,0:T(8,128)(2,1)}, bf16[320,5760]{1,0:T(8,128)(2,1)}, bf16[160,5760]{1,0:T(8,128)(2,1)}, bf16[160,5760]{1,0:T(8,128)(2,1)}) custom-call(bf16[768,2560]{1,0:T(8,128)(2,1)} %get-tuple-element.76.normed, bf16[768,2560]{1,0:T(8,128)(2,1)} %get-tuple-element.79.normed_other, ...), custom_call_target="tpu_custom_call" | custom-call | tf_op jit(solution)/shard_map/feed_forward_products/pallas_call | solution.py:834
  471.6 13.4 %fusion.9 = bf16[768,2560]{1,0:T(8,128)(2,1)} fusion(bf16[768,1920]{1,0:T(8,128)(2,1)} %get-tuple-element.85.hidden, bf16[2560,5760]{1,0:T(8,128)(2,1)} %all-gather.6.cloned.1.call-done.weights), kind=kOutput, calls=%fused_computation.10 | convolution fusion | flops 7551713280 | bytes 16711680 | tf_op jit(solution)/shard_map/dot_general | solution.py:62
  485.2 1.9 collective-permute-start.5
  487.1 2.8 multiply_reduce_fusion.2
  489.9 3.1 fusion.40
  492.9 6.7 fusion.2.grad_mixed
  499.8 12.8 %mixer_backward_scan.1 = (bf16[192,2560]{1,0:T(8,128)(2,1)S(1)}, f32[192,2560]{1,0:T(8,128)S(1)}, f32[192,2560]{1,0:T(8,128)S(1)}, f32[8,2560]{1,0:T(8,128)S(1)}) custom-call(f32[192,2560]{1,0:T(8,128)S(1)} %fusion.2.grad_mixed, f32[192,2560]{1,0:T(8,128)S(1)} %copy-done.8, f32[192,2560]{1,0:T(8,128)S(1)} %copy-done.7, ...), custom_call_target="tpu_custom_call" | custom-call | flops 1 | bytes 1 | tf_op jit(solution)/shard_map/mixer_backward_scan/pallas_call | solution.py:1218
  512.6 14.8 %collective-permute-done.4 = bf16[160,5760]{1,0:T(8,128)(2,1)S(1)} collective-permute-done((bf16[160,5760]{1,0:T(8,128)(2,1)}, bf16[160,5760]{1,0:T(8,128)(2,1)S(1)}, u32[]{:S(2)}, u32[]{:S(2)}) %collective-permute-start.4) | collective-permute-done | bytes 1843232 | tf_op jit(solution)/shard_map/ppermute | solution.py:1145
  527.5 9.4 %all-gather.3 = f32[8,2,2560]{2,1,0:T(2,128)S(1)} all-gather(f32[1,2,2560]{2,1,0:T(2,128)S(1)} %fusion.34), channel_id=3, replica_groups=mesh['seq'=8,'fsdp'=4] {'seq'}, dimensions={0}, use_global_device_ids=true | all-gather | bytes 184320 | tf_op jit(solution)/shard_map/all_gather | solution.py:29
  537.4 11.3 %mixer_backward.1 = (f32[192,2560]{1,0:T(8,128)S(1)}, f32[8,2560]{1,0:T(8,128)S(1)}, bf16[2560,256]{1,0:T(8,128)(2,1)S(1)}, bf16[2560,256]{1,0:T(8,128)(2,1)S(1)}, f32[8,2560]{1,0:T(8,128)S(1)}) custom-call(f32[192,2560]{1,0:T(8,128)S(1)} %get-tuple-element.90.rev_cum, f32[192,2560]{1,0:T(8,128)S(1)} %get-tuple-element.91.rev_grad, ...), custom_call_target="tpu_custom_call" | custom-call | flops 1 | bytes 1 | tf_op jit(solution)/shard_map/mixer_backward/pallas_call | solution.py:1218
  549.8 1.3 copy-done.16
  551.1 1.3 collective-permute-start.8
  554.7 1.7 slice.392
  556.4 1.6 collective-permute-start.12
  558.9 1.5 pad_maximum_fusion.refs_4_.grad_both
  561.5 1.7 copy-done.22
  563.2 1.3 dynamic-slice_bitcast_fusion
  565.4 23.5 %mixer_products.1 = bf16[1280,7680]{1,0:T(8,128)(2,1)} custom-call(s32[5]{0:T(128)} %stack.59.place, bf16[192,2560]{1,0:T(8,128)(2,1)} %fusion.19.refs_0_, bf16[192,2560]{1,0:T(8,128)(2,1)} %collective-permute-done.6.refs_1_, bf16[192,2560]{1,0:T(8,128)(2,1)} %copy-done.31, bf16[192,2560]{1,0:T(8,128)(2,1)} %collective-permute-done.7.refs_3_, ...), custom_call_target="tpu_custom_call" | custom-call | flops 1 | bytes 1 | tf_op jit(solution)/shard_map/mixer_products/pallas_call | solution.py:682
  588.9 2.5 fusion.29
  591.4 1.9 fusion.16
  593.5 1.4 pad_maximum_fusion.1.rest
  594.9 4.2 collective-permute-done.12
  599.1 8.2 %collective-permute-done.13 = bf16[160,5760]{1,0:T(8,128)(2,1)} collective-permute-done((bf16[160,5760]{1,0:T(8,128)(2,1)}, bf16[160,5760]{1,0:T(8,128)(2,1)}, u32[]{:S(2)}, u32[]{:S(2)}) %collective-permute-start.13) | collective-permute-done | bytes 1843232 | tf_op jit(solution)/shard_map/ppermute | solution.py:1149
  607.3 5.3 add_convert_fusion
  613.3 178.5 %scatter_gradients.1 = (bf16[80,8320]{1,0:T(8,128)(2,1)}, bf16[3,80,7680]{2,1,0:T(8,128)(2,1)}, bf16[192,2560]{1,0:T(8,128)(2,1)}) custom-call(bf16[4,320,7680]{2,1,0:T(8,128)(2,1)} %bitcast.65, bf16[4,320,640]{2,1,0:T(8,128)(2,1)} %pad_maximum_fusion.1.rest, bf16[160,5760]{1,0:T(8,128)(2,1)} %get-tuple-element.267.mlp_low, ...), custom_call_target="tpu_custom_call" | custom-call | tf_op jit(solution)/shard_map/scatter_gradients/pallas_call | solution.py:1094
  791.9 3.0 multiply_reduce_fusion.4
  796.7 3.0 multiply_reduce_fusion
  799.8 1.6 bitcast_convert_fusion
  (170 shorter events, 21.9 us)
Async XLA Ops:
  7.2 346.9 %all-gather.6.cloned.1.call-start = ((), (), s32[]{:S(2)}) async-start(), calls=%async_computation.2 | async-start | bytes 33177600 | tf_op jit(solution)/shard_map/all_gather | solution.py:1275
  194.0 291.0 %reduce-scatter.3.cloned.1.call-start = ((), (), s32[]{:S(2)}) async-start(), calls=%async_computation.3 | async-start | bytes 4915200 | tf_op jit(solution)/shard_map/reduce_scatter | solution.py:1341
  194.1 76.2 %collective-permute-start.1 = (bf16[192,2560]{1,0:T(8,128)(2,1)}, bf16[192,2560]{1,0:T(8,128)(2,1)}, u32[]{:S(2)}, u32[]{:S(2)}) collective-permute-start(bf16[192,2560]{1,0:T(8,128)(2,1)} %bitcast.13.grad0), channel_id=1, source_target_pairs={{0,1},{1,2},{2,3},{3,0},{4,5},{5,6},{6,7},{7,4},{8,9},{9,10},{10,1... | collective-permute-start | bytes 2949128 | tf_op jit(solution)/shard_map/ppermute | solution.py:1135
  199.5 70.7 %collective-permute-start.2 = (bf16[192,2560]{1,0:T(8,128)(2,1)}, bf16[192,2560]{1,0:T(8,128)(2,1)}, u32[]{:S(2)}, u32[]{:S(2)}) collective-permute-start(bf16[192,2560]{1,0:T(8,128)(2,1)} %bitcast.13.grad0), channel_id=1, source_target_pairs={{0,2},{1,3},{2,0},{3,1},{4,6},{5,7},{6,4},{7,5},{8,10},{9,11},{10,... | collective-permute-start | bytes 2949128 | tf_op jit(solution)/shard_map/ppermute | solution.py:1135
  202.9 67.4 %collective-permute-start.3 = (bf16[192,2560]{1,0:T(8,128)(2,1)}, bf16[192,2560]{1,0:T(8,128)(2,1)}, u32[]{:S(2)}, u32[]{:S(2)}) collective-permute-start(bf16[192,2560]{1,0:T(8,128)(2,1)} %bitcast.13.grad0), channel_id=1, source_target_pairs={{0,3},{1,0},{2,1},{3,2},{4,7},{5,4},{6,5},{7,6},{8,11},{9,8},{10,9... | collective-permute-start | bytes 2949128 | tf_op jit(solution)/shard_map/ppermute | solution.py:1135
  225.4 8.1 %collective-permute-start = (bf16[3,2560]{1,0:T(4,128)(2,1)S(1)}, bf16[3,2560]{1,0:T(4,128)(2,1)S(1)}, u32[]{:S(2)}, u32[]{:S(2)}) collective-permute-start(bf16[3,2560]{1,0:T(4,128)(2,1)S(1)} %slice.271), channel_id=1, source_target_pairs={{0,4},{4,8},{8,12},{12,16},{16,20},{20,24},{24,28},{1,5},{5,9},{9,... | collective-permute-start | bytes 46088 | tf_op jit(solution)/shard_map/ppermute | solution.py:23
  236.1 19.4 %copy-start.41 = (f32[192,5120]{1,0:T(8,128)S(1)}, f32[192,5120]{1,0:T(8,128)}, u32[]{:S(2)}) copy-start(f32[192,5120]{1,0:T(8,128)} %get-tuple-element.263) | copy-start | bytes 11796484
  243.3 14.1 %copy-start.1 = (f32[192,2560]{1,0:T(8,128)}, f32[192,2560]{1,0:T(8,128)S(1)}, u32[]{:S(2)}) copy-start(f32[192,2560]{1,0:T(8,128)S(1)} %get-tuple-element.72.local) | copy-start | bytes 5898244
  243.3 14.1 %copy-start.6 = (f32[192,2560]{1,0:T(8,128)}, f32[192,2560]{1,0:T(8,128)S(1)}, u32[]{:S(2)}) copy-start(f32[192,2560]{1,0:T(8,128)S(1)} %get-tuple-element.89.rate_pre) | copy-start | bytes 5898244
  243.4 14.1 %copy-start.9 = (f32[192,2560]{1,0:T(8,128)}, f32[192,2560]{1,0:T(8,128)S(1)}, u32[]{:S(2)}) copy-start(f32[192,2560]{1,0:T(8,128)S(1)} %get-tuple-element.99.input_pre) | copy-start | bytes 5898244
  243.4 14.1 %copy-start.14 = (bf16[192,2560]{1,0:T(8,128)(2,1)}, bf16[192,2560]{1,0:T(8,128)(2,1)S(1)}, u32[]{:S(2)}) copy-start(bf16[192,2560]{1,0:T(8,128)(2,1)S(1)} %get-tuple-element.100.conv) | copy-start | bytes 2949124
  243.4 256.3 %copy-start = (f32[192,2560]{1,0:T(8,128)}, f32[192,2560]{1,0:T(8,128)S(1)}, u32[]{:S(2)}) copy-start(f32[192,2560]{1,0:T(8,128)S(1)} %get-tuple-element.73.cum) | copy-start | bytes 5898244
  257.5 10.3 %copy-start.30 = (bf16[192,2560]{1,0:T(8,128)(2,1)}, bf16[192,2560]{1,0:T(8,128)(2,1)S(1)}, u32[]{:S(2)}) copy-start(bf16[192,2560]{1,0:T(8,128)(2,1)S(1)} %get-tuple-element.240.refs_6_) | copy-start | bytes 2949124
  406.1 154.4 %reduce-scatter.5.cloned.1.call-start = ((), (), s32[]{:S(2)}) async-start(), calls=%async_computation.4 | async-start | bytes 4915200 | tf_op jit(solution)/shard_map/reduce_scatter | solution.py:1359
  485.1 4.8 copy-start.20
  485.1 4.8 copy-start.32
  485.1 42.3 %collective-permute-start.4 = (bf16[160,5760]{1,0:T(8,128)(2,1)}, bf16[160,5760]{1,0:T(8,128)(2,1)S(1)}, u32[]{:S(2)}, u32[]{:S(2)}) collective-permute-start(bf16[160,5760]{1,0:T(8,128)(2,1)} %get-tuple-element.94), channel_id=1, source_target_pairs={{0,8},{4,12},{8,0},{12,4},{16,24},{20,28},{24,16},{28,20},{1,9},{5... | collective-permute-start | bytes 5529608 | tf_op jit(solution)/shard_map/ppermute | solution.py:1145
  485.2 42.3 %collective-permute-start.5 = (bf16[160,5760]{1,0:T(8,128)(2,1)}, bf16[160,5760]{1,0:T(8,128)(2,1)S(1)}, u32[]{:S(2)}, u32[]{:S(2)}) collective-permute-start(bf16[160,5760]{1,0:T(8,128)(2,1)} %get-tuple-element.95), channel_id=1, source_target_pairs={{0,16},{4,20},{8,24},{12,28},{16,0},{20,4},{24,8},{28,12},{1,17},{... | collective-permute-start | bytes 5529608 | tf_op jit(solution)/shard_map/ppermute | solution.py:1149
  492.9 6.7 copy-start.31
  492.9 6.7 copy-start.46
  492.9 6.8 copy-start.7
  492.9 6.8 copy-start.8
  499.7 27.8 %copy-start.48 = (f32[1,2560]{1,0:T(1,128)S(1)}, f32[1,2560]{1,0:T(1,128)}, u32[]{:S(2)}) copy-start(f32[1,2560]{1,0:T(1,128)} %copy-done.47) | copy-start | bytes 30724
  499.7 37.7 %copy-start.3 = (bf16[2560,256]{1,0:T(8,128)(2,1)S(1)}, bf16[2560,256]{1,0:T(8,128)(2,1)}, u32[]{:S(2)}) copy-start(bf16[2560,256]{1,0:T(8,128)(2,1)} %get-tuple-element.246.rate_w) | copy-start | bytes 3932164
  499.7 37.7 %copy-start.5 = (bf16[192,2560]{1,0:T(8,128)(2,1)S(1)}, bf16[192,2560]{1,0:T(8,128)(2,1)}, u32[]{:S(2)}) copy-start(bf16[192,2560]{1,0:T(8,128)(2,1)} %slice.270.branch) | copy-start | bytes 2949124
  499.8 37.7 %copy-start.15 = (bf16[192,2560]{1,0:T(8,128)(2,1)S(1)}, bf16[192,2560]{1,0:T(8,128)(2,1)}, u32[]{:S(2)}) copy-start(bf16[192,2560]{1,0:T(8,128)(2,1)} %copy-done.14) | copy-start | bytes 2949124
  512.6 36.1 %copy-start.12 = (bf16[192,2560]{1,0:T(8,128)(2,1)}, bf16[192,2560]{1,0:T(8,128)(2,1)S(1)}, u32[]{:S(2)}) copy-start(bf16[192,2560]{1,0:T(8,128)(2,1)S(1)} %get-tuple-element.106) | copy-start | bytes 2949124
  527.4 21.3 %copy-start.35 = (bf16[160,5760]{1,0:T(8,128)(2,1)}, bf16[160,5760]{1,0:T(8,128)(2,1)S(1)}, u32[]{:S(2)}) copy-start(bf16[160,5760]{1,0:T(8,128)(2,1)S(1)} %collective-permute-done.4) | copy-start | bytes 5529604
  527.5 21.2 %copy-start.37 = (bf16[160,5760]{1,0:T(8,128)(2,1)}, bf16[160,5760]{1,0:T(8,128)(2,1)S(1)}, u32[]{:S(2)}) copy-start(bf16[160,5760]{1,0:T(8,128)(2,1)S(1)} %collective-permute-done.5) | copy-start | bytes 5529604
  551.1 7.8 copy-start.17
  551.1 6.9 collective-permute-start.8
  552.4 12.1 %collective-permute-start.6 = (bf16[192,2560]{1,0:T(8,128)(2,1)}, bf16[192,2560]{1,0:T(8,128)(2,1)}, u32[]{:S(2)}, u32[]{:S(2)}) collective-permute-start(bf16[192,2560]{1,0:T(8,128)(2,1)} %fusion.19.refs_0_), channel_id=1, source_target_pairs={{0,4},{4,0},{8,12},{12,8},{16,20},{20,16},{24,28},{28,24},{1,5},{5... | collective-permute-start | bytes 2949128 | tf_op jit(solution)/shard_map/ppermute | solution.py:1141
  554.2 4.7 copy-start.13
  554.2 10.7 %collective-permute-start.10 = (bf16[192,2560]{1,0:T(8,128)(2,1)}, bf16[192,2560]{1,0:T(8,128)(2,1)}, u32[]{:S(2)}, u32[]{:S(2)}) collective-permute-start(bf16[192,2560]{1,0:T(8,128)(2,1)} %copy-done.30), channel_id=1, source_target_pairs={{0,4},{4,0},{8,12},{12,8},{16,20},{20,16},{24,28},{28,24},{1,5},{5... | collective-permute-start | bytes 2949128 | tf_op jit(solution)/shard_map/ppermute | solution.py:1141
  554.3 11.1 %collective-permute-start.7 = (bf16[192,2560]{1,0:T(8,128)(2,1)}, bf16[192,2560]{1,0:T(8,128)(2,1)}, u32[]{:S(2)}, u32[]{:S(2)}) collective-permute-start(bf16[192,2560]{1,0:T(8,128)(2,1)} %copy-done.31), channel_id=1, source_target_pairs={{0,4},{4,0},{8,12},{12,8},{16,20},{20,16},{24,28},{28,24},{1,5},{5... | collective-permute-start | bytes 2949128 | tf_op jit(solution)/shard_map/ppermute | solution.py:1141
  556.4 42.7 %collective-permute-start.12 = (bf16[160,5760]{1,0:T(8,128)(2,1)}, bf16[160,5760]{1,0:T(8,128)(2,1)}, u32[]{:S(2)}, u32[]{:S(2)}) collective-permute-start(bf16[160,5760]{1,0:T(8,128)(2,1)} %get-tuple-element.111), channel_id=1, source_target_pairs={{0,8},{4,12},{8,0},{12,4},{16,24},{20,28},{24,16},{28,20},{1,9},{5... | collective-permute-start | bytes 5529608 | tf_op jit(solution)/shard_map/ppermute | solution.py:1145
  560.4 4.9 collective-permute-start.9
  560.9 4.2 copy-start.34
  564.5 42.8 %collective-permute-start.13 = (bf16[160,5760]{1,0:T(8,128)(2,1)}, bf16[160,5760]{1,0:T(8,128)(2,1)}, u32[]{:S(2)}, u32[]{:S(2)}) collective-permute-start(bf16[160,5760]{1,0:T(8,128)(2,1)} %get-tuple-element.112), channel_id=1, source_target_pairs={{0,16},{4,20},{8,24},{12,28},{16,0},{20,4},{24,8},{28,12},{1,17},{... | collective-permute-start | bytes 5529608 | tf_op jit(solution)/shard_map/ppermute | solution.py:1149
  564.9 26.5 %collective-permute-start.11 = (bf16[4,320,640]{2,1,0:T(8,128)(2,1)}, bf16[4,320,640]{2,1,0:T(8,128)(2,1)}, u32[]{:S(2)}, u32[]{:S(2)}) collective-permute-start(bf16[4,320,640]{2,1,0:T(8,128)(2,1)} %dynamic-slice_bitcast_fusion), channel_id=1, source_target_pairs={{0,4},{4,0},{8,12},{12,8},{16,20},{20,16},{24,28},{28,24},{1,5},{5... | collective-permute-start | bytes 4915208 | tf_op jit(solution)/shard_map/ppermute | solution.py:1141
  565.4 23.6 %copy-start.21 = (f32[192,2560]{1,0:T(8,128)S(1)}, f32[192,2560]{1,0:T(8,128)}, u32[]{:S(2)}) copy-start(f32[192,2560]{1,0:T(8,128)} %copy-done.19) | copy-start | bytes 5898244
  593.3 14.0 %copy-start.38 = (bf16[160,5760]{1,0:T(8,128)(2,1)S(1)}, bf16[160,5760]{1,0:T(8,128)(2,1)}, u32[]{:S(2)}) copy-start(bf16[160,5760]{1,0:T(8,128)(2,1)} %copy-done.37) | copy-start | bytes 5529604
  593.5 13.8 %copy-start.36 = (bf16[160,5760]{1,0:T(8,128)(2,1)S(1)}, bf16[160,5760]{1,0:T(8,128)(2,1)}, u32[]{:S(2)}) copy-start(bf16[160,5760]{1,0:T(8,128)(2,1)} %copy-done.35) | copy-start | bytes 5529604
  613.3 178.6 %copy-start.39 = (bf16[80,2560]{1,0:T(8,128)(2,1)S(1)}, bf16[80,2560]{1,0:T(8,128)(2,1)}, u32[]{:S(2)}) copy-start(bf16[80,2560]{1,0:T(8,128)(2,1)} %branch.1) | copy-start | bytes 1228804
  613.3 178.6 %copy-start.40 = (bf16[80,2560]{1,0:T(8,128)(2,1)S(1)}, bf16[80,2560]{1,0:T(8,128)(2,1)}, u32[]{:S(2)}) copy-start(bf16[80,2560]{1,0:T(8,128)(2,1)} %gelu.1) | copy-start | bytes 1228804
  799.7 3.7 copy-start.49
  799.8 4.3 copy-start.50
  799.8 4.8 copy-start.42
  (20 other events, 38.2 us)
Sparse Core Ops, SparseCore 0:
  194.1 149.8 all-gather.5
  406.3 70.8 reduce-scatter.2
  485.2 69.7 reduce-scatter.4

commit v11 on v10

--- a/solution.py
+++ b/solution.py
@@ -592,114 +592,6 @@
     )(normed, grad_out, weights)
 
 
-def products_kernel(sides, cuts, chips, spots, place, *refs):
-    lefts = 1 + max(side for side, _ in sides)
-    left_refs = refs[: 2 * lefts]
-    right_refs = refs[2 * lefts : 2 * lefts + 2 * len(sides)]
-    outs = refs[2 * lefts + 2 * len(sides) : -4]
-    turned, slots, stage, sems = refs[-4:]
-    tok = left_refs[0].shape[0]
-    chip_cols = left_refs[0].shape[1] // 4
-    half = chip_cols // 2
-    step = pl.program_id(0)
-
-    def load(side, q, who):
-        cols = pl.ds(pl.multiple_of(place[chips[q]] * chip_cols, 128), chip_cols)
-        return pltpu.make_async_copy(
-            left_refs[2 * side + who].at[:, cols], slots.at[q % 2, who], sems.at[q % 2, who]
-        )
-
-    def fetch(side):
-        for q in range(min(2, len(chips))):
-            for who in range(2):
-                load(side, q, who).start()
-
-    def turn(side):
-        piece = half // 2
-        for q in range(len(chips)):
-            for who in range(2):
-                load(side, q, who).wait()
-                stage[...] = slots[q % 2, who].T
-                for part in range(2):
-                    spot = spots[2 * q + part] * piece
-                    turned[who, spot : spot + piece, :] = stage[
-                        pl.ds(pl.multiple_of(place[4] * half + part * piece, 16), piece), :
-                    ]
-                if q + 2 < len(chips):
-                    load(side, q + 2, who).start()
-
-    def multiply(own, other):
-        def tile(cols):
-            block = mm(turned[0], own[:, cols], ((1,), (0,)))
-            block = (block + mm(turned[1], other[:, cols], ((1,), (0,)))).astype(bf16)
-            start = 0
-            for out, size in zip(outs, cuts):
-                out[:, cols] = block[start : start + size]
-                start += size
-
-        width = own.shape[1]
-
-        def one(turn, carry):
-            tile(pl.ds(pl.multiple_of(turn * 512, 512), 512))
-            return carry
-
-        lax.fori_loop(0, width // 512, one, 0)
-        if width % 512:
-            tile(slice(width // 512 * 512, width))
-
-    first = 0
-    before = None
-    for n, (side, blocks) in enumerate(sides):
-        if side != before:
-            if first == 0:
-                pl.when(step == 0)(functools.partial(fetch, side))
-            pl.when(step == first)(functools.partial(turn, side))
-        before = side
-        inside = (step >= first) & (step < first + blocks)
-        pl.when(inside)(functools.partial(multiply, right_refs[2 * n], right_refs[2 * n + 1]))
-        first += blocks
-        if n + 1 < len(sides) and sides[n + 1][0] != side:
-            pl.when(step == first - 1)(functools.partial(fetch, sides[n + 1][0]))
-
-
-def products(lefts, rights, cuts, chips, spots, width, name):
-    seq = lax.axis_index("seq")
-    core, x, y = seq % 2, (seq // 2) % 2, seq // 4
-    place = jnp.stack([(1 - y) * 2 + 1 - x, y * 2 + 1 - x, (1 - y) * 2 + x, y * 2 + x, core]).astype(jnp.int32)
-    tok, model = lefts[0][0].shape
-    sides = tuple((side, own.shape[1] // width) for side, own, _ in rights)
-    total = sum(blocks for _, blocks in sides)
-    in_specs = [pl.BlockSpec(memory_space=pl.ANY)] * (2 * len(lefts))
-    first = 0
-    for _, blocks in sides:
-
-        def index(j, place, first=first, blocks=blocks):
-            return (0, jnp.clip(j - first, 0, blocks - 1))
-
-        in_specs += [pl.BlockSpec((tok, width), index)] * 2
-        first += blocks
-    half = model // 8
-    return pl.pallas_call(
-        functools.partial(products_kernel, sides, cuts, chips, spots),
-        grid_spec=pltpu.PrefetchScalarGridSpec(
-            num_scalar_prefetch=1,
-            grid=(total,),
-            in_specs=in_specs,
-            out_specs=[pl.BlockSpec((rows, width), lambda j, place: (0, j)) for rows in cuts],
-            scratch_shapes=[
-                pltpu.VMEM((2, len(chips) * half, tok), bf16),
-                pltpu.VMEM((2, 2, tok, 2 * half), bf16),
-                pltpu.VMEM((2 * half, tok), bf16),
-                pltpu.SemaphoreType.DMA((2, 2)),
-            ],
-        ),
-        out_shape=[jax.ShapeDtypeStruct((rows, total * width), bf16) for rows in cuts],
-        compiler_params=pltpu.CompilerParams(vmem_limit_bytes=58 * 1024 * 1024),
-        cost_estimate=pl.CostEstimate(flops=1, bytes_accessed=1, transcendentals=0),
-        name=name,
-    )(place, *[a for pair in lefts for a in pair], *[a for _, own, other in rights for a in (own, other)])
-
-
 def add_columns(target, sources, start, size, step):
     def one(turn, carry):
         cols = pl.ds(pl.multiple_of(start + turn * step, 128), step)
@@ -713,9 +605,10 @@
 
 
 def shared_products_kernel(
-    normed, normed_other, grad, grad_other, pair, pair_other, hidden, hidden_other,
-    beside_high, across_low, mine, beside_low, across_high,
-    turned, slots, stage, diag, landed, waiting, load_sem, send_sem, recv_sem, store_sem,
+    normed, normed_other, grad, grad_other, weights, pair, pair_other, hidden, hidden_other,
+    beside_high, across_low, mine, beside_low, across_high, out,
+    turned, slots, stage, diag, landed, waiting, down_now, out_now,
+    load_sem, send_sem, recv_sem, store_sem, down_sem, out_sem,
 ):
     s, z, _, beside, across = places()
     step = pl.program_id(0)
@@ -788,13 +681,40 @@
             waiting.at[way, :, cols], (beside_low, across_high)[way].at[:, cols], store_sem.at[way, j]
         )
 
+    out_rows = down_now.shape[1]
+    out_tiles = weights.shape[0] // out_rows
+
+    def down(t):
+        source = weights.at[pl.ds(t * out_rows, out_rows), pl.ds(2 * width, width)]
+        return pltpu.make_async_copy(source, down_now.at[t % 2], down_sem.at[t % 2])
+
+    def out_store(t):
+        return pltpu.make_async_copy(
+            out_now.at[t % 2], out.at[:, pl.ds(t * out_rows, out_rows)], out_sem.at[t % 2]
+        )
+
+    def out_product():
+        for t in range(out_tiles):
+            down(t).wait()
+            if t > 1:
+                out_store(t - 2).wait()
+            out_now[t % 2] = mm(hidden[...], down_now[t % 2], ((1,), (1,))).astype(bf16)
+            out_store(t).start()
+            if t + 2 < out_tiles:
+                down(t + 2).start()
+
     @pl.when(step == 0)
     def _():
         fetch(0)
         greet([(beside, z), (across, z)])
         turn(0)
 
-    pl.when(step == 2)(functools.partial(turn, 1))
+    @pl.when(step == 2)
+    def _():
+        down(0).start()
+        down(1).start()
+        turn(1)
+
     pl.when(step < 2)(functools.partial(multiply, pair, pair_other))
     pl.when(step == 1)(functools.partial(fetch, 1))
     pl.when(step == 2)(functools.partial(multiply, hidden, hidden_other))
@@ -807,6 +727,7 @@
 
     @pl.when(step == 2)
     def _():
+        out_product()
         for j in range(3):
             for way in range(2):
                 push(way, j).wait_recv()
@@ -816,9 +737,11 @@
             for way in range(2):
                 push(way, j).wait_send()
                 store(way, j).wait()
-
-
-def shared_products(lefts, pair, hidden):
+        for t in range(out_tiles - 2, out_tiles):
+            out_store(t).wait()
+
+
+def shared_products(lefts, weights, pair, hidden):
     tok, model = lefts[0].shape
     width = hidden[0].shape[1]
     half = model // 8
@@ -834,9 +757,10 @@
     return pl.pallas_call(
         shared_products_kernel,
         grid=(3,),
-        in_specs=[anyspec] * 4 + [pair_spec] * 2 + [hidden_spec] * 2,
-        out_specs=[block(rows) for rows in rows_out[:3]] + [anyspec] * 2,
-        out_shape=[jax.ShapeDtypeStruct((rows, 3 * width), bf16) for rows in rows_out],
+        in_specs=[anyspec] * 5 + [pair_spec] * 2 + [hidden_spec] * 2,
+        out_specs=[block(rows) for rows in rows_out[:3]] + [anyspec] * 3,
+        out_shape=[jax.ShapeDtypeStruct((rows, 3 * width), bf16) for rows in rows_out]
+        + [jax.ShapeDtypeStruct((tok, model), bf16)],
         scratch_shapes=[
             pltpu.VMEM((2, 4 * half, tok), bf16),
             pltpu.VMEM((2, 2, tok, 2 * half), bf16),
@@ -844,27 +768,34 @@
             pltpu.VMEM((2, half // 2, 3 * width), bf16),
             pltpu.VMEM((2, half // 2, 3 * width), bf16),
             pltpu.VMEM((2, half // 2, 3 * width), bf16),
-            dma((2, 2)), dma((2, 3)), dma((2, 3)), dma((2, 3)),
+            pltpu.VMEM((2, 512, width), bf16),
+            pltpu.VMEM((2, tok, 512), bf16),
+            dma((2, 2)), dma((2, 3)), dma((2, 3)), dma((2, 3)), dma((2,)), dma((2,)),
         ],
         compiler_params=pltpu.CompilerParams(
             collective_id=5, has_side_effects=True, vmem_limit_bytes=60 * 1024 * 1024
         ),
         name="feed_forward_products",
-    )(*lefts, *pair, *hidden)
+    )(*lefts, weights, *pair, *hidden)
 
 
 def scatter_kernel(
-    main, rest, mlp_low, mlp_high, grad_both, mixer_w, tokens, grad_middle, gain, mixer_sum, mlp_back, input_grad,
-    held, cross, near, lined, both_now, wide_now, back_now, tokens_now, middle_now, gain_now, wide_sem,
-    load_sem, flow_send, flow_recv, line_send, line_recv, swap_send, swap_recv, own_sem,
+    normed, grad_mix, grad_both, mixed, rest, mlp_low, mlp_high, mixer_w, tokens, gain, mixer_sum, mlp_back, input_grad,
+    held, cross, near, lined, left_now, both_now, mixed_now, turned, stage, rest_other, back_now, wide_now, gain_now,
+    load_sem, core_send, core_recv, wide_sem,
+    flow_send, flow_recv, line_send, line_recv, swap_send, swap_recv, own_sem,
 ):
-    s, z, _, beside, across = places()
+    s, z, core, beside, across = places()
     chip_diag, chip_beside, chip_across, chip = 0, 1, 2, 3
+    chips = [q // 2 for q in (beside + across - s, beside, across, s)]
     rows = held.shape[1] // 4
     cols = held.shape[2]
     cut = cols // 256 * 128
     ff_part = mlp_low.shape[1] // 3
-    parts = (main, rest)
+    tok, model = tokens.shape
+    half = 4 * rows
+    lru2 = grad_both.shape[1]
+    rest_start = lru2 + mixed.shape[1]
     order = (3 * (1 - z // 2), (2 + 3 * z) % 5, 1 + z % 2, z)
 
     def remote(src, dst, send, recv, target):
@@ -875,17 +806,56 @@
     def span(k):
         return pl.ds(pl.multiple_of(k * rows, 16), rows)
 
-    def loads(i):
-        copies, start = [], 0
-        for n, part in enumerate(parts):
-            size = part.shape[2]
-            copies.append(
-                pltpu.make_async_copy(
-                    part.at[:, span(order[i]), :], held.at[:, span(order[i]), pl.ds(start, size)], load_sem.at[i, n]
-                )
-            )
-            start += size
-        return copies
+    shared = (
+        (normed, left_now.at[0]), (grad_both, both_now), (grad_mix, left_now.at[1]), (mixed, mixed_now),
+    )
+    loads = [
+        pltpu.make_async_copy(source, target.at[pl.ds(0, tok), :], load_sem.at[n])
+        for n, (source, target) in enumerate(shared)
+    ]
+    pushes = [
+        (source, target.at[pl.ds(tok, tok), :]) for source, target in shared
+    ]
+
+    def push(n):
+        if n < 4:
+            source, target = pushes[n]
+        else:
+            source = rest.at[pl.ds(pl.multiple_of(chips[n - 4] * 2 * half + (1 - s % 2) * half, 16), half), :]
+            target = rest_other.at[n - 4]
+        return pltpu.make_async_remote_copy(
+            src_ref=source,
+            dst_ref=target,
+            send_sem=core_send.at[n],
+            recv_sem=core_recv.at[n],
+            device_id=(core, z),
+            device_id_type=MESH,
+        )
+
+    def rest_load(q):
+        source = rest.at[pl.ds(pl.multiple_of(chips[q] * 2 * half + s % 2 * half, 16), half), :]
+        return pltpu.make_async_copy(
+            source, held.at[q, :, pl.ds(rest_start, cols - rest_start)], load_sem.at[4 + q]
+        )
+
+    def turn(side):
+        for q in range(4):
+            source = left_now[side, :, pl.ds(pl.multiple_of(chips[q] * 2 * half, 128), 2 * half)]
+            stage[...] = source.T
+            turned[side, q * half : (q + 1) * half, :] = stage[
+                pl.ds(pl.multiple_of(s % 2 * half, 16), half), :
+            ]
+
+    def multiply(q):
+        for side, right, start in ((0, both_now, 0), (1, mixed_now, lru2)):
+
+            def one(turn, carry, side=side, right=right, start=start):
+                here = pl.multiple_of(turn * 512, 512)
+                block = mm(turned[side, q * half : (q + 1) * half, :], right[:, pl.ds(here, 512)], ((1,), (0,)))
+                held[q, :, pl.ds(pl.multiple_of(start + here, 512), 512)] = block.astype(bf16)
+                return carry
+
+            lax.fori_loop(0, right.shape[1] // 512, one, 0)
 
     left, right = pl.ds(0, cut), pl.ds(cut, cols - cut)
 
@@ -988,37 +958,44 @@
             for m in range(3)
         ]
 
-    wide_rows = wide_now.shape[1]
-    wide_start = mixer_w.shape[1] - wide_now.shape[2] - tokens.shape[1]
+    wide_rows = wide_now.shape[0]
+    wide_tiles = mixer_w.shape[0] // wide_rows
+    wide_start = mixer_w.shape[1] - lru2 - model
+    wide_slots = (both_now.at[pl.ds(tok, wide_rows), :], wide_now)
 
     def wide(j):
-        source = mixer_w.at[pl.ds(j * wide_rows, wide_rows), pl.ds(wide_start, wide_now.shape[2])]
-        return pltpu.make_async_copy(source, wide_now.at[j % 2], wide_sem.at[j % 2])
+        source = mixer_w.at[pl.ds(j * wide_rows, wide_rows), pl.ds(wide_start, lru2)]
+        return pltpu.make_async_copy(source, wide_slots[j % 2], wide_sem.at[j % 2])
 
     plain_loads = [
-        pltpu.make_async_copy(source, target, wide_sem.at[2 + n])
-        for n, (source, target) in enumerate(
-            ((grad_both, both_now), (tokens, tokens_now), (grad_middle, middle_now), (gain, gain_now))
-        )
+        pltpu.make_async_copy(tokens, left_now.at[0, pl.ds(0, tok), :], wide_sem.at[2]),
+        pltpu.make_async_copy(gain, gain_now, wide_sem.at[3]),
     ]
 
     def back(first, last):
         for j in range(first, last):
             wide(j).wait()
-            back_now[:, pl.ds(j * wide_rows, wide_rows)] = mm(both_now[...], wide_now[j % 2], ((1,), (1,)))
-            if (j + 2) * wide_rows < mixer_w.shape[0]:
+            back_now[:, pl.ds(j * wide_rows, wide_rows)] = mm(
+                both_now[0:tok, :], wide_slots[j % 2][...], ((1,), (1,))
+            )
+            if j + 2 < wide_tiles:
                 wide(j + 2).start()
 
     def finish_rows(turn, carry):
-        rows = pl.ds(pl.multiple_of(turn * 16, 16), 16)
-        result = middle_now[rows, :] + norm_back(tokens_now[rows, :].astype(f32), gain_now[0:1, :], back_now[rows, :])
-        tokens_now[rows, :] = result.astype(bf16)
+        at = pl.ds(pl.multiple_of(turn * 16, 16), 16)
+        result = left_now[1, at, :].astype(f32) + norm_back(
+            left_now[0, at, :].astype(f32), gain_now[0:1, :], back_now[at, :]
+        )
+        left_now[0, at, :] = result.astype(bf16)
         return carry
 
-    for i in range(4):
-        for copy in loads(i):
-            copy.start()
-    greet([(beside, z), (across, z)] + [(s, (z + k) % 4) for k in range(1, 4)])
+    for copy in loads:
+        copy.start()
+    for q in range(4):
+        rest_load(q).start()
+    greet([(core, z), (beside, z), (across, z)] + [(s, (z + k) % 4) for k in range(1, 4)])
+    for n in range(8):
+        push(n).start()
     for k in (1, 3, 2):
         swap_start(k)
 
@@ -1032,40 +1009,47 @@
         for copy in own(True):
             copy.start()
 
+    for n in (0, 1):
+        loads[n].wait()
+        push(n).wait_recv()
+    turn(0)
+    for n in (2, 3):
+        loads[n].wait()
+        push(n).wait_recv()
+    turn(1)
+    multiply(chip_diag)
+    for q in range(4):
+        rest_load(q).wait()
+        push(4 + q).wait_recv()
+        held[q, :, rest_start:] = add_low(held[q, :, rest_start:], rest_other[q])
     for i in range(2):
-        for copy in loads(i):
-            copy.wait()
         flow(i, 0).start()
         flow(i, 1).start()
-        if i == 0:
-            flow(i, 2).start()
-            flow(i, 4).start()
+    multiply(chip_beside)
+    flow(0, 2).start()
+    multiply(chip_across)
+    flow(0, 4).start()
+    multiply(chip)
+    for copy in plain_loads:
+        copy.start()
+    wide(0).start()
+    wide(1).start()
     for i in range(4):
         cross_step(i)
         if i + 1 < 4:
             flow(i + 1, 2).start()
             flow(i + 1, 4).start()
         if i + 2 < 4:
-            for copy in loads(i + 2):
-                copy.wait()
             flow(i + 2, 0).start()
             flow(i + 2, 1).start()
-        if i == 0:
-            for copy in plain_loads:
-                copy.start()
-            wide(0).start()
-            wide(1).start()
         if i > 0:
             near_step(i - 1)
             chain(i - 1)
-        if i == 1:
-            for copy in plain_loads:
-                copy.wait()
-        if i > 0:
-            back(3 * i - 3, 3 * i)
-    back(9, mixer_w.shape[0] // wide_rows)
-    lax.fori_loop(0, tokens.shape[0] // 16, finish_rows, 0)
-    finished = pltpu.make_async_copy(tokens_now, input_grad, wide_sem.at[2])
+            back(wide_tiles * (i - 1) // 3, wide_tiles * i // 3)
+    for copy in plain_loads:
+        copy.wait()
+    lax.fori_loop(0, tok // 16, finish_rows, 0)
+    finished = pltpu.make_async_copy(left_now.at[0, pl.ds(0, tok), :], input_grad, wide_sem.at[2])
     finished.start()
     near_step(3)
     chain(3)
@@ -1080,20 +1064,22 @@
             copy.wait()
     for copy in own():
         copy.wait()
+    for n in range(8):
+        push(n).wait_send()
     finished.wait()
     done.wait()
 
 
-def scatter(main, rest, mlp_low, mlp_high, grad_both, mixer_w, tokens, grad_middle, gain):
-    rows = main.shape[1] // 4
-    cols = main.shape[2] + rest.shape[2]
+def scatter(normed, grad_mix, grad_both, mixed, rest, mlp_low, mlp_high, mixer_w, tokens, gain):
+    tok, model = tokens.shape
+    rows = model // 32
+    cols = grad_both.shape[1] + mixed.shape[1] + rest.shape[1]
     ff_part = mlp_low.shape[1] // 3
-    tok, model = tokens.shape
     anyspec = pl.BlockSpec(memory_space=pl.ANY)
     dma = pltpu.SemaphoreType.DMA
     return pl.pallas_call(
         scatter_kernel,
-        in_specs=[anyspec] * 9,
+        in_specs=[anyspec] * 10,
         out_specs=[anyspec] * 3,
         out_shape=[
             jax.ShapeDtypeStruct((rows, cols), bf16),
@@ -1105,20 +1091,23 @@
             pltpu.VMEM((4, rows, cols), bf16),
             pltpu.VMEM((2, 4, rows, cols), bf16),
             pltpu.VMEM((5, rows, cols), bf16),
-            pltpu.VMEM(grad_both.shape, bf16),
-            pltpu.VMEM((2, 256, grad_both.shape[1]), bf16),
+            pltpu.VMEM((2, 2 * tok, model), bf16),
+            pltpu.VMEM((2 * tok, grad_both.shape[1]), bf16),
+            pltpu.VMEM((2 * tok, mixed.shape[1]), bf16),
+            pltpu.VMEM((2, 16 * rows, 2 * tok), bf16),
+            pltpu.VMEM((8 * rows, 2 * tok), bf16),
+            pltpu.VMEM((4, 4 * rows, rest.shape[1]), bf16),
             pltpu.VMEM((tok, model), f32),
-            pltpu.VMEM((tok, model), bf16),
-            pltpu.VMEM((tok, model), f32),
+            pltpu.VMEM((128, grad_both.shape[1]), bf16),
             pltpu.VMEM((8, model), f32),
-            dma((6,)),
-            dma((4, 2)), dma((4, 6)), dma((4, 6)), dma((4,)), dma((5,)), dma((3, 3)), dma((3, 3)), dma((4,)),
+            dma((8,)), dma((8,)), dma((8,)), dma((4,)),
+            dma((4, 6)), dma((4, 6)), dma((4,)), dma((5,)), dma((3, 3)), dma((3, 3)), dma((4,)),
         ],
         compiler_params=pltpu.CompilerParams(
             collective_id=2, has_side_effects=True, vmem_limit_bytes=62 * 1024 * 1024
         ),
         name="scatter_gradients",
-    )(main, rest, mlp_low, mlp_high, grad_both, mixer_w, tokens, grad_middle, gain)
+    )(normed, grad_mix, grad_both, mixed, rest, mlp_low, mlp_high, mixer_w, tokens, gain)
 
 
 def gather_plain(mixer, gate, up, down):
@@ -1151,39 +1140,6 @@
 
 def add_low(left, right):
     return (left.astype(f32) + right.astype(f32)).astype(bf16)
-
-
-def scatter_paired(
-    normed, grad_both, grad_mix, mixed, rest, mlp_parts, mixer_w, tokens, grad_middle, gain
-):
-    seq = lax.axis_index("seq")
-    core, x, y = seq % 2, (seq // 2) % 2, seq // 4
-    main = products(
-        [(normed, swap_cores(normed)), (grad_mix, swap_cores(grad_mix))],
-        [(0, grad_both, swap_cores(grad_both)), (1, mixed, swap_cores(mixed))],
-        (normed.shape[1] // 2,),
-        (0, 1, 2, 3),
-        tuple(range(8)),
-        normed.shape[1] // 2,
-        "mixer_products",
-    )[0]
-    grouped = rest.reshape(4, 2, -1, rest.shape[1])
-    own = lax.dynamic_index_in_dim(grouped, core, 1, False)
-    other = swap_cores(lax.dynamic_index_in_dim(grouped, 1 - core, 1, False))
-    rest = (own.astype(f32) + other.astype(f32)).astype(bf16)
-    rest = jnp.concatenate(
-        [
-            lax.dynamic_slice_in_dim(rest, q, 1, 0)
-            for q in ((1 - y) * 2 + 1 - x, y * 2 + 1 - x, (1 - y) * 2 + x, y * 2 + x)
-        ],
-        axis=0,
-    )
-    main, rest, mlp_parts = lax.optimization_barrier((main, rest, mlp_parts))
-    low, high = [sum(part.astype(f32) for part in parts).astype(bf16) for parts in mlp_parts]
-    gain = jnp.broadcast_to(gain[None], (8, gain.shape[0]))
-    return scatter(
-        main.reshape(4, -1, main.shape[1]), rest, low, high, grad_both, mixer_w, tokens, grad_middle, gain
-    )
 
 
 def scatter_plain(normed, grad_both, grad_mix, mixed, rest, mlp_sum):
@@ -1341,13 +1297,13 @@
     grad_normed_two = lax.psum_scatter(grad_normed_part, "fsdp", scatter_dimension=0, tiled=True)
     if custom:
         half = model // 16
-        beside_high, across_low, mine, beside_low, across_high = shared_products(
-            (normed_all, normed_other, grad_out_all, grad_out_other), (grad_pair, pair_other), (hidden, hidden_other)
+        beside_high, across_low, mine, beside_low, across_high, out_part = shared_products(
+            (normed_all, normed_other, grad_out_all, grad_out_other),
+            mlp_w,
+            (grad_pair, pair_other),
+            (hidden, hidden_other),
         )
         from_beside_high, from_across_low = swap_beside(beside_high), swap_across(across_low)
-        hidden = lax.optimization_barrier((hidden, mine))[0]
-        out_part = mm(hidden, w_down, ((1,), (1,))).astype(bf16)
-        out_part, grad_normed_two = lax.optimization_barrier((out_part, grad_normed_two))
     else:
         grad_pair = jnp.concatenate([grad_gate, grad_up], axis=1)
         term_pair = mm(normed_all, grad_pair, ((0,), (0,))).astype(bf16)
@@ -1408,8 +1364,10 @@
             (mine[:half], from_across_low, from_beside_low),
             (mine[half:], from_across_high, from_beside_high),
         )
-        mixer_sum, mlp_back, input_grad = scatter_paired(
-            normed, grad_both, grad_mix, mixed, rest, mlp_parts, mixer_w, block_input[0], grad_middle, gain_one
+        low, high = [sum(part.astype(f32) for part in parts).astype(bf16) for parts in mlp_parts]
+        gain_rows = jnp.broadcast_to(gain_one[None], (8, model))
+        mixer_sum, mlp_back, input_grad = scatter(
+            normed, grad_mix, grad_both, mixed, rest, low, high, mixer_w, block_input[0], gain_rows
         )
     else:
         mixer_sum, mlp_back = scatter_plain(normed, grad_both, grad_mix, mixed, rest, mlp_sum)

time: 821 us -> 828 us (level)
  waiting for transfers between devices: 27.4 us -> 62.1 us
  matrix products: 45.4 us -> 32.8 us
    ppermute x2, waiting for transfers between devices: 8.29 us -> 32.1 us  [swap_across(): return lax.ppermute(shard, 'seq', [(i, i ^ 4) for i in range(8)])]
    reduce_scatter x1, waiting for transfers between devices: 0.01 us -> 13.9 us  [on_device(): lax.psum_scatter(out_part, 'fsdp', scatter_dimension=0, tiled=True)]
    dot_general x4 -> x3, matrix products: 45.4 us -> 32.8 us  [mm(): lax.dot_general(left, right, (dims, ((), ())), preferred_element_type=f32)]
    pallas_call x3 -> x2, Pallas kernels: 268 us -> 259 us  [the longest x1 193 us: scatter(): pl.pallas_call(scatter_kernel, in_specs=[anyspec] * 10, out_specs=[anyspe...]
  transfers between devices with their start and end apart: 17 -> 12, of which waited for: 4 -> 6; matrix products, arithmetic and copies ran while one was open for 10% -> 7% of each run, Pallas kernels for 25% -> 22%
where the time goes in v11:
time: 828 us; the launch traced here: 818 us
  Pallas kernels  610 us (74%)
  waiting for transfers between devices  62.1 us (8%)
  other arithmetic  33.6 us (4%)
  matrix products  32.8 us (4%)
  local copies, waits for them, and re-layouts  27.9 us (3%)
  blocking collectives  20.7 us (2%)
  starting transfers between devices  17.2 us (2%)
  between operations  14.7 us (2%)
    pallas_call x1, Pallas kernels, scatter(): pl.pallas_call(scatter_kernel, in_specs=[anyspec] * 10, out_specs=[anyspe...  193 us
    pallas_call x1, Pallas kernels, gather(): pl.pallas_call(gather_kernel, in_specs=[anyspec] * 7, out_specs=[anyspec]...  183 us
    pallas_call x1, Pallas kernels, gather_rows(): pl.pallas_call(rows_kernel, in_specs=[anyspec] * 5, out_specs=[anyspec] *...  84.2 us
    pallas_call x1, Pallas kernels, shared_products(): pl.pallas_call(shared_products_kernel, grid=(3,), in_specs=[anyspec] * 5...  65.8 us
    pallas_call x1, Pallas kernels, feed_forward(): pl.pallas_call(feed_forward_kernel, grid=(2,), in_specs=[block, block, an...  52.1 us
    dot_general x3, matrix products, mm(): lax.dot_general(left, right, (dims, ((), ())), preferred_element_type=f32)  32.8 us
    ppermute x2, waiting for transfers between devices, swap_across(): return lax.ppermute(shard, 'seq', [(i, i ^ 4) for i in range(8)])  32.1 us
    pallas_call x3, Pallas kernels, call_heads(): pl.pallas_call(kernel, grid=(heads,), in_specs=in_specs, out_specs=out_sp...  31.3 us
  transfers between devices with their start and end apart: 12, of which 6 were waited for; matrix products, arithmetic and copies ran while one was open for 7% of the time, Pallas kernels for 22%

profile of v11, /device:TPU:0, one launch (start us, length us, event | category | flops | bytes accessed | tf_op | source)
XLA Modules:
  0.0 818.4 jit_solution(14388696614716547960)
XLA Ops:
  8.1 1.4 stack.33
  9.6 1.5 fusion.26.first
  11.1 182.9 %gather_weights.1 = (bf16[2560,8320]{1,0:T(8,128)(2,1)}, bf16[320,5760]{1,0:T(8,128)(2,1)}) custom-call(bf16[80,640]{1,0:T(8,128)(2,1)} %fusion.26.first, bf16[80,2560]{1,0:T(8,128)(2,1)} %branch.1, bf16[80,2560]{1,0:T(8,128)(2,1)} %gelu.1, bf16[80,2560]{1,0:T(8,128)(2,1)} %outer.1, bf16[80,7680]{1,0:T(8,128)(2,1)} %gate.1, bf16[80,7680]{1,0:T(8,128)(2,1)} %up.1, ...), custom_call_target="tpu_custom_call" | custom-call | tf_op jit(solution)/shard_map/gather_weights/pallas_call | solution.py:351
  194.1 5.5 collective-permute-start.1
  199.5 3.4 collective-permute-start.2
  202.9 2.3 slice.203
  205.6 2.2 slice_reduce_fusion
  208.2 15.2 %fusion.37 = (bf16[192,5120]{1,0:T(8,128)(2,1)S(1)}, f32[192,5120]{1,0:T(8,128)}) fusion(bf16[192,2560]{1,0:T(8,128)(2,1)S(1)} %fusion.13.normed, bf16[2560,8320]{1,0:T(8,128)(2,1)} %get-tuple-element.61.mixer_w), kind=kOutput, calls=%fused_computation.115 | convolution fusion | flops 5034147840 | bytes 33095680 | tf_op jit(solution)/shard_map/dot_general | solution.py:62
  223.4 1.3 copy-done.38
  224.7 1.3 collective-permute-start
  226.0 1.7 copy.75
  228.6 3.1 fusion.35
  231.8 1.0 slice.266.branch
  232.9 1.3 copy-done.2
  234.2 1.2 copy-done.4
  235.4 7.2 mixer_forward.1
  243.4 11.3 %all-gather.2 = f32[8,2,2560]{2,1,0:T(2,128)S(1)} all-gather(f32[1,2,2560]{2,1,0:T(2,128)S(1)} %fusion.27), channel_id=2, replica_groups=mesh['seq'=8,'fsdp'=4] {'seq'}, dimensions={0}, use_global_device_ids=true | all-gather | bytes 184320 | tf_op jit(solution)/shard_map/all_gather | solution.py:29
  255.1 2.0 fusion.34
  257.2 10.2 %multiply_reduce_fusion.3 = (f32[192]{0:T(256)S(1)}, f32[192,2560]{1,0:T(8,128)S(1)}) fusion(bf16[192,2560]{1,0:T(8,128)(2,1)S(1)} %get-tuple-element.218.mixed, bf16[2560,8320]{1,0:T(8,128)(2,1)} %get-tuple-element.61.mixer_w, bf16[1,192,2560]{2,1,0:T(8,128)(2,1)S(1)} %copy-done.25), kind=kOutput, calls=%fused_computation.37 | convolution fusion | flops 2518548224 | bytes 17040128 | tf_op jit(solution)/shard_map/dot_general | solution.py:62
  267.5 1.2 copy-done.20
  268.7 1.2 multiply_convert_fusion.normed
  269.9 84.2 %gather_rows.1 = (bf16[768,2560]{1,0:T(8,128)(2,1)}, bf16[768,2560]{1,0:T(8,128)(2,1)}, bf16[768,2560]{1,0:T(8,128)(2,1)}, bf16[768,2560]{1,0:T(8,128)(2,1)}) custom-call(bf16[192,2560]{1,0:T(8,128)(2,1)} %multiply_convert_fusion.normed, bf16[192,2560]{1,0:T(8,128)(2,1)} %bitcast.13.grad0, bf16[192,2560]{1,0:T(8,128)(2,1)} %collective-permute-done.1.grad1, ...), custom_call_target="tpu_custom_call" | custom-call | tf_op jit(solution)/shard_map/gather_rows/pallas_call | solution.py:470
  354.1 52.1 %feed_forward.1 = (bf16[768,1920]{1,0:T(8,128)(2,1)}, bf16[768,1920]{1,0:T(8,128)(2,1)}, bf16[768,3840]{1,0:T(8,128)(2,1)}, bf16[768,3840]{1,0:T(8,128)(2,1)}, bf16[768,2560]{1,0:T(8,128)(2,1)}) custom-call(bf16[768,2560]{1,0:T(8,128)(2,1)} %get-tuple-element.66.normed, bf16[768,2560]{1,0:T(8,128)(2,1)} %get-tuple-element.68.grad_out.grad, ...), custom_call_target="tpu_custom_call" | custom-call | tf_op jit(solution)/shard_map/feed_forward/pallas_call | solution.py:573
  406.3 65.8 %feed_forward_products.1 = (bf16[160,5760]{1,0:T(8,128)(2,1)}, bf16[160,5760]{1,0:T(8,128)(2,1)}, bf16[320,5760]{1,0:T(8,128)(2,1)}, bf16[160,5760]{1,0:T(8,128)...) custom-call(bf16[768,2560]{1,0:T(8,128)(2,1)} %get-tuple-element.66.normed, ...), custom_call_target="tpu_custom_call" | custom-call | tf_op jit(solution)/shard_map/feed_forward_products/pallas_call | solution.py:757
  472.2 1.8 collective-permute-start.5
  474.0 3.3 reduce-scatter.5.cloned.1.call-done
  477.3 2.3 multiply_reduce_fusion.2
  479.9 1.8 add_convert_fusion.3.grad_mix
  481.8 7.3 fusion.2.grad_mixed
  489.2 12.8 %mixer_backward_scan.1 = (bf16[192,2560]{1,0:T(8,128)(2,1)S(1)}, f32[192,2560]{1,0:T(8,128)S(1)}, f32[192,2560]{1,0:T(8,128)S(1)}, f32[8,2560]{1,0:T(8,128)S(1)}) custom-call(f32[192,2560]{1,0:T(8,128)S(1)} %fusion.2.grad_mixed, f32[192,2560]{1,0:T(8,128)S(1)} %copy-done.8, f32[192,2560]{1,0:T(8,128)S(1)} %copy-done.7, ...), custom_call_target="tpu_custom_call" | custom-call | flops 1 | bytes 1 | tf_op jit(solution)/shard_map/mixer_backward_scan/pallas_call | solution.py:1174
  503.0 11.5 %collective-permute-done.4 = bf16[160,5760]{1,0:T(8,128)(2,1)} collective-permute-done((bf16[160,5760]{1,0:T(8,128)(2,1)}, bf16[160,5760]{1,0:T(8,128)(2,1)}, u32[]{:S(2)}, u32[]{:S(2)}) %collective-permute-start.4) | collective-permute-done | bytes 1843232 | tf_op jit(solution)/shard_map/ppermute | solution.py:1134
  514.6 9.4 %all-gather.3 = f32[8,2,2560]{2,1,0:T(2,128)S(1)} all-gather(f32[1,2,2560]{2,1,0:T(2,128)S(1)} %fusion.28), channel_id=3, replica_groups=mesh['seq'=8,'fsdp'=4] {'seq'}, dimensions={0}, use_global_device_ids=true | all-gather | bytes 184320 | tf_op jit(solution)/shard_map/all_gather | solution.py:29
  524.5 11.3 %mixer_backward.1 = (f32[192,2560]{1,0:T(8,128)S(1)}, f32[8,2560]{1,0:T(8,128)S(1)}, bf16[2560,256]{1,0:T(8,128)(2,1)S(1)}, bf16[2560,256]{1,0:T(8,128)(2,1)S(1)}, f32[8,2560]{1,0:T(8,128)S(1)}) custom-call(f32[192,2560]{1,0:T(8,128)S(1)} %get-tuple-element.77.rev_cum, f32[192,2560]{1,0:T(8,128)S(1)} %get-tuple-element.78.rev_grad, ...), custom_call_target="tpu_custom_call" | custom-call | flops 1 | bytes 1 | tf_op jit(solution)/shard_map/mixer_backward/pallas_call | solution.py:1174
  535.8 1.0 copy-done.10
  536.9 1.3 copy-done.16
  538.8 13.9 %reduce-scatter.3.cloned.1.call-done = bf16[192,2560]{1,0:T(8,128)(2,1)} async-done(((bf16[768,2560]{1,0:T(8,128)(2,1)}), bf16[192,2560]{1,0:T(8,128)(2,1)}) %reduce-scatter.3.cloned.1.call-update) | async-done | bytes 983056 | tf_op jit(solution)/shard_map/reduce_scatter | solution.py:1315
  552.7 1.4 collective-permute-start.6
  554.1 2.7 collective-permute-start.8
  557.8 2.9 fusion.23
  561.0 1.8 fusion.10.rest
  564.2 1.5 pad_maximum_fusion.grad_both
  565.7 32.0 %collective-permute-done.8 = bf16[160,5760]{1,0:T(8,128)(2,1)} collective-permute-done((bf16[160,5760]{1,0:T(8,128)(2,1)}, bf16[160,5760]{1,0:T(8,128)(2,1)}, u32[]{:S(2)}, u32[]{:S(2)}) %collective-permute-start.8) | collective-permute-done | bytes 1843232 | tf_op jit(solution)/shard_map/ppermute | solution.py:1138
  597.7 1.2 collective-permute-done.7
  598.9 6.3 add_convert_fusion
  605.9 193.3 %scatter_gradients.1 = (bf16[80,8320]{1,0:T(8,128)(2,1)}, bf16[3,80,7680]{2,1,0:T(8,128)(2,1)}, bf16[192,2560]{1,0:T(8,128)(2,1)}) custom-call(bf16[192,2560]{1,0:T(8,128)(2,1)} %copy-done.28, bf16[192,2560]{1,0:T(8,128)(2,1)} %copy-done.30, bf16[192,5120]{1,0:T(8,128)(2,1)} %pad_maximum_fusion.grad_both, bf16[192,2560]{1,0:T(8,128)(2,1)} %copy-done.29, ...), custom_call_target="tpu_custom_call" | custom-call | tf_op jit(solution)/shard_map/scatter_gradients/pallas_call | solution.py:1080
  799.2 3.0 multiply_reduce_fusion.4
  804.1 3.0 multiply_reduce_fusion
  807.2 1.6 bitcast_convert_fusion
  (141 shorter events, 14.7 us)
Async XLA Ops:
  7.2 346.9 %all-gather.6.cloned.1.call-start = ((), (), s32[]{:S(2)}) async-start(), calls=%async_computation.2 | async-start | bytes 33177600 | tf_op jit(solution)/shard_map/all_gather | solution.py:1231
  194.0 283.2 %reduce-scatter.5.cloned.1.call-start = ((), (), s32[]{:S(2)}) async-start(), calls=%async_computation.4 | async-start | bytes 4915200 | tf_op jit(solution)/shard_map/reduce_scatter | solution.py:1297
  194.1 75.8 %collective-permute-start.1 = (bf16[192,2560]{1,0:T(8,128)(2,1)}, bf16[192,2560]{1,0:T(8,128)(2,1)}, u32[]{:S(2)}, u32[]{:S(2)}) collective-permute-start(bf16[192,2560]{1,0:T(8,128)(2,1)} %bitcast.13.grad0), channel_id=1, source_target_pairs={{0,1},{1,2},{2,3},{3,0},{4,5},{5,6},{6,7},{7,4},{8,9},{9,10},{10,1... | collective-permute-start | bytes 2949128 | tf_op jit(solution)/shard_map/ppermute | solution.py:1124
  199.5 70.3 %collective-permute-start.2 = (bf16[192,2560]{1,0:T(8,128)(2,1)}, bf16[192,2560]{1,0:T(8,128)(2,1)}, u32[]{:S(2)}, u32[]{:S(2)}) collective-permute-start(bf16[192,2560]{1,0:T(8,128)(2,1)} %bitcast.13.grad0), channel_id=1, source_target_pairs={{0,2},{1,3},{2,0},{3,1},{4,6},{5,7},{6,4},{7,5},{8,10},{9,11},{10,... | collective-permute-start | bytes 2949128 | tf_op jit(solution)/shard_map/ppermute | solution.py:1124
  202.9 67.0 %collective-permute-start.3 = (bf16[192,2560]{1,0:T(8,128)(2,1)}, bf16[192,2560]{1,0:T(8,128)(2,1)}, u32[]{:S(2)}, u32[]{:S(2)}) collective-permute-start(bf16[192,2560]{1,0:T(8,128)(2,1)} %bitcast.13.grad0), channel_id=1, source_target_pairs={{0,3},{1,0},{2,1},{3,2},{4,7},{5,4},{6,5},{7,6},{8,11},{9,8},{10,9... | collective-permute-start | bytes 2949128 | tf_op jit(solution)/shard_map/ppermute | solution.py:1124
  202.9 2.3 copy-start.24
  205.2 2.7 copy-start.22
  208.2 15.2 %copy-start.28 = (bf16[192,2560]{1,0:T(8,128)(2,1)}, bf16[192,2560]{1,0:T(8,128)(2,1)S(1)}, u32[]{:S(2)}) copy-start(bf16[192,2560]{1,0:T(8,128)(2,1)S(1)} %fusion.13.normed) | copy-start | bytes 2949124
  224.7 8.1 collective-permute-start
  228.6 3.2 copy-start.39
  235.4 19.7 %copy-start.36 = (f32[192,5120]{1,0:T(8,128)S(1)}, f32[192,5120]{1,0:T(8,128)}, u32[]{:S(2)}) copy-start(f32[192,5120]{1,0:T(8,128)} %get-tuple-element.237) | copy-start | bytes 11796484
  242.6 14.5 %copy-start.1 = (f32[192,2560]{1,0:T(8,128)}, f32[192,2560]{1,0:T(8,128)S(1)}, u32[]{:S(2)}) copy-start(f32[192,2560]{1,0:T(8,128)S(1)} %get-tuple-element.62.local) | copy-start | bytes 5898244
  242.6 14.5 %copy-start.6 = (f32[192,2560]{1,0:T(8,128)}, f32[192,2560]{1,0:T(8,128)S(1)}, u32[]{:S(2)}) copy-start(f32[192,2560]{1,0:T(8,128)S(1)} %get-tuple-element.76.rate_pre) | copy-start | bytes 5898244
  242.6 14.5 %copy-start.9 = (f32[192,2560]{1,0:T(8,128)}, f32[192,2560]{1,0:T(8,128)S(1)}, u32[]{:S(2)}) copy-start(f32[192,2560]{1,0:T(8,128)S(1)} %get-tuple-element.86.input_pre) | copy-start | bytes 5898244
  242.6 14.5 %copy-start.12 = (bf16[192,2560]{1,0:T(8,128)(2,1)}, bf16[192,2560]{1,0:T(8,128)(2,1)S(1)}, u32[]{:S(2)}) copy-start(bf16[192,2560]{1,0:T(8,128)(2,1)S(1)} %get-tuple-element.87.conv) | copy-start | bytes 2949124
  242.6 246.5 %copy-start = (f32[192,2560]{1,0:T(8,128)}, f32[192,2560]{1,0:T(8,128)S(1)}, u32[]{:S(2)}) copy-start(f32[192,2560]{1,0:T(8,128)S(1)} %get-tuple-element.63.cum) | copy-start | bytes 5898244
  255.1 2.0 copy-start.40
  255.1 2.0 copy-start.25
  257.2 10.3 %copy-start.29 = (bf16[192,2560]{1,0:T(8,128)(2,1)}, bf16[192,2560]{1,0:T(8,128)(2,1)S(1)}, u32[]{:S(2)}) copy-start(bf16[192,2560]{1,0:T(8,128)(2,1)S(1)} %get-tuple-element.218.mixed) | copy-start | bytes 2949124
  406.2 146.4 %reduce-scatter.3.cloned.1.call-start = ((), (), s32[]{:S(2)}) async-start(), calls=%async_computation.3 | async-start | bytes 4915200 | tf_op jit(solution)/shard_map/reduce_scatter | solution.py:1315
  472.1 42.4 %collective-permute-start.4 = (bf16[160,5760]{1,0:T(8,128)(2,1)}, bf16[160,5760]{1,0:T(8,128)(2,1)}, u32[]{:S(2)}, u32[]{:S(2)}) collective-permute-start(bf16[160,5760]{1,0:T(8,128)(2,1)} %get-tuple-element.81), channel_id=1, source_target_pairs={{0,8},{4,12},{8,0},{12,4},{16,24},{20,28},{24,16},{28,20},{1,9},{5... | collective-permute-start | bytes 5529608 | tf_op jit(solution)/shard_map/ppermute | solution.py:1134
  472.2 42.4 %collective-permute-start.5 = (bf16[160,5760]{1,0:T(8,128)(2,1)}, bf16[160,5760]{1,0:T(8,128)(2,1)}, u32[]{:S(2)}, u32[]{:S(2)}) collective-permute-start(bf16[160,5760]{1,0:T(8,128)(2,1)} %get-tuple-element.82), channel_id=1, source_target_pairs={{0,16},{4,20},{8,24},{12,28},{16,0},{20,4},{24,8},{28,12},{1,17},{... | collective-permute-start | bytes 5529608 | tf_op jit(solution)/shard_map/ppermute | solution.py:1138
  477.3 2.4 copy-start.21
  477.3 2.7 copy-start.31
  481.7 7.4 copy-start.30
  481.7 7.4 copy-start.41
  481.8 7.4 copy-start.7
  481.8 7.4 copy-start.8
  489.2 25.4 %copy-start.43 = (f32[1,2560]{1,0:T(1,128)S(1)}, f32[1,2560]{1,0:T(1,128)}, u32[]{:S(2)}) copy-start(f32[1,2560]{1,0:T(1,128)} %copy-done.42) | copy-start | bytes 30724
  489.2 35.3 %copy-start.3 = (bf16[2560,256]{1,0:T(8,128)(2,1)S(1)}, bf16[2560,256]{1,0:T(8,128)(2,1)}, u32[]{:S(2)}) copy-start(bf16[2560,256]{1,0:T(8,128)(2,1)} %get-tuple-element.224.rate_w) | copy-start | bytes 3932164
  489.2 35.3 %copy-start.5 = (bf16[192,2560]{1,0:T(8,128)(2,1)S(1)}, bf16[192,2560]{1,0:T(8,128)(2,1)}, u32[]{:S(2)}) copy-start(bf16[192,2560]{1,0:T(8,128)(2,1)} %slice.266.branch) | copy-start | bytes 2949124
  489.2 35.3 %copy-start.13 = (bf16[192,2560]{1,0:T(8,128)(2,1)S(1)}, bf16[192,2560]{1,0:T(8,128)(2,1)}, u32[]{:S(2)}) copy-start(bf16[192,2560]{1,0:T(8,128)(2,1)} %copy-done.12) | copy-start | bytes 2949124
  552.7 8.0 copy-start.19
  552.7 8.3 %copy-start.11 = (bf16[2560,256]{1,0:T(8,128)(2,1)S(1)}, bf16[2560,256]{1,0:T(8,128)(2,1)}, u32[]{:S(2)}) copy-start(bf16[2560,256]{1,0:T(8,128)(2,1)} %copy-done.10) | copy-start | bytes 3932164
  552.7 11.0 %collective-permute-start.6 = (f32[3,2560]{1,0:T(4,128)S(1)}, f32[3,2560]{1,0:T(4,128)S(1)}, u32[]{:S(2)}, u32[]{:S(2)}) collective-permute-start(f32[3,2560]{1,0:T(4,128)S(1)} %slice.253), channel_id=1, source_target_pairs={{4,0},{8,4},{12,8},{16,12},{20,16},{24,20},{28,24},{5,1},{9,5},{13... | collective-permute-start | bytes 92168 | tf_op jit(solution)/shard_map/ppermute | solution.py:23
  554.1 43.6 %collective-permute-start.8 = (bf16[160,5760]{1,0:T(8,128)(2,1)}, bf16[160,5760]{1,0:T(8,128)(2,1)}, u32[]{:S(2)}, u32[]{:S(2)}) collective-permute-start(bf16[160,5760]{1,0:T(8,128)(2,1)} %get-tuple-element.100), channel_id=1, source_target_pairs={{0,16},{4,20},{8,24},{12,28},{16,0},{20,4},{24,8},{28,12},{1,17},{... | collective-permute-start | bytes 5529608 | tf_op jit(solution)/shard_map/ppermute | solution.py:1138
  556.8 42.1 %collective-permute-start.7 = (bf16[160,5760]{1,0:T(8,128)(2,1)}, bf16[160,5760]{1,0:T(8,128)(2,1)}, u32[]{:S(2)}, u32[]{:S(2)}) collective-permute-start(bf16[160,5760]{1,0:T(8,128)(2,1)} %get-tuple-element.99), channel_id=1, source_target_pairs={{0,8},{4,12},{8,0},{12,4},{16,24},{20,28},{24,16},{28,20},{1,9},{5... | collective-permute-start | bytes 5529608 | tf_op jit(solution)/shard_map/ppermute | solution.py:1134
  561.0 2.5 copy-start.17
  564.2 34.7 %copy-start.33 = (bf16[320,5760]{1,0:T(8,128)(2,1)S(1)}, bf16[320,5760]{1,0:T(8,128)(2,1)}, u32[]{:S(2)}) copy-start(bf16[320,5760]{1,0:T(8,128)(2,1)} %get-tuple-element.97) | copy-start | bytes 11059204
  605.9 193.3 %copy-start.34 = (bf16[80,2560]{1,0:T(8,128)(2,1)S(1)}, bf16[80,2560]{1,0:T(8,128)(2,1)}, u32[]{:S(2)}) copy-start(bf16[80,2560]{1,0:T(8,128)(2,1)} %branch.1) | copy-start | bytes 1228804
  605.9 193.3 %copy-start.35 = (bf16[80,2560]{1,0:T(8,128)(2,1)S(1)}, bf16[80,2560]{1,0:T(8,128)(2,1)}, u32[]{:S(2)}) copy-start(bf16[80,2560]{1,0:T(8,128)(2,1)} %gelu.1) | copy-start | bytes 1228804
  799.2 3.0 copy-start.23
  799.2 3.9 copy-start.32
  802.3 1.5 copy-start.26
  802.3 1.9 copy-start.27
  807.2 3.1 copy-start.44
  807.2 3.1 copy-start.45
  807.2 3.6 copy-start.37
  (10 other events, 11.0 us)
Sparse Core Ops, SparseCore 0:
  194.1 149.8 all-gather.5
  406.3 70.8 reduce-scatter.4
  479.6 73.0 reduce-scatter.2

commit v12 on v11

--- a/solution.py
+++ b/solution.py
@@ -366,8 +366,8 @@
 
 
 def rows_kernel(
-    normed, grad0, grad1, grad2, grad3, normed_all, normed_other, grad_all, grad_other,
-    line_send, line_recv, core_send, core_recv, own_sem, held,
+    normed, grad0, grad1, grad2, grad3, first, mixed, normed_all, normed_other, grad_all, grad_other,
+    first_other, mixed_other, line_send, line_recv, core_send, core_recv, own_sem, held, give_send, give_recv,
 ):
     s, z, core, _, _ = places()
     tok = normed.shape[0]
@@ -431,6 +431,10 @@
         pl.when(z >= hop)(below)
         pl.when(z + hop <= 3)(above)
 
+    given = [
+        remote(source, target, give_send.at[n], give_recv.at[n], (core, z))
+        for n, (source, target) in enumerate(((first, first_other), (mixed, mixed_other)))
+    ]
     local = [pltpu.make_async_copy(grads[k], held.at[k], own_sem.at[k]) for k in range(4)]
     local.append(pltpu.make_async_copy(normed, held.at[4], own_sem.at[4]))
     stored = [
@@ -444,6 +448,8 @@
         copy.start()
     for k in range(4):
         grad_over(k).start()
+    for copy in given:
+        copy.start()
     for copy, store in zip(local, stored):
         copy.wait()
         store.start()
@@ -453,6 +459,8 @@
         copy.wait()
     for k in range(4):
         grad_over(k).wait()
+    for copy in given:
+        copy.wait()
     over(z, True).wait()
     for k in range(1, 4):
         over((z + k) % 4).wait()
@@ -463,19 +471,23 @@
         pl.when((z + hop <= 3) & (z > 0))(lambda: line_drain(z + hop, False, hop))
 
 
-def gather_rows(normed, grads):
+def gather_rows(normed, grads, first, mixed):
     tok, model = normed.shape
     anyspec = pl.BlockSpec(memory_space=pl.ANY)
     dma = pltpu.SemaphoreType.DMA
     return pl.pallas_call(
         rows_kernel,
-        in_specs=[anyspec] * 5,
-        out_specs=[anyspec] * 4,
-        out_shape=[jax.ShapeDtypeStruct((4 * tok, model), bf16)] * 4,
-        scratch_shapes=[dma((2, 3, 4)), dma((2, 3, 4)), dma((2, 4)), dma((2, 4)), dma((5,)), pltpu.VMEM((5, tok, model), bf16)],
+        in_specs=[anyspec] * 7,
+        out_specs=[anyspec] * 6,
+        out_shape=[jax.ShapeDtypeStruct((4 * tok, model), bf16)] * 4
+        + [jax.ShapeDtypeStruct(first.shape, bf16), jax.ShapeDtypeStruct(mixed.shape, bf16)],
+        scratch_shapes=[
+            dma((2, 3, 4)), dma((2, 3, 4)), dma((2, 4)), dma((2, 4)), dma((5,)),
+            pltpu.VMEM((5, tok, model), bf16), dma((2,)), dma((2,)),
+        ],
         compiler_params=pltpu.CompilerParams(collective_id=3, has_side_effects=True),
         name="gather_rows",
-    )(normed, *grads)
+    )(normed, *grads, first, mixed)
 
 
 def column_tiles(cols, size=512):
@@ -780,7 +792,8 @@
 
 
 def scatter_kernel(
-    normed, grad_mix, grad_both, mixed, rest, mlp_low, mlp_high, mixer_w, tokens, gain, mixer_sum, mlp_back, input_grad,
+    normed, normed_other, grad_mix, mix_other, mixed, mixed_other, grad_both, rest, mlp_low, mlp_high, mixer_w,
+    tokens, gain, mixer_sum, mlp_back, input_grad,
     held, cross, near, lined, left_now, both_now, mixed_now, turned, stage, rest_other, back_now, wide_now, gain_now,
     load_sem, core_send, core_recv, wide_sem,
     flow_send, flow_recv, line_send, line_recv, swap_send, swap_recv, own_sem,
@@ -806,23 +819,28 @@
     def span(k):
         return pl.ds(pl.multiple_of(k * rows, 16), rows)
 
-    shared = (
-        (normed, left_now.at[0]), (grad_both, both_now), (grad_mix, left_now.at[1]), (mixed, mixed_now),
-    )
+    mine, other = pl.ds(0, tok), pl.ds(tok, tok)
     loads = [
-        pltpu.make_async_copy(source, target.at[pl.ds(0, tok), :], load_sem.at[n])
-        for n, (source, target) in enumerate(shared)
+        pltpu.make_async_copy(source, target, load_sem.at[n])
+        for n, (source, target) in enumerate(
+            (
+                (grad_mix, left_now.at[1, mine, :]),
+                (mix_other, left_now.at[1, other, :]),
+                (mixed, mixed_now.at[mine, :]),
+                (mixed_other, mixed_now.at[other, :]),
+                (normed, left_now.at[0, mine, :]),
+                (normed_other, left_now.at[0, other, :]),
+                (grad_both, both_now.at[mine, :]),
+            )
+        )
     ]
-    pushes = [
-        (source, target.at[pl.ds(tok, tok), :]) for source, target in shared
-    ]
 
     def push(n):
-        if n < 4:
-            source, target = pushes[n]
+        if n == 0:
+            source, target = grad_both, both_now.at[other, :]
         else:
-            source = rest.at[pl.ds(pl.multiple_of(chips[n - 4] * 2 * half + (1 - s % 2) * half, 16), half), :]
-            target = rest_other.at[n - 4]
+            source = rest.at[pl.ds(pl.multiple_of(chips[n - 1] * 2 * half + (1 - s % 2) * half, 16), half), :]
+            target = rest_other.at[n - 1]
         return pltpu.make_async_remote_copy(
             src_ref=source,
             dst_ref=target,
@@ -835,7 +853,7 @@
     def rest_load(q):
         source = rest.at[pl.ds(pl.multiple_of(chips[q] * 2 * half + s % 2 * half, 16), half), :]
         return pltpu.make_async_copy(
-            source, held.at[q, :, pl.ds(rest_start, cols - rest_start)], load_sem.at[4 + q]
+            source, held.at[q, :, pl.ds(rest_start, cols - rest_start)], load_sem.at[7 + q]
         )
 
     def turn(side):
@@ -846,16 +864,21 @@
                 pl.ds(pl.multiple_of(s % 2 * half, 16), half), :
             ]
 
-    def multiply(q):
-        for side, right, start in ((0, both_now, 0), (1, mixed_now, lru2)):
-
-            def one(turn, carry, side=side, right=right, start=start):
-                here = pl.multiple_of(turn * 512, 512)
-                block = mm(turned[side, q * half : (q + 1) * half, :], right[:, pl.ds(here, 512)], ((1,), (0,)))
-                held[q, :, pl.ds(pl.multiple_of(start + here, 512), 512)] = block.astype(bf16)
-                return carry
-
-            lax.fori_loop(0, right.shape[1] // 512, one, 0)
+    def multiply(q, side):
+        right, start = ((both_now, 0), (mixed_now, lru2))[side]
+
+        def one(turn, carry):
+            here = pl.multiple_of(turn * 512, 512)
+            block = mm(turned[side, q * half : (q + 1) * half, :], right[:, pl.ds(here, 512)], ((1,), (0,)))
+            held[q, :, pl.ds(pl.multiple_of(start + here, 512), 512)] = block.astype(bf16)
+            return carry
+
+        lax.fori_loop(0, right.shape[1] // 512, one, 0)
+
+    def add_rest(q):
+        rest_load(q).wait()
+        push(1 + q).wait_recv()
+        held[q, :, rest_start:] = add_low(held[q, :, rest_start:], rest_other[q])
 
     left, right = pl.ds(0, cut), pl.ds(cut, cols - cut)
 
@@ -994,7 +1017,7 @@
     for q in range(4):
         rest_load(q).start()
     greet([(core, z), (beside, z), (across, z)] + [(s, (z + k) % 4) for k in range(1, 4)])
-    for n in range(8):
+    for n in range(5):
         push(n).start()
     for k in (1, 3, 2):
         swap_start(k)
@@ -1009,27 +1032,27 @@
         for copy in own(True):
             copy.start()
 
-    for n in (0, 1):
-        loads[n].wait()
-        push(n).wait_recv()
+    for copy in loads[:4]:
+        copy.wait()
+    turn(1)
+    multiply(chip_diag, 1)
+    for copy in loads[4:]:
+        copy.wait()
     turn(0)
-    for n in (2, 3):
-        loads[n].wait()
-        push(n).wait_recv()
-    turn(1)
-    multiply(chip_diag)
-    for q in range(4):
-        rest_load(q).wait()
-        push(4 + q).wait_recv()
-        held[q, :, rest_start:] = add_low(held[q, :, rest_start:], rest_other[q])
+    push(0).wait_recv()
+    multiply(chip_diag, 0)
+    add_rest(chip_diag)
     for i in range(2):
         flow(i, 0).start()
         flow(i, 1).start()
-    multiply(chip_beside)
-    flow(0, 2).start()
-    multiply(chip_across)
-    flow(0, 4).start()
-    multiply(chip)
+    for q in (chip_beside, chip_across, chip):
+        multiply(q, 0)
+        multiply(q, 1)
+        add_rest(q)
+        if q == chip_beside:
+            flow(0, 2).start()
+        if q == chip_across:
+            flow(0, 4).start()
     for copy in plain_loads:
         copy.start()
     wide(0).start()
@@ -1064,22 +1087,23 @@
             copy.wait()
     for copy in own():
         copy.wait()
-    for n in range(8):
+    for n in range(5):
         push(n).wait_send()
     finished.wait()
     done.wait()
 
 
-def scatter(normed, grad_mix, grad_both, mixed, rest, mlp_low, mlp_high, mixer_w, tokens, gain):
+def scatter(rows_pairs, grad_both, rest, mlp_low, mlp_high, mixer_w, tokens, gain):
     tok, model = tokens.shape
     rows = model // 32
+    mixed = rows_pairs[4]
     cols = grad_both.shape[1] + mixed.shape[1] + rest.shape[1]
     ff_part = mlp_low.shape[1] // 3
     anyspec = pl.BlockSpec(memory_space=pl.ANY)
     dma = pltpu.SemaphoreType.DMA
     return pl.pallas_call(
         scatter_kernel,
-        in_specs=[anyspec] * 10,
+        in_specs=[anyspec] * 13,
         out_specs=[anyspec] * 3,
         out_shape=[
             jax.ShapeDtypeStruct((rows, cols), bf16),
@@ -1100,14 +1124,14 @@
             pltpu.VMEM((tok, model), f32),
             pltpu.VMEM((128, grad_both.shape[1]), bf16),
             pltpu.VMEM((8, model), f32),
-            dma((8,)), dma((8,)), dma((8,)), dma((4,)),
+            dma((11,)), dma((5,)), dma((5,)), dma((4,)),
             dma((4, 6)), dma((4, 6)), dma((4,)), dma((5,)), dma((3, 3)), dma((3, 3)), dma((4,)),
         ],
         compiler_params=pltpu.CompilerParams(
             collective_id=2, has_side_effects=True, vmem_limit_bytes=62 * 1024 * 1024
         ),
         name="scatter_gradients",
-    )(normed, grad_mix, grad_both, mixed, rest, mlp_low, mlp_high, mixer_w, tokens, gain)
+    )(*rows_pairs, grad_both, rest, mlp_low, mlp_high, mixer_w, tokens, gain)
 
 
 def gather_plain(mixer, gate, up, down):
@@ -1159,14 +1183,13 @@
 
 
 def call_heads(kernel, width, heads, ins, outs, scratch, name):
-    def spec(rows_cols):
-        rows, by_row = rows_cols
-        if by_row:
-            return pl.BlockSpec((rows, width), lambda h: (h, 0))
-        return pl.BlockSpec((rows, width), lambda h: (0, h))
-
-    in_specs = [spec((width, True)) if rowwise else spec((a.shape[0], False)) for a, rowwise in ins]
-    out_specs = [spec((width, True)) if rowwise else spec((rows, False)) for rows, _, rowwise in outs]
+    def spec(rows, place):
+        if place is None:
+            return pl.BlockSpec((rows, width), lambda h: (0, h))
+        return pl.BlockSpec((width, width), lambda h: (h, place))
+
+    in_specs = [spec(a.shape[0], place) for a, place in ins]
+    out_specs = [spec(rows, 0 if rowwise else None) for rows, _, rowwise in outs]
     out_shape = [
         jax.ShapeDtypeStruct((heads * width, width) if rowwise else (rows, heads * width), kind)
         for rows, kind, rowwise in outs
@@ -1221,7 +1244,7 @@
     )
     small_count = smalls.shape[1]
     smalls = jnp.pad(smalls, ((0, 0), (0, 128 - small_count)))
-    first_own = jnp.concatenate([smalls, rate_blocks, input_blocks], axis=1)
+    first_own = jnp.concatenate([rate_blocks, input_blocks, smalls], axis=1)
     mixer_own = (first_own, branch_proj, gelu_proj, out_proj)
     custom = lax.axis_size("seq") == 8 and groups == 4
     if custom:
@@ -1232,13 +1255,11 @@
     grad_out_late = lax.optimization_barrier((grad_out, mlp_mine))[0]
     if custom:
         grad_pieces = from_line(grad_out_late)
-    first = lax.optimization_barrier(mixer_w[:, : 128 + 2 * width])
+    smalls = lax.optimization_barrier(mixer_w[:, 2 * width : 2 * width + 128])
     wide = mixer_w[:, 128 + 2 * width : 128 + 2 * width + 2 * lru]
     proj_out = mixer_w[:, 128 + 2 * width + 2 * lru :]
 
-    table = first[:, :small_count].astype(f32).T
-    blocks_rate = first[:, 128 : 128 + width]
-    blocks_input = first[:, 128 + width :]
+    table = smalls[:, :small_count].astype(f32).T
     param_decay = table[margin + 4]
     gain_one = table[margin + 5]
     gain_two = table[margin + 6]
@@ -1262,7 +1283,7 @@
         mixer_forward,
         width,
         heads,
-        [(branch, False), (prior, False), (small, False), (blocks_rate, True), (blocks_input, True)],
+        [(branch, None), (prior, None), (small, None), (mixer_w, 0), (mixer_w, 1)],
         [(tok_count, bf16, False)] + [(tok_count, f32, False)] * 4,
         [tok_count + 8],
         "mixer_forward",
@@ -1274,7 +1295,9 @@
     normed_two = norm_rows(middle, gain_two).astype(bf16)
 
     if custom:
-        normed_all, normed_other, grad_out_all, grad_out_other = gather_rows(normed_two, grad_pieces)
+        normed_all, normed_other, grad_out_all, grad_out_other, first_other, mixed_other = gather_rows(
+            normed_two, grad_pieces, normed, mixed
+        )
     else:
         normed_all = lax.all_gather(normed_two, "fsdp", axis=0, tiled=True)
         grad_out_all = lax.all_gather(grad_out_late, "fsdp", axis=0, tiled=True)
@@ -1317,13 +1340,15 @@
 
     grad_middle = grad_out.astype(f32) + norm_back(middle, gain_two, grad_normed_two)
     grad_mix = grad_middle.astype(bf16)
+    if custom:
+        mix_other = swap_cores(grad_mix)
     grad_mixed = mm(grad_mix, proj_out, ((1,), (0,)))
     carried_rows = jnp.broadcast_to(carried[None], (8, lru))
     grad_gelu_pre, rev_cum, rev_grad, pair_grad = call_heads(
         mixer_backward_scan,
         width,
         heads,
-        [(a, False) for a in (grad_mixed, gelu_pre, rate_pre, cum, local, carried_rows, small)],
+        [(a, None) for a in (grad_mixed, gelu_pre, rate_pre, cum, local, carried_rows, small)],
         [(tok_count, bf16, False), (tok_count, f32, False), (tok_count, f32, False), (8, f32, False)],
         [tok_count + 8],
         "mixer_backward_scan",
@@ -1342,10 +1367,10 @@
         width,
         heads,
         [
-            (a, False)
+            (a, None)
             for a in (rev_cum, rev_grad, incoming_rows, cum, local, carried_rows, rate_pre, input_pre, conv, branch, prior, small)
         ]
-        + [(blocks_rate, True), (blocks_input, True)],
+        + [(mixer_w, 0), (mixer_w, 1)],
         [(tok_count, f32, False), (8, f32, False), (0, bf16, True), (0, bf16, True), (8, f32, False)],
         [tok_count + 8, tok_count + 16],
         "mixer_backward",
@@ -1355,8 +1380,6 @@
         [own[: tok_count - margin], own[tok_count - margin :] + received], axis=0
     ).astype(bf16)
     grad_both = jnp.concatenate([grad_branch, grad_gelu_pre], axis=1)
-    middle, out_sum, sums = lax.optimization_barrier((middle, out_sum, sums))
-    block_output = (middle + out_sum.astype(f32)).astype(bf16)[None]
     vectors = jnp.pad(sums.T, ((0, 0), (0, 128 - sums.shape[0]))).astype(bf16)
     rest = jnp.concatenate([rate_w_grad, input_w_grad, vectors], axis=1)
     if custom:
@@ -1367,13 +1390,16 @@
         low, high = [sum(part.astype(f32) for part in parts).astype(bf16) for parts in mlp_parts]
         gain_rows = jnp.broadcast_to(gain_one[None], (8, model))
         mixer_sum, mlp_back, input_grad = scatter(
-            normed, grad_mix, grad_both, mixed, rest, low, high, mixer_w, block_input[0], gain_rows
+            (normed, first_other, grad_mix, mix_other, mixed, mixed_other),
+            grad_both, rest, low, high, mixer_w, block_input[0], gain_rows,
         )
     else:
         mixer_sum, mlp_back = scatter_plain(normed, grad_both, grad_mix, mixed, rest, mlp_sum)
         grad_normed = mm(grad_both, wide, ((1,), (1,)))
         input_grad = (grad_middle + norm_back(tokens, gain_one, grad_normed)).astype(bf16)
     input_grad = input_grad[None]
+    middle = lax.optimization_barrier((middle, mixer_sum))[0]
+    block_output = (middle + out_sum.astype(f32)).astype(bf16)[None]
     mlp_grads = [mlp_back[m].astype(f32) for m in range(3)]
     mixer_sum = mixer_sum.astype(f32)
     edges = [lru, 2 * lru, 3 * lru, 3 * lru + width, 3 * lru + 2 * width]

time: 828 us -> 827 us (level)
  local copies, waits for them, and re-layouts: 27.9 us -> 65.3 us
  waiting for transfers between devices: 62.1 us -> 36.6 us
  Pallas kernels: 610 us -> 592 us
    pallas_call x0 -> x1, local copies, waits for them, and re-layouts: none -> 50.7 us  [gather(): pl.pallas_call(gather_kernel, in_specs=[anyspec] * 7, out_specs=[anyspec]...]
    ppermute x2, waiting for transfers between devices: 32.1 us -> 2.85 us  [swap_across(): return lax.ppermute(shard, 'seq', [(i, i ^ 4) for i in range(8)])]
    pallas_call x2, Pallas kernels: 278 us -> 260 us  [the longest x1 187 us: scatter(): pl.pallas_call(scatter_kernel, in_specs=[anyspec] * 13, out_specs=[anyspe...]
    ppermute x2, waiting for transfers between devices: 12.7 us -> 28.7 us  [swap_beside(): return lax.ppermute(shard, 'seq', [(i, i ^ 2) for i in range(8)])]
    reduce_scatter x1, waiting for transfers between devices: 13.9 us -> 0.01 us  [on_device(): lax.psum_scatter(out_part, 'fsdp', scatter_dimension=0, tiled=True)]
  transfers between devices with their start and end apart: 12 -> 13, of which waited for: 6 -> 6; matrix products, arithmetic and copies ran while one was open for 7% -> 15% of each run, Pallas kernels for 22% -> 44%
where the time goes in v12:
time: 827 us; the launch traced here: 817 us
  Pallas kernels  592 us (72%)
  local copies, waits for them, and re-layouts  65.3 us (8%)
  waiting for transfers between devices  36.6 us (4%)
  other arithmetic  36.4 us (4%)
  matrix products  33.2 us (4%)
  blocking collectives  23.3 us (3%)
  starting transfers between devices  16.2 us (2%)
  between operations  14.6 us (2%)
    pallas_call x1, Pallas kernels, scatter(): pl.pallas_call(scatter_kernel, in_specs=[anyspec] * 13, out_specs=[anyspe...  187 us
    pallas_call x1, Pallas kernels, gather(): pl.pallas_call(gather_kernel, in_specs=[anyspec] * 7, out_specs=[anyspec]...  183 us
    pallas_call x1, Pallas kernels, gather_rows(): pl.pallas_call(rows_kernel, in_specs=[anyspec] * 7, out_specs=[anyspec] *...  72.9 us
    pallas_call x1, Pallas kernels, shared_products(): pl.pallas_call(shared_products_kernel, grid=(3,), in_specs=[anyspec] * 5...  63.1 us
    pallas_call x1, Pallas kernels, feed_forward(): pl.pallas_call(feed_forward_kernel, grid=(2,), in_specs=[block, block, an...  52 us
    pallas_call x1, local copies, waits for them, and re-layouts, gather(): pl.pallas_call(gather_kernel, in_specs=[anyspec] * 7, out_specs=[anyspec]...  50.7 us
    pallas_call x3, Pallas kernels, call_heads(): pl.pallas_call(kernel, grid=(heads,), in_specs=in_specs, out_specs=out_sp...  33.7 us
    dot_general x3, matrix products, mm(): lax.dot_general(left, right, (dims, ((), ())), preferred_element_type=f32)  33.2 us
  transfers between devices with their start and end apart: 13, of which 6 were waited for; matrix products, arithmetic and copies ran while one was open for 15% of the time, Pallas kernels for 44%

profile of v12, /device:TPU:0, one launch (start us, length us, event | category | flops | bytes accessed | tf_op | source)
XLA Modules:
  0.0 817.2 jit_solution(1670345387791295517)
XLA Ops:
  7.2 0.8 slice_bitcast_fusion.1
  8.1 1.4 stack.33
  9.6 1.5 fusion.25.first
  11.1 182.9 %gather_weights.1 = (bf16[2560,8320]{1,0:T(8,128)(2,1)}, bf16[320,5760]{1,0:T(8,128)(2,1)}) custom-call(bf16[80,640]{1,0:T(8,128)(2,1)} %fusion.25.first, bf16[80,2560]{1,0:T(8,128)(2,1)} %branch.1, bf16[80,2560]{1,0:T(8,128)(2,1)} %gelu.1, bf16[80,2560]{1,0:T(8,128)(2,1)} %outer.1, bf16[80,7680]{1,0:T(8,128)(2,1)} %gate.1, bf16[80,7680]{1,0:T(8,128)(2,1)} %up.1, ...), custom_call_target="tpu_custom_call" | custom-call | tf_op jit(solution)/shard_map/gather_weights/pallas_call | solution.py:351
  194.1 5.5 collective-permute-start.1
  199.5 3.4 collective-permute-start.2
  202.9 50.7 %copy.61 = bf16[2560,8320]{0,1:T(8,128)(2,1)} copy(bf16[2560,8320]{1,0:T(8,128)(2,1)} %get-tuple-element.61.rate_w.input_w.mixer_w) | data formatting | bytes 85196800 | tf_op jit(solution)/shard_map/gather_weights/pallas_call | solution.py:351
  253.9 0.8 slice-done
  255.2 17.9 %fusion.35 = (bf16[192,5120]{1,0:T(8,128)(2,1)S(1)}, f32[192,5120]{1,0:T(8,128)}) fusion(bf16[192,2560]{1,0:T(8,128)(2,1)S(1)} %fusion.13.first.normed, bf16[2560,8320]{1,0:T(8,128)(2,1)} %get-tuple-element.61.rate_w.input_w.mixer_w), kind=kOutput, calls=%fused_computation.113 | convolution fusion | flops 5034147840 | bytes 33095680 | tf_op jit(solution)/shard_map/dot_general | solution.py:62
  273.1 1.3 collective-permute-start
  275.3 9.6 %mixer_forward.1 = (bf16[192,2560]{1,0:T(8,128)(2,1)S(1)}, f32[192,2560]{1,0:T(8,128)S(1)}, f32[192,2560]{1,0:T(8,128)S(1)}, f32[192,2560]{1,0:T(8,128)S(1)}, f32[192,2560]{1,0:T(8,128)S(1)}) custom-call(bf16[192,2560]{1,0:T(8,128)(2,1)S(1)} %slice.259.branch, f32[8,2560]{1,0:T(8,128)S(1)} %pad_convert_fusion.prior, ...), custom_call_target="tpu_custom_call" | custom-call | flops 1 | bytes 1 | tf_op jit(solution)/shard_map/mixer_forward/pallas_call | solution.py:1197
  285.0 15.2 %all-gather.2 = f32[8,2,2560]{2,1,0:T(2,128)S(1)} all-gather(f32[1,2,2560]{2,1,0:T(2,128)S(1)} %fusion.26), channel_id=2, replica_groups=mesh['seq'=8,'fsdp'=4] {'seq'}, dimensions={0}, use_global_device_ids=true | all-gather | bytes 184320 | tf_op jit(solution)/shard_map/all_gather | solution.py:29
  300.6 2.0 fusion.33
  302.7 7.9 multiply_reduce_fusion.3
  310.6 1.3 copy-done.13
  311.9 1.2 multiply_convert_fusion.normed
  313.1 72.9 %gather_rows.1 = (bf16[768,2560]{1,0:T(8,128)(2,1)}, bf16[768,2560]{1,0:T(8,128)(2,1)}, bf16[768,2560]{1,0:T(8,128)(2,1)}, bf16[768,2560]{1,0:T(8,128)(2,1)}, bf...) custom-call(bf16[192,2560]{1,0:T(8,128)(2,1)} %multiply_convert_fusion.normed, bf16[192,2560]{1,0:T(8,128)(2,1)} %bitcast.13.grad0, ...), custom_call_target="tpu_custom_call" | custom-call | tf_op jit(solution)/shard_map/gather_rows/pallas_call | solution.py:478
  386.0 52.0 %feed_forward.1 = (bf16[768,1920]{1,0:T(8,128)(2,1)}, bf16[768,1920]{1,0:T(8,128)(2,1)}, bf16[768,3840]{1,0:T(8,128)(2,1)}, bf16[768,3840]{1,0:T(8,128)(2,1)}, bf16[768,2560]{1,0:T(8,128)(2,1)}) custom-call(bf16[768,2560]{1,0:T(8,128)(2,1)} %get-tuple-element.67.normed, bf16[768,2560]{1,0:T(8,128)(2,1)} %get-tuple-element.68.grad_out.grad, ...), custom_call_target="tpu_custom_call" | custom-call | tf_op jit(solution)/shard_map/feed_forward/pallas_call | solution.py:585
  438.2 63.1 %feed_forward_products.1 = (bf16[160,5760]{1,0:T(8,128)(2,1)}, bf16[160,5760]{1,0:T(8,128)(2,1)}, bf16[320,5760]{1,0:T(8,128)(2,1)}, bf16[160,5760]{1,0:T(8,128)...) custom-call(bf16[768,2560]{1,0:T(8,128)(2,1)} %get-tuple-element.67.normed, ...), custom_call_target="tpu_custom_call" | custom-call | tf_op jit(solution)/shard_map/feed_forward_products/pallas_call | solution.py:769
  501.2 2.4 collective-permute-start.5
  503.8 4.4 reduce-scatter.3.cloned.1.call-done
  508.2 2.3 multiply_reduce_fusion.2
  510.8 2.8 add_convert_fusion.3.grad_mix
  513.6 7.4 fusion.2.grad_mixed
  521.0 12.7 %mixer_backward_scan.1 = (bf16[192,2560]{1,0:T(8,128)(2,1)S(1)}, f32[192,2560]{1,0:T(8,128)S(1)}, f32[192,2560]{1,0:T(8,128)S(1)}, f32[8,2560]{1,0:T(8,128)S(1)}) custom-call(f32[192,2560]{1,0:T(8,128)S(1)} %fusion.2.grad_mixed, f32[192,2560]{1,0:T(8,128)S(1)} %copy-done.3, f32[192,2560]{1,0:T(8,128)S(1)} %copy-done.2, ...), custom_call_target="tpu_custom_call" | custom-call | flops 1 | bytes 1 | tf_op jit(solution)/shard_map/mixer_backward_scan/pallas_call | solution.py:1197
  533.8 10.4 %collective-permute-done.5 = bf16[160,5760]{1,0:T(8,128)(2,1)} collective-permute-done((bf16[160,5760]{1,0:T(8,128)(2,1)}, bf16[160,5760]{1,0:T(8,128)(2,1)}, u32[]{:S(2)}, u32[]{:S(2)}) %collective-permute-start.5) | collective-permute-done | bytes 1843232 | tf_op jit(solution)/shard_map/ppermute | solution.py:1158
  544.2 1.5 collective-permute-done.6
  545.7 8.2 %all-gather.3 = f32[8,2,2560]{2,1,0:T(2,128)S(1)} all-gather(f32[1,2,2560]{2,1,0:T(2,128)S(1)} %fusion.27), channel_id=3, replica_groups=mesh['seq'=8,'fsdp'=4] {'seq'}, dimensions={0}, use_global_device_ids=true | all-gather | bytes 184320 | tf_op jit(solution)/shard_map/all_gather | solution.py:29
  554.3 1.7 collective-permute-start.8
  556.4 11.4 %mixer_backward.1 = (f32[192,2560]{1,0:T(8,128)S(1)}, f32[8,2560]{1,0:T(8,128)S(1)}, bf16[2560,256]{1,0:T(8,128)(2,1)S(1)}, bf16[2560,256]{1,0:T(8,128)(2,1)S(1)}, f32[8,2560]{1,0:T(8,128)S(1)}) custom-call(f32[192,2560]{1,0:T(8,128)S(1)} %get-tuple-element.72.rev_cum, f32[192,2560]{1,0:T(8,128)S(1)} %get-tuple-element.73.rev_grad, ...), custom_call_target="tpu_custom_call" | custom-call | flops 1 | bytes 1 | tf_op jit(solution)/shard_map/mixer_backward/pallas_call | solution.py:1197
  567.8 1.0 copy-done.5
  568.9 1.1 copy-done.6
  569.9 1.3 copy-done.11
  571.6 1.3 collective-permute-start.7
  572.9 3.3 fusion.10.rest
  576.3 1.1 copy-done.10
  577.4 1.5 pad_maximum_fusion.grad_both
  578.9 18.3 %collective-permute-done.8 = bf16[160,5760]{1,0:T(8,128)(2,1)} collective-permute-done((bf16[160,5760]{1,0:T(8,128)(2,1)}, bf16[160,5760]{1,0:T(8,128)(2,1)}, u32[]{:S(2)}, u32[]{:S(2)}) %collective-permute-start.8) | collective-permute-done | bytes 1843232 | tf_op jit(solution)/shard_map/ppermute | solution.py:1158
  597.1 1.4 collective-permute-done.9
  598.5 6.3 add_convert_fusion
  605.5 187.0 %scatter_gradients.1 = (bf16[80,8320]{1,0:T(8,128)(2,1)}, bf16[3,80,7680]{2,1,0:T(8,128)(2,1)}, bf16[192,2560]{1,0:T(8,128)(2,1)}) custom-call(bf16[192,2560]{1,0:T(8,128)(2,1)} %copy-done.19, bf16[192,2560]{1,0:T(8,128)(2,1)} %get-tuple-element.66.normed_other, bf16[192,2560]{1,0:T(8,128)(2,1)} %add_convert_fusion.3.grad_mix, ...), custom_call_target="tpu_custom_call" | custom-call | tf_op jit(solution)/shard_map/scatter_gradients/pallas_call | solution.py:1104
  792.6 1.6 convert_element_type.117
  794.9 0.7 slice_reduce_fusion
  795.7 1.6 multiply_reduce_fusion.4
  798.2 4.7 multiply_reduce_fusion
  804.1 2.9 bitcast_convert_fusion
  807.1 2.4 fusion.23
  809.5 0.9 copy.65
  (112 shorter events, 7.7 us)
Async XLA Ops:
  7.2 378.8 %all-gather.6.cloned.1.call-start = ((), (), s32[]{:S(2)}) async-start(), calls=%async_computation.2 | async-start | bytes 33177600 | tf_op jit(solution)/shard_map/all_gather | solution.py:1254
  194.0 314.2 %reduce-scatter.3.cloned.1.call-start = ((), (), s32[]{:S(2)}) async-start(), calls=%async_computation.3 | async-start | bytes 4915200 | tf_op jit(solution)/shard_map/reduce_scatter | solution.py:1320
  194.1 119.0 %collective-permute-start.1 = (bf16[192,2560]{1,0:T(8,128)(2,1)}, bf16[192,2560]{1,0:T(8,128)(2,1)}, u32[]{:S(2)}, u32[]{:S(2)}) collective-permute-start(bf16[192,2560]{1,0:T(8,128)(2,1)} %bitcast.13.grad0), channel_id=1, source_target_pairs={{0,1},{1,2},{2,3},{3,0},{4,5},{5,6},{6,7},{7,4},{8,9},{9,10},{10,1... | collective-permute-start | bytes 2949128 | tf_op jit(solution)/shard_map/ppermute | solution.py:1148
  199.5 113.6 %collective-permute-start.2 = (bf16[192,2560]{1,0:T(8,128)(2,1)}, bf16[192,2560]{1,0:T(8,128)(2,1)}, u32[]{:S(2)}, u32[]{:S(2)}) collective-permute-start(bf16[192,2560]{1,0:T(8,128)(2,1)} %bitcast.13.grad0), channel_id=1, source_target_pairs={{0,2},{1,3},{2,0},{3,1},{4,6},{5,7},{6,4},{7,5},{8,10},{9,11},{10,... | collective-permute-start | bytes 2949128 | tf_op jit(solution)/shard_map/ppermute | solution.py:1148
  202.9 110.2 %collective-permute-start.3 = (bf16[192,2560]{1,0:T(8,128)(2,1)}, bf16[192,2560]{1,0:T(8,128)(2,1)}, u32[]{:S(2)}, u32[]{:S(2)}) collective-permute-start(bf16[192,2560]{1,0:T(8,128)(2,1)} %bitcast.13.grad0), channel_id=1, source_target_pairs={{0,3},{1,0},{2,1},{3,2},{4,7},{5,4},{6,5},{7,6},{8,11},{9,8},{10,9... | collective-permute-start | bytes 2949128 | tf_op jit(solution)/shard_map/ppermute | solution.py:1148
  202.9 50.7 %copy-start.17 = (bf16[1,192,2560]{2,1,0:T(8,128)(2,1)S(1)}, bf16[1,192,2560]{2,1,0:T(8,128)(2,1)}, u32[]{:S(2)}) copy-start(bf16[1,192,2560]{2,1,0:T(8,128)(2,1)} %param.17) | copy-start | bytes 2949124
  253.6 1.1 slice-start
  255.1 18.0 %copy-start.19 = (bf16[192,2560]{1,0:T(8,128)(2,1)}, bf16[192,2560]{1,0:T(8,128)(2,1)S(1)}, u32[]{:S(2)}) copy-start(bf16[192,2560]{1,0:T(8,128)(2,1)S(1)} %fusion.13.first.normed) | copy-start | bytes 2949124
  273.1 2.1 collective-permute-start
  275.3 25.4 %copy-start.27 = (f32[192,5120]{1,0:T(8,128)S(1)}, f32[192,5120]{1,0:T(8,128)}, u32[]{:S(2)}) copy-start(f32[192,5120]{1,0:T(8,128)} %get-tuple-element.218) | copy-start | bytes 11796484
  284.9 17.7 %copy-start = (f32[192,2560]{1,0:T(8,128)}, f32[192,2560]{1,0:T(8,128)S(1)}, u32[]{:S(2)}) copy-start(f32[192,2560]{1,0:T(8,128)S(1)} %get-tuple-element.62.local) | copy-start | bytes 5898244
  284.9 17.7 %copy-start.1 = (f32[192,2560]{1,0:T(8,128)}, f32[192,2560]{1,0:T(8,128)S(1)}, u32[]{:S(2)}) copy-start(f32[192,2560]{1,0:T(8,128)S(1)} %get-tuple-element.71.rate_pre) | copy-start | bytes 5898244
  284.9 17.7 %copy-start.4 = (f32[192,2560]{1,0:T(8,128)}, f32[192,2560]{1,0:T(8,128)S(1)}, u32[]{:S(2)}) copy-start(f32[192,2560]{1,0:T(8,128)S(1)} %get-tuple-element.87.input_pre) | copy-start | bytes 5898244
  284.9 17.7 %copy-start.7 = (bf16[192,2560]{1,0:T(8,128)(2,1)}, bf16[192,2560]{1,0:T(8,128)(2,1)S(1)}, u32[]{:S(2)}) copy-start(bf16[192,2560]{1,0:T(8,128)(2,1)S(1)} %get-tuple-element.88.conv) | copy-start | bytes 2949124
  300.6 2.0 copy-start.18
  302.7 8.0 copy-start.20
  310.6 1.3 copy-start.13
  438.1 369.0 %reduce-scatter.5.cloned.1.call-start = ((), (), s32[]{:S(2)}) async-start(), calls=%async_computation.4 | async-start | bytes 4915200 | tf_op jit(solution)/shard_map/reduce_scatter | solution.py:1338
  501.2 43.0 %collective-permute-start.5 = (bf16[160,5760]{1,0:T(8,128)(2,1)}, bf16[160,5760]{1,0:T(8,128)(2,1)}, u32[]{:S(2)}, u32[]{:S(2)}) collective-permute-start(bf16[160,5760]{1,0:T(8,128)(2,1)} %get-tuple-element.82), channel_id=1, source_target_pairs={{0,8},{4,12},{8,0},{12,4},{16,24},{20,28},{24,16},{28,20},{1,9},{5... | collective-permute-start | bytes 5529608 | tf_op jit(solution)/shard_map/ppermute | solution.py:1158
  503.6 42.1 %collective-permute-start.6 = (bf16[160,5760]{1,0:T(8,128)(2,1)}, bf16[160,5760]{1,0:T(8,128)(2,1)}, u32[]{:S(2)}, u32[]{:S(2)}) collective-permute-start(bf16[160,5760]{1,0:T(8,128)(2,1)} %get-tuple-element.83), channel_id=1, source_target_pairs={{0,16},{4,20},{8,24},{12,28},{16,0},{20,4},{24,8},{28,12},{1,17},{... | collective-permute-start | bytes 5529608 | tf_op jit(solution)/shard_map/ppermute | solution.py:1162
  508.2 2.4 copy-start.14
  508.2 2.7 copy-start.23
  513.6 7.4 copy-start.2
  513.6 7.4 copy-start.3
  521.0 35.4 %copy-start.8 = (bf16[192,2560]{1,0:T(8,128)(2,1)S(1)}, bf16[192,2560]{1,0:T(8,128)(2,1)}, u32[]{:S(2)}) copy-start(bf16[192,2560]{1,0:T(8,128)(2,1)} %copy-done.7) | copy-start | bytes 2949124
  533.8 34.0 %copy-start.9 = (bf16[192,2560]{1,0:T(8,128)(2,1)}, bf16[192,2560]{1,0:T(8,128)(2,1)S(1)}, u32[]{:S(2)}) copy-start(bf16[192,2560]{1,0:T(8,128)(2,1)S(1)} %get-tuple-element.91) | copy-start | bytes 2949124
  554.3 42.8 %collective-permute-start.8 = (bf16[160,5760]{1,0:T(8,128)(2,1)}, bf16[160,5760]{1,0:T(8,128)(2,1)}, u32[]{:S(2)}, u32[]{:S(2)}) collective-permute-start(bf16[160,5760]{1,0:T(8,128)(2,1)} %get-tuple-element.97), channel_id=1, source_target_pairs={{0,8},{4,12},{8,0},{12,4},{16,24},{20,28},{24,16},{28,20},{1,9},{5... | collective-permute-start | bytes 5529608 | tf_op jit(solution)/shard_map/ppermute | solution.py:1158
  556.1 42.5 %collective-permute-start.9 = (bf16[160,5760]{1,0:T(8,128)(2,1)}, bf16[160,5760]{1,0:T(8,128)(2,1)}, u32[]{:S(2)}, u32[]{:S(2)}) collective-permute-start(bf16[160,5760]{1,0:T(8,128)(2,1)} %get-tuple-element.98), channel_id=1, source_target_pairs={{0,16},{4,20},{8,24},{12,28},{16,0},{20,4},{24,8},{28,12},{1,17},{... | collective-permute-start | bytes 5529608 | tf_op jit(solution)/shard_map/ppermute | solution.py:1162
  556.4 48.5 %collective-permute-start.4 = (bf16[192,2560]{1,0:T(8,128)(2,1)}, bf16[192,2560]{1,0:T(8,128)(2,1)}, u32[]{:S(2)}, u32[]{:S(2)}) collective-permute-start(bf16[192,2560]{1,0:T(8,128)(2,1)} %add_convert_fusion.3.grad_mix), channel_id=1, source_target_pairs={{0,4},{4,0},{8,12},{12,8},{16,20},{20,16},{24,28},{28,24},{1,5},{5... | collective-permute-start | bytes 2949128 | tf_op jit(solution)/shard_map/ppermute | solution.py:1154
  567.8 1.1 copy-start.5
  568.9 1.1 copy-start.6
  569.9 1.3 copy-start.11
  571.6 4.7 collective-permute-start.7
  572.9 3.3 copy-start.12
  576.2 1.2 copy-start.10
  577.4 21.2 %copy-start.24 = (bf16[320,5760]{1,0:T(8,128)(2,1)S(1)}, bf16[320,5760]{1,0:T(8,128)(2,1)}, u32[]{:S(2)}) copy-start(bf16[320,5760]{1,0:T(8,128)(2,1)} %get-tuple-element.95) | copy-start | bytes 11059204
  792.6 3.1 copy-start.16
  792.6 3.1 copy-start.25
  792.6 3.1 copy-start.26
  795.7 2.0 copy-start.21
  795.7 2.5 copy-start.22
  798.2 4.7 copy-start.29
  798.2 4.7 copy-start.30
  803.5 3.6 copy-start.15
  807.1 2.4 copy-start.28
Sparse Core Ops, SparseCore 0:
  194.1 149.8 all-gather.5
  438.2 69.9 reduce-scatter.2
  510.5 73.0 reduce-scatter.4

commit v13 on v12

--- a/solution.py
+++ b/solution.py
@@ -12,7 +12,7 @@
 bf16 = jnp.bfloat16
 both = ("seq", "fsdp")
 MESH = pl.DeviceIdType.MESH
-TAP, CONV_BIAS, RATE_BIAS, INPUT_BIAS, SOFT, SOFT_SLOPE = 0, 4, 5, 6, 7, 8
+TAP, CONV_BIAS, RATE_BIAS, INPUT_BIAS, SOFT, SOFT_SLOPE, GAIN_ONE, GAIN_TWO = 0, 4, 5, 6, 7, 8, 9, 10
 GELU_C = 0.7978845608028654
 GELU_A = 0.044715
 
@@ -88,6 +88,29 @@
     square = decay * decay
     root = jnp.sqrt(-jnp.tanh(log_decay) * (1.0 + square))
     return rate, decay, square, root, sigmoid(input_pre)
+
+
+def table_kernel(columns, table):
+    rows = columns[...].T[0:16, :].astype(f32)
+    decay_param = rows[7:8, :]
+    fast = jnp.exp(-decay_param)
+    table[0:7, :] = rows[0:7, :]
+    table[7:8, :] = jnp.log1p(fast)
+    table[8:9, :] = -fast / (1.0 + fast)
+    table[9:11, :] = rows[8:10, :]
+    table[11:16, :] = jnp.zeros((5, rows.shape[1]), f32)
+
+
+def small_table(mixer_w, block):
+    model = mixer_w.shape[0]
+    return pl.pallas_call(
+        table_kernel,
+        grid=(1,),
+        in_specs=[pl.BlockSpec((model, 128), lambda i: (0, block))],
+        out_specs=pl.BlockSpec((16, model), lambda i: (0, 0)),
+        out_shape=jax.ShapeDtypeStruct((16, model), f32),
+        name="small_table",
+    )(mixer_w)
 
 
 def mixer_forward(branch, prior, small, rate_w, input_w, conv, rate_pre, input_pre, cum, local, ext):
@@ -792,8 +815,8 @@
 
 
 def scatter_kernel(
-    normed, normed_other, grad_mix, mix_other, mixed, mixed_other, grad_both, rest, mlp_low, mlp_high, mixer_w,
-    tokens, gain, mixer_sum, mlp_back, input_grad,
+    normed, normed_other, grad_mix, mix_other, mixed, mixed_other, grad_gelu, gelu_other, grad_branch, rest,
+    mlp_low, mlp_high, mixer_w, tokens, gain, mixer_sum, mlp_back, input_grad,
     held, cross, near, lined, left_now, both_now, mixed_now, turned, stage, rest_other, back_now, wide_now, gain_now,
     load_sem, core_send, core_recv, wide_sem,
     flow_send, flow_recv, line_send, line_recv, swap_send, swap_recv, own_sem,
@@ -807,7 +830,8 @@
     ff_part = mlp_low.shape[1] // 3
     tok, model = tokens.shape
     half = 4 * rows
-    lru2 = grad_both.shape[1]
+    lru = grad_branch.shape[1]
+    lru2 = 2 * lru
     rest_start = lru2 + mixed.shape[1]
     order = (3 * (1 - z // 2), (2 + 3 * z) % 5, 1 + z % 2, z)
 
@@ -830,14 +854,16 @@
                 (mixed_other, mixed_now.at[other, :]),
                 (normed, left_now.at[0, mine, :]),
                 (normed_other, left_now.at[0, other, :]),
-                (grad_both, both_now.at[mine, :]),
+                (grad_gelu, both_now.at[mine, pl.ds(lru, lru)]),
+                (gelu_other, both_now.at[other, pl.ds(lru, lru)]),
+                (grad_branch, both_now.at[mine, pl.ds(0, lru)]),
             )
         )
     ]
 
     def push(n):
         if n == 0:
-            source, target = grad_both, both_now.at[other, :]
+            source, target = grad_branch, both_now.at[other, pl.ds(0, lru)]
         else:
             source = rest.at[pl.ds(pl.multiple_of(chips[n - 1] * 2 * half + (1 - s % 2) * half, 16), half), :]
             target = rest_other.at[n - 1]
@@ -853,7 +879,7 @@
     def rest_load(q):
         source = rest.at[pl.ds(pl.multiple_of(chips[q] * 2 * half + s % 2 * half, 16), half), :]
         return pltpu.make_async_copy(
-            source, held.at[q, :, pl.ds(rest_start, cols - rest_start)], load_sem.at[7 + q]
+            source, held.at[q, :, pl.ds(rest_start, cols - rest_start)], load_sem.at[9 + q]
         )
 
     def turn(side):
@@ -864,7 +890,7 @@
                 pl.ds(pl.multiple_of(s % 2 * half, 16), half), :
             ]
 
-    def multiply(q, side):
+    def multiply(q, side, first=0, last=None):
         right, start = ((both_now, 0), (mixed_now, lru2))[side]
 
         def one(turn, carry):
@@ -873,7 +899,7 @@
             held[q, :, pl.ds(pl.multiple_of(start + here, 512), 512)] = block.astype(bf16)
             return carry
 
-        lax.fori_loop(0, right.shape[1] // 512, one, 0)
+        lax.fori_loop(first // 512, (right.shape[1] if last is None else last) // 512, one, 0)
 
     def add_rest(q):
         rest_load(q).wait()
@@ -1007,7 +1033,7 @@
     def finish_rows(turn, carry):
         at = pl.ds(pl.multiple_of(turn * 16, 16), 16)
         result = left_now[1, at, :].astype(f32) + norm_back(
-            left_now[0, at, :].astype(f32), gain_now[0:1, :], back_now[at, :]
+            left_now[0, at, :].astype(f32), gain_now[GAIN_ONE : GAIN_ONE + 1, :], back_now[at, :]
         )
         left_now[0, at, :] = result.astype(bf16)
         return carry
@@ -1039,8 +1065,9 @@
     for copy in loads[4:]:
         copy.wait()
     turn(0)
+    multiply(chip_diag, 0, lru)
     push(0).wait_recv()
-    multiply(chip_diag, 0)
+    multiply(chip_diag, 0, 0, lru)
     add_rest(chip_diag)
     for i in range(2):
         flow(i, 0).start()
@@ -1093,17 +1120,17 @@
     done.wait()
 
 
-def scatter(rows_pairs, grad_both, rest, mlp_low, mlp_high, mixer_w, tokens, gain):
+def scatter(rows_pairs, grad_branch, rest, mlp_low, mlp_high, mixer_w, tokens, gain):
     tok, model = tokens.shape
     rows = model // 32
-    mixed = rows_pairs[4]
-    cols = grad_both.shape[1] + mixed.shape[1] + rest.shape[1]
+    lru = grad_branch.shape[1]
+    cols = 3 * lru + rest.shape[1]
     ff_part = mlp_low.shape[1] // 3
     anyspec = pl.BlockSpec(memory_space=pl.ANY)
     dma = pltpu.SemaphoreType.DMA
     return pl.pallas_call(
         scatter_kernel,
-        in_specs=[anyspec] * 13,
+        in_specs=[anyspec] * 15,
         out_specs=[anyspec] * 3,
         out_shape=[
             jax.ShapeDtypeStruct((rows, cols), bf16),
@@ -1116,22 +1143,22 @@
             pltpu.VMEM((2, 4, rows, cols), bf16),
             pltpu.VMEM((5, rows, cols), bf16),
             pltpu.VMEM((2, 2 * tok, model), bf16),
-            pltpu.VMEM((2 * tok, grad_both.shape[1]), bf16),
-            pltpu.VMEM((2 * tok, mixed.shape[1]), bf16),
+            pltpu.VMEM((2 * tok, 2 * lru), bf16),
+            pltpu.VMEM((2 * tok, lru), bf16),
             pltpu.VMEM((2, 16 * rows, 2 * tok), bf16),
             pltpu.VMEM((8 * rows, 2 * tok), bf16),
             pltpu.VMEM((4, 4 * rows, rest.shape[1]), bf16),
             pltpu.VMEM((tok, model), f32),
-            pltpu.VMEM((128, grad_both.shape[1]), bf16),
-            pltpu.VMEM((8, model), f32),
-            dma((11,)), dma((5,)), dma((5,)), dma((4,)),
+            pltpu.VMEM((128, 2 * lru), bf16),
+            pltpu.VMEM(gain.shape, f32),
+            dma((13,)), dma((5,)), dma((5,)), dma((4,)),
             dma((4, 6)), dma((4, 6)), dma((4,)), dma((5,)), dma((3, 3)), dma((3, 3)), dma((4,)),
         ],
         compiler_params=pltpu.CompilerParams(
             collective_id=2, has_side_effects=True, vmem_limit_bytes=62 * 1024 * 1024
         ),
         name="scatter_gradients",
-    )(*rows_pairs, grad_both, rest, mlp_low, mlp_high, mixer_w, tokens, gain)
+    )(*rows_pairs, grad_branch, rest, mlp_low, mlp_high, mixer_w, tokens, gain)
 
 
 def gather_plain(mixer, gate, up, down):
@@ -1255,23 +1282,11 @@
     grad_out_late = lax.optimization_barrier((grad_out, mlp_mine))[0]
     if custom:
         grad_pieces = from_line(grad_out_late)
-    smalls = lax.optimization_barrier(mixer_w[:, 2 * width : 2 * width + 128])
     wide = mixer_w[:, 128 + 2 * width : 128 + 2 * width + 2 * lru]
     proj_out = mixer_w[:, 128 + 2 * width + 2 * lru :]
 
-    table = smalls[:, :small_count].astype(f32).T
-    param_decay = table[margin + 4]
-    gain_one = table[margin + 5]
-    gain_two = table[margin + 6]
-    small = jnp.concatenate(
-        [
-            table[: margin + 4],
-            jax.nn.softplus(-param_decay)[None],
-            -jax.nn.sigmoid(-param_decay)[None],
-            jnp.zeros((16 - margin - 6, lru), f32),
-        ],
-        axis=0,
-    )
+    small = small_table(mixer_w, 2 * width // 128)
+    gain_one, gain_two = small[GAIN_ONE], small[GAIN_TWO]
 
     normed = norm_rows(tokens, gain_one).astype(bf16)
     both_pre = mm(normed, wide, ((1,), (0,)))
@@ -1357,6 +1372,8 @@
         from_beside_high, from_across_low, pair_grad = lax.optimization_barrier(
             (from_beside_high, from_across_low, pair_grad)
         )
+    if custom:
+        gelu_other = swap_cores(grad_gelu_pre)
     incoming = prefix((cum[-1], pair_grad[0]), "seq", True)
     if custom:
         beside_low, across_high, incoming = lax.optimization_barrier((beside_low, across_high, incoming))
@@ -1383,15 +1400,13 @@
     vectors = jnp.pad(sums.T, ((0, 0), (0, 128 - sums.shape[0]))).astype(bf16)
     rest = jnp.concatenate([rate_w_grad, input_w_grad, vectors], axis=1)
     if custom:
-        mlp_parts = (
-            (mine[:half], from_across_low, from_beside_low),
-            (mine[half:], from_across_high, from_beside_high),
-        )
-        low, high = [sum(part.astype(f32) for part in parts).astype(bf16) for parts in mlp_parts]
-        gain_rows = jnp.broadcast_to(gain_one[None], (8, model))
+        low = add_low(mine[:half], from_across_low)
+        high = add_low(mine[half:], from_beside_high)
+        low, high, grad_branch = lax.optimization_barrier((low, high, grad_branch))
+        low, high = add_low(low, from_beside_low), add_low(high, from_across_high)
         mixer_sum, mlp_back, input_grad = scatter(
-            (normed, first_other, grad_mix, mix_other, mixed, mixed_other),
-            grad_both, rest, low, high, mixer_w, block_input[0], gain_rows,
+            (normed, first_other, grad_mix, mix_other, mixed, mixed_other, grad_gelu_pre, gelu_other),
+            grad_branch, rest, low, high, mixer_w, block_input[0], small,
         )
     else:
         mixer_sum, mlp_back = scatter_plain(normed, grad_both, grad_mix, mixed, rest, mlp_sum)

time: 827 us -> 831 us (level)
  local copies, waits for them, and re-layouts: 65.3 us -> 10.6 us
  waiting for transfers between devices: 36.6 us -> 77.3 us
  Pallas kernels: 592 us -> 612 us
    pallas_call x1 -> x0, local copies, waits for them, and re-layouts: 50.7 us -> none  [gather(): pl.pallas_call(gather_kernel, in_specs=[anyspec] * 7, out_specs=[anyspec]...]
    ppermute x3, waiting for transfers between devices: 0.01 us -> 31 us  [from_line(): lax.ppermute(shard, 'fsdp', [(i, (i + k) % count) for i in range(count)])]
    ppermute x2, waiting for transfers between devices: 2.85 us -> 31.8 us  [swap_across(): return lax.ppermute(shard, 'seq', [(i, i ^ 4) for i in range(8)])]
    pallas_call x1, Pallas kernels: 72.9 us -> 91.7 us  [gather_rows(): pl.pallas_call(rows_kernel, in_specs=[anyspec] * 7, out_specs=[anyspec] *...]
    ppermute x2, waiting for transfers between devices: 28.7 us -> 11.4 us  [swap_beside(): return lax.ppermute(shard, 'seq', [(i, i ^ 2) for i in range(8)])]
    pallas_call x1 -> x2, Pallas kernels: 187 us -> 186 us  [the longest x1 184 us: scatter(): pl.pallas_call(scatter_kernel, in_specs=[anyspec] * 15, out_specs=[anyspe...]
  transfers between devices with their start and end apart: 13 -> 14, of which waited for: 6 -> 5; matrix products, arithmetic and copies ran while one was open for 15% -> 9% of each run, Pallas kernels for 44% -> 46%
where the time goes in v13:
time: 831 us; the launch traced here: 824 us
  Pallas kernels  612 us (74%)
  waiting for transfers between devices  77.3 us (9%)
  other arithmetic  39.9 us (5%)
  matrix products  29.7 us (4%)
  blocking collectives  20.3 us (2%)
  starting transfers between devices  19.5 us (2%)
  between operations  14.6 us (2%)
  local copies, waits for them, and re-layouts  10.6 us (1%)
    pallas_call x1, Pallas kernels, scatter(): pl.pallas_call(scatter_kernel, in_specs=[anyspec] * 15, out_specs=[anyspe...  184 us
    pallas_call x1, Pallas kernels, gather(): pl.pallas_call(gather_kernel, in_specs=[anyspec] * 7, out_specs=[anyspec]...  183 us
    pallas_call x1, Pallas kernels, gather_rows(): pl.pallas_call(rows_kernel, in_specs=[anyspec] * 7, out_specs=[anyspec] *...  91.7 us
    pallas_call x1, Pallas kernels, shared_products(): pl.pallas_call(shared_products_kernel, grid=(3,), in_specs=[anyspec] * 5...  65.2 us
    pallas_call x1, Pallas kernels, feed_forward(): pl.pallas_call(feed_forward_kernel, grid=(2,), in_specs=[block, block, an...  52.1 us
    pallas_call x3, Pallas kernels, call_heads(): pl.pallas_call(kernel, grid=(heads,), in_specs=in_specs, out_specs=out_sp...  33.9 us
    ppermute x2, waiting for transfers between devices, swap_across(): return lax.ppermute(shard, 'seq', [(i, i ^ 4) for i in range(8)])  31.8 us
    ppermute x3, waiting for transfers between devices, from_line(): lax.ppermute(shard, 'fsdp', [(i, (i + k) % count) for i in range(count)])  31 us
  transfers between devices with their start and end apart: 14, of which 5 were waited for; matrix products, arithmetic and copies ran while one was open for 9% of the time, Pallas kernels for 46%

profile of v13, /device:TPU:0, one launch (start us, length us, event | category | flops | bytes accessed | tf_op | source)
XLA Modules:
  0.0 824.1 jit_solution(5763908875289124597)
XLA Ops:
  7.2 0.8 slice_bitcast_fusion.1
  8.1 1.4 stack.33
  9.6 1.5 fusion.25.first
  11.1 182.9 %gather_weights.1 = (bf16[2560,8320]{1,0:T(8,128)(2,1)}, bf16[320,5760]{1,0:T(8,128)(2,1)}) custom-call(bf16[80,640]{1,0:T(8,128)(2,1)} %fusion.25.first, bf16[80,2560]{1,0:T(8,128)(2,1)} %branch.1, bf16[80,2560]{1,0:T(8,128)(2,1)} %gelu.1, bf16[80,2560]{1,0:T(8,128)(2,1)} %outer.1, bf16[80,7680]{1,0:T(8,128)(2,1)} %gate.1, bf16[80,7680]{1,0:T(8,128)(2,1)} %up.1, ...), custom_call_target="tpu_custom_call" | custom-call | tf_op jit(solution)/shard_map/gather_weights/pallas_call | solution.py:374
  194.1 2.1 small_table.1.small.gain
  196.1 1.0 slice_reduce_fusion.18
  197.8 14.3 %fusion.35 = (bf16[192,5120]{1,0:T(8,128)(2,1)S(1)}, f32[192,5120]{1,0:T(8,128)}) fusion(bf16[192,2560]{1,0:T(8,128)(2,1)S(1)} %fusion.13.first.normed, bf16[2560,8320]{1,0:T(8,128)(2,1)} %get-tuple-element.64.columns.rate_w.input_w.mixer_w), kind=kOutput, calls=%fused_computation.111 | convolution fusion | flops 5034147840 | bytes 33095680 | tf_op jit(solution)/shard_map/dot_general | solution.py:62
  212.1 2.4 collective-permute-start
  214.6 6.8 collective-permute-start.1
  221.4 3.6 collective-permute-start.2
  225.1 9.5 %mixer_forward.1 = (bf16[192,2560]{1,0:T(8,128)(2,1)S(1)}, f32[192,2560]{1,0:T(8,128)S(1)}, f32[192,2560]{1,0:T(8,128)S(1)}, f32[192,2560]{1,0:T(8,128)S(1)}, f32[192,2560]{1,0:T(8,128)S(1)}) custom-call(bf16[192,2560]{1,0:T(8,128)(2,1)S(1)} %slice.241.branch, f32[8,2560]{1,0:T(8,128)S(1)} %pad_convert_fusion.prior, f32[16,2560]{1,0:T(8,128)S(1)} %copy-done.4, ...), custom_call_target="tpu_custom_call" | custom-call | flops 1 | bytes 1 | tf_op jit(solution)/shard_map/mixer_forward/pallas_call | solution.py:1224
  234.8 10.8 %all-gather.2 = f32[8,2,2560]{2,1,0:T(2,128)S(1)} all-gather(f32[1,2,2560]{2,1,0:T(2,128)S(1)} %fusion.26), channel_id=2, replica_groups=mesh['seq'=8,'fsdp'=4] {'seq'}, dimensions={0}, use_global_device_ids=true | all-gather | bytes 184320 | tf_op jit(solution)/shard_map/all_gather | solution.py:29
  246.0 2.0 fusion.33
  248.1 7.9 multiply_reduce_fusion.3
  256.0 1.2 copy-done.12
  257.3 1.2 multiply_convert_fusion.normed
  258.4 31.0 %collective-permute-done.2.grad2 = bf16[192,2560]{1,0:T(8,128)(2,1)} collective-permute-done((bf16[192,2560]{1,0:T(8,128)(2,1)}, bf16[192,2560]{1,0:T(8,128)(2,1)}, u32[]{:S(2)}, u32[]{:S(2)}) %collective-permute-start.2) | collective-permute-done | bytes 983072 | tf_op jit(solution)/shard_map/ppermute | solution.py:1175
  289.4 91.7 %gather_rows.1 = (bf16[768,2560]{1,0:T(8,128)(2,1)}, bf16[768,2560]{1,0:T(8,128)(2,1)}, bf16[768,2560]{1,0:T(8,128)(2,1)}, bf16[768,2560]{1,0:T(8,128)(2,1)}, bf...) custom-call(bf16[192,2560]{1,0:T(8,128)(2,1)} %multiply_convert_fusion.normed, bf16[192,2560]{1,0:T(8,128)(2,1)} %bitcast.12.grad0, ...), custom_call_target="tpu_custom_call" | custom-call | tf_op jit(solution)/shard_map/gather_rows/pallas_call | solution.py:501
  381.2 52.1 %feed_forward.1 = (bf16[768,1920]{1,0:T(8,128)(2,1)}, bf16[768,1920]{1,0:T(8,128)(2,1)}, bf16[768,3840]{1,0:T(8,128)(2,1)}, bf16[768,3840]{1,0:T(8,128)(2,1)}, bf16[768,2560]{1,0:T(8,128)(2,1)}) custom-call(bf16[768,2560]{1,0:T(8,128)(2,1)} %get-tuple-element.70.normed, bf16[768,2560]{1,0:T(8,128)(2,1)} %get-tuple-element.71.grad_out.grad, ...), custom_call_target="tpu_custom_call" | custom-call | tf_op jit(solution)/shard_map/feed_forward/pallas_call | solution.py:608
  433.3 65.2 %feed_forward_products.1 = (bf16[160,5760]{1,0:T(8,128)(2,1)}, bf16[160,5760]{1,0:T(8,128)(2,1)}, bf16[320,5760]{1,0:T(8,128)(2,1)}, bf16[160,5760]{1,0:T(8,128)...) custom-call(bf16[768,2560]{1,0:T(8,128)(2,1)} %get-tuple-element.70.normed, ...), custom_call_target="tpu_custom_call" | custom-call | tf_op jit(solution)/shard_map/feed_forward_products/pallas_call | solution.py:792
  498.7 2.1 collective-permute-start.7
  500.8 3.0 reduce-scatter.3.cloned.1.call-done
  503.8 2.3 multiply_reduce_fusion.2
  506.5 2.8 add_convert_fusion.5.grad_mix
  509.3 7.4 fusion.2.grad_mixed
  516.7 12.7 %mixer_backward_scan.1 = (bf16[192,2560]{1,0:T(8,128)(2,1)}, f32[192,2560]{1,0:T(8,128)S(1)}, f32[192,2560]{1,0:T(8,128)S(1)}, f32[8,2560]{1,0:T(8,128)S(1)}) custom-call(f32[192,2560]{1,0:T(8,128)S(1)} %fusion.2.grad_mixed, f32[192,2560]{1,0:T(8,128)S(1)} %copy-done.3, f32[192,2560]{1,0:T(8,128)S(1)} %copy-done.2, f32[192,2560]{1,0:T(8,128)S(1)} %get-tuple-element.66.cum, ...), custom_call_target="tpu_custom_call" | custom-call | flops 1 | bytes 1 | tf_op jit(solution)/shard_map/mixer_backward_scan/pallas_call | solution.py:1224
  529.5 11.4 %collective-permute-done.6 = bf16[160,5760]{1,0:T(8,128)(2,1)} collective-permute-done((bf16[160,5760]{1,0:T(8,128)(2,1)}, bf16[160,5760]{1,0:T(8,128)(2,1)}, u32[]{:S(2)}, u32[]{:S(2)}) %collective-permute-start.6) | collective-permute-done | bytes 1843232 | tf_op jit(solution)/shard_map/ppermute | solution.py:1185
  541.1 9.5 %all-gather.3 = f32[8,2,2560]{2,1,0:T(2,128)S(1)} all-gather(f32[1,2,2560]{2,1,0:T(2,128)S(1)} %fusion.27), channel_id=3, replica_groups=mesh['seq'=8,'fsdp'=4] {'seq'}, dimensions={0}, use_global_device_ids=true | all-gather | bytes 184320 | tf_op jit(solution)/shard_map/all_gather | solution.py:29
  551.1 11.6 %mixer_backward.1 = (f32[192,2560]{1,0:T(8,128)S(1)}, f32[8,2560]{1,0:T(8,128)S(1)}, bf16[2560,256]{1,0:T(8,128)(2,1)S(1)}, bf16[2560,256]{1,0:T(8,128)(2,1)S(1)}, f32[8,2560]{1,0:T(8,128)S(1)}) custom-call(f32[192,2560]{1,0:T(8,128)S(1)} %get-tuple-element.88.rev_cum, f32[192,2560]{1,0:T(8,128)S(1)} %get-tuple-element.89.rev_grad, ...), custom_call_target="tpu_custom_call" | custom-call | flops 1 | bytes 1 | tf_op jit(solution)/shard_map/mixer_backward/pallas_call | solution.py:1224
  562.8 1.3 collective-permute-start.8
  564.1 2.5 collective-permute-start.10
  567.1 4.2 add_convert_fusion.2
  571.6 3.2 fusion.10.rest
  575.0 1.0 pad_maximum_fusion.grad_branch
  576.0 31.6 %collective-permute-done.10 = bf16[160,5760]{1,0:T(8,128)(2,1)} collective-permute-done((bf16[160,5760]{1,0:T(8,128)(2,1)}, bf16[160,5760]{1,0:T(8,128)(2,1)}, u32[]{:S(2)}, u32[]{:S(2)}) %collective-permute-start.10) | collective-permute-done | bytes 1843232 | tf_op jit(solution)/shard_map/ppermute | solution.py:1189
  607.7 3.3 add_convert_fusion.mlp_high
  610.9 3.2 add_convert_fusion.1.mlp_low
  614.1 184.4 %scatter_gradients.1 = (bf16[80,8320]{1,0:T(8,128)(2,1)}, bf16[3,80,7680]{2,1,0:T(8,128)(2,1)}, bf16[192,2560]{1,0:T(8,128)(2,1)}) custom-call(bf16[192,2560]{1,0:T(8,128)(2,1)} %copy-done.18, bf16[192,2560]{1,0:T(8,128)(2,1)} %get-tuple-element.69.normed_other, bf16[192,2560]{1,0:T(8,128)(2,1)} %add_convert_fusion.5.grad_mix, ...), custom_call_target="tpu_custom_call" | custom-call | tf_op jit(solution)/shard_map/scatter_gradients/pallas_call | solution.py:1131
  798.5 1.6 convert_element_type.132
  800.2 0.7 copy.60
  800.8 0.7 slice_reduce_fusion
  801.6 1.6 multiply_reduce_fusion.4
  803.5 0.6 copy-done.22
  804.1 4.7 multiply_reduce_fusion
  809.4 1.6 fusion.34
  811.0 2.9 bitcast_convert_fusion
  813.9 2.4 fusion.23
  816.4 0.9 copy.62
  (108 shorter events, 4.7 us)
Async XLA Ops:
  7.2 374.0 %all-gather.6.cloned.1.call-start = ((), (), s32[]{:S(2)}) async-start(), calls=%async_computation.2 | async-start | bytes 33177600 | tf_op jit(solution)/shard_map/all_gather | solution.py:1281
  194.0 309.8 %reduce-scatter.3.cloned.1.call-start = ((), (), s32[]{:S(2)}) async-start(), calls=%async_computation.3 | async-start | bytes 4915200 | tf_op jit(solution)/shard_map/reduce_scatter | solution.py:1335
  194.1 3.1 copy-start.16
  197.8 14.4 %copy-start.18 = (bf16[192,2560]{1,0:T(8,128)(2,1)}, bf16[192,2560]{1,0:T(8,128)(2,1)S(1)}, u32[]{:S(2)}) copy-start(bf16[192,2560]{1,0:T(8,128)(2,1)S(1)} %fusion.13.first.normed) | copy-start | bytes 2949124
  212.1 13.0 %copy-start.4 = (f32[16,2560]{1,0:T(8,128)S(1)}, f32[16,2560]{1,0:T(8,128)}, u32[]{:S(2)}) copy-start(f32[16,2560]{1,0:T(8,128)} %small_table.1.small.gain) | copy-start | bytes 491524
  212.1 12.9 %collective-permute-start = (bf16[3,2560]{1,0:T(4,128)(2,1)S(1)}, bf16[3,2560]{1,0:T(4,128)(2,1)S(1)}, u32[]{:S(2)}, u32[]{:S(2)}) collective-permute-start(bf16[3,2560]{1,0:T(4,128)(2,1)S(1)} %slice.242), channel_id=1, source_target_pairs={{0,4},{4,8},{8,12},{12,16},{16,20},{20,24},{24,28},{1,5},{5,9},{9,... | collective-permute-start | bytes 46088 | tf_op jit(solution)/shard_map/ppermute | solution.py:23
  214.6 43.9 %collective-permute-start.1 = (bf16[192,2560]{1,0:T(8,128)(2,1)}, bf16[192,2560]{1,0:T(8,128)(2,1)}, u32[]{:S(2)}, u32[]{:S(2)}) collective-permute-start(bf16[192,2560]{1,0:T(8,128)(2,1)} %bitcast.12.grad0), channel_id=1, source_target_pairs={{0,1},{1,2},{2,3},{3,0},{4,5},{5,6},{6,7},{7,4},{8,9},{9,10},{10,1... | collective-permute-start | bytes 2949128 | tf_op jit(solution)/shard_map/ppermute | solution.py:1175
  221.4 68.0 %collective-permute-start.2 = (bf16[192,2560]{1,0:T(8,128)(2,1)}, bf16[192,2560]{1,0:T(8,128)(2,1)}, u32[]{:S(2)}, u32[]{:S(2)}) collective-permute-start(bf16[192,2560]{1,0:T(8,128)(2,1)} %bitcast.12.grad0), channel_id=1, source_target_pairs={{0,2},{1,3},{2,0},{3,1},{4,6},{5,7},{6,4},{7,5},{8,10},{9,11},{10,... | collective-permute-start | bytes 2949128 | tf_op jit(solution)/shard_map/ppermute | solution.py:1175
  225.0 64.4 %collective-permute-start.3 = (bf16[192,2560]{1,0:T(8,128)(2,1)}, bf16[192,2560]{1,0:T(8,128)(2,1)}, u32[]{:S(2)}, u32[]{:S(2)}) collective-permute-start(bf16[192,2560]{1,0:T(8,128)(2,1)} %bitcast.12.grad0), channel_id=1, source_target_pairs={{0,3},{1,0},{2,1},{3,2},{4,7},{5,4},{6,5},{7,6},{8,11},{9,8},{10,9... | collective-permute-start | bytes 2949128 | tf_op jit(solution)/shard_map/ppermute | solution.py:1175
  225.1 20.9 %copy-start.27 = (f32[192,5120]{1,0:T(8,128)S(1)}, f32[192,5120]{1,0:T(8,128)}, u32[]{:S(2)}) copy-start(f32[192,5120]{1,0:T(8,128)} %get-tuple-element.222) | copy-start | bytes 11796484
  234.7 13.3 %copy-start = (f32[192,2560]{1,0:T(8,128)}, f32[192,2560]{1,0:T(8,128)S(1)}, u32[]{:S(2)}) copy-start(f32[192,2560]{1,0:T(8,128)S(1)} %get-tuple-element.65.local) | copy-start | bytes 5898244
  234.7 13.3 %copy-start.1 = (f32[192,2560]{1,0:T(8,128)}, f32[192,2560]{1,0:T(8,128)S(1)}, u32[]{:S(2)}) copy-start(f32[192,2560]{1,0:T(8,128)S(1)} %get-tuple-element.74.rate_pre) | copy-start | bytes 5898244
  234.7 13.3 %copy-start.5 = (f32[192,2560]{1,0:T(8,128)}, f32[192,2560]{1,0:T(8,128)S(1)}, u32[]{:S(2)}) copy-start(f32[192,2560]{1,0:T(8,128)S(1)} %get-tuple-element.94.input_pre) | copy-start | bytes 5898244
  234.7 13.3 %copy-start.8 = (bf16[192,2560]{1,0:T(8,128)(2,1)}, bf16[192,2560]{1,0:T(8,128)(2,1)S(1)}, u32[]{:S(2)}) copy-start(bf16[192,2560]{1,0:T(8,128)(2,1)S(1)} %get-tuple-element.95.conv) | copy-start | bytes 2949124
  246.0 2.0 copy-start.17
  248.0 8.0 copy-start.19
  256.0 1.3 copy-start.12
  433.3 380.7 %reduce-scatter.5.cloned.1.call-start = ((), (), s32[]{:S(2)}) async-start(), calls=%async_computation.4 | async-start | bytes 4915200 | tf_op jit(solution)/shard_map/reduce_scatter | solution.py:1353
  498.5 42.4 %collective-permute-start.6 = (bf16[160,5760]{1,0:T(8,128)(2,1)}, bf16[160,5760]{1,0:T(8,128)(2,1)}, u32[]{:S(2)}, u32[]{:S(2)}) collective-permute-start(bf16[160,5760]{1,0:T(8,128)(2,1)} %get-tuple-element.83), channel_id=1, source_target_pairs={{0,8},{4,12},{8,0},{12,4},{16,24},{20,28},{24,16},{28,20},{1,9},{5... | collective-permute-start | bytes 5529608 | tf_op jit(solution)/shard_map/ppermute | solution.py:1185
  498.7 42.4 %collective-permute-start.7 = (bf16[160,5760]{1,0:T(8,128)(2,1)}, bf16[160,5760]{1,0:T(8,128)(2,1)}, u32[]{:S(2)}, u32[]{:S(2)}) collective-permute-start(bf16[160,5760]{1,0:T(8,128)(2,1)} %get-tuple-element.84), channel_id=1, source_target_pairs={{0,16},{4,20},{8,24},{12,28},{16,0},{20,4},{24,8},{28,12},{1,17},{... | collective-permute-start | bytes 5529608 | tf_op jit(solution)/shard_map/ppermute | solution.py:1189
  503.8 2.4 copy-start.13
  503.8 2.7 copy-start.23
  509.3 7.4 copy-start.2
  509.3 7.4 copy-start.3
  509.3 104.8 %collective-permute-start.4 = (bf16[192,2560]{1,0:T(8,128)(2,1)}, bf16[192,2560]{1,0:T(8,128)(2,1)}, u32[]{:S(2)}, u32[]{:S(2)}) collective-permute-start(bf16[192,2560]{1,0:T(8,128)(2,1)} %add_convert_fusion.5.grad_mix), channel_id=1, source_target_pairs={{0,4},{4,0},{8,12},{12,8},{16,20},{20,16},{24,28},{28,24},{1,5},{5... | collective-permute-start | bytes 2949128 | tf_op jit(solution)/shard_map/ppermute | solution.py:1181
  516.7 34.3 %copy-start.9 = (bf16[192,2560]{1,0:T(8,128)(2,1)S(1)}, bf16[192,2560]{1,0:T(8,128)(2,1)}, u32[]{:S(2)}) copy-start(bf16[192,2560]{1,0:T(8,128)(2,1)} %copy-done.8) | copy-start | bytes 2949124
  551.1 16.0 %copy-start.24 = (bf16[320,5760]{1,0:T(8,128)(2,1)S(1)}, bf16[320,5760]{1,0:T(8,128)(2,1)}, u32[]{:S(2)}) copy-start(bf16[320,5760]{1,0:T(8,128)(2,1)} %get-tuple-element.82) | copy-start | bytes 11059204
  562.7 8.6 %copy-start.6 = (bf16[2560,256]{1,0:T(8,128)(2,1)}, bf16[2560,256]{1,0:T(8,128)(2,1)S(1)}, u32[]{:S(2)}) copy-start(bf16[2560,256]{1,0:T(8,128)(2,1)S(1)} %get-tuple-element.99) | copy-start | bytes 3932164
  562.7 8.6 %copy-start.7 = (bf16[2560,256]{1,0:T(8,128)(2,1)}, bf16[2560,256]{1,0:T(8,128)(2,1)S(1)}, u32[]{:S(2)}) copy-start(bf16[2560,256]{1,0:T(8,128)(2,1)S(1)} %get-tuple-element.100) | copy-start | bytes 3932164
  562.7 8.5 %copy-start.10 = (f32[192,2560]{1,0:T(8,128)}, f32[192,2560]{1,0:T(8,128)S(1)}, u32[]{:S(2)}) copy-start(f32[192,2560]{1,0:T(8,128)S(1)} %get-tuple-element.96) | copy-start | bytes 5898244
  562.8 12.2 %collective-permute-start.8 = (f32[3,2560]{1,0:T(4,128)S(1)}, f32[3,2560]{1,0:T(4,128)S(1)}, u32[]{:S(2)}, u32[]{:S(2)}) collective-permute-start(f32[3,2560]{1,0:T(4,128)S(1)} %slice.231), channel_id=1, source_target_pairs={{4,0},{8,4},{12,8},{16,12},{20,16},{24,20},{28,24},{5,1},{9,5},{13... | collective-permute-start | bytes 92168 | tf_op jit(solution)/shard_map/ppermute | solution.py:23
  564.1 43.6 %collective-permute-start.10 = (bf16[160,5760]{1,0:T(8,128)(2,1)}, bf16[160,5760]{1,0:T(8,128)(2,1)}, u32[]{:S(2)}, u32[]{:S(2)}) collective-permute-start(bf16[160,5760]{1,0:T(8,128)(2,1)} %get-tuple-element.105), channel_id=1, source_target_pairs={{0,16},{4,20},{8,24},{12,28},{16,0},{20,4},{24,8},{28,12},{1,17},{... | collective-permute-start | bytes 5529608 | tf_op jit(solution)/shard_map/ppermute | solution.py:1189
  566.5 44.4 %collective-permute-start.9 = (bf16[160,5760]{1,0:T(8,128)(2,1)}, bf16[160,5760]{1,0:T(8,128)(2,1)}, u32[]{:S(2)}, u32[]{:S(2)}) collective-permute-start(bf16[160,5760]{1,0:T(8,128)(2,1)} %get-tuple-element.103), channel_id=1, source_target_pairs={{0,8},{4,12},{8,0},{12,4},{16,24},{20,28},{24,16},{28,20},{1,9},{5... | collective-permute-start | bytes 5529608 | tf_op jit(solution)/shard_map/ppermute | solution.py:1185
  567.1 47.0 %collective-permute-start.5 = (bf16[192,2560]{1,0:T(8,128)(2,1)}, bf16[192,2560]{1,0:T(8,128)(2,1)}, u32[]{:S(2)}, u32[]{:S(2)}) collective-permute-start(bf16[192,2560]{1,0:T(8,128)(2,1)} %get-tuple-element.75.grad_gelu), channel_id=1, source_target_pairs={{0,4},{4,0},{8,12},{12,8},{16,20},{20,16},{24,28},{28,24},{1,5},{5... | collective-permute-start | bytes 2949128 | tf_op jit(solution)/shard_map/ppermute | solution.py:1181
  571.6 3.3 copy-start.11
  574.9 32.8 %copy-start.20 = (bf16[160,5760]{1,0:T(8,128)(2,1)S(1)}, bf16[160,5760]{1,0:T(8,128)(2,1)}, u32[]{:S(2)}) copy-start(bf16[160,5760]{1,0:T(8,128)(2,1)} %get-tuple-element.104) | copy-start | bytes 5529604
  798.5 3.1 copy-start.15
  798.5 3.1 copy-start.25
  798.5 3.1 copy-start.26
  801.6 2.0 copy-start.21
  801.6 2.5 copy-start.22
  804.1 4.7 copy-start.29
  804.1 4.7 copy-start.30
  809.4 4.5 copy-start.14
  813.9 2.4 copy-start.28
Sparse Core Ops, SparseCore 0:
  194.1 149.1 all-gather.5
  433.4 70.3 reduce-scatter.2
  506.1 73.0 reduce-scatter.4

commit v14 on v13

--- a/solution.py
+++ b/solution.py
@@ -46,9 +46,8 @@
     return inverse * scaled - values * (inverse * inverse * inverse * shared)
 
 
-def gain_back(gain, *pairs):
-    total = sum(jnp.sum(weight.astype(f32) * grad, axis=1) for weight, grad in pairs)
-    return total / gain.astype(f32)
+def gain_back(*pairs):
+    return sum(jnp.sum(weight.astype(f32) * grad, axis=1) for weight, grad in pairs)
 
 
 def gelu_parts(x):
@@ -111,6 +110,100 @@
         out_shape=jax.ShapeDtypeStruct((16, model), f32),
         name="small_table",
     )(mixer_w)
+
+
+def mixer_in_kernel(tokens, table, weights, normed, branch, gelu_pre):
+    step = pl.program_id(0)
+
+    @pl.when(step == 0)
+    def _():
+        normed[...] = norm_rows(tokens[...].astype(f32), table[GAIN_ONE : GAIN_ONE + 1, :]).astype(bf16)
+
+    product = mm(normed[...], weights[...], ((1,), (0,)))
+    half = pl.num_programs(0) // 2
+
+    @pl.when(step < half)
+    def _():
+        branch[...] = product.astype(bf16)
+
+    @pl.when(step >= half)
+    def _():
+        gelu_pre[...] = product
+
+
+def mixer_in(tokens, table, mixer_w, lru, start):
+    tok, model = tokens.shape
+    tile = start
+    tiles = lru // tile
+    return pl.pallas_call(
+        mixer_in_kernel,
+        grid=(2 * tiles,),
+        in_specs=[
+            pl.BlockSpec((tok, model), lambda j: (0, 0)),
+            pl.BlockSpec(table.shape, lambda j: (0, 0)),
+            pl.BlockSpec((model, tile), lambda j: (0, 1 + j)),
+        ],
+        out_specs=[
+            pl.BlockSpec((tok, model), lambda j: (0, 0)),
+            pl.BlockSpec((tok, tile), lambda j: (0, jnp.minimum(j, tiles - 1))),
+            pl.BlockSpec((tok, tile), lambda j: (0, jnp.maximum(j - tiles, 0))),
+        ],
+        out_shape=[
+            jax.ShapeDtypeStruct((tok, model), bf16),
+            jax.ShapeDtypeStruct((tok, lru), bf16),
+            jax.ShapeDtypeStruct((tok, lru), f32),
+        ],
+        compiler_params=pltpu.CompilerParams(vmem_limit_bytes=40 * 1024 * 1024),
+        cost_estimate=pl.CostEstimate(flops=1, bytes_accessed=1, transcendentals=0),
+        name="mixer_in",
+    )(tokens, table, mixer_w)
+
+
+def finish_kernel(mixer, mlp, branch, gelu, gate, up, dbranch, dgelu, dout, drate, dinput, dgate, dup, ddown, totals):
+    lru = branch.shape[1]
+    width = drate.shape[1]
+    ff = gate.shape[1]
+
+    def met(weight, grad, cols):
+        def one(turn, carry):
+            here = pl.ds(pl.multiple_of(turn * 512, 512), 512)
+            return carry + jnp.sum(weight[:, here].astype(f32) * grad[:, here], axis=1, keepdims=True)
+
+        return lax.fori_loop(0, cols // 512, one, jnp.zeros((weight.shape[0], 1), f32))
+
+    start = 0
+    for grad in (dbranch, dgelu, dout, drate, dinput):
+        size = grad.shape[1]
+        grad[...] = mixer[:, start : start + size].astype(f32)
+        start += size
+    for m, grad in enumerate((dgate, dup, ddown)):
+        grad[...] = mlp[m].astype(f32)
+    first = met(branch, dbranch, lru) + met(gelu, dgelu, lru)
+    second = met(gate, dgate, ff) + met(up, dup, ff)
+    totals[...] = jnp.concatenate([jnp.broadcast_to(first, (first.shape[0], 128)), jnp.broadcast_to(second, (second.shape[0], 128))], axis=1)
+
+
+def finish(mixer, mlp, branch, gelu, gate, up, width):
+    rows, ff = gate.shape
+    lru = branch.shape[1]
+    step = 16
+
+    def spec(cols):
+        return pl.BlockSpec((step, cols), lambda i: (i, 0))
+
+    sizes = [lru, lru, lru, width, width, ff, ff, ff, 256]
+    return pl.pallas_call(
+        finish_kernel,
+        grid=(rows // step,),
+        in_specs=[
+            spec(mixer.shape[1]), pl.BlockSpec((3, step, ff), lambda i: (0, i, 0)),
+            spec(lru), spec(lru), spec(ff), spec(ff),
+        ],
+        out_specs=[spec(cols) for cols in sizes],
+        out_shape=[jax.ShapeDtypeStruct((rows, cols), f32) for cols in sizes],
+        compiler_params=pltpu.CompilerParams(vmem_limit_bytes=40 * 1024 * 1024),
+        name="finish_gradients",
+    )(mixer, mlp, branch, gelu, gate, up)
 
 
 def mixer_forward(branch, prior, small, rate_w, input_w, conv, rate_pre, input_pre, cum, local, ext):
@@ -1288,10 +1381,7 @@
     small = small_table(mixer_w, 2 * width // 128)
     gain_one, gain_two = small[GAIN_ONE], small[GAIN_TWO]
 
-    normed = norm_rows(tokens, gain_one).astype(bf16)
-    both_pre = mm(normed, wide, ((1,), (0,)))
-    branch = both_pre[:, :lru].astype(bf16)
-    gelu_pre = both_pre[:, lru:]
+    normed, branch, gelu_pre = mixer_in(block_input[0], small, mixer_w, lru, 2 * width + 128)
     prior = from_behind(branch[tok_count - margin :], "seq", 1).astype(f32)
     prior = jnp.concatenate([jnp.zeros((8 - margin, lru), f32), prior], axis=0)
     conv, rate_pre, input_pre, cum, local = call_heads(
@@ -1403,6 +1493,7 @@
         low = add_low(mine[:half], from_across_low)
         high = add_low(mine[half:], from_beside_high)
         low, high, grad_branch = lax.optimization_barrier((low, high, grad_branch))
+        middle = lax.optimization_barrier((middle, low))[0]
         low, high = add_low(low, from_beside_low), add_low(high, from_across_high)
         mixer_sum, mlp_back, input_grad = scatter(
             (normed, first_other, grad_mix, mix_other, mixed, mixed_other, grad_gelu_pre, gelu_other),
@@ -1413,17 +1504,23 @@
         grad_normed = mm(grad_both, wide, ((1,), (1,)))
         input_grad = (grad_middle + norm_back(tokens, gain_one, grad_normed)).astype(bf16)
     input_grad = input_grad[None]
-    middle = lax.optimization_barrier((middle, mixer_sum))[0]
     block_output = (middle + out_sum.astype(f32)).astype(bf16)[None]
-    mlp_grads = [mlp_back[m].astype(f32) for m in range(3)]
-    mixer_sum = mixer_sum.astype(f32)
-    edges = [lru, 2 * lru, 3 * lru, 3 * lru + width, 3 * lru + 2 * width]
-    dbranch, dgelu, dout, drate, dinput, vec = jnp.split(mixer_sum, edges, axis=1)
-    vec = vec.T
+    edge = 3 * lru + 2 * width
+    vec = mixer_sum[:, edge:].astype(f32).T
+    if custom:
+        *weight_grads, totals = finish(mixer_sum, mlp_back, branch_proj, gelu_proj, gate_proj, up_proj, width)
+        first_total, second_total = totals[:, 0], totals[:, 128]
+    else:
+        weight_grads = list(
+            jnp.split(mixer_sum[:, :edge].astype(f32), [lru, 2 * lru, 3 * lru, 3 * lru + width], axis=1)
+        ) + [mlp_back[m].astype(f32) for m in range(3)]
+        first_total = gain_back((branch_proj, weight_grads[0]), (gelu_proj, weight_grads[1]))
+        second_total = gain_back((gate_proj, weight_grads[5]), (up_proj, weight_grads[6]))
+    dbranch, dgelu, dout, drate, dinput, dgate, dup, ddown = weight_grads
     return (
         block_output,
         input_grad,
-        gain_back(mixer_gain, (branch_proj, dbranch), (gelu_proj, dgelu)),
+        first_total / mixer_gain.astype(f32),
         dbranch,
         dgelu,
         vec[: margin + 1],
@@ -1434,10 +1531,10 @@
         vec[5],
         vec[6],
         dout,
-        gain_back(mlp_gain, (gate_proj, mlp_grads[0]), (up_proj, mlp_grads[1])),
-        mlp_grads[0],
-        mlp_grads[1],
-        mlp_grads[2],
+        second_total / mlp_gain.astype(f32),
+        dgate,
+        dup,
+        ddown,
     )
 
 

time: 831 us -> 824 us (level)
  waiting for transfers between devices: 77.3 us -> 44.2 us
  Pallas kernels: 612 us -> 642 us
  local copies, waits for them, and re-layouts: 10.6 us -> 23.8 us
  matrix products: 29.7 us -> 19.1 us
  other arithmetic: 39.9 us -> 30.5 us
    pallas_call x0 -> x2, Pallas kernels: none -> 35 us  [the longest x1 19.3 us: finish(): pl.pallas_call(finish_kernel, grid=(rows // step,), in_specs=[spec(mixer....]
    ppermute x2, waiting for transfers between devices: 31.8 us -> 0.08 us  [swap_across(): return lax.ppermute(shard, 'seq', [(i, i ^ 4) for i in range(8)])]
    ppermute x3, waiting for transfers between devices: 31 us -> 0.01 us  [from_line(): lax.ppermute(shard, 'fsdp', [(i, (i + k) % count) for i in range(count)])]
    ppermute x2, waiting for transfers between devices: 11.4 us -> 39.9 us  [swap_beside(): return lax.ppermute(shard, 'seq', [(i, i ^ 2) for i in range(8)])]
    unnamed x64 -> x68, local copies, waits for them, and re-layouts: 4.28 us -> 19.4 us
    dot_general x3 -> x2, matrix products: 29.7 us -> 19.1 us  [mm(): lax.dot_general(left, right, (dims, ((), ())), preferred_element_type=f32)]
  transfers between devices with their start and end apart: 14 -> 14, of which waited for: 5 -> 5; matrix products, arithmetic and copies ran while one was open for 9% -> 6% of each run, Pallas kernels for 46% -> 25%
where the time goes in v14:
time: 824 us; the launch traced here: 815 us
  Pallas kernels  642 us (78%)
  waiting for transfers between devices  44.2 us (5%)
  other arithmetic  30.5 us (4%)
  blocking collectives  24.3 us (3%)
  local copies, waits for them, and re-layouts  23.8 us (3%)
  matrix products  19.1 us (2%)
  starting transfers between devices  16.7 us (2%)
  between operations  14.4 us (2%)
    pallas_call x1, Pallas kernels, scatter(): pl.pallas_call(scatter_kernel, in_specs=[anyspec] * 15, out_specs=[anyspe...  186 us
    pallas_call x1, Pallas kernels, gather(): pl.pallas_call(gather_kernel, in_specs=[anyspec] * 7, out_specs=[anyspec]...  183 us
    pallas_call x1, Pallas kernels, gather_rows(): pl.pallas_call(rows_kernel, in_specs=[anyspec] * 7, out_specs=[anyspec] *...  84.1 us
    pallas_call x1, Pallas kernels, shared_products(): pl.pallas_call(shared_products_kernel, grid=(3,), in_specs=[anyspec] * 5...  65.7 us
    pallas_call x1, Pallas kernels, feed_forward(): pl.pallas_call(feed_forward_kernel, grid=(2,), in_specs=[block, block, an...  52.2 us
    ppermute x2, waiting for transfers between devices, swap_beside(): return lax.ppermute(shard, 'seq', [(i, i ^ 2) for i in range(8)])  39.9 us
    pallas_call x3, Pallas kernels, call_heads(): pl.pallas_call(kernel, grid=(heads,), in_specs=in_specs, out_specs=out_sp...  33.8 us
    all_gather x2, blocking collectives, prefix(): gathered = lax.all_gather(jnp.stack(part), axis)  24.3 us
  transfers between devices with their start and end apart: 14, of which 5 were waited for; matrix products, arithmetic and copies ran while one was open for 6% of the time, Pallas kernels for 25%

profile of v14, /device:TPU:0, one launch (start us, length us, event | category | flops | bytes accessed | tf_op | source)
XLA Modules:
  0.0 814.9 jit_solution(14175342511887577856)
XLA Ops:
  8.1 1.4 stack.33
  9.6 1.5 fusion.20.first
  11.1 182.9 %gather_weights.1 = (bf16[2560,8320]{1,0:T(8,128)(2,1)}, bf16[320,5760]{1,0:T(8,128)(2,1)}) custom-call(bf16[80,640]{1,0:T(8,128)(2,1)} %fusion.20.first, bf16[80,2560]{1,0:T(8,128)(2,1)} %branch.3, bf16[80,2560]{1,0:T(8,128)(2,1)} %gelu.3, bf16[80,2560]{1,0:T(8,128)(2,1)} %outer.1, bf16[80,7680]{1,0:T(8,128)(2,1)} %gate.3, bf16[80,7680]{1,0:T(8,128)(2,1)} %up.3, ...), custom_call_target="tpu_custom_call" | custom-call | tf_op jit(solution)/shard_map/gather_weights/pallas_call | solution.py:467
  194.1 5.5 collective-permute-start.1
  199.5 3.4 collective-permute-start.2
  202.9 2.1 small_table.1.table.small.gain
  205.9 15.7 %mixer_in.1 = (bf16[192,2560]{1,0:T(8,128)(2,1)S(1)}, bf16[192,2560]{1,0:T(8,128)(2,1)S(1)}, f32[192,2560]{1,0:T(8,128)S(1)}) custom-call(bf16[192,2560]{1,0:T(8,128)(2,1)S(1)} %bitcast.32, f32[16,2560]{1,0:T(8,128)S(1)} %copy-done.6, bf16[2560,8320]{1,0:T(8,128)(2,1)} %get-tuple-element.76.columns.weights.rate_w.input_w.mixer_w), custom_call_target="tpu_custom_call" | custom-call | flops 1 | bytes 1 | tf_op jit(solution)/shard_map/mixer_in/pallas_call | solution.py:138
  221.6 1.3 copy-done.3
  223.8 1.3 collective-permute-start
  226.0 9.5 %mixer_forward.1 = (bf16[192,2560]{1,0:T(8,128)(2,1)S(1)}, f32[192,2560]{1,0:T(8,128)S(1)}, f32[192,2560]{1,0:T(8,128)S(1)}, f32[192,2560]{1,0:T(8,128)S(1)}, f32[192,2560]{1,0:T(8,128)S(1)}) custom-call(bf16[192,2560]{1,0:T(8,128)(2,1)S(1)} %get-tuple-element.77.branch, f32[8,2560]{1,0:T(8,128)S(1)} %pad_convert_fusion.prior, f32[16,2560]{1,0:T(8,128)S(1)} %copy-done.7, ...), custom_call_target="tpu_custom_call" | custom-call | flops 1 | bytes 1 | tf_op jit(solution)/shard_map/mixer_forward/pallas_call | solution.py:1317
  235.5 1.3 copy-done.1
  236.8 1.3 copy-done.14
  238.1 0.9 copy-done.22
  239.1 14.9 %all-gather.2 = f32[8,2,2560]{2,1,0:T(2,128)S(1)} all-gather(f32[1,2,2560]{2,1,0:T(2,128)S(1)} %fusion.21), channel_id=2, replica_groups=mesh['seq'=8,'fsdp'=4] {'seq'}, dimensions={0}, use_global_device_ids=true | all-gather | bytes 184320 | tf_op jit(solution)/shard_map/all_gather | solution.py:29
  255.6 11.7 %multiply_reduce_fusion.1 = (f32[192]{0:T(256)S(1)}, f32[192,2560]{1,0:T(8,128)}) fusion(bf16[192,2560]{1,0:T(8,128)(2,1)S(1)} %fusion.17.mixed, bf16[2560,8320]{1,0:T(8,128)(2,1)} %get-tuple-element.76.columns.weights.rate_w.input_w.mixer_w, bf16[1,192,2560]{2,1,0:T(8,128)(2,1)S(1)} %copy-done.11), kind=kOutput, calls=%fused_computation.28 | convolution fusion | flops 2518548224 | bytes 17040128 | tf_op jit(solution)/shard_map/dot_general | solution.py:61
  267.3 2.7 multiply_convert_fusion.normed
  270.1 84.1 %gather_rows.1 = (bf16[768,2560]{1,0:T(8,128)(2,1)}, bf16[768,2560]{1,0:T(8,128)(2,1)}, bf16[768,2560]{1,0:T(8,128)(2,1)}, bf16[768,2560]{1,0:T(8,128)(2,1)}, bf...) custom-call(bf16[192,2560]{1,0:T(8,128)(2,1)} %multiply_convert_fusion.normed, bf16[192,2560]{1,0:T(8,128)(2,1)} %bitcast.12.grad0, ...), custom_call_target="tpu_custom_call" | custom-call | tf_op jit(solution)/shard_map/gather_rows/pallas_call | solution.py:594
  354.2 52.2 %feed_forward.1 = (bf16[768,1920]{1,0:T(8,128)(2,1)}, bf16[768,1920]{1,0:T(8,128)(2,1)}, bf16[768,3840]{1,0:T(8,128)(2,1)}, bf16[768,3840]{1,0:T(8,128)(2,1)}, bf16[768,2560]{1,0:T(8,128)(2,1)}) custom-call(bf16[768,2560]{1,0:T(8,128)(2,1)} %get-tuple-element.84.normed, bf16[768,2560]{1,0:T(8,128)(2,1)} %get-tuple-element.86.grad_out.grad, ...), custom_call_target="tpu_custom_call" | custom-call | tf_op jit(solution)/shard_map/feed_forward/pallas_call | solution.py:701
  406.5 65.7 %feed_forward_products.1 = (bf16[160,5760]{1,0:T(8,128)(2,1)}, bf16[160,5760]{1,0:T(8,128)(2,1)}, bf16[320,5760]{1,0:T(8,128)(2,1)}, bf16[160,5760]{1,0:T(8,128)...) custom-call(bf16[768,2560]{1,0:T(8,128)(2,1)} %get-tuple-element.84.normed, ...), custom_call_target="tpu_custom_call" | custom-call | tf_op jit(solution)/shard_map/feed_forward_products/pallas_call | solution.py:885
  472.3 1.8 collective-permute-start.5
  474.1 3.3 reduce-scatter.3.cloned.1.call-done
  477.5 2.2 multiply_reduce_fusion
  479.7 3.3 add_convert_fusion.5.grad_mix
  483.0 7.4 fusion.grad_mixed
  490.5 12.7 %mixer_backward_scan.1 = (bf16[192,2560]{1,0:T(8,128)(2,1)}, f32[192,2560]{1,0:T(8,128)S(1)}, f32[192,2560]{1,0:T(8,128)S(1)}, f32[8,2560]{1,0:T(8,128)S(1)}) custom-call(f32[192,2560]{1,0:T(8,128)S(1)} %fusion.grad_mixed, f32[192,2560]{1,0:T(8,128)S(1)} %copy-done.5, f32[192,2560]{1,0:T(8,128)S(1)} %copy-done.2, f32[192,2560]{1,0:T(8,128)S(1)} %get-tuple-element.79.cum, ...), custom_call_target="tpu_custom_call" | custom-call | flops 1 | bytes 1 | tf_op jit(solution)/shard_map/mixer_backward_scan/pallas_call | solution.py:1317
  503.2 11.4 %collective-permute-done.4 = bf16[160,5760]{1,0:T(8,128)(2,1)} collective-permute-done((bf16[160,5760]{1,0:T(8,128)(2,1)}, bf16[160,5760]{1,0:T(8,128)(2,1)}, u32[]{:S(2)}, u32[]{:S(2)}) %collective-permute-start.4) | collective-permute-done | bytes 1843232 | tf_op jit(solution)/shard_map/ppermute | solution.py:1278
  514.8 9.4 %all-gather.3 = f32[8,2,2560]{2,1,0:T(2,128)S(1)} all-gather(f32[1,2,2560]{2,1,0:T(2,128)S(1)} %fusion.22), channel_id=3, replica_groups=mesh['seq'=8,'fsdp'=4] {'seq'}, dimensions={0}, use_global_device_ids=true | all-gather | bytes 184320 | tf_op jit(solution)/shard_map/all_gather | solution.py:29
  524.6 11.5 %mixer_backward.1 = (f32[192,2560]{1,0:T(8,128)S(1)}, f32[8,2560]{1,0:T(8,128)S(1)}, bf16[2560,256]{1,0:T(8,128)(2,1)S(1)}, bf16[2560,256]{1,0:T(8,128)(2,1)S(1)}, f32[8,2560]{1,0:T(8,128)S(1)}) custom-call(f32[192,2560]{1,0:T(8,128)S(1)} %get-tuple-element.100.rev_cum, f32[192,2560]{1,0:T(8,128)S(1)} %get-tuple-element.101.rev_grad, ...), custom_call_target="tpu_custom_call" | custom-call | flops 1 | bytes 1 | tf_op jit(solution)/shard_map/mixer_backward/pallas_call | solution.py:1317
  536.1 1.0 copy-done.18
  537.2 1.1 copy-done.20
  538.3 1.3 copy-done.24
  540.2 1.3 collective-permute-start.6
  541.5 1.2 collective-permute-start.8
  543.0 1.5 collective-permute-start.9
  545.1 5.5 add_convert_fusion.2
  550.5 1.8 fusion.8.rest
  553.2 1.0 pad_maximum_fusion.grad_branch
  554.3 3.1 fusion.18
  557.3 28.5 %collective-permute-done.9 = bf16[160,5760]{1,0:T(8,128)(2,1)} collective-permute-done((bf16[160,5760]{1,0:T(8,128)(2,1)}, bf16[160,5760]{1,0:T(8,128)(2,1)}, u32[]{:S(2)}, u32[]{:S(2)}) %collective-permute-start.9) | collective-permute-done | bytes 1843232 | tf_op jit(solution)/shard_map/ppermute | solution.py:1278
  585.8 3.3 add_convert_fusion.1.mlp_low
  589.1 3.2 add_convert_fusion.mlp_high
  593.2 186.2 %scatter_gradients.1 = (bf16[80,8320]{1,0:T(8,128)(2,1)}, bf16[3,80,7680]{2,1,0:T(8,128)(2,1)}, bf16[192,2560]{1,0:T(8,128)(2,1)}) custom-call(bf16[192,2560]{1,0:T(8,128)(2,1)} %copy-done.12, bf16[192,2560]{1,0:T(8,128)(2,1)} %get-tuple-element.113.normed_other, bf16[192,2560]{1,0:T(8,128)(2,1)} %add_convert_fusion.5.grad_mix, ...), custom_call_target="tpu_custom_call" | custom-call | tf_op jit(solution)/shard_map/scatter_gradients/pallas_call | solution.py:1224
  780.2 1.3 copy-done.9
  781.4 2.0 copy-done.13
  783.5 1.0 copy-done.16
  784.5 1.3 copy-done.17
  785.8 19.3 %finish_gradients.1 = (f32[80,2560]{1,0:T(8,128)}, f32[80,2560]{1,0:T(8,128)}, f32[80,2560]{1,0:T(8,128)}, f32[80,256]{1,0:T(8,128)}, f32[80,256]{1,0:T(8,128)},...) custom-call(bf16[80,8320]{1,0:T(8,128)(2,1)S(1)} %copy-done.17, ...), custom_call_target="tpu_custom_call" | custom-call | tf_op jit(solution)/shard_map/finish_gradients/pallas_call | solution.py:195
  807.2 0.9 copy.62
  (105 shorter events, 12.3 us)
Async XLA Ops:
  7.2 347.0 %all-gather.6.cloned.1.call-start = ((), (), s32[]{:S(2)}) async-start(), calls=%async_computation.2 | async-start | bytes 33177600 | tf_op jit(solution)/shard_map/all_gather | solution.py:1374
  194.0 283.5 %reduce-scatter.3.cloned.1.call-start = ((), (), s32[]{:S(2)}) async-start(), calls=%async_computation.3 | async-start | bytes 4915200 | tf_op jit(solution)/shard_map/reduce_scatter | solution.py:1425
  194.1 76.0 %collective-permute-start.1 = (bf16[192,2560]{1,0:T(8,128)(2,1)}, bf16[192,2560]{1,0:T(8,128)(2,1)}, u32[]{:S(2)}, u32[]{:S(2)}) collective-permute-start(bf16[192,2560]{1,0:T(8,128)(2,1)} %bitcast.12.grad0), channel_id=1, source_target_pairs={{0,1},{1,2},{2,3},{3,0},{4,5},{5,6},{6,7},{7,4},{8,9},{9,10},{10,1... | collective-permute-start | bytes 2949128 | tf_op jit(solution)/shard_map/ppermute | solution.py:1268
  199.5 70.5 %collective-permute-start.2 = (bf16[192,2560]{1,0:T(8,128)(2,1)}, bf16[192,2560]{1,0:T(8,128)(2,1)}, u32[]{:S(2)}, u32[]{:S(2)}) collective-permute-start(bf16[192,2560]{1,0:T(8,128)(2,1)} %bitcast.12.grad0), channel_id=1, source_target_pairs={{0,2},{1,3},{2,0},{3,1},{4,6},{5,7},{6,4},{7,5},{8,10},{9,11},{10,... | collective-permute-start | bytes 2949128 | tf_op jit(solution)/shard_map/ppermute | solution.py:1268
  202.9 67.2 %collective-permute-start.3 = (bf16[192,2560]{1,0:T(8,128)(2,1)}, bf16[192,2560]{1,0:T(8,128)(2,1)}, u32[]{:S(2)}, u32[]{:S(2)}) collective-permute-start(bf16[192,2560]{1,0:T(8,128)(2,1)} %bitcast.12.grad0), channel_id=1, source_target_pairs={{0,3},{1,0},{2,1},{3,2},{4,7},{5,4},{6,5},{7,6},{8,11},{9,8},{10,9... | collective-permute-start | bytes 2949128 | tf_op jit(solution)/shard_map/ppermute | solution.py:1268
  202.9 2.1 copy-start.10
  205.0 0.9 copy-start.6
  205.9 20.1 %copy-start.7 = (f32[16,2560]{1,0:T(8,128)S(1)}, f32[16,2560]{1,0:T(8,128)}, u32[]{:S(2)}) copy-start(f32[16,2560]{1,0:T(8,128)} %small_table.1.table.small.gain) | copy-start | bytes 491524
  221.6 1.3 copy-start.3
  222.9 0.9 copy-start.12
  223.8 2.1 collective-permute-start
  226.0 28.4 %copy-start.4 = (f32[192,2560]{1,0:T(8,128)S(1)}, f32[192,2560]{1,0:T(8,128)}, u32[]{:S(2)}) copy-start(f32[192,2560]{1,0:T(8,128)} %copy-done.3) | copy-start | bytes 5898244
  235.5 1.3 copy-start.1
  236.8 1.3 copy-start.14
  238.1 0.9 copy-start.22
  239.0 15.4 %copy-start = (f32[192,2560]{1,0:T(8,128)}, f32[192,2560]{1,0:T(8,128)S(1)}, u32[]{:S(2)}) copy-start(f32[192,2560]{1,0:T(8,128)S(1)} %get-tuple-element.78.local) | copy-start | bytes 5898244
  254.4 1.2 copy-start.11
  255.6 11.7 %copy-start.26 = (bf16[192,2560]{1,0:T(8,128)(2,1)}, bf16[192,2560]{1,0:T(8,128)(2,1)S(1)}, u32[]{:S(2)}) copy-start(bf16[192,2560]{1,0:T(8,128)(2,1)S(1)} %fusion.17.mixed) | copy-start | bytes 2949124
  406.4 147.8 %reduce-scatter.5.cloned.1.call-start = ((), (), s32[]{:S(2)}) async-start(), calls=%async_computation.4 | async-start | bytes 4915200 | tf_op jit(solution)/shard_map/reduce_scatter | solution.py:1443
  472.2 42.4 %collective-permute-start.4 = (bf16[160,5760]{1,0:T(8,128)(2,1)}, bf16[160,5760]{1,0:T(8,128)(2,1)}, u32[]{:S(2)}, u32[]{:S(2)}) collective-permute-start(bf16[160,5760]{1,0:T(8,128)(2,1)} %get-tuple-element.93), channel_id=1, source_target_pairs={{0,8},{4,12},{8,0},{12,4},{16,24},{20,28},{24,16},{28,20},{1,9},{5... | collective-permute-start | bytes 5529608 | tf_op jit(solution)/shard_map/ppermute | solution.py:1278
  472.3 42.4 %collective-permute-start.5 = (bf16[160,5760]{1,0:T(8,128)(2,1)}, bf16[160,5760]{1,0:T(8,128)(2,1)}, u32[]{:S(2)}, u32[]{:S(2)}) collective-permute-start(bf16[160,5760]{1,0:T(8,128)(2,1)} %get-tuple-element.94), channel_id=1, source_target_pairs={{0,16},{4,20},{8,24},{12,28},{16,0},{20,4},{24,8},{28,12},{1,17},{... | collective-permute-start | bytes 5529608 | tf_op jit(solution)/shard_map/ppermute | solution.py:1282
  477.5 2.2 copy-start.28
  483.0 7.4 copy-start.2
  483.0 7.4 copy-start.5
  483.0 109.2 %collective-permute-start.7 = (bf16[192,2560]{1,0:T(8,128)(2,1)}, bf16[192,2560]{1,0:T(8,128)(2,1)}, u32[]{:S(2)}, u32[]{:S(2)}) collective-permute-start(bf16[192,2560]{1,0:T(8,128)(2,1)} %add_convert_fusion.5.grad_mix), channel_id=1, source_target_pairs={{0,4},{4,0},{8,12},{12,8},{16,20},{20,16},{24,28},{28,24},{1,5},{5... | collective-permute-start | bytes 2949128 | tf_op jit(solution)/shard_map/ppermute | solution.py:1274
  490.5 34.2 %copy-start.23 = (bf16[192,2560]{1,0:T(8,128)(2,1)S(1)}, bf16[192,2560]{1,0:T(8,128)(2,1)}, u32[]{:S(2)}) copy-start(bf16[192,2560]{1,0:T(8,128)(2,1)} %copy-done.22) | copy-start | bytes 2949124
  536.1 1.1 copy-start.18
  537.2 1.1 copy-start.20
  538.3 1.3 copy-start.24
  540.2 13.0 %collective-permute-start.6 = (f32[3,2560]{1,0:T(4,128)}, f32[3,2560]{1,0:T(4,128)S(1)}, u32[]{:S(2)}, u32[]{:S(2)}) collective-permute-start(f32[3,2560]{1,0:T(4,128)} %slice.213), channel_id=1, source_target_pairs={{4,0},{8,4},{12,8},{16,12},{20,16},{24,20},{28,24},{5,1},{9,5},{13... | collective-permute-start | bytes 92168 | tf_op jit(solution)/shard_map/ppermute | solution.py:23
  541.5 50.8 %collective-permute-start.8 = (bf16[192,2560]{1,0:T(8,128)(2,1)}, bf16[192,2560]{1,0:T(8,128)(2,1)S(1)}, u32[]{:S(2)}, u32[]{:S(2)}) collective-permute-start(bf16[192,2560]{1,0:T(8,128)(2,1)} %get-tuple-element.115.grad_gelu), channel_id=1, source_target_pairs={{0,4},{4,0},{8,12},{12,8},{16,20},{20,16},{24,28},{28,24},{1,5},{5... | collective-permute-start | bytes 2949128 | tf_op jit(solution)/shard_map/ppermute | solution.py:1274
  543.0 42.8 %collective-permute-start.9 = (bf16[160,5760]{1,0:T(8,128)(2,1)}, bf16[160,5760]{1,0:T(8,128)(2,1)}, u32[]{:S(2)}, u32[]{:S(2)}) collective-permute-start(bf16[160,5760]{1,0:T(8,128)(2,1)} %get-tuple-element.120), channel_id=1, source_target_pairs={{0,8},{4,12},{8,0},{12,4},{16,24},{20,28},{24,16},{28,20},{1,9},{5... | collective-permute-start | bytes 5529608 | tf_op jit(solution)/shard_map/ppermute | solution.py:1278
  544.5 44.6 %collective-permute-start.10 = (bf16[160,5760]{1,0:T(8,128)(2,1)}, bf16[160,5760]{1,0:T(8,128)(2,1)}, u32[]{:S(2)}, u32[]{:S(2)}) collective-permute-start(bf16[160,5760]{1,0:T(8,128)(2,1)} %get-tuple-element.122), channel_id=1, source_target_pairs={{0,16},{4,20},{8,24},{12,28},{16,0},{20,4},{24,8},{28,12},{1,17},{... | collective-permute-start | bytes 5529608 | tf_op jit(solution)/shard_map/ppermute | solution.py:1282
  545.0 5.5 copy-start.19
  545.1 5.5 copy-start.21
  550.5 2.6 copy-start.25
  554.3 31.6 %copy-start.27 = (bf16[160,5760]{1,0:T(8,128)(2,1)S(1)}, bf16[160,5760]{1,0:T(8,128)(2,1)}, u32[]{:S(2)}) copy-start(bf16[160,5760]{1,0:T(8,128)(2,1)} %get-tuple-element.110) | copy-start | bytes 5529604
  592.2 0.9 copy-start.30
  593.2 186.9 %copy-start.8 = (bf16[80,7680]{1,0:T(8,128)(2,1)S(1)}, bf16[80,7680]{1,0:T(8,128)(2,1)}, u32[]{:S(2)}) copy-start(bf16[80,7680]{1,0:T(8,128)(2,1)} %gate.3) | copy-start | bytes 3686404
  593.2 186.9 %copy-start.15 = (bf16[80,2560]{1,0:T(8,128)(2,1)S(1)}, bf16[80,2560]{1,0:T(8,128)(2,1)}, u32[]{:S(2)}) copy-start(bf16[80,2560]{1,0:T(8,128)(2,1)} %branch.3) | copy-start | bytes 1228804
  780.1 1.3 copy-start.9
  781.4 2.0 copy-start.13
  783.5 1.0 copy-start.16
  784.5 1.3 copy-start.17
  785.8 20.9 %copy-start.31 = (bf16[80]{0:T(256)(128)(2,1)S(1)}, bf16[80]{0:T(256)(128)(2,1)}, u32[]{:S(2)}) copy-start(bf16[80]{0:T(256)(128)(2,1)} %param.19) | copy-start | bytes 484
  785.8 20.9 %copy-start.32 = (bf16[80]{0:T(256)(128)(2,1)S(1)}, bf16[80]{0:T(256)(128)(2,1)}, u32[]{:S(2)}) copy-start(bf16[80]{0:T(256)(128)(2,1)} %param.30) | copy-start | bytes 484
  785.8 21.4 %copy-start.29 = (bf16[192,2560]{1,0:T(8,128)(2,1)S(1)}, bf16[192,2560]{1,0:T(8,128)(2,1)}, u32[]{:S(2)}) copy-start(bf16[192,2560]{1,0:T(8,128)(2,1)} %get-tuple-element.123) | copy-start | bytes 2949124
Sparse Core Ops, SparseCore 0:
  194.1 149.8 all-gather.5
  406.6 70.8 reduce-scatter.2
  479.8 73.0 reduce-scatter.4

commit v15 on v14

--- a/solution.py
+++ b/solution.py
@@ -157,53 +157,6 @@
         cost_estimate=pl.CostEstimate(flops=1, bytes_accessed=1, transcendentals=0),
         name="mixer_in",
     )(tokens, table, mixer_w)
-
-
-def finish_kernel(mixer, mlp, branch, gelu, gate, up, dbranch, dgelu, dout, drate, dinput, dgate, dup, ddown, totals):
-    lru = branch.shape[1]
-    width = drate.shape[1]
-    ff = gate.shape[1]
-
-    def met(weight, grad, cols):
-        def one(turn, carry):
-            here = pl.ds(pl.multiple_of(turn * 512, 512), 512)
-            return carry + jnp.sum(weight[:, here].astype(f32) * grad[:, here], axis=1, keepdims=True)
-
-        return lax.fori_loop(0, cols // 512, one, jnp.zeros((weight.shape[0], 1), f32))
-
-    start = 0
-    for grad in (dbranch, dgelu, dout, drate, dinput):
-        size = grad.shape[1]
-        grad[...] = mixer[:, start : start + size].astype(f32)
-        start += size
-    for m, grad in enumerate((dgate, dup, ddown)):
-        grad[...] = mlp[m].astype(f32)
-    first = met(branch, dbranch, lru) + met(gelu, dgelu, lru)
-    second = met(gate, dgate, ff) + met(up, dup, ff)
-    totals[...] = jnp.concatenate([jnp.broadcast_to(first, (first.shape[0], 128)), jnp.broadcast_to(second, (second.shape[0], 128))], axis=1)
-
-
-def finish(mixer, mlp, branch, gelu, gate, up, width):
-    rows, ff = gate.shape
-    lru = branch.shape[1]
-    step = 16
-
-    def spec(cols):
-        return pl.BlockSpec((step, cols), lambda i: (i, 0))
-
-    sizes = [lru, lru, lru, width, width, ff, ff, ff, 256]
-    return pl.pallas_call(
-        finish_kernel,
-        grid=(rows // step,),
-        in_specs=[
-            spec(mixer.shape[1]), pl.BlockSpec((3, step, ff), lambda i: (0, i, 0)),
-            spec(lru), spec(lru), spec(ff), spec(ff),
-        ],
-        out_specs=[spec(cols) for cols in sizes],
-        out_shape=[jax.ShapeDtypeStruct((rows, cols), f32) for cols in sizes],
-        compiler_params=pltpu.CompilerParams(vmem_limit_bytes=40 * 1024 * 1024),
-        name="finish_gradients",
-    )(mixer, mlp, branch, gelu, gate, up)
 
 
 def mixer_forward(branch, prior, small, rate_w, input_w, conv, rate_pre, input_pre, cum, local, ext):
@@ -1490,11 +1443,13 @@
     vectors = jnp.pad(sums.T, ((0, 0), (0, 128 - sums.shape[0]))).astype(bf16)
     rest = jnp.concatenate([rate_w_grad, input_w_grad, vectors], axis=1)
     if custom:
-        low = add_low(mine[:half], from_across_low)
-        high = add_low(mine[half:], from_beside_high)
-        low, high, grad_branch = lax.optimization_barrier((low, high, grad_branch))
-        middle = lax.optimization_barrier((middle, low))[0]
-        low, high = add_low(low, from_beside_low), add_low(high, from_across_high)
+        low, high = [
+            sum(part.astype(f32) for part in parts).astype(bf16)
+            for parts in (
+                (mine[:half], from_across_low, from_beside_low),
+                (mine[half:], from_across_high, from_beside_high),
+            )
+        ]
         mixer_sum, mlp_back, input_grad = scatter(
             (normed, first_other, grad_mix, mix_other, mixed, mixed_other, grad_gelu_pre, gelu_other),
             grad_branch, rest, low, high, mixer_w, block_input[0], small,
@@ -1504,18 +1459,15 @@
         grad_normed = mm(grad_both, wide, ((1,), (1,)))
         input_grad = (grad_middle + norm_back(tokens, gain_one, grad_normed)).astype(bf16)
     input_grad = input_grad[None]
+    middle = lax.optimization_barrier((middle, mixer_sum))[0]
     block_output = (middle + out_sum.astype(f32)).astype(bf16)[None]
     edge = 3 * lru + 2 * width
     vec = mixer_sum[:, edge:].astype(f32).T
-    if custom:
-        *weight_grads, totals = finish(mixer_sum, mlp_back, branch_proj, gelu_proj, gate_proj, up_proj, width)
-        first_total, second_total = totals[:, 0], totals[:, 128]
-    else:
-        weight_grads = list(
-            jnp.split(mixer_sum[:, :edge].astype(f32), [lru, 2 * lru, 3 * lru, 3 * lru + width], axis=1)
-        ) + [mlp_back[m].astype(f32) for m in range(3)]
-        first_total = gain_back((branch_proj, weight_grads[0]), (gelu_proj, weight_grads[1]))
-        second_total = gain_back((gate_proj, weight_grads[5]), (up_proj, weight_grads[6]))
+    weight_grads = list(
+        jnp.split(mixer_sum[:, :edge].astype(f32), [lru, 2 * lru, 3 * lru, 3 * lru + width], axis=1)
+    ) + [mlp_back[m].astype(f32) for m in range(3)]
+    first_total = gain_back((branch_proj, weight_grads[0]), (gelu_proj, weight_grads[1]))
+    second_total = gain_back((gate_proj, weight_grads[5]), (up_proj, weight_grads[6]))
     dbranch, dgelu, dout, drate, dinput, dgate, dup, ddown = weight_grads
     return (
         block_output,

time: 824 us -> 791 us (0.960)
  waiting for transfers between devices: 44.2 us -> 28 us
  Pallas kernels: 642 us -> 626 us
    ppermute x2, waiting for transfers between devices: 39.9 us -> 9.82 us  [swap_beside(): return lax.ppermute(shard, 'seq', [(i, i ^ 2) for i in range(8)])]
    pallas_call x1 -> x0, Pallas kernels: 19.3 us -> none  [finish(): pl.pallas_call(finish_kernel, grid=(rows // step,), in_specs=[spec(mixer....]
    ppermute x2, waiting for transfers between devices: 0.08 us -> 13.9 us  [swap_across(): return lax.ppermute(shard, 'seq', [(i, i ^ 4) for i in range(8)])]
    unnamed x68 -> x80, local copies, waits for them, and re-layouts: 19.4 us -> 23.8 us
  transfers between devices with their start and end apart: 14 -> 14, of which waited for: 5 -> 6; matrix products, arithmetic and copies ran while one was open for 6% -> 6% of each run, Pallas kernels for 25% -> 50%
where the time goes in v15:
time: 791 us; the launch traced here: 784 us
  Pallas kernels  626 us (79%)
  other arithmetic  30.9 us (4%)
  local copies, waits for them, and re-layouts  28.1 us (4%)
  waiting for transfers between devices  28 us (4%)
  blocking collectives  24.3 us (3%)
  starting transfers between devices  16.8 us (2%)
  matrix products  15.2 us (2%)
  between operations  14.5 us (2%)
    pallas_call x1, Pallas kernels, scatter(): pl.pallas_call(scatter_kernel, in_specs=[anyspec] * 15, out_specs=[anyspe...  186 us
    pallas_call x1, Pallas kernels, gather(): pl.pallas_call(gather_kernel, in_specs=[anyspec] * 7, out_specs=[anyspec]...  183 us
    pallas_call x1, Pallas kernels, gather_rows(): pl.pallas_call(rows_kernel, in_specs=[anyspec] * 7, out_specs=[anyspec] *...  87.4 us
    pallas_call x1, Pallas kernels, shared_products(): pl.pallas_call(shared_products_kernel, grid=(3,), in_specs=[anyspec] * 5...  65.7 us
    pallas_call x1, Pallas kernels, feed_forward(): pl.pallas_call(feed_forward_kernel, grid=(2,), in_specs=[block, block, an...  52.1 us
    pallas_call x3, Pallas kernels, call_heads(): pl.pallas_call(kernel, grid=(heads,), in_specs=in_specs, out_specs=out_sp...  33.6 us
    all_gather x2, blocking collectives, prefix(): gathered = lax.all_gather(jnp.stack(part), axis)  24.3 us
    unnamed x80, local copies, waits for them, and re-layouts  23.8 us
  transfers between devices with their start and end apart: 14, of which 6 were waited for; matrix products, arithmetic and copies ran while one was open for 6% of the time, Pallas kernels for 50%

profile of v15, /device:TPU:0, one launch (start us, length us, event | category | flops | bytes accessed | tf_op | source)
XLA Modules:
  0.0 783.7 jit_solution(7039912046770797138)
XLA Ops:
  8.1 1.4 stack.33
  9.6 1.5 fusion.20.first
  11.1 182.9 %gather_weights.1 = (bf16[2560,8320]{1,0:T(8,128)(2,1)}, bf16[320,5760]{1,0:T(8,128)(2,1)}) custom-call(bf16[80,640]{1,0:T(8,128)(2,1)} %fusion.20.first, bf16[80,2560]{1,0:T(8,128)(2,1)} %branch.1, bf16[80,2560]{1,0:T(8,128)(2,1)} %gelu.1, bf16[80,2560]{1,0:T(8,128)(2,1)} %outer.1, bf16[80,7680]{1,0:T(8,128)(2,1)} %gate.1, bf16[80,7680]{1,0:T(8,128)(2,1)} %up.1, ...), custom_call_target="tpu_custom_call" | custom-call | tf_op jit(solution)/shard_map/gather_weights/pallas_call | solution.py:420
  194.1 5.5 collective-permute-start.1
  199.5 3.4 collective-permute-start.2
  202.9 2.1 small_table.1.table.small.gain
  205.9 15.7 %mixer_in.1 = (bf16[192,2560]{1,0:T(8,128)(2,1)S(1)}, bf16[192,2560]{1,0:T(8,128)(2,1)S(1)}, f32[192,2560]{1,0:T(8,128)S(1)}) custom-call(bf16[192,2560]{1,0:T(8,128)(2,1)S(1)} %bitcast.43, f32[16,2560]{1,0:T(8,128)S(1)} %copy-done.6, bf16[2560,8320]{1,0:T(8,128)(2,1)} %get-tuple-element.64.columns.weights.rate_w.input_w.mixer_w), custom_call_target="tpu_custom_call" | custom-call | flops 1 | bytes 1 | tf_op jit(solution)/shard_map/mixer_in/pallas_call | solution.py:138
  221.6 1.3 copy-done.3
  223.8 1.3 collective-permute-start
  226.0 9.5 %mixer_forward.1 = (bf16[192,2560]{1,0:T(8,128)(2,1)S(1)}, f32[192,2560]{1,0:T(8,128)S(1)}, f32[192,2560]{1,0:T(8,128)S(1)}, f32[192,2560]{1,0:T(8,128)S(1)}, f32[192,2560]{1,0:T(8,128)S(1)}) custom-call(bf16[192,2560]{1,0:T(8,128)(2,1)S(1)} %get-tuple-element.65.branch, f32[8,2560]{1,0:T(8,128)S(1)} %pad_convert_fusion.prior, f32[16,2560]{1,0:T(8,128)S(1)} %copy-done.7, ...), custom_call_target="tpu_custom_call" | custom-call | flops 1 | bytes 1 | tf_op jit(solution)/shard_map/mixer_forward/pallas_call | solution.py:1270
  235.5 1.3 copy-done.1
  236.8 1.3 copy-done.11
  239.2 14.9 %all-gather.2 = f32[8,2,2560]{2,1,0:T(2,128)S(1)} all-gather(f32[1,2,2560]{2,1,0:T(2,128)S(1)} %fusion.21), channel_id=2, replica_groups=mesh['seq'=8,'fsdp'=4] {'seq'}, dimensions={0}, use_global_device_ids=true | all-gather | bytes 184320 | tf_op jit(solution)/shard_map/all_gather | solution.py:29
  255.7 8.6 %multiply_reduce_fusion.3 = (f32[192]{0:T(256)S(1)}, f32[192,2560]{1,0:T(8,128)S(1)}) fusion(bf16[192,2560]{1,0:T(8,128)(2,1)S(1)} %fusion.17.mixed, bf16[2560,8320]{1,0:T(8,128)(2,1)} %get-tuple-element.64.columns.weights.rate_w.input_w.mixer_w, bf16[1,192,2560]{2,1,0:T(8,128)(2,1)S(1)} %copy-done.9), kind=kOutput, calls=%fused_computation.28 | convolution fusion | flops 2518548224 | bytes 17040128 | tf_op jit(solution)/shard_map/dot_general | solution.py:61
  264.3 1.2 copy-done.23
  265.6 1.2 multiply_convert_fusion.normed
  266.7 87.4 %gather_rows.1 = (bf16[768,2560]{1,0:T(8,128)(2,1)}, bf16[768,2560]{1,0:T(8,128)(2,1)}, bf16[768,2560]{1,0:T(8,128)(2,1)}, bf16[768,2560]{1,0:T(8,128)(2,1)}, bf...) custom-call(bf16[192,2560]{1,0:T(8,128)(2,1)} %multiply_convert_fusion.normed, bf16[192,2560]{1,0:T(8,128)(2,1)} %bitcast.12.grad0, ...), custom_call_target="tpu_custom_call" | custom-call | tf_op jit(solution)/shard_map/gather_rows/pallas_call | solution.py:547
  354.2 52.1 %feed_forward.1 = (bf16[768,1920]{1,0:T(8,128)(2,1)}, bf16[768,1920]{1,0:T(8,128)(2,1)}, bf16[768,3840]{1,0:T(8,128)(2,1)}, bf16[768,3840]{1,0:T(8,128)(2,1)}, bf16[768,2560]{1,0:T(8,128)(2,1)}) custom-call(bf16[768,2560]{1,0:T(8,128)(2,1)} %get-tuple-element.73.normed, bf16[768,2560]{1,0:T(8,128)(2,1)} %get-tuple-element.74.grad_out.grad, ...), custom_call_target="tpu_custom_call" | custom-call | tf_op jit(solution)/shard_map/feed_forward/pallas_call | solution.py:654
  406.3 65.7 %feed_forward_products.1 = (bf16[160,5760]{1,0:T(8,128)(2,1)}, bf16[160,5760]{1,0:T(8,128)(2,1)}, bf16[320,5760]{1,0:T(8,128)(2,1)}, bf16[160,5760]{1,0:T(8,128)...) custom-call(bf16[768,2560]{1,0:T(8,128)(2,1)} %get-tuple-element.73.normed, ...), custom_call_target="tpu_custom_call" | custom-call | tf_op jit(solution)/shard_map/feed_forward_products/pallas_call | solution.py:838
  472.1 1.8 collective-permute-start.7
  473.9 3.4 reduce-scatter.3.cloned.1.call-done
  477.3 2.3 multiply_reduce_fusion.2
  480.0 1.8 add_convert_fusion.3.grad_mix
  481.8 6.6 fusion.grad_mixed
  488.5 12.7 %mixer_backward_scan.1 = (bf16[192,2560]{1,0:T(8,128)(2,1)S(1)}, f32[192,2560]{1,0:T(8,128)S(1)}, f32[192,2560]{1,0:T(8,128)S(1)}, f32[8,2560]{1,0:T(8,128)S(1)}) custom-call(f32[192,2560]{1,0:T(8,128)S(1)} %fusion.grad_mixed, f32[192,2560]{1,0:T(8,128)S(1)} %copy-done.5, f32[192,2560]{1,0:T(8,128)S(1)} %copy-done.2, f32[192,2560]{1,0:T(8,128)S(1)} %get-tuple-element.67.cum, ...), custom_call_target="tpu_custom_call" | custom-call | flops 1 | bytes 1 | tf_op jit(solution)/shard_map/mixer_backward_scan/pallas_call | solution.py:1270
  501.2 1.3 copy-done.12
  502.4 1.3 copy-done.14
  504.7 9.7 %collective-permute-done.6 = bf16[160,5760]{1,0:T(8,128)(2,1)} collective-permute-done((bf16[160,5760]{1,0:T(8,128)(2,1)}, bf16[160,5760]{1,0:T(8,128)(2,1)}, u32[]{:S(2)}, u32[]{:S(2)}) %collective-permute-start.6) | collective-permute-done | bytes 1843232 | tf_op jit(solution)/shard_map/ppermute | solution.py:1231
  514.5 9.4 %all-gather.3 = f32[8,2,2560]{2,1,0:T(2,128)S(1)} all-gather(f32[1,2,2560]{2,1,0:T(2,128)S(1)} %fusion.22), channel_id=3, replica_groups=mesh['seq'=8,'fsdp'=4] {'seq'}, dimensions={0}, use_global_device_ids=true | all-gather | bytes 184320 | tf_op jit(solution)/shard_map/all_gather | solution.py:29
  524.8 1.7 collective-permute-start.9
  526.6 1.5 copy-done.13
  528.2 1.5 copy-done.15
  529.7 1.5 copy-done.19
  531.2 11.4 %mixer_backward.1 = (f32[192,2560]{1,0:T(8,128)S(1)}, f32[8,2560]{1,0:T(8,128)S(1)}, bf16[2560,256]{1,0:T(8,128)(2,1)S(1)}, bf16[2560,256]{1,0:T(8,128)(2,1)S(1)}, f32[8,2560]{1,0:T(8,128)S(1)}) custom-call(f32[192,2560]{1,0:T(8,128)S(1)} %copy-done.13, f32[192,2560]{1,0:T(8,128)S(1)} %copy-done.15, f32[8,2560]{1,0:T(8,128)S(1)} %broadcast_in_dim.9.incoming, ...), custom_call_target="tpu_custom_call" | custom-call | flops 1 | bytes 1 | tf_op jit(solution)/shard_map/mixer_backward/pallas_call | solution.py:1270
  543.6 1.1 copy-done.17
  544.7 1.3 copy-done.21
  546.3 1.3 collective-permute-start.8
  547.6 1.2 collective-permute-start.5
  548.8 3.3 fusion.8.rest
  552.3 1.1 pad_maximum_fusion.grad_branch
  553.3 13.9 %collective-permute-done.10 = bf16[160,5760]{1,0:T(8,128)(2,1)} collective-permute-done((bf16[160,5760]{1,0:T(8,128)(2,1)}, bf16[160,5760]{1,0:T(8,128)(2,1)}, u32[]{:S(2)}, u32[]{:S(2)}) %collective-permute-start.10) | collective-permute-done | bytes 1843232 | tf_op jit(solution)/shard_map/ppermute | solution.py:1235
  567.3 6.4 add_convert_fusion
  574.6 186.5 %scatter_gradients.1 = (bf16[80,8320]{1,0:T(8,128)(2,1)}, bf16[3,80,7680]{2,1,0:T(8,128)(2,1)}, bf16[192,2560]{1,0:T(8,128)(2,1)}) custom-call(bf16[192,2560]{1,0:T(8,128)(2,1)} %copy-done.10, bf16[192,2560]{1,0:T(8,128)(2,1)} %get-tuple-element.72.normed_other, bf16[192,2560]{1,0:T(8,128)(2,1)} %copy-done.30, ...), custom_call_target="tpu_custom_call" | custom-call | tf_op jit(solution)/shard_map/scatter_gradients/pallas_call | solution.py:1177
  763.3 1.7 slice_convert_fusion.1
  765.0 1.6 multiply_reduce_fusion.4
  767.7 3.0 multiply_reduce_fusion
  771.9 1.6 bitcast_convert_fusion
  773.6 2.4 fusion.18
  (118 shorter events, 17.0 us)
Async XLA Ops:
  7.2 347.0 %all-gather.6.cloned.1.call-start = ((), (), s32[]{:S(2)}) async-start(), calls=%async_computation.2 | async-start | bytes 33177600 | tf_op jit(solution)/shard_map/all_gather | solution.py:1327
  194.0 283.3 %reduce-scatter.3.cloned.1.call-start = ((), (), s32[]{:S(2)}) async-start(), calls=%async_computation.3 | async-start | bytes 4915200 | tf_op jit(solution)/shard_map/reduce_scatter | solution.py:1378
  194.1 72.7 %collective-permute-start.1 = (bf16[192,2560]{1,0:T(8,128)(2,1)}, bf16[192,2560]{1,0:T(8,128)(2,1)}, u32[]{:S(2)}, u32[]{:S(2)}) collective-permute-start(bf16[192,2560]{1,0:T(8,128)(2,1)} %bitcast.12.grad0), channel_id=1, source_target_pairs={{0,1},{1,2},{2,3},{3,0},{4,5},{5,6},{6,7},{7,4},{8,9},{9,10},{10,1... | collective-permute-start | bytes 2949128 | tf_op jit(solution)/shard_map/ppermute | solution.py:1221
  199.5 67.2 %collective-permute-start.2 = (bf16[192,2560]{1,0:T(8,128)(2,1)}, bf16[192,2560]{1,0:T(8,128)(2,1)}, u32[]{:S(2)}, u32[]{:S(2)}) collective-permute-start(bf16[192,2560]{1,0:T(8,128)(2,1)} %bitcast.12.grad0), channel_id=1, source_target_pairs={{0,2},{1,3},{2,0},{3,1},{4,6},{5,7},{6,4},{7,5},{8,10},{9,11},{10,... | collective-permute-start | bytes 2949128 | tf_op jit(solution)/shard_map/ppermute | solution.py:1221
  202.9 63.8 %collective-permute-start.3 = (bf16[192,2560]{1,0:T(8,128)(2,1)}, bf16[192,2560]{1,0:T(8,128)(2,1)}, u32[]{:S(2)}, u32[]{:S(2)}) collective-permute-start(bf16[192,2560]{1,0:T(8,128)(2,1)} %bitcast.12.grad0), channel_id=1, source_target_pairs={{0,3},{1,0},{2,1},{3,2},{4,7},{5,4},{6,5},{7,6},{8,11},{9,8},{10,9... | collective-permute-start | bytes 2949128 | tf_op jit(solution)/shard_map/ppermute | solution.py:1221
  202.9 2.1 copy-start.8
  205.9 20.1 %copy-start.7 = (f32[16,2560]{1,0:T(8,128)S(1)}, f32[16,2560]{1,0:T(8,128)}, u32[]{:S(2)}) copy-start(f32[16,2560]{1,0:T(8,128)} %small_table.1.table.small.gain) | copy-start | bytes 491524
  221.6 1.3 copy-start.3
  223.8 2.1 collective-permute-start
  226.0 28.5 %copy-start.4 = (f32[192,2560]{1,0:T(8,128)S(1)}, f32[192,2560]{1,0:T(8,128)}, u32[]{:S(2)}) copy-start(f32[192,2560]{1,0:T(8,128)} %copy-done.3) | copy-start | bytes 5898244
  235.5 1.3 copy-start.1
  236.8 1.3 copy-start.11
  239.1 15.4 %copy-start = (f32[192,2560]{1,0:T(8,128)}, f32[192,2560]{1,0:T(8,128)S(1)}, u32[]{:S(2)}) copy-start(f32[192,2560]{1,0:T(8,128)S(1)} %get-tuple-element.66.local) | copy-start | bytes 5898244
  254.5 1.2 copy-start.9
  255.7 8.6 %copy-start.26 = (bf16[192,2560]{1,0:T(8,128)(2,1)}, bf16[192,2560]{1,0:T(8,128)(2,1)S(1)}, u32[]{:S(2)}) copy-start(bf16[192,2560]{1,0:T(8,128)(2,1)S(1)} %fusion.17.mixed) | copy-start | bytes 2949124
  264.3 1.3 copy-start.23
  406.3 367.3 %reduce-scatter.5.cloned.1.call-start = ((), (), s32[]{:S(2)}) async-start(), calls=%async_computation.4 | async-start | bytes 4915200 | tf_op jit(solution)/shard_map/reduce_scatter | solution.py:1396
  472.0 42.4 %collective-permute-start.6 = (bf16[160,5760]{1,0:T(8,128)(2,1)}, bf16[160,5760]{1,0:T(8,128)(2,1)}, u32[]{:S(2)}, u32[]{:S(2)}) collective-permute-start(bf16[160,5760]{1,0:T(8,128)(2,1)} %get-tuple-element.89), channel_id=1, source_target_pairs={{0,8},{4,12},{8,0},{12,4},{16,24},{20,28},{24,16},{28,20},{1,9},{5... | collective-permute-start | bytes 5529608 | tf_op jit(solution)/shard_map/ppermute | solution.py:1231
  472.1 42.4 %collective-permute-start.7 = (bf16[160,5760]{1,0:T(8,128)(2,1)}, bf16[160,5760]{1,0:T(8,128)(2,1)}, u32[]{:S(2)}, u32[]{:S(2)}) collective-permute-start(bf16[160,5760]{1,0:T(8,128)(2,1)} %get-tuple-element.90), channel_id=1, source_target_pairs={{0,16},{4,20},{8,24},{12,28},{16,0},{20,4},{24,8},{28,12},{1,17},{... | collective-permute-start | bytes 5529608 | tf_op jit(solution)/shard_map/ppermute | solution.py:1235
  477.3 2.4 copy-start.24
  477.3 2.7 copy-start.29
  481.8 6.6 copy-start.30
  481.8 6.7 copy-start.2
  481.8 6.7 copy-start.5
  501.2 1.3 copy-start.12
  502.4 1.3 copy-start.14
  524.4 42.8 %collective-permute-start.10 = (bf16[160,5760]{1,0:T(8,128)(2,1)}, bf16[160,5760]{1,0:T(8,128)(2,1)}, u32[]{:S(2)}, u32[]{:S(2)}) collective-permute-start(bf16[160,5760]{1,0:T(8,128)(2,1)} %get-tuple-element.104), channel_id=1, source_target_pairs={{0,16},{4,20},{8,24},{12,28},{16,0},{20,4},{24,8},{28,12},{1,17},{... | collective-permute-start | bytes 5529608 | tf_op jit(solution)/shard_map/ppermute | solution.py:1235
  524.8 42.5 %collective-permute-start.9 = (bf16[160,5760]{1,0:T(8,128)(2,1)}, bf16[160,5760]{1,0:T(8,128)(2,1)}, u32[]{:S(2)}, u32[]{:S(2)}) collective-permute-start(bf16[160,5760]{1,0:T(8,128)(2,1)} %get-tuple-element.103), channel_id=1, source_target_pairs={{0,8},{4,12},{8,0},{12,4},{16,24},{20,28},{24,16},{28,20},{1,9},{5... | collective-permute-start | bytes 5529608 | tf_op jit(solution)/shard_map/ppermute | solution.py:1231
  526.5 47.2 %collective-permute-start.4 = (bf16[192,2560]{1,0:T(8,128)(2,1)}, bf16[192,2560]{1,0:T(8,128)(2,1)}, u32[]{:S(2)}, u32[]{:S(2)}) collective-permute-start(bf16[192,2560]{1,0:T(8,128)(2,1)} %copy-done.30), channel_id=1, source_target_pairs={{0,4},{4,0},{8,12},{12,8},{16,20},{20,16},{24,28},{28,24},{1,5},{5... | collective-permute-start | bytes 2949128 | tf_op jit(solution)/shard_map/ppermute | solution.py:1227
  526.6 1.5 copy-start.13
  528.1 1.5 copy-start.15
  529.7 1.5 copy-start.19
  542.6 1.1 copy-start.16
  543.6 1.1 copy-start.17
  544.7 1.3 copy-start.21
  546.3 6.0 collective-permute-start.8
  547.6 26.1 %collective-permute-start.5 = (bf16[192,2560]{1,0:T(8,128)(2,1)}, bf16[192,2560]{1,0:T(8,128)(2,1)S(1)}, u32[]{:S(2)}, u32[]{:S(2)}) collective-permute-start(bf16[192,2560]{1,0:T(8,128)(2,1)} %copy-done.20), channel_id=1, source_target_pairs={{0,4},{4,0},{8,12},{12,8},{16,20},{20,16},{24,28},{28,24},{1,5},{5... | collective-permute-start | bytes 2949128 | tf_op jit(solution)/shard_map/ppermute | solution.py:1227
  548.8 3.3 copy-start.22
  552.2 15.1 %copy-start.32 = (bf16[320,5760]{1,0:T(8,128)(2,1)S(1)}, bf16[320,5760]{1,0:T(8,128)(2,1)}, u32[]{:S(2)}) copy-start(bf16[320,5760]{1,0:T(8,128)(2,1)} %get-tuple-element.101) | copy-start | bytes 11059204
  574.6 190.3 %copy-start.33 = (bf16[80,2560]{1,0:T(8,128)(2,1)S(1)}, bf16[80,2560]{1,0:T(8,128)(2,1)}, u32[]{:S(2)}) copy-start(bf16[80,2560]{1,0:T(8,128)(2,1)} %branch.1) | copy-start | bytes 1228804
  574.6 190.3 %copy-start.34 = (bf16[80,2560]{1,0:T(8,128)(2,1)S(1)}, bf16[80,2560]{1,0:T(8,128)(2,1)}, u32[]{:S(2)}) copy-start(bf16[80,2560]{1,0:T(8,128)(2,1)} %gelu.1) | copy-start | bytes 1228804
  763.3 3.3 copy-start.31
  765.0 2.1 copy-start.27
  765.0 2.7 copy-start.28
  767.7 3.0 copy-start.37
  767.7 3.1 copy-start.38
  771.3 2.3 copy-start.25
  773.6 2.4 copy-start.35
  (5 other events, 4.8 us)
Sparse Core Ops, SparseCore 0:
  194.1 149.8 all-gather.5
  406.4 70.8 reduce-scatter.2
  526.6 97.7 reduce-scatter.4

commit v16 on v15

--- a/solution.py
+++ b/solution.py
@@ -153,7 +153,7 @@
             jax.ShapeDtypeStruct((tok, lru), bf16),
             jax.ShapeDtypeStruct((tok, lru), f32),
         ],
-        compiler_params=pltpu.CompilerParams(vmem_limit_bytes=40 * 1024 * 1024),
+        compiler_params=pltpu.CompilerParams(vmem_limit_bytes=16 * 1024 * 1024),
         cost_estimate=pl.CostEstimate(flops=1, bytes_accessed=1, transcendentals=0),
         name="mixer_in",
     )(tokens, table, mixer_w)
@@ -688,8 +688,8 @@
 def shared_products_kernel(
     normed, normed_other, grad, grad_other, weights, pair, pair_other, hidden, hidden_other,
     beside_high, across_low, mine, beside_low, across_high, out,
-    turned, slots, stage, diag, landed, waiting, down_now, out_now,
-    load_sem, send_sem, recv_sem, store_sem, down_sem, out_sem,
+    turned, slots, stage, right, diag, landed, waiting, down_now, out_now,
+    load_sem, right_sem, send_sem, recv_sem, store_sem, down_sem, out_sem,
 ):
     s, z, _, beside, across = places()
     step = pl.program_id(0)
@@ -697,7 +697,8 @@
     chip_cols = normed.shape[1] // 4
     half = chip_cols // 2
     piece = half // 2
-    width = pair.shape[1]
+    width = hidden.shape[1]
+    tok = normed.shape[0]
     diagonal = beside + across - s
     chips = [q // 2 for q in (diagonal, beside, across, s)]
 
@@ -715,16 +716,34 @@
             for who in range(2):
                 load(side, q, who).wait()
                 stage[...] = slots[q % 2, who].T
-                turned[who, q * half : (q + 1) * half, :] = stage[
+                turned[q * half : (q + 1) * half, who * tok : (who + 1) * tok] = stage[
                     pl.ds(pl.multiple_of(s % 2 * half, 16), half), :
                 ]
                 if q < 2:
                     load(side, q + 2, who).start()
 
-    def tile(own, other, start, size):
+    def take(j):
+        sources = (hidden, hidden_other) if j == 2 else (pair, pair_other)
+        return [
+            pltpu.make_async_copy(
+                source.at[:, pl.ds(0 if j == 2 else j * width, width)],
+                right.at[j % 2, pl.ds(who * tok, tok), :],
+                right_sem.at[j % 2, who],
+            )
+            for who, source in enumerate(sources)
+        ]
+
+    def take_start(j):
+        for copy in take(j):
+            copy.start()
+
+    def take_wait(j):
+        for copy in take(j):
+            copy.wait()
+
+    def tile(start, size):
         cols = pl.ds(start, size)
-        block = mm(turned[0], own[:, cols], ((1,), (0,)))
-        block = (block + mm(turned[1], other[:, cols], ((1,), (0,)))).astype(bf16)
+        block = mm(turned[...], right[step % 2, :, cols], ((1,), (0,))).astype(bf16)
         parts = [block[n * piece : (n + 1) * piece] for n in range(8)]
         there = pl.ds(pl.multiple_of(step * width + start, 128), size)
         diag[0, :, there] = parts[0]
@@ -736,14 +755,14 @@
         mine[0:piece, cols] = parts[6]
         mine[piece:, cols] = parts[7]
 
-    def multiply(own, other):
+    def multiply():
         def one(turn, carry):
-            tile(own, other, pl.multiple_of(turn * 512, 512), 512)
+            tile(pl.multiple_of(turn * 512, 512), 512)
             return carry
 
         lax.fori_loop(0, width // 512, one, 0)
         if width % 512:
-            tile(own, other, width // 512 * 512, width % 512)
+            tile(width // 512 * 512, width % 512)
 
     def push(way, j):
         cols = pl.ds(j * width, width)
@@ -779,7 +798,7 @@
             down(t).wait()
             if t > 1:
                 out_store(t - 2).wait()
-            out_now[t % 2] = mm(hidden[...], down_now[t % 2], ((1,), (1,))).astype(bf16)
+            out_now[t % 2] = mm(right[0, 0:tok, :], down_now[t % 2], ((1,), (1,))).astype(bf16)
             out_store(t).start()
             if t + 2 < out_tiles:
                 down(t + 2).start()
@@ -787,18 +806,26 @@
     @pl.when(step == 0)
     def _():
         fetch(0)
+        take_start(0)
+        take_start(1)
         greet([(beside, z), (across, z)])
         turn(0)
+        take_wait(0)
+
+    @pl.when(step == 1)
+    def _():
+        take_wait(1)
+        take_start(2)
+        fetch(1)
 
     @pl.when(step == 2)
     def _():
         down(0).start()
         down(1).start()
         turn(1)
-
-    pl.when(step < 2)(functools.partial(multiply, pair, pair_other))
-    pl.when(step == 1)(functools.partial(fetch, 1))
-    pl.when(step == 2)(functools.partial(multiply, hidden, hidden_other))
+        take_wait(2)
+
+    multiply()
     for j in range(3):
 
         @pl.when(step == j)
@@ -832,26 +859,25 @@
     def block(rows):
         return pl.BlockSpec((rows, width), lambda j: (0, j))
 
-    pair_spec = pl.BlockSpec((tok, width), lambda j: (0, jnp.minimum(j, 1)))
-    hidden_spec = pl.BlockSpec((tok, width), lambda j: (0, 0))
     rows_out = (half // 2, half // 2, half, half // 2, half // 2)
     return pl.pallas_call(
         shared_products_kernel,
         grid=(3,),
-        in_specs=[anyspec] * 5 + [pair_spec] * 2 + [hidden_spec] * 2,
+        in_specs=[anyspec] * 9,
         out_specs=[block(rows) for rows in rows_out[:3]] + [anyspec] * 3,
         out_shape=[jax.ShapeDtypeStruct((rows, 3 * width), bf16) for rows in rows_out]
         + [jax.ShapeDtypeStruct((tok, model), bf16)],
         scratch_shapes=[
-            pltpu.VMEM((2, 4 * half, tok), bf16),
+            pltpu.VMEM((4 * half, 2 * tok), bf16),
             pltpu.VMEM((2, 2, tok, 2 * half), bf16),
             pltpu.VMEM((2 * half, tok), bf16),
+            pltpu.VMEM((2, 2 * tok, width), bf16),
             pltpu.VMEM((2, half // 2, 3 * width), bf16),
             pltpu.VMEM((2, half // 2, 3 * width), bf16),
             pltpu.VMEM((2, half // 2, 3 * width), bf16),
             pltpu.VMEM((2, 512, width), bf16),
             pltpu.VMEM((2, tok, 512), bf16),
-            dma((2, 2)), dma((2, 3)), dma((2, 3)), dma((2, 3)), dma((2,)), dma((2,)),
+            dma((2, 2)), dma((2, 2)), dma((2, 3)), dma((2, 3)), dma((2, 3)), dma((2,)), dma((2,)),
         ],
         compiler_params=pltpu.CompilerParams(
             collective_id=5, has_side_effects=True, vmem_limit_bytes=60 * 1024 * 1024
@@ -1112,12 +1138,13 @@
         copy.wait()
     turn(0)
     multiply(chip_diag, 0, lru)
+    add_rest(chip_diag)
+    for i in range(2):
+        flow(i, 1).start()
     push(0).wait_recv()
     multiply(chip_diag, 0, 0, lru)
-    add_rest(chip_diag)
     for i in range(2):
         flow(i, 0).start()
-        flow(i, 1).start()
     for q in (chip_beside, chip_across, chip):
         multiply(q, 0)
         multiply(q, 1)
@@ -1274,7 +1301,7 @@
         out_specs=out_specs,
         out_shape=out_shape,
         scratch_shapes=[pltpu.VMEM((rows, width), f32) for rows in scratch],
-        compiler_params=pltpu.CompilerParams(vmem_limit_bytes=40 * 1024 * 1024),
+        compiler_params=pltpu.CompilerParams(vmem_limit_bytes=16 * 1024 * 1024),
         cost_estimate=pl.CostEstimate(flops=1, bytes_accessed=1, transcendentals=0),
         name=name,
     )(*[a for a, _ in ins])

time: 791 us -> 787 us (level)
  Pallas kernels: 626 us -> 618 us
    unnamed x80 -> x88, local copies, waits for them, and re-layouts: 23.8 us -> 29.6 us
  transfers between devices with their start and end apart: 14 -> 14, of which waited for: 6 -> 6; matrix products, arithmetic and copies ran while one was open for 6% -> 6% of each run, Pallas kernels for 50% -> 49%
where the time goes in v16:
time: 787 us; the launch traced here: 780 us
  Pallas kernels  618 us (79%)
  local copies, waits for them, and re-layouts  33.9 us (4%)
  other arithmetic  30.8 us (4%)
  waiting for transfers between devices  24.9 us (3%)
  blocking collectives  24.3 us (3%)
  starting transfers between devices  16.8 us (2%)
  matrix products  16.1 us (2%)
  between operations  14.6 us (2%)
    pallas_call x1, Pallas kernels, scatter(): pl.pallas_call(scatter_kernel, in_specs=[anyspec] * 15, out_specs=[anyspe...  185 us
    pallas_call x1, Pallas kernels, gather(): pl.pallas_call(gather_kernel, in_specs=[anyspec] * 7, out_specs=[anyspec]...  183 us
    pallas_call x1, Pallas kernels, gather_rows(): pl.pallas_call(rows_kernel, in_specs=[anyspec] * 7, out_specs=[anyspec] *...  85.6 us
    pallas_call x1, Pallas kernels, shared_products(): pl.pallas_call(shared_products_kernel, grid=(3,), in_specs=[anyspec] * 9,...  63.5 us
    pallas_call x1, Pallas kernels, feed_forward(): pl.pallas_call(feed_forward_kernel, grid=(2,), in_specs=[block, block, an...  52.1 us
    pallas_call x3, Pallas kernels, call_heads(): pl.pallas_call(kernel, grid=(heads,), in_specs=in_specs, out_specs=out_sp...  31.8 us
    unnamed x88, local copies, waits for them, and re-layouts  29.6 us
    all_gather x2, blocking collectives, prefix(): gathered = lax.all_gather(jnp.stack(part), axis)  24.3 us
  transfers between devices with their start and end apart: 14, of which 6 were waited for; matrix products, arithmetic and copies ran while one was open for 6% of the time, Pallas kernels for 49%

profile of v16, /device:TPU:0, one launch (start us, length us, event | category | flops | bytes accessed | tf_op | source)
XLA Modules:
  0.0 779.9 jit_solution(16983347223539607051)
XLA Ops:
  8.1 1.4 stack.33
  9.6 1.5 fusion.20.first
  11.1 182.9 %gather_weights.1 = (bf16[2560,8320]{1,0:T(8,128)(2,1)}, bf16[320,5760]{1,0:T(8,128)(2,1)}) custom-call(bf16[80,640]{1,0:T(8,128)(2,1)} %fusion.20.first, bf16[80,2560]{1,0:T(8,128)(2,1)} %branch.1, bf16[80,2560]{1,0:T(8,128)(2,1)} %gelu.1, bf16[80,2560]{1,0:T(8,128)(2,1)} %outer.1, bf16[80,7680]{1,0:T(8,128)(2,1)} %gate.1, bf16[80,7680]{1,0:T(8,128)(2,1)} %up.1, ...), custom_call_target="tpu_custom_call" | custom-call | tf_op jit(solution)/shard_map/gather_weights/pallas_call | solution.py:420
  194.1 5.5 collective-permute-start.1
  199.5 3.4 collective-permute-start.2
  202.9 2.1 small_table.1.table.small.gain
  205.9 15.7 %mixer_in.1 = (bf16[192,2560]{1,0:T(8,128)(2,1)S(1)}, bf16[192,2560]{1,0:T(8,128)(2,1)S(1)}, f32[192,2560]{1,0:T(8,128)S(1)}) custom-call(bf16[192,2560]{1,0:T(8,128)(2,1)S(1)} %bitcast.43, f32[16,2560]{1,0:T(8,128)S(1)} %copy-done.9, bf16[2560,8320]{1,0:T(8,128)(2,1)} %get-tuple-element.64.columns.weights.rate_w.input_w.mixer_w), custom_call_target="tpu_custom_call" | custom-call | flops 1 | bytes 1 | tf_op jit(solution)/shard_map/mixer_in/pallas_call | solution.py:138
  221.6 1.3 copy-done.6
  223.8 1.3 collective-permute-start
  226.0 9.5 %mixer_forward.1 = (bf16[192,2560]{1,0:T(8,128)(2,1)S(1)}, f32[192,2560]{1,0:T(8,128)S(1)}, f32[192,2560]{1,0:T(8,128)S(1)}, f32[192,2560]{1,0:T(8,128)S(1)}, f32[192,2560]{1,0:T(8,128)S(1)}) custom-call(bf16[192,2560]{1,0:T(8,128)(2,1)S(1)} %get-tuple-element.65.branch, f32[8,2560]{1,0:T(8,128)S(1)} %pad_convert_fusion.prior, f32[16,2560]{1,0:T(8,128)S(1)} %copy-done.10, ...), custom_call_target="tpu_custom_call" | custom-call | flops 1 | bytes 1 | tf_op jit(solution)/shard_map/mixer_forward/pallas_call | solution.py:1297
  235.5 1.3 copy-done.3
  236.8 1.3 copy-done.14
  239.2 14.9 %all-gather.2 = f32[8,2,2560]{2,1,0:T(2,128)S(1)} all-gather(f32[1,2,2560]{2,1,0:T(2,128)S(1)} %fusion.21), channel_id=2, replica_groups=mesh['seq'=8,'fsdp'=4] {'seq'}, dimensions={0}, use_global_device_ids=true | all-gather | bytes 184320 | tf_op jit(solution)/shard_map/all_gather | solution.py:29
  255.4 1.3 copy-done
  256.6 9.5 %multiply_reduce_fusion.3 = (f32[192]{0:T(256)S(1)}, f32[192,2560]{1,0:T(8,128)S(1)}) fusion(bf16[192,2560]{1,0:T(8,128)(2,1)S(1)} %fusion.17.mixed, bf16[2560,8320]{1,0:T(8,128)(2,1)} %get-tuple-element.64.columns.weights.rate_w.input_w.mixer_w, bf16[1,192,2560]{2,1,0:T(8,128)(2,1)S(1)} %copy-done.12), kind=kOutput, calls=%fused_computation.28 | convolution fusion | flops 2518548224 | bytes 17040128 | tf_op jit(solution)/shard_map/dot_general | solution.py:61
  266.1 1.2 copy-done.27
  268.5 85.6 %gather_rows.1 = (bf16[768,2560]{1,0:T(8,128)(2,1)}, bf16[768,2560]{1,0:T(8,128)(2,1)}, bf16[768,2560]{1,0:T(8,128)(2,1)}, bf16[768,2560]{1,0:T(8,128)(2,1)}, bf...) custom-call(bf16[192,2560]{1,0:T(8,128)(2,1)} %multiply_convert_fusion.normed, bf16[192,2560]{1,0:T(8,128)(2,1)} %bitcast.12.grad0, ...), custom_call_target="tpu_custom_call" | custom-call | tf_op jit(solution)/shard_map/gather_rows/pallas_call | solution.py:547
  354.2 52.1 %feed_forward.1 = (bf16[768,1920]{1,0:T(8,128)(2,1)}, bf16[768,1920]{1,0:T(8,128)(2,1)}, bf16[768,3840]{1,0:T(8,128)(2,1)}, bf16[768,3840]{1,0:T(8,128)(2,1)}, bf16[768,2560]{1,0:T(8,128)(2,1)}) custom-call(bf16[768,2560]{1,0:T(8,128)(2,1)} %get-tuple-element.73.normed, bf16[768,2560]{1,0:T(8,128)(2,1)} %get-tuple-element.74.grad_out.grad, ...), custom_call_target="tpu_custom_call" | custom-call | tf_op jit(solution)/shard_map/feed_forward/pallas_call | solution.py:654
  406.3 63.5 %feed_forward_products.1 = (bf16[160,5760]{1,0:T(8,128)(2,1)}, bf16[160,5760]{1,0:T(8,128)(2,1)}, bf16[320,5760]{1,0:T(8,128)(2,1)}, bf16[160,5760]{1,0:T(8,128)...) custom-call(bf16[768,2560]{1,0:T(8,128)(2,1)} %get-tuple-element.73.normed, ...), custom_call_target="tpu_custom_call" | custom-call | tf_op jit(solution)/shard_map/feed_forward_products/pallas_call | solution.py:863
  469.9 1.8 collective-permute-start.7
  471.8 5.5 reduce-scatter.3.cloned.1.call-done
  477.3 2.3 multiply_reduce_fusion.2
  480.0 1.8 add_convert_fusion.3.grad_mix
  481.9 6.6 fusion.grad_mixed
  488.7 11.7 %mixer_backward_scan.1 = (bf16[192,2560]{1,0:T(8,128)(2,1)S(1)}, f32[192,2560]{1,0:T(8,128)S(1)}, f32[192,2560]{1,0:T(8,128)S(1)}, f32[8,2560]{1,0:T(8,128)S(1)}) custom-call(f32[192,2560]{1,0:T(8,128)S(1)} %fusion.grad_mixed, f32[192,2560]{1,0:T(8,128)S(1)} %copy-done.8, f32[192,2560]{1,0:T(8,128)S(1)} %copy-done.4, f32[192,2560]{1,0:T(8,128)S(1)} %get-tuple-element.67.cum, ...), custom_call_target="tpu_custom_call" | custom-call | flops 1 | bytes 1 | tf_op jit(solution)/shard_map/mixer_backward_scan/pallas_call | solution.py:1297
  500.4 1.3 copy-done.16
  501.7 1.3 copy-done.18
  504.0 8.3 %collective-permute-done.6 = bf16[160,5760]{1,0:T(8,128)(2,1)} collective-permute-done((bf16[160,5760]{1,0:T(8,128)(2,1)}, bf16[160,5760]{1,0:T(8,128)(2,1)}, u32[]{:S(2)}, u32[]{:S(2)}) %collective-permute-start.6) | collective-permute-done | bytes 1843232 | tf_op jit(solution)/shard_map/ppermute | solution.py:1258
  512.4 9.4 %all-gather.3 = f32[8,2,2560]{2,1,0:T(2,128)S(1)} all-gather(f32[1,2,2560]{2,1,0:T(2,128)S(1)} %fusion.22), channel_id=3, replica_groups=mesh['seq'=8,'fsdp'=4] {'seq'}, dimensions={0}, use_global_device_ids=true | all-gather | bytes 184320 | tf_op jit(solution)/shard_map/all_gather | solution.py:29
  522.7 1.7 collective-permute-start.9
  524.5 1.5 copy-done.2
  526.0 1.5 copy-done.5
  527.6 1.9 copy-done.15
  529.4 1.5 copy-done.17
  531.0 1.5 copy-done.19
  532.5 1.2 copy-done.23
  533.7 10.6 %mixer_backward.1 = (f32[192,2560]{1,0:T(8,128)S(1)}, f32[8,2560]{1,0:T(8,128)S(1)}, bf16[2560,256]{1,0:T(8,128)(2,1)S(1)}, bf16[2560,256]{1,0:T(8,128)(2,1)S(1)}, f32[8,2560]{1,0:T(8,128)S(1)}) custom-call(f32[192,2560]{1,0:T(8,128)S(1)} %copy-done.17, f32[192,2560]{1,0:T(8,128)S(1)} %copy-done.19, f32[8,2560]{1,0:T(8,128)S(1)} %broadcast_in_dim.9.incoming, ...), custom_call_target="tpu_custom_call" | custom-call | flops 1 | bytes 1 | tf_op jit(solution)/shard_map/mixer_backward/pallas_call | solution.py:1297
  546.4 1.3 copy-done.25
  548.1 1.3 collective-permute-start.8
  550.6 3.3 fusion.8.rest
  555.0 10.0 %collective-permute-done.10 = bf16[160,5760]{1,0:T(8,128)(2,1)} collective-permute-done((bf16[160,5760]{1,0:T(8,128)(2,1)}, bf16[160,5760]{1,0:T(8,128)(2,1)}, u32[]{:S(2)}, u32[]{:S(2)}) %collective-permute-start.10) | collective-permute-done | bytes 1843232 | tf_op jit(solution)/shard_map/ppermute | solution.py:1262
  565.2 6.4 add_convert_fusion
  572.5 184.8 %scatter_gradients.1 = (bf16[80,8320]{1,0:T(8,128)(2,1)}, bf16[3,80,7680]{2,1,0:T(8,128)(2,1)}, bf16[192,2560]{1,0:T(8,128)(2,1)}) custom-call(bf16[192,2560]{1,0:T(8,128)(2,1)} %copy-done.13, bf16[192,2560]{1,0:T(8,128)(2,1)} %get-tuple-element.72.normed_other, bf16[192,2560]{1,0:T(8,128)(2,1)} %copy-done.34, ...), custom_call_target="tpu_custom_call" | custom-call | tf_op jit(solution)/shard_map/scatter_gradients/pallas_call | solution.py:1204
  759.4 1.7 slice_convert_fusion.1
  761.1 1.6 multiply_reduce_fusion.4
  763.9 3.0 multiply_reduce_fusion
  768.1 1.6 bitcast_convert_fusion
  769.7 2.4 fusion.18
  (126 shorter events, 21.3 us)
Async XLA Ops:
  7.2 347.0 %all-gather.6.cloned.1.call-start = ((), (), s32[]{:S(2)}) async-start(), calls=%async_computation.2 | async-start | bytes 33177600 | tf_op jit(solution)/shard_map/all_gather | solution.py:1354
  194.0 283.3 %reduce-scatter.3.cloned.1.call-start = ((), (), s32[]{:S(2)}) async-start(), calls=%async_computation.3 | async-start | bytes 4915200 | tf_op jit(solution)/shard_map/reduce_scatter | solution.py:1405
  194.1 74.5 %collective-permute-start.1 = (bf16[192,2560]{1,0:T(8,128)(2,1)}, bf16[192,2560]{1,0:T(8,128)(2,1)}, u32[]{:S(2)}, u32[]{:S(2)}) collective-permute-start(bf16[192,2560]{1,0:T(8,128)(2,1)} %bitcast.12.grad0), channel_id=1, source_target_pairs={{0,1},{1,2},{2,3},{3,0},{4,5},{5,6},{6,7},{7,4},{8,9},{9,10},{10,1... | collective-permute-start | bytes 2949128 | tf_op jit(solution)/shard_map/ppermute | solution.py:1248
  199.5 69.0 %collective-permute-start.2 = (bf16[192,2560]{1,0:T(8,128)(2,1)}, bf16[192,2560]{1,0:T(8,128)(2,1)}, u32[]{:S(2)}, u32[]{:S(2)}) collective-permute-start(bf16[192,2560]{1,0:T(8,128)(2,1)} %bitcast.12.grad0), channel_id=1, source_target_pairs={{0,2},{1,3},{2,0},{3,1},{4,6},{5,7},{6,4},{7,5},{8,10},{9,11},{10,... | collective-permute-start | bytes 2949128 | tf_op jit(solution)/shard_map/ppermute | solution.py:1248
  202.9 65.6 %collective-permute-start.3 = (bf16[192,2560]{1,0:T(8,128)(2,1)}, bf16[192,2560]{1,0:T(8,128)(2,1)}, u32[]{:S(2)}, u32[]{:S(2)}) collective-permute-start(bf16[192,2560]{1,0:T(8,128)(2,1)} %bitcast.12.grad0), channel_id=1, source_target_pairs={{0,3},{1,0},{2,1},{3,2},{4,7},{5,4},{6,5},{7,6},{8,11},{9,8},{10,9... | collective-permute-start | bytes 2949128 | tf_op jit(solution)/shard_map/ppermute | solution.py:1248
  202.9 2.1 copy-start.11
  205.9 20.1 %copy-start.10 = (f32[16,2560]{1,0:T(8,128)S(1)}, f32[16,2560]{1,0:T(8,128)}, u32[]{:S(2)}) copy-start(f32[16,2560]{1,0:T(8,128)} %small_table.1.table.small.gain) | copy-start | bytes 491524
  221.6 1.3 copy-start.6
  223.8 2.1 collective-permute-start
  226.0 28.5 %copy-start.7 = (f32[192,2560]{1,0:T(8,128)S(1)}, f32[192,2560]{1,0:T(8,128)}, u32[]{:S(2)}) copy-start(f32[192,2560]{1,0:T(8,128)} %copy-done.6) | copy-start | bytes 5898244
  235.5 1.3 copy-start.3
  236.8 1.3 copy-start.14
  254.5 2.1 copy-start.12
  255.3 1.3 copy-start
  256.6 9.5 %copy-start.30 = (bf16[192,2560]{1,0:T(8,128)(2,1)}, bf16[192,2560]{1,0:T(8,128)(2,1)S(1)}, u32[]{:S(2)}) copy-start(bf16[192,2560]{1,0:T(8,128)(2,1)S(1)} %fusion.17.mixed) | copy-start | bytes 2949124
  406.3 363.5 %reduce-scatter.5.cloned.1.call-start = ((), (), s32[]{:S(2)}) async-start(), calls=%async_computation.4 | async-start | bytes 4915200 | tf_op jit(solution)/shard_map/reduce_scatter | solution.py:1423
  469.9 42.4 %collective-permute-start.6 = (bf16[160,5760]{1,0:T(8,128)(2,1)}, bf16[160,5760]{1,0:T(8,128)(2,1)}, u32[]{:S(2)}, u32[]{:S(2)}) collective-permute-start(bf16[160,5760]{1,0:T(8,128)(2,1)} %get-tuple-element.89), channel_id=1, source_target_pairs={{0,8},{4,12},{8,0},{12,4},{16,24},{20,28},{24,16},{28,20},{1,9},{5... | collective-permute-start | bytes 5529608 | tf_op jit(solution)/shard_map/ppermute | solution.py:1258
  469.9 42.4 %collective-permute-start.7 = (bf16[160,5760]{1,0:T(8,128)(2,1)}, bf16[160,5760]{1,0:T(8,128)(2,1)}, u32[]{:S(2)}, u32[]{:S(2)}) collective-permute-start(bf16[160,5760]{1,0:T(8,128)(2,1)} %get-tuple-element.90), channel_id=1, source_target_pairs={{0,16},{4,20},{8,24},{12,28},{16,0},{20,4},{24,8},{28,12},{1,17},{... | collective-permute-start | bytes 5529608 | tf_op jit(solution)/shard_map/ppermute | solution.py:1262
  477.3 2.4 copy-start.28
  477.3 2.7 copy-start.33
  481.8 6.7 copy-start.34
  481.8 6.7 copy-start.1
  481.8 6.7 copy-start.4
  481.9 6.8 copy-start.8
  500.4 1.3 copy-start.16
  501.7 1.3 copy-start.18
  522.3 42.8 %collective-permute-start.10 = (bf16[160,5760]{1,0:T(8,128)(2,1)}, bf16[160,5760]{1,0:T(8,128)(2,1)}, u32[]{:S(2)}, u32[]{:S(2)}) collective-permute-start(bf16[160,5760]{1,0:T(8,128)(2,1)} %get-tuple-element.104), channel_id=1, source_target_pairs={{0,16},{4,20},{8,24},{12,28},{16,0},{20,4},{24,8},{28,12},{1,17},{... | collective-permute-start | bytes 5529608 | tf_op jit(solution)/shard_map/ppermute | solution.py:1262
  522.7 42.5 %collective-permute-start.9 = (bf16[160,5760]{1,0:T(8,128)(2,1)}, bf16[160,5760]{1,0:T(8,128)(2,1)}, u32[]{:S(2)}, u32[]{:S(2)}) collective-permute-start(bf16[160,5760]{1,0:T(8,128)(2,1)} %get-tuple-element.103), channel_id=1, source_target_pairs={{0,8},{4,12},{8,0},{12,4},{16,24},{20,28},{24,16},{28,20},{1,9},{5... | collective-permute-start | bytes 5529608 | tf_op jit(solution)/shard_map/ppermute | solution.py:1258
  524.4 47.2 %collective-permute-start.4 = (bf16[192,2560]{1,0:T(8,128)(2,1)}, bf16[192,2560]{1,0:T(8,128)(2,1)}, u32[]{:S(2)}, u32[]{:S(2)}) collective-permute-start(bf16[192,2560]{1,0:T(8,128)(2,1)} %copy-done.34), channel_id=1, source_target_pairs={{0,4},{4,0},{8,12},{12,8},{16,20},{20,16},{24,28},{28,24},{1,5},{5... | collective-permute-start | bytes 2949128 | tf_op jit(solution)/shard_map/ppermute | solution.py:1254
  524.5 1.5 copy-start.2
  526.0 1.6 copy-start.5
  527.6 1.9 copy-start.15
  529.4 1.5 copy-start.17
  531.0 1.5 copy-start.19
  546.4 1.3 copy-start.25
  548.1 5.9 collective-permute-start.8
  549.4 22.2 %collective-permute-start.5 = (bf16[192,2560]{1,0:T(8,128)(2,1)}, bf16[192,2560]{1,0:T(8,128)(2,1)S(1)}, u32[]{:S(2)}, u32[]{:S(2)}) collective-permute-start(bf16[192,2560]{1,0:T(8,128)(2,1)} %copy-done.24), channel_id=1, source_target_pairs={{0,4},{4,0},{8,12},{12,8},{16,20},{20,16},{24,28},{28,24},{1,5},{5... | collective-permute-start | bytes 2949128 | tf_op jit(solution)/shard_map/ppermute | solution.py:1254
  550.6 3.3 copy-start.26
  553.8 11.3 %copy-start.36 = (bf16[320,5760]{1,0:T(8,128)(2,1)S(1)}, bf16[320,5760]{1,0:T(8,128)(2,1)}, u32[]{:S(2)}) copy-start(bf16[320,5760]{1,0:T(8,128)(2,1)} %get-tuple-element.101) | copy-start | bytes 11059204
  572.5 188.6 %copy-start.37 = (bf16[80,2560]{1,0:T(8,128)(2,1)S(1)}, bf16[80,2560]{1,0:T(8,128)(2,1)}, u32[]{:S(2)}) copy-start(bf16[80,2560]{1,0:T(8,128)(2,1)} %branch.1) | copy-start | bytes 1228804
  572.5 188.6 %copy-start.38 = (bf16[80,2560]{1,0:T(8,128)(2,1)S(1)}, bf16[80,2560]{1,0:T(8,128)(2,1)}, u32[]{:S(2)}) copy-start(bf16[80,2560]{1,0:T(8,128)(2,1)} %gelu.1) | copy-start | bytes 1228804
  759.4 3.3 copy-start.35
  761.1 2.1 copy-start.31
  761.1 2.7 copy-start.32
  763.8 3.0 copy-start.41
  763.8 3.1 copy-start.42
  767.4 2.3 copy-start.29
  769.7 2.4 copy-start.39
  (9 other events, 9.4 us)
Sparse Core Ops, SparseCore 0:
  194.1 149.8 all-gather.5
  406.4 70.8 reduce-scatter.2
  524.5 97.7 reduce-scatter.4

commit v17 on v16

--- a/solution.py
+++ b/solution.py
@@ -51,10 +51,11 @@
 
 
 def gelu_parts(x):
-    inner = jnp.tanh(GELU_C * (x + GELU_A * x * x * x))
-    return 0.5 * x * (1.0 + inner), 0.5 * (1.0 + inner) + 0.5 * x * (1.0 - inner * inner) * (
-        GELU_C * (1.0 + 3.0 * GELU_A * x * x)
-    )
+    square = x * x
+    inner = jnp.tanh(x * (GELU_C + GELU_C * GELU_A * square))
+    open_part = 0.5 + 0.5 * inner
+    value = x * open_part
+    return value, open_part + value * (1.0 - inner) * (GELU_C + 3.0 * GELU_C * GELU_A * square)
 
 
 def mm(left, right, dims):
@@ -722,6 +723,18 @@
                 if q < 2:
                     load(side, q + 2, who).start()
 
+    pieces = column_tiles(width)
+
+    def push(way, cols, index):
+        return pltpu.make_async_remote_copy(
+            src_ref=diag.at[way, :, cols],
+            dst_ref=landed.at[way, :, cols],
+            send_sem=send_sem.at[way, index],
+            recv_sem=recv_sem.at[way, index],
+            device_id=(across if way == 0 else beside, z),
+            device_id_type=MESH,
+        )
+
     def take(j):
         sources = (hidden, hidden_other) if j == 2 else (pair, pair_other)
         return [
@@ -746,6 +759,7 @@
         block = mm(turned[...], right[step % 2, :, cols], ((1,), (0,))).astype(bf16)
         parts = [block[n * piece : (n + 1) * piece] for n in range(8)]
         there = pl.ds(pl.multiple_of(step * width + start, 128), size)
+        index = step * len(pieces) + start // 512
         diag[0, :, there] = parts[0]
         diag[1, :, there] = parts[1]
         waiting[0, :, there] = parts[2]
@@ -754,6 +768,8 @@
         waiting[1, :, there] = parts[5]
         mine[0:piece, cols] = parts[6]
         mine[piece:, cols] = parts[7]
+        for way in range(2):
+            push(way, there, index).start()
 
     def multiply():
         def one(turn, carry):
@@ -763,17 +779,6 @@
         lax.fori_loop(0, width // 512, one, 0)
         if width % 512:
             tile(width // 512 * 512, width % 512)
-
-    def push(way, j):
-        cols = pl.ds(j * width, width)
-        return pltpu.make_async_remote_copy(
-            src_ref=diag.at[way, :, cols],
-            dst_ref=landed.at[way, :, cols],
-            send_sem=send_sem.at[way, j],
-            recv_sem=recv_sem.at[way, j],
-            device_id=(across if way == 0 else beside, z),
-            device_id_type=MESH,
-        )
 
     def store(way, j):
         cols = pl.ds(j * width, width)
@@ -826,24 +831,24 @@
         take_wait(2)
 
     multiply()
-    for j in range(3):
-
-        @pl.when(step == j)
-        def _(j=j):
-            push(0, j).start()
-            push(1, j).start()
-
     @pl.when(step == 2)
     def _():
         out_product()
+        pushed = [
+            (way, pl.ds(j * width + start, size), j * len(pieces) + n, j)
+            for j in range(3)
+            for n, (start, size) in enumerate(pieces)
+            for way in range(2)
+        ]
+        for way, cols, index, j in pushed:
+            push(way, cols, index).wait_recv()
+            if index % len(pieces) == len(pieces) - 1:
+                add_columns(waiting.at[way], [landed.at[way]], j * width, width, 384)
+                store(way, j).start()
+        for way, cols, index, j in pushed:
+            push(way, cols, index).wait_send()
         for j in range(3):
             for way in range(2):
-                push(way, j).wait_recv()
-                add_columns(waiting.at[way], [landed.at[way]], j * width, width, 384)
-                store(way, j).start()
-        for j in range(3):
-            for way in range(2):
-                push(way, j).wait_send()
                 store(way, j).wait()
         for t in range(out_tiles - 2, out_tiles):
             out_store(t).wait()
@@ -877,7 +882,7 @@
             pltpu.VMEM((2, half // 2, 3 * width), bf16),
             pltpu.VMEM((2, 512, width), bf16),
             pltpu.VMEM((2, tok, 512), bf16),
-            dma((2, 2)), dma((2, 2)), dma((2, 3)), dma((2, 3)), dma((2, 3)), dma((2,)), dma((2,)),
+            dma((2, 2)), dma((2, 2)), dma((2, 12)), dma((2, 12)), dma((2, 3)), dma((2,)), dma((2,)),
         ],
         compiler_params=pltpu.CompilerParams(
             collective_id=5, has_side_effects=True, vmem_limit_bytes=60 * 1024 * 1024

time: 787 us -> 783 us (level)
  no operation moved by 1% of the time
where the time goes in v17:
time: 783 us; the launch traced here: 774 us
  Pallas kernels  612 us (78%)
  local copies, waits for them, and re-layouts  33.9 us (4%)
  other arithmetic  30.8 us (4%)
  waiting for transfers between devices  25.5 us (3%)
  blocking collectives  24.3 us (3%)
  starting transfers between devices  16.8 us (2%)
  matrix products  16.1 us (2%)
  between operations  14.5 us (2%)
    pallas_call x1, Pallas kernels, scatter(): pl.pallas_call(scatter_kernel, in_specs=[anyspec] * 15, out_specs=[anyspe...  185 us
    pallas_call x1, Pallas kernels, gather(): pl.pallas_call(gather_kernel, in_specs=[anyspec] * 7, out_specs=[anyspec]...  183 us
    pallas_call x1, Pallas kernels, gather_rows(): pl.pallas_call(rows_kernel, in_specs=[anyspec] * 7, out_specs=[anyspec] *...  85.6 us
    pallas_call x1, Pallas kernels, shared_products(): pl.pallas_call(shared_products_kernel, grid=(3,), in_specs=[anyspec] * 9,...  57.2 us
    pallas_call x1, Pallas kernels, feed_forward(): pl.pallas_call(feed_forward_kernel, grid=(2,), in_specs=[block, block, an...  52.6 us
    pallas_call x3, Pallas kernels, call_heads(): pl.pallas_call(kernel, grid=(heads,), in_specs=in_specs, out_specs=out_sp...  31.3 us
    unnamed x88, local copies, waits for them, and re-layouts  29.6 us
    all_gather x2, blocking collectives, prefix(): gathered = lax.all_gather(jnp.stack(part), axis)  24.3 us
  transfers between devices with their start and end apart: 14, of which 6 were waited for; matrix products, arithmetic and copies ran while one was open for 6% of the time, Pallas kernels for 49%

profile of v17, /device:TPU:0, one launch (start us, length us, event | category | flops | bytes accessed | tf_op | source)
XLA Modules:
  0.0 774.0 jit_solution(5305389539222703135)
XLA Ops:
  8.1 1.4 stack.33
  9.6 1.5 fusion.20.first
  11.1 182.9 %gather_weights.1 = (bf16[2560,8320]{1,0:T(8,128)(2,1)}, bf16[320,5760]{1,0:T(8,128)(2,1)}) custom-call(bf16[80,640]{1,0:T(8,128)(2,1)} %fusion.20.first, bf16[80,2560]{1,0:T(8,128)(2,1)} %branch.1, bf16[80,2560]{1,0:T(8,128)(2,1)} %gelu.1, bf16[80,2560]{1,0:T(8,128)(2,1)} %outer.1, bf16[80,7680]{1,0:T(8,128)(2,1)} %gate.1, bf16[80,7680]{1,0:T(8,128)(2,1)} %up.1, ...), custom_call_target="tpu_custom_call" | custom-call | tf_op jit(solution)/shard_map/gather_weights/pallas_call | solution.py:421
  194.1 5.5 collective-permute-start.1
  199.5 3.4 collective-permute-start.2
  202.9 2.1 small_table.1.table.small.gain
  205.9 15.7 %mixer_in.1 = (bf16[192,2560]{1,0:T(8,128)(2,1)S(1)}, bf16[192,2560]{1,0:T(8,128)(2,1)S(1)}, f32[192,2560]{1,0:T(8,128)S(1)}) custom-call(bf16[192,2560]{1,0:T(8,128)(2,1)S(1)} %bitcast.43, f32[16,2560]{1,0:T(8,128)S(1)} %copy-done.9, bf16[2560,8320]{1,0:T(8,128)(2,1)} %get-tuple-element.64.columns.weights.rate_w.input_w.mixer_w), custom_call_target="tpu_custom_call" | custom-call | flops 1 | bytes 1 | tf_op jit(solution)/shard_map/mixer_in/pallas_call | solution.py:139
  221.6 1.3 copy-done.6
  223.8 1.3 collective-permute-start
  226.0 9.5 %mixer_forward.1 = (bf16[192,2560]{1,0:T(8,128)(2,1)S(1)}, f32[192,2560]{1,0:T(8,128)S(1)}, f32[192,2560]{1,0:T(8,128)S(1)}, f32[192,2560]{1,0:T(8,128)S(1)}, f32[192,2560]{1,0:T(8,128)S(1)}) custom-call(bf16[192,2560]{1,0:T(8,128)(2,1)S(1)} %get-tuple-element.65.branch, f32[8,2560]{1,0:T(8,128)S(1)} %pad_convert_fusion.prior, f32[16,2560]{1,0:T(8,128)S(1)} %copy-done.10, ...), custom_call_target="tpu_custom_call" | custom-call | flops 1 | bytes 1 | tf_op jit(solution)/shard_map/mixer_forward/pallas_call | solution.py:1302
  235.5 1.3 copy-done.3
  236.8 1.3 copy-done.14
  239.2 14.9 %all-gather.2 = f32[8,2,2560]{2,1,0:T(2,128)S(1)} all-gather(f32[1,2,2560]{2,1,0:T(2,128)S(1)} %fusion.21), channel_id=2, replica_groups=mesh['seq'=8,'fsdp'=4] {'seq'}, dimensions={0}, use_global_device_ids=true | all-gather | bytes 184320 | tf_op jit(solution)/shard_map/all_gather | solution.py:29
  255.4 1.3 copy-done
  256.6 9.5 %multiply_reduce_fusion.3 = (f32[192]{0:T(256)S(1)}, f32[192,2560]{1,0:T(8,128)S(1)}) fusion(bf16[192,2560]{1,0:T(8,128)(2,1)S(1)} %fusion.17.mixed, bf16[2560,8320]{1,0:T(8,128)(2,1)} %get-tuple-element.64.columns.weights.rate_w.input_w.mixer_w, bf16[1,192,2560]{2,1,0:T(8,128)(2,1)S(1)} %copy-done.12), kind=kOutput, calls=%fused_computation.28 | convolution fusion | flops 2518548224 | bytes 17040128 | tf_op jit(solution)/shard_map/dot_general | solution.py:62
  266.1 1.2 copy-done.27
  268.5 85.6 %gather_rows.1 = (bf16[768,2560]{1,0:T(8,128)(2,1)}, bf16[768,2560]{1,0:T(8,128)(2,1)}, bf16[768,2560]{1,0:T(8,128)(2,1)}, bf16[768,2560]{1,0:T(8,128)(2,1)}, bf...) custom-call(bf16[192,2560]{1,0:T(8,128)(2,1)} %multiply_convert_fusion.normed, bf16[192,2560]{1,0:T(8,128)(2,1)} %bitcast.12.grad0, ...), custom_call_target="tpu_custom_call" | custom-call | tf_op jit(solution)/shard_map/gather_rows/pallas_call | solution.py:548
  354.2 52.6 %feed_forward.1 = (bf16[768,1920]{1,0:T(8,128)(2,1)}, bf16[768,1920]{1,0:T(8,128)(2,1)}, bf16[768,3840]{1,0:T(8,128)(2,1)}, bf16[768,3840]{1,0:T(8,128)(2,1)}, bf16[768,2560]{1,0:T(8,128)(2,1)}) custom-call(bf16[768,2560]{1,0:T(8,128)(2,1)} %get-tuple-element.73.normed, bf16[768,2560]{1,0:T(8,128)(2,1)} %get-tuple-element.74.grad_out.grad, ...), custom_call_target="tpu_custom_call" | custom-call | tf_op jit(solution)/shard_map/feed_forward/pallas_call | solution.py:655
  406.8 57.2 %feed_forward_products.1 = (bf16[160,5760]{1,0:T(8,128)(2,1)}, bf16[160,5760]{1,0:T(8,128)(2,1)}, bf16[320,5760]{1,0:T(8,128)(2,1)}, bf16[160,5760]{1,0:T(8,128)...) custom-call(bf16[768,2560]{1,0:T(8,128)(2,1)} %get-tuple-element.73.normed, ...), custom_call_target="tpu_custom_call" | custom-call | tf_op jit(solution)/shard_map/feed_forward_products/pallas_call | solution.py:868
  464.2 1.8 collective-permute-start.7
  466.0 11.8 %reduce-scatter.3.cloned.1.call-done = bf16[192,2560]{1,0:T(8,128)(2,1)} async-done(((bf16[768,2560]{1,0:T(8,128)(2,1)}), bf16[192,2560]{1,0:T(8,128)(2,1)}) %reduce-scatter.3.cloned.1.call-update) | async-done | bytes 983056 | tf_op jit(solution)/shard_map/reduce_scatter | solution.py:1410
  477.8 2.3 multiply_reduce_fusion.2
  480.5 1.8 add_convert_fusion.3.grad_mix
  482.4 6.6 fusion.grad_mixed
  489.2 11.2 %mixer_backward_scan.1 = (bf16[192,2560]{1,0:T(8,128)(2,1)S(1)}, f32[192,2560]{1,0:T(8,128)S(1)}, f32[192,2560]{1,0:T(8,128)S(1)}, f32[8,2560]{1,0:T(8,128)S(1)}) custom-call(f32[192,2560]{1,0:T(8,128)S(1)} %fusion.grad_mixed, f32[192,2560]{1,0:T(8,128)S(1)} %copy-done.8, f32[192,2560]{1,0:T(8,128)S(1)} %copy-done.4, f32[192,2560]{1,0:T(8,128)S(1)} %get-tuple-element.67.cum, ...), custom_call_target="tpu_custom_call" | custom-call | flops 1 | bytes 1 | tf_op jit(solution)/shard_map/mixer_backward_scan/pallas_call | solution.py:1302
  500.4 1.3 copy-done.16
  501.7 1.3 copy-done.18
  503.9 2.6 collective-permute-done.6
  506.6 9.4 %all-gather.3 = f32[8,2,2560]{2,1,0:T(2,128)S(1)} all-gather(f32[1,2,2560]{2,1,0:T(2,128)S(1)} %fusion.22), channel_id=3, replica_groups=mesh['seq'=8,'fsdp'=4] {'seq'}, dimensions={0}, use_global_device_ids=true | all-gather | bytes 184320 | tf_op jit(solution)/shard_map/all_gather | solution.py:29
  516.9 1.7 collective-permute-start.9
  518.7 1.5 copy-done.2
  520.3 1.5 copy-done.5
  521.8 1.9 copy-done.15
  523.7 1.5 copy-done.17
  525.2 1.5 copy-done.19
  526.7 1.2 copy-done.23
  527.9 10.6 %mixer_backward.1 = (f32[192,2560]{1,0:T(8,128)S(1)}, f32[8,2560]{1,0:T(8,128)S(1)}, bf16[2560,256]{1,0:T(8,128)(2,1)S(1)}, bf16[2560,256]{1,0:T(8,128)(2,1)S(1)}, f32[8,2560]{1,0:T(8,128)S(1)}) custom-call(f32[192,2560]{1,0:T(8,128)S(1)} %copy-done.17, f32[192,2560]{1,0:T(8,128)S(1)} %copy-done.19, f32[8,2560]{1,0:T(8,128)S(1)} %broadcast_in_dim.9.incoming, ...), custom_call_target="tpu_custom_call" | custom-call | flops 1 | bytes 1 | tf_op jit(solution)/shard_map/mixer_backward/pallas_call | solution.py:1302
  540.6 1.3 copy-done.25
  542.3 1.3 collective-permute-start.8
  544.8 3.3 fusion.8.rest
  549.2 10.1 %collective-permute-done.10 = bf16[160,5760]{1,0:T(8,128)(2,1)} collective-permute-done((bf16[160,5760]{1,0:T(8,128)(2,1)}, bf16[160,5760]{1,0:T(8,128)(2,1)}, u32[]{:S(2)}, u32[]{:S(2)}) %collective-permute-start.10) | collective-permute-done | bytes 1843232 | tf_op jit(solution)/shard_map/ppermute | solution.py:1267
  559.4 6.4 add_convert_fusion
  566.7 184.8 %scatter_gradients.1 = (bf16[80,8320]{1,0:T(8,128)(2,1)}, bf16[3,80,7680]{2,1,0:T(8,128)(2,1)}, bf16[192,2560]{1,0:T(8,128)(2,1)}) custom-call(bf16[192,2560]{1,0:T(8,128)(2,1)} %copy-done.13, bf16[192,2560]{1,0:T(8,128)(2,1)} %get-tuple-element.72.normed_other, bf16[192,2560]{1,0:T(8,128)(2,1)} %copy-done.34, ...), custom_call_target="tpu_custom_call" | custom-call | tf_op jit(solution)/shard_map/scatter_gradients/pallas_call | solution.py:1209
  753.6 1.7 slice_convert_fusion.1
  755.4 1.6 multiply_reduce_fusion.4
  758.1 3.0 multiply_reduce_fusion
  762.3 1.6 bitcast_convert_fusion
  764.0 2.4 fusion.18
  (126 shorter events, 21.3 us)
Async XLA Ops:
  7.2 347.0 %all-gather.6.cloned.1.call-start = ((), (), s32[]{:S(2)}) async-start(), calls=%async_computation.2 | async-start | bytes 33177600 | tf_op jit(solution)/shard_map/all_gather | solution.py:1359
  194.0 283.8 %reduce-scatter.3.cloned.1.call-start = ((), (), s32[]{:S(2)}) async-start(), calls=%async_computation.3 | async-start | bytes 4915200 | tf_op jit(solution)/shard_map/reduce_scatter | solution.py:1410
  194.1 74.5 %collective-permute-start.1 = (bf16[192,2560]{1,0:T(8,128)(2,1)}, bf16[192,2560]{1,0:T(8,128)(2,1)}, u32[]{:S(2)}, u32[]{:S(2)}) collective-permute-start(bf16[192,2560]{1,0:T(8,128)(2,1)} %bitcast.12.grad0), channel_id=1, source_target_pairs={{0,1},{1,2},{2,3},{3,0},{4,5},{5,6},{6,7},{7,4},{8,9},{9,10},{10,1... | collective-permute-start | bytes 2949128 | tf_op jit(solution)/shard_map/ppermute | solution.py:1253
  199.5 69.0 %collective-permute-start.2 = (bf16[192,2560]{1,0:T(8,128)(2,1)}, bf16[192,2560]{1,0:T(8,128)(2,1)}, u32[]{:S(2)}, u32[]{:S(2)}) collective-permute-start(bf16[192,2560]{1,0:T(8,128)(2,1)} %bitcast.12.grad0), channel_id=1, source_target_pairs={{0,2},{1,3},{2,0},{3,1},{4,6},{5,7},{6,4},{7,5},{8,10},{9,11},{10,... | collective-permute-start | bytes 2949128 | tf_op jit(solution)/shard_map/ppermute | solution.py:1253
  202.9 65.6 %collective-permute-start.3 = (bf16[192,2560]{1,0:T(8,128)(2,1)}, bf16[192,2560]{1,0:T(8,128)(2,1)}, u32[]{:S(2)}, u32[]{:S(2)}) collective-permute-start(bf16[192,2560]{1,0:T(8,128)(2,1)} %bitcast.12.grad0), channel_id=1, source_target_pairs={{0,3},{1,0},{2,1},{3,2},{4,7},{5,4},{6,5},{7,6},{8,11},{9,8},{10,9... | collective-permute-start | bytes 2949128 | tf_op jit(solution)/shard_map/ppermute | solution.py:1253
  202.9 2.1 copy-start.11
  205.9 20.1 %copy-start.10 = (f32[16,2560]{1,0:T(8,128)S(1)}, f32[16,2560]{1,0:T(8,128)}, u32[]{:S(2)}) copy-start(f32[16,2560]{1,0:T(8,128)} %small_table.1.table.small.gain) | copy-start | bytes 491524
  221.6 1.3 copy-start.6
  223.8 2.1 collective-permute-start
  226.0 28.5 %copy-start.7 = (f32[192,2560]{1,0:T(8,128)S(1)}, f32[192,2560]{1,0:T(8,128)}, u32[]{:S(2)}) copy-start(f32[192,2560]{1,0:T(8,128)} %copy-done.6) | copy-start | bytes 5898244
  235.5 1.3 copy-start.3
  236.8 1.3 copy-start.14
  254.5 2.1 copy-start.12
  255.4 1.3 copy-start
  256.6 9.5 %copy-start.30 = (bf16[192,2560]{1,0:T(8,128)(2,1)}, bf16[192,2560]{1,0:T(8,128)(2,1)S(1)}, u32[]{:S(2)}) copy-start(bf16[192,2560]{1,0:T(8,128)(2,1)S(1)} %fusion.17.mixed) | copy-start | bytes 2949124
  406.8 357.2 %reduce-scatter.5.cloned.1.call-start = ((), (), s32[]{:S(2)}) async-start(), calls=%async_computation.4 | async-start | bytes 4915200 | tf_op jit(solution)/shard_map/reduce_scatter | solution.py:1428
  464.1 42.4 %collective-permute-start.6 = (bf16[160,5760]{1,0:T(8,128)(2,1)}, bf16[160,5760]{1,0:T(8,128)(2,1)}, u32[]{:S(2)}, u32[]{:S(2)}) collective-permute-start(bf16[160,5760]{1,0:T(8,128)(2,1)} %get-tuple-element.89), channel_id=1, source_target_pairs={{0,8},{4,12},{8,0},{12,4},{16,24},{20,28},{24,16},{28,20},{1,9},{5... | collective-permute-start | bytes 5529608 | tf_op jit(solution)/shard_map/ppermute | solution.py:1263
  464.2 42.4 %collective-permute-start.7 = (bf16[160,5760]{1,0:T(8,128)(2,1)}, bf16[160,5760]{1,0:T(8,128)(2,1)}, u32[]{:S(2)}, u32[]{:S(2)}) collective-permute-start(bf16[160,5760]{1,0:T(8,128)(2,1)} %get-tuple-element.90), channel_id=1, source_target_pairs={{0,16},{4,20},{8,24},{12,28},{16,0},{20,4},{24,8},{28,12},{1,17},{... | collective-permute-start | bytes 5529608 | tf_op jit(solution)/shard_map/ppermute | solution.py:1267
  477.8 2.4 copy-start.28
  477.8 2.7 copy-start.33
  482.3 6.7 copy-start.34
  482.3 6.7 copy-start.1
  482.3 6.7 copy-start.4
  482.3 6.8 copy-start.8
  500.4 1.3 copy-start.16
  501.7 1.3 copy-start.18
  516.5 42.8 %collective-permute-start.10 = (bf16[160,5760]{1,0:T(8,128)(2,1)}, bf16[160,5760]{1,0:T(8,128)(2,1)}, u32[]{:S(2)}, u32[]{:S(2)}) collective-permute-start(bf16[160,5760]{1,0:T(8,128)(2,1)} %get-tuple-element.104), channel_id=1, source_target_pairs={{0,16},{4,20},{8,24},{12,28},{16,0},{20,4},{24,8},{28,12},{1,17},{... | collective-permute-start | bytes 5529608 | tf_op jit(solution)/shard_map/ppermute | solution.py:1267
  516.9 42.5 %collective-permute-start.9 = (bf16[160,5760]{1,0:T(8,128)(2,1)}, bf16[160,5760]{1,0:T(8,128)(2,1)}, u32[]{:S(2)}, u32[]{:S(2)}) collective-permute-start(bf16[160,5760]{1,0:T(8,128)(2,1)} %get-tuple-element.103), channel_id=1, source_target_pairs={{0,8},{4,12},{8,0},{12,4},{16,24},{20,28},{24,16},{28,20},{1,9},{5... | collective-permute-start | bytes 5529608 | tf_op jit(solution)/shard_map/ppermute | solution.py:1263
  518.6 47.2 %collective-permute-start.4 = (bf16[192,2560]{1,0:T(8,128)(2,1)}, bf16[192,2560]{1,0:T(8,128)(2,1)}, u32[]{:S(2)}, u32[]{:S(2)}) collective-permute-start(bf16[192,2560]{1,0:T(8,128)(2,1)} %copy-done.34), channel_id=1, source_target_pairs={{0,4},{4,0},{8,12},{12,8},{16,20},{20,16},{24,28},{28,24},{1,5},{5... | collective-permute-start | bytes 2949128 | tf_op jit(solution)/shard_map/ppermute | solution.py:1259
  518.7 1.5 copy-start.2
  520.2 1.6 copy-start.5
  521.8 1.9 copy-start.15
  523.7 1.5 copy-start.17
  525.2 1.5 copy-start.19
  540.6 1.3 copy-start.25
  542.3 5.9 collective-permute-start.8
  543.6 22.2 %collective-permute-start.5 = (bf16[192,2560]{1,0:T(8,128)(2,1)}, bf16[192,2560]{1,0:T(8,128)(2,1)S(1)}, u32[]{:S(2)}, u32[]{:S(2)}) collective-permute-start(bf16[192,2560]{1,0:T(8,128)(2,1)} %copy-done.24), channel_id=1, source_target_pairs={{0,4},{4,0},{8,12},{12,8},{16,20},{20,16},{24,28},{28,24},{1,5},{5... | collective-permute-start | bytes 2949128 | tf_op jit(solution)/shard_map/ppermute | solution.py:1259
  544.8 3.3 copy-start.26
  548.1 11.3 %copy-start.36 = (bf16[320,5760]{1,0:T(8,128)(2,1)S(1)}, bf16[320,5760]{1,0:T(8,128)(2,1)}, u32[]{:S(2)}) copy-start(bf16[320,5760]{1,0:T(8,128)(2,1)} %get-tuple-element.101) | copy-start | bytes 11059204
  566.7 188.6 %copy-start.37 = (bf16[80,2560]{1,0:T(8,128)(2,1)S(1)}, bf16[80,2560]{1,0:T(8,128)(2,1)}, u32[]{:S(2)}) copy-start(bf16[80,2560]{1,0:T(8,128)(2,1)} %branch.1) | copy-start | bytes 1228804
  566.7 188.6 %copy-start.38 = (bf16[80,2560]{1,0:T(8,128)(2,1)S(1)}, bf16[80,2560]{1,0:T(8,128)(2,1)}, u32[]{:S(2)}) copy-start(bf16[80,2560]{1,0:T(8,128)(2,1)} %gelu.1) | copy-start | bytes 1228804
  753.6 3.3 copy-start.35
  755.3 2.1 copy-start.31
  755.4 2.7 copy-start.32
  758.1 3.0 copy-start.41
  758.1 3.1 copy-start.42
  761.7 2.3 copy-start.29
  764.0 2.4 copy-start.39
  (9 other events, 9.4 us)
Sparse Core Ops, SparseCore 0:
  194.1 149.8 all-gather.5
  406.9 70.8 reduce-scatter.2
  518.7 97.7 reduce-scatter.4

commit v18 on v17

--- a/solution.py
+++ b/solution.py
@@ -604,29 +604,25 @@
                 load(n, m).start()
         greet([(core, z)])
 
-    for n, (start, size) in enumerate(tiles):
-        cols = slice(start, start + size)
-
-        @pl.when(step == 0)
-        def _(n=n):
-            for m in range(3):
-                load(n, m).wait()
-
-        gate = mm(normed[...], held[0, :, cols], ((1,), (0,)))
-        value, slope = gelu_parts(gate)
-        up = mm(normed[...], held[1, :, cols], ((1,), (0,)))
-        hidden_now[step, :, cols] = (value * up).astype(bf16)
-        grad_hidden = mm(grad_out[...], held[2, :, cols], ((1,), (0,)))
-        pair_now[step, :, cols] = (grad_hidden * up * slope).astype(bf16)
-        pair_now[step, :, slice(ff_part + start, ff_part + start + size)] = (grad_hidden * value).astype(bf16)
+    def forth(turn):
+        for n, (start, size) in enumerate(tiles):
+            cols = slice(start, start + size)
+            if turn == 0:
+                for m in range(3):
+                    load(n, m).wait()
+            gate = mm(normed[...], held[0, :, cols], ((1,), (0,)))
+            up = mm(normed[...], held[1, :, cols], ((1,), (0,)))
+            grad_hidden = mm(grad_out[...], held[2, :, cols], ((1,), (0,)))
+            value, slope = gelu_parts(gate)
+            hidden_now[turn, :, cols] = (value * up).astype(bf16)
+            pair_now[turn, :, cols] = (grad_hidden * up * slope).astype(bf16)
+            pair_now[turn, :, slice(ff_part + start, ff_part + start + size)] = (grad_hidden * value).astype(bf16)
+        for n in range(2):
+            handed(n, turn).start()
+            kept(n, turn).start()
 
     for turn in range(2):
-
-        @pl.when(step == turn)
-        def _(turn=turn):
-            for n in range(2):
-                handed(n, turn).start()
-                kept(n, turn).start()
+        pl.when(step == turn)(functools.partial(forth, turn))
 
     def back_tile(turn, carry):
         cols = pl.ds(pl.multiple_of(turn * 512, 512), 512)
@@ -1491,7 +1487,7 @@
         grad_normed = mm(grad_both, wide, ((1,), (1,)))
         input_grad = (grad_middle + norm_back(tokens, gain_one, grad_normed)).astype(bf16)
     input_grad = input_grad[None]
-    middle = lax.optimization_barrier((middle, mixer_sum))[0]
+    middle = lax.optimization_barrier((middle, rest))[0]
     block_output = (middle + out_sum.astype(f32)).astype(bf16)[None]
     edge = 3 * lru + 2 * width
     vec = mixer_sum[:, edge:].astype(f32).T

time: 783 us -> 780 us (level)
  local copies, waits for them, and re-layouts: 33.9 us -> 18.7 us
  waiting for transfers between devices: 25.5 us -> 33.7 us
    unnamed x88 -> x68, local copies, waits for them, and re-layouts: 29.6 us -> 14.4 us
    reduce_scatter x1, waiting for transfers between devices: 0.01 us -> 14.7 us  [on_device(): lax.psum_scatter(out_part, 'fsdp', scatter_dimension=0, tiled=True)]
    ppermute x2, waiting for transfers between devices: 10.1 us -> 1.9 us  [swap_across(): return lax.ppermute(shard, 'seq', [(i, i ^ 4) for i in range(8)])]
  transfers between devices with their start and end apart: 14 -> 14, of which waited for: 6 -> 7; matrix products, arithmetic and copies ran while one was open for 6% -> 6% of each run, Pallas kernels for 49% -> 24%
where the time goes in v18:
time: 780 us; the launch traced here: 771 us
  Pallas kernels  609 us (78%)
  other arithmetic  34.1 us (4%)
  waiting for transfers between devices  33.7 us (4%)
  blocking collectives  24.3 us (3%)
  matrix products  20 us (3%)
  local copies, waits for them, and re-layouts  18.7 us (2%)
  starting transfers between devices  16.7 us (2%)
  between operations  14.5 us (2%)
    pallas_call x1, Pallas kernels, scatter(): pl.pallas_call(scatter_kernel, in_specs=[anyspec] * 15, out_specs=[anyspe...  185 us
    pallas_call x1, Pallas kernels, gather(): pl.pallas_call(gather_kernel, in_specs=[anyspec] * 7, out_specs=[anyspec]...  183 us
    pallas_call x1, Pallas kernels, gather_rows(): pl.pallas_call(rows_kernel, in_specs=[anyspec] * 7, out_specs=[anyspec] *...  82.3 us
    pallas_call x1, Pallas kernels, shared_products(): pl.pallas_call(shared_products_kernel, grid=(3,), in_specs=[anyspec] * 9,...  57.1 us
    pallas_call x1, Pallas kernels, feed_forward(): pl.pallas_call(feed_forward_kernel, grid=(2,), in_specs=[block, block, an...  52.3 us
    pallas_call x3, Pallas kernels, call_heads(): pl.pallas_call(kernel, grid=(heads,), in_specs=in_specs, out_specs=out_sp...  31.4 us
    all_gather x2, blocking collectives, prefix(): gathered = lax.all_gather(jnp.stack(part), axis)  24.3 us
    dot_general x2, matrix products, mm(): lax.dot_general(left, right, (dims, ((), ())), preferred_element_type=f32)  20 us
  transfers between devices with their start and end apart: 14, of which 7 were waited for; matrix products, arithmetic and copies ran while one was open for 6% of the time, Pallas kernels for 24%

profile of v18, /device:TPU:0, one launch (start us, length us, event | category | flops | bytes accessed | tf_op | source)
XLA Modules:
  0.0 770.9 jit_solution(11171297958041854242)
XLA Ops:
  8.1 1.4 stack.33
  9.6 1.5 fusion.20.first
  11.1 182.9 %gather_weights.1 = (bf16[2560,8320]{1,0:T(8,128)(2,1)}, bf16[320,5760]{1,0:T(8,128)(2,1)}) custom-call(bf16[80,640]{1,0:T(8,128)(2,1)} %fusion.20.first, bf16[80,2560]{1,0:T(8,128)(2,1)} %branch.1, bf16[80,2560]{1,0:T(8,128)(2,1)} %gelu.1, bf16[80,2560]{1,0:T(8,128)(2,1)} %outer.1, bf16[80,7680]{1,0:T(8,128)(2,1)} %gate.1, bf16[80,7680]{1,0:T(8,128)(2,1)} %up.1, ...), custom_call_target="tpu_custom_call" | custom-call | tf_op jit(solution)/shard_map/gather_weights/pallas_call | solution.py:421
  194.1 5.5 collective-permute-start.1
  199.5 3.4 collective-permute-start.2
  202.9 2.1 small_table.1.table.small.gain
  205.9 15.7 %mixer_in.1 = (bf16[192,2560]{1,0:T(8,128)(2,1)S(1)}, bf16[192,2560]{1,0:T(8,128)(2,1)S(1)}, f32[192,2560]{1,0:T(8,128)S(1)}) custom-call(bf16[192,2560]{1,0:T(8,128)(2,1)S(1)} %bitcast.43, f32[16,2560]{1,0:T(8,128)S(1)} %copy-done.7, bf16[2560,8320]{1,0:T(8,128)(2,1)} %get-tuple-element.64.columns.weights.rate_w.input_w.mixer_w), custom_call_target="tpu_custom_call" | custom-call | flops 1 | bytes 1 | tf_op jit(solution)/shard_map/mixer_in/pallas_call | solution.py:139
  221.6 1.3 copy-done.4
  222.9 0.9 copy-done.11
  223.8 1.3 collective-permute-start
  226.0 9.5 %mixer_forward.1 = (bf16[192,2560]{1,0:T(8,128)(2,1)S(1)}, f32[192,2560]{1,0:T(8,128)S(1)}, f32[192,2560]{1,0:T(8,128)S(1)}, f32[192,2560]{1,0:T(8,128)S(1)}, f32[192,2560]{1,0:T(8,128)S(1)}) custom-call(bf16[192,2560]{1,0:T(8,128)(2,1)S(1)} %get-tuple-element.65.branch, f32[8,2560]{1,0:T(8,128)S(1)} %pad_convert_fusion.prior, f32[16,2560]{1,0:T(8,128)S(1)} %copy-done.8, ...), custom_call_target="tpu_custom_call" | custom-call | flops 1 | bytes 1 | tf_op jit(solution)/shard_map/mixer_forward/pallas_call | solution.py:1298
  235.5 1.3 copy-done.2
  236.8 1.3 copy-done.12
  238.1 0.9 copy-done.16
  239.1 14.9 %all-gather.2 = f32[8,2,2560]{2,1,0:T(2,128)S(1)} all-gather(f32[1,2,2560]{2,1,0:T(2,128)S(1)} %fusion.21), channel_id=2, replica_groups=mesh['seq'=8,'fsdp'=4] {'seq'}, dimensions={0}, use_global_device_ids=true | all-gather | bytes 184320 | tf_op jit(solution)/shard_map/all_gather | solution.py:29
  255.3 1.3 copy-done
  256.5 12.6 %multiply_reduce_fusion.3 = (f32[192]{0:T(256)S(1)}, f32[192,2560]{1,0:T(8,128)}) fusion(bf16[192,2560]{1,0:T(8,128)(2,1)S(1)} %fusion.17.mixed, bf16[2560,8320]{1,0:T(8,128)(2,1)} %get-tuple-element.64.columns.weights.rate_w.input_w.mixer_w, bf16[1,192,2560]{2,1,0:T(8,128)(2,1)S(1)} %copy-done.10), kind=kOutput, calls=%fused_computation.28 | convolution fusion | flops 2518548224 | bytes 17040128 | tf_op jit(solution)/shard_map/dot_general | solution.py:62
  269.1 2.7 multiply_convert_fusion.normed
  271.8 82.3 %gather_rows.1 = (bf16[768,2560]{1,0:T(8,128)(2,1)}, bf16[768,2560]{1,0:T(8,128)(2,1)}, bf16[768,2560]{1,0:T(8,128)(2,1)}, bf16[768,2560]{1,0:T(8,128)(2,1)}, bf...) custom-call(bf16[192,2560]{1,0:T(8,128)(2,1)} %multiply_convert_fusion.normed, bf16[192,2560]{1,0:T(8,128)(2,1)} %bitcast.12.grad0, ...), custom_call_target="tpu_custom_call" | custom-call | tf_op jit(solution)/shard_map/gather_rows/pallas_call | solution.py:548
  354.2 52.3 %feed_forward.1 = (bf16[768,1920]{1,0:T(8,128)(2,1)}, bf16[768,1920]{1,0:T(8,128)(2,1)}, bf16[768,3840]{1,0:T(8,128)(2,1)}, bf16[768,3840]{1,0:T(8,128)(2,1)}, bf16[768,2560]{1,0:T(8,128)(2,1)}) custom-call(bf16[768,2560]{1,0:T(8,128)(2,1)} %get-tuple-element.72.normed, bf16[768,2560]{1,0:T(8,128)(2,1)} %get-tuple-element.73.grad_out.grad, ...), custom_call_target="tpu_custom_call" | custom-call | tf_op jit(solution)/shard_map/feed_forward/pallas_call | solution.py:651
  406.6 57.1 %feed_forward_products.1 = (bf16[160,5760]{1,0:T(8,128)(2,1)}, bf16[160,5760]{1,0:T(8,128)(2,1)}, bf16[320,5760]{1,0:T(8,128)(2,1)}, bf16[160,5760]{1,0:T(8,128)...) custom-call(bf16[768,2560]{1,0:T(8,128)(2,1)} %get-tuple-element.72.normed, ...), custom_call_target="tpu_custom_call" | custom-call | tf_op jit(solution)/shard_map/feed_forward_products/pallas_call | solution.py:864
  463.7 1.8 collective-permute-start.5
  465.6 12.0 %reduce-scatter.3.cloned.1.call-done = bf16[192,2560]{1,0:T(8,128)(2,1)} async-done(((bf16[768,2560]{1,0:T(8,128)(2,1)}), bf16[192,2560]{1,0:T(8,128)(2,1)}) %reduce-scatter.3.cloned.1.call-update) | async-done | bytes 983056 | tf_op jit(solution)/shard_map/reduce_scatter | solution.py:1406
  477.6 2.2 multiply_reduce_fusion.2
  479.8 3.3 add_convert_fusion.3.grad_mix
  483.1 7.4 fusion.grad_mixed
  490.7 11.2 %mixer_backward_scan.1 = (bf16[192,2560]{1,0:T(8,128)(2,1)S(1)}, f32[192,2560]{1,0:T(8,128)S(1)}, f32[192,2560]{1,0:T(8,128)S(1)}, f32[8,2560]{1,0:T(8,128)S(1)}) custom-call(f32[192,2560]{1,0:T(8,128)S(1)} %fusion.grad_mixed, f32[192,2560]{1,0:T(8,128)S(1)} %copy-done.6, f32[192,2560]{1,0:T(8,128)S(1)} %copy-done.3, f32[192,2560]{1,0:T(8,128)S(1)} %get-tuple-element.67.cum, ...), custom_call_target="tpu_custom_call" | custom-call | flops 1 | bytes 1 | tf_op jit(solution)/shard_map/mixer_backward_scan/pallas_call | solution.py:1298
  501.9 4.2 collective-permute-done.4
  506.2 9.4 %all-gather.3 = f32[8,2,2560]{2,1,0:T(2,128)S(1)} all-gather(f32[1,2,2560]{2,1,0:T(2,128)S(1)} %fusion.22), channel_id=3, replica_groups=mesh['seq'=8,'fsdp'=4] {'seq'}, dimensions={0}, use_global_device_ids=true | all-gather | bytes 184320 | tf_op jit(solution)/shard_map/all_gather | solution.py:29
  516.5 1.7 collective-permute-start.9
  518.2 10.6 %mixer_backward.1 = (f32[192,2560]{1,0:T(8,128)S(1)}, f32[8,2560]{1,0:T(8,128)S(1)}, bf16[2560,256]{1,0:T(8,128)(2,1)S(1)}, bf16[2560,256]{1,0:T(8,128)(2,1)S(1)}, f32[8,2560]{1,0:T(8,128)S(1)}) custom-call(f32[192,2560]{1,0:T(8,128)S(1)} %get-tuple-element.76.rev_cum, f32[192,2560]{1,0:T(8,128)S(1)} %get-tuple-element.77.rev_grad, ...), custom_call_target="tpu_custom_call" | custom-call | flops 1 | bytes 1 | tf_op jit(solution)/shard_map/mixer_backward/pallas_call | solution.py:1298
  528.8 1.1 copy-done.14
  529.9 1.1 copy-done.15
  530.9 1.3 copy-done.19
  532.2 1.3 collective-permute-start.8
  533.9 1.2 collective-permute-start.7
  535.1 3.1 fusion.8.rest
  538.2 14.7 %reduce-scatter.5.cloned.1.call-done = bf16[192,2560]{1,0:T(8,128)(2,1)} async-done(((bf16[768,2560]{1,0:T(8,128)(2,1)}), bf16[192,2560]{1,0:T(8,128)(2,1)}) %reduce-scatter.5.cloned.1.call-update) | async-done | bytes 983056 | tf_op jit(solution)/shard_map/reduce_scatter | solution.py:1424
  552.9 2.9 fusion.18
  556.0 1.0 pad_maximum_fusion.grad_branch
  557.0 1.8 collective-permute-done.10
  558.9 6.3 add_convert_fusion
  566.2 185.1 %scatter_gradients.1 = (bf16[80,8320]{1,0:T(8,128)(2,1)}, bf16[3,80,7680]{2,1,0:T(8,128)(2,1)}, bf16[192,2560]{1,0:T(8,128)(2,1)}) custom-call(bf16[192,2560]{1,0:T(8,128)(2,1)} %copy-done.11, bf16[192,2560]{1,0:T(8,128)(2,1)} %get-tuple-element.98.normed_other, bf16[192,2560]{1,0:T(8,128)(2,1)} %add_convert_fusion.3.grad_mix, ...), custom_call_target="tpu_custom_call" | custom-call | tf_op jit(solution)/shard_map/scatter_gradients/pallas_call | solution.py:1205
  751.4 1.7 slice_convert_fusion.1
  753.1 1.6 multiply_reduce_fusion.4
  755.8 3.0 multiply_reduce_fusion
  758.9 1.6 bitcast_convert_fusion
  763.2 0.9 copy.62
  (106 shorter events, 10.7 us)
Async XLA Ops:
  7.2 347.0 %all-gather.6.cloned.1.call-start = ((), (), s32[]{:S(2)}) async-start(), calls=%async_computation.2 | async-start | bytes 33177600 | tf_op jit(solution)/shard_map/all_gather | solution.py:1355
  194.0 283.6 %reduce-scatter.3.cloned.1.call-start = ((), (), s32[]{:S(2)}) async-start(), calls=%async_computation.3 | async-start | bytes 4915200 | tf_op jit(solution)/shard_map/reduce_scatter | solution.py:1406
  194.1 77.8 %collective-permute-start.1 = (bf16[192,2560]{1,0:T(8,128)(2,1)}, bf16[192,2560]{1,0:T(8,128)(2,1)}, u32[]{:S(2)}, u32[]{:S(2)}) collective-permute-start(bf16[192,2560]{1,0:T(8,128)(2,1)} %bitcast.12.grad0), channel_id=1, source_target_pairs={{0,1},{1,2},{2,3},{3,0},{4,5},{5,6},{6,7},{7,4},{8,9},{9,10},{10,1... | collective-permute-start | bytes 2949128 | tf_op jit(solution)/shard_map/ppermute | solution.py:1249
  199.5 72.3 %collective-permute-start.2 = (bf16[192,2560]{1,0:T(8,128)(2,1)}, bf16[192,2560]{1,0:T(8,128)(2,1)}, u32[]{:S(2)}, u32[]{:S(2)}) collective-permute-start(bf16[192,2560]{1,0:T(8,128)(2,1)} %bitcast.12.grad0), channel_id=1, source_target_pairs={{0,2},{1,3},{2,0},{3,1},{4,6},{5,7},{6,4},{7,5},{8,10},{9,11},{10,... | collective-permute-start | bytes 2949128 | tf_op jit(solution)/shard_map/ppermute | solution.py:1249
  202.9 68.9 %collective-permute-start.3 = (bf16[192,2560]{1,0:T(8,128)(2,1)}, bf16[192,2560]{1,0:T(8,128)(2,1)}, u32[]{:S(2)}, u32[]{:S(2)}) collective-permute-start(bf16[192,2560]{1,0:T(8,128)(2,1)} %bitcast.12.grad0), channel_id=1, source_target_pairs={{0,3},{1,0},{2,1},{3,2},{4,7},{5,4},{6,5},{7,6},{8,11},{9,8},{10,9... | collective-permute-start | bytes 2949128 | tf_op jit(solution)/shard_map/ppermute | solution.py:1249
  202.9 2.1 copy-start.9
  205.0 0.9 copy-start.7
  205.9 20.1 %copy-start.8 = (f32[16,2560]{1,0:T(8,128)S(1)}, f32[16,2560]{1,0:T(8,128)}, u32[]{:S(2)}) copy-start(f32[16,2560]{1,0:T(8,128)} %small_table.1.table.small.gain) | copy-start | bytes 491524
  221.6 1.3 copy-start.4
  222.9 0.9 copy-start.11
  223.8 2.1 collective-permute-start
  226.0 28.4 %copy-start.5 = (f32[192,2560]{1,0:T(8,128)S(1)}, f32[192,2560]{1,0:T(8,128)}, u32[]{:S(2)}) copy-start(f32[192,2560]{1,0:T(8,128)} %copy-done.4) | copy-start | bytes 5898244
  235.5 1.3 copy-start.2
  236.8 1.3 copy-start.12
  238.1 0.9 copy-start.16
  254.4 2.1 copy-start.10
  255.3 1.3 copy-start
  256.5 12.6 %copy-start.21 = (bf16[192,2560]{1,0:T(8,128)(2,1)}, bf16[192,2560]{1,0:T(8,128)(2,1)S(1)}, u32[]{:S(2)}) copy-start(bf16[192,2560]{1,0:T(8,128)(2,1)S(1)} %fusion.17.mixed) | copy-start | bytes 2949124
  406.5 146.4 %reduce-scatter.5.cloned.1.call-start = ((), (), s32[]{:S(2)}) async-start(), calls=%async_computation.4 | async-start | bytes 4915200 | tf_op jit(solution)/shard_map/reduce_scatter | solution.py:1424
  463.7 42.4 %collective-permute-start.4 = (bf16[160,5760]{1,0:T(8,128)(2,1)}, bf16[160,5760]{1,0:T(8,128)(2,1)}, u32[]{:S(2)}, u32[]{:S(2)}) collective-permute-start(bf16[160,5760]{1,0:T(8,128)(2,1)} %get-tuple-element.86), channel_id=1, source_target_pairs={{0,8},{4,12},{8,0},{12,4},{16,24},{20,28},{24,16},{28,20},{1,9},{5... | collective-permute-start | bytes 5529608 | tf_op jit(solution)/shard_map/ppermute | solution.py:1259
  463.7 42.4 %collective-permute-start.5 = (bf16[160,5760]{1,0:T(8,128)(2,1)}, bf16[160,5760]{1,0:T(8,128)(2,1)}, u32[]{:S(2)}, u32[]{:S(2)}) collective-permute-start(bf16[160,5760]{1,0:T(8,128)(2,1)} %get-tuple-element.87), channel_id=1, source_target_pairs={{0,16},{4,20},{8,24},{12,28},{16,0},{20,4},{24,8},{28,12},{1,17},{... | collective-permute-start | bytes 5529608 | tf_op jit(solution)/shard_map/ppermute | solution.py:1263
  477.6 2.2 copy-start.24
  483.1 7.4 copy-start.1
  483.1 7.4 copy-start.3
  483.1 7.5 copy-start.6
  483.1 82.2 %collective-permute-start.6 = (bf16[192,2560]{1,0:T(8,128)(2,1)}, bf16[192,2560]{1,0:T(8,128)(2,1)}, u32[]{:S(2)}, u32[]{:S(2)}) collective-permute-start(bf16[192,2560]{1,0:T(8,128)(2,1)} %add_convert_fusion.3.grad_mix), channel_id=1, source_target_pairs={{0,4},{4,0},{8,12},{12,8},{16,20},{20,16},{24,28},{28,24},{1,5},{5... | collective-permute-start | bytes 2949128 | tf_op jit(solution)/shard_map/ppermute | solution.py:1255
  490.6 27.5 %copy-start.13 = (f32[192,2560]{1,0:T(8,128)S(1)}, f32[192,2560]{1,0:T(8,128)}, u32[]{:S(2)}) copy-start(f32[192,2560]{1,0:T(8,128)} %copy-done.12) | copy-start | bytes 5898244
  490.7 27.5 %copy-start.17 = (bf16[192,2560]{1,0:T(8,128)(2,1)S(1)}, bf16[192,2560]{1,0:T(8,128)(2,1)}, u32[]{:S(2)}) copy-start(bf16[192,2560]{1,0:T(8,128)(2,1)} %copy-done.16) | copy-start | bytes 2949124
  501.9 16.3 %copy-start.18 = (bf16[192,2560]{1,0:T(8,128)(2,1)}, bf16[192,2560]{1,0:T(8,128)(2,1)S(1)}, u32[]{:S(2)}) copy-start(bf16[192,2560]{1,0:T(8,128)(2,1)S(1)} %get-tuple-element.100.grad_gelu) | copy-start | bytes 2949124
  516.0 42.8 %collective-permute-start.10 = (bf16[160,5760]{1,0:T(8,128)(2,1)}, bf16[160,5760]{1,0:T(8,128)(2,1)}, u32[]{:S(2)}, u32[]{:S(2)}) collective-permute-start(bf16[160,5760]{1,0:T(8,128)(2,1)} %get-tuple-element.106), channel_id=1, source_target_pairs={{0,16},{4,20},{8,24},{12,28},{16,0},{20,4},{24,8},{28,12},{1,17},{... | collective-permute-start | bytes 5529608 | tf_op jit(solution)/shard_map/ppermute | solution.py:1263
  516.5 42.5 %collective-permute-start.9 = (bf16[160,5760]{1,0:T(8,128)(2,1)}, bf16[160,5760]{1,0:T(8,128)(2,1)}, u32[]{:S(2)}, u32[]{:S(2)}) collective-permute-start(bf16[160,5760]{1,0:T(8,128)(2,1)} %get-tuple-element.105), channel_id=1, source_target_pairs={{0,8},{4,12},{8,0},{12,4},{16,24},{20,28},{24,16},{28,20},{1,9},{5... | collective-permute-start | bytes 5529608 | tf_op jit(solution)/shard_map/ppermute | solution.py:1259
  528.8 1.1 copy-start.14
  529.9 1.1 copy-start.15
  530.9 1.3 copy-start.19
  532.2 23.7 %collective-permute-start.8 = (f32[3,2560]{1,0:T(4,128)S(1)}, f32[3,2560]{1,0:T(4,128)S(1)}, u32[]{:S(2)}, u32[]{:S(2)}) collective-permute-start(f32[3,2560]{1,0:T(4,128)S(1)} %slice.217), channel_id=1, source_target_pairs={{4,0},{8,4},{12,8},{16,12},{20,16},{24,20},{28,24},{5,1},{9,5},{13... | collective-permute-start | bytes 92168 | tf_op jit(solution)/shard_map/ppermute | solution.py:23
  533.9 31.4 %collective-permute-start.7 = (bf16[192,2560]{1,0:T(8,128)(2,1)}, bf16[192,2560]{1,0:T(8,128)(2,1)S(1)}, u32[]{:S(2)}, u32[]{:S(2)}) collective-permute-start(bf16[192,2560]{1,0:T(8,128)(2,1)} %copy-done.18), channel_id=1, source_target_pairs={{0,4},{4,0},{8,12},{12,8},{16,20},{20,16},{24,28},{28,24},{1,5},{5... | collective-permute-start | bytes 2949128 | tf_op jit(solution)/shard_map/ppermute | solution.py:1255
  538.2 17.7 %copy-start.20 = (f32[192,2560]{1,0:T(8,128)S(1)}, f32[192,2560]{1,0:T(8,128)}, u32[]{:S(2)}) copy-start(f32[192,2560]{1,0:T(8,128)} %copy-done.19) | copy-start | bytes 5898244
  555.9 3.1 copy-start.26
  565.3 0.9 copy-start.30
  566.2 186.9 %copy-start.27 = (bf16[80,2560]{1,0:T(8,128)(2,1)S(1)}, bf16[80,2560]{1,0:T(8,128)(2,1)}, u32[]{:S(2)}) copy-start(bf16[80,2560]{1,0:T(8,128)(2,1)} %branch.1) | copy-start | bytes 1228804
  566.2 186.9 %copy-start.28 = (bf16[80,2560]{1,0:T(8,128)(2,1)S(1)}, bf16[80,2560]{1,0:T(8,128)(2,1)}, u32[]{:S(2)}) copy-start(bf16[80,2560]{1,0:T(8,128)(2,1)} %gelu.1) | copy-start | bytes 1228804
  751.4 4.0 copy-start.25
  753.1 2.3 copy-start.22
  753.1 2.7 copy-start.23
  758.9 3.8 copy-start.31
  758.9 3.8 copy-start.32
  758.9 4.3 copy-start.29
Sparse Core Ops, SparseCore 0:
  194.1 149.8 all-gather.5
  406.6 70.8 reduce-scatter.2
  479.9 73.0 reduce-scatter.4

commit v19 on v18

--- a/solution.py
+++ b/solution.py
@@ -95,7 +95,10 @@
     decay_param = rows[7:8, :]
     fast = jnp.exp(-decay_param)
     table[0:7, :] = rows[0:7, :]
-    table[7:8, :] = jnp.log1p(fast)
+    series = 1.0 / 6.0
+    for term in (5, 4, 3, 2, 1):
+        series = 1.0 / term - fast * series
+    table[7:8, :] = jnp.where(fast < 0.05, fast * series, jnp.log1p(fast))
     table[8:9, :] = -fast / (1.0 + fast)
     table[9:11, :] = rows[8:10, :]
     table[11:16, :] = jnp.zeros((5, rows.shape[1]), f32)

time: 780 us -> 780 us (level)
  no operation moved by 1% of the time
where the time goes in v19:
time: 780 us; the launch traced here: 771 us
  Pallas kernels  609 us (78%)
  other arithmetic  34.1 us (4%)
  waiting for transfers between devices  33.7 us (4%)
  blocking collectives  24.3 us (3%)
  matrix products  20 us (3%)
  local copies, waits for them, and re-layouts  18.7 us (2%)
  starting transfers between devices  16.7 us (2%)
  between operations  14.5 us (2%)
    pallas_call x1, Pallas kernels, scatter(): pl.pallas_call(scatter_kernel, in_specs=[anyspec] * 15, out_specs=[anyspe...  185 us
    pallas_call x1, Pallas kernels, gather(): pl.pallas_call(gather_kernel, in_specs=[anyspec] * 7, out_specs=[anyspec]...  183 us
    pallas_call x1, Pallas kernels, gather_rows(): pl.pallas_call(rows_kernel, in_specs=[anyspec] * 7, out_specs=[anyspec] *...  82.3 us
    pallas_call x1, Pallas kernels, shared_products(): pl.pallas_call(shared_products_kernel, grid=(3,), in_specs=[anyspec] * 9,...  57.1 us
    pallas_call x1, Pallas kernels, feed_forward(): pl.pallas_call(feed_forward_kernel, grid=(2,), in_specs=[block, block, an...  52.3 us
    pallas_call x3, Pallas kernels, call_heads(): pl.pallas_call(kernel, grid=(heads,), in_specs=in_specs, out_specs=out_sp...  31.4 us
    all_gather x2, blocking collectives, prefix(): gathered = lax.all_gather(jnp.stack(part), axis)  24.3 us
    dot_general x2, matrix products, mm(): lax.dot_general(left, right, (dims, ((), ())), preferred_element_type=f32)  20 us
  transfers between devices with their start and end apart: 14, of which 7 were waited for; matrix products, arithmetic and copies ran while one was open for 6% of the time, Pallas kernels for 24%

profile of v19, /device:TPU:0, one launch (start us, length us, event | category | flops | bytes accessed | tf_op | source)
XLA Modules:
  0.0 770.9 jit_solution(4251331299298295795)
XLA Ops:
  8.1 1.4 stack.33
  9.6 1.5 fusion.20.first
  11.1 182.9 %gather_weights.1 = (bf16[2560,8320]{1,0:T(8,128)(2,1)}, bf16[320,5760]{1,0:T(8,128)(2,1)}) custom-call(bf16[80,640]{1,0:T(8,128)(2,1)} %fusion.20.first, bf16[80,2560]{1,0:T(8,128)(2,1)} %branch.1, bf16[80,2560]{1,0:T(8,128)(2,1)} %gelu.1, bf16[80,2560]{1,0:T(8,128)(2,1)} %outer.1, bf16[80,7680]{1,0:T(8,128)(2,1)} %gate.1, bf16[80,7680]{1,0:T(8,128)(2,1)} %up.1, ...), custom_call_target="tpu_custom_call" | custom-call | tf_op jit(solution)/shard_map/gather_weights/pallas_call | solution.py:424
  194.1 5.5 collective-permute-start.1
  199.5 3.4 collective-permute-start.2
  202.9 2.1 small_table.1.table.small.gain
  205.9 15.7 %mixer_in.1 = (bf16[192,2560]{1,0:T(8,128)(2,1)S(1)}, bf16[192,2560]{1,0:T(8,128)(2,1)S(1)}, f32[192,2560]{1,0:T(8,128)S(1)}) custom-call(bf16[192,2560]{1,0:T(8,128)(2,1)S(1)} %bitcast.43, f32[16,2560]{1,0:T(8,128)S(1)} %copy-done.7, bf16[2560,8320]{1,0:T(8,128)(2,1)} %get-tuple-element.64.columns.weights.rate_w.input_w.mixer_w), custom_call_target="tpu_custom_call" | custom-call | flops 1 | bytes 1 | tf_op jit(solution)/shard_map/mixer_in/pallas_call | solution.py:142
  221.6 1.3 copy-done.4
  222.9 0.9 copy-done.11
  223.8 1.3 collective-permute-start
  226.0 9.5 %mixer_forward.1 = (bf16[192,2560]{1,0:T(8,128)(2,1)S(1)}, f32[192,2560]{1,0:T(8,128)S(1)}, f32[192,2560]{1,0:T(8,128)S(1)}, f32[192,2560]{1,0:T(8,128)S(1)}, f32[192,2560]{1,0:T(8,128)S(1)}) custom-call(bf16[192,2560]{1,0:T(8,128)(2,1)S(1)} %get-tuple-element.65.branch, f32[8,2560]{1,0:T(8,128)S(1)} %pad_convert_fusion.prior, f32[16,2560]{1,0:T(8,128)S(1)} %copy-done.8, ...), custom_call_target="tpu_custom_call" | custom-call | flops 1 | bytes 1 | tf_op jit(solution)/shard_map/mixer_forward/pallas_call | solution.py:1301
  235.5 1.3 copy-done.2
  236.8 1.3 copy-done.12
  238.1 0.9 copy-done.16
  239.1 14.9 %all-gather.2 = f32[8,2,2560]{2,1,0:T(2,128)S(1)} all-gather(f32[1,2,2560]{2,1,0:T(2,128)S(1)} %fusion.21), channel_id=2, replica_groups=mesh['seq'=8,'fsdp'=4] {'seq'}, dimensions={0}, use_global_device_ids=true | all-gather | bytes 184320 | tf_op jit(solution)/shard_map/all_gather | solution.py:29
  255.3 1.3 copy-done
  256.5 12.6 %multiply_reduce_fusion.3 = (f32[192]{0:T(256)S(1)}, f32[192,2560]{1,0:T(8,128)}) fusion(bf16[192,2560]{1,0:T(8,128)(2,1)S(1)} %fusion.17.mixed, bf16[2560,8320]{1,0:T(8,128)(2,1)} %get-tuple-element.64.columns.weights.rate_w.input_w.mixer_w, bf16[1,192,2560]{2,1,0:T(8,128)(2,1)S(1)} %copy-done.10), kind=kOutput, calls=%fused_computation.28 | convolution fusion | flops 2518548224 | bytes 17040128 | tf_op jit(solution)/shard_map/dot_general | solution.py:62
  269.1 2.7 multiply_convert_fusion.normed
  271.9 82.3 %gather_rows.1 = (bf16[768,2560]{1,0:T(8,128)(2,1)}, bf16[768,2560]{1,0:T(8,128)(2,1)}, bf16[768,2560]{1,0:T(8,128)(2,1)}, bf16[768,2560]{1,0:T(8,128)(2,1)}, bf...) custom-call(bf16[192,2560]{1,0:T(8,128)(2,1)} %multiply_convert_fusion.normed, bf16[192,2560]{1,0:T(8,128)(2,1)} %bitcast.12.grad0, ...), custom_call_target="tpu_custom_call" | custom-call | tf_op jit(solution)/shard_map/gather_rows/pallas_call | solution.py:551
  354.2 52.3 %feed_forward.1 = (bf16[768,1920]{1,0:T(8,128)(2,1)}, bf16[768,1920]{1,0:T(8,128)(2,1)}, bf16[768,3840]{1,0:T(8,128)(2,1)}, bf16[768,3840]{1,0:T(8,128)(2,1)}, bf16[768,2560]{1,0:T(8,128)(2,1)}) custom-call(bf16[768,2560]{1,0:T(8,128)(2,1)} %get-tuple-element.72.normed, bf16[768,2560]{1,0:T(8,128)(2,1)} %get-tuple-element.73.grad_out.grad, ...), custom_call_target="tpu_custom_call" | custom-call | tf_op jit(solution)/shard_map/feed_forward/pallas_call | solution.py:654
  406.6 57.1 %feed_forward_products.1 = (bf16[160,5760]{1,0:T(8,128)(2,1)}, bf16[160,5760]{1,0:T(8,128)(2,1)}, bf16[320,5760]{1,0:T(8,128)(2,1)}, bf16[160,5760]{1,0:T(8,128)...) custom-call(bf16[768,2560]{1,0:T(8,128)(2,1)} %get-tuple-element.72.normed, ...), custom_call_target="tpu_custom_call" | custom-call | tf_op jit(solution)/shard_map/feed_forward_products/pallas_call | solution.py:867
  463.7 1.8 collective-permute-start.5
  465.6 12.0 %reduce-scatter.3.cloned.1.call-done = bf16[192,2560]{1,0:T(8,128)(2,1)} async-done(((bf16[768,2560]{1,0:T(8,128)(2,1)}), bf16[192,2560]{1,0:T(8,128)(2,1)}) %reduce-scatter.3.cloned.1.call-update) | async-done | bytes 983056 | tf_op jit(solution)/shard_map/reduce_scatter | solution.py:1409
  477.6 2.2 multiply_reduce_fusion.2
  479.8 3.3 add_convert_fusion.3.grad_mix
  483.1 7.4 fusion.grad_mixed
  490.7 11.2 %mixer_backward_scan.1 = (bf16[192,2560]{1,0:T(8,128)(2,1)S(1)}, f32[192,2560]{1,0:T(8,128)S(1)}, f32[192,2560]{1,0:T(8,128)S(1)}, f32[8,2560]{1,0:T(8,128)S(1)}) custom-call(f32[192,2560]{1,0:T(8,128)S(1)} %fusion.grad_mixed, f32[192,2560]{1,0:T(8,128)S(1)} %copy-done.6, f32[192,2560]{1,0:T(8,128)S(1)} %copy-done.3, f32[192,2560]{1,0:T(8,128)S(1)} %get-tuple-element.67.cum, ...), custom_call_target="tpu_custom_call" | custom-call | flops 1 | bytes 1 | tf_op jit(solution)/shard_map/mixer_backward_scan/pallas_call | solution.py:1301
  501.9 4.2 collective-permute-done.4
  506.2 9.4 %all-gather.3 = f32[8,2,2560]{2,1,0:T(2,128)S(1)} all-gather(f32[1,2,2560]{2,1,0:T(2,128)S(1)} %fusion.22), channel_id=3, replica_groups=mesh['seq'=8,'fsdp'=4] {'seq'}, dimensions={0}, use_global_device_ids=true | all-gather | bytes 184320 | tf_op jit(solution)/shard_map/all_gather | solution.py:29
  516.5 1.7 collective-permute-start.9
  518.2 10.6 %mixer_backward.1 = (f32[192,2560]{1,0:T(8,128)S(1)}, f32[8,2560]{1,0:T(8,128)S(1)}, bf16[2560,256]{1,0:T(8,128)(2,1)S(1)}, bf16[2560,256]{1,0:T(8,128)(2,1)S(1)}, f32[8,2560]{1,0:T(8,128)S(1)}) custom-call(f32[192,2560]{1,0:T(8,128)S(1)} %get-tuple-element.76.rev_cum, f32[192,2560]{1,0:T(8,128)S(1)} %get-tuple-element.77.rev_grad, ...), custom_call_target="tpu_custom_call" | custom-call | flops 1 | bytes 1 | tf_op jit(solution)/shard_map/mixer_backward/pallas_call | solution.py:1301
  528.8 1.1 copy-done.14
  529.9 1.1 copy-done.15
  530.9 1.3 copy-done.19
  532.2 1.3 collective-permute-start.8
  533.9 1.2 collective-permute-start.7
  535.1 3.1 fusion.8.rest
  538.2 14.7 %reduce-scatter.5.cloned.1.call-done = bf16[192,2560]{1,0:T(8,128)(2,1)} async-done(((bf16[768,2560]{1,0:T(8,128)(2,1)}), bf16[192,2560]{1,0:T(8,128)(2,1)}) %reduce-scatter.5.cloned.1.call-update) | async-done | bytes 983056 | tf_op jit(solution)/shard_map/reduce_scatter | solution.py:1427
  552.9 2.9 fusion.18
  556.0 1.0 pad_maximum_fusion.grad_branch
  557.0 1.8 collective-permute-done.10
  558.9 6.3 add_convert_fusion
  566.2 185.1 %scatter_gradients.1 = (bf16[80,8320]{1,0:T(8,128)(2,1)}, bf16[3,80,7680]{2,1,0:T(8,128)(2,1)}, bf16[192,2560]{1,0:T(8,128)(2,1)}) custom-call(bf16[192,2560]{1,0:T(8,128)(2,1)} %copy-done.11, bf16[192,2560]{1,0:T(8,128)(2,1)} %get-tuple-element.98.normed_other, bf16[192,2560]{1,0:T(8,128)(2,1)} %add_convert_fusion.3.grad_mix, ...), custom_call_target="tpu_custom_call" | custom-call | tf_op jit(solution)/shard_map/scatter_gradients/pallas_call | solution.py:1208
  751.4 1.7 slice_convert_fusion.1
  753.1 1.6 multiply_reduce_fusion.4
  755.8 3.0 multiply_reduce_fusion
  758.9 1.6 bitcast_convert_fusion
  763.2 0.9 copy.62
  (106 shorter events, 10.7 us)
Async XLA Ops:
  7.2 347.0 %all-gather.6.cloned.1.call-start = ((), (), s32[]{:S(2)}) async-start(), calls=%async_computation.2 | async-start | bytes 33177600 | tf_op jit(solution)/shard_map/all_gather | solution.py:1358
  194.0 283.6 %reduce-scatter.3.cloned.1.call-start = ((), (), s32[]{:S(2)}) async-start(), calls=%async_computation.3 | async-start | bytes 4915200 | tf_op jit(solution)/shard_map/reduce_scatter | solution.py:1409
  194.1 77.8 %collective-permute-start.1 = (bf16[192,2560]{1,0:T(8,128)(2,1)}, bf16[192,2560]{1,0:T(8,128)(2,1)}, u32[]{:S(2)}, u32[]{:S(2)}) collective-permute-start(bf16[192,2560]{1,0:T(8,128)(2,1)} %bitcast.12.grad0), channel_id=1, source_target_pairs={{0,1},{1,2},{2,3},{3,0},{4,5},{5,6},{6,7},{7,4},{8,9},{9,10},{10,1... | collective-permute-start | bytes 2949128 | tf_op jit(solution)/shard_map/ppermute | solution.py:1252
  199.5 72.3 %collective-permute-start.2 = (bf16[192,2560]{1,0:T(8,128)(2,1)}, bf16[192,2560]{1,0:T(8,128)(2,1)}, u32[]{:S(2)}, u32[]{:S(2)}) collective-permute-start(bf16[192,2560]{1,0:T(8,128)(2,1)} %bitcast.12.grad0), channel_id=1, source_target_pairs={{0,2},{1,3},{2,0},{3,1},{4,6},{5,7},{6,4},{7,5},{8,10},{9,11},{10,... | collective-permute-start | bytes 2949128 | tf_op jit(solution)/shard_map/ppermute | solution.py:1252
  202.9 69.0 %collective-permute-start.3 = (bf16[192,2560]{1,0:T(8,128)(2,1)}, bf16[192,2560]{1,0:T(8,128)(2,1)}, u32[]{:S(2)}, u32[]{:S(2)}) collective-permute-start(bf16[192,2560]{1,0:T(8,128)(2,1)} %bitcast.12.grad0), channel_id=1, source_target_pairs={{0,3},{1,0},{2,1},{3,2},{4,7},{5,4},{6,5},{7,6},{8,11},{9,8},{10,9... | collective-permute-start | bytes 2949128 | tf_op jit(solution)/shard_map/ppermute | solution.py:1252
  202.9 2.1 copy-start.9
  205.0 0.9 copy-start.7
  205.9 20.1 %copy-start.8 = (f32[16,2560]{1,0:T(8,128)S(1)}, f32[16,2560]{1,0:T(8,128)}, u32[]{:S(2)}) copy-start(f32[16,2560]{1,0:T(8,128)} %small_table.1.table.small.gain) | copy-start | bytes 491524
  221.6 1.3 copy-start.4
  222.9 0.9 copy-start.11
  223.8 2.1 collective-permute-start
  226.0 28.4 %copy-start.5 = (f32[192,2560]{1,0:T(8,128)S(1)}, f32[192,2560]{1,0:T(8,128)}, u32[]{:S(2)}) copy-start(f32[192,2560]{1,0:T(8,128)} %copy-done.4) | copy-start | bytes 5898244
  235.5 1.3 copy-start.2
  236.8 1.3 copy-start.12
  238.1 0.9 copy-start.16
  254.4 2.1 copy-start.10
  255.3 1.3 copy-start
  256.5 12.6 %copy-start.21 = (bf16[192,2560]{1,0:T(8,128)(2,1)}, bf16[192,2560]{1,0:T(8,128)(2,1)S(1)}, u32[]{:S(2)}) copy-start(bf16[192,2560]{1,0:T(8,128)(2,1)S(1)} %fusion.17.mixed) | copy-start | bytes 2949124
  406.5 146.4 %reduce-scatter.5.cloned.1.call-start = ((), (), s32[]{:S(2)}) async-start(), calls=%async_computation.4 | async-start | bytes 4915200 | tf_op jit(solution)/shard_map/reduce_scatter | solution.py:1427
  463.7 42.4 %collective-permute-start.4 = (bf16[160,5760]{1,0:T(8,128)(2,1)}, bf16[160,5760]{1,0:T(8,128)(2,1)}, u32[]{:S(2)}, u32[]{:S(2)}) collective-permute-start(bf16[160,5760]{1,0:T(8,128)(2,1)} %get-tuple-element.86), channel_id=1, source_target_pairs={{0,8},{4,12},{8,0},{12,4},{16,24},{20,28},{24,16},{28,20},{1,9},{5... | collective-permute-start | bytes 5529608 | tf_op jit(solution)/shard_map/ppermute | solution.py:1262
  463.7 42.4 %collective-permute-start.5 = (bf16[160,5760]{1,0:T(8,128)(2,1)}, bf16[160,5760]{1,0:T(8,128)(2,1)}, u32[]{:S(2)}, u32[]{:S(2)}) collective-permute-start(bf16[160,5760]{1,0:T(8,128)(2,1)} %get-tuple-element.87), channel_id=1, source_target_pairs={{0,16},{4,20},{8,24},{12,28},{16,0},{20,4},{24,8},{28,12},{1,17},{... | collective-permute-start | bytes 5529608 | tf_op jit(solution)/shard_map/ppermute | solution.py:1266
  477.6 2.2 copy-start.24
  483.1 7.4 copy-start.1
  483.1 7.4 copy-start.3
  483.1 7.5 copy-start.6
  483.1 82.2 %collective-permute-start.6 = (bf16[192,2560]{1,0:T(8,128)(2,1)}, bf16[192,2560]{1,0:T(8,128)(2,1)}, u32[]{:S(2)}, u32[]{:S(2)}) collective-permute-start(bf16[192,2560]{1,0:T(8,128)(2,1)} %add_convert_fusion.3.grad_mix), channel_id=1, source_target_pairs={{0,4},{4,0},{8,12},{12,8},{16,20},{20,16},{24,28},{28,24},{1,5},{5... | collective-permute-start | bytes 2949128 | tf_op jit(solution)/shard_map/ppermute | solution.py:1258
  490.6 27.5 %copy-start.13 = (f32[192,2560]{1,0:T(8,128)S(1)}, f32[192,2560]{1,0:T(8,128)}, u32[]{:S(2)}) copy-start(f32[192,2560]{1,0:T(8,128)} %copy-done.12) | copy-start | bytes 5898244
  490.7 27.5 %copy-start.17 = (bf16[192,2560]{1,0:T(8,128)(2,1)S(1)}, bf16[192,2560]{1,0:T(8,128)(2,1)}, u32[]{:S(2)}) copy-start(bf16[192,2560]{1,0:T(8,128)(2,1)} %copy-done.16) | copy-start | bytes 2949124
  501.9 16.3 %copy-start.18 = (bf16[192,2560]{1,0:T(8,128)(2,1)}, bf16[192,2560]{1,0:T(8,128)(2,1)S(1)}, u32[]{:S(2)}) copy-start(bf16[192,2560]{1,0:T(8,128)(2,1)S(1)} %get-tuple-element.100.grad_gelu) | copy-start | bytes 2949124
  516.0 42.8 %collective-permute-start.10 = (bf16[160,5760]{1,0:T(8,128)(2,1)}, bf16[160,5760]{1,0:T(8,128)(2,1)}, u32[]{:S(2)}, u32[]{:S(2)}) collective-permute-start(bf16[160,5760]{1,0:T(8,128)(2,1)} %get-tuple-element.106), channel_id=1, source_target_pairs={{0,16},{4,20},{8,24},{12,28},{16,0},{20,4},{24,8},{28,12},{1,17},{... | collective-permute-start | bytes 5529608 | tf_op jit(solution)/shard_map/ppermute | solution.py:1266
  516.5 42.5 %collective-permute-start.9 = (bf16[160,5760]{1,0:T(8,128)(2,1)}, bf16[160,5760]{1,0:T(8,128)(2,1)}, u32[]{:S(2)}, u32[]{:S(2)}) collective-permute-start(bf16[160,5760]{1,0:T(8,128)(2,1)} %get-tuple-element.105), channel_id=1, source_target_pairs={{0,8},{4,12},{8,0},{12,4},{16,24},{20,28},{24,16},{28,20},{1,9},{5... | collective-permute-start | bytes 5529608 | tf_op jit(solution)/shard_map/ppermute | solution.py:1262
  528.8 1.1 copy-start.14
  529.9 1.1 copy-start.15
  530.9 1.3 copy-start.19
  532.2 23.7 %collective-permute-start.8 = (f32[3,2560]{1,0:T(4,128)S(1)}, f32[3,2560]{1,0:T(4,128)S(1)}, u32[]{:S(2)}, u32[]{:S(2)}) collective-permute-start(f32[3,2560]{1,0:T(4,128)S(1)} %slice.217), channel_id=1, source_target_pairs={{4,0},{8,4},{12,8},{16,12},{20,16},{24,20},{28,24},{5,1},{9,5},{13... | collective-permute-start | bytes 92168 | tf_op jit(solution)/shard_map/ppermute | solution.py:23
  533.9 31.4 %collective-permute-start.7 = (bf16[192,2560]{1,0:T(8,128)(2,1)}, bf16[192,2560]{1,0:T(8,128)(2,1)S(1)}, u32[]{:S(2)}, u32[]{:S(2)}) collective-permute-start(bf16[192,2560]{1,0:T(8,128)(2,1)} %copy-done.18), channel_id=1, source_target_pairs={{0,4},{4,0},{8,12},{12,8},{16,20},{20,16},{24,28},{28,24},{1,5},{5... | collective-permute-start | bytes 2949128 | tf_op jit(solution)/shard_map/ppermute | solution.py:1258
  538.2 17.7 %copy-start.20 = (f32[192,2560]{1,0:T(8,128)S(1)}, f32[192,2560]{1,0:T(8,128)}, u32[]{:S(2)}) copy-start(f32[192,2560]{1,0:T(8,128)} %copy-done.19) | copy-start | bytes 5898244
  555.9 3.1 copy-start.26
  565.3 0.9 copy-start.30
  566.2 186.9 %copy-start.27 = (bf16[80,2560]{1,0:T(8,128)(2,1)S(1)}, bf16[80,2560]{1,0:T(8,128)(2,1)}, u32[]{:S(2)}) copy-start(bf16[80,2560]{1,0:T(8,128)(2,1)} %branch.1) | copy-start | bytes 1228804
  566.2 186.9 %copy-start.28 = (bf16[80,2560]{1,0:T(8,128)(2,1)S(1)}, bf16[80,2560]{1,0:T(8,128)(2,1)}, u32[]{:S(2)}) copy-start(bf16[80,2560]{1,0:T(8,128)(2,1)} %gelu.1) | copy-start | bytes 1228804
  751.4 4.0 copy-start.25
  753.1 2.3 copy-start.22
  753.1 2.7 copy-start.23
  758.9 3.8 copy-start.31
  758.9 3.8 copy-start.32
  758.9 4.3 copy-start.29
Sparse Core Ops, SparseCore 0:
  194.1 149.8 all-gather.5
  406.6 70.8 reduce-scatter.2
  479.9 73.0 reduce-scatter.4
